TPU v7x, 32 devices: a whole 2x2x4 slice. The times are simulated.
32 devices in a mesh: groups: 2 (over x), wide: 16 (over z, y, core).
Axes of the slice: x: 2, y: 2, z: 4, core: 2. Of those that a mesh axis runs over, the one named last changes fastest.
Arguments:
- token_adapter_index: int32 [4096, 1], P(('groups', 'wide')), parts along dimension 0, may hold values from 0 to 15; in each aligned block of 128 rows (0 to 127, 128 to 255, ...) at most 16 rows name the same one
- hidden: bfloat16 [4096, 8192], P(('groups', 'wide')), parts along dimension 0, may hold values from -6 to 6
- adapter_down_maps: bfloat16 [16, 8192, 64], P('wide'), may hold values from -0.0625 to 0.0625
- adapter_up_maps: bfloat16 [16, 64, 8192], P('wide'), may hold values from -0.75 to 0.75
Outputs:
- lora_delta: bfloat16 [4096, 8192], P(('groups', 'wide')), parts along dimension 0
There are 2 independent parts, one for each index of `groups`. A program takes and returns all parts, laid end to end along the dimension named above; an argument that names none is the same for every part. Nothing has to cross between parts.
Inputs may be any that keep to these rules, and one draw needn't show every extreme that they name: `token_adapter_index`: within the rows of one device at most 16 tokens name the same adapter, and 16 is reached in some device's rows; every adapter is named by some token.
All inputs are finite; a program needn't handle non-finite values.
Results may differ from a plain program's by a relative error of at most 0.0049.
Values may be sent and summed in bfloat16 or wider, within the bound.
No kernel may reach another device: no remote copies, remote signals or barrier semaphores. Data moves between devices by JAX's collectives and lax.ppermute only.
A program may use at most 64 MiB of HBM per device.

v0:
```python
import jax
import jax.numpy as jnp
from jax import lax
from jax.sharding import PartitionSpec as P

adapter_scale = 2.0


def per_device(token_adapter_index, hidden, adapter_down_maps, adapter_up_maps):
    owners = lax.axis_size("wide")
    tok_count = hidden.shape[0]
    width = hidden.shape[1]
    output_width = adapter_up_maps.shape[2]
    capacity = max(2, 2 * tok_count // owners)
    ids = token_adapter_index[:, 0]
    order = jnp.arange(tok_count, dtype=jnp.int32)
    same = (ids[None, :] == ids[:, None]) & (order[None, :] < order[:, None])
    ranks = jnp.sum(same.astype(jnp.int32), axis=1)
    flat = ids * capacity + ranks
    outgoing = jnp.zeros((owners * capacity, width), hidden.dtype).at[flat].set(hidden)
    outgoing = outgoing.reshape(owners, capacity, width)
    arrived = lax.all_to_all(outgoing, "wide", split_axis=0, concat_axis=0, tiled=True)
    token_rows = arrived.reshape(-1, width)
    reduced_rows = jnp.dot(
        token_rows, adapter_down_maps[0], preferred_element_type=jnp.float32
    ).astype(jnp.bfloat16)
    query_delta = (
        adapter_scale
        * jnp.dot(reduced_rows, adapter_up_maps[0], preferred_element_type=jnp.float32)
    ).astype(jnp.bfloat16)
    returned = lax.all_to_all(
        query_delta.reshape(arrived.shape[0], arrived.shape[1], output_width),
        "wide",
        split_axis=0,
        concat_axis=0,
        tiled=True,
    )
    return returned.reshape(owners * capacity, output_width)[flat]


def solution(mesh):
    placed = (
        P(("groups", "wide"), None),
        P(("groups", "wide"), None),
        P("wide", None, None),
        P("wide", None, None),
    )
    return jax.shard_map(
        per_device,
        mesh=mesh,
        in_specs=placed,
        out_specs=P(("groups", "wide"), None),
        check_vma=False,
    )
```

profile of v0, /device:TPU:15, one launch (start us, length us, event | category | flops | bytes accessed | tf_op | source)
XLA Modules:
  0.0 222.1 jit_solution(4369851065959861697)
XLA Ops:
  0.0 0.0 copy-start
  0.0 0.9 convert_reduce_fusion
  0.9 0.7 fusion.7
  1.6 7.0 %scatter_custom_fusion = bf16[256,8192]{1,0:T(8,128)(2,1)} fusion(s32[128]{0:T(128)S(1)} %fusion.7, bf16[128,8192]{1,0:T(8,128)(2,1)} %param.5, bf16[]{:T(256)} %constant.5.clone.1), kind=kCustom, calls=%fused_computation.4 | custom fusion | bytes 4194816 | tf_op jit(solution)/shard_map/scatter | solution.py:20
  8.6 0.0 copy-start.1
  8.6 99.0 %all_to_all.10 = bf16[16,16,8192]{2,1,0:T(8,128)(2,1)} all-to-all(bf16[16,16,8192]{2,1,0:T(8,128)(2,1)} %bitcast.20), channel_id=1, replica_groups=mesh['groups'=2,'wide'=16] {'wide'}, dimensions={0} | all-to-all | bytes 8388608 | tf_op jit(solution)/shard_map/all_to_all | solution.py:22
  107.7 0.0 copy-done
  107.7 0.0 copy-done.1
  107.7 8.9 %fusion = bf16[256,8192]{1,0:T(8,128)(2,1)} fusion(bf16[256,8192]{1,0:T(8,128)(2,1)} %bitcast.21, bf16[1,64,8192]{2,1,0:T(8,128)(2,1)S(1)} %copy-done, bf16[1,8192,64]{1,2,0:T(8,128)(2,1)S(1)} %copy-done.1), kind=kOutput, calls=%fused_computation.3 | convolution fusion | flops 541081600 | bytes 10485760 | tf_op jit(solution)/shard_map/dot_general | solution.py:29
  116.6 5.3 %all-to-all-start.1 = ((bf16[16,16,8192]{2,1,0:T(8,128)(2,1)}), bf16[16,16,8192]{2,1,0:T(8,128)(2,1)}, u32[]{:S(2)}, u32[]{:S(2)}) async-start(bf16[16,16,8192]{2,1,0:T(8,128)(2,1)} %bitcast.19), calls=%async_computation.1 | async-start | bytes 8388608 | tf_op jit(solution)/shard_map/all_to_all | solution.py:31
  121.9 92.5 %all-to-all-done.1 = bf16[16,16,8192]{2,1,0:T(8,128)(2,1)} async-done(((bf16[16,16,8192]{2,1,0:T(8,128)(2,1)}), bf16[16,16,8192]{2,1,0:T(8,128)(2,1)}, u32[]{:S(2)}, u32[]{:S(2)}) %all-to-all-start.1) | async-done | bytes 4194336 | tf_op jit(solution)/shard_map/all_to_all | solution.py:31
  214.3 7.8 %gather_fusion = bf16[128,8192]{1,0:T(8,128)(2,1)} fusion(bf16[256,8192]{1,0:T(8,128)(2,1)} %bitcast.8, s32[1024]{0:T(1024)S(1)} %pad_clamp_fusion), kind=kCustom, calls=%fused_computation | custom fusion | bytes 4194816 | tf_op jit(solution)/shard_map/gather | solution.py:38
  (1 shorter events, 0.0 us)
Async XLA Ops:
  0.0 107.7 %copy-start = (bf16[1,64,8192]{2,1,0:T(8,128)(2,1)S(1)}, bf16[1,64,8192]{2,1,0:T(8,128)(2,1)}, u32[]{:S(2)}) copy-start(bf16[1,64,8192]{2,1,0:T(8,128)(2,1)} %param.7) | copy-start | bytes 3145732
  8.6 99.0 %copy-start.1 = (bf16[1,8192,64]{1,2,0:T(8,128)(2,1)S(1)}, bf16[1,8192,64]{1,2,0:T(8,128)(2,1)}, u32[]{:S(2)}) copy-start(bf16[1,8192,64]{1,2,0:T(8,128)(2,1)} %param.6) | copy-start | bytes 3145732
  116.6 97.8 %all-to-all-start.1 = ((bf16[16,16,8192]{2,1,0:T(8,128)(2,1)}), bf16[16,16,8192]{2,1,0:T(8,128)(2,1)}, u32[]{:S(2)}, u32[]{:S(2)}) async-start(bf16[16,16,8192]{2,1,0:T(8,128)(2,1)} %bitcast.19), calls=%async_computation.1 | async-start | bytes 8388608 | tf_op jit(solution)/shard_map/all_to_all | solution.py:31
where the time goes:
time: 223 us; the launch traced here: 222 us
  blocking collectives  99 us (44%)
  waiting for transfers between devices  92.5 us (41%)
  local copies, waits for them, and re-layouts  14.8 us (7%)
  matrix products  8.89 us (4%)
  starting transfers between devices  5.32 us (2%)
    all_to_all x1, blocking collectives, per_device(): lax.all_to_all(outgoing, 'wide', split_axis=0, concat_axis=0, tiled=True)  99 us
    all_to_all x1, waiting for transfers between devices, per_device(): lax.all_to_all(query_delta.reshape(arrived.shape[0], arrived.shape[1], ou...  92.5 us
    dot_general x1, matrix products, per_device(): jnp.dot(reduced_rows, adapter_up_maps[0], preferred_element_type=jnp.floa...  8.89 us
    gather x1, local copies, waits for them, and re-layouts, per_device(): return returned.reshape(owners * capacity, output_width)[flat]  7.81 us
    scatter x1, local copies, waits for them, and re-layouts, per_device(): jnp.zeros((owners * capacity, width), hidden.dtype).at[flat].set(hidden)  7.02 us
    all_to_all x1, starting transfers between devices, per_device(): lax.all_to_all(query_delta.reshape(arrived.shape[0], arrived.shape[1], ou...  5.32 us
  transfers between devices with their start and end apart: 1, of which 1 were waited for; matrix products, arithmetic and copies ran while one was open for 0% of the time, Pallas kernels for 0%

commit v1 on v0

v1 whole, which is shorter than its diff:
```python
import jax
import jax.numpy as jnp
from jax import lax
from jax.sharding import Mesh
from jax.sharding import PartitionSpec as P

adapter_scale = 2.0
PLANE = ("groups", "inner")


def own_width_slices(adapter, parts):
    rank, width = adapter.shape
    share = width // lax.axis_size("groups")
    half = lax.dynamic_slice_in_dim(adapter, lax.axis_index("groups") * share, share, axis=1)
    return half.reshape(rank, parts, share // parts).transpose(1, 0, 2)


def gathered(adapter):
    inner = lax.axis_size("inner")
    in_plane = lax.all_to_all(
        own_width_slices(adapter, inner), "inner", split_axis=0, concat_axis=0, tiled=True
    )
    return lax.all_gather(in_plane, "outer", axis=0, tiled=True)


def per_device(token_adapter_index, hidden, adapter_down_maps, adapter_up_maps):
    tok_count = hidden.shape[0]
    adapters = lax.axis_size("outer") * lax.axis_size("inner")
    down = gathered(adapter_down_maps[0].T)
    up = gathered(adapter_up_maps[0])
    rank, share = down.shape[1], down.shape[2]
    ids = lax.all_gather(token_adapter_index[:, 0], PLANE, axis=0, tiled=True)
    rows = lax.all_to_all(hidden, PLANE, split_axis=1, concat_axis=0, tiled=True)
    named = ids[None, None, :] == jnp.arange(adapters, dtype=jnp.int32)[:, None, None]

    partial = lax.dot_general(
        down.reshape(adapters * rank, share), rows, (((1,), (1,)), ((), ())), preferred_element_type=jnp.float32
    ).reshape(adapters, rank, rows.shape[0])
    partial = jnp.sum(jnp.where(named, partial, 0.0), axis=0)
    shrunk = lax.psum(partial, PLANE).astype(jnp.bfloat16)

    spread = jnp.where(named, shrunk[None], jnp.zeros((), jnp.bfloat16)).reshape(adapters * rank, rows.shape[0])
    delta = adapter_scale * lax.dot_general(
        spread, up.reshape(adapters * rank, share), (((0,), (0,)), ((), ())), preferred_element_type=jnp.float32
    )
    return lax.all_to_all(delta.astype(jnp.bfloat16), PLANE, split_axis=0, concat_axis=1, tiled=True)


def solution(mesh):
    groups, wide = mesh.shape["groups"], mesh.shape["wide"]
    outer = 1 << ((wide.bit_length() - 1) // 2)
    fine = Mesh(mesh.devices.reshape(groups, outer, wide // outer), ("groups", "outer", "inner"))
    owner = ("outer", "inner")
    rows = P(("groups",) + owner, None)
    return jax.shard_map(
        per_device,
        mesh=fine,
        in_specs=(rows, rows, P(owner, None, None), P(owner, None, None)),
        out_specs=rows,
        check_vma=False,
    )
```

time: 223 us -> 157 us (0.70)
  the two profiles are of different devices: /device:TPU:15 before, /device:TPU:0 now
where the time goes in v1:
time: 157 us; the launch traced here: 156 us
  blocking collectives  112 us (71%)
  between operations  13.5 us (9%)
  local copies, waits for them, and re-layouts  12.7 us (8%)
  matrix products  8.74 us (6%)
  waiting for transfers between devices  5.51 us (4%)
  starting transfers between devices  3.78 us (2%)
    all_gather x1, blocking collectives, per_device(): ids = lax.all_gather(token_adapter_index[:, 0], PLANE, axis=0, tiled=True)  29.5 us
    all_to_all x1, blocking collectives, per_device(): lax.all_to_all(delta.astype(jnp.bfloat16), PLANE, split_axis=0, concat_ax...  29.4 us
    psum x1, blocking collectives, per_device(): shrunk = lax.psum(partial, PLANE).astype(jnp.bfloat16)  28 us
    all_to_all x2, blocking collectives, gathered(): lax.all_to_all(own_width_slices(adapter, inner), 'inner', split_axis=0, c...  24.9 us
    all_gather x2, waiting for transfers between devices, gathered(): return lax.all_gather(in_plane, 'outer', axis=0, tiled=True)  5.47 us
    dot_general x1, matrix products, per_device(): lax.dot_general(down.reshape(adapters * rank, share), rows, (((1,), (1,))...  4.78 us
    dot_general x1, matrix products, per_device(): lax.dot_general(spread, up.reshape(adapters * rank, share), (((0,), (0,))...  3.96 us
    all_to_all x1, starting transfers between devices, per_device(): lax.all_to_all(hidden, PLANE, split_axis=1, concat_axis=0, tiled=True)  3.74 us
  transfers between devices with their start and end apart: 3, of which 1 were waited for; matrix products, arithmetic and copies ran while one was open for 9% of the time, Pallas kernels for 0%

profile of v1, /device:TPU:0, one launch (start us, length us, event | category | flops | bytes accessed | tf_op | source)
XLA Modules:
  0.0 156.1 jit_solution(17234357444243548840)
XLA Ops:
  6.5 0.0 copy-start
  6.5 0.0 all-gather.4.cloned.1.call-start
  6.5 1.2 copy-done
  7.8 0.0 copy-start.2
  7.8 0.4 reshape.46
  8.2 0.2 copy.22
  8.4 13.0 %all_to_all.48 = bf16[4,64,1024]{2,1,0:T(8,128)(2,1)} all-to-all(bf16[4,64,1024]{2,1,0:T(8,128)(2,1)S(1)} %copy.22), channel_id=1, replica_groups=mesh['groups'=2,'outer'=4,'inner'=4] {'inner'}, dimensions={0} | all-to-all | bytes 1048576 | tf_op jit(solution)/shard_map/all_to_all | solution.py:20
  21.3 0.0 all-gather.4.cloned.1.call-update
  21.4 0.0 all-gather.6.cloned.1.call-start
  21.4 0.0 copy-done.2
  21.4 0.8 constant_dynamic-slice_fusion
  22.3 0.0 copy-start.1
  22.3 2.4 %reshape.47 = bf16[64,4,1024]{2,1,0:T(4,128)(2,1)} reshape(bf16[1,64,4096]{2,1,0:T(8,128)(2,1)} %constant_dynamic-slice_fusion) | data formatting | bytes 1048576 | tf_op jit(solution)/shard_map/reshape | solution.py:15
  24.7 1.2 copy.25
  25.9 11.9 %all_to_all.49 = bf16[4,64,1024]{2,1,0:T(8,128)(2,1)} all-to-all(bf16[4,64,1024]{2,1,0:T(8,128)(2,1)S(1)} %copy.25), channel_id=1, replica_groups=mesh['groups'=2,'outer'=4,'inner'=4] {'inner'}, dimensions={0} | all-to-all | bytes 1048576 | tf_op jit(solution)/shard_map/all_to_all | solution.py:20
  37.8 0.0 all-gather.6.cloned.1.call-update
  37.8 0.0 copy-done.1
  37.8 2.4 %copy.23 = bf16[128,8192]{0,1:T(8,128)(2,1)} copy(bf16[128,8192]{1,0:T(8,128)(2,1)S(1)} %copy-done.1) | data formatting | bytes 4194304 | tf_op args[1]
  40.3 0.0 copy-start.3
  40.3 3.7 %all-to-all-start.1 = ((bf16[128,8,1024]{0,2,1:T(8,128)(2,1)}), bf16[128,8,1024]{0,2,1:T(8,128)(2,1)S(1)}, u32[]{:S(2)}, u32[]{:S(2)}) async-start(bf16[128,8,1024]{0,2,1:T(8,128)(2,1)} %bitcast.24), calls=%async_computation.1 | async-start | bytes 4194304 | tf_op jit(solution)/shard_map/all_to_all | solution.py:33
  44.0 0.0 copy-done.3
  44.0 29.5 %all-gather = s32[1024,1]{0,1:T(1,128)S(1)} all-gather(s32[128,1]{0,1:T(1,128)S(1)} %copy-done.3), channel_id=2, replica_groups=mesh['groups'=2,'outer'=4,'inner'=4] {'groups','inner'}, dimensions={0}, use_global_device_ids=true | all-gather | bytes 4608 | tf_op jit(solution)/shard_map/all_gather | solution.py:32
  73.6 0.0 all-to-all-done.1
  73.6 2.6 %copy.24 = bf16[8,128,1024]{2,1,0:T(8,128)(2,1)} copy(bf16[8,128,1024]{1,2,0:T(8,128)(2,1)S(1)} %bitcast.23) | data formatting | bytes 4194304 | tf_op jit(solution)/shard_map/all_to_all | solution.py:33
  76.2 0.0 all-gather.4.cloned.1.call-done
  76.2 4.8 %select_reduce_fusion = f32[64,1024]{1,0:T(8,128)S(1)} fusion(pred[16,1024]{1,0:T(8,128)(4,1)S(1)} %iota_compare_fusion, bf16[16,64,1024]{2,1,0:T(8,128)(2,1)} %all-gather.4.cloned.1.call-done, bf16[1024,1024,1]{1,0,2:T(8,128)(2,1)} %bitcast.26), kind=kOutput, calls=%fused_computation.2 | convolution fusion | flops 2149515264 | bytes 4472832 | tf_op jit(solution)/shard_map/dot_general | solution.py:36
  81.0 28.0 %all-reduce.1 = bf16[64,1024]{1,0:T(8,128)(2,1)S(1)} all-reduce(f32[64,1024]{1,0:T(8,128)S(1)} %select_reduce_fusion), channel_id=1, replica_groups=mesh['groups'=2,'outer'=4,'inner'=4] {'groups','inner'}, use_global_device_ids=true, to_apply=%region_1.2 | all-reduce | flops 65536 | bytes 393216 | tf_op jit(solution)/shard_map/psum | solution.py:40
  108.9 5.5 %all-gather.6.cloned.1.call-done = bf16[16,64,1024]{2,1,0:T(8,128)(2,1)} async-done(((bf16[4,64,1024]{2,1,0:T(8,128)(2,1)}), bf16[16,64,1024]{2,1,0:T(8,128)(2,1)}) %all-gather.6.cloned.1.call-update) | async-done | bytes 2097168 | tf_op jit(solution)/shard_map/all_gather | solution.py:23
  114.4 4.0 %fusion = bf16[1024,1024]{1,0:T(8,128)(2,1)S(1)} fusion(bf16[16,64,1024]{2,1,0:T(8,128)(2,1)} %all-gather.6.cloned.1.call-done, pred[16,1024]{1,0:T(8,128)(4,1)S(1)} %iota_compare_fusion, bf16[64,1024]{1,0:T(8,128)(2,1)S(1)} %all-reduce.1), kind=kOutput, calls=%fused_computation.1 | convolution fusion | flops 2150629376 | bytes 4341760 | tf_op jit(solution)/shard_map/dot_general | solution.py:43
  118.4 29.4 %all_to_all.50 = bf16[8,128,1024]{2,1,0:T(8,128)(2,1)S(1)} all-to-all(bf16[8,128,1024]{2,1,0:T(8,128)(2,1)S(1)} %bitcast.27), channel_id=1, replica_groups=mesh['groups'=2,'outer'=4,'inner'=4] {'groups','inner'}, dimensions={0} | all-to-all | bytes 4194304 | tf_op jit(solution)/shard_map/all_to_all | solution.py:46
  147.8 1.5 copy.27
  (2 shorter events, 0.0 us)
Async XLA Ops:
  6.5 1.2 copy-start
  6.5 69.6 %all-gather.4.cloned.1.call-start = ((), (), s32[]{:S(2)}) async-start(), calls=%async_computation.4 | async-start | bytes 2621440 | tf_op jit(solution)/shard_map/all_gather | solution.py:23
  7.8 13.6 %copy-start.2 = (bf16[1,64,8192]{2,1,0:T(8,128)(2,1)S(1)}, bf16[1,64,8192]{2,1,0:T(8,128)(2,1)}, u32[]{:S(2)}) copy-start(bf16[1,64,8192]{2,1,0:T(8,128)(2,1)} %param.7) | copy-start | bytes 3145732
  21.4 93.0 %all-gather.6.cloned.1.call-start = ((), (), s32[]{:S(2)}) async-start(), calls=%async_computation.5 | async-start | bytes 2621440 | tf_op jit(solution)/shard_map/all_gather | solution.py:23
  22.3 15.5 %copy-start.1 = (bf16[128,8192]{1,0:T(8,128)(2,1)S(1)}, bf16[128,8192]{1,0:T(8,128)(2,1)}, u32[]{:S(2)}) copy-start(bf16[128,8192]{1,0:T(8,128)(2,1)} %param.5) | copy-start | bytes 6291460
  40.3 3.7 %copy-start.3 = (s32[128,1]{0,1:T(1,128)S(1)}, s32[128,1]{0,1:T(1,128)}, u32[]{:S(2)}) copy-start(s32[128,1]{0,1:T(1,128)} %param.4) | copy-start | bytes 1540
  40.3 33.3 %all-to-all-start.1 = ((bf16[128,8,1024]{0,2,1:T(8,128)(2,1)}), bf16[128,8,1024]{0,2,1:T(8,128)(2,1)S(1)}, u32[]{:S(2)}, u32[]{:S(2)}) async-start(bf16[128,8,1024]{0,2,1:T(8,128)(2,1)} %bitcast.24), calls=%async_computation.1 | async-start | bytes 4194304 | tf_op jit(solution)/shard_map/all_to_all | solution.py:33
Sparse Core Ops, SparseCore 0:
  21.5 46.6 all-gather.3
  69.7 44.6 all-gather.5

commit v2 on v1

--- a/solution.py
+++ b/solution.py
@@ -16,34 +16,57 @@
 
 
 def gathered(adapter):
-    inner = lax.axis_size("inner")
-    in_plane = lax.all_to_all(
+    inner, outer = lax.axis_size("inner"), lax.axis_size("outer")
+    block = lax.all_to_all(
         own_width_slices(adapter, inner), "inner", split_axis=0, concat_axis=0, tiled=True
     )
-    return lax.all_gather(in_plane, "outer", axis=0, tiled=True)
+    blocks = [block]
+    for _ in range(outer - 1):
+        block = lax.ppermute(block, "outer", [(i, (i + 1) % outer) for i in range(outer)])
+        blocks.append(block)
+    return jnp.concatenate(blocks, axis=0)
 
 
 def per_device(token_adapter_index, hidden, adapter_down_maps, adapter_up_maps):
-    tok_count = hidden.shape[0]
-    adapters = lax.axis_size("outer") * lax.axis_size("inner")
+    tok_count, width = hidden.shape
+    inner, outer = lax.axis_size("inner"), lax.axis_size("outer")
+    members = lax.axis_size("groups") * inner
+    share = width // members
+    adapters = outer * inner
     down = gathered(adapter_down_maps[0].T)
     up = gathered(adapter_up_maps[0])
-    rank, share = down.shape[1], down.shape[2]
-    ids = lax.all_gather(token_adapter_index[:, 0], PLANE, axis=0, tiled=True)
-    rows = lax.all_to_all(hidden, PLANE, split_axis=1, concat_axis=0, tiled=True)
-    named = ids[None, None, :] == jnp.arange(adapters, dtype=jnp.int32)[:, None, None]
+    rank = down.shape[1]
+
+    ids = token_adapter_index[:, 0].astype(jnp.bfloat16)
+    ids = jnp.pad(ids, (0, 8 * share - tok_count)).reshape(1, 8, share)
+    outgoing = hidden.reshape(tok_count, members, share).transpose(1, 0, 2)
+    outgoing = jnp.concatenate([outgoing, jnp.broadcast_to(ids, (members, 8, share))], axis=1)
+    arrived = lax.all_to_all(outgoing, PLANE, split_axis=0, concat_axis=0, tiled=True)
+    rows = arrived[:, :tok_count].reshape(members * tok_count, share)
+    ids = arrived[:, tok_count:].reshape(members, 8 * share)[:, :tok_count].reshape(-1).astype(jnp.int32)
+
+    steps_back = jnp.arange(outer, dtype=jnp.int32)
+    owners = (lax.axis_index("outer") - steps_back + outer) % outer
+    labels = (owners[:, None] * inner + jnp.arange(inner, dtype=jnp.int32)[None, :]).reshape(-1)
+    named = ids[None, None, :] == labels[:, None, None]
 
     partial = lax.dot_general(
         down.reshape(adapters * rank, share), rows, (((1,), (1,)), ((), ())), preferred_element_type=jnp.float32
     ).reshape(adapters, rank, rows.shape[0])
     partial = jnp.sum(jnp.where(named, partial, 0.0), axis=0)
-    shrunk = lax.psum(partial, PLANE).astype(jnp.bfloat16)
+    partial = partial.reshape(rank, members, tok_count).transpose(1, 0, 2)
+    terms = lax.all_to_all(partial, PLANE, split_axis=0, concat_axis=0, tiled=True)
+    own = jnp.sum(terms, axis=0).astype(jnp.bfloat16)
+    shrunk = lax.all_gather(own, PLANE, axis=0)
+    shrunk = shrunk.transpose(1, 0, 2).reshape(rank, members * tok_count)
 
     spread = jnp.where(named, shrunk[None], jnp.zeros((), jnp.bfloat16)).reshape(adapters * rank, rows.shape[0])
     delta = adapter_scale * lax.dot_general(
         spread, up.reshape(adapters * rank, share), (((0,), (0,)), ((), ())), preferred_element_type=jnp.float32
     )
-    return lax.all_to_all(delta.astype(jnp.bfloat16), PLANE, split_axis=0, concat_axis=1, tiled=True)
+    delta = delta.astype(jnp.bfloat16).reshape(members, tok_count, share)
+    returned = lax.all_to_all(delta, PLANE, split_axis=0, concat_axis=0, tiled=True)
+    return returned.transpose(1, 0, 2).reshape(tok_count, width)
 
 
 def solution(mesh):

time: 157 us -> 152 us (0.968)
  waiting for transfers between devices: 5.51 us -> 70.6 us
  blocking collectives: 112 us -> 47.6 us
  between operations: 13.5 us -> 0.19 us
  starting transfers between devices: 3.78 us -> 15.8 us
  local copies, waits for them, and re-layouts: 12.7 us -> 7.34 us
  other arithmetic: 0.01 us -> 1.86 us
    ppermute x0 -> x6, waiting for transfers between devices: none -> 57.9 us  [gathered(): lax.ppermute(block, 'outer', [(i, (i + 1) % outer) for i in range(outer)])]
    psum x1 -> x0, blocking collectives: 28 us -> none  [per_device(): shrunk = lax.psum(partial, PLANE).astype(jnp.bfloat16)]
    all_gather x1, blocking collectives: 29.5 us -> 9.21 us  [per_device(): shrunk = lax.all_gather(own, PLANE, axis=0)]
    all_to_all x3 -> x2, blocking collectives: 54.4 us -> 38.4 us  [the longest x1 28.5 us: per_device(): lax.all_to_all(delta, PLANE, split_axis=0, concat_axis=0, tiled=True)]
    all_to_all x1 -> x3, waiting for transfers between devices: 0.01 us -> 12.8 us  [the longest x2 12.8 us: gathered(): lax.all_to_all(own_width_slices(adapter, inner), 'inner', split_axis=0, c...]
    all_to_all x1 -> x3, starting transfers between devices: 3.74 us -> 12 us  [the longest x2 8.37 us: gathered(): lax.all_to_all(own_width_slices(adapter, inner), 'inner', split_axis=0, c...]
    all_gather x2 -> x0, waiting for transfers between devices: 5.47 us -> none  [gathered(): return lax.all_gather(in_plane, 'outer', axis=0, tiled=True)]
    all_to_all x2 -> x0, local copies, waits for them, and re-layouts: 4.09 us -> none  [the longest x1 2.6 us: per_device(): lax.all_to_all(hidden, PLANE, split_axis=1, concat_axis=0, tiled=True)]
  transfers between devices with their start and end apart: 3 -> 9, of which waited for: 1 -> 7; matrix products, arithmetic and copies ran while one was open for 9% -> 6% of each run, Pallas kernels for 0% -> 0%
where the time goes in v2:
time: 152 us; the launch traced here: 151 us
  waiting for transfers between devices  70.6 us (46%)
  blocking collectives  47.6 us (31%)
  starting transfers between devices  15.8 us (10%)
  matrix products  7.64 us (5%)
  local copies, waits for them, and re-layouts  7.34 us (5%)
  other arithmetic  1.86 us (1%)
    ppermute x6, waiting for transfers between devices, gathered(): lax.ppermute(block, 'outer', [(i, (i + 1) % outer) for i in range(outer)])  57.9 us
    all_to_all x1, blocking collectives, per_device(): lax.all_to_all(delta, PLANE, split_axis=0, concat_axis=0, tiled=True)  28.5 us
    all_to_all x2, waiting for transfers between devices, gathered(): lax.all_to_all(own_width_slices(adapter, inner), 'inner', split_axis=0, c...  12.8 us
    all_to_all x1, blocking collectives, per_device(): lax.all_to_all(partial, PLANE, split_axis=0, concat_axis=0, tiled=True)  9.85 us
    all_gather x1, blocking collectives, per_device(): shrunk = lax.all_gather(own, PLANE, axis=0)  9.21 us
    all_to_all x2, starting transfers between devices, gathered(): lax.all_to_all(own_width_slices(adapter, inner), 'inner', split_axis=0, c...  8.37 us
    dot_general x1, matrix products, per_device(): lax.dot_general(spread, up.reshape(adapters * rank, share), (((0,), (0,))...  3.9 us
    ppermute x6, starting transfers between devices, gathered(): lax.ppermute(block, 'outer', [(i, (i + 1) % outer) for i in range(outer)])  3.87 us
  transfers between devices with their start and end apart: 9, of which 7 were waited for; matrix products, arithmetic and copies ran while one was open for 6% of the time, Pallas kernels for 0%

profile of v2, /device:TPU:0, one launch (start us, length us, event | category | flops | bytes accessed | tf_op | source)
XLA Modules:
  0.0 151.1 jit_solution(14811654160845440141)
XLA Ops:
  0.0 1.2 copy-done
  1.3 0.8 copy.38
  2.1 4.2 %all-to-all-start.1 = ((bf16[4,64,1024]{2,1,0:T(8,128)(2,1)}), bf16[4,64,1024]{2,1,0:T(8,128)(2,1)S(1)}, u32[]{:S(2)}, u32[]{:S(2)}) async-start(bf16[4,64,1024]{2,1,0:T(8,128)(2,1)} %bitcast.50), calls=%async_computation.1 | async-start | bytes 1048576 | tf_op jit(solution)/shard_map/all_to_all | solution.py:20
  6.4 0.4 reshape.123
  6.8 1.0 copy.39
  7.7 7.5 %all-to-all-done.1 = bf16[4,64,1024]{2,1,0:T(8,128)(2,1)S(1)} async-done(((bf16[4,64,1024]{2,1,0:T(8,128)(2,1)}), bf16[4,64,1024]{2,1,0:T(8,128)(2,1)S(1)}, u32[]{:S(2)}, u32[]{:S(2)}) %all-to-all-start.1) | async-done | bytes 524320 | tf_op jit(solution)/shard_map/all_to_all | solution.py:20
  15.2 4.1 %all-to-all-start.3 = ((bf16[4,64,1024]{2,1,0:T(8,128)(2,1)}), bf16[4,64,1024]{2,1,0:T(8,128)(2,1)}, u32[]{:S(2)}, u32[]{:S(2)}) async-start(bf16[4,64,1024]{2,1,0:T(8,128)(2,1)} %bitcast.51), calls=%async_computation.3 | async-start | bytes 1048576 | tf_op jit(solution)/shard_map/all_to_all | solution.py:20
  19.3 0.0 copy-start.4
  19.3 1.8 %copy.37 = bf16[16,8,8,1024]{3,2,0,1:T(8,128)(2,1)S(1)} copy(bf16[16,8,8,1024]{3,2,1,0:T(8,128)(2,1)} %bitcast.55) | data formatting | bytes 4194304 | tf_op jit(solution)/shard_map/reshape | solution.py:42
  21.3 1.7 %pad_maximum_fusion = bf16[8,136,1024]{2,1,0:T(8,128)(2,1)} fusion(bf16[8,8,1024]{2,1,0:T(8,128)(2,1)S(1)} %broadcast_in_dim.43, bf16[8,128,1024]{2,1,0:T(8,128)(2,1)S(1)} %bitcast.53), kind=kLoop, calls=%fused_computation.3 | loop fusion | flops 4456448 | bytes 4456448 | tf_op jit(solution)/shard_map/concatenate | solution.py:43
  22.9 5.3 %all-to-all-done.3 = bf16[4,64,1024]{2,1,0:T(8,128)(2,1)} async-done(((bf16[4,64,1024]{2,1,0:T(8,128)(2,1)}), bf16[4,64,1024]{2,1,0:T(8,128)(2,1)}, u32[]{:S(2)}, u32[]{:S(2)}) %all-to-all-start.3) | async-done | bytes 524320 | tf_op jit(solution)/shard_map/all_to_all | solution.py:20
  28.2 3.6 %all-to-all-start = ((bf16[8,136,1024]{2,1,0:T(8,128)(2,1)}), bf16[8,136,1024]{2,1,0:T(8,128)(2,1)S(1)}, u32[]{:S(2)}, u32[]{:S(2)}) async-start(bf16[8,136,1024]{2,1,0:T(8,128)(2,1)} %pad_maximum_fusion), calls=%async_computation | async-start | bytes 4456448 | tf_op jit(solution)/shard_map/all_to_all | solution.py:44
  31.8 2.3 %collective-permute-start = (bf16[4,64,1024]{2,1,0:T(8,128)(2,1)}, bf16[4,64,1024]{2,1,0:T(8,128)(2,1)}, u32[]{:S(2)}, u32[]{:S(2)}) collective-permute-start(bf16[4,64,1024]{2,1,0:T(8,128)(2,1)} %copy-done.1), channel_id=1, source_target_pairs={{0,4},{4,8},{8,12},{12,0},{1,5},{5,9},{9,13},{13,1},{2,6},{6,10},{... | collective-permute-start | bytes 1572872 | tf_op jit(solution)/shard_map/ppermute | solution.py:25
  34.1 1.6 %collective-permute-start.3 = (bf16[4,64,1024]{2,1,0:T(8,128)(2,1)}, bf16[4,64,1024]{2,1,0:T(8,128)(2,1)}, u32[]{:S(2)}, u32[]{:S(2)}) collective-permute-start(bf16[4,64,1024]{2,1,0:T(8,128)(2,1)} %all-to-all-done.3), channel_id=1, source_target_pairs={{0,4},{4,8},{8,12},{12,0},{1,5},{5,9},{9,13},{13,1},{2,6},{6,10},{... | collective-permute-start | bytes 1572872 | tf_op jit(solution)/shard_map/ppermute | solution.py:25
  35.7 13.5 %collective-permute-done = bf16[4,64,1024]{2,1,0:T(8,128)(2,1)} collective-permute-done((bf16[4,64,1024]{2,1,0:T(8,128)(2,1)}, bf16[4,64,1024]{2,1,0:T(8,128)(2,1)}, u32[]{:S(2)}, u32[]{:S(2)}) %collective-permute-start) | collective-permute-done | bytes 524320 | tf_op jit(solution)/shard_map/ppermute | solution.py:25
  49.2 0.0 collective-permute-start.1
  49.2 11.2 %collective-permute-done.3 = bf16[4,64,1024]{2,1,0:T(8,128)(2,1)} collective-permute-done((bf16[4,64,1024]{2,1,0:T(8,128)(2,1)}, bf16[4,64,1024]{2,1,0:T(8,128)(2,1)}, u32[]{:S(2)}, u32[]{:S(2)}) %collective-permute-start.3) | collective-permute-done | bytes 524320 | tf_op jit(solution)/shard_map/ppermute | solution.py:25
  60.5 0.1 iota_add_fusion
  60.6 0.1 add.48
  60.7 11.1 %collective-permute-done.1 = bf16[4,64,1024]{2,1,0:T(8,128)(2,1)} collective-permute-done((bf16[4,64,1024]{2,1,0:T(8,128)(2,1)}, bf16[4,64,1024]{2,1,0:T(8,128)(2,1)}, u32[]{:S(2)}, u32[]{:S(2)}) %collective-permute-start.1) | collective-permute-done | bytes 524320 | tf_op jit(solution)/shard_map/ppermute | solution.py:25
  71.7 11.2 %collective-permute-done.4 = bf16[4,64,1024]{2,1,0:T(8,128)(2,1)} collective-permute-done((bf16[4,64,1024]{2,1,0:T(8,128)(2,1)}, bf16[4,64,1024]{2,1,0:T(8,128)(2,1)}, u32[]{:S(2)}, u32[]{:S(2)}) %collective-permute-start.4) | collective-permute-done | bytes 524320 | tf_op jit(solution)/shard_map/ppermute | solution.py:25
  83.0 0.1 copy.31
  83.1 0.2 slice.14
  83.3 0.1 broadcast_compare_fusion
  83.4 10.8 %collective-permute-done.2 = bf16[4,64,1024]{2,1,0:T(8,128)(2,1)} collective-permute-done((bf16[4,64,1024]{2,1,0:T(8,128)(2,1)}, bf16[4,64,1024]{2,1,0:T(8,128)(2,1)}, u32[]{:S(2)}, u32[]{:S(2)}) %collective-permute-start.2) | collective-permute-done | bytes 524320 | tf_op jit(solution)/shard_map/ppermute | solution.py:25
  94.2 3.7 %select_reduce_fusion = f32[64,1024]{1,0:T(8,128)S(1)} fusion(pred[16,1024]{1,0:T(8,128)(4,1)S(1)} %broadcast_compare_fusion, bf16[1024,1024,1]{1,0,2:T(8,128)(2,1)S(1)} %bitcast.56, bf16[4,64,1024]{2,1,0:T(8,128)(2,1)} %collective-permute-done.2, bf16[4,64,1024]{2,1,0:T(8,128)(2,1)} %collective-permute-done.1, ...), kind=kOutput, calls=%fused_computation.2 | convolution fusion | flops 2152660992 | bytes 4472832 | tf_op jit(solution)/shard_map/dot_general | solution.py:53
  98.0 0.1 copy.23
  98.1 9.9 %all_to_all.25 = f32[8,64,128]{2,1,0:T(8,128)S(1)} all-to-all(f32[8,64,128]{2,1,0:T(8,128)S(1)} %copy.23), channel_id=1, replica_groups=mesh['groups'=2,'outer'=4,'inner'=4] {'groups','inner'}, dimensions={0} | all-to-all | bytes 524288 | tf_op jit(solution)/shard_map/all_to_all | solution.py:58
  107.9 9.2 %all-gather = bf16[512,128]{1,0:T(8,128)(2,1)S(1)} all-gather(bf16[64,128]{1,0:T(8,128)(2,1)S(1)} %reduce_sum.19), channel_id=2, replica_groups=mesh['groups'=2,'outer'=4,'inner'=4] {'groups','inner'}, dimensions={0}, use_global_device_ids=true | all-gather | bytes 147456 | tf_op jit(solution)/shard_map/all_gather | solution.py:60
  117.2 3.9 %fusion = bf16[1024,1024]{1,0:T(8,128)(2,1)S(1)} fusion(bf16[4,64,1024]{2,1,0:T(8,128)(2,1)} %collective-permute-done.5, bf16[4,64,1024]{2,1,0:T(8,128)(2,1)} %collective-permute-done.4, bf16[4,64,1024]{2,1,0:T(8,128)(2,1)} %collective-permute-done.3, bf16[4,64,1024]{2,1,0:T(8,128)(2,1)} %all-to-all-done.3, pred[16,1024]{1,0:T(8,128)(4,1)S(1)} %broadcast_compare_fusion, ...), kind=kOutput, calls=%fused_computation.1 | convolution fusion | flops 2153775104 | bytes 4341760 | tf_op jit(solution)/shard_map/dot_general | solution.py:64
  121.1 28.5 %all_to_all.26 = bf16[8,128,1024]{2,1,0:T(8,128)(2,1)S(1)} all-to-all(bf16[8,128,1024]{2,1,0:T(8,128)(2,1)S(1)} %bitcast.57), channel_id=1, replica_groups=mesh['groups'=2,'outer'=4,'inner'=4] {'groups','inner'}, dimensions={0} | all-to-all | bytes 4194304 | tf_op jit(solution)/shard_map/all_to_all | solution.py:68
  149.6 1.5 copy.30
  (25 shorter events, 0.3 us)
Async XLA Ops:
  0.0 1.2 copy-start
  0.0 6.3 %copy-start.3 = (bf16[1,64,8192]{2,1,0:T(8,128)(2,1)S(1)}, bf16[1,64,8192]{2,1,0:T(8,128)(2,1)}, u32[]{:S(2)}) copy-start(bf16[1,64,8192]{2,1,0:T(8,128)(2,1)} %param.7) | copy-start | bytes 3145732
  2.1 13.1 %all-to-all-start.1 = ((bf16[4,64,1024]{2,1,0:T(8,128)(2,1)}), bf16[4,64,1024]{2,1,0:T(8,128)(2,1)S(1)}, u32[]{:S(2)}, u32[]{:S(2)}) async-start(bf16[4,64,1024]{2,1,0:T(8,128)(2,1)} %bitcast.50), calls=%async_computation.1 | async-start | bytes 1048576 | tf_op jit(solution)/shard_map/all_to_all | solution.py:20
  15.2 4.1 %copy-start.1 = (bf16[4,64,1024]{2,1,0:T(8,128)(2,1)}, bf16[4,64,1024]{2,1,0:T(8,128)(2,1)S(1)}, u32[]{:S(2)}) copy-start(bf16[4,64,1024]{2,1,0:T(8,128)(2,1)S(1)} %all-to-all-done.1) | copy-start | bytes 1572868
  15.2 13.0 %all-to-all-start.3 = ((bf16[4,64,1024]{2,1,0:T(8,128)(2,1)}), bf16[4,64,1024]{2,1,0:T(8,128)(2,1)}, u32[]{:S(2)}, u32[]{:S(2)}) async-start(bf16[4,64,1024]{2,1,0:T(8,128)(2,1)} %bitcast.51), calls=%async_computation.3 | async-start | bytes 1048576 | tf_op jit(solution)/shard_map/all_to_all | solution.py:20
  19.3 1.9 %copy-start.4 = (s32[128,1]{0,1:T(1,128)S(1)}, s32[128,1]{0,1:T(1,128)}, u32[]{:S(2)}) copy-start(s32[128,1]{0,1:T(1,128)} %param.4) | copy-start | bytes 1540
  28.2 54.7 %all-to-all-start = ((bf16[8,136,1024]{2,1,0:T(8,128)(2,1)}), bf16[8,136,1024]{2,1,0:T(8,128)(2,1)S(1)}, u32[]{:S(2)}, u32[]{:S(2)}) async-start(bf16[8,136,1024]{2,1,0:T(8,128)(2,1)} %pad_maximum_fusion), calls=%async_computation | async-start | bytes 4456448 | tf_op jit(solution)/shard_map/all_to_all | solution.py:44
  31.8 17.4 %collective-permute-start = (bf16[4,64,1024]{2,1,0:T(8,128)(2,1)}, bf16[4,64,1024]{2,1,0:T(8,128)(2,1)}, u32[]{:S(2)}, u32[]{:S(2)}) collective-permute-start(bf16[4,64,1024]{2,1,0:T(8,128)(2,1)} %copy-done.1), channel_id=1, source_target_pairs={{0,4},{4,8},{8,12},{12,0},{1,5},{5,9},{9,13},{13,1},{2,6},{6,10},{... | collective-permute-start | bytes 1572872 | tf_op jit(solution)/shard_map/ppermute | solution.py:25
  34.1 26.4 %collective-permute-start.3 = (bf16[4,64,1024]{2,1,0:T(8,128)(2,1)}, bf16[4,64,1024]{2,1,0:T(8,128)(2,1)}, u32[]{:S(2)}, u32[]{:S(2)}) collective-permute-start(bf16[4,64,1024]{2,1,0:T(8,128)(2,1)} %all-to-all-done.3), channel_id=1, source_target_pairs={{0,4},{4,8},{8,12},{12,0},{1,5},{5,9},{9,13},{13,1},{2,6},{6,10},{... | collective-permute-start | bytes 1572872 | tf_op jit(solution)/shard_map/ppermute | solution.py:25
  49.2 22.5 %collective-permute-start.1 = (bf16[4,64,1024]{2,1,0:T(8,128)(2,1)}, bf16[4,64,1024]{2,1,0:T(8,128)(2,1)}, u32[]{:S(2)}, u32[]{:S(2)}) collective-permute-start(bf16[4,64,1024]{2,1,0:T(8,128)(2,1)} %collective-permute-done), channel_id=1, source_target_pairs={{0,4},{4,8},{8,12},{12,0},{1,5},{5,9},{9,13},{13,1},{2,6},{6,10},{... | collective-permute-start | bytes 1572872 | tf_op jit(solution)/shard_map/ppermute | solution.py:25
  60.5 22.5 %collective-permute-start.4 = (bf16[4,64,1024]{2,1,0:T(8,128)(2,1)}, bf16[4,64,1024]{2,1,0:T(8,128)(2,1)}, u32[]{:S(2)}, u32[]{:S(2)}) collective-permute-start(bf16[4,64,1024]{2,1,0:T(8,128)(2,1)} %collective-permute-done.3), channel_id=1, source_target_pairs={{0,4},{4,8},{8,12},{12,0},{1,5},{5,9},{9,13},{13,1},{2,6},{6,10},{... | collective-permute-start | bytes 1572872 | tf_op jit(solution)/shard_map/ppermute | solution.py:25
  71.7 22.5 %collective-permute-start.2 = (bf16[4,64,1024]{2,1,0:T(8,128)(2,1)}, bf16[4,64,1024]{2,1,0:T(8,128)(2,1)}, u32[]{:S(2)}, u32[]{:S(2)}) collective-permute-start(bf16[4,64,1024]{2,1,0:T(8,128)(2,1)} %collective-permute-done.1), channel_id=1, source_target_pairs={{0,4},{4,8},{8,12},{12,0},{1,5},{5,9},{9,13},{13,1},{2,6},{6,10},{... | collective-permute-start | bytes 1572872 | tf_op jit(solution)/shard_map/ppermute | solution.py:25
  83.0 34.2 %collective-permute-start.5 = (bf16[4,64,1024]{2,1,0:T(8,128)(2,1)}, bf16[4,64,1024]{2,1,0:T(8,128)(2,1)}, u32[]{:S(2)}, u32[]{:S(2)}) collective-permute-start(bf16[4,64,1024]{2,1,0:T(8,128)(2,1)} %collective-permute-done.4), channel_id=1, source_target_pairs={{0,4},{4,8},{8,12},{12,0},{1,5},{5,9},{9,13},{13,1},{2,6},{6,10},{... | collective-permute-start | bytes 1572872 | tf_op jit(solution)/shard_map/ppermute | solution.py:25
  83.1 11.1 %copy-start.2 = (bf16[4,64,1024]{2,1,0:T(8,128)(2,1)S(1)}, bf16[4,64,1024]{2,1,0:T(8,128)(2,1)}, u32[]{:S(2)}) copy-start(bf16[4,64,1024]{2,1,0:T(8,128)(2,1)} %copy-done.1) | copy-start | bytes 1572868

commit v3 on v1

v3 whole, which is shorter than its diff:
```python
import functools

import jax
import jax.numpy as jnp
from jax import lax
from jax.experimental import pallas as pl
from jax.experimental.pallas import tpu as pltpu
from jax.sharding import Mesh
from jax.sharding import PartitionSpec as P

adapter_scale = 2.0
PLANE = ("groups", "inner")
VMEM_BYTES = 32 << 20


def to_partner(value, axes, size, offset):
    return lax.ppermute(value, axes, [(i, i ^ offset) for i in range(size)])


def ring(block, outer):
    blocks = [block]
    for _ in range(outer - 1):
        block = lax.ppermute(block, "outer", [(i, (i + 1) % outer) for i in range(outer)])
        blocks.append(block)
    return blocks


def load_all(sources, target, sems):
    copies, at = [], 0
    for n, source in enumerate(sources):
        rows = source.shape[0]
        copies.append(pltpu.make_async_copy(source, target.at[pl.ds(at, rows)], sems.at[n]))
        at += rows
    for copy in copies:
        copy.start()
    return copies


def down_kernel(counts, tok, rank, labels_ref, ids_ref, *refs):
    map_count, members = counts
    maps, rows = refs[:map_count], refs[map_count : map_count + members]
    outs = refs[map_count + members : map_count + 2 * members]
    map_buf, row_buf, sums, sems = refs[map_count + 2 * members :]
    copies = load_all(list(maps), map_buf, sems)
    copies += load_all(list(rows), row_buf, sems.at[pl.ds(map_count, members)])
    for copy in copies:
        copy.wait()
    adapters = map_buf.shape[0] // rank
    batch = min(4, adapters)

    def one(member, _):
        tokens = row_buf[pl.ds(pl.multiple_of(member * tok, tok), tok), :]
        ids = ids_ref[pl.ds(member, 1), :]
        total = jnp.zeros((rank, tok), jnp.float32)
        for first in range(0, adapters, batch):
            product = lax.dot_general(
                map_buf[first * rank : (first + batch) * rank, :],
                tokens,
                (((1,), (1,)), ((), ())),
                preferred_element_type=jnp.float32,
            )
            for n in range(batch):
                named = ids == labels_ref[first + n]
                total += jnp.where(named, product[n * rank : (n + 1) * rank, :], 0.0)
        sums[member] = total
        return 0

    lax.fori_loop(0, members, one, 0)
    for member in range(members):
        outs[member][...] = sums[member]


def down_product(labels, ids, maps, rows, rank):
    tok, share = rows[0].shape
    map_rows = sum(m.shape[0] for m in maps)
    anywhere = pl.BlockSpec(memory_space=pl.ANY)
    in_vmem = pl.BlockSpec(memory_space=pltpu.VMEM)
    return pl.pallas_call(
        functools.partial(down_kernel, (len(maps), len(rows)), tok, rank),
        out_shape=[jax.ShapeDtypeStruct((rank, tok), jnp.float32)] * len(rows),
        in_specs=[pl.BlockSpec(memory_space=pltpu.SMEM), in_vmem] + [anywhere] * (len(maps) + len(rows)),
        out_specs=[in_vmem] * len(rows),
        scratch_shapes=[
            pltpu.VMEM((map_rows, share), jnp.bfloat16),
            pltpu.VMEM((len(rows) * tok, share), jnp.bfloat16),
            pltpu.VMEM((len(rows), rank, tok), jnp.float32),
            pltpu.SemaphoreType.DMA((len(maps) + len(rows),)),
        ],
        compiler_params=pltpu.CompilerParams(vmem_limit_bytes=VMEM_BYTES),
        cost_estimate=pl.CostEstimate(
            flops=2 * map_rows * len(rows) * tok * share,
            bytes_accessed=2 * share * (map_rows + len(rows) * tok),
            transcendentals=0,
        ),
        name="down_product",
    )(labels, ids, *maps, *rows)


def up_kernel(counts, tok, rank, labels_ref, ids_ref, *refs):
    map_count, members = counts
    maps, rows = refs[:map_count], refs[map_count : map_count + members]
    outs = refs[map_count + members : map_count + 2 * members]
    map_buf, row_buf, results, sems = refs[map_count + 2 * members :]
    copies = load_all(list(maps), map_buf, sems)
    for member in range(members):
        row_buf[member] = rows[member][...]
    for copy in copies:
        copy.wait()
    adapters = map_buf.shape[0] // rank
    per_tile = max(1, 128 // rank)
    lane = lax.broadcasted_iota(jnp.int32, (tok, per_tile * rank), 1)

    def one(member, _):
        shrunk = row_buf[member].astype(jnp.float32).T
        shrunk = jnp.concatenate([shrunk] * per_tile, axis=1)
        ids = jnp.broadcast_to(ids_ref[pl.ds(member, 1), :], (per_tile * rank, tok)).T
        pieces = []
        for first in range(0, adapters, per_tile):
            label = jnp.full(lane.shape, labels_ref[first], jnp.int32)
            for n in range(1, per_tile):
                label = jnp.where(lane >= n * rank, labels_ref[first + n], label)
            pieces.append(jnp.where(ids == label, shrunk, 0.0).astype(jnp.bfloat16))
        spread = jnp.concatenate(pieces, axis=1)
        product = jnp.dot(spread, map_buf[...], preferred_element_type=jnp.float32)
        results[member] = (adapter_scale * product).astype(jnp.bfloat16)
        return 0

    lax.fori_loop(0, members, one, 0)
    for member in range(members):
        outs[member][...] = results[member]


def up_product(labels, ids, maps, rows):
    rank, tok = rows[0].shape
    map_rows, piece = sum(m.shape[0] for m in maps), maps[0].shape[1]
    anywhere = pl.BlockSpec(memory_space=pl.ANY)
    in_vmem = pl.BlockSpec(memory_space=pltpu.VMEM)
    return pl.pallas_call(
        functools.partial(up_kernel, (len(maps), len(rows)), tok, rank),
        out_shape=[jax.ShapeDtypeStruct((tok, piece), jnp.bfloat16)] * len(rows),
        in_specs=[pl.BlockSpec(memory_space=pltpu.SMEM), in_vmem] + [anywhere] * len(maps) + [in_vmem] * len(rows),
        out_specs=[in_vmem] * len(rows),
        scratch_shapes=[
            pltpu.VMEM((map_rows, piece), jnp.bfloat16),
            pltpu.VMEM((len(rows), rank, tok), jnp.bfloat16),
            pltpu.VMEM((len(rows), tok, piece), jnp.bfloat16),
            pltpu.SemaphoreType.DMA((len(maps),)),
        ],
        compiler_params=pltpu.CompilerParams(vmem_limit_bytes=VMEM_BYTES),
        cost_estimate=pl.CostEstimate(
            flops=2 * map_rows * len(rows) * tok * piece,
            bytes_accessed=2 * piece * (map_rows + len(rows) * tok),
            transcendentals=0,
        ),
        name="up_product",
    )(labels, ids, *maps, *rows)


def place_kernel(members, pieces, me_ref, *refs):
    blocks, out_ref, sems = refs[: members * pieces], refs[-2], refs[-1]
    piece = blocks[0].shape[1]
    copies = []
    for n in range(members * pieces):
        offset, part = n % members, n // members
        at = (me_ref[0] ^ offset) * (pieces * piece) + part * piece
        target = out_ref.at[:, pl.ds(pl.multiple_of(at, 128), piece)]
        copies.append(pltpu.make_async_copy(blocks[n], target, sems.at[n]))
    for copy in copies:
        copy.start()
    for copy in copies:
        copy.wait()


def place(me, results):
    members, pieces = len(results[0]), len(results)
    tok, piece = results[0][0].shape
    anywhere = pl.BlockSpec(memory_space=pl.ANY)
    return pl.pallas_call(
        functools.partial(place_kernel, members, pieces),
        out_shape=jax.ShapeDtypeStruct((tok, members * pieces * piece), jnp.bfloat16),
        in_specs=[pl.BlockSpec(memory_space=pltpu.SMEM)] + [anywhere] * (members * pieces),
        out_specs=anywhere,
        scratch_shapes=[pltpu.SemaphoreType.DMA((members * pieces,))],
        compiler_params=pltpu.CompilerParams(vmem_limit_bytes=VMEM_BYTES),
        name="place_results",
    )(me, *[block for part in results for block in part])


def per_device(token_adapter_index, hidden, adapter_down_maps, adapter_up_maps):
    tok, width = hidden.shape
    groups, inner, outer = lax.axis_size("groups"), lax.axis_size("inner"), lax.axis_size("outer")
    members = groups * inner
    share = width // members
    rank = adapter_up_maps.shape[1]
    pieces = max(1, min(4, share // 256))
    piece = share // pieces
    per_ring = max(1, inner // 4)
    group, place_in_group, level = lax.axis_index("groups"), lax.axis_index("inner"), lax.axis_index("outer")
    me = group * inner + place_in_group

    def columns(array, offset):
        return lax.dynamic_slice_in_dim(array, (me ^ offset) * share, share, axis=1)

    def exchanged(array):
        blocks = [columns(array, 0)]
        for offset in range(1, inner):
            blocks.append(to_partner(columns(array, offset), "inner", inner, offset))
        return blocks

    blocks = exchanged(adapter_down_maps[0].T)
    rings = []
    for first in range(0, inner, per_ring):
        some = blocks[first : first + per_ring]
        rings.append(ring(some[0] if per_ring == 1 else jnp.concatenate(some, axis=0), outer))
    down_maps = [r[k] for k in range(outer) for r in rings]

    rows = [columns(hidden, 0)]
    for offset in range(1, members):
        rows.append(to_partner(columns(hidden, offset), PLANE, members, offset))
    ids = token_adapter_index[:, 0].reshape(1, tok)
    bit = 1
    while bit < members:
        ids = jnp.concatenate([ids, to_partner(ids, PLANE, members, bit)], axis=0)
        bit *= 2

    steps_back = jnp.arange(outer, dtype=jnp.int32)[:, None]
    labels = ((level - steps_back + outer) % outer) * inner + (
        place_in_group ^ jnp.arange(inner, dtype=jnp.int32)[None, :]
    )
    labels = labels.reshape(-1)

    partial = down_product(labels, ids, down_maps, rows, rank)
    total = partial[0]
    for offset in range(1, members):
        total = total + to_partner(partial[offset], PLANE, members, offset)
    own = total.astype(jnp.bfloat16)
    shrunk = [own] + [to_partner(own, PLANE, members, offset) for offset in range(1, members)]

    up_blocks = exchanged(adapter_up_maps[0])
    results = []
    for part in range(pieces):
        block = jnp.concatenate([b[:, part * piece : (part + 1) * piece] for b in up_blocks], axis=0)
        delta = up_product(labels, ids, ring(block, outer), shrunk)
        results.append(
            [delta[0]] + [to_partner(delta[offset], PLANE, members, offset) for offset in range(1, members)]
        )
    return place(me.reshape(1), results)


def solution(mesh):
    groups, wide = mesh.shape["groups"], mesh.shape["wide"]
    outer = 1 << ((wide.bit_length() - 1) // 2)
    fine = Mesh(mesh.devices.reshape(groups, outer, wide // outer), ("groups", "outer", "inner"))
    owner = ("outer", "inner")
    rows = P(("groups",) + owner, None)
    return jax.shard_map(
        per_device,
        mesh=fine,
        in_specs=(rows, rows, P(owner, None, None), P(owner, None, None)),
        out_specs=rows,
        check_vma=False,
    )
```

time: 157 us -> 179 us (1.14)
  blocking collectives: 112 us -> 0 us
  waiting for transfers between devices: 5.51 us -> 73.7 us
  starting transfers between devices: 3.78 us -> 71 us
  Pallas kernels: 0 us -> 29.2 us
  between operations: 13.5 us -> 0.31 us
  local copies, waits for them, and re-layouts: 12.7 us -> 3.38 us
  matrix products: 8.74 us -> 0 us
    ppermute x0 -> x82, waiting for transfers between devices: none -> 73.7 us  [the longest x24 39.3 us: ring(): lax.ppermute(block, 'outer', [(i, (i + 1) % outer) for i in range(outer)])]
    ppermute x0 -> x82, starting transfers between devices: none -> 71 us  [the longest x58 56 us: to_partner(): return lax.ppermute(value, axes, [(i, i ^ offset) for i in range(size)])]
    all_to_all x3 -> x0, blocking collectives: 54.4 us -> none  [the longest x1 29.4 us: per_device(): lax.all_to_all(delta.astype(jnp.bfloat16), PLANE, split_axis=0, concat_ax...]
    all_gather x1 -> x0, blocking collectives: 29.5 us -> none  [per_device(): ids = lax.all_gather(token_adapter_index[:, 0], PLANE, axis=0, tiled=True)]
    pallas_call x0 -> x6, Pallas kernels: none -> 29.2 us  [the longest x4 18.1 us: up_product(): pl.pallas_call(functools.partial(up_kernel, (len(maps), len(rows)), tok,...]
    psum x1 -> x0, blocking collectives: 28 us -> none  [per_device(): shrunk = lax.psum(partial, PLANE).astype(jnp.bfloat16)]
    dot_general x2 -> x0, matrix products: 8.74 us -> none  [the longest x1 4.78 us: per_device(): lax.dot_general(down.reshape(adapters * rank, share), rows, (((1,), (1,))...]
    all_gather x2 -> x0, waiting for transfers between devices: 5.47 us -> none  [gathered(): return lax.all_gather(in_plane, 'outer', axis=0, tiled=True)]
  transfers between devices with their start and end apart: 3 -> 82, of which waited for: 1 -> 32; matrix products, arithmetic and copies ran while one was open for 9% -> 2% of each run, Pallas kernels for 0% -> 15%
where the time goes in v3:
time: 179 us
  waiting for transfers between devices  73.7 us (41%)
  starting transfers between devices  71 us (40%)
  Pallas kernels  29.2 us (16%)
  local copies, waits for them, and re-layouts  3.38 us (2%)
    ppermute x58, starting transfers between devices, to_partner(): return lax.ppermute(value, axes, [(i, i ^ offset) for i in range(size)])  56 us
    ppermute x24, waiting for transfers between devices, ring(): lax.ppermute(block, 'outer', [(i, (i + 1) % outer) for i in range(outer)])  39.3 us
    ppermute x58, waiting for transfers between devices, to_partner(): return lax.ppermute(value, axes, [(i, i ^ offset) for i in range(size)])  34.4 us
    pallas_call x4, Pallas kernels, up_product(): pl.pallas_call(functools.partial(up_kernel, (len(maps), len(rows)), tok,...  18.1 us
    ppermute x24, starting transfers between devices, ring(): lax.ppermute(block, 'outer', [(i, (i + 1) % outer) for i in range(outer)])  15 us
    pallas_call x1, Pallas kernels, down_product(): pl.pallas_call(functools.partial(down_kernel, (len(maps), len(rows)), tok...  9.48 us
  transfers between devices with their start and end apart: 82, of which 32 were waited for; matrix products, arithmetic and copies ran while one was open for 2% of the time, Pallas kernels for 15%

profile of v3, /device:TPU:0, one launch (start us, length us, event | category | flops | bytes accessed | tf_op | source)
XLA Modules:
  0.0 179.0 jit_solution(11763353890825538368)
XLA Ops:
  1.8 2.6 %collective-permute-start.10 = (bf16[64,1024]{1,0:T(8,128)(2,1)S(1)}, bf16[64,1024]{1,0:T(8,128)(2,1)S(1)}, u32[]{:S(2)}, u32[]{:S(2)}) collective-permute-start(bf16[64,1024]{1,0:T(8,128)(2,1)S(1)} %get-tuple-element.96), channel_id=1, source_target_pairs={{0,2},{1,3},{2,0},{3,1},{4,6},{5,7},{6,4},{7,5},{8,10},{9,11},{10,... | collective-permute-start | bytes 393224 | tf_op jit(solution)/shard_map/ppermute | solution.py:17
  4.5 1.8 collective-permute-start.12
  9.7 2.0 %collective-permute-done.1 = s32[2,128]{1,0:T(2,128)S(1)} collective-permute-done((s32[2,128]{1,0:T(2,128)S(1)}, s32[2,128]{1,0:T(2,128)S(1)}, u32[]{:S(2)}, u32[]{:S(2)}) %collective-permute-start.1) | collective-permute-done | bytes 1056 | tf_op jit(solution)/shard_map/ppermute | solution.py:17
  14.0 2.3 %collective-permute-done.2 = s32[4,128]{1,0:T(4,128)} collective-permute-done((s32[4,128]{1,0:T(4,128)}, s32[4,128]{1,0:T(4,128)}, u32[]{:S(2)}, u32[]{:S(2)}) %collective-permute-start.2) | collective-permute-done | bytes 2080 | tf_op jit(solution)/shard_map/ppermute | solution.py:17
  20.4 2.2 %collective-permute-done.4 = bf16[64,1024]{1,0:T(8,128)(2,1)S(1)} collective-permute-done((bf16[64,1024]{1,0:T(8,128)(2,1)S(1)}, bf16[64,1024]{1,0:T(8,128)(2,1)S(1)}, u32[]{:S(2)}, u32[]{:S(2)}) %collective-permute-start.4) | collective-permute-done | bytes 131104 | tf_op jit(solution)/shard_map/ppermute | solution.py:17
  24.6 1.7 collective-permute-start.28
  27.9 3.1 %collective-permute-done.25.refs_18_ = bf16[128,1024]{1,0:T(8,128)(2,1)S(1)} collective-permute-done((bf16[128,1024]{1,0:T(8,128)(2,1)S(1)}, bf16[128,1024]{1,0:T(8,128)(2,1)S(1)}, u32[]{:S(2)}, u32[]{:S(2)}) %collective-permute-start.25) | collective-permute-done | bytes 262176 | tf_op jit(solution)/shard_map/ppermute | solution.py:17
  32.4 14.1 %collective-permute-done.26.refs_19_ = bf16[128,1024]{1,0:T(8,128)(2,1)S(1)} collective-permute-done((bf16[128,1024]{1,0:T(8,128)(2,1)S(1)}, bf16[128,1024]{1,0:T(8,128)(2,1)S(1)}, u32[]{:S(2)}, u32[]{:S(2)}) %collective-permute-start.26) | collective-permute-done | bytes 262176 | tf_op jit(solution)/shard_map/ppermute | solution.py:17
  54.8 2.5 %collective-permute-done.14.refs_6_ = bf16[64,1024]{1,0:T(8,128)(2,1)S(1)} collective-permute-done((bf16[64,1024]{1,0:T(8,128)(2,1)S(1)}, bf16[64,1024]{1,0:T(8,128)(2,1)S(1)}, u32[]{:S(2)}, u32[]{:S(2)}) %collective-permute-start.14) | collective-permute-done | bytes 131104 | tf_op jit(solution)/shard_map/ppermute | solution.py:23
  57.3 2.8 %collective-permute-done.15.refs_7_ = bf16[64,1024]{1,0:T(8,128)(2,1)S(1)} collective-permute-done((bf16[64,1024]{1,0:T(8,128)(2,1)S(1)}, bf16[64,1024]{1,0:T(8,128)(2,1)S(1)}, u32[]{:S(2)}, u32[]{:S(2)}) %collective-permute-start.15) | collective-permute-done | bytes 131104 | tf_op jit(solution)/shard_map/ppermute | solution.py:23
  60.7 4.9 %collective-permute-done.16.refs_8_ = bf16[64,1024]{1,0:T(8,128)(2,1)S(1)} collective-permute-done((bf16[64,1024]{1,0:T(8,128)(2,1)S(1)}, bf16[64,1024]{1,0:T(8,128)(2,1)S(1)}, u32[]{:S(2)}, u32[]{:S(2)}) %collective-permute-start.16) | collective-permute-done | bytes 131104 | tf_op jit(solution)/shard_map/ppermute | solution.py:23
  68.5 2.8 %collective-permute-done.18.refs_10_ = bf16[64,1024]{1,0:T(8,128)(2,1)S(1)} collective-permute-done((bf16[64,1024]{1,0:T(8,128)(2,1)S(1)}, bf16[64,1024]{1,0:T(8,128)(2,1)S(1)}, u32[]{:S(2)}, u32[]{:S(2)}) %collective-permute-start.18) | collective-permute-done | bytes 131104 | tf_op jit(solution)/shard_map/ppermute | solution.py:23
  71.3 2.8 %collective-permute-done.19.refs_11_ = bf16[64,1024]{1,0:T(8,128)(2,1)S(1)} collective-permute-done((bf16[64,1024]{1,0:T(8,128)(2,1)S(1)}, bf16[64,1024]{1,0:T(8,128)(2,1)S(1)}, u32[]{:S(2)}, u32[]{:S(2)}) %collective-permute-start.19) | collective-permute-done | bytes 131104 | tf_op jit(solution)/shard_map/ppermute | solution.py:23
  74.2 2.8 %collective-permute-done.62.refs_1_ = bf16[256,256]{1,0:T(8,128)(2,1)S(1)} collective-permute-done((bf16[256,256]{1,0:T(8,128)(2,1)S(1)}, bf16[256,256]{1,0:T(8,128)(2,1)S(1)}, u32[]{:S(2)}, u32[]{:S(2)}) %collective-permute-start.62) | collective-permute-done | bytes 131104 | tf_op jit(solution)/shard_map/ppermute | solution.py:23
  76.9 2.8 %collective-permute-done.20.refs_12_ = bf16[64,1024]{1,0:T(8,128)(2,1)S(1)} collective-permute-done((bf16[64,1024]{1,0:T(8,128)(2,1)S(1)}, bf16[64,1024]{1,0:T(8,128)(2,1)S(1)}, u32[]{:S(2)}, u32[]{:S(2)}) %collective-permute-start.20) | collective-permute-done | bytes 131104 | tf_op jit(solution)/shard_map/ppermute | solution.py:23
  79.7 2.8 %collective-permute-done.21.refs_13_ = bf16[64,1024]{1,0:T(8,128)(2,1)S(1)} collective-permute-done((bf16[64,1024]{1,0:T(8,128)(2,1)S(1)}, bf16[64,1024]{1,0:T(8,128)(2,1)S(1)}, u32[]{:S(2)}, u32[]{:S(2)}) %collective-permute-start.21) | collective-permute-done | bytes 131104 | tf_op jit(solution)/shard_map/ppermute | solution.py:23
  82.5 2.8 %collective-permute-done.22.refs_14_ = bf16[64,1024]{1,0:T(8,128)(2,1)S(1)} collective-permute-done((bf16[64,1024]{1,0:T(8,128)(2,1)S(1)}, bf16[64,1024]{1,0:T(8,128)(2,1)S(1)}, u32[]{:S(2)}, u32[]{:S(2)}) %collective-permute-start.22) | collective-permute-done | bytes 131104 | tf_op jit(solution)/shard_map/ppermute | solution.py:23
  85.4 2.8 %collective-permute-done.23.refs_15_ = bf16[64,1024]{1,0:T(8,128)(2,1)S(1)} collective-permute-done((bf16[64,1024]{1,0:T(8,128)(2,1)S(1)}, bf16[64,1024]{1,0:T(8,128)(2,1)S(1)}, u32[]{:S(2)}, u32[]{:S(2)}) %collective-permute-start.23) | collective-permute-done | bytes 131104 | tf_op jit(solution)/shard_map/ppermute | solution.py:23
  88.2 9.5 %down_product.1 = (f32[64,128]{1,0:T(8,128)S(1)}, f32[64,128]{1,0:T(8,128)S(1)}, f32[64,128]{1,0:T(8,128)S(1)}, f32[64,128]{1,0:T(8,128)S(1)}, f32[64,128]{1,0:T...) custom-call(s32[16]{0:T(128)S(1)} %add.98.labels_ref, ...), custom_call_target="tpu_custom_call" | custom-call | flops 2147483648 | bytes 4194304 | tf_op jit(solution)/shard_map/down_product/pallas_call | solution.py:78
  97.7 2.3 %collective-permute-start.32 = (f32[64,128]{1,0:T(8,128)S(1)}, f32[64,128]{1,0:T(8,128)S(1)}, u32[]{:S(2)}, u32[]{:S(2)}) collective-permute-start(f32[64,128]{1,0:T(8,128)S(1)} %get-tuple-element.47), channel_id=1, source_target_pairs={{0,2},{1,3},{2,0},{3,1},{16,18},{17,19},{18,16},{19,17},{4,6},{5,7... | collective-permute-start | bytes 98312 | tf_op jit(solution)/shard_map/ppermute | solution.py:17
  101.7 2.8 %collective-permute-start.36 = (f32[64,128]{1,0:T(8,128)S(1)}, f32[64,128]{1,0:T(8,128)S(1)}, u32[]{:S(2)}, u32[]{:S(2)}) collective-permute-start(f32[64,128]{1,0:T(8,128)S(1)} %get-tuple-element.51), channel_id=1, source_target_pairs={{0,18},{1,19},{2,16},{3,17},{16,2},{17,3},{18,0},{19,1},{4,22},{5,... | collective-permute-start | bytes 98312 | tf_op jit(solution)/shard_map/ppermute | solution.py:17
  107.4 2.2 %collective-permute-start.64 = (bf16[256,256]{1,0:T(8,128)(2,1)S(1)}, bf16[256,256]{1,0:T(8,128)(2,1)S(1)}, u32[]{:S(2)}, u32[]{:S(2)}) collective-permute-start(bf16[256,256]{1,0:T(8,128)(2,1)S(1)} %collective-permute-done.63.refs_2_), channel_id=1, source_target_pairs={{0,4},{4,8},{8,12},{12,0},{1,5},{5,9},{9,13},{13,1},{2,6},{6,10},{... | collective-permute-start | bytes 393224 | tf_op jit(solution)/shard_map/ppermute | solution.py:23
  109.7 3.0 %collective-permute-done.53.refs_2_ = bf16[256,256]{1,0:T(8,128)(2,1)S(1)} collective-permute-done((bf16[256,256]{1,0:T(8,128)(2,1)S(1)}, bf16[256,256]{1,0:T(8,128)(2,1)S(1)}, u32[]{:S(2)}, u32[]{:S(2)}) %collective-permute-start.53) | collective-permute-done | bytes 131104 | tf_op jit(solution)/shard_map/ppermute | solution.py:23
  115.8 2.6 %collective-permute-done.74.refs_3_ = bf16[256,256]{1,0:T(8,128)(2,1)S(1)} collective-permute-done((bf16[256,256]{1,0:T(8,128)(2,1)S(1)}, bf16[256,256]{1,0:T(8,128)(2,1)S(1)}, u32[]{:S(2)}, u32[]{:S(2)}) %collective-permute-start.74) | collective-permute-done | bytes 131104 | tf_op jit(solution)/shard_map/ppermute | solution.py:23
  125.6 4.5 %up_product.7 = (bf16[128,256]{1,0:T(8,128)(2,1)S(1)}, bf16[128,256]{1,0:T(8,128)(2,1)S(1)}, bf16[128,256]{1,0:T(8,128)(2,1)S(1)}, bf16[128,256]{1,0:T(8,128)(2,...) custom-call(s32[16]{0:T(128)S(1)} %add.98.labels_ref, ...), custom_call_target="tpu_custom_call" | custom-call | flops 536870912 | bytes 1048576 | tf_op jit(solution)/shard_map/up_product/pallas_call | solution.py:138
  132.9 4.5 %up_product.6 = (bf16[128,256]{1,0:T(8,128)(2,1)S(1)}, bf16[128,256]{1,0:T(8,128)(2,1)S(1)}, bf16[128,256]{1,0:T(8,128)(2,1)S(1)}, bf16[128,256]{1,0:T(8,128)(2,...) custom-call(s32[16]{0:T(128)S(1)} %add.98.labels_ref, ...), custom_call_target="tpu_custom_call" | custom-call | flops 536870912 | bytes 1048576 | tf_op jit(solution)/shard_map/up_product/pallas_call | solution.py:138
  140.0 2.0 %collective-permute-start.81 = (bf16[128,256]{1,0:T(8,128)(2,1)S(1)}, bf16[128,256]{1,0:T(8,128)(2,1)S(1)}, u32[]{:S(2)}, u32[]{:S(2)}) collective-permute-start(bf16[128,256]{1,0:T(8,128)(2,1)S(1)} %get-tuple-element.84), channel_id=1, source_target_pairs={{0,19},{1,18},{2,17},{3,16},{16,3},{17,2},{18,1},{19,0},{4,23},{5,... | collective-permute-start | bytes 196616 | tf_op jit(solution)/shard_map/ppermute | solution.py:17
  146.4 2.5 %collective-permute-start.70 = (bf16[128,256]{1,0:T(8,128)(2,1)S(1)}, bf16[128,256]{1,0:T(8,128)(2,1)S(1)}, u32[]{:S(2)}, u32[]{:S(2)}) collective-permute-start(bf16[128,256]{1,0:T(8,128)(2,1)S(1)} %get-tuple-element.75), channel_id=1, source_target_pairs={{0,18},{1,19},{2,16},{3,17},{16,2},{17,3},{18,0},{19,1},{4,22},{5,... | collective-permute-start | bytes 196616 | tf_op jit(solution)/shard_map/ppermute | solution.py:17
  148.9 4.5 %up_product.5 = (bf16[128,256]{1,0:T(8,128)(2,1)S(1)}, bf16[128,256]{1,0:T(8,128)(2,1)S(1)}, bf16[128,256]{1,0:T(8,128)(2,1)S(1)}, bf16[128,256]{1,0:T(8,128)(2,...) custom-call(s32[16]{0:T(128)S(1)} %add.98.labels_ref, ...), custom_call_target="tpu_custom_call" | custom-call | flops 536870912 | bytes 1048576 | tf_op jit(solution)/shard_map/up_product/pallas_call | solution.py:138
  157.2 4.5 %up_product.4 = (bf16[128,256]{1,0:T(8,128)(2,1)S(1)}, bf16[128,256]{1,0:T(8,128)(2,1)S(1)}, bf16[128,256]{1,0:T(8,128)(2,1)S(1)}, bf16[128,256]{1,0:T(8,128)(2,...) custom-call(s32[16]{0:T(128)S(1)} %add.98.labels_ref, ...), custom_call_target="tpu_custom_call" | custom-call | flops 536870912 | bytes 1048576 | tf_op jit(solution)/shard_map/up_product/pallas_call | solution.py:138
  162.7 2.0 %collective-permute-start.60 = (bf16[128,256]{1,0:T(8,128)(2,1)S(1)}, bf16[128,256]{1,0:T(8,128)(2,1)S(1)}, u32[]{:S(2)}, u32[]{:S(2)}) collective-permute-start(bf16[128,256]{1,0:T(8,128)(2,1)S(1)} %get-tuple-element.67), channel_id=1, source_target_pairs={{0,18},{1,19},{2,16},{3,17},{16,2},{17,3},{18,0},{19,1},{4,22},{5,... | collective-permute-start | bytes 196616 | tf_op jit(solution)/shard_map/ppermute | solution.py:17
  174.1 2.5 %collective-permute-done.50.refs_6_ = bf16[128,256]{1,0:T(8,128)(2,1)S(1)} collective-permute-done((bf16[128,256]{1,0:T(8,128)(2,1)S(1)}, bf16[128,256]{1,0:T(8,128)(2,1)S(1)}, u32[]{:S(2)}, u32[]{:S(2)}) %collective-permute-start.50) | collective-permute-done | bytes 65568 | tf_op jit(solution)/shard_map/ppermute | solution.py:17
  (172 shorter events, 69.5 us)
Async XLA Ops:
  1.3 15.0 %collective-permute-start.9 = (bf16[64,1024]{1,0:T(8,128)(2,1)S(1)}, bf16[64,1024]{1,0:T(8,128)(2,1)S(1)}, u32[]{:S(2)}, u32[]{:S(2)}) collective-permute-start(bf16[64,1024]{1,0:T(8,128)(2,1)S(1)} %get-tuple-element.94), channel_id=1, source_target_pairs={{0,1},{1,0},{2,3},{3,2},{4,5},{5,4},{6,7},{7,6},{8,9},{9,8},{10,11... | collective-permute-start | bytes 393224 | tf_op jit(solution)/shard_map/ppermute | solution.py:17
  1.8 16.0 %collective-permute-start.10 = (bf16[64,1024]{1,0:T(8,128)(2,1)S(1)}, bf16[64,1024]{1,0:T(8,128)(2,1)S(1)}, u32[]{:S(2)}, u32[]{:S(2)}) collective-permute-start(bf16[64,1024]{1,0:T(8,128)(2,1)S(1)} %get-tuple-element.96), channel_id=1, source_target_pairs={{0,2},{1,3},{2,0},{3,1},{4,6},{5,7},{6,4},{7,5},{8,10},{9,11},{10,... | collective-permute-start | bytes 393224 | tf_op jit(solution)/shard_map/ppermute | solution.py:17
  4.4 14.0 %collective-permute-start.11 = (bf16[64,1024]{1,0:T(8,128)(2,1)S(1)}, bf16[64,1024]{1,0:T(8,128)(2,1)S(1)}, u32[]{:S(2)}, u32[]{:S(2)}) collective-permute-start(bf16[64,1024]{1,0:T(8,128)(2,1)S(1)} %get-tuple-element.93), channel_id=1, source_target_pairs={{0,3},{1,2},{2,1},{3,0},{4,7},{5,6},{6,5},{7,4},{8,11},{9,10},{10,... | collective-permute-start | bytes 393224 | tf_op jit(solution)/shard_map/ppermute | solution.py:17
  4.5 14.3 %collective-permute-start.12 = (bf16[64,1024]{1,0:T(8,128)(2,1)S(1)}, bf16[64,1024]{1,0:T(8,128)(2,1)S(1)}, u32[]{:S(2)}, u32[]{:S(2)}) collective-permute-start(bf16[64,1024]{1,0:T(8,128)(2,1)S(1)} %get-tuple-element.95.refs_0_), channel_id=1, source_target_pairs={{0,4},{4,8},{8,12},{12,0},{1,5},{5,9},{9,13},{13,1},{2,6},{6,10},{... | collective-permute-start | bytes 393224 | tf_op jit(solution)/shard_map/ppermute | solution.py:23
  18.8 12.2 %collective-permute-start.25 = (bf16[128,1024]{1,0:T(8,128)(2,1)S(1)}, bf16[128,1024]{1,0:T(8,128)(2,1)S(1)}, u32[]{:S(2)}, u32[]{:S(2)}) collective-permute-start(bf16[128,1024]{1,0:T(8,128)(2,1)S(1)} %get-tuple-element.89), channel_id=1, source_target_pairs={{0,2},{1,3},{2,0},{3,1},{16,18},{17,19},{18,16},{19,17},{4,6},{5,7... | collective-permute-start | bytes 786440 | tf_op jit(solution)/shard_map/ppermute | solution.py:17
  20.3 26.2 %collective-permute-start.26 = (bf16[128,1024]{1,0:T(8,128)(2,1)S(1)}, bf16[128,1024]{1,0:T(8,128)(2,1)S(1)}, u32[]{:S(2)}, u32[]{:S(2)}) collective-permute-start(bf16[128,1024]{1,0:T(8,128)(2,1)S(1)} %get-tuple-element.88), channel_id=1, source_target_pairs={{0,3},{1,2},{2,1},{3,0},{16,19},{17,18},{18,17},{19,16},{4,7},{5,6... | collective-permute-start | bytes 786440 | tf_op jit(solution)/shard_map/ppermute | solution.py:17
  22.6 25.5 %collective-permute-start.27 = (bf16[128,1024]{1,0:T(8,128)(2,1)S(1)}, bf16[128,1024]{1,0:T(8,128)(2,1)S(1)}, u32[]{:S(2)}, u32[]{:S(2)}) collective-permute-start(bf16[128,1024]{1,0:T(8,128)(2,1)S(1)} %get-tuple-element.87), channel_id=1, source_target_pairs={{0,16},{1,17},{2,18},{3,19},{16,0},{17,1},{18,2},{19,3},{4,20},{5,... | collective-permute-start | bytes 786440 | tf_op jit(solution)/shard_map/ppermute | solution.py:17
  24.6 25.1 %collective-permute-start.28 = (bf16[128,1024]{1,0:T(8,128)(2,1)S(1)}, bf16[128,1024]{1,0:T(8,128)(2,1)S(1)}, u32[]{:S(2)}, u32[]{:S(2)}) collective-permute-start(bf16[128,1024]{1,0:T(8,128)(2,1)S(1)} %get-tuple-element.86), channel_id=1, source_target_pairs={{0,17},{1,16},{2,19},{3,18},{16,1},{17,0},{18,3},{19,2},{4,21},{5,... | collective-permute-start | bytes 786440 | tf_op jit(solution)/shard_map/ppermute | solution.py:17
  26.3 24.8 %collective-permute-start.29 = (bf16[128,1024]{1,0:T(8,128)(2,1)S(1)}, bf16[128,1024]{1,0:T(8,128)(2,1)S(1)}, u32[]{:S(2)}, u32[]{:S(2)}) collective-permute-start(bf16[128,1024]{1,0:T(8,128)(2,1)S(1)} %get-tuple-element.92), channel_id=1, source_target_pairs={{0,18},{1,19},{2,16},{3,17},{16,2},{17,3},{18,0},{19,1},{4,22},{5,... | collective-permute-start | bytes 786440 | tf_op jit(solution)/shard_map/ppermute | solution.py:17
  31.0 20.6 %collective-permute-start.30 = (bf16[128,1024]{1,0:T(8,128)(2,1)S(1)}, bf16[128,1024]{1,0:T(8,128)(2,1)S(1)}, u32[]{:S(2)}, u32[]{:S(2)}) collective-permute-start(bf16[128,1024]{1,0:T(8,128)(2,1)S(1)} %get-tuple-element.85), channel_id=1, source_target_pairs={{0,19},{1,18},{2,17},{3,16},{16,3},{17,2},{18,1},{19,0},{4,23},{5,... | collective-permute-start | bytes 786440 | tf_op jit(solution)/shard_map/ppermute | solution.py:17
  49.7 10.4 %collective-permute-start.15 = (bf16[64,1024]{1,0:T(8,128)(2,1)S(1)}, bf16[64,1024]{1,0:T(8,128)(2,1)S(1)}, u32[]{:S(2)}, u32[]{:S(2)}) collective-permute-start(bf16[64,1024]{1,0:T(8,128)(2,1)S(1)} %collective-permute-done.11.refs_3_), channel_id=1, source_target_pairs={{0,4},{4,8},{8,12},{12,0},{1,5},{5,9},{9,13},{13,1},{2,6},{6,10},{... | collective-permute-start | bytes 393224 | tf_op jit(solution)/shard_map/ppermute | solution.py:23
  51.1 14.6 %collective-permute-start.72 = (bf16[256,256]{1,0:T(8,128)(2,1)S(1)}, bf16[256,256]{1,0:T(8,128)(2,1)S(1)}, u32[]{:S(2)}, u32[]{:S(2)}) collective-permute-start(bf16[256,256]{1,0:T(8,128)(2,1)S(1)} %pad_maximum_fusion.3.refs_0_), channel_id=1, source_target_pairs={{0,4},{4,8},{8,12},{12,0},{1,5},{5,9},{9,13},{13,1},{2,6},{6,10},{... | collective-permute-start | bytes 393224 | tf_op jit(solution)/shard_map/ppermute | solution.py:23
  51.6 14.1 %collective-permute-start.16 = (bf16[64,1024]{1,0:T(8,128)(2,1)S(1)}, bf16[64,1024]{1,0:T(8,128)(2,1)S(1)}, u32[]{:S(2)}, u32[]{:S(2)}) collective-permute-start(bf16[64,1024]{1,0:T(8,128)(2,1)S(1)} %collective-permute-done.12.refs_4_), channel_id=1, source_target_pairs={{0,4},{4,8},{8,12},{12,0},{1,5},{5,9},{9,13},{13,1},{2,6},{6,10},{... | collective-permute-start | bytes 393224 | tf_op jit(solution)/shard_map/ppermute | solution.py:23
  54.5 14.0 %collective-permute-start.17 = (bf16[64,1024]{1,0:T(8,128)(2,1)S(1)}, bf16[64,1024]{1,0:T(8,128)(2,1)S(1)}, u32[]{:S(2)}, u32[]{:S(2)}) collective-permute-start(bf16[64,1024]{1,0:T(8,128)(2,1)S(1)} %collective-permute-done.13.refs_5_), channel_id=1, source_target_pairs={{0,4},{4,8},{8,12},{12,0},{1,5},{5,9},{9,13},{13,1},{2,6},{6,10},{... | collective-permute-start | bytes 393224 | tf_op jit(solution)/shard_map/ppermute | solution.py:23
  57.3 14.0 %collective-permute-start.18 = (bf16[64,1024]{1,0:T(8,128)(2,1)S(1)}, bf16[64,1024]{1,0:T(8,128)(2,1)S(1)}, u32[]{:S(2)}, u32[]{:S(2)}) collective-permute-start(bf16[64,1024]{1,0:T(8,128)(2,1)S(1)} %collective-permute-done.14.refs_6_), channel_id=1, source_target_pairs={{0,4},{4,8},{8,12},{12,0},{1,5},{5,9},{9,13},{13,1},{2,6},{6,10},{... | collective-permute-start | bytes 393224 | tf_op jit(solution)/shard_map/ppermute | solution.py:23
  60.1 14.0 %collective-permute-start.19 = (bf16[64,1024]{1,0:T(8,128)(2,1)S(1)}, bf16[64,1024]{1,0:T(8,128)(2,1)S(1)}, u32[]{:S(2)}, u32[]{:S(2)}) collective-permute-start(bf16[64,1024]{1,0:T(8,128)(2,1)S(1)} %collective-permute-done.15.refs_7_), channel_id=1, source_target_pairs={{0,4},{4,8},{8,12},{12,0},{1,5},{5,9},{9,13},{13,1},{2,6},{6,10},{... | collective-permute-start | bytes 393224 | tf_op jit(solution)/shard_map/ppermute | solution.py:23
  65.7 11.2 %collective-permute-start.62 = (bf16[256,256]{1,0:T(8,128)(2,1)S(1)}, bf16[256,256]{1,0:T(8,128)(2,1)S(1)}, u32[]{:S(2)}, u32[]{:S(2)}) collective-permute-start(bf16[256,256]{1,0:T(8,128)(2,1)S(1)} %pad_maximum_fusion.2.refs_0_), channel_id=1, source_target_pairs={{0,4},{4,8},{8,12},{12,0},{1,5},{5,9},{9,13},{13,1},{2,6},{6,10},{... | collective-permute-start | bytes 393224 | tf_op jit(solution)/shard_map/ppermute | solution.py:23
  65.7 14.0 %collective-permute-start.20 = (bf16[64,1024]{1,0:T(8,128)(2,1)S(1)}, bf16[64,1024]{1,0:T(8,128)(2,1)S(1)}, u32[]{:S(2)}, u32[]{:S(2)}) collective-permute-start(bf16[64,1024]{1,0:T(8,128)(2,1)S(1)} %collective-permute-done.16.refs_8_), channel_id=1, source_target_pairs={{0,4},{4,8},{8,12},{12,0},{1,5},{5,9},{9,13},{13,1},{2,6},{6,10},{... | collective-permute-start | bytes 393224 | tf_op jit(solution)/shard_map/ppermute | solution.py:23
  68.5 14.0 %collective-permute-start.21 = (bf16[64,1024]{1,0:T(8,128)(2,1)S(1)}, bf16[64,1024]{1,0:T(8,128)(2,1)S(1)}, u32[]{:S(2)}, u32[]{:S(2)}) collective-permute-start(bf16[64,1024]{1,0:T(8,128)(2,1)S(1)} %collective-permute-done.17.refs_9_), channel_id=1, source_target_pairs={{0,4},{4,8},{8,12},{12,0},{1,5},{5,9},{9,13},{13,1},{2,6},{6,10},{... | collective-permute-start | bytes 393224 | tf_op jit(solution)/shard_map/ppermute | solution.py:23
  71.3 14.0 %collective-permute-start.22 = (bf16[64,1024]{1,0:T(8,128)(2,1)S(1)}, bf16[64,1024]{1,0:T(8,128)(2,1)S(1)}, u32[]{:S(2)}, u32[]{:S(2)}) collective-permute-start(bf16[64,1024]{1,0:T(8,128)(2,1)S(1)} %collective-permute-done.18.refs_10_), channel_id=1, source_target_pairs={{0,4},{4,8},{8,12},{12,0},{1,5},{5,9},{9,13},{13,1},{2,6},{6,10},{... | collective-permute-start | bytes 393224 | tf_op jit(solution)/shard_map/ppermute | solution.py:23
  74.1 14.0 %collective-permute-start.23 = (bf16[64,1024]{1,0:T(8,128)(2,1)S(1)}, bf16[64,1024]{1,0:T(8,128)(2,1)S(1)}, u32[]{:S(2)}, u32[]{:S(2)}) collective-permute-start(bf16[64,1024]{1,0:T(8,128)(2,1)S(1)} %collective-permute-done.19.refs_11_), channel_id=1, source_target_pairs={{0,4},{4,8},{8,12},{12,0},{1,5},{5,9},{9,13},{13,1},{2,6},{6,10},{... | collective-permute-start | bytes 393224 | tf_op jit(solution)/shard_map/ppermute | solution.py:23
  76.9 20.8 %collective-permute-start.52 = (bf16[256,256]{1,0:T(8,128)(2,1)S(1)}, bf16[256,256]{1,0:T(8,128)(2,1)S(1)}, u32[]{:S(2)}, u32[]{:S(2)}) collective-permute-start(bf16[256,256]{1,0:T(8,128)(2,1)S(1)} %pad_maximum_fusion.1.refs_0_), channel_id=1, source_target_pairs={{0,4},{4,8},{8,12},{12,0},{1,5},{5,9},{9,13},{13,1},{2,6},{6,10},{... | collective-permute-start | bytes 393224 | tf_op jit(solution)/shard_map/ppermute | solution.py:23
  79.7 20.3 %collective-permute-start.6 = (bf16[256,256]{1,0:T(8,128)(2,1)S(1)}, bf16[256,256]{1,0:T(8,128)(2,1)S(1)}, u32[]{:S(2)}, u32[]{:S(2)}) collective-permute-start(bf16[256,256]{1,0:T(8,128)(2,1)S(1)} %pad_maximum_fusion.refs_0_), channel_id=1, source_target_pairs={{0,4},{4,8},{8,12},{12,0},{1,5},{5,9},{9,13},{13,1},{2,6},{6,10},{... | collective-permute-start | bytes 393224 | tf_op jit(solution)/shard_map/ppermute | solution.py:23
  82.5 17.6 %collective-permute-start.73 = (bf16[256,256]{1,0:T(8,128)(2,1)S(1)}, bf16[256,256]{1,0:T(8,128)(2,1)S(1)}, u32[]{:S(2)}, u32[]{:S(2)}) collective-permute-start(bf16[256,256]{1,0:T(8,128)(2,1)S(1)} %collective-permute-done.72.refs_1_), channel_id=1, source_target_pairs={{0,4},{4,8},{8,12},{12,0},{1,5},{5,9},{9,13},{13,1},{2,6},{6,10},{... | collective-permute-start | bytes 393224 | tf_op jit(solution)/shard_map/ppermute | solution.py:23
  85.4 16.3 %collective-permute-start.63 = (bf16[256,256]{1,0:T(8,128)(2,1)S(1)}, bf16[256,256]{1,0:T(8,128)(2,1)S(1)}, u32[]{:S(2)}, u32[]{:S(2)}) collective-permute-start(bf16[256,256]{1,0:T(8,128)(2,1)S(1)} %collective-permute-done.62.refs_1_), channel_id=1, source_target_pairs={{0,4},{4,8},{8,12},{12,0},{1,5},{5,9},{9,13},{13,1},{2,6},{6,10},{... | collective-permute-start | bytes 393224 | tf_op jit(solution)/shard_map/ppermute | solution.py:23
  104.6 10.9 %collective-permute-start.7 = (bf16[256,256]{1,0:T(8,128)(2,1)S(1)}, bf16[256,256]{1,0:T(8,128)(2,1)S(1)}, u32[]{:S(2)}, u32[]{:S(2)}) collective-permute-start(bf16[256,256]{1,0:T(8,128)(2,1)S(1)} %collective-permute-done.6.refs_1_), channel_id=1, source_target_pairs={{0,4},{4,8},{8,12},{12,0},{1,5},{5,9},{9,13},{13,1},{2,6},{6,10},{... | collective-permute-start | bytes 393224 | tf_op jit(solution)/shard_map/ppermute | solution.py:23
  106.0 12.4 %collective-permute-start.74 = (bf16[256,256]{1,0:T(8,128)(2,1)S(1)}, bf16[256,256]{1,0:T(8,128)(2,1)S(1)}, u32[]{:S(2)}, u32[]{:S(2)}) collective-permute-start(bf16[256,256]{1,0:T(8,128)(2,1)S(1)} %collective-permute-done.73.refs_2_), channel_id=1, source_target_pairs={{0,4},{4,8},{8,12},{12,0},{1,5},{5,9},{9,13},{13,1},{2,6},{6,10},{... | collective-permute-start | bytes 393224 | tf_op jit(solution)/shard_map/ppermute | solution.py:23
  107.4 24.6 %collective-permute-start.64 = (bf16[256,256]{1,0:T(8,128)(2,1)S(1)}, bf16[256,256]{1,0:T(8,128)(2,1)S(1)}, u32[]{:S(2)}, u32[]{:S(2)}) collective-permute-start(bf16[256,256]{1,0:T(8,128)(2,1)S(1)} %collective-permute-done.63.refs_2_), channel_id=1, source_target_pairs={{0,4},{4,8},{8,12},{12,0},{1,5},{5,9},{9,13},{13,1},{2,6},{6,10},{... | collective-permute-start | bytes 393224 | tf_op jit(solution)/shard_map/ppermute | solution.py:23
  122.8 14.7 %collective-permute-start.54 = (bf16[256,256]{1,0:T(8,128)(2,1)S(1)}, bf16[256,256]{1,0:T(8,128)(2,1)S(1)}, u32[]{:S(2)}, u32[]{:S(2)}) collective-permute-start(bf16[256,256]{1,0:T(8,128)(2,1)S(1)} %collective-permute-done.53.refs_2_), channel_id=1, source_target_pairs={{0,4},{4,8},{8,12},{12,0},{1,5},{5,9},{9,13},{13,1},{2,6},{6,10},{... | collective-permute-start | bytes 393224 | tf_op jit(solution)/shard_map/ppermute | solution.py:23
  123.1 15.2 %collective-permute-start.8 = (bf16[256,256]{1,0:T(8,128)(2,1)S(1)}, bf16[256,256]{1,0:T(8,128)(2,1)S(1)}, u32[]{:S(2)}, u32[]{:S(2)}) collective-permute-start(bf16[256,256]{1,0:T(8,128)(2,1)S(1)} %collective-permute-done.7.refs_2_), channel_id=1, source_target_pairs={{0,4},{4,8},{8,12},{12,0},{1,5},{5,9},{9,13},{13,1},{2,6},{6,10},{... | collective-permute-start | bytes 393224 | tf_op jit(solution)/shard_map/ppermute | solution.py:23
  142.7 10.8 %collective-permute-start.66 = (bf16[128,256]{1,0:T(8,128)(2,1)S(1)}, bf16[128,256]{1,0:T(8,128)(2,1)S(1)}, u32[]{:S(2)}, u32[]{:S(2)}) collective-permute-start(bf16[128,256]{1,0:T(8,128)(2,1)S(1)} %get-tuple-element.71), channel_id=1, source_target_pairs={{0,2},{1,3},{2,0},{3,1},{16,18},{17,19},{18,16},{19,17},{4,6},{5,7... | collective-permute-start | bytes 196616 | tf_op jit(solution)/shard_map/ppermute | solution.py:17
  143.4 11.1 %collective-permute-start.67 = (bf16[128,256]{1,0:T(8,128)(2,1)S(1)}, bf16[128,256]{1,0:T(8,128)(2,1)S(1)}, u32[]{:S(2)}, u32[]{:S(2)}) collective-permute-start(bf16[128,256]{1,0:T(8,128)(2,1)S(1)} %get-tuple-element.72), channel_id=1, source_target_pairs={{0,3},{1,2},{2,1},{3,0},{16,19},{17,18},{18,17},{19,16},{4,7},{5,6... | collective-permute-start | bytes 196616 | tf_op jit(solution)/shard_map/ppermute | solution.py:17
  (58 other events, 577.7 us)

commit v4 on v1

v4 whole, which is shorter than its diff:
```python
import functools

import jax
import jax.numpy as jnp
from jax import lax
from jax.experimental import pallas as pl
from jax.experimental.pallas import tpu as pltpu
from jax.sharding import Mesh
from jax.sharding import PartitionSpec as P

adapter_scale = 2.0
PLANE = ("groups", "mid")
LANES = 128
CORES = 2
VMEM_BYTES = 40 << 20


def to_partner(value, axes, size, offset):
    return lax.ppermute(value, axes, [(i, i ^ offset) for i in range(size)])


def ring(block, outer):
    blocks = [block]
    for _ in range(outer - 1):
        block = lax.ppermute(block, "outer", [(i, (i + 1) % outer) for i in range(outer)])
        blocks.append(block)
    return blocks


def load_maps(sources, target, sems, rank):
    copies = []
    for first in range(0, len(sources), CORES):
        for at in range(0, sources[first].shape[0], rank):
            for source in sources[first : first + CORES]:
                n = len(copies)
                target_rows = target.at[pl.ds(n * rank, rank)]
                copies.append(pltpu.make_async_copy(source.at[pl.ds(at, rank)], target_rows, sems.at[n]))
    for copy in copies:
        copy.start()
    return copies


def pair_labels(labels_ref, pair, rank, shape):
    per_tile = LANES // rank
    lane = lax.broadcasted_iota(jnp.int32, shape, 1)
    label = jnp.full(shape, labels_ref[pair * per_tile], jnp.int32)
    for n in range(1, per_tile):
        label = jnp.where(lane >= n * rank, labels_ref[pair * per_tile + n], label)
    return label


def outgoing_kernel(members, share, hidden_ref, ids_ref, out_ref):
    for member in range(members):
        out_ref[member, :, :share] = hidden_ref[:, member * share : (member + 1) * share]
        out_ref[member, :, share:] = ids_ref[...]


def outgoing_rows(hidden, ids, members):
    tok, width = hidden.shape
    share = width // members
    in_vmem = pl.BlockSpec(memory_space=pltpu.VMEM)
    return pl.pallas_call(
        functools.partial(outgoing_kernel, members, share),
        out_shape=jax.ShapeDtypeStruct((members, tok, share + LANES), jnp.bfloat16),
        in_specs=[in_vmem, in_vmem],
        out_specs=in_vmem,
        compiler_params=pltpu.CompilerParams(vmem_limit_bytes=VMEM_BYTES),
        name="outgoing_rows",
    )(hidden, ids)


def down_kernel(map_count, rank, labels_ref, rows_ref, *refs):
    maps, (sums_ref, map_buf, sems) = refs[:map_count], refs[map_count:]
    for copy in load_maps(maps, map_buf, sems, rank):
        copy.wait()
    members, tok, _ = rows_ref.shape
    share = map_buf.shape[1]
    tiles = map_buf.shape[0] // LANES
    batch = 2 if tiles % 2 == 0 else 1

    def one(member, _):
        ids = rows_ref[member, :, share:].astype(jnp.float32).astype(jnp.int32)
        tokens = rows_ref[member, :, :share]
        total = jnp.zeros((tok, LANES), jnp.float32)
        for first in range(0, tiles, batch):
            product = lax.dot_general(
                tokens,
                map_buf[first * LANES : (first + batch) * LANES, :],
                (((1,), (1,)), ((), ())),
                preferred_element_type=jnp.float32,
            )
            for n in range(batch):
                named = ids == pair_labels(labels_ref, first + n, rank, ids.shape)
                total += jnp.where(named, product[:, n * LANES : (n + 1) * LANES], 0.0)
        sums_ref[member] = total
        return 0

    lax.fori_loop(0, members, one, 0)


def down_product(labels, rows, maps, rank):
    members, tok, wide_share = rows.shape
    share = wide_share - LANES
    map_rows = sum(m.shape[0] for m in maps)
    in_vmem = pl.BlockSpec(memory_space=pltpu.VMEM)
    return pl.pallas_call(
        functools.partial(down_kernel, len(maps), rank),
        out_shape=jax.ShapeDtypeStruct((members, tok, LANES), jnp.float32),
        in_specs=[pl.BlockSpec(memory_space=pltpu.SMEM), in_vmem]
        + [pl.BlockSpec(memory_space=pl.ANY)] * len(maps),
        out_specs=in_vmem,
        scratch_shapes=[
            pltpu.VMEM((map_rows, share), jnp.bfloat16),
            pltpu.SemaphoreType.DMA((map_rows // rank,)),
        ],
        compiler_params=pltpu.CompilerParams(vmem_limit_bytes=VMEM_BYTES),
        cost_estimate=pl.CostEstimate(
            flops=2 * map_rows * members * tok * share,
            bytes_accessed=2 * share * (map_rows + members * tok),
            transcendentals=0,
        ),
        name="down_product",
    )(labels, rows, *maps)


def up_kernel(map_count, rank, labels_ref, rows_ref, shrunk_ref, *refs):
    maps, (out_ref, map_buf, sems) = refs[:map_count], refs[map_count:]
    for copy in load_maps(maps, map_buf, sems, rank):
        copy.wait()
    members, tok, _ = shrunk_ref.shape
    tiles = map_buf.shape[0] // LANES

    def one(member, _):
        ids = rows_ref[member, :, :].astype(jnp.float32).astype(jnp.int32)
        shrunk = shrunk_ref[member].astype(jnp.float32)
        spread = [
            jnp.where(ids == pair_labels(labels_ref, tile, rank, ids.shape), shrunk, 0.0).astype(jnp.bfloat16)
            for tile in range(tiles)
        ]
        product = jnp.dot(
            jnp.concatenate(spread, axis=1), map_buf[...], preferred_element_type=jnp.float32
        )
        out_ref[member] = (adapter_scale * product).astype(jnp.bfloat16)
        return 0

    lax.fori_loop(0, members, one, 0)


def up_product(labels, rows, shrunk, maps, rank):
    members, tok, _ = shrunk.shape
    share = rows.shape[2] - LANES
    map_rows, piece = sum(m.shape[0] for m in maps), maps[0].shape[1]
    in_vmem = pl.BlockSpec(memory_space=pltpu.VMEM)
    return pl.pallas_call(
        functools.partial(up_kernel, len(maps), rank),
        grid=(1,),
        out_shape=jax.ShapeDtypeStruct((members, tok, piece), jnp.bfloat16),
        in_specs=[
            pl.BlockSpec(memory_space=pltpu.SMEM),
            pl.BlockSpec((members, tok, LANES), lambda _: (0, 0, share // LANES)),
            in_vmem,
        ]
        + [pl.BlockSpec(memory_space=pl.ANY)] * len(maps),
        out_specs=in_vmem,
        scratch_shapes=[
            pltpu.VMEM((map_rows, piece), jnp.bfloat16),
            pltpu.SemaphoreType.DMA((map_rows // rank,)),
        ],
        compiler_params=pltpu.CompilerParams(vmem_limit_bytes=VMEM_BYTES),
        cost_estimate=pl.CostEstimate(
            flops=2 * map_rows * members * tok * piece,
            bytes_accessed=2 * piece * (map_rows + members * tok),
            transcendentals=0,
        ),
        name="up_product",
    )(labels, rows, shrunk, *maps)


def place_kernel(pieces, *refs):
    parts, out_ref, sems = refs[:pieces], refs[-2], refs[-1]
    members, _, piece = parts[0].shape
    copies = []
    for n in range(members * pieces):
        member, part = n // pieces, n % pieces
        target = out_ref.at[:, pl.ds(n * piece, piece)]
        copies.append(pltpu.make_async_copy(parts[part].at[member], target, sems.at[n]))
    for copy in copies:
        copy.start()
    for copy in copies:
        copy.wait()


def place(parts):
    members, tok, piece = parts[0].shape
    anywhere = pl.BlockSpec(memory_space=pl.ANY)
    return pl.pallas_call(
        functools.partial(place_kernel, len(parts)),
        out_shape=jax.ShapeDtypeStruct((tok, members * len(parts) * piece), jnp.bfloat16),
        in_specs=[anywhere] * len(parts),
        out_specs=anywhere,
        scratch_shapes=[pltpu.SemaphoreType.DMA((members * len(parts),))],
        compiler_params=pltpu.CompilerParams(vmem_limit_bytes=VMEM_BYTES),
        name="place_results",
    )(*parts)


def after(value, earlier):
    return lax.optimization_barrier((value, earlier))[0]


def per_device(token_adapter_index, hidden, adapter_down_maps, adapter_up_maps):
    tok, width = hidden.shape
    groups, outer, mid, cores = (lax.axis_size(a) for a in ("groups", "outer", "mid", "cores"))
    members = groups * mid
    share = width // members
    rank = adapter_up_maps.shape[1]
    pieces = 2
    piece = share // pieces
    group, row, level, core = (lax.axis_index(a) for a in ("groups", "mid", "outer", "cores"))
    me = group * mid + row

    def columns(array, offset):
        return lax.dynamic_slice_in_dim(array, (me ^ offset) * share, share, axis=1)

    def exchanged(array):
        return [columns(array, 0)] + [
            to_partner(columns(array, offset), "mid", mid, offset) for offset in range(1, mid)
        ]

    def with_other_core(block):
        return [block] + [to_partner(block, "cores", cores, offset) for offset in range(1, cores)]

    rows_per_ring = max(1, mid // 2)

    def labels_of(first_row, row_count):
        back = jnp.arange(outer, dtype=jnp.int32)[:, None, None]
        rows_ = first_row + jnp.arange(row_count, dtype=jnp.int32)[None, :, None]
        cores_ = jnp.arange(cores, dtype=jnp.int32)[None, None, :]
        owner = ((level - back + outer) % outer) * mid + (row ^ rows_)
        return (owner * cores + (core ^ cores_)).reshape(-1)

    down_blocks = exchanged(adapter_down_maps[0].T)
    down_maps, down_labels, last = [], [], None
    for first in range(0, mid, rows_per_ring):
        some = down_blocks[first : first + rows_per_ring]
        blocks = ring(some[0] if len(some) == 1 else jnp.concatenate(some, axis=0), outer)
        last = blocks[-2]
        down_maps += [b for block in blocks for b in with_other_core(block)]
        down_labels.append(labels_of(first, rows_per_ring))
    down_labels = jnp.concatenate(down_labels)

    ids = jnp.broadcast_to(token_adapter_index.astype(jnp.bfloat16), (tok, LANES))
    rows = lax.all_to_all(outgoing_rows(hidden, ids, members), PLANE, split_axis=0, concat_axis=0, tiled=True)

    partial = down_product(down_labels, rows, down_maps, rank)
    terms = lax.all_to_all(partial, PLANE, split_axis=0, concat_axis=0, tiled=True)
    own = jnp.sum(terms, axis=0).astype(jnp.bfloat16)
    shrunk = lax.all_to_all(
        jnp.broadcast_to(own[None], (members,) + own.shape), PLANE, split_axis=0, concat_axis=0, tiled=True
    )

    up_blocks = exchanged(after(adapter_up_maps[0], last))
    up_labels = labels_of(0, mid)
    parts = []
    for part in range(pieces):
        block = jnp.concatenate([b[:, part * piece : (part + 1) * piece] for b in up_blocks], axis=0)
        maps = [b for held in ring(block, outer) for b in with_other_core(held)]
        delta = up_product(up_labels, rows, shrunk, maps, rank)
        parts.append(lax.all_to_all(delta, PLANE, split_axis=0, concat_axis=0, tiled=True))
    return place(parts)


def solution(mesh):
    groups, wide = mesh.shape["groups"], mesh.shape["wide"]
    outer = 1 << ((wide.bit_length() - 1) // 2)
    fine = Mesh(
        mesh.devices.reshape(groups, outer, wide // (outer * CORES), CORES), ("groups", "outer", "mid", "cores")
    )
    owner = ("outer", "mid", "cores")
    rows = P(("groups",) + owner, None)
    return jax.shard_map(
        per_device,
        mesh=fine,
        in_specs=(rows, rows, P(owner, None, None), P(owner, None, None)),
        out_specs=rows,
        check_vma=False,
    )
```

time: 157 us -> 167 us (1.064)
  blocking collectives: 112 us -> 18.3 us
  waiting for transfers between devices: 5.51 us -> 70.2 us
  starting transfers between devices: 3.78 us -> 34.8 us
  Pallas kernels: 0 us -> 20.7 us
  between operations: 13.5 us -> 0.24 us
  matrix products: 8.74 us -> 0 us
  other arithmetic: 0.01 us -> 4.94 us
  local copies, waits for them, and re-layouts: 12.7 us -> 16.9 us
    ppermute x0 -> x30, waiting for transfers between devices: none -> 61.8 us  [the longest x12 33.4 us: ring(): lax.ppermute(block, 'outer', [(i, (i + 1) % outer) for i in range(outer)])]
    all_to_all x3 -> x1, blocking collectives: 54.4 us -> 18.3 us  [per_device(): lax.all_to_all(delta, PLANE, split_axis=0, concat_axis=0, tiled=True)]
    all_gather x1 -> x0, blocking collectives: 29.5 us -> none  [per_device(): ids = lax.all_gather(token_adapter_index[:, 0], PLANE, axis=0, tiled=True)]
    psum x1 -> x0, blocking collectives: 28 us -> none  [per_device(): shrunk = lax.psum(partial, PLANE).astype(jnp.bfloat16)]
    pallas_call x0 -> x5, Pallas kernels: none -> 20.7 us  [the longest x2 10 us: up_product(): pl.pallas_call(functools.partial(up_kernel, len(maps), rank), grid=(1,),...]
    ppermute x0 -> x30, starting transfers between devices: none -> 20.6 us  [the longest x12 13.3 us: ring(): lax.ppermute(block, 'outer', [(i, (i + 1) % outer) for i in range(outer)])]
    all_to_all x1 -> x4, starting transfers between devices: 3.74 us -> 14.2 us  [the longest x1 3.71 us: per_device(): lax.all_to_all(partial, PLANE, split_axis=0, concat_axis=0, tiled=True)]
    dot_general x2 -> x0, matrix products: 8.74 us -> none  [the longest x1 4.78 us: per_device(): lax.dot_general(down.reshape(adapters * rank, share), rows, (((1,), (1,))...]
  transfers between devices with their start and end apart: 3 -> 34, of which waited for: 1 -> 12; matrix products, arithmetic and copies ran while one was open for 9% -> 7% of each run, Pallas kernels for 0% -> 12%
where the time goes in v4:
time: 167 us; the launch traced here: 166 us
  waiting for transfers between devices  70.2 us (42%)
  starting transfers between devices  34.8 us (21%)
  Pallas kernels  20.7 us (12%)
  blocking collectives  18.3 us (11%)
  local copies, waits for them, and re-layouts  16.9 us (10%)
  other arithmetic  4.94 us (3%)
    ppermute x12, waiting for transfers between devices, ring(): lax.ppermute(block, 'outer', [(i, (i + 1) % outer) for i in range(outer)])  33.4 us
    ppermute x18, waiting for transfers between devices, to_partner(): return lax.ppermute(value, axes, [(i, i ^ offset) for i in range(size)])  28.4 us
    all_to_all x1, blocking collectives, per_device(): lax.all_to_all(delta, PLANE, split_axis=0, concat_axis=0, tiled=True)  18.3 us
    ppermute x12, starting transfers between devices, ring(): lax.ppermute(block, 'outer', [(i, (i + 1) % outer) for i in range(outer)])  13.3 us
    pallas_call x2, Pallas kernels, up_product(): pl.pallas_call(functools.partial(up_kernel, len(maps), rank), grid=(1,),...  10 us
    unnamed x24, local copies, waits for them, and re-layouts  9.2 us
    pallas_call x1, Pallas kernels, down_product(): pl.pallas_call(functools.partial(down_kernel, len(maps), rank), out_shape...  9.12 us
    ppermute x18, starting transfers between devices, to_partner(): return lax.ppermute(value, axes, [(i, i ^ offset) for i in range(size)])  7.3 us
  transfers between devices with their start and end apart: 34, of which 12 were waited for; matrix products, arithmetic and copies ran while one was open for 7% of the time, Pallas kernels for 12%

profile of v4, /device:TPU:0, one launch (start us, length us, event | category | flops | bytes accessed | tf_op | source)
XLA Modules:
  0.0 166.0 jit_solution(5066143708821301509)
XLA Ops:
  1.1 3.0 %collective-permute-start.7 = (bf16[64,2048]{1,0:T(8,128)(2,1)S(1)}, bf16[64,2048]{1,0:T(8,128)(2,1)S(1)}, u32[]{:S(2)}, u32[]{:S(2)}) collective-permute-start(bf16[64,2048]{1,0:T(8,128)(2,1)S(1)} %get-tuple-element.9), channel_id=1, source_target_pairs={{0,2},{2,0},{1,3},{3,1},{4,6},{6,4},{5,7},{7,5},{8,10},{10,8},{9,1... | collective-permute-start | bytes 786440 | tf_op jit(solution)/shard_map/ppermute | solution.py:19
  4.1 6.3 %collective-permute-done.7.refs_8_ = bf16[64,2048]{1,0:T(8,128)(2,1)S(1)} collective-permute-done((bf16[64,2048]{1,0:T(8,128)(2,1)S(1)}, bf16[64,2048]{1,0:T(8,128)(2,1)S(1)}, u32[]{:S(2)}, u32[]{:S(2)}) %collective-permute-start.7) | collective-permute-done | bytes 262176 | tf_op jit(solution)/shard_map/ppermute | solution.py:19
  10.4 1.8 %collective-permute-start.9 = (bf16[64,2048]{1,0:T(8,128)(2,1)S(1)}, bf16[64,2048]{1,0:T(8,128)(2,1)}, u32[]{:S(2)}, u32[]{:S(2)}) collective-permute-start(bf16[64,2048]{1,0:T(8,128)(2,1)S(1)} %collective-permute-done.7.refs_8_), channel_id=1, source_target_pairs={{0,4},{4,8},{8,12},{12,0},{1,5},{5,9},{9,13},{13,1},{2,6},{6,10},{... | collective-permute-start | bytes 786440 | tf_op jit(solution)/shard_map/ppermute | solution.py:25
  12.2 7.6 %collective-permute-done.9.refs_10_ = bf16[64,2048]{1,0:T(8,128)(2,1)} collective-permute-done((bf16[64,2048]{1,0:T(8,128)(2,1)S(1)}, bf16[64,2048]{1,0:T(8,128)(2,1)}, u32[]{:S(2)}, u32[]{:S(2)}) %collective-permute-start.9) | collective-permute-done | bytes 262176 | tf_op jit(solution)/shard_map/ppermute | solution.py:25
  20.6 1.6 copy-done.2
  22.3 1.4 copy-done
  23.7 3.7 %all-to-all-start = ((bf16[4,128,2176]{2,1,0:T(8,128)(2,1)}), bf16[4,128,2176]{2,1,0:T(8,128)(2,1)S(1)}, u32[]{:S(2)}, u32[]{:S(2)}) async-start(bf16[4,128,2176]{2,1,0:T(8,128)(2,1)} %copy-done), calls=%async_computation | async-start | bytes 4456448 | tf_op jit(solution)/shard_map/all_to_all | solution.py:253
  29.6 2.1 %collective-permute-start.15 = (bf16[64,2048]{1,0:T(8,128)(2,1)S(1)}, bf16[64,2048]{1,0:T(8,128)(2,1)}, u32[]{:S(2)}, u32[]{:S(2)}) collective-permute-start(bf16[64,2048]{1,0:T(8,128)(2,1)S(1)} %constant_dynamic-slice_fusion.1), channel_id=1, source_target_pairs={{0,2},{2,0},{1,3},{3,1},{4,6},{6,4},{5,7},{7,5},{8,10},{10,8},{9,1... | collective-permute-start | bytes 786440 | tf_op jit(solution)/shard_map/ppermute | solution.py:19
  31.7 4.0 %collective-permute-done.1.refs_2_ = bf16[64,2048]{1,0:T(8,128)(2,1)S(1)} collective-permute-done((bf16[64,2048]{1,0:T(8,128)(2,1)S(1)}, bf16[64,2048]{1,0:T(8,128)(2,1)S(1)}, u32[]{:S(2)}, u32[]{:S(2)}) %collective-permute-start.1) | collective-permute-done | bytes 262176 | tf_op jit(solution)/shard_map/ppermute | solution.py:25
  35.8 1.7 %constant_dynamic-slice_fusion.2 = (bf16[64,1024]{1,0:T(8,128)(2,1)}, bf16[64,1024]{1,0:T(8,128)(2,1)S(1)}) fusion(bf16[64,8192]{1,0:T(8,128)(2,1)} %bitcast.16, s32[]{:T(128)S(6)} %add.169, s32[]{:T(128)S(6)} %select_n.31), kind=kLoop, calls=%fused_computation.11 | loop fusion | bytes 524296 | tf_op jit(solution)/shard_map/slice | solution.py:266
  37.5 20.5 %collective-permute-done.15 = bf16[64,2048]{1,0:T(8,128)(2,1)} collective-permute-done((bf16[64,2048]{1,0:T(8,128)(2,1)S(1)}, bf16[64,2048]{1,0:T(8,128)(2,1)}, u32[]{:S(2)}, u32[]{:S(2)}) %collective-permute-start.15) | collective-permute-done | bytes 262176 | tf_op jit(solution)/shard_map/ppermute | solution.py:19
  58.0 1.7 %fusion.2 = (bf16[64,1024]{1,0:T(8,128)(2,1)}, bf16[64,1024]{1,0:T(8,128)(2,1)S(1)}) fusion(bf16[64,2048]{1,0:T(8,128)(2,1)} %collective-permute-done.15), kind=kLoop, calls=%fused_computation.22 | loop fusion | bytes 524288 | tf_op jit(solution)/shard_map/slice | solution.py:266
  61.6 1.6 collective-permute-start.5
  63.2 2.4 %collective-permute-start.13 = (bf16[64,2048]{1,0:T(8,128)(2,1)}, bf16[64,2048]{1,0:T(8,128)(2,1)}, u32[]{:S(2)}, u32[]{:S(2)}) collective-permute-start(bf16[64,2048]{1,0:T(8,128)(2,1)} %collective-permute-done.11.refs_12_), channel_id=1, source_target_pairs={{0,4},{4,8},{8,12},{12,0},{1,5},{5,9},{9,13},{13,1},{2,6},{6,10},{... | collective-permute-start | bytes 786440 | tf_op jit(solution)/shard_map/ppermute | solution.py:25
  65.6 5.2 %collective-permute-done.17.refs_2_ = bf16[128,1024]{1,0:T(8,128)(2,1)S(1)} collective-permute-done((bf16[128,1024]{1,0:T(8,128)(2,1)S(1)}, bf16[128,1024]{1,0:T(8,128)(2,1)S(1)}, u32[]{:S(2)}, u32[]{:S(2)}) %collective-permute-start.17) | collective-permute-done | bytes 262176 | tf_op jit(solution)/shard_map/ppermute | solution.py:25
  73.5 3.1 %collective-permute-done.5.refs_6_ = bf16[64,2048]{1,0:T(8,128)(2,1)} collective-permute-done((bf16[64,2048]{1,0:T(8,128)(2,1)}, bf16[64,2048]{1,0:T(8,128)(2,1)}, u32[]{:S(2)}, u32[]{:S(2)}) %collective-permute-start.5) | collective-permute-done | bytes 262176 | tf_op jit(solution)/shard_map/ppermute | solution.py:25
  76.5 5.6 %collective-permute-done.13.refs_14_ = bf16[64,2048]{1,0:T(8,128)(2,1)} collective-permute-done((bf16[64,2048]{1,0:T(8,128)(2,1)}, bf16[64,2048]{1,0:T(8,128)(2,1)}, u32[]{:S(2)}, u32[]{:S(2)}) %collective-permute-start.13) | collective-permute-done | bytes 262176 | tf_op jit(solution)/shard_map/ppermute | solution.py:25
  84.1 1.7 %collective-permute-done.19.refs_4_ = bf16[128,1024]{1,0:T(8,128)(2,1)} collective-permute-done((bf16[128,1024]{1,0:T(8,128)(2,1)S(1)}, bf16[128,1024]{1,0:T(8,128)(2,1)}, u32[]{:S(2)}, u32[]{:S(2)}) %collective-permute-start.19) | collective-permute-done | bytes 262176 | tf_op jit(solution)/shard_map/ppermute | solution.py:25
  90.8 9.1 %down_product.1 = f32[4,128,128]{2,1,0:T(8,128)} custom-call(s32[16]{0:T(128)S(1)} %pad_add_fusion.labels_ref, bf16[4,128,2176]{2,1,0:T(8,128)(2,1)S(1)} %all-to-all-done.rows_ref, bf16[64,2048]{1,0:T(8,128)(2,1)S(1)} %get-tuple-element.10.refs_0_, bf16[64,2048]{1,0:T(8,128)(2,1)} %collective-permute-done.refs_1_, bf16[64,2048]{1,0:T(8,128)(2,1)S(1)} %copy-done.6, ...), custom_call_target="tpu_custom_call" | custom-call | flops 2147483648 | bytes 6291456 | tf_op jit(solution)/shard_map/down_product/pallas_call | solution.py:106
  99.9 3.7 %all-to-all-start.1 = ((f32[4,128,128]{2,1,0:T(8,128)}), f32[4,128,128]{2,1,0:T(8,128)S(1)}, u32[]{:S(2)}, u32[]{:S(2)}) async-start(f32[4,128,128]{2,1,0:T(8,128)} %down_product.1), calls=%async_computation.1 | async-start | bytes 524288 | tf_op jit(solution)/shard_map/all_to_all | solution.py:256
  103.7 6.0 %all-to-all-done.1 = f32[4,128,128]{2,1,0:T(8,128)S(1)} async-done(((f32[4,128,128]{2,1,0:T(8,128)}), f32[4,128,128]{2,1,0:T(8,128)S(1)}, u32[]{:S(2)}, u32[]{:S(2)}) %all-to-all-start.1) | async-done | bytes 262176 | tf_op jit(solution)/shard_map/all_to_all | solution.py:256
  110.4 1.4 broadcast_in_dim.8
  111.8 3.3 %all-to-all-start.2 = ((bf16[4,128,128]{2,1,0:T(8,128)(2,1)}), bf16[4,128,128]{2,1,0:T(8,128)(2,1)S(1)}, u32[]{:S(2)}, u32[]{:S(2)}) async-start(bf16[4,128,128]{2,1,0:T(8,128)(2,1)} %broadcast_in_dim.8), calls=%async_computation.2 | async-start | bytes 262144 | tf_op jit(solution)/shard_map/all_to_all | solution.py:258
  115.3 2.5 %collective-permute-start.26 = (bf16[128,1024]{1,0:T(8,128)(2,1)}, bf16[128,1024]{1,0:T(8,128)(2,1)}, u32[]{:S(2)}, u32[]{:S(2)}) collective-permute-start(bf16[128,1024]{1,0:T(8,128)(2,1)} %collective-permute-done.24.refs_2_), channel_id=1, source_target_pairs={{0,4},{4,8},{8,12},{12,0},{1,5},{5,9},{9,13},{13,1},{2,6},{6,10},{... | collective-permute-start | bytes 786440 | tf_op jit(solution)/shard_map/ppermute | solution.py:25
  117.8 2.3 %all-to-all-done.2.shrunk_ref = bf16[4,128,128]{2,1,0:T(8,128)(2,1)S(1)} async-done(((bf16[4,128,128]{2,1,0:T(8,128)(2,1)}), bf16[4,128,128]{2,1,0:T(8,128)(2,1)S(1)}, u32[]{:S(2)}, u32[]{:S(2)}) %all-to-all-start.2) | async-done | bytes 131104 | tf_op jit(solution)/shard_map/all_to_all | solution.py:258
  120.1 5.4 %up_product.2 = bf16[4,128,1024]{2,1,0:T(8,128)(2,1)} custom-call(s32[16]{0:T(128)S(1)} %add.153.labels_ref, bf16[4,128,2176]{2,1,0:T(8,128)(2,1)S(1)} %all-to-all-done.rows_ref, bf16[4,128,128]{2,1,0:T(8,128)(2,1)S(1)} %all-to-all-done.2.shrunk_ref, bf16[128,1024]{1,0:T(8,128)(2,1)S(1)} %pad_maximum_fusion.refs_0_, ...), custom_call_target="tpu_custom_call" | custom-call | flops 1073741824 | bytes 3145728 | tf_op jit(solution)/shard_map/up_product/pallas_call | solution.py:154
  125.5 3.5 %all-to-all-start.3 = ((bf16[4,128,1024]{2,1,0:T(8,128)(2,1)}), bf16[4,128,1024]{2,1,0:T(8,128)(2,1)S(1)}, u32[]{:S(2)}, u32[]{:S(2)}) async-start(bf16[4,128,1024]{2,1,0:T(8,128)(2,1)} %up_product.2), calls=%async_computation.3 | async-start | bytes 2097152 | tf_op jit(solution)/shard_map/all_to_all | solution.py:269
  129.1 2.5 %collective-permute-start.28 = (bf16[128,1024]{1,0:T(8,128)(2,1)}, bf16[128,1024]{1,0:T(8,128)(2,1)S(1)}, u32[]{:S(2)}, u32[]{:S(2)}) collective-permute-start(bf16[128,1024]{1,0:T(8,128)(2,1)} %collective-permute-done.26.refs_4_), channel_id=1, source_target_pairs={{0,4},{4,8},{8,12},{12,0},{1,5},{5,9},{9,13},{13,1},{2,6},{6,10},{... | collective-permute-start | bytes 786440 | tf_op jit(solution)/shard_map/ppermute | solution.py:25
  132.1 6.2 %collective-permute-done.28.refs_6_ = bf16[128,1024]{1,0:T(8,128)(2,1)S(1)} collective-permute-done((bf16[128,1024]{1,0:T(8,128)(2,1)}, bf16[128,1024]{1,0:T(8,128)(2,1)S(1)}, u32[]{:S(2)}, u32[]{:S(2)}) %collective-permute-start.28) | collective-permute-done | bytes 262176 | tf_op jit(solution)/shard_map/ppermute | solution.py:25
  138.3 1.5 collective-permute-done.29.refs_7_
  140.8 4.6 %up_product.3 = bf16[4,128,1024]{2,1,0:T(8,128)(2,1)S(1)} custom-call(s32[16]{0:T(128)S(1)} %add.153.labels_ref, bf16[4,128,2176]{2,1,0:T(8,128)(2,1)S(1)} %all-to-all-done.rows_ref, bf16[4,128,128]{2,1,0:T(8,128)(2,1)S(1)} %all-to-all-done.2.shrunk_ref, bf16[128,1024]{1,0:T(8,128)(2,1)S(1)} %copy-done.4, ...), custom_call_target="tpu_custom_call" | custom-call | flops 1073741824 | bytes 3145728 | tf_op jit(solution)/shard_map/up_product/pallas_call | solution.py:154
  146.4 18.3 %all_to_all.25.refs_1_ = bf16[4,128,1024]{2,1,0:T(8,128)(2,1)S(1)} all-to-all(bf16[4,128,1024]{2,1,0:T(8,128)(2,1)} %copy-done.1), channel_id=1, replica_groups=mesh['groups'=2,'outer'=4,'mid'=2,'cores'=2] {'groups','mid'}, dimensions={0} | all-to-all | bytes 2097152 | tf_op jit(solution)/shard_map/all_to_all | solution.py:269
  (87 shorter events, 20.3 us)
Async XLA Ops:
  1.1 9.3 %collective-permute-start.7 = (bf16[64,2048]{1,0:T(8,128)(2,1)S(1)}, bf16[64,2048]{1,0:T(8,128)(2,1)S(1)}, u32[]{:S(2)}, u32[]{:S(2)}) collective-permute-start(bf16[64,2048]{1,0:T(8,128)(2,1)S(1)} %get-tuple-element.9), channel_id=1, source_target_pairs={{0,2},{2,0},{1,3},{3,1},{4,6},{6,4},{5,7},{7,5},{8,10},{10,8},{9,1... | collective-permute-start | bytes 786440 | tf_op jit(solution)/shard_map/ppermute | solution.py:19
  10.4 9.4 %collective-permute-start.9 = (bf16[64,2048]{1,0:T(8,128)(2,1)S(1)}, bf16[64,2048]{1,0:T(8,128)(2,1)}, u32[]{:S(2)}, u32[]{:S(2)}) collective-permute-start(bf16[64,2048]{1,0:T(8,128)(2,1)S(1)} %collective-permute-done.7.refs_8_), channel_id=1, source_target_pairs={{0,4},{4,8},{8,12},{12,0},{1,5},{5,9},{9,13},{13,1},{2,6},{6,10},{... | collective-permute-start | bytes 786440 | tf_op jit(solution)/shard_map/ppermute | solution.py:25
  19.8 8.9 %collective-permute-start.11 = (bf16[64,2048]{1,0:T(8,128)(2,1)}, bf16[64,2048]{1,0:T(8,128)(2,1)}, u32[]{:S(2)}, u32[]{:S(2)}) collective-permute-start(bf16[64,2048]{1,0:T(8,128)(2,1)} %collective-permute-done.9.refs_10_), channel_id=1, source_target_pairs={{0,4},{4,8},{8,12},{12,0},{1,5},{5,9},{9,13},{13,1},{2,6},{6,10},{... | collective-permute-start | bytes 786440 | tf_op jit(solution)/shard_map/ppermute | solution.py:25
  23.7 64.2 %all-to-all-start = ((bf16[4,128,2176]{2,1,0:T(8,128)(2,1)}), bf16[4,128,2176]{2,1,0:T(8,128)(2,1)S(1)}, u32[]{:S(2)}, u32[]{:S(2)}) async-start(bf16[4,128,2176]{2,1,0:T(8,128)(2,1)} %copy-done), calls=%async_computation | async-start | bytes 4456448 | tf_op jit(solution)/shard_map/all_to_all | solution.py:253
  27.4 8.4 %collective-permute-start.1 = (bf16[64,2048]{1,0:T(8,128)(2,1)S(1)}, bf16[64,2048]{1,0:T(8,128)(2,1)S(1)}, u32[]{:S(2)}, u32[]{:S(2)}) collective-permute-start(bf16[64,2048]{1,0:T(8,128)(2,1)S(1)} %get-tuple-element.10.refs_0_), channel_id=1, source_target_pairs={{0,4},{4,8},{8,12},{12,0},{1,5},{5,9},{9,13},{13,1},{2,6},{6,10},{... | collective-permute-start | bytes 786440 | tf_op jit(solution)/shard_map/ppermute | solution.py:25
  29.6 28.4 %collective-permute-start.15 = (bf16[64,2048]{1,0:T(8,128)(2,1)S(1)}, bf16[64,2048]{1,0:T(8,128)(2,1)}, u32[]{:S(2)}, u32[]{:S(2)}) collective-permute-start(bf16[64,2048]{1,0:T(8,128)(2,1)S(1)} %constant_dynamic-slice_fusion.1), channel_id=1, source_target_pairs={{0,2},{2,0},{1,3},{3,1},{4,6},{6,4},{5,7},{7,5},{8,10},{10,8},{9,1... | collective-permute-start | bytes 786440 | tf_op jit(solution)/shard_map/ppermute | solution.py:19
  31.7 29.9 %collective-permute-start = (bf16[64,2048]{1,0:T(8,128)(2,1)S(1)}, bf16[64,2048]{1,0:T(8,128)(2,1)}, u32[]{:S(2)}, u32[]{:S(2)}) collective-permute-start(bf16[64,2048]{1,0:T(8,128)(2,1)S(1)} %get-tuple-element.10.refs_0_), channel_id=1, source_target_pairs={{0,1},{1,0},{2,3},{3,2},{4,5},{5,4},{6,7},{7,6},{8,9},{9,8},{10,11... | collective-permute-start | bytes 786440 | tf_op jit(solution)/shard_map/ppermute | solution.py:19
  35.7 27.4 %collective-permute-start.2 = (bf16[64,2048]{1,0:T(8,128)(2,1)S(1)}, bf16[64,2048]{1,0:T(8,128)(2,1)}, u32[]{:S(2)}, u32[]{:S(2)}) collective-permute-start(bf16[64,2048]{1,0:T(8,128)(2,1)S(1)} %collective-permute-done.1.refs_2_), channel_id=1, source_target_pairs={{0,1},{1,0},{2,3},{3,2},{4,5},{5,4},{6,7},{7,6},{8,9},{9,8},{10,11... | collective-permute-start | bytes 786440 | tf_op jit(solution)/shard_map/ppermute | solution.py:19
  35.7 25.3 %collective-permute-start.3 = (bf16[64,2048]{1,0:T(8,128)(2,1)S(1)}, bf16[64,2048]{1,0:T(8,128)(2,1)}, u32[]{:S(2)}, u32[]{:S(2)}) collective-permute-start(bf16[64,2048]{1,0:T(8,128)(2,1)S(1)} %collective-permute-done.1.refs_2_), channel_id=1, source_target_pairs={{0,4},{4,8},{8,12},{12,0},{1,5},{5,9},{9,13},{13,1},{2,6},{6,10},{... | collective-permute-start | bytes 786440 | tf_op jit(solution)/shard_map/ppermute | solution.py:25
  59.7 11.1 %collective-permute-start.17 = (bf16[128,1024]{1,0:T(8,128)(2,1)S(1)}, bf16[128,1024]{1,0:T(8,128)(2,1)S(1)}, u32[]{:S(2)}, u32[]{:S(2)}) collective-permute-start(bf16[128,1024]{1,0:T(8,128)(2,1)S(1)} %pad_maximum_fusion.refs_0_), channel_id=1, source_target_pairs={{0,4},{4,8},{8,12},{12,0},{1,5},{5,9},{9,13},{13,1},{2,6},{6,10},{... | collective-permute-start | bytes 786440 | tf_op jit(solution)/shard_map/ppermute | solution.py:25
  61.0 10.5 %collective-permute-start.8 = (bf16[64,2048]{1,0:T(8,128)(2,1)S(1)}, bf16[64,2048]{1,0:T(8,128)(2,1)S(1)}, u32[]{:S(2)}, u32[]{:S(2)}) collective-permute-start(bf16[64,2048]{1,0:T(8,128)(2,1)S(1)} %collective-permute-done.7.refs_8_), channel_id=1, source_target_pairs={{0,1},{1,0},{2,3},{3,2},{4,5},{5,4},{6,7},{7,6},{8,9},{9,8},{10,11... | collective-permute-start | bytes 786440 | tf_op jit(solution)/shard_map/ppermute | solution.py:19
  61.1 11.2 %collective-permute-start.4 = (bf16[64,2048]{1,0:T(8,128)(2,1)}, bf16[64,2048]{1,0:T(8,128)(2,1)S(1)}, u32[]{:S(2)}, u32[]{:S(2)}) collective-permute-start(bf16[64,2048]{1,0:T(8,128)(2,1)} %collective-permute-done.3.refs_4_), channel_id=1, source_target_pairs={{0,1},{1,0},{2,3},{3,2},{4,5},{5,4},{6,7},{7,6},{8,9},{9,8},{10,11... | collective-permute-start | bytes 786440 | tf_op jit(solution)/shard_map/ppermute | solution.py:19
  61.6 15.0 %collective-permute-start.5 = (bf16[64,2048]{1,0:T(8,128)(2,1)}, bf16[64,2048]{1,0:T(8,128)(2,1)}, u32[]{:S(2)}, u32[]{:S(2)}) collective-permute-start(bf16[64,2048]{1,0:T(8,128)(2,1)} %collective-permute-done.3.refs_4_), channel_id=1, source_target_pairs={{0,4},{4,8},{8,12},{12,0},{1,5},{5,9},{9,13},{13,1},{2,6},{6,10},{... | collective-permute-start | bytes 786440 | tf_op jit(solution)/shard_map/ppermute | solution.py:25
  63.2 19.0 %collective-permute-start.13 = (bf16[64,2048]{1,0:T(8,128)(2,1)}, bf16[64,2048]{1,0:T(8,128)(2,1)}, u32[]{:S(2)}, u32[]{:S(2)}) collective-permute-start(bf16[64,2048]{1,0:T(8,128)(2,1)} %collective-permute-done.11.refs_12_), channel_id=1, source_target_pairs={{0,4},{4,8},{8,12},{12,0},{1,5},{5,9},{9,13},{13,1},{2,6},{6,10},{... | collective-permute-start | bytes 786440 | tf_op jit(solution)/shard_map/ppermute | solution.py:25
  70.8 15.0 %collective-permute-start.19 = (bf16[128,1024]{1,0:T(8,128)(2,1)S(1)}, bf16[128,1024]{1,0:T(8,128)(2,1)}, u32[]{:S(2)}, u32[]{:S(2)}) collective-permute-start(bf16[128,1024]{1,0:T(8,128)(2,1)S(1)} %collective-permute-done.17.refs_2_), channel_id=1, source_target_pairs={{0,4},{4,8},{8,12},{12,0},{1,5},{5,9},{9,13},{13,1},{2,6},{6,10},{... | collective-permute-start | bytes 786440 | tf_op jit(solution)/shard_map/ppermute | solution.py:25
  72.2 14.6 %collective-permute-start.10 = (bf16[64,2048]{1,0:T(8,128)(2,1)}, bf16[64,2048]{1,0:T(8,128)(2,1)}, u32[]{:S(2)}, u32[]{:S(2)}) collective-permute-start(bf16[64,2048]{1,0:T(8,128)(2,1)} %collective-permute-done.9.refs_10_), channel_id=1, source_target_pairs={{0,1},{1,0},{2,3},{3,2},{4,5},{5,4},{6,7},{7,6},{8,9},{9,8},{10,11... | collective-permute-start | bytes 786440 | tf_op jit(solution)/shard_map/ppermute | solution.py:19
  73.0 14.4 %collective-permute-start.12 = (bf16[64,2048]{1,0:T(8,128)(2,1)}, bf16[64,2048]{1,0:T(8,128)(2,1)}, u32[]{:S(2)}, u32[]{:S(2)}) collective-permute-start(bf16[64,2048]{1,0:T(8,128)(2,1)} %collective-permute-done.11.refs_12_), channel_id=1, source_target_pairs={{0,1},{1,0},{2,3},{3,2},{4,5},{5,4},{6,7},{7,6},{8,9},{9,8},{10,11... | collective-permute-start | bytes 786440 | tf_op jit(solution)/shard_map/ppermute | solution.py:19
  76.5 10.4 %collective-permute-start.6 = (bf16[64,2048]{1,0:T(8,128)(2,1)}, bf16[64,2048]{1,0:T(8,128)(2,1)}, u32[]{:S(2)}, u32[]{:S(2)}) collective-permute-start(bf16[64,2048]{1,0:T(8,128)(2,1)} %collective-permute-done.5.refs_6_), channel_id=1, source_target_pairs={{0,1},{1,0},{2,3},{3,2},{4,5},{5,4},{6,7},{7,6},{8,9},{9,8},{10,11... | collective-permute-start | bytes 786440 | tf_op jit(solution)/shard_map/ppermute | solution.py:19
  85.8 17.8 %collective-permute-start.21 = (bf16[128,1024]{1,0:T(8,128)(2,1)}, bf16[128,1024]{1,0:T(8,128)(2,1)}, u32[]{:S(2)}, u32[]{:S(2)}) collective-permute-start(bf16[128,1024]{1,0:T(8,128)(2,1)} %collective-permute-done.19.refs_4_), channel_id=1, source_target_pairs={{0,4},{4,8},{8,12},{12,0},{1,5},{5,9},{9,13},{13,1},{2,6},{6,10},{... | collective-permute-start | bytes 786440 | tf_op jit(solution)/shard_map/ppermute | solution.py:25
  86.8 31.0 %collective-permute-start.16 = (bf16[128,1024]{1,0:T(8,128)(2,1)S(1)}, bf16[128,1024]{1,0:T(8,128)(2,1)}, u32[]{:S(2)}, u32[]{:S(2)}) collective-permute-start(bf16[128,1024]{1,0:T(8,128)(2,1)S(1)} %pad_maximum_fusion.refs_0_), channel_id=1, source_target_pairs={{0,1},{1,0},{2,3},{3,2},{4,5},{5,4},{6,7},{7,6},{8,9},{9,8},{10,11... | collective-permute-start | bytes 786440 | tf_op jit(solution)/shard_map/ppermute | solution.py:19
  86.9 28.4 %collective-permute-start.24 = (bf16[128,1024]{1,0:T(8,128)(2,1)S(1)}, bf16[128,1024]{1,0:T(8,128)(2,1)}, u32[]{:S(2)}, u32[]{:S(2)}) collective-permute-start(bf16[128,1024]{1,0:T(8,128)(2,1)S(1)} %pad_maximum_fusion.1.refs_0_), channel_id=1, source_target_pairs={{0,4},{4,8},{8,12},{12,0},{1,5},{5,9},{9,13},{13,1},{2,6},{6,10},{... | collective-permute-start | bytes 786440 | tf_op jit(solution)/shard_map/ppermute | solution.py:25
  87.4 30.4 %collective-permute-start.18 = (bf16[128,1024]{1,0:T(8,128)(2,1)S(1)}, bf16[128,1024]{1,0:T(8,128)(2,1)}, u32[]{:S(2)}, u32[]{:S(2)}) collective-permute-start(bf16[128,1024]{1,0:T(8,128)(2,1)S(1)} %collective-permute-done.17.refs_2_), channel_id=1, source_target_pairs={{0,1},{1,0},{2,3},{3,2},{4,5},{5,4},{6,7},{7,6},{8,9},{9,8},{10,11... | collective-permute-start | bytes 786440 | tf_op jit(solution)/shard_map/ppermute | solution.py:19
  87.5 30.3 %collective-permute-start.20 = (bf16[128,1024]{1,0:T(8,128)(2,1)}, bf16[128,1024]{1,0:T(8,128)(2,1)}, u32[]{:S(2)}, u32[]{:S(2)}) collective-permute-start(bf16[128,1024]{1,0:T(8,128)(2,1)} %collective-permute-done.19.refs_4_), channel_id=1, source_target_pairs={{0,1},{1,0},{2,3},{3,2},{4,5},{5,4},{6,7},{7,6},{8,9},{9,8},{10,11... | collective-permute-start | bytes 786440 | tf_op jit(solution)/shard_map/ppermute | solution.py:19
  99.9 9.9 %all-to-all-start.1 = ((f32[4,128,128]{2,1,0:T(8,128)}), f32[4,128,128]{2,1,0:T(8,128)S(1)}, u32[]{:S(2)}, u32[]{:S(2)}) async-start(f32[4,128,128]{2,1,0:T(8,128)} %down_product.1), calls=%async_computation.1 | async-start | bytes 524288 | tf_op jit(solution)/shard_map/all_to_all | solution.py:256
  103.6 16.5 %collective-permute-start.22 = (bf16[128,1024]{1,0:T(8,128)(2,1)}, bf16[128,1024]{1,0:T(8,128)(2,1)S(1)}, u32[]{:S(2)}, u32[]{:S(2)}) collective-permute-start(bf16[128,1024]{1,0:T(8,128)(2,1)} %collective-permute-done.21.refs_6_), channel_id=1, source_target_pairs={{0,1},{1,0},{2,3},{3,2},{4,5},{5,4},{6,7},{7,6},{8,9},{9,8},{10,11... | collective-permute-start | bytes 786440 | tf_op jit(solution)/shard_map/ppermute | solution.py:19
  111.8 8.3 %all-to-all-start.2 = ((bf16[4,128,128]{2,1,0:T(8,128)(2,1)}), bf16[4,128,128]{2,1,0:T(8,128)(2,1)S(1)}, u32[]{:S(2)}, u32[]{:S(2)}) async-start(bf16[4,128,128]{2,1,0:T(8,128)(2,1)} %broadcast_in_dim.8), calls=%async_computation.2 | async-start | bytes 262144 | tf_op jit(solution)/shard_map/all_to_all | solution.py:258
  115.3 13.8 %collective-permute-start.26 = (bf16[128,1024]{1,0:T(8,128)(2,1)}, bf16[128,1024]{1,0:T(8,128)(2,1)}, u32[]{:S(2)}, u32[]{:S(2)}) collective-permute-start(bf16[128,1024]{1,0:T(8,128)(2,1)} %collective-permute-done.24.refs_2_), channel_id=1, source_target_pairs={{0,4},{4,8},{8,12},{12,0},{1,5},{5,9},{9,13},{13,1},{2,6},{6,10},{... | collective-permute-start | bytes 786440 | tf_op jit(solution)/shard_map/ppermute | solution.py:25
  125.5 20.9 %all-to-all-start.3 = ((bf16[4,128,1024]{2,1,0:T(8,128)(2,1)}), bf16[4,128,1024]{2,1,0:T(8,128)(2,1)S(1)}, u32[]{:S(2)}, u32[]{:S(2)}) async-start(bf16[4,128,1024]{2,1,0:T(8,128)(2,1)} %up_product.2), calls=%async_computation.3 | async-start | bytes 2097152 | tf_op jit(solution)/shard_map/all_to_all | solution.py:269
  129.1 9.2 %collective-permute-start.28 = (bf16[128,1024]{1,0:T(8,128)(2,1)}, bf16[128,1024]{1,0:T(8,128)(2,1)S(1)}, u32[]{:S(2)}, u32[]{:S(2)}) collective-permute-start(bf16[128,1024]{1,0:T(8,128)(2,1)} %collective-permute-done.26.refs_4_), channel_id=1, source_target_pairs={{0,4},{4,8},{8,12},{12,0},{1,5},{5,9},{9,13},{13,1},{2,6},{6,10},{... | collective-permute-start | bytes 786440 | tf_op jit(solution)/shard_map/ppermute | solution.py:25
  131.6 6.7 %collective-permute-start.23 = (bf16[128,1024]{1,0:T(8,128)(2,1)}, bf16[128,1024]{1,0:T(8,128)(2,1)S(1)}, u32[]{:S(2)}, u32[]{:S(2)}) collective-permute-start(bf16[128,1024]{1,0:T(8,128)(2,1)} %copy-done.3), channel_id=1, source_target_pairs={{0,1},{1,0},{2,3},{3,2},{4,5},{5,4},{6,7},{7,6},{8,9},{9,8},{10,11... | collective-permute-start | bytes 786440 | tf_op jit(solution)/shard_map/ppermute | solution.py:19
  131.6 6.7 %collective-permute-start.25 = (bf16[128,1024]{1,0:T(8,128)(2,1)}, bf16[128,1024]{1,0:T(8,128)(2,1)S(1)}, u32[]{:S(2)}, u32[]{:S(2)}) collective-permute-start(bf16[128,1024]{1,0:T(8,128)(2,1)} %collective-permute-done.24.refs_2_), channel_id=1, source_target_pairs={{0,1},{1,0},{2,3},{3,2},{4,5},{5,4},{6,7},{7,6},{8,9},{9,8},{10,11... | collective-permute-start | bytes 786440 | tf_op jit(solution)/shard_map/ppermute | solution.py:19
  132.1 6.2 %collective-permute-start.27 = (bf16[128,1024]{1,0:T(8,128)(2,1)}, bf16[128,1024]{1,0:T(8,128)(2,1)S(1)}, u32[]{:S(2)}, u32[]{:S(2)}) collective-permute-start(bf16[128,1024]{1,0:T(8,128)(2,1)} %collective-permute-done.26.refs_4_), channel_id=1, source_target_pairs={{0,1},{1,0},{2,3},{3,2},{4,5},{5,4},{6,7},{7,6},{8,9},{9,8},{10,11... | collective-permute-start | bytes 786440 | tf_op jit(solution)/shard_map/ppermute | solution.py:19
  (14 other events, 122.8 us)

commit v5 on v1

v5 whole, which is shorter than its diff:
```python
import functools

import jax
import jax.numpy as jnp
from jax import lax
from jax.experimental import pallas as pl
from jax.experimental.pallas import tpu as pltpu
from jax.sharding import Mesh
from jax.sharding import PartitionSpec as P

adapter_scale = 2.0
PLANE = ("groups", "inner")
LANES = 128
ID_ROWS = 8
BLOCK = 8
VMEM_BYTES = 48 << 20
IN_VMEM = pl.BlockSpec(memory_space=pltpu.VMEM)
IN_SMEM = pl.BlockSpec(memory_space=pltpu.SMEM)
ANYWHERE = pl.BlockSpec(memory_space=pl.ANY)
PARAMS = pltpu.CompilerParams(vmem_limit_bytes=VMEM_BYTES)


def to_partner(value, axes, size, offset):
    return lax.ppermute(value, axes, [(i, i ^ offset) for i in range(size)])


def next_on_ring(block, outer):
    return lax.ppermute(block, "outer", [(i, (i + 1) % outer) for i in range(outer)])


def after(value, *earlier):
    return lax.optimization_barrier((value,) + earlier)[0]


def swap(value):
    return lax.all_to_all(value, PLANE, split_axis=0, concat_axis=0, tiled=True)


def tile_labels(labels_ref, tile, rank, shape):
    per_tile = LANES // rank
    lane = lax.broadcasted_iota(jnp.int32, shape, 1)
    label = jnp.full(shape, labels_ref[tile * per_tile], jnp.int32)
    for n in range(1, per_tile):
        label = jnp.where(lane >= n * rank, labels_ref[tile * per_tile + n], label)
    return label.astype(jnp.float32)


def outgoing_kernel(hidden_ref, ids_ref, out_ref):
    members, rows, share = out_ref.shape
    tok = rows - ID_ROWS
    for member in range(members):
        out_ref[member, :tok, :] = hidden_ref[:, member * share : (member + 1) * share]
        out_ref[member, tok:, :] = ids_ref[...]


def outgoing_rows(hidden, ids, members):
    tok, width = hidden.shape
    share = width // members
    ids = jnp.broadcast_to(jnp.pad(ids, ((0, 0), (0, share - tok))), (ID_ROWS, share))
    return pl.pallas_call(
        outgoing_kernel,
        out_shape=jax.ShapeDtypeStruct((members, tok + ID_ROWS, share), jnp.bfloat16),
        in_specs=[IN_VMEM, IN_VMEM],
        out_specs=IN_VMEM,
        compiler_params=PARAMS,
        name="outgoing_rows",
    )(hidden, ids)


def down_kernel(map_count, rank, labels_ref, rows_ref, *refs):
    maps, (packed_ref, ids_ref, total_ref) = refs[:map_count], refs[map_count:]
    members, rows, share = rows_ref.shape
    tok = rows - ID_ROWS
    block = min(BLOCK, members)
    half = tok // 2
    lane = lax.broadcasted_iota(jnp.int32, (half, LANES), 1)

    def one(step, _):
        first = step * block
        for n in range(block):
            row = rows_ref[first + n, tok : tok + 1, :LANES].astype(jnp.float32)
            ids_ref[first + n] = jnp.broadcast_to(row, (LANES, tok)).T
        tokens = rows_ref[pl.ds(first, block), :tok, :].reshape(block * tok, share)
        ids = ids_ref[pl.ds(first, block)].reshape(block * tok, LANES)
        tile = 0
        for at in range(0, map_count, 2):
            some = jnp.concatenate([m[...] for m in maps[at : at + 2]], axis=0)
            product = lax.dot_general(
                tokens, some, (((1,), (1,)), ((), ())), preferred_element_type=jnp.float32
            )
            total = jnp.zeros((block * tok, LANES), jnp.float32) if tile == 0 else total_ref[...]
            for n in range(some.shape[0] // LANES):
                named = ids == tile_labels(labels_ref, tile, rank, (1, LANES))
                total += jnp.where(named, product[:, n * LANES : (n + 1) * LANES], 0.0)
                tile += 1
            total_ref[...] = total
        for n in range(block):
            total = total_ref[n * tok : (n + 1) * tok, :]
            total += pltpu.roll(total, LANES // 2, 1)
            packed_ref[first + n] = jnp.where(lane < rank, total[:half], total[half:])
        return 0

    lax.fori_loop(0, members // block, one, 0)


def down_product(labels, rows, maps, rank):
    members, tok, share = rows.shape
    tok -= ID_ROWS
    map_rows = sum(m.shape[0] for m in maps)
    return pl.pallas_call(
        functools.partial(down_kernel, len(maps), rank),
        out_shape=[
            jax.ShapeDtypeStruct((members, tok // 2, LANES), jnp.float32),
            jax.ShapeDtypeStruct((members, tok, LANES), jnp.float32),
        ],
        in_specs=[IN_SMEM, IN_VMEM] + [IN_VMEM] * len(maps),
        out_specs=[IN_VMEM, IN_VMEM],
        scratch_shapes=[pltpu.VMEM((min(BLOCK, members) * tok, LANES), jnp.float32)],
        compiler_params=PARAMS,
        cost_estimate=pl.CostEstimate(
            flops=2 * map_rows * members * tok * share,
            bytes_accessed=2 * share * (map_rows + members * tok),
            transcendentals=0,
        ),
        name="down_product",
    )(labels, rows, *maps)


def copies_kernel(terms_ref, out_ref):
    own = jnp.sum(terms_ref[...], axis=0).astype(jnp.bfloat16)
    for member in range(out_ref.shape[0]):
        out_ref[member] = own


def summed_copies(terms):
    return pl.pallas_call(
        copies_kernel,
        out_shape=jax.ShapeDtypeStruct(terms.shape, jnp.bfloat16),
        in_specs=[IN_VMEM],
        out_specs=IN_VMEM,
        compiler_params=PARAMS,
        name="summed_copies",
    )(terms)


def up_kernel(map_count, rank, labels_ref, ids_ref, shrunk_ref, *refs):
    maps, (out_ref, spread_ref) = refs[:map_count], refs[map_count:]
    members, half, _ = shrunk_ref.shape
    tok = 2 * half
    block = min(BLOCK, members)
    tiles = spread_ref.shape[1] // LANES
    lane = lax.broadcasted_iota(jnp.int32, (half, LANES), 1)
    held = jnp.concatenate([m[...] for m in maps], axis=0)

    def one(step, _):
        first = step * block
        for n in range(block):
            packed = shrunk_ref[first + n].astype(jnp.float32)
            turned = pltpu.roll(packed, LANES // 2, 1)
            shrunk = jnp.concatenate(
                [jnp.where(lane < rank, packed, turned), jnp.where(lane < rank, turned, packed)], axis=0
            )
            ids = ids_ref[first + n]
            for tile in range(tiles):
                named = ids == tile_labels(labels_ref, tile, rank, (1, LANES))
                spread_ref[n * tok : (n + 1) * tok, tile * LANES : (tile + 1) * LANES] = jnp.where(
                    named, shrunk, 0.0
                ).astype(jnp.bfloat16)
        product = jnp.dot(spread_ref[...], held, preferred_element_type=jnp.float32)
        product = (adapter_scale * product).astype(jnp.bfloat16)
        out_ref[pl.ds(first, block)] = product.reshape(block, tok, product.shape[1])
        return 0

    lax.fori_loop(0, members // block, one, 0)


def up_product(labels, ids, shrunk, maps, rank):
    members, tok, _ = ids.shape
    map_rows, piece = sum(m.shape[0] for m in maps), maps[0].shape[1]
    return pl.pallas_call(
        functools.partial(up_kernel, len(maps), rank),
        out_shape=jax.ShapeDtypeStruct((members, tok, piece), jnp.bfloat16),
        in_specs=[IN_SMEM, IN_VMEM, IN_VMEM] + [IN_VMEM] * len(maps),
        out_specs=IN_VMEM,
        scratch_shapes=[pltpu.VMEM((min(BLOCK, members) * tok, map_rows), jnp.bfloat16)],
        compiler_params=PARAMS,
        cost_estimate=pl.CostEstimate(
            flops=2 * map_rows * members * tok * piece,
            bytes_accessed=2 * piece * (map_rows + members * tok),
            transcendentals=0,
        ),
        name="up_product",
    )(labels, ids, shrunk, *maps)


def place_kernel(pieces, *refs):
    parts, out_ref, sems = refs[:pieces], refs[-2], refs[-1]
    members, _, piece = parts[0].shape
    copies = []
    for n in range(members * pieces):
        member, part = n // pieces, n % pieces
        target = out_ref.at[:, pl.ds(n * piece, piece)]
        copies.append(pltpu.make_async_copy(parts[part].at[member], target, sems.at[n]))
    for copy in copies:
        copy.start()
    for copy in copies:
        copy.wait()


def place(parts):
    members, tok, piece = parts[0].shape
    return pl.pallas_call(
        functools.partial(place_kernel, len(parts)),
        out_shape=jax.ShapeDtypeStruct((tok, members * len(parts) * piece), jnp.bfloat16),
        in_specs=[ANYWHERE] * len(parts),
        out_specs=ANYWHERE,
        scratch_shapes=[pltpu.SemaphoreType.DMA((members * len(parts),))],
        compiler_params=PARAMS,
        name="place_results",
    )(*parts)


def per_device(token_adapter_index, hidden, adapter_down_maps, adapter_up_maps):
    tok, width = hidden.shape
    groups, outer, inner = (lax.axis_size(a) for a in ("groups", "outer", "inner"))
    group, level, place_in_group = (lax.axis_index(a) for a in ("groups", "outer", "inner"))
    members = groups * inner
    share = width // members
    rank = adapter_up_maps.shape[1]
    pieces = 2 if share % (2 * LANES) == 0 else 1
    piece = share // pieces
    me = group * inner + place_in_group

    def slices(array):
        return [
            lax.dynamic_slice_in_dim(array, (me ^ offset) * share, share, axis=1) for offset in range(inner)
        ]

    def exchanged(blocks):
        return blocks[:1] + [to_partner(blocks[n], "inner", inner, n) for n in range(1, inner)]

    steps_back = jnp.arange(outer, dtype=jnp.int32)[:, None]
    labels = ((level - steps_back + outer) % outer) * inner + (
        place_in_group ^ jnp.arange(inner, dtype=jnp.int32)[None, :]
    )
    labels = labels.reshape(-1)

    down = exchanged(slices(adapter_down_maps[0].T))
    near = [jnp.concatenate(down[: inner // 2], axis=0)]
    far = [jnp.concatenate(down[inner // 2 :], axis=0)]
    for _ in range(outer - 1):
        near.append(next_on_ring(near[-1], outer))
        far.append(next_on_ring(far[-1], outer))
    down_maps = [m for pair in zip(near, far) for m in pair]

    ids = token_adapter_index.astype(jnp.bfloat16).reshape(1, tok)
    rows = swap(after(outgoing_rows(hidden, ids, members), *down[inner // 2 :]))

    own_slices = slices(adapter_up_maps[0])
    up = exchanged([after(block, rows) for block in own_slices])
    held = [
        [jnp.concatenate([b[:, n * piece : (n + 1) * piece] for b in up], axis=0)] for n in range(pieces)
    ]
    held[0][0] = after(held[0][0], near[-1])
    held[-1][0] = after(held[-1][0], far[-1])
    for ring in held:
        for _ in range(outer - 1):
            ring.append(next_on_ring(ring[-1], outer))

    packed, id_columns = down_product(labels, rows, down_maps, rank)
    shrunk = swap(summed_copies(swap(packed)))
    return place([swap(up_product(labels, id_columns, shrunk, ring, rank)) for ring in held])


def solution(mesh):
    groups, wide = mesh.shape["groups"], mesh.shape["wide"]
    outer = 1 << ((wide.bit_length() - 1) // 2)
    fine = Mesh(mesh.devices.reshape(groups, outer, wide // outer), ("groups", "outer", "inner"))
    owner = ("outer", "inner")
    rows = P(("groups",) + owner, None)
    return jax.shard_map(
        per_device,
        mesh=fine,
        in_specs=(rows, rows, P(owner, None, None), P(owner, None, None)),
        out_specs=rows,
        check_vma=False,
    )
```

time: 157 us -> 146 us (0.930)
  blocking collectives: 112 us -> 25.7 us
  waiting for transfers between devices: 5.51 us -> 74.9 us
  starting transfers between devices: 3.78 us -> 22 us
  between operations: 13.5 us -> 0.14 us
  Pallas kernels: 0 us -> 13.1 us
  matrix products: 8.74 us -> 0 us
  local copies, waits for them, and re-layouts: 12.7 us -> 9.05 us
    ppermute x0 -> x18, waiting for transfers between devices: none -> 69.8 us  [the longest x12 61 us: next_on_ring(): lax.ppermute(block, 'outer', [(i, (i + 1) % outer) for i in range(outer)])]
    all_gather x1 -> x0, blocking collectives: 29.5 us -> none  [per_device(): ids = lax.all_gather(token_adapter_index[:, 0], PLANE, axis=0, tiled=True)]
    all_to_all x3 -> x2, blocking collectives: 54.4 us -> 25.7 us  [swap(): return lax.all_to_all(value, PLANE, split_axis=0, concat_axis=0, tiled=True)]
    psum x1 -> x0, blocking collectives: 28 us -> none  [per_device(): shrunk = lax.psum(partial, PLANE).astype(jnp.bfloat16)]
    pallas_call x0 -> x6, Pallas kernels: none -> 13.1 us  [the longest x2 5.8 us: up_product(): pl.pallas_call(functools.partial(up_kernel, len(maps), rank), out_shape=j...]
    ppermute x0 -> x18, starting transfers between devices: none -> 11.1 us  [the longest x12 5.6 us: next_on_ring(): lax.ppermute(block, 'outer', [(i, (i + 1) % outer) for i in range(outer)])]
    dot_general x2 -> x0, matrix products: 8.74 us -> none  [the longest x1 4.78 us: per_device(): lax.dot_general(down.reshape(adapters * rank, share), rows, (((1,), (1,))...]
    all_to_all x1 -> x3, starting transfers between devices: 3.74 us -> 11 us  [swap(): return lax.all_to_all(value, PLANE, split_axis=0, concat_axis=0, tiled=True)]
  transfers between devices with their start and end apart: 3 -> 21, of which waited for: 1 -> 15; matrix products, arithmetic and copies ran while one was open for 9% -> 4% of each run, Pallas kernels for 0% -> 6%
where the time goes in v5:
time: 146 us
  waiting for transfers between devices  74.9 us (51%)
  blocking collectives  25.7 us (18%)
  starting transfers between devices  22 us (15%)
  Pallas kernels  13.1 us (9%)
  local copies, waits for them, and re-layouts  9.05 us (6%)
    ppermute x12, waiting for transfers between devices, next_on_ring(): lax.ppermute(block, 'outer', [(i, (i + 1) % outer) for i in range(outer)])  61 us
    all_to_all x2, blocking collectives, swap(): return lax.all_to_all(value, PLANE, split_axis=0, concat_axis=0, tiled=True)  25.7 us
    all_to_all x3, starting transfers between devices, swap(): return lax.all_to_all(value, PLANE, split_axis=0, concat_axis=0, tiled=True)  11 us
    ppermute x6, waiting for transfers between devices, to_partner(): return lax.ppermute(value, axes, [(i, i ^ offset) for i in range(size)])  8.79 us
    pallas_call x2, Pallas kernels, up_product(): pl.pallas_call(functools.partial(up_kernel, len(maps), rank), out_shape=j...  5.8 us
    ppermute x12, starting transfers between devices, next_on_ring(): lax.ppermute(block, 'outer', [(i, (i + 1) % outer) for i in range(outer)])  5.6 us
    ppermute x6, starting transfers between devices, to_partner(): return lax.ppermute(value, axes, [(i, i ^ offset) for i in range(size)])  5.45 us
    all_to_all x3, waiting for transfers between devices, swap(): return lax.all_to_all(value, PLANE, split_axis=0, concat_axis=0, tiled=True)  5.06 us
  transfers between devices with their start and end apart: 21, of which 15 were waited for; matrix products, arithmetic and copies ran while one was open for 4% of the time, Pallas kernels for 6%

profile of v5, /device:TPU:0, one launch (start us, length us, event | category | flops | bytes accessed | tf_op | source)
XLA Modules:
  0.0 145.7 jit_solution(7608205646161775416)
XLA Ops:
  0.0 1.1 dynamic-slice_bitcast_fusion.5
  1.1 3.0 %collective-permute-start = (bf16[64,1024]{1,0:T(8,128)(2,1)S(1)}, bf16[64,1024]{1,0:T(8,128)(2,1)S(1)}, u32[]{:S(2)}, u32[]{:S(2)}) collective-permute-start(bf16[64,1024]{1,0:T(8,128)(2,1)S(1)} %get-tuple-element.29), channel_id=1, source_target_pairs={{0,2},{1,3},{2,0},{3,1},{4,6},{5,7},{6,4},{7,5},{8,10},{9,11},{10,... | collective-permute-start | bytes 393224 | tf_op jit(solution)/shard_map/ppermute | solution.py:24
  4.9 1.6 %copy-done = bf16[128,8192]{1,0:T(8,128)(2,1)S(1)} copy-done((bf16[128,8192]{1,0:T(8,128)(2,1)S(1)}, bf16[128,8192]{1,0:T(8,128)(2,1)}, u32[]{:S(2)}) %copy-start) | copy-done | bytes 2097176
  6.5 1.5 %outgoing_rows.1 = bf16[8,136,1024]{2,1,0:T(8,128)(2,1)} custom-call(bf16[128,8192]{1,0:T(8,128)(2,1)S(1)} %copy-done, bf16[8,1024]{1,0:T(8,128)(2,1)S(1)} %broadcast_in_dim.10.ids_ref), custom_call_target="tpu_custom_call" | custom-call | tf_op jit(solution)/shard_map/outgoing_rows/pallas_call | solution.py:60
  8.1 1.9 %collective-permute-done.1 = bf16[64,1024]{1,0:T(8,128)(2,1)S(1)} collective-permute-done((bf16[64,1024]{1,0:T(8,128)(2,1)S(1)}, bf16[64,1024]{1,0:T(8,128)(2,1)S(1)}, u32[]{:S(2)}, u32[]{:S(2)}) %collective-permute-start.1) | collective-permute-done | bytes 131104 | tf_op jit(solution)/shard_map/ppermute | solution.py:24
  10.0 3.8 %all-to-all-start = ((bf16[8,136,1024]{2,1,0:T(8,128)(2,1)}), bf16[8,136,1024]{2,1,0:T(8,128)(2,1)S(1)}, u32[]{:S(2)}, u32[]{:S(2)}) async-start(bf16[8,136,1024]{2,1,0:T(8,128)(2,1)} %outgoing_rows.1), calls=%async_computation | async-start | bytes 4456448 | tf_op jit(solution)/shard_map/all_to_all | solution.py:36
  14.3 1.1 collective-permute-done.2
  15.5 1.6 %collective-permute-start.3 = (bf16[128,1024]{1,0:T(8,128)(2,1)S(1)}, bf16[128,1024]{1,0:T(8,128)(2,1)S(1)}, u32[]{:S(2)}, u32[]{:S(2)}) collective-permute-start(bf16[128,1024]{1,0:T(8,128)(2,1)S(1)} %pad_maximum_fusion.refs_0_), channel_id=1, source_target_pairs={{0,4},{4,8},{8,12},{12,0},{1,5},{5,9},{9,13},{13,1},{2,6},{6,10},{... | collective-permute-start | bytes 786440 | tf_op jit(solution)/shard_map/ppermute | solution.py:28
  17.1 1.6 %collective-permute-start.4 = (bf16[128,1024]{1,0:T(8,128)(2,1)S(1)}, bf16[128,1024]{1,0:T(8,128)(2,1)S(1)}, u32[]{:S(2)}, u32[]{:S(2)}) collective-permute-start(bf16[128,1024]{1,0:T(8,128)(2,1)S(1)} %constant_dynamic-update-slice_fusion.refs_1_), channel_id=1, source_target_pairs={{0,4},{4,8},{8,12},{12,0},{1,5},{5,9},{9,13},{13,1},{2,6},{6,10},{... | collective-permute-start | bytes 786440 | tf_op jit(solution)/shard_map/ppermute | solution.py:28
  18.8 7.7 %collective-permute-done.3.refs_2_ = bf16[128,1024]{1,0:T(8,128)(2,1)S(1)} collective-permute-done((bf16[128,1024]{1,0:T(8,128)(2,1)S(1)}, bf16[128,1024]{1,0:T(8,128)(2,1)S(1)}, u32[]{:S(2)}, u32[]{:S(2)}) %collective-permute-start.3) | collective-permute-done | bytes 262176 | tf_op jit(solution)/shard_map/ppermute | solution.py:28
  26.5 5.6 %collective-permute-done.4.refs_3_ = bf16[128,1024]{1,0:T(8,128)(2,1)S(1)} collective-permute-done((bf16[128,1024]{1,0:T(8,128)(2,1)S(1)}, bf16[128,1024]{1,0:T(8,128)(2,1)S(1)}, u32[]{:S(2)}, u32[]{:S(2)}) %collective-permute-start.4) | collective-permute-done | bytes 262176 | tf_op jit(solution)/shard_map/ppermute | solution.py:28
  32.1 1.8 %dynamic-slice_bitcast_fusion.3 = (bf16[64,1024]{1,0:T(8,128)(2,1)S(1)}, bf16[64,1024]{1,0:T(8,128)(2,1)}, bf16[64,1024]{1,0:T(8,128)(2,1)}, bf16[64,1024]{1,0:T(8,128)(2,1)}) fusion(bf16[1,64,8192]{2,1,0:T(8,128)(2,1)} %param.7, s32[]{:T(128)S(6)} %select_n.31, s32[]{:T(128)S(6)} %select_n.32, s32[]{:T(128)S(6)} %select_n.30, s32[]{:T(128)S(6)} %select_n.29), kind=kLoop, calls=%fused_computation.6 | loop fusion | bytes 1048592 | tf_op jit(solution)/shard_map/dynamic_slice | solution.py:236
  33.9 3.9 %collective-permute-done.5.refs_4_ = bf16[128,1024]{1,0:T(8,128)(2,1)} collective-permute-done((bf16[128,1024]{1,0:T(8,128)(2,1)S(1)}, bf16[128,1024]{1,0:T(8,128)(2,1)}, u32[]{:S(2)}, u32[]{:S(2)}) %collective-permute-start.5) | collective-permute-done | bytes 262176 | tf_op jit(solution)/shard_map/ppermute | solution.py:28
  37.8 5.6 %collective-permute-done.6.refs_5_ = bf16[128,1024]{1,0:T(8,128)(2,1)} collective-permute-done((bf16[128,1024]{1,0:T(8,128)(2,1)S(1)}, bf16[128,1024]{1,0:T(8,128)(2,1)}, u32[]{:S(2)}, u32[]{:S(2)}) %collective-permute-start.6) | collective-permute-done | bytes 262176 | tf_op jit(solution)/shard_map/ppermute | solution.py:28
  44.0 1.3 collective-permute-start.10
  46.0 3.1 %collective-permute-done.11 = bf16[64,1024]{1,0:T(8,128)(2,1)S(1)} collective-permute-done((bf16[64,1024]{1,0:T(8,128)(2,1)}, bf16[64,1024]{1,0:T(8,128)(2,1)S(1)}, u32[]{:S(2)}, u32[]{:S(2)}) %collective-permute-start.11) | collective-permute-done | bytes 131104 | tf_op jit(solution)/shard_map/ppermute | solution.py:24
  49.7 2.5 %collective-permute-done.10 = bf16[64,1024]{1,0:T(8,128)(2,1)S(1)} collective-permute-done((bf16[64,1024]{1,0:T(8,128)(2,1)}, bf16[64,1024]{1,0:T(8,128)(2,1)S(1)}, u32[]{:S(2)}, u32[]{:S(2)}) %collective-permute-start.10) | collective-permute-done | bytes 131104 | tf_op jit(solution)/shard_map/ppermute | solution.py:24
  53.5 1.4 collective-permute-start.12
  55.1 8.7 %collective-permute-done.12.refs_1_ = bf16[256,512]{1,0:T(8,128)(2,1)} collective-permute-done((bf16[256,512]{1,0:T(8,128)(2,1)S(1)}, bf16[256,512]{1,0:T(8,128)(2,1)}, u32[]{:S(2)}, u32[]{:S(2)}) %collective-permute-start.12) | collective-permute-done | bytes 262176 | tf_op jit(solution)/shard_map/ppermute | solution.py:28
  63.8 4.3 %down_product.1 = (f32[8,64,128]{2,1,0:T(8,128)}, f32[8,128,128]{2,1,0:T(8,128)S(1)}) custom-call(s32[16]{0:T(128)S(1)} %add.62.labels_ref, bf16[8,136,1024]{2,1,0:T(8,128)(2,1)S(1)} %all-to-all-done.rows_ref, bf16[128,1024]{1,0:T(8,128)(2,1)S(1)} %pad_maximum_fusion.refs_0_, bf16[128,1024]{1,0:T(8,128)(2,1)S(1)} %constant_dynamic-update-slice_fusion.refs_1_, ...), custom_call_target="tpu_custom_call" | custom-call | flops 2147483648 | bytes 4194304 | tf_op jit(solution)/shard_map/down_product/pallas_call | solution.py:110
  68.9 3.5 %all-to-all-start.1 = ((f32[8,64,128]{2,1,0:T(8,128)}), f32[8,64,128]{2,1,0:T(8,128)S(1)}, u32[]{:S(2)}, u32[]{:S(2)}) async-start(f32[8,64,128]{2,1,0:T(8,128)} %get-tuple-element.16), calls=%async_computation.1 | async-start | bytes 524288 | tf_op jit(solution)/shard_map/all_to_all | solution.py:36
  73.4 5.1 %all-to-all-done.1.terms_ref = f32[8,64,128]{2,1,0:T(8,128)S(1)} async-done(((f32[8,64,128]{2,1,0:T(8,128)}), f32[8,64,128]{2,1,0:T(8,128)S(1)}, u32[]{:S(2)}, u32[]{:S(2)}) %all-to-all-start.1) | async-done | bytes 262176 | tf_op jit(solution)/shard_map/all_to_all | solution.py:36
  78.5 7.8 %all_to_all.25.shrunk_ref = bf16[8,64,128]{2,1,0:T(8,128)(2,1)S(1)} all-to-all(bf16[8,64,128]{2,1,0:T(8,128)(2,1)S(1)} %summed_copies.1), channel_id=1, replica_groups=mesh['groups'=2,'outer'=4,'inner'=4] {'groups','inner'}, dimensions={0} | all-to-all | bytes 262144 | tf_op jit(solution)/shard_map/all_to_all | solution.py:36
  86.3 1.0 copy-done.2
  87.3 3.7 %up_product.2 = bf16[8,128,512]{2,1,0:T(8,128)(2,1)} custom-call(s32[16]{0:T(128)S(1)} %add.62.labels_ref, f32[8,128,128]{2,1,0:T(8,128)S(1)} %copy-done.2, bf16[8,64,128]{2,1,0:T(8,128)(2,1)S(1)} %all_to_all.25.shrunk_ref, bf16[256,512]{1,0:T(8,128)(2,1)S(1)} %pad_maximum_fusion.1.refs_0_, bf16[256,512]{1,0:T(8,128)(2,1)} %collective-permute-done.12.refs_1_, ...), custom_call_target="tpu_custom_call" | custom-call | flops 1073741824 | bytes 2097152 | tf_op jit(solution)/shard_map/up_product/pallas_call | solution.py:180
  91.0 3.7 %all-to-all-start.3 = ((bf16[8,128,512]{2,1,0:T(8,128)(2,1)}), bf16[8,128,512]{2,1,0:T(8,128)(2,1)S(1)}, u32[]{:S(2)}, u32[]{:S(2)}) async-start(bf16[8,128,512]{2,1,0:T(8,128)(2,1)} %up_product.2), calls=%async_computation.3 | async-start | bytes 2097152 | tf_op jit(solution)/shard_map/all_to_all | solution.py:36
  95.6 9.8 %collective-permute-done.15.refs_1_ = bf16[256,512]{1,0:T(8,128)(2,1)S(1)} collective-permute-done((bf16[256,512]{1,0:T(8,128)(2,1)S(1)}, bf16[256,512]{1,0:T(8,128)(2,1)S(1)}, u32[]{:S(2)}, u32[]{:S(2)}) %collective-permute-start.15) | collective-permute-done | bytes 262176 | tf_op jit(solution)/shard_map/ppermute | solution.py:28
  105.5 9.8 %collective-permute-done.16.refs_2_ = bf16[256,512]{1,0:T(8,128)(2,1)S(1)} collective-permute-done((bf16[256,512]{1,0:T(8,128)(2,1)S(1)}, bf16[256,512]{1,0:T(8,128)(2,1)S(1)}, u32[]{:S(2)}, u32[]{:S(2)}) %collective-permute-start.16) | collective-permute-done | bytes 262176 | tf_op jit(solution)/shard_map/ppermute | solution.py:28
  115.3 8.9 %collective-permute-done.17.refs_3_ = bf16[256,512]{1,0:T(8,128)(2,1)S(1)} collective-permute-done((bf16[256,512]{1,0:T(8,128)(2,1)S(1)}, bf16[256,512]{1,0:T(8,128)(2,1)S(1)}, u32[]{:S(2)}, u32[]{:S(2)}) %collective-permute-start.17) | collective-permute-done | bytes 262176 | tf_op jit(solution)/shard_map/ppermute | solution.py:28
  124.2 2.2 %up_product.3 = bf16[8,128,512]{2,1,0:T(8,128)(2,1)S(1)} custom-call(s32[16]{0:T(128)S(1)} %add.62.labels_ref, f32[8,128,128]{2,1,0:T(8,128)S(1)} %copy-done.3, bf16[8,64,128]{2,1,0:T(8,128)(2,1)S(1)} %all_to_all.25.shrunk_ref, bf16[256,512]{1,0:T(8,128)(2,1)S(1)} %pad_maximum_fusion.2.refs_0_, bf16[256,512]{1,0:T(8,128)(2,1)S(1)} %collective-permute-done.15.refs_1_, ...), custom_call_target="tpu_custom_call" | custom-call | flops 1073741824 | bytes 2097152 | tf_op jit(solution)/shard_map/up_product/pallas_call | solution.py:180
  126.3 17.9 %all_to_all.26.refs_1_ = bf16[8,128,512]{2,1,0:T(8,128)(2,1)S(1)} all-to-all(bf16[8,128,512]{2,1,0:T(8,128)(2,1)S(1)} %up_product.3), channel_id=1, replica_groups=mesh['groups'=2,'outer'=4,'inner'=4] {'groups','inner'}, dimensions={0} | all-to-all | bytes 2097152 | tf_op jit(solution)/shard_map/all_to_all | solution.py:36
  144.3 1.4 place_results.1
  (51 shorter events, 7.4 us)
Async XLA Ops:
  1.1 7.0 %collective-permute-start = (bf16[64,1024]{1,0:T(8,128)(2,1)S(1)}, bf16[64,1024]{1,0:T(8,128)(2,1)S(1)}, u32[]{:S(2)}, u32[]{:S(2)}) collective-permute-start(bf16[64,1024]{1,0:T(8,128)(2,1)S(1)} %get-tuple-element.29), channel_id=1, source_target_pairs={{0,2},{1,3},{2,0},{3,1},{4,6},{5,7},{6,4},{7,5},{8,10},{9,11},{10,... | collective-permute-start | bytes 393224 | tf_op jit(solution)/shard_map/ppermute | solution.py:24
  4.2 5.9 %collective-permute-start.1 = (bf16[64,1024]{1,0:T(8,128)(2,1)S(1)}, bf16[64,1024]{1,0:T(8,128)(2,1)S(1)}, u32[]{:S(2)}, u32[]{:S(2)}) collective-permute-start(bf16[64,1024]{1,0:T(8,128)(2,1)S(1)} %get-tuple-element.28), channel_id=1, source_target_pairs={{0,3},{1,2},{2,1},{3,0},{4,7},{5,6},{6,5},{7,4},{8,11},{9,10},{10,... | collective-permute-start | bytes 393224 | tf_op jit(solution)/shard_map/ppermute | solution.py:24
  4.9 1.6 %copy-start = (bf16[128,8192]{1,0:T(8,128)(2,1)S(1)}, bf16[128,8192]{1,0:T(8,128)(2,1)}, u32[]{:S(2)}) copy-start(bf16[128,8192]{1,0:T(8,128)(2,1)} %hidden_ref.1) | copy-start | bytes 6291460
  10.0 33.4 %all-to-all-start = ((bf16[8,136,1024]{2,1,0:T(8,128)(2,1)}), bf16[8,136,1024]{2,1,0:T(8,128)(2,1)S(1)}, u32[]{:S(2)}, u32[]{:S(2)}) async-start(bf16[8,136,1024]{2,1,0:T(8,128)(2,1)} %outgoing_rows.1), calls=%async_computation | async-start | bytes 4456448 | tf_op jit(solution)/shard_map/all_to_all | solution.py:36
  13.8 1.6 %collective-permute-start.2 = (bf16[64,1024]{1,0:T(8,128)(2,1)S(1)}, bf16[64,1024]{1,0:T(8,128)(2,1)S(1)}, u32[]{:S(2)}, u32[]{:S(2)}) collective-permute-start(bf16[64,1024]{1,0:T(8,128)(2,1)S(1)} %get-tuple-element.30), channel_id=1, source_target_pairs={{0,1},{1,0},{2,3},{3,2},{4,5},{5,4},{6,7},{7,6},{8,9},{9,8},{10,11... | collective-permute-start | bytes 393224 | tf_op jit(solution)/shard_map/ppermute | solution.py:24
  15.5 11.0 %collective-permute-start.3 = (bf16[128,1024]{1,0:T(8,128)(2,1)S(1)}, bf16[128,1024]{1,0:T(8,128)(2,1)S(1)}, u32[]{:S(2)}, u32[]{:S(2)}) collective-permute-start(bf16[128,1024]{1,0:T(8,128)(2,1)S(1)} %pad_maximum_fusion.refs_0_), channel_id=1, source_target_pairs={{0,4},{4,8},{8,12},{12,0},{1,5},{5,9},{9,13},{13,1},{2,6},{6,10},{... | collective-permute-start | bytes 786440 | tf_op jit(solution)/shard_map/ppermute | solution.py:28
  17.1 14.9 %collective-permute-start.4 = (bf16[128,1024]{1,0:T(8,128)(2,1)S(1)}, bf16[128,1024]{1,0:T(8,128)(2,1)S(1)}, u32[]{:S(2)}, u32[]{:S(2)}) collective-permute-start(bf16[128,1024]{1,0:T(8,128)(2,1)S(1)} %constant_dynamic-update-slice_fusion.refs_1_), channel_id=1, source_target_pairs={{0,4},{4,8},{8,12},{12,0},{1,5},{5,9},{9,13},{13,1},{2,6},{6,10},{... | collective-permute-start | bytes 786440 | tf_op jit(solution)/shard_map/ppermute | solution.py:28
  26.5 11.3 %collective-permute-start.5 = (bf16[128,1024]{1,0:T(8,128)(2,1)S(1)}, bf16[128,1024]{1,0:T(8,128)(2,1)}, u32[]{:S(2)}, u32[]{:S(2)}) collective-permute-start(bf16[128,1024]{1,0:T(8,128)(2,1)S(1)} %collective-permute-done.3.refs_2_), channel_id=1, source_target_pairs={{0,4},{4,8},{8,12},{12,0},{1,5},{5,9},{9,13},{13,1},{2,6},{6,10},{... | collective-permute-start | bytes 786440 | tf_op jit(solution)/shard_map/ppermute | solution.py:28
  32.1 11.3 %collective-permute-start.6 = (bf16[128,1024]{1,0:T(8,128)(2,1)S(1)}, bf16[128,1024]{1,0:T(8,128)(2,1)}, u32[]{:S(2)}, u32[]{:S(2)}) collective-permute-start(bf16[128,1024]{1,0:T(8,128)(2,1)S(1)} %collective-permute-done.4.refs_3_), channel_id=1, source_target_pairs={{0,4},{4,8},{8,12},{12,0},{1,5},{5,9},{9,13},{13,1},{2,6},{6,10},{... | collective-permute-start | bytes 786440 | tf_op jit(solution)/shard_map/ppermute | solution.py:28
  37.8 15.7 %collective-permute-start.7 = (bf16[128,1024]{1,0:T(8,128)(2,1)}, bf16[128,1024]{1,0:T(8,128)(2,1)}, u32[]{:S(2)}, u32[]{:S(2)}) collective-permute-start(bf16[128,1024]{1,0:T(8,128)(2,1)} %collective-permute-done.5.refs_4_), channel_id=1, source_target_pairs={{0,4},{4,8},{8,12},{12,0},{1,5},{5,9},{9,13},{13,1},{2,6},{6,10},{... | collective-permute-start | bytes 786440 | tf_op jit(solution)/shard_map/ppermute | solution.py:28
  43.4 20.4 %collective-permute-start.8 = (bf16[128,1024]{1,0:T(8,128)(2,1)}, bf16[128,1024]{1,0:T(8,128)(2,1)}, u32[]{:S(2)}, u32[]{:S(2)}) collective-permute-start(bf16[128,1024]{1,0:T(8,128)(2,1)} %collective-permute-done.6.refs_5_), channel_id=1, source_target_pairs={{0,4},{4,8},{8,12},{12,0},{1,5},{5,9},{9,13},{13,1},{2,6},{6,10},{... | collective-permute-start | bytes 786440 | tf_op jit(solution)/shard_map/ppermute | solution.py:28
  43.4 5.7 %collective-permute-start.11 = (bf16[64,1024]{1,0:T(8,128)(2,1)}, bf16[64,1024]{1,0:T(8,128)(2,1)S(1)}, u32[]{:S(2)}, u32[]{:S(2)}) collective-permute-start(bf16[64,1024]{1,0:T(8,128)(2,1)} %get-tuple-element.20), channel_id=1, source_target_pairs={{0,3},{1,2},{2,1},{3,0},{4,7},{5,6},{6,5},{7,4},{8,11},{9,10},{10,... | collective-permute-start | bytes 393224 | tf_op jit(solution)/shard_map/ppermute | solution.py:24
  44.0 8.3 %collective-permute-start.10 = (bf16[64,1024]{1,0:T(8,128)(2,1)}, bf16[64,1024]{1,0:T(8,128)(2,1)S(1)}, u32[]{:S(2)}, u32[]{:S(2)}) collective-permute-start(bf16[64,1024]{1,0:T(8,128)(2,1)} %get-tuple-element.19), channel_id=1, source_target_pairs={{0,2},{1,3},{2,0},{3,1},{4,6},{5,7},{6,4},{7,5},{8,10},{9,11},{10,... | collective-permute-start | bytes 393224 | tf_op jit(solution)/shard_map/ppermute | solution.py:24
  45.3 7.6 %collective-permute-start.9 = (bf16[64,1024]{1,0:T(8,128)(2,1)}, bf16[64,1024]{1,0:T(8,128)(2,1)S(1)}, u32[]{:S(2)}, u32[]{:S(2)}) collective-permute-start(bf16[64,1024]{1,0:T(8,128)(2,1)} %get-tuple-element.18), channel_id=1, source_target_pairs={{0,1},{1,0},{2,3},{3,2},{4,5},{5,4},{6,7},{7,6},{8,9},{9,8},{10,11... | collective-permute-start | bytes 393224 | tf_op jit(solution)/shard_map/ppermute | solution.py:24
  53.5 10.3 %collective-permute-start.12 = (bf16[256,512]{1,0:T(8,128)(2,1)S(1)}, bf16[256,512]{1,0:T(8,128)(2,1)}, u32[]{:S(2)}, u32[]{:S(2)}) collective-permute-start(bf16[256,512]{1,0:T(8,128)(2,1)S(1)} %pad_maximum_fusion.1.refs_0_), channel_id=1, source_target_pairs={{0,4},{4,8},{8,12},{12,0},{1,5},{5,9},{9,13},{13,1},{2,6},{6,10},{... | collective-permute-start | bytes 786440 | tf_op jit(solution)/shard_map/ppermute | solution.py:28
  63.8 9.6 %collective-permute-start.13 = (bf16[256,512]{1,0:T(8,128)(2,1)}, bf16[256,512]{1,0:T(8,128)(2,1)}, u32[]{:S(2)}, u32[]{:S(2)}) collective-permute-start(bf16[256,512]{1,0:T(8,128)(2,1)} %collective-permute-done.12.refs_1_), channel_id=1, source_target_pairs={{0,4},{4,8},{8,12},{12,0},{1,5},{5,9},{9,13},{13,1},{2,6},{6,10},{... | collective-permute-start | bytes 786440 | tf_op jit(solution)/shard_map/ppermute | solution.py:28
  68.2 0.8 copy-start.1
  68.9 9.5 %all-to-all-start.1 = ((f32[8,64,128]{2,1,0:T(8,128)}), f32[8,64,128]{2,1,0:T(8,128)S(1)}, u32[]{:S(2)}, u32[]{:S(2)}) async-start(f32[8,64,128]{2,1,0:T(8,128)} %get-tuple-element.16), calls=%async_computation.1 | async-start | bytes 524288 | tf_op jit(solution)/shard_map/all_to_all | solution.py:36
  73.4 12.8 %collective-permute-start.14 = (bf16[256,512]{1,0:T(8,128)(2,1)}, bf16[256,512]{1,0:T(8,128)(2,1)S(1)}, u32[]{:S(2)}, u32[]{:S(2)}) collective-permute-start(bf16[256,512]{1,0:T(8,128)(2,1)} %collective-permute-done.13.refs_2_), channel_id=1, source_target_pairs={{0,4},{4,8},{8,12},{12,0},{1,5},{5,9},{9,13},{13,1},{2,6},{6,10},{... | collective-permute-start | bytes 786440 | tf_op jit(solution)/shard_map/ppermute | solution.py:28
  86.2 1.0 copy-start.2
  87.3 7.4 %copy-start.4 = (bf16[64,512]{1,0:T(8,128)(2,1)S(1)}, bf16[64,512]{1,0:T(8,128)(2,1)}, u32[]{:S(2)}) copy-start(bf16[64,512]{1,0:T(8,128)(2,1)} %get-tuple-element.31) | copy-start | bytes 196612
  87.3 7.4 %copy-start.5 = (bf16[64,512]{1,0:T(8,128)(2,1)S(1)}, bf16[64,512]{1,0:T(8,128)(2,1)}, u32[]{:S(2)}) copy-start(bf16[64,512]{1,0:T(8,128)(2,1)} %get-tuple-element.37) | copy-start | bytes 196612
  87.3 7.4 %copy-start.6 = (bf16[64,512]{1,0:T(8,128)(2,1)S(1)}, bf16[64,512]{1,0:T(8,128)(2,1)}, u32[]{:S(2)}) copy-start(bf16[64,512]{1,0:T(8,128)(2,1)} %get-tuple-element.35) | copy-start | bytes 196612
  87.3 7.4 %copy-start.7 = (bf16[64,512]{1,0:T(8,128)(2,1)S(1)}, bf16[64,512]{1,0:T(8,128)(2,1)}, u32[]{:S(2)}) copy-start(bf16[64,512]{1,0:T(8,128)(2,1)} %get-tuple-element.33) | copy-start | bytes 196612
  91.0 33.2 %copy-start.3 = (f32[8,128,128]{2,1,0:T(8,128)S(1)}, f32[8,128,128]{2,1,0:T(8,128)}, u32[]{:S(2)}) copy-start(f32[8,128,128]{2,1,0:T(8,128)} %copy-done.1) | copy-start | bytes 1572868
  91.0 35.4 %all-to-all-start.3 = ((bf16[8,128,512]{2,1,0:T(8,128)(2,1)}), bf16[8,128,512]{2,1,0:T(8,128)(2,1)S(1)}, u32[]{:S(2)}, u32[]{:S(2)}) async-start(bf16[8,128,512]{2,1,0:T(8,128)(2,1)} %up_product.2), calls=%async_computation.3 | async-start | bytes 2097152 | tf_op jit(solution)/shard_map/all_to_all | solution.py:36
  94.7 10.7 %collective-permute-start.15 = (bf16[256,512]{1,0:T(8,128)(2,1)S(1)}, bf16[256,512]{1,0:T(8,128)(2,1)S(1)}, u32[]{:S(2)}, u32[]{:S(2)}) collective-permute-start(bf16[256,512]{1,0:T(8,128)(2,1)S(1)} %pad_maximum_fusion.2.refs_0_), channel_id=1, source_target_pairs={{0,4},{4,8},{8,12},{12,0},{1,5},{5,9},{9,13},{13,1},{2,6},{6,10},{... | collective-permute-start | bytes 786440 | tf_op jit(solution)/shard_map/ppermute | solution.py:28
  105.5 9.8 %collective-permute-start.16 = (bf16[256,512]{1,0:T(8,128)(2,1)S(1)}, bf16[256,512]{1,0:T(8,128)(2,1)S(1)}, u32[]{:S(2)}, u32[]{:S(2)}) collective-permute-start(bf16[256,512]{1,0:T(8,128)(2,1)S(1)} %collective-permute-done.15.refs_1_), channel_id=1, source_target_pairs={{0,4},{4,8},{8,12},{12,0},{1,5},{5,9},{9,13},{13,1},{2,6},{6,10},{... | collective-permute-start | bytes 786440 | tf_op jit(solution)/shard_map/ppermute | solution.py:28
  115.2 8.9 %collective-permute-start.17 = (bf16[256,512]{1,0:T(8,128)(2,1)S(1)}, bf16[256,512]{1,0:T(8,128)(2,1)S(1)}, u32[]{:S(2)}, u32[]{:S(2)}) collective-permute-start(bf16[256,512]{1,0:T(8,128)(2,1)S(1)} %collective-permute-done.16.refs_2_), channel_id=1, source_target_pairs={{0,4},{4,8},{8,12},{12,0},{1,5},{5,9},{9,13},{13,1},{2,6},{6,10},{... | collective-permute-start | bytes 786440 | tf_op jit(solution)/shard_map/ppermute | solution.py:28

commit v6 on v5

--- a/solution.py
+++ b/solution.py
@@ -231,13 +231,17 @@
     piece = share // pieces
     me = group * inner + place_in_group
 
-    def slices(array):
-        return [
-            lax.dynamic_slice_in_dim(array, (me ^ offset) * share, share, axis=1) for offset in range(inner)
-        ]
-
-    def exchanged(blocks):
-        return blocks[:1] + [to_partner(blocks[n], "inner", inner, n) for n in range(1, inner)]
+    def slices(offset):
+        start = (me ^ offset) * share
+        return jnp.concatenate(
+            [
+                lax.dynamic_slice_in_dim(adapter_down_maps[0].T, start, share, axis=1),
+                lax.dynamic_slice_in_dim(adapter_up_maps[0], start, share, axis=1),
+            ],
+            axis=0,
+        )
+
+    got = [slices(0)] + [to_partner(slices(n), "inner", inner, n) for n in range(1, inner)]
 
     steps_back = jnp.arange(outer, dtype=jnp.int32)[:, None]
     labels = ((level - steps_back + outer) % outer) * inner + (
@@ -245,30 +249,30 @@
     )
     labels = labels.reshape(-1)
 
-    down = exchanged(slices(adapter_down_maps[0].T))
-    near = [jnp.concatenate(down[: inner // 2], axis=0)]
-    far = [jnp.concatenate(down[inner // 2 :], axis=0)]
+    near = [jnp.concatenate([g[:rank] for g in got[: inner // 2]], axis=0)]
+    far = [jnp.concatenate([g[:rank] for g in got[inner // 2 :]], axis=0)]
     for _ in range(outer - 1):
         near.append(next_on_ring(near[-1], outer))
         far.append(next_on_ring(far[-1], outer))
     down_maps = [m for pair in zip(near, far) for m in pair]
 
     ids = token_adapter_index.astype(jnp.bfloat16).reshape(1, tok)
-    rows = swap(after(outgoing_rows(hidden, ids, members), *down[inner // 2 :]))
-
-    own_slices = slices(adapter_up_maps[0])
-    up = exchanged([after(block, rows) for block in own_slices])
+    rows = swap(after(outgoing_rows(hidden, ids, members), got[1]))
+
     held = [
-        [jnp.concatenate([b[:, n * piece : (n + 1) * piece] for b in up], axis=0)] for n in range(pieces)
+        [jnp.concatenate([g[rank:, n * piece : (n + 1) * piece] for g in got], axis=0)] for n in range(pieces)
     ]
-    held[0][0] = after(held[0][0], near[-1])
+    held[0][0] = after(held[0][0], near[-1], rows)
     held[-1][0] = after(held[-1][0], far[-1])
-    for ring in held:
-        for _ in range(outer - 1):
-            ring.append(next_on_ring(ring[-1], outer))
+    for step in range(1, outer):
+        for n in range(pieces):
+            block = held[n][-1]
+            if n == 0 and step > 1:
+                block = after(block, held[-1][step - 2])
+            held[n].append(next_on_ring(block, outer))
 
     packed, id_columns = down_product(labels, rows, down_maps, rank)
-    shrunk = swap(summed_copies(swap(packed)))
+    shrunk = after(swap(summed_copies(swap(packed))), held[-1][-2])
     return place([swap(up_product(labels, id_columns, shrunk, ring, rank)) for ring in held])
 
 

time: 146 us -> 172 us (1.18)
  waiting for transfers between devices: 74.9 us -> 96.8 us
  local copies, waits for them, and re-layouts: 9.05 us -> 13 us
    ppermute x6 -> x3, waiting for transfers between devices: 8.79 us -> 30 us  [to_partner(): return lax.ppermute(value, axes, [(i, i ^ offset) for i in range(size)])]
    slice x4 -> x7, local copies, waits for them, and re-layouts: 2.51 us -> 5.26 us  [the longest x4 5.23 us: per_device(): g[rank:, n * piece:(n + 1) * piece]]
    unnamed x17 -> x32, local copies, waits for them, and re-layouts: 3.45 us -> 5.17 us
    ppermute x6 -> x3, starting transfers between devices: 5.45 us -> 5.14 us  [to_partner(): return lax.ppermute(value, axes, [(i, i ^ offset) for i in range(size)])]
  transfers between devices with their start and end apart: 21 -> 18, of which waited for: 15 -> 11; matrix products, arithmetic and copies ran while one was open for 4% -> 4% of each run, Pallas kernels for 6% -> 5%
where the time goes in v6:
time: 172 us; the launch traced here: 171 us
  waiting for transfers between devices  96.8 us (56%)
  blocking collectives  25.7 us (15%)
  starting transfers between devices  21.8 us (13%)
  local copies, waits for them, and re-layouts  13 us (8%)
  Pallas kernels  13 us (8%)
    ppermute x12, waiting for transfers between devices, next_on_ring(): lax.ppermute(block, 'outer', [(i, (i + 1) % outer) for i in range(outer)])  62.2 us
    ppermute x3, waiting for transfers between devices, to_partner(): return lax.ppermute(value, axes, [(i, i ^ offset) for i in range(size)])  30 us
    all_to_all x2, blocking collectives, swap(): return lax.all_to_all(value, PLANE, split_axis=0, concat_axis=0, tiled=True)  25.7 us
    all_to_all x3, starting transfers between devices, swap(): return lax.all_to_all(value, PLANE, split_axis=0, concat_axis=0, tiled=True)  10.7 us
    ppermute x12, starting transfers between devices, next_on_ring(): lax.ppermute(block, 'outer', [(i, (i + 1) % outer) for i in range(outer)])  5.98 us
    pallas_call x2, Pallas kernels, up_product(): pl.pallas_call(functools.partial(up_kernel, len(maps), rank), out_shape=j...  5.8 us
    slice x4, local copies, waits for them, and re-layouts, per_device(): g[rank:, n * piece:(n + 1) * piece]  5.23 us
    unnamed x32, local copies, waits for them, and re-layouts  5.17 us
  transfers between devices with their start and end apart: 18, of which 11 were waited for; matrix products, arithmetic and copies ran while one was open for 4% of the time, Pallas kernels for 5%

profile of v6, /device:TPU:0, one launch (start us, length us, event | category | flops | bytes accessed | tf_op | source)
XLA Modules:
  0.0 171.4 jit_solution(3104962396159787805)
XLA Ops:
  0.0 1.3 dynamic-slice_bitcast_fusion
  1.3 1.1 dynamic-slice_bitcast_fusion.4
  3.0 2.7 %collective-permute-start.2 = (bf16[128,1024]{1,0:T(8,128)(2,1)S(1)}, bf16[128,1024]{1,0:T(8,128)(2,1)S(1)}, u32[]{:S(2)}, u32[]{:S(2)}) collective-permute-start(bf16[128,1024]{1,0:T(8,128)(2,1)S(1)} %pad_maximum_fusion.3), channel_id=1, source_target_pairs={{0,3},{1,2},{2,1},{3,0},{4,7},{5,6},{6,5},{7,4},{8,11},{9,10},{10,... | collective-permute-start | bytes 786440 | tf_op jit(solution)/shard_map/ppermute | solution.py:24
  5.8 1.5 outgoing_rows.1
  7.3 3.6 %all-to-all-start = ((bf16[8,136,1024]{2,1,0:T(8,128)(2,1)}), bf16[8,136,1024]{2,1,0:T(8,128)(2,1)S(1)}, u32[]{:S(2)}, u32[]{:S(2)}) async-start(bf16[8,136,1024]{2,1,0:T(8,128)(2,1)} %outgoing_rows.1), calls=%async_computation | async-start | bytes 4456448 | tf_op jit(solution)/shard_map/all_to_all | solution.py:36
  11.6 1.9 %collective-permute-start.1 = (bf16[128,1024]{1,0:T(8,128)(2,1)}, bf16[128,1024]{1,0:T(8,128)(2,1)S(1)}, u32[]{:S(2)}, u32[]{:S(2)}) collective-permute-start(bf16[128,1024]{1,0:T(8,128)(2,1)} %pad_maximum_fusion.2), channel_id=1, source_target_pairs={{0,2},{1,3},{2,0},{3,1},{4,6},{5,7},{6,4},{7,5},{8,10},{9,11},{10,... | collective-permute-start | bytes 786440 | tf_op jit(solution)/shard_map/ppermute | solution.py:24
  13.6 30.0 %collective-permute-done.1 = bf16[128,1024]{1,0:T(8,128)(2,1)S(1)} collective-permute-done((bf16[128,1024]{1,0:T(8,128)(2,1)}, bf16[128,1024]{1,0:T(8,128)(2,1)S(1)}, u32[]{:S(2)}, u32[]{:S(2)}) %collective-permute-start.1) | collective-permute-done | bytes 262176 | tf_op jit(solution)/shard_map/ppermute | solution.py:24
  44.3 1.6 collective-permute-start.4
  46.6 1.6 collective-permute-start.3
  48.2 7.1 %collective-permute-done.4.refs_3_ = bf16[128,1024]{1,0:T(8,128)(2,1)S(1)} collective-permute-done((bf16[128,1024]{1,0:T(8,128)(2,1)S(1)}, bf16[128,1024]{1,0:T(8,128)(2,1)S(1)}, u32[]{:S(2)}, u32[]{:S(2)}) %collective-permute-start.4) | collective-permute-done | bytes 262176 | tf_op jit(solution)/shard_map/ppermute | solution.py:28
  55.3 1.5 fusion.4
  56.8 1.5 fusion.3
  58.3 2.6 %collective-permute-done.3.refs_2_ = bf16[128,1024]{1,0:T(8,128)(2,1)S(1)} collective-permute-done((bf16[128,1024]{1,0:T(8,128)(2,1)S(1)}, bf16[128,1024]{1,0:T(8,128)(2,1)S(1)}, u32[]{:S(2)}, u32[]{:S(2)}) %collective-permute-start.3) | collective-permute-done | bytes 262176 | tf_op jit(solution)/shard_map/ppermute | solution.py:28
  61.0 5.6 %collective-permute-done.6.refs_5_ = bf16[128,1024]{1,0:T(8,128)(2,1)S(1)} collective-permute-done((bf16[128,1024]{1,0:T(8,128)(2,1)S(1)}, bf16[128,1024]{1,0:T(8,128)(2,1)S(1)}, u32[]{:S(2)}, u32[]{:S(2)}) %collective-permute-start.6) | collective-permute-done | bytes 262176 | tf_op jit(solution)/shard_map/ppermute | solution.py:28
  66.6 1.6 fusion.2
  68.2 4.1 %collective-permute-done.5.refs_4_ = bf16[128,1024]{1,0:T(8,128)(2,1)} collective-permute-done((bf16[128,1024]{1,0:T(8,128)(2,1)S(1)}, bf16[128,1024]{1,0:T(8,128)(2,1)}, u32[]{:S(2)}, u32[]{:S(2)}) %collective-permute-start.5) | collective-permute-done | bytes 262176 | tf_op jit(solution)/shard_map/ppermute | solution.py:28
  72.3 5.5 %collective-permute-done.8.refs_7_ = bf16[128,1024]{1,0:T(8,128)(2,1)S(1)} collective-permute-done((bf16[128,1024]{1,0:T(8,128)(2,1)S(1)}, bf16[128,1024]{1,0:T(8,128)(2,1)S(1)}, u32[]{:S(2)}, u32[]{:S(2)}) %collective-permute-start.8) | collective-permute-done | bytes 262176 | tf_op jit(solution)/shard_map/ppermute | solution.py:28
  78.7 9.1 %collective-permute-done.9.refs_1_ = bf16[256,512]{1,0:T(8,128)(2,1)} collective-permute-done((bf16[256,512]{1,0:T(8,128)(2,1)S(1)}, bf16[256,512]{1,0:T(8,128)(2,1)}, u32[]{:S(2)}, u32[]{:S(2)}) %collective-permute-start.9) | collective-permute-done | bytes 262176 | tf_op jit(solution)/shard_map/ppermute | solution.py:28
  89.8 4.2 %down_product.1 = (f32[8,64,128]{2,1,0:T(8,128)}, f32[8,128,128]{2,1,0:T(8,128)S(1)}) custom-call(s32[16]{0:T(128)S(1)} %add.62.labels_ref, bf16[8,136,1024]{2,1,0:T(8,128)(2,1)S(1)} %all-to-all-done.rows_ref, bf16[128,1024]{1,0:T(8,128)(2,1)S(1)} %pad_maximum_fusion.1.refs_0_, bf16[128,1024]{1,0:T(8,128)(2,1)S(1)} %pad_maximum_fusion.4.refs_1_, ...), custom_call_target="tpu_custom_call" | custom-call | flops 2147483648 | bytes 4194304 | tf_op jit(solution)/shard_map/down_product/pallas_call | solution.py:110
  94.7 3.4 %all-to-all-start.1 = ((f32[8,64,128]{2,1,0:T(8,128)}), f32[8,64,128]{2,1,0:T(8,128)S(1)}, u32[]{:S(2)}, u32[]{:S(2)}) async-start(f32[8,64,128]{2,1,0:T(8,128)} %get-tuple-element.15), calls=%async_computation.1 | async-start | bytes 524288 | tf_op jit(solution)/shard_map/all_to_all | solution.py:36
  98.2 1.3 collective-permute-start.14
  99.5 4.6 %all-to-all-done.1.terms_ref = f32[8,64,128]{2,1,0:T(8,128)S(1)} async-done(((f32[8,64,128]{2,1,0:T(8,128)}), f32[8,64,128]{2,1,0:T(8,128)S(1)}, u32[]{:S(2)}, u32[]{:S(2)}) %all-to-all-start.1) | async-done | bytes 262176 | tf_op jit(solution)/shard_map/all_to_all | solution.py:36
  104.2 7.8 %all_to_all.25.shrunk_ref = bf16[8,64,128]{2,1,0:T(8,128)(2,1)S(1)} all-to-all(bf16[8,64,128]{2,1,0:T(8,128)(2,1)S(1)} %summed_copies.1), channel_id=1, replica_groups=mesh['groups'=2,'outer'=4,'inner'=4] {'groups','inner'}, dimensions={0} | all-to-all | bytes 262144 | tf_op jit(solution)/shard_map/all_to_all | solution.py:36
  113.0 3.7 %up_product.3 = bf16[8,128,512]{2,1,0:T(8,128)(2,1)} custom-call(s32[16]{0:T(128)S(1)} %add.62.labels_ref, f32[8,128,128]{2,1,0:T(8,128)S(1)} %copy-done.6, bf16[8,64,128]{2,1,0:T(8,128)(2,1)S(1)} %all_to_all.25.shrunk_ref, bf16[256,512]{1,0:T(8,128)(2,1)S(1)} %pad_maximum_fusion.5.refs_0_, bf16[256,512]{1,0:T(8,128)(2,1)} %collective-permute-done.9.refs_1_, ...), custom_call_target="tpu_custom_call" | custom-call | flops 1073741824 | bytes 2097152 | tf_op jit(solution)/shard_map/up_product/pallas_call | solution.py:180
  116.6 3.7 %all-to-all-start.4 = ((bf16[8,128,512]{2,1,0:T(8,128)(2,1)}), bf16[8,128,512]{2,1,0:T(8,128)(2,1)S(1)}, u32[]{:S(2)}, u32[]{:S(2)}) async-start(bf16[8,128,512]{2,1,0:T(8,128)(2,1)} %up_product.3), calls=%async_computation.4 | async-start | bytes 2097152 | tf_op jit(solution)/shard_map/all_to_all | solution.py:36
  120.4 1.4 collective-permute-start.11
  121.7 9.4 %collective-permute-done.11.refs_1_ = bf16[256,512]{1,0:T(8,128)(2,1)S(1)} collective-permute-done((bf16[256,512]{1,0:T(8,128)(2,1)S(1)}, bf16[256,512]{1,0:T(8,128)(2,1)S(1)}, u32[]{:S(2)}, u32[]{:S(2)}) %collective-permute-start.11) | collective-permute-done | bytes 262176 | tf_op jit(solution)/shard_map/ppermute | solution.py:28
  131.1 9.8 %collective-permute-done.12.refs_2_ = bf16[256,512]{1,0:T(8,128)(2,1)S(1)} collective-permute-done((bf16[256,512]{1,0:T(8,128)(2,1)S(1)}, bf16[256,512]{1,0:T(8,128)(2,1)S(1)}, u32[]{:S(2)}, u32[]{:S(2)}) %collective-permute-start.12) | collective-permute-done | bytes 262176 | tf_op jit(solution)/shard_map/ppermute | solution.py:28
  140.9 8.9 %collective-permute-done.13.refs_3_ = bf16[256,512]{1,0:T(8,128)(2,1)S(1)} collective-permute-done((bf16[256,512]{1,0:T(8,128)(2,1)S(1)}, bf16[256,512]{1,0:T(8,128)(2,1)S(1)}, u32[]{:S(2)}, u32[]{:S(2)}) %collective-permute-start.13) | collective-permute-done | bytes 262176 | tf_op jit(solution)/shard_map/ppermute | solution.py:28
  149.8 2.2 %up_product.2 = bf16[8,128,512]{2,1,0:T(8,128)(2,1)S(1)} custom-call(s32[16]{0:T(128)S(1)} %add.62.labels_ref, f32[8,128,128]{2,1,0:T(8,128)S(1)} %copy-done.7, bf16[8,64,128]{2,1,0:T(8,128)(2,1)S(1)} %all_to_all.25.shrunk_ref, bf16[256,512]{1,0:T(8,128)(2,1)S(1)} %pad_maximum_fusion.6.refs_0_, bf16[256,512]{1,0:T(8,128)(2,1)S(1)} %collective-permute-done.11.refs_1_, ...), custom_call_target="tpu_custom_call" | custom-call | flops 1073741824 | bytes 2097152 | tf_op jit(solution)/shard_map/up_product/pallas_call | solution.py:180
  152.0 17.9 %all_to_all.26.refs_0_ = bf16[8,128,512]{2,1,0:T(8,128)(2,1)S(1)} all-to-all(bf16[8,128,512]{2,1,0:T(8,128)(2,1)S(1)} %up_product.2), channel_id=1, replica_groups=mesh['groups'=2,'outer'=4,'inner'=4] {'groups','inner'}, dimensions={0} | all-to-all | bytes 2097152 | tf_op jit(solution)/shard_map/all_to_all | solution.py:36
  169.9 1.4 place_results.1
  (66 shorter events, 7.4 us)
Async XLA Ops:
  0.0 5.7 %copy-start.15 = (s32[128,1]{0,1:T(1,128)S(1)}, s32[128,1]{0,1:T(1,128)}, u32[]{:S(2)}) copy-start(s32[128,1]{0,1:T(1,128)} %param.4) | copy-start | bytes 1540
  0.0 5.7 %copy-start = (bf16[128,8192]{1,0:T(8,128)(2,1)S(1)}, bf16[128,8192]{1,0:T(8,128)(2,1)}, u32[]{:S(2)}) copy-start(bf16[128,8192]{1,0:T(8,128)(2,1)} %hidden_ref.1) | copy-start | bytes 6291460
  2.5 4.8 %collective-permute-start = (bf16[128,1024]{1,0:T(8,128)(2,1)S(1)}, bf16[128,1024]{1,0:T(8,128)(2,1)S(1)}, u32[]{:S(2)}, u32[]{:S(2)}) collective-permute-start(bf16[128,1024]{1,0:T(8,128)(2,1)S(1)} %pad_maximum_fusion), channel_id=1, source_target_pairs={{0,1},{1,0},{2,3},{3,2},{4,5},{5,4},{6,7},{7,6},{8,9},{9,8},{10,11... | collective-permute-start | bytes 786440 | tf_op jit(solution)/shard_map/ppermute | solution.py:24
  3.0 10.6 %collective-permute-start.2 = (bf16[128,1024]{1,0:T(8,128)(2,1)S(1)}, bf16[128,1024]{1,0:T(8,128)(2,1)S(1)}, u32[]{:S(2)}, u32[]{:S(2)}) collective-permute-start(bf16[128,1024]{1,0:T(8,128)(2,1)S(1)} %pad_maximum_fusion.3), channel_id=1, source_target_pairs={{0,3},{1,2},{2,1},{3,0},{4,7},{5,6},{6,5},{7,4},{8,11},{9,10},{10,... | collective-permute-start | bytes 786440 | tf_op jit(solution)/shard_map/ppermute | solution.py:24
  7.3 39.3 %copy-start.8 = (bf16[128,1024]{1,0:T(8,128)(2,1)}, bf16[128,1024]{1,0:T(8,128)(2,1)S(1)}, u32[]{:S(2)}) copy-start(bf16[128,1024]{1,0:T(8,128)(2,1)S(1)} %collective-permute-done) | copy-start | bytes 786436
  7.3 80.6 %all-to-all-start = ((bf16[8,136,1024]{2,1,0:T(8,128)(2,1)}), bf16[8,136,1024]{2,1,0:T(8,128)(2,1)S(1)}, u32[]{:S(2)}, u32[]{:S(2)}) async-start(bf16[8,136,1024]{2,1,0:T(8,128)(2,1)} %outgoing_rows.1), calls=%async_computation | async-start | bytes 4456448 | tf_op jit(solution)/shard_map/all_to_all | solution.py:36
  11.6 31.9 %collective-permute-start.1 = (bf16[128,1024]{1,0:T(8,128)(2,1)}, bf16[128,1024]{1,0:T(8,128)(2,1)S(1)}, u32[]{:S(2)}, u32[]{:S(2)}) collective-permute-start(bf16[128,1024]{1,0:T(8,128)(2,1)} %pad_maximum_fusion.2), channel_id=1, source_target_pairs={{0,2},{1,3},{2,0},{3,1},{4,6},{5,7},{6,4},{7,5},{8,10},{9,11},{10,... | collective-permute-start | bytes 786440 | tf_op jit(solution)/shard_map/ppermute | solution.py:24
  13.6 32.3 %copy-start.9 = (bf16[128,1024]{1,0:T(8,128)(2,1)}, bf16[128,1024]{1,0:T(8,128)(2,1)S(1)}, u32[]{:S(2)}) copy-start(bf16[128,1024]{1,0:T(8,128)(2,1)S(1)} %collective-permute-done.2) | copy-start | bytes 786436
  44.3 11.1 %collective-permute-start.4 = (bf16[128,1024]{1,0:T(8,128)(2,1)S(1)}, bf16[128,1024]{1,0:T(8,128)(2,1)S(1)}, u32[]{:S(2)}, u32[]{:S(2)}) collective-permute-start(bf16[128,1024]{1,0:T(8,128)(2,1)S(1)} %pad_maximum_fusion.4.refs_1_), channel_id=1, source_target_pairs={{0,4},{4,8},{8,12},{12,0},{1,5},{5,9},{9,13},{13,1},{2,6},{6,10},{... | collective-permute-start | bytes 786440 | tf_op jit(solution)/shard_map/ppermute | solution.py:28
  46.6 14.4 %collective-permute-start.3 = (bf16[128,1024]{1,0:T(8,128)(2,1)S(1)}, bf16[128,1024]{1,0:T(8,128)(2,1)S(1)}, u32[]{:S(2)}, u32[]{:S(2)}) collective-permute-start(bf16[128,1024]{1,0:T(8,128)(2,1)S(1)} %pad_maximum_fusion.1.refs_0_), channel_id=1, source_target_pairs={{0,4},{4,8},{8,12},{12,0},{1,5},{5,9},{9,13},{13,1},{2,6},{6,10},{... | collective-permute-start | bytes 786440 | tf_op jit(solution)/shard_map/ppermute | solution.py:28
  55.3 11.2 %collective-permute-start.6 = (bf16[128,1024]{1,0:T(8,128)(2,1)S(1)}, bf16[128,1024]{1,0:T(8,128)(2,1)S(1)}, u32[]{:S(2)}, u32[]{:S(2)}) collective-permute-start(bf16[128,1024]{1,0:T(8,128)(2,1)S(1)} %collective-permute-done.4.refs_3_), channel_id=1, source_target_pairs={{0,4},{4,8},{8,12},{12,0},{1,5},{5,9},{9,13},{13,1},{2,6},{6,10},{... | collective-permute-start | bytes 786440 | tf_op jit(solution)/shard_map/ppermute | solution.py:28
  61.0 11.3 %collective-permute-start.5 = (bf16[128,1024]{1,0:T(8,128)(2,1)S(1)}, bf16[128,1024]{1,0:T(8,128)(2,1)}, u32[]{:S(2)}, u32[]{:S(2)}) collective-permute-start(bf16[128,1024]{1,0:T(8,128)(2,1)S(1)} %collective-permute-done.3.refs_2_), channel_id=1, source_target_pairs={{0,4},{4,8},{8,12},{12,0},{1,5},{5,9},{9,13},{13,1},{2,6},{6,10},{... | collective-permute-start | bytes 786440 | tf_op jit(solution)/shard_map/ppermute | solution.py:28
  66.6 12.0 %copy-start.1 = (bf16[128,1024]{1,0:T(8,128)(2,1)}, bf16[128,1024]{1,0:T(8,128)(2,1)S(1)}, u32[]{:S(2)}) copy-start(bf16[128,1024]{1,0:T(8,128)(2,1)S(1)} %collective-permute-done.6.refs_5_) | copy-start | bytes 786436
  66.6 11.2 %collective-permute-start.8 = (bf16[128,1024]{1,0:T(8,128)(2,1)S(1)}, bf16[128,1024]{1,0:T(8,128)(2,1)S(1)}, u32[]{:S(2)}, u32[]{:S(2)}) collective-permute-start(bf16[128,1024]{1,0:T(8,128)(2,1)S(1)} %collective-permute-done.6.refs_5_), channel_id=1, source_target_pairs={{0,4},{4,8},{8,12},{12,0},{1,5},{5,9},{9,13},{13,1},{2,6},{6,10},{... | collective-permute-start | bytes 786440 | tf_op jit(solution)/shard_map/ppermute | solution.py:28
  72.3 15.6 %collective-permute-start.7 = (bf16[128,1024]{1,0:T(8,128)(2,1)}, bf16[128,1024]{1,0:T(8,128)(2,1)}, u32[]{:S(2)}, u32[]{:S(2)}) collective-permute-start(bf16[128,1024]{1,0:T(8,128)(2,1)} %collective-permute-done.5.refs_4_), channel_id=1, source_target_pairs={{0,4},{4,8},{8,12},{12,0},{1,5},{5,9},{9,13},{13,1},{2,6},{6,10},{... | collective-permute-start | bytes 786440 | tf_op jit(solution)/shard_map/ppermute | solution.py:28
  78.5 9.3 %collective-permute-start.9 = (bf16[256,512]{1,0:T(8,128)(2,1)S(1)}, bf16[256,512]{1,0:T(8,128)(2,1)}, u32[]{:S(2)}, u32[]{:S(2)}) collective-permute-start(bf16[256,512]{1,0:T(8,128)(2,1)S(1)} %pad_maximum_fusion.5.refs_0_), channel_id=1, source_target_pairs={{0,4},{4,8},{8,12},{12,0},{1,5},{5,9},{9,13},{13,1},{2,6},{6,10},{... | collective-permute-start | bytes 786440 | tf_op jit(solution)/shard_map/ppermute | solution.py:28
  87.8 10.3 %collective-permute-start.10 = (bf16[256,512]{1,0:T(8,128)(2,1)}, bf16[256,512]{1,0:T(8,128)(2,1)}, u32[]{:S(2)}, u32[]{:S(2)}) collective-permute-start(bf16[256,512]{1,0:T(8,128)(2,1)} %collective-permute-done.9.refs_1_), channel_id=1, source_target_pairs={{0,4},{4,8},{8,12},{12,0},{1,5},{5,9},{9,13},{13,1},{2,6},{6,10},{... | collective-permute-start | bytes 786440 | tf_op jit(solution)/shard_map/ppermute | solution.py:28
  87.9 1.0 copy-start.2
  88.8 0.9 copy-start.4
  94.0 0.8 copy-start.5
  94.7 9.4 %all-to-all-start.1 = ((f32[8,64,128]{2,1,0:T(8,128)}), f32[8,64,128]{2,1,0:T(8,128)S(1)}, u32[]{:S(2)}, u32[]{:S(2)}) async-start(f32[8,64,128]{2,1,0:T(8,128)} %get-tuple-element.15), calls=%async_computation.1 | async-start | bytes 524288 | tf_op jit(solution)/shard_map/all_to_all | solution.py:36
  98.2 13.7 %collective-permute-start.14 = (bf16[256,512]{1,0:T(8,128)(2,1)}, bf16[256,512]{1,0:T(8,128)(2,1)S(1)}, u32[]{:S(2)}, u32[]{:S(2)}) collective-permute-start(bf16[256,512]{1,0:T(8,128)(2,1)} %collective-permute-done.10.refs_2_), channel_id=1, source_target_pairs={{0,4},{4,8},{8,12},{12,0},{1,5},{5,9},{9,13},{13,1},{2,6},{6,10},{... | collective-permute-start | bytes 786440 | tf_op jit(solution)/shard_map/ppermute | solution.py:28
  111.9 1.0 copy-start.6
  113.0 7.4 %copy-start.11 = (bf16[64,512]{1,0:T(8,128)(2,1)S(1)}, bf16[64,512]{1,0:T(8,128)(2,1)}, u32[]{:S(2)}) copy-start(bf16[64,512]{1,0:T(8,128)(2,1)} %get-tuple-element.35) | copy-start | bytes 196612
  113.0 7.4 %copy-start.12 = (bf16[64,512]{1,0:T(8,128)(2,1)S(1)}, bf16[64,512]{1,0:T(8,128)(2,1)}, u32[]{:S(2)}) copy-start(bf16[64,512]{1,0:T(8,128)(2,1)} %get-tuple-element.33) | copy-start | bytes 196612
  113.0 7.4 %copy-start.13 = (bf16[64,512]{1,0:T(8,128)(2,1)S(1)}, bf16[64,512]{1,0:T(8,128)(2,1)}, u32[]{:S(2)}) copy-start(bf16[64,512]{1,0:T(8,128)(2,1)} %get-tuple-element.31) | copy-start | bytes 196612
  113.0 7.4 %copy-start.14 = (bf16[64,512]{1,0:T(8,128)(2,1)S(1)}, bf16[64,512]{1,0:T(8,128)(2,1)}, u32[]{:S(2)}) copy-start(bf16[64,512]{1,0:T(8,128)(2,1)} %get-tuple-element.29) | copy-start | bytes 196612
  116.6 33.2 %copy-start.7 = (f32[8,128,128]{2,1,0:T(8,128)S(1)}, f32[8,128,128]{2,1,0:T(8,128)}, u32[]{:S(2)}) copy-start(f32[8,128,128]{2,1,0:T(8,128)} %copy-done.5) | copy-start | bytes 1572868
  116.6 35.4 %all-to-all-start.4 = ((bf16[8,128,512]{2,1,0:T(8,128)(2,1)}), bf16[8,128,512]{2,1,0:T(8,128)(2,1)S(1)}, u32[]{:S(2)}, u32[]{:S(2)}) async-start(bf16[8,128,512]{2,1,0:T(8,128)(2,1)} %up_product.3), calls=%async_computation.4 | async-start | bytes 2097152 | tf_op jit(solution)/shard_map/all_to_all | solution.py:36
  120.4 10.7 %collective-permute-start.11 = (bf16[256,512]{1,0:T(8,128)(2,1)S(1)}, bf16[256,512]{1,0:T(8,128)(2,1)S(1)}, u32[]{:S(2)}, u32[]{:S(2)}) collective-permute-start(bf16[256,512]{1,0:T(8,128)(2,1)S(1)} %pad_maximum_fusion.6.refs_0_), channel_id=1, source_target_pairs={{0,4},{4,8},{8,12},{12,0},{1,5},{5,9},{9,13},{13,1},{2,6},{6,10},{... | collective-permute-start | bytes 786440 | tf_op jit(solution)/shard_map/ppermute | solution.py:28
  131.1 9.8 %collective-permute-start.12 = (bf16[256,512]{1,0:T(8,128)(2,1)S(1)}, bf16[256,512]{1,0:T(8,128)(2,1)S(1)}, u32[]{:S(2)}, u32[]{:S(2)}) collective-permute-start(bf16[256,512]{1,0:T(8,128)(2,1)S(1)} %collective-permute-done.11.refs_1_), channel_id=1, source_target_pairs={{0,4},{4,8},{8,12},{12,0},{1,5},{5,9},{9,13},{13,1},{2,6},{6,10},{... | collective-permute-start | bytes 786440 | tf_op jit(solution)/shard_map/ppermute | solution.py:28
  140.9 8.9 %collective-permute-start.13 = (bf16[256,512]{1,0:T(8,128)(2,1)S(1)}, bf16[256,512]{1,0:T(8,128)(2,1)S(1)}, u32[]{:S(2)}, u32[]{:S(2)}) collective-permute-start(bf16[256,512]{1,0:T(8,128)(2,1)S(1)} %collective-permute-done.12.refs_2_), channel_id=1, source_target_pairs={{0,4},{4,8},{8,12},{12,0},{1,5},{5,9},{9,13},{13,1},{2,6},{6,10},{... | collective-permute-start | bytes 786440 | tf_op jit(solution)/shard_map/ppermute | solution.py:28
  (2 other events, 1.4 us)

commit v7 on v5

--- a/solution.py
+++ b/solution.py
@@ -13,11 +13,13 @@
 LANES = 128
 ID_ROWS = 8
 BLOCK = 8
-VMEM_BYTES = 48 << 20
 IN_VMEM = pl.BlockSpec(memory_space=pltpu.VMEM)
 IN_SMEM = pl.BlockSpec(memory_space=pltpu.SMEM)
 ANYWHERE = pl.BlockSpec(memory_space=pl.ANY)
-PARAMS = pltpu.CompilerParams(vmem_limit_bytes=VMEM_BYTES)
+
+
+def params(scratch_bytes=0):
+    return pltpu.CompilerParams(vmem_limit_bytes=(12 << 20) + 2 * scratch_bytes)
 
 
 def to_partner(value, axes, size, offset):
@@ -62,7 +64,7 @@
         out_shape=jax.ShapeDtypeStruct((members, tok + ID_ROWS, share), jnp.bfloat16),
         in_specs=[IN_VMEM, IN_VMEM],
         out_specs=IN_VMEM,
-        compiler_params=PARAMS,
+        compiler_params=params(),
         name="outgoing_rows",
     )(hidden, ids)
 
@@ -116,7 +118,7 @@
         in_specs=[IN_SMEM, IN_VMEM] + [IN_VMEM] * len(maps),
         out_specs=[IN_VMEM, IN_VMEM],
         scratch_shapes=[pltpu.VMEM((min(BLOCK, members) * tok, LANES), jnp.float32)],
-        compiler_params=PARAMS,
+        compiler_params=params(4 * min(BLOCK, members) * tok * LANES),
         cost_estimate=pl.CostEstimate(
             flops=2 * map_rows * members * tok * share,
             bytes_accessed=2 * share * (map_rows + members * tok),
@@ -138,7 +140,7 @@
         out_shape=jax.ShapeDtypeStruct(terms.shape, jnp.bfloat16),
         in_specs=[IN_VMEM],
         out_specs=IN_VMEM,
-        compiler_params=PARAMS,
+        compiler_params=params(),
         name="summed_copies",
     )(terms)
 
@@ -183,7 +185,7 @@
         in_specs=[IN_SMEM, IN_VMEM, IN_VMEM] + [IN_VMEM] * len(maps),
         out_specs=IN_VMEM,
         scratch_shapes=[pltpu.VMEM((min(BLOCK, members) * tok, map_rows), jnp.bfloat16)],
-        compiler_params=PARAMS,
+        compiler_params=params(2 * min(BLOCK, members) * tok * map_rows),
         cost_estimate=pl.CostEstimate(
             flops=2 * map_rows * members * tok * piece,
             bytes_accessed=2 * piece * (map_rows + members * tok),
@@ -215,7 +217,7 @@
         in_specs=[ANYWHERE] * len(parts),
         out_specs=ANYWHERE,
         scratch_shapes=[pltpu.SemaphoreType.DMA((members * len(parts),))],
-        compiler_params=PARAMS,
+        compiler_params=params(),
         name="place_results",
     )(*parts)
 
@@ -227,8 +229,6 @@
     members = groups * inner
     share = width // members
     rank = adapter_up_maps.shape[1]
-    pieces = 2 if share % (2 * LANES) == 0 else 1
-    piece = share // pieces
     me = group * inner + place_in_group
 
     def slices(array):
@@ -238,6 +238,14 @@
 
     def exchanged(blocks):
         return blocks[:1] + [to_partner(blocks[n], "inner", inner, n) for n in range(1, inner)]
+
+    def rings(blocks, near_after=(), far_after=(), second_after=()):
+        near = [after(jnp.concatenate(blocks[: inner // 2], axis=0), *near_after)]
+        far = [after(jnp.concatenate(blocks[inner // 2 :], axis=0), *far_after)]
+        for step in range(1, outer):
+            near.append(next_on_ring(after(near[-1], *second_after) if step == 2 else near[-1], outer))
+            far.append(next_on_ring(far[-1], outer))
+        return near, far
 
     steps_back = jnp.arange(outer, dtype=jnp.int32)[:, None]
     labels = ((level - steps_back + outer) % outer) * inner + (
@@ -246,30 +254,17 @@
     labels = labels.reshape(-1)
 
     down = exchanged(slices(adapter_down_maps[0].T))
-    near = [jnp.concatenate(down[: inner // 2], axis=0)]
-    far = [jnp.concatenate(down[inner // 2 :], axis=0)]
-    for _ in range(outer - 1):
-        near.append(next_on_ring(near[-1], outer))
-        far.append(next_on_ring(far[-1], outer))
-    down_maps = [m for pair in zip(near, far) for m in pair]
-
+    up = exchanged([after(block, down[1]) for block in slices(adapter_up_maps[0])])
     ids = token_adapter_index.astype(jnp.bfloat16).reshape(1, tok)
-    rows = swap(after(outgoing_rows(hidden, ids, members), *down[inner // 2 :]))
-
-    own_slices = slices(adapter_up_maps[0])
-    up = exchanged([after(block, rows) for block in own_slices])
-    held = [
-        [jnp.concatenate([b[:, n * piece : (n + 1) * piece] for b in up], axis=0)] for n in range(pieces)
-    ]
-    held[0][0] = after(held[0][0], near[-1])
-    held[-1][0] = after(held[-1][0], far[-1])
-    for ring in held:
-        for _ in range(outer - 1):
-            ring.append(next_on_ring(ring[-1], outer))
-
+    rows = swap(after(outgoing_rows(hidden, ids, members), *down[1:], *up[1:]))
+    down_near, down_far = rings(down, second_after=up[1:])
+    up_near, up_far = rings(up, near_after=[down_near[-1], rows], far_after=[down_far[-1]])
+
+    down_maps = [m for pair in zip(down_near, down_far) for m in pair]
+    up_maps = [m for pair in zip(up_near, up_far) for m in pair]
     packed, id_columns = down_product(labels, rows, down_maps, rank)
     shrunk = swap(summed_copies(swap(packed)))
-    return place([swap(up_product(labels, id_columns, shrunk, ring, rank)) for ring in held])
+    return place([swap(up_product(labels, id_columns, shrunk, up_maps, rank))])
 
 
 def solution(mesh):

time: 146 us -> 134 us (0.918)
  waiting for transfers between devices: 74.9 us -> 61.7 us
  blocking collectives: 25.7 us -> 29.7 us
  local copies, waits for them, and re-layouts: 9.05 us -> 6.67 us
    ppermute x12, waiting for transfers between devices: 61 us -> 47.9 us  [next_on_ring(): lax.ppermute(block, 'outer', [(i, (i + 1) % outer) for i in range(outer)])]
    all_to_all x2 -> x1, blocking collectives: 25.7 us -> 29.7 us  [swap(): return lax.all_to_all(value, PLANE, split_axis=0, concat_axis=0, tiled=True)]
    slice x4 -> x0, local copies, waits for them, and re-layouts: 2.51 us -> none  [per_device(): b[:, n * piece:(n + 1) * piece]]
    all_to_all x3, waiting for transfers between devices: 5.06 us -> 7.14 us  [swap(): return lax.all_to_all(value, PLANE, split_axis=0, concat_axis=0, tiled=True)]
    ppermute x6, waiting for transfers between devices: 8.79 us -> 6.72 us  [to_partner(): return lax.ppermute(value, axes, [(i, i ^ offset) for i in range(size)])]
    pallas_call x2 -> x1, Pallas kernels: 5.8 us -> 3.88 us  [up_product(): pl.pallas_call(functools.partial(up_kernel, len(maps), rank), out_shape=j...]
    unnamed x17 -> x12, local copies, waits for them, and re-layouts: 3.45 us -> 3.49 us
  transfers between devices with their start and end apart: 21 -> 21, of which waited for: 15 -> 15; matrix products, arithmetic and copies ran while one was open for 4% -> 2% of each run, Pallas kernels for 6% -> 5%
where the time goes in v7:
time: 134 us
  waiting for transfers between devices  61.7 us (46%)
  blocking collectives  29.7 us (22%)
  starting transfers between devices  22.8 us (17%)
  Pallas kernels  11.8 us (9%)
  local copies, waits for them, and re-layouts  6.67 us (5%)
    ppermute x12, waiting for transfers between devices, next_on_ring(): lax.ppermute(block, 'outer', [(i, (i + 1) % outer) for i in range(outer)])  47.9 us
    all_to_all x1, blocking collectives, swap(): return lax.all_to_all(value, PLANE, split_axis=0, concat_axis=0, tiled=True)  29.7 us
    all_to_all x3, starting transfers between devices, swap(): return lax.all_to_all(value, PLANE, split_axis=0, concat_axis=0, tiled=True)  11.4 us
    all_to_all x3, waiting for transfers between devices, swap(): return lax.all_to_all(value, PLANE, split_axis=0, concat_axis=0, tiled=True)  7.14 us
    ppermute x6, waiting for transfers between devices, to_partner(): return lax.ppermute(value, axes, [(i, i ^ offset) for i in range(size)])  6.72 us
    ppermute x12, starting transfers between devices, next_on_ring(): lax.ppermute(block, 'outer', [(i, (i + 1) % outer) for i in range(outer)])  6.14 us
    ppermute x6, starting transfers between devices, to_partner(): return lax.ppermute(value, axes, [(i, i ^ offset) for i in range(size)])  5.25 us
    pallas_call x1, Pallas kernels, down_product(): pl.pallas_call(functools.partial(down_kernel, len(maps), rank), out_shape...  4.35 us
  transfers between devices with their start and end apart: 21, of which 15 were waited for; matrix products, arithmetic and copies ran while one was open for 2% of the time, Pallas kernels for 5%

profile of v7, /device:TPU:0, one launch (start us, length us, event | category | flops | bytes accessed | tf_op | source)
XLA Modules:
  0.0 133.9 jit_solution(2961377821016133443)
XLA Ops:
  0.0 1.3 dynamic-slice_bitcast_fusion.1
  1.8 2.6 %collective-permute-start.1 = (bf16[64,1024]{1,0:T(8,128)(2,1)S(1)}, bf16[64,1024]{1,0:T(8,128)(2,1)S(1)}, u32[]{:S(2)}, u32[]{:S(2)}) collective-permute-start(bf16[64,1024]{1,0:T(8,128)(2,1)S(1)} %get-tuple-element.30), channel_id=1, source_target_pairs={{0,2},{1,3},{2,0},{3,1},{4,6},{5,7},{6,4},{7,5},{8,10},{9,11},{10,... | collective-permute-start | bytes 393224 | tf_op jit(solution)/shard_map/ppermute | solution.py:26
  4.5 1.8 %dynamic-slice_bitcast_fusion = (bf16[64,1024]{1,0:T(8,128)(2,1)}, bf16[64,1024]{1,0:T(8,128)(2,1)S(1)}, bf16[64,1024]{1,0:T(8,128)(2,1)S(1)}, bf16[64,1024]{1,0:T(8,128)(2,1)S(1)}) fusion(bf16[1,64,8192]{2,1,0:T(8,128)(2,1)} %param.7, s32[]{:T(128)S(6)} %select_n.32, s32[]{:T(128)S(6)} %select_n.30, s32[]{:T(128)S(6)} %select_n.29, s32[]{:T(128)S(6)} %select_n.31), kind=kLoop, calls=%fused_computation.4 | loop fusion | bytes 1048592 | tf_op jit(solution)/shard_map/dynamic_slice | solution.py:236
  6.4 1.9 %collective-permute-start.4 = (bf16[64,1024]{1,0:T(8,128)(2,1)S(1)}, bf16[64,1024]{1,0:T(8,128)(2,1)S(1)}, u32[]{:S(2)}, u32[]{:S(2)}) collective-permute-start(bf16[64,1024]{1,0:T(8,128)(2,1)S(1)} %get-tuple-element.16), channel_id=1, source_target_pairs={{0,2},{1,3},{2,0},{3,1},{4,6},{5,7},{6,4},{7,5},{8,10},{9,11},{10,... | collective-permute-start | bytes 393224 | tf_op jit(solution)/shard_map/ppermute | solution.py:26
  8.4 1.5 %outgoing_rows.1 = bf16[8,136,1024]{2,1,0:T(8,128)(2,1)} custom-call(bf16[128,8192]{1,0:T(8,128)(2,1)S(1)} %copy-done, bf16[8,1024]{1,0:T(8,128)(2,1)S(1)} %broadcast_in_dim.10.ids_ref), custom_call_target="tpu_custom_call" | custom-call | tf_op jit(solution)/shard_map/outgoing_rows/pallas_call | solution.py:62
  9.9 1.1 collective-permute-done.2
  11.0 3.3 %collective-permute-done.4 = bf16[64,1024]{1,0:T(8,128)(2,1)S(1)} collective-permute-done((bf16[64,1024]{1,0:T(8,128)(2,1)S(1)}, bf16[64,1024]{1,0:T(8,128)(2,1)S(1)}, u32[]{:S(2)}, u32[]{:S(2)}) %collective-permute-start.4) | collective-permute-done | bytes 131104 | tf_op jit(solution)/shard_map/ppermute | solution.py:26
  14.4 2.3 %collective-permute-done.5 = bf16[64,1024]{1,0:T(8,128)(2,1)S(1)} collective-permute-done((bf16[64,1024]{1,0:T(8,128)(2,1)S(1)}, bf16[64,1024]{1,0:T(8,128)(2,1)S(1)}, u32[]{:S(2)}, u32[]{:S(2)}) %collective-permute-start.5) | collective-permute-done | bytes 131104 | tf_op jit(solution)/shard_map/ppermute | solution.py:26
  16.7 3.8 %all-to-all-start = ((bf16[8,136,1024]{2,1,0:T(8,128)(2,1)}), bf16[8,136,1024]{2,1,0:T(8,128)(2,1)S(1)}, u32[]{:S(2)}, u32[]{:S(2)}) async-start(bf16[8,136,1024]{2,1,0:T(8,128)(2,1)} %outgoing_rows.1), calls=%async_computation | async-start | bytes 4456448 | tf_op jit(solution)/shard_map/all_to_all | solution.py:38
  20.4 1.6 %collective-permute-start.7 = (bf16[128,1024]{1,0:T(8,128)(2,1)S(1)}, bf16[128,1024]{1,0:T(8,128)(2,1)S(1)}, u32[]{:S(2)}, u32[]{:S(2)}) collective-permute-start(bf16[128,1024]{1,0:T(8,128)(2,1)S(1)} %pad_maximum_fusion.1.refs_1_), channel_id=1, source_target_pairs={{0,4},{4,8},{8,12},{12,0},{1,5},{5,9},{9,13},{13,1},{2,6},{6,10},{... | collective-permute-start | bytes 786440 | tf_op jit(solution)/shard_map/ppermute | solution.py:30
  22.1 1.6 %collective-permute-start.6 = (bf16[128,1024]{1,0:T(8,128)(2,1)S(1)}, bf16[128,1024]{1,0:T(8,128)(2,1)S(1)}, u32[]{:S(2)}, u32[]{:S(2)}) collective-permute-start(bf16[128,1024]{1,0:T(8,128)(2,1)S(1)} %pad_maximum_fusion.refs_0_), channel_id=1, source_target_pairs={{0,4},{4,8},{8,12},{12,0},{1,5},{5,9},{9,13},{13,1},{2,6},{6,10},{... | collective-permute-start | bytes 786440 | tf_op jit(solution)/shard_map/ppermute | solution.py:30
  23.7 7.7 %collective-permute-done.7.refs_3_ = bf16[128,1024]{1,0:T(8,128)(2,1)S(1)} collective-permute-done((bf16[128,1024]{1,0:T(8,128)(2,1)S(1)}, bf16[128,1024]{1,0:T(8,128)(2,1)S(1)}, u32[]{:S(2)}, u32[]{:S(2)}) %collective-permute-start.7) | collective-permute-done | bytes 262176 | tf_op jit(solution)/shard_map/ppermute | solution.py:30
  31.4 5.6 %collective-permute-done.6.refs_2_ = bf16[128,1024]{1,0:T(8,128)(2,1)S(1)} collective-permute-done((bf16[128,1024]{1,0:T(8,128)(2,1)S(1)}, bf16[128,1024]{1,0:T(8,128)(2,1)S(1)}, u32[]{:S(2)}, u32[]{:S(2)}) %collective-permute-start.6) | collective-permute-done | bytes 262176 | tf_op jit(solution)/shard_map/ppermute | solution.py:30
  37.7 5.0 %collective-permute-done.9.refs_5_ = bf16[128,1024]{1,0:T(8,128)(2,1)} collective-permute-done((bf16[128,1024]{1,0:T(8,128)(2,1)S(1)}, bf16[128,1024]{1,0:T(8,128)(2,1)}, u32[]{:S(2)}, u32[]{:S(2)}) %collective-permute-start.9) | collective-permute-done | bytes 262176 | tf_op jit(solution)/shard_map/ppermute | solution.py:30
  42.7 5.6 %collective-permute-done.8.refs_4_ = bf16[128,1024]{1,0:T(8,128)(2,1)} collective-permute-done((bf16[128,1024]{1,0:T(8,128)(2,1)S(1)}, bf16[128,1024]{1,0:T(8,128)(2,1)}, u32[]{:S(2)}, u32[]{:S(2)}) %collective-permute-start.8) | collective-permute-done | bytes 262176 | tf_op jit(solution)/shard_map/ppermute | solution.py:30
  49.4 4.7 %collective-permute-done.11.refs_7_ = bf16[128,1024]{1,0:T(8,128)(2,1)} collective-permute-done((bf16[128,1024]{1,0:T(8,128)(2,1)}, bf16[128,1024]{1,0:T(8,128)(2,1)}, u32[]{:S(2)}, u32[]{:S(2)}) %collective-permute-start.11) | collective-permute-done | bytes 262176 | tf_op jit(solution)/shard_map/ppermute | solution.py:30
  54.1 5.6 %collective-permute-done.10.refs_6_ = bf16[128,1024]{1,0:T(8,128)(2,1)} collective-permute-done((bf16[128,1024]{1,0:T(8,128)(2,1)}, bf16[128,1024]{1,0:T(8,128)(2,1)}, u32[]{:S(2)}, u32[]{:S(2)}) %collective-permute-start.10) | collective-permute-done | bytes 262176 | tf_op jit(solution)/shard_map/ppermute | solution.py:30
  59.9 5.4 %collective-permute-done.13.refs_3_ = bf16[128,1024]{1,0:T(8,128)(2,1)} collective-permute-done((bf16[128,1024]{1,0:T(8,128)(2,1)S(1)}, bf16[128,1024]{1,0:T(8,128)(2,1)}, u32[]{:S(2)}, u32[]{:S(2)}) %collective-permute-start.13) | collective-permute-done | bytes 262176 | tf_op jit(solution)/shard_map/ppermute | solution.py:30
  65.3 5.6 %collective-permute-done.12.refs_2_ = bf16[128,1024]{1,0:T(8,128)(2,1)} collective-permute-done((bf16[128,1024]{1,0:T(8,128)(2,1)S(1)}, bf16[128,1024]{1,0:T(8,128)(2,1)}, u32[]{:S(2)}, u32[]{:S(2)}) %collective-permute-start.12) | collective-permute-done | bytes 262176 | tf_op jit(solution)/shard_map/ppermute | solution.py:30
  71.9 4.3 %down_product.1 = (f32[8,64,128]{2,1,0:T(8,128)}, f32[8,128,128]{2,1,0:T(8,128)S(1)}) custom-call(s32[16]{0:T(128)S(1)} %add.62.labels_ref, bf16[8,136,1024]{2,1,0:T(8,128)(2,1)S(1)} %all-to-all-done.rows_ref, bf16[128,1024]{1,0:T(8,128)(2,1)S(1)} %pad_maximum_fusion.refs_0_, bf16[128,1024]{1,0:T(8,128)(2,1)S(1)} %pad_maximum_fusion.1.refs_1_, ...), custom_call_target="tpu_custom_call" | custom-call | flops 2147483648 | bytes 4194304 | tf_op jit(solution)/shard_map/down_product/pallas_call | solution.py:112
  77.0 4.2 %all-to-all-start.1 = ((f32[8,64,128]{2,1,0:T(8,128)}), f32[8,64,128]{2,1,0:T(8,128)S(1)}, u32[]{:S(2)}, u32[]{:S(2)}) async-start(f32[8,64,128]{2,1,0:T(8,128)} %get-tuple-element.21), calls=%async_computation.1 | async-start | bytes 524288 | tf_op jit(solution)/shard_map/all_to_all | solution.py:38
  81.3 1.3 collective-permute-start.17
  82.6 1.6 %collective-permute-start.16 = (bf16[128,1024]{1,0:T(8,128)(2,1)}, bf16[128,1024]{1,0:T(8,128)(2,1)S(1)}, u32[]{:S(2)}, u32[]{:S(2)}) collective-permute-start(bf16[128,1024]{1,0:T(8,128)(2,1)} %collective-permute-done.14.refs_4_), channel_id=1, source_target_pairs={{0,4},{4,8},{8,12},{12,0},{1,5},{5,9},{9,13},{13,1},{2,6},{6,10},{... | collective-permute-start | bytes 786440 | tf_op jit(solution)/shard_map/ppermute | solution.py:30
  84.2 3.2 %all-to-all-done.1.terms_ref = f32[8,64,128]{2,1,0:T(8,128)S(1)} async-done(((f32[8,64,128]{2,1,0:T(8,128)}), f32[8,64,128]{2,1,0:T(8,128)S(1)}, u32[]{:S(2)}, u32[]{:S(2)}) %all-to-all-start.1) | async-done | bytes 262176 | tf_op jit(solution)/shard_map/all_to_all | solution.py:38
  88.0 3.4 %all-to-all-start.2 = ((bf16[8,64,128]{2,1,0:T(8,128)(2,1)}), bf16[8,64,128]{2,1,0:T(8,128)(2,1)S(1)}, u32[]{:S(2)}, u32[]{:S(2)}) async-start(bf16[8,64,128]{2,1,0:T(8,128)(2,1)} %summed_copies.1), calls=%async_computation.2 | async-start | bytes 262144 | tf_op jit(solution)/shard_map/all_to_all | solution.py:38
  91.4 1.2 collective-permute-done.17.refs_7_
  92.5 4.0 %all-to-all-done.2.shrunk_ref = bf16[8,64,128]{2,1,0:T(8,128)(2,1)S(1)} async-done(((bf16[8,64,128]{2,1,0:T(8,128)(2,1)}), bf16[8,64,128]{2,1,0:T(8,128)(2,1)S(1)}, u32[]{:S(2)}, u32[]{:S(2)}) %all-to-all-start.2) | async-done | bytes 131104 | tf_op jit(solution)/shard_map/all_to_all | solution.py:38
  96.5 1.4 %collective-permute-done.16.refs_6_ = bf16[128,1024]{1,0:T(8,128)(2,1)S(1)} collective-permute-done((bf16[128,1024]{1,0:T(8,128)(2,1)}, bf16[128,1024]{1,0:T(8,128)(2,1)S(1)}, u32[]{:S(2)}, u32[]{:S(2)}) %collective-permute-start.16) | collective-permute-done | bytes 262176 | tf_op jit(solution)/shard_map/ppermute | solution.py:30
  97.9 1.0 copy-done.4
  99.0 3.9 %up_product.1 = bf16[8,128,1024]{2,1,0:T(8,128)(2,1)S(1)} custom-call(s32[16]{0:T(128)S(1)} %add.62.labels_ref, f32[8,128,128]{2,1,0:T(8,128)S(1)} %copy-done.4, bf16[8,64,128]{2,1,0:T(8,128)(2,1)S(1)} %all-to-all-done.2.shrunk_ref, bf16[128,1024]{1,0:T(8,128)(2,1)S(1)} %pad_maximum_fusion.2.refs_0_, bf16[128,1024]{1,0:T(8,128)(2,1)S(1)} %pad_maximum_fusion.3.refs_1_, ...), custom_call_target="tpu_custom_call" | custom-call | flops 2147483648 | bytes 4194304 | tf_op jit(solution)/shard_map/up_product/pallas_call | solution.py:182
  102.8 29.7 %all_to_all.20.refs_0_ = bf16[8,128,1024]{2,1,0:T(8,128)(2,1)S(1)} all-to-all(bf16[8,128,1024]{2,1,0:T(8,128)(2,1)S(1)} %up_product.1), channel_id=1, replica_groups=mesh['groups'=2,'outer'=4,'inner'=4] {'groups','inner'}, dimensions={0} | all-to-all | bytes 4194304 | tf_op jit(solution)/shard_map/all_to_all | solution.py:38
  132.5 1.4 %place_results.1 = bf16[128,8192]{1,0:T(8,128)(2,1)} custom-call(bf16[8,128,1024]{2,1,0:T(8,128)(2,1)S(1)} %all_to_all.20.refs_0_), custom_call_target="tpu_custom_call" | custom-call | tf_op jit(solution)/shard_map/place_results/pallas_call | solution.py:214
  (40 shorter events, 5.1 us)
Async XLA Ops:
  0.0 8.3 %copy-start.5 = (s32[128,1]{0,1:T(1,128)S(1)}, s32[128,1]{0,1:T(1,128)}, u32[]{:S(2)}) copy-start(s32[128,1]{0,1:T(1,128)} %param.4) | copy-start | bytes 1540
  0.0 8.4 %copy-start = (bf16[128,8192]{1,0:T(8,128)(2,1)S(1)}, bf16[128,8192]{1,0:T(8,128)(2,1)}, u32[]{:S(2)}) copy-start(bf16[128,8192]{1,0:T(8,128)(2,1)} %hidden_ref.1) | copy-start | bytes 6291460
  1.3 5.0 %collective-permute-start = (bf16[64,1024]{1,0:T(8,128)(2,1)S(1)}, bf16[64,1024]{1,0:T(8,128)(2,1)S(1)}, u32[]{:S(2)}, u32[]{:S(2)}) collective-permute-start(bf16[64,1024]{1,0:T(8,128)(2,1)S(1)} %get-tuple-element.31), channel_id=1, source_target_pairs={{0,1},{1,0},{2,3},{3,2},{4,5},{5,4},{6,7},{7,6},{8,9},{9,8},{10,11... | collective-permute-start | bytes 393224 | tf_op jit(solution)/shard_map/ppermute | solution.py:26
  1.8 8.1 %collective-permute-start.1 = (bf16[64,1024]{1,0:T(8,128)(2,1)S(1)}, bf16[64,1024]{1,0:T(8,128)(2,1)S(1)}, u32[]{:S(2)}, u32[]{:S(2)}) collective-permute-start(bf16[64,1024]{1,0:T(8,128)(2,1)S(1)} %get-tuple-element.30), channel_id=1, source_target_pairs={{0,2},{1,3},{2,0},{3,1},{4,6},{5,7},{6,4},{7,5},{8,10},{9,11},{10,... | collective-permute-start | bytes 393224 | tf_op jit(solution)/shard_map/ppermute | solution.py:26
  4.4 6.6 %collective-permute-start.2 = (bf16[64,1024]{1,0:T(8,128)(2,1)S(1)}, bf16[64,1024]{1,0:T(8,128)(2,1)S(1)}, u32[]{:S(2)}, u32[]{:S(2)}) collective-permute-start(bf16[64,1024]{1,0:T(8,128)(2,1)S(1)} %get-tuple-element.32), channel_id=1, source_target_pairs={{0,3},{1,2},{2,1},{3,0},{4,7},{5,6},{6,5},{7,4},{8,11},{9,10},{10,... | collective-permute-start | bytes 393224 | tf_op jit(solution)/shard_map/ppermute | solution.py:26
  6.3 4.8 %collective-permute-start.3 = (bf16[64,1024]{1,0:T(8,128)(2,1)S(1)}, bf16[64,1024]{1,0:T(8,128)(2,1)}, u32[]{:S(2)}, u32[]{:S(2)}) collective-permute-start(bf16[64,1024]{1,0:T(8,128)(2,1)S(1)} %get-tuple-element.15), channel_id=1, source_target_pairs={{0,1},{1,0},{2,3},{3,2},{4,5},{5,4},{6,7},{7,6},{8,9},{9,8},{10,11... | collective-permute-start | bytes 393224 | tf_op jit(solution)/shard_map/ppermute | solution.py:26
  6.4 8.0 %collective-permute-start.4 = (bf16[64,1024]{1,0:T(8,128)(2,1)S(1)}, bf16[64,1024]{1,0:T(8,128)(2,1)S(1)}, u32[]{:S(2)}, u32[]{:S(2)}) collective-permute-start(bf16[64,1024]{1,0:T(8,128)(2,1)S(1)} %get-tuple-element.16), channel_id=1, source_target_pairs={{0,2},{1,3},{2,0},{3,1},{4,6},{5,7},{6,4},{7,5},{8,10},{9,11},{10,... | collective-permute-start | bytes 393224 | tf_op jit(solution)/shard_map/ppermute | solution.py:26
  8.3 8.3 %collective-permute-start.5 = (bf16[64,1024]{1,0:T(8,128)(2,1)S(1)}, bf16[64,1024]{1,0:T(8,128)(2,1)S(1)}, u32[]{:S(2)}, u32[]{:S(2)}) collective-permute-start(bf16[64,1024]{1,0:T(8,128)(2,1)S(1)} %get-tuple-element.17), channel_id=1, source_target_pairs={{0,3},{1,2},{2,1},{3,0},{4,7},{5,6},{6,5},{7,4},{8,11},{9,10},{10,... | collective-permute-start | bytes 393224 | tf_op jit(solution)/shard_map/ppermute | solution.py:26
  16.7 43.1 %all-to-all-start = ((bf16[8,136,1024]{2,1,0:T(8,128)(2,1)}), bf16[8,136,1024]{2,1,0:T(8,128)(2,1)S(1)}, u32[]{:S(2)}, u32[]{:S(2)}) async-start(bf16[8,136,1024]{2,1,0:T(8,128)(2,1)} %outgoing_rows.1), calls=%async_computation | async-start | bytes 4456448 | tf_op jit(solution)/shard_map/all_to_all | solution.py:38
  20.4 10.9 %collective-permute-start.7 = (bf16[128,1024]{1,0:T(8,128)(2,1)S(1)}, bf16[128,1024]{1,0:T(8,128)(2,1)S(1)}, u32[]{:S(2)}, u32[]{:S(2)}) collective-permute-start(bf16[128,1024]{1,0:T(8,128)(2,1)S(1)} %pad_maximum_fusion.1.refs_1_), channel_id=1, source_target_pairs={{0,4},{4,8},{8,12},{12,0},{1,5},{5,9},{9,13},{13,1},{2,6},{6,10},{... | collective-permute-start | bytes 786440 | tf_op jit(solution)/shard_map/ppermute | solution.py:30
  22.1 14.9 %collective-permute-start.6 = (bf16[128,1024]{1,0:T(8,128)(2,1)S(1)}, bf16[128,1024]{1,0:T(8,128)(2,1)S(1)}, u32[]{:S(2)}, u32[]{:S(2)}) collective-permute-start(bf16[128,1024]{1,0:T(8,128)(2,1)S(1)} %pad_maximum_fusion.refs_0_), channel_id=1, source_target_pairs={{0,4},{4,8},{8,12},{12,0},{1,5},{5,9},{9,13},{13,1},{2,6},{6,10},{... | collective-permute-start | bytes 786440 | tf_op jit(solution)/shard_map/ppermute | solution.py:30
  31.4 11.3 %collective-permute-start.9 = (bf16[128,1024]{1,0:T(8,128)(2,1)S(1)}, bf16[128,1024]{1,0:T(8,128)(2,1)}, u32[]{:S(2)}, u32[]{:S(2)}) collective-permute-start(bf16[128,1024]{1,0:T(8,128)(2,1)S(1)} %collective-permute-done.7.refs_3_), channel_id=1, source_target_pairs={{0,4},{4,8},{8,12},{12,0},{1,5},{5,9},{9,13},{13,1},{2,6},{6,10},{... | collective-permute-start | bytes 786440 | tf_op jit(solution)/shard_map/ppermute | solution.py:30
  37.0 11.3 %collective-permute-start.8 = (bf16[128,1024]{1,0:T(8,128)(2,1)S(1)}, bf16[128,1024]{1,0:T(8,128)(2,1)}, u32[]{:S(2)}, u32[]{:S(2)}) collective-permute-start(bf16[128,1024]{1,0:T(8,128)(2,1)S(1)} %collective-permute-done.6.refs_2_), channel_id=1, source_target_pairs={{0,4},{4,8},{8,12},{12,0},{1,5},{5,9},{9,13},{13,1},{2,6},{6,10},{... | collective-permute-start | bytes 786440 | tf_op jit(solution)/shard_map/ppermute | solution.py:30
  37.0 0.7 copy-start.1
  42.7 11.4 %collective-permute-start.11 = (bf16[128,1024]{1,0:T(8,128)(2,1)}, bf16[128,1024]{1,0:T(8,128)(2,1)}, u32[]{:S(2)}, u32[]{:S(2)}) collective-permute-start(bf16[128,1024]{1,0:T(8,128)(2,1)} %collective-permute-done.9.refs_5_), channel_id=1, source_target_pairs={{0,4},{4,8},{8,12},{12,0},{1,5},{5,9},{9,13},{13,1},{2,6},{6,10},{... | collective-permute-start | bytes 786440 | tf_op jit(solution)/shard_map/ppermute | solution.py:30
  48.3 11.4 %collective-permute-start.10 = (bf16[128,1024]{1,0:T(8,128)(2,1)}, bf16[128,1024]{1,0:T(8,128)(2,1)}, u32[]{:S(2)}, u32[]{:S(2)}) collective-permute-start(bf16[128,1024]{1,0:T(8,128)(2,1)} %collective-permute-done.8.refs_4_), channel_id=1, source_target_pairs={{0,4},{4,8},{8,12},{12,0},{1,5},{5,9},{9,13},{13,1},{2,6},{6,10},{... | collective-permute-start | bytes 786440 | tf_op jit(solution)/shard_map/ppermute | solution.py:30
  54.1 11.2 %collective-permute-start.13 = (bf16[128,1024]{1,0:T(8,128)(2,1)S(1)}, bf16[128,1024]{1,0:T(8,128)(2,1)}, u32[]{:S(2)}, u32[]{:S(2)}) collective-permute-start(bf16[128,1024]{1,0:T(8,128)(2,1)S(1)} %pad_maximum_fusion.3.refs_1_), channel_id=1, source_target_pairs={{0,4},{4,8},{8,12},{12,0},{1,5},{5,9},{9,13},{13,1},{2,6},{6,10},{... | collective-permute-start | bytes 786440 | tf_op jit(solution)/shard_map/ppermute | solution.py:30
  59.7 11.2 %collective-permute-start.12 = (bf16[128,1024]{1,0:T(8,128)(2,1)S(1)}, bf16[128,1024]{1,0:T(8,128)(2,1)}, u32[]{:S(2)}, u32[]{:S(2)}) collective-permute-start(bf16[128,1024]{1,0:T(8,128)(2,1)S(1)} %pad_maximum_fusion.2.refs_0_), channel_id=1, source_target_pairs={{0,4},{4,8},{8,12},{12,0},{1,5},{5,9},{9,13},{13,1},{2,6},{6,10},{... | collective-permute-start | bytes 786440 | tf_op jit(solution)/shard_map/ppermute | solution.py:30
  65.3 16.0 %collective-permute-start.15 = (bf16[128,1024]{1,0:T(8,128)(2,1)}, bf16[128,1024]{1,0:T(8,128)(2,1)}, u32[]{:S(2)}, u32[]{:S(2)}) collective-permute-start(bf16[128,1024]{1,0:T(8,128)(2,1)} %collective-permute-done.13.refs_3_), channel_id=1, source_target_pairs={{0,4},{4,8},{8,12},{12,0},{1,5},{5,9},{9,13},{13,1},{2,6},{6,10},{... | collective-permute-start | bytes 786440 | tf_op jit(solution)/shard_map/ppermute | solution.py:30
  70.9 11.7 %collective-permute-start.14 = (bf16[128,1024]{1,0:T(8,128)(2,1)}, bf16[128,1024]{1,0:T(8,128)(2,1)}, u32[]{:S(2)}, u32[]{:S(2)}) collective-permute-start(bf16[128,1024]{1,0:T(8,128)(2,1)} %collective-permute-done.12.refs_2_), channel_id=1, source_target_pairs={{0,4},{4,8},{8,12},{12,0},{1,5},{5,9},{9,13},{13,1},{2,6},{6,10},{... | collective-permute-start | bytes 786440 | tf_op jit(solution)/shard_map/ppermute | solution.py:30
  70.9 1.0 copy-start.2
  76.2 0.8 copy-start.3
  77.0 10.3 %all-to-all-start.1 = ((f32[8,64,128]{2,1,0:T(8,128)}), f32[8,64,128]{2,1,0:T(8,128)S(1)}, u32[]{:S(2)}, u32[]{:S(2)}) async-start(f32[8,64,128]{2,1,0:T(8,128)} %get-tuple-element.21), calls=%async_computation.1 | async-start | bytes 524288 | tf_op jit(solution)/shard_map/all_to_all | solution.py:38
  81.3 11.2 %collective-permute-start.17 = (bf16[128,1024]{1,0:T(8,128)(2,1)}, bf16[128,1024]{1,0:T(8,128)(2,1)S(1)}, u32[]{:S(2)}, u32[]{:S(2)}) collective-permute-start(bf16[128,1024]{1,0:T(8,128)(2,1)} %collective-permute-done.15.refs_5_), channel_id=1, source_target_pairs={{0,4},{4,8},{8,12},{12,0},{1,5},{5,9},{9,13},{13,1},{2,6},{6,10},{... | collective-permute-start | bytes 786440 | tf_op jit(solution)/shard_map/ppermute | solution.py:30
  82.6 15.3 %collective-permute-start.16 = (bf16[128,1024]{1,0:T(8,128)(2,1)}, bf16[128,1024]{1,0:T(8,128)(2,1)S(1)}, u32[]{:S(2)}, u32[]{:S(2)}) collective-permute-start(bf16[128,1024]{1,0:T(8,128)(2,1)} %collective-permute-done.14.refs_4_), channel_id=1, source_target_pairs={{0,4},{4,8},{8,12},{12,0},{1,5},{5,9},{9,13},{13,1},{2,6},{6,10},{... | collective-permute-start | bytes 786440 | tf_op jit(solution)/shard_map/ppermute | solution.py:30
  88.0 8.5 %all-to-all-start.2 = ((bf16[8,64,128]{2,1,0:T(8,128)(2,1)}), bf16[8,64,128]{2,1,0:T(8,128)(2,1)S(1)}, u32[]{:S(2)}, u32[]{:S(2)}) async-start(bf16[8,64,128]{2,1,0:T(8,128)(2,1)} %summed_copies.1), calls=%async_computation.2 | async-start | bytes 262144 | tf_op jit(solution)/shard_map/all_to_all | solution.py:38
  97.9 1.0 copy-start.4

commit v8 on v7

--- a/solution.py
+++ b/solution.py
@@ -15,6 +15,7 @@
 BLOCK = 8
 IN_VMEM = pl.BlockSpec(memory_space=pltpu.VMEM)
 IN_SMEM = pl.BlockSpec(memory_space=pltpu.SMEM)
+IN_HBM = pl.BlockSpec(memory_space=pltpu.HBM)
 ANYWHERE = pl.BlockSpec(memory_space=pl.ANY)
 
 
@@ -70,7 +71,7 @@
 
 
 def down_kernel(map_count, rank, labels_ref, rows_ref, *refs):
-    maps, (packed_ref, ids_ref, total_ref) = refs[:map_count], refs[map_count:]
+    maps, (packed_ref, ids_out, total_ref, ids_ref, sem) = refs[:map_count], refs[map_count:]
     members, rows, share = rows_ref.shape
     tok = rows - ID_ROWS
     block = min(BLOCK, members)
@@ -83,7 +84,10 @@
             row = rows_ref[first + n, tok : tok + 1, :LANES].astype(jnp.float32)
             ids_ref[first + n] = jnp.broadcast_to(row, (LANES, tok)).T
         tokens = rows_ref[pl.ds(first, block), :tok, :].reshape(block * tok, share)
-        ids = ids_ref[pl.ds(first, block)].reshape(block * tok, LANES)
+        here = pl.ds(first, block)
+        kept = pltpu.make_async_copy(ids_ref.at[here], ids_out.at[here], sem)
+        kept.start()
+        ids = ids_ref[here].reshape(block * tok, LANES)
         tile = 0
         for at in range(0, map_count, 2):
             some = jnp.concatenate([m[...] for m in maps[at : at + 2]], axis=0)
@@ -100,6 +104,7 @@
             total = total_ref[n * tok : (n + 1) * tok, :]
             total += pltpu.roll(total, LANES // 2, 1)
             packed_ref[first + n] = jnp.where(lane < rank, total[:half], total[half:])
+        kept.wait()
         return 0
 
     lax.fori_loop(0, members // block, one, 0)
@@ -116,9 +121,13 @@
             jax.ShapeDtypeStruct((members, tok, LANES), jnp.float32),
         ],
         in_specs=[IN_SMEM, IN_VMEM] + [IN_VMEM] * len(maps),
-        out_specs=[IN_VMEM, IN_VMEM],
-        scratch_shapes=[pltpu.VMEM((min(BLOCK, members) * tok, LANES), jnp.float32)],
-        compiler_params=params(4 * min(BLOCK, members) * tok * LANES),
+        out_specs=[IN_VMEM, IN_HBM],
+        scratch_shapes=[
+            pltpu.VMEM((min(BLOCK, members) * tok, LANES), jnp.float32),
+            pltpu.VMEM((members, tok, LANES), jnp.float32),
+            pltpu.SemaphoreType.DMA,
+        ],
+        compiler_params=params(8 * members * tok * LANES),
         cost_estimate=pl.CostEstimate(
             flops=2 * map_rows * members * tok * share,
             bytes_accessed=2 * share * (map_rows + members * tok),
@@ -146,13 +155,16 @@
 
 
 def up_kernel(map_count, rank, labels_ref, ids_ref, shrunk_ref, *refs):
-    maps, (out_ref, spread_ref) = refs[:map_count], refs[map_count:]
+    maps, (out_ref, spread_ref, ids_buf, sem) = refs[:map_count], refs[map_count:]
+    kept = pltpu.make_async_copy(ids_ref, ids_buf, sem)
+    kept.start()
     members, half, _ = shrunk_ref.shape
     tok = 2 * half
     block = min(BLOCK, members)
     tiles = spread_ref.shape[1] // LANES
     lane = lax.broadcasted_iota(jnp.int32, (half, LANES), 1)
     held = jnp.concatenate([m[...] for m in maps], axis=0)
+    kept.wait()
 
     def one(step, _):
         first = step * block
@@ -162,7 +174,7 @@
             shrunk = jnp.concatenate(
                 [jnp.where(lane < rank, packed, turned), jnp.where(lane < rank, turned, packed)], axis=0
             )
-            ids = ids_ref[first + n]
+            ids = ids_buf[first + n]
             for tile in range(tiles):
                 named = ids == tile_labels(labels_ref, tile, rank, (1, LANES))
                 spread_ref[n * tok : (n + 1) * tok, tile * LANES : (tile + 1) * LANES] = jnp.where(
@@ -182,10 +194,14 @@
     return pl.pallas_call(
         functools.partial(up_kernel, len(maps), rank),
         out_shape=jax.ShapeDtypeStruct((members, tok, piece), jnp.bfloat16),
-        in_specs=[IN_SMEM, IN_VMEM, IN_VMEM] + [IN_VMEM] * len(maps),
+        in_specs=[IN_SMEM, IN_HBM, IN_VMEM] + [IN_VMEM] * len(maps),
         out_specs=IN_VMEM,
-        scratch_shapes=[pltpu.VMEM((min(BLOCK, members) * tok, map_rows), jnp.bfloat16)],
-        compiler_params=params(2 * min(BLOCK, members) * tok * map_rows),
+        scratch_shapes=[
+            pltpu.VMEM((min(BLOCK, members) * tok, map_rows), jnp.bfloat16),
+            pltpu.VMEM((members, tok, LANES), jnp.float32),
+            pltpu.SemaphoreType.DMA,
+        ],
+        compiler_params=params(2 * min(BLOCK, members) * tok * map_rows + 4 * members * tok * LANES),
         cost_estimate=pl.CostEstimate(
             flops=2 * map_rows * members * tok * piece,
             bytes_accessed=2 * piece * (map_rows + members * tok),
@@ -255,14 +271,14 @@
 
     down = exchanged(slices(adapter_down_maps[0].T))
     up = exchanged([after(block, down[1]) for block in slices(adapter_up_maps[0])])
+    down_near, down_far = rings(down, second_after=up[1:])
     ids = token_adapter_index.astype(jnp.bfloat16).reshape(1, tok)
-    rows = swap(after(outgoing_rows(hidden, ids, members), *down[1:], *up[1:]))
-    down_near, down_far = rings(down, second_after=up[1:])
-    up_near, up_far = rings(up, near_after=[down_near[-1], rows], far_after=[down_far[-1]])
+    rows = swap(after(outgoing_rows(hidden, ids, members), *up[1:], down_near[1], down_far[1]))
 
     down_maps = [m for pair in zip(down_near, down_far) for m in pair]
+    packed, id_columns = down_product(labels, rows, down_maps, rank)
+    up_near, up_far = rings(up, [down_near[-1]], [down_far[-1]], second_after=[packed])
     up_maps = [m for pair in zip(up_near, up_far) for m in pair]
-    packed, id_columns = down_product(labels, rows, down_maps, rank)
     shrunk = swap(summed_copies(swap(packed)))
     return place([swap(up_product(labels, id_columns, shrunk, up_maps, rank))])
 

time: 134 us -> 128 us (0.955)
  waiting for transfers between devices: 61.7 us -> 49.2 us
  local copies, waits for them, and re-layouts: 6.67 us -> 9.24 us
  starting transfers between devices: 22.8 us -> 25 us
    ppermute x12, waiting for transfers between devices: 47.9 us -> 33.3 us  [next_on_ring(): lax.ppermute(block, 'outer', [(i, (i + 1) % outer) for i in range(outer)])]
    ppermute x6, waiting for transfers between devices: 6.72 us -> 9.57 us  [to_partner(): return lax.ppermute(value, axes, [(i, i ^ offset) for i in range(size)])]
    unnamed x12 -> x26, local copies, waits for them, and re-layouts: 3.49 us -> 6.07 us
    ppermute x12, starting transfers between devices: 6.14 us -> 8.63 us  [next_on_ring(): lax.ppermute(block, 'outer', [(i, (i + 1) % outer) for i in range(outer)])]
  transfers between devices with their start and end apart: 21 -> 21, of which waited for: 15 -> 14; matrix products, arithmetic and copies ran while one was open for 2% -> 3% of each run, Pallas kernels for 5% -> 5%
where the time goes in v8:
time: 128 us; the launch traced here: 127 us
  waiting for transfers between devices  49.2 us (38%)
  blocking collectives  29.6 us (23%)
  starting transfers between devices  25 us (20%)
  Pallas kernels  12.2 us (10%)
  local copies, waits for them, and re-layouts  9.24 us (7%)
  other arithmetic  2.1 us (2%)
    ppermute x12, waiting for transfers between devices, next_on_ring(): lax.ppermute(block, 'outer', [(i, (i + 1) % outer) for i in range(outer)])  33.3 us
    all_to_all x1, blocking collectives, swap(): return lax.all_to_all(value, PLANE, split_axis=0, concat_axis=0, tiled=True)  29.6 us
    all_to_all x3, starting transfers between devices, swap(): return lax.all_to_all(value, PLANE, split_axis=0, concat_axis=0, tiled=True)  11.3 us
    ppermute x6, waiting for transfers between devices, to_partner(): return lax.ppermute(value, axes, [(i, i ^ offset) for i in range(size)])  9.57 us
    ppermute x12, starting transfers between devices, next_on_ring(): lax.ppermute(block, 'outer', [(i, (i + 1) % outer) for i in range(outer)])  8.63 us
    all_to_all x3, waiting for transfers between devices, swap(): return lax.all_to_all(value, PLANE, split_axis=0, concat_axis=0, tiled=True)  6.31 us
    unnamed x26, local copies, waits for them, and re-layouts  6.07 us
    ppermute x6, starting transfers between devices, to_partner(): return lax.ppermute(value, axes, [(i, i ^ offset) for i in range(size)])  5.06 us
  transfers between devices with their start and end apart: 21, of which 14 were waited for; matrix products, arithmetic and copies ran while one was open for 3% of the time, Pallas kernels for 5%

profile of v8, /device:TPU:0, one launch (start us, length us, event | category | flops | bytes accessed | tf_op | source)
XLA Modules:
  0.0 127.4 jit_solution(14531378492553551360)
XLA Ops:
  0.0 1.3 %dynamic-slice_bitcast_fusion.2 = (bf16[64,1024]{1,0:T(8,128)(2,1)S(1)}, bf16[64,1024]{1,0:T(8,128)(2,1)S(1)}, bf16[64,1024]{1,0:T(8,128)(2,1)S(1)}, bf16[64,1024]{1,0:T(8,128)(2,1)S(1)}) fusion(bf16[1,8192,64]{1,2,0:T(8,128)(2,1)} %param.6, s32[]{:T(128)S(6)} %select_n.30, s32[]{:T(128)S(6)} %select_n.32, s32[]{:T(128)S(6)} %select_n.29, s32[]{:T(128)S(6)} %select_n.31), kind=kLoop, calls=%fused_computation.6 | loop fusion | bytes 1048592 | tf_op jit(solution)/shard_map/dynamic_slice | solution.py:252
  1.8 2.6 %collective-permute-start.6 = (bf16[64,1024]{1,0:T(8,128)(2,1)S(1)}, bf16[64,1024]{1,0:T(8,128)(2,1)S(1)}, u32[]{:S(2)}, u32[]{:S(2)}) collective-permute-start(bf16[64,1024]{1,0:T(8,128)(2,1)S(1)} %get-tuple-element.34), channel_id=1, source_target_pairs={{0,3},{1,2},{2,1},{3,0},{4,7},{5,6},{6,5},{7,4},{8,11},{9,10},{10,... | collective-permute-start | bytes 393224 | tf_op jit(solution)/shard_map/ppermute | solution.py:27
  4.5 2.1 %collective-permute-start.4 = (bf16[128,1024]{1,0:T(8,128)(2,1)S(1)}, bf16[128,1024]{1,0:T(8,128)(2,1)S(1)}, u32[]{:S(2)}, u32[]{:S(2)}) collective-permute-start(bf16[128,1024]{1,0:T(8,128)(2,1)S(1)} %pad_maximum_fusion.refs_0_), channel_id=1, source_target_pairs={{0,4},{4,8},{8,12},{12,0},{1,5},{5,9},{9,13},{13,1},{2,6},{6,10},{... | collective-permute-start | bytes 786440 | tf_op jit(solution)/shard_map/ppermute | solution.py:31
  6.6 1.7 %collective-permute-done.6 = bf16[64,1024]{1,0:T(8,128)(2,1)S(1)} collective-permute-done((bf16[64,1024]{1,0:T(8,128)(2,1)S(1)}, bf16[64,1024]{1,0:T(8,128)(2,1)S(1)}, u32[]{:S(2)}, u32[]{:S(2)}) %collective-permute-start.6) | collective-permute-done | bytes 131104 | tf_op jit(solution)/shard_map/ppermute | solution.py:27
  8.3 3.0 %collective-permute-done.5 = bf16[64,1024]{1,0:T(8,128)(2,1)S(1)} collective-permute-done((bf16[64,1024]{1,0:T(8,128)(2,1)S(1)}, bf16[64,1024]{1,0:T(8,128)(2,1)S(1)}, u32[]{:S(2)}, u32[]{:S(2)}) %collective-permute-start.5) | collective-permute-done | bytes 131104 | tf_op jit(solution)/shard_map/ppermute | solution.py:27
  11.3 1.8 %collective-permute-start.7 = (bf16[128,1024]{1,0:T(8,128)(2,1)S(1)}, bf16[128,1024]{1,0:T(8,128)(2,1)S(1)}, u32[]{:S(2)}, u32[]{:S(2)}) collective-permute-start(bf16[128,1024]{1,0:T(8,128)(2,1)S(1)} %pad_maximum_fusion.1.refs_1_), channel_id=1, source_target_pairs={{0,4},{4,8},{8,12},{12,0},{1,5},{5,9},{9,13},{13,1},{2,6},{6,10},{... | collective-permute-start | bytes 786440 | tf_op jit(solution)/shard_map/ppermute | solution.py:31
  13.1 1.8 %dynamic-slice_bitcast_fusion = (bf16[64,1024]{1,0:T(8,128)(2,1)}, bf16[64,1024]{1,0:T(8,128)(2,1)S(1)}, bf16[64,1024]{1,0:T(8,128)(2,1)S(1)}, bf16[64,1024]{1,0:T(8,128)(2,1)S(1)}) fusion(bf16[1,64,8192]{2,1,0:T(8,128)(2,1)} %param.7, s32[]{:T(128)S(6)} %select_n.32, s32[]{:T(128)S(6)} %select_n.30, s32[]{:T(128)S(6)} %select_n.29, s32[]{:T(128)S(6)} %select_n.31), kind=kLoop, calls=%fused_computation.4 | loop fusion | bytes 1048592 | tf_op jit(solution)/shard_map/dynamic_slice | solution.py:252
  14.9 1.5 %collective-permute-start.2 = (bf16[64,1024]{1,0:T(8,128)(2,1)S(1)}, bf16[64,1024]{1,0:T(8,128)(2,1)S(1)}, u32[]{:S(2)}, u32[]{:S(2)}) collective-permute-start(bf16[64,1024]{1,0:T(8,128)(2,1)S(1)} %get-tuple-element.17), channel_id=1, source_target_pairs={{0,2},{1,3},{2,0},{3,1},{4,6},{5,7},{6,4},{7,5},{8,10},{9,11},{10,... | collective-permute-start | bytes 393224 | tf_op jit(solution)/shard_map/ppermute | solution.py:27
  16.8 1.5 %outgoing_rows.1 = bf16[8,136,1024]{2,1,0:T(8,128)(2,1)} custom-call(bf16[128,8192]{1,0:T(8,128)(2,1)S(1)} %copy-done, bf16[8,1024]{1,0:T(8,128)(2,1)S(1)} %broadcast_in_dim.10.ids_ref), custom_call_target="tpu_custom_call" | custom-call | tf_op jit(solution)/shard_map/outgoing_rows/pallas_call | solution.py:63
  18.4 2.8 %collective-permute-done.2 = bf16[64,1024]{1,0:T(8,128)(2,1)S(1)} collective-permute-done((bf16[64,1024]{1,0:T(8,128)(2,1)S(1)}, bf16[64,1024]{1,0:T(8,128)(2,1)S(1)}, u32[]{:S(2)}, u32[]{:S(2)}) %collective-permute-start.2) | collective-permute-done | bytes 131104 | tf_op jit(solution)/shard_map/ppermute | solution.py:27
  21.2 2.0 %collective-permute-done.3 = bf16[64,1024]{1,0:T(8,128)(2,1)S(1)} collective-permute-done((bf16[64,1024]{1,0:T(8,128)(2,1)S(1)}, bf16[64,1024]{1,0:T(8,128)(2,1)S(1)}, u32[]{:S(2)}, u32[]{:S(2)}) %collective-permute-start.3) | collective-permute-done | bytes 131104 | tf_op jit(solution)/shard_map/ppermute | solution.py:27
  23.9 3.7 %all-to-all-start = ((bf16[8,136,1024]{2,1,0:T(8,128)(2,1)}), bf16[8,136,1024]{2,1,0:T(8,128)(2,1)S(1)}, u32[]{:S(2)}, u32[]{:S(2)}) async-start(bf16[8,136,1024]{2,1,0:T(8,128)(2,1)} %outgoing_rows.1), calls=%async_computation | async-start | bytes 4456448 | tf_op jit(solution)/shard_map/all_to_all | solution.py:39
  27.7 1.6 %collective-permute-start.9 = (bf16[128,1024]{1,0:T(8,128)(2,1)S(1)}, bf16[128,1024]{1,0:T(8,128)(2,1)S(1)}, u32[]{:S(2)}, u32[]{:S(2)}) collective-permute-start(bf16[128,1024]{1,0:T(8,128)(2,1)S(1)} %collective-permute-done.7.refs_3_), channel_id=1, source_target_pairs={{0,4},{4,8},{8,12},{12,0},{1,5},{5,9},{9,13},{13,1},{2,6},{6,10},{... | collective-permute-start | bytes 786440 | tf_op jit(solution)/shard_map/ppermute | solution.py:31
  29.3 1.6 %collective-permute-start.8 = (bf16[128,1024]{1,0:T(8,128)(2,1)S(1)}, bf16[128,1024]{1,0:T(8,128)(2,1)}, u32[]{:S(2)}, u32[]{:S(2)}) collective-permute-start(bf16[128,1024]{1,0:T(8,128)(2,1)S(1)} %collective-permute-done.4.refs_2_), channel_id=1, source_target_pairs={{0,4},{4,8},{8,12},{12,0},{1,5},{5,9},{9,13},{13,1},{2,6},{6,10},{... | collective-permute-start | bytes 786440 | tf_op jit(solution)/shard_map/ppermute | solution.py:31
  30.9 7.7 %collective-permute-done.9.refs_5_ = bf16[128,1024]{1,0:T(8,128)(2,1)S(1)} collective-permute-done((bf16[128,1024]{1,0:T(8,128)(2,1)S(1)}, bf16[128,1024]{1,0:T(8,128)(2,1)S(1)}, u32[]{:S(2)}, u32[]{:S(2)}) %collective-permute-start.9) | collective-permute-done | bytes 262176 | tf_op jit(solution)/shard_map/ppermute | solution.py:31
  38.6 5.7 %collective-permute-done.8.refs_4_ = bf16[128,1024]{1,0:T(8,128)(2,1)} collective-permute-done((bf16[128,1024]{1,0:T(8,128)(2,1)S(1)}, bf16[128,1024]{1,0:T(8,128)(2,1)}, u32[]{:S(2)}, u32[]{:S(2)}) %collective-permute-start.8) | collective-permute-done | bytes 262176 | tf_op jit(solution)/shard_map/ppermute | solution.py:31
  45.3 4.6 %collective-permute-done.11.refs_7_ = bf16[128,1024]{1,0:T(8,128)(2,1)} collective-permute-done((bf16[128,1024]{1,0:T(8,128)(2,1)S(1)}, bf16[128,1024]{1,0:T(8,128)(2,1)}, u32[]{:S(2)}, u32[]{:S(2)}) %collective-permute-start.11) | collective-permute-done | bytes 262176 | tf_op jit(solution)/shard_map/ppermute | solution.py:31
  51.0 4.6 %collective-permute-done.10.refs_6_ = bf16[128,1024]{1,0:T(8,128)(2,1)S(1)} collective-permute-done((bf16[128,1024]{1,0:T(8,128)(2,1)}, bf16[128,1024]{1,0:T(8,128)(2,1)S(1)}, u32[]{:S(2)}, u32[]{:S(2)}) %collective-permute-start.10) | collective-permute-done | bytes 262176 | tf_op jit(solution)/shard_map/ppermute | solution.py:31
  56.5 4.9 %collective-permute-done.13.refs_3_ = bf16[128,1024]{1,0:T(8,128)(2,1)} collective-permute-done((bf16[128,1024]{1,0:T(8,128)(2,1)S(1)}, bf16[128,1024]{1,0:T(8,128)(2,1)}, u32[]{:S(2)}, u32[]{:S(2)}) %collective-permute-start.13) | collective-permute-done | bytes 262176 | tf_op jit(solution)/shard_map/ppermute | solution.py:31
  64.2 4.5 %down_product.1 = (f32[8,64,128]{2,1,0:T(8,128)}, f32[8,128,128]{2,1,0:T(8,128)S(1)}) custom-call(s32[16]{0:T(128)S(1)} %add.62.labels_ref, bf16[8,136,1024]{2,1,0:T(8,128)(2,1)S(1)} %all-to-all-done.rows_ref, bf16[128,1024]{1,0:T(8,128)(2,1)S(1)} %pad_maximum_fusion.refs_0_, bf16[128,1024]{1,0:T(8,128)(2,1)S(1)} %pad_maximum_fusion.1.refs_1_, ...), custom_call_target="tpu_custom_call" | custom-call | flops 2147483648 | bytes 4194304 | tf_op jit(solution)/shard_map/down_product/pallas_call | solution.py:117
  69.4 1.2 collective-permute-start.14
  70.7 4.2 %all-to-all-start.1 = ((f32[8,64,128]{2,1,0:T(8,128)}), f32[8,64,128]{2,1,0:T(8,128)S(1)}, u32[]{:S(2)}, u32[]{:S(2)}) async-start(f32[8,64,128]{2,1,0:T(8,128)} %get-tuple-element.22), calls=%async_computation.1 | async-start | bytes 524288 | tf_op jit(solution)/shard_map/all_to_all | solution.py:39
  75.1 3.5 %collective-permute-done.14.refs_4_ = bf16[128,1024]{1,0:T(8,128)(2,1)S(1)} collective-permute-done((bf16[128,1024]{1,0:T(8,128)(2,1)}, bf16[128,1024]{1,0:T(8,128)(2,1)S(1)}, u32[]{:S(2)}, u32[]{:S(2)}) %collective-permute-start.14) | collective-permute-done | bytes 262176 | tf_op jit(solution)/shard_map/ppermute | solution.py:31
  78.7 2.3 %all-to-all-done.1.terms_ref = f32[8,64,128]{2,1,0:T(8,128)S(1)} async-done(((f32[8,64,128]{2,1,0:T(8,128)}), f32[8,64,128]{2,1,0:T(8,128)S(1)}, u32[]{:S(2)}, u32[]{:S(2)}) %all-to-all-start.1) | async-done | bytes 262176 | tf_op jit(solution)/shard_map/all_to_all | solution.py:39
  81.6 3.4 %all-to-all-start.2 = ((bf16[8,64,128]{2,1,0:T(8,128)(2,1)}), bf16[8,64,128]{2,1,0:T(8,128)(2,1)S(1)}, u32[]{:S(2)}, u32[]{:S(2)}) async-start(bf16[8,64,128]{2,1,0:T(8,128)(2,1)} %summed_copies.1), calls=%async_computation.2 | async-start | bytes 262144 | tf_op jit(solution)/shard_map/all_to_all | solution.py:39
  85.0 1.1 collective-permute-done.17.refs_7_
  86.0 4.0 %all-to-all-done.2.shrunk_ref = bf16[8,64,128]{2,1,0:T(8,128)(2,1)S(1)} async-done(((bf16[8,64,128]{2,1,0:T(8,128)(2,1)}), bf16[8,64,128]{2,1,0:T(8,128)(2,1)S(1)}, u32[]{:S(2)}, u32[]{:S(2)}) %all-to-all-start.2) | async-done | bytes 131104 | tf_op jit(solution)/shard_map/all_to_all | solution.py:39
  90.1 1.1 collective-permute-done.16.refs_6_
  91.2 1.0 copy-done.8
  92.3 4.1 %up_product.1 = bf16[8,128,1024]{2,1,0:T(8,128)(2,1)S(1)} custom-call(s32[16]{0:T(128)S(1)} %add.62.labels_ref, f32[8,128,128]{2,1,0:T(8,128)S(1)} %copy-done.8, bf16[8,64,128]{2,1,0:T(8,128)(2,1)S(1)} %all-to-all-done.2.shrunk_ref, bf16[128,1024]{1,0:T(8,128)(2,1)S(1)} %pad_maximum_fusion.2.refs_0_, bf16[128,1024]{1,0:T(8,128)(2,1)S(1)} %pad_maximum_fusion.3.refs_1_, ...), custom_call_target="tpu_custom_call" | custom-call | flops 2147483648 | bytes 4194304 | tf_op jit(solution)/shard_map/up_product/pallas_call | solution.py:194
  96.4 29.6 %all_to_all.20.refs_0_ = bf16[8,128,1024]{2,1,0:T(8,128)(2,1)S(1)} all-to-all(bf16[8,128,1024]{2,1,0:T(8,128)(2,1)S(1)} %up_product.1), channel_id=1, replica_groups=mesh['groups'=2,'outer'=4,'inner'=4] {'groups','inner'}, dimensions={0} | all-to-all | bytes 4194304 | tf_op jit(solution)/shard_map/all_to_all | solution.py:39
  126.1 1.4 %place_results.1 = bf16[128,8192]{1,0:T(8,128)(2,1)} custom-call(bf16[8,128,1024]{2,1,0:T(8,128)(2,1)S(1)} %all_to_all.20.refs_0_), custom_call_target="tpu_custom_call" | custom-call | tf_op jit(solution)/shard_map/place_results/pallas_call | solution.py:230
  (54 shorter events, 9.1 us)
Async XLA Ops:
  0.0 16.8 %copy-start.12 = (s32[128,1]{0,1:T(1,128)S(1)}, s32[128,1]{0,1:T(1,128)}, u32[]{:S(2)}) copy-start(s32[128,1]{0,1:T(1,128)} %param.4) | copy-start | bytes 1540
  0.0 16.8 %copy-start = (bf16[128,8192]{1,0:T(8,128)(2,1)S(1)}, bf16[128,8192]{1,0:T(8,128)(2,1)}, u32[]{:S(2)}) copy-start(bf16[128,8192]{1,0:T(8,128)(2,1)} %hidden_ref.1) | copy-start | bytes 6291460
  1.3 3.2 %collective-permute-start = (bf16[64,1024]{1,0:T(8,128)(2,1)S(1)}, bf16[64,1024]{1,0:T(8,128)(2,1)S(1)}, u32[]{:S(2)}, u32[]{:S(2)}) collective-permute-start(bf16[64,1024]{1,0:T(8,128)(2,1)S(1)} %get-tuple-element.33), channel_id=1, source_target_pairs={{0,1},{1,0},{2,3},{3,2},{4,5},{5,4},{6,7},{7,6},{8,9},{9,8},{10,11... | collective-permute-start | bytes 393224 | tf_op jit(solution)/shard_map/ppermute | solution.py:27
  1.8 6.5 %collective-permute-start.6 = (bf16[64,1024]{1,0:T(8,128)(2,1)S(1)}, bf16[64,1024]{1,0:T(8,128)(2,1)S(1)}, u32[]{:S(2)}, u32[]{:S(2)}) collective-permute-start(bf16[64,1024]{1,0:T(8,128)(2,1)S(1)} %get-tuple-element.34), channel_id=1, source_target_pairs={{0,3},{1,2},{2,1},{3,0},{4,7},{5,6},{6,5},{7,4},{8,11},{9,10},{10,... | collective-permute-start | bytes 393224 | tf_op jit(solution)/shard_map/ppermute | solution.py:27
  4.4 6.8 %collective-permute-start.5 = (bf16[64,1024]{1,0:T(8,128)(2,1)S(1)}, bf16[64,1024]{1,0:T(8,128)(2,1)S(1)}, u32[]{:S(2)}, u32[]{:S(2)}) collective-permute-start(bf16[64,1024]{1,0:T(8,128)(2,1)S(1)} %get-tuple-element.31), channel_id=1, source_target_pairs={{0,2},{1,3},{2,0},{3,1},{4,6},{5,7},{6,4},{7,5},{8,10},{9,11},{10,... | collective-permute-start | bytes 393224 | tf_op jit(solution)/shard_map/ppermute | solution.py:27
  4.5 18.7 %collective-permute-start.4 = (bf16[128,1024]{1,0:T(8,128)(2,1)S(1)}, bf16[128,1024]{1,0:T(8,128)(2,1)S(1)}, u32[]{:S(2)}, u32[]{:S(2)}) collective-permute-start(bf16[128,1024]{1,0:T(8,128)(2,1)S(1)} %pad_maximum_fusion.refs_0_), channel_id=1, source_target_pairs={{0,4},{4,8},{8,12},{12,0},{1,5},{5,9},{9,13},{13,1},{2,6},{6,10},{... | collective-permute-start | bytes 786440 | tf_op jit(solution)/shard_map/ppermute | solution.py:31
  11.3 12.6 %collective-permute-start.7 = (bf16[128,1024]{1,0:T(8,128)(2,1)S(1)}, bf16[128,1024]{1,0:T(8,128)(2,1)S(1)}, u32[]{:S(2)}, u32[]{:S(2)}) collective-permute-start(bf16[128,1024]{1,0:T(8,128)(2,1)S(1)} %pad_maximum_fusion.1.refs_1_), channel_id=1, source_target_pairs={{0,4},{4,8},{8,12},{12,0},{1,5},{5,9},{9,13},{13,1},{2,6},{6,10},{... | collective-permute-start | bytes 786440 | tf_op jit(solution)/shard_map/ppermute | solution.py:31
  14.9 3.5 %collective-permute-start.1 = (bf16[64,1024]{1,0:T(8,128)(2,1)S(1)}, bf16[64,1024]{1,0:T(8,128)(2,1)S(1)}, u32[]{:S(2)}, u32[]{:S(2)}) collective-permute-start(bf16[64,1024]{1,0:T(8,128)(2,1)S(1)} %get-tuple-element.16), channel_id=1, source_target_pairs={{0,1},{1,0},{2,3},{3,2},{4,5},{5,4},{6,7},{7,6},{8,9},{9,8},{10,11... | collective-permute-start | bytes 393224 | tf_op jit(solution)/shard_map/ppermute | solution.py:27
  14.9 6.3 %collective-permute-start.2 = (bf16[64,1024]{1,0:T(8,128)(2,1)S(1)}, bf16[64,1024]{1,0:T(8,128)(2,1)S(1)}, u32[]{:S(2)}, u32[]{:S(2)}) collective-permute-start(bf16[64,1024]{1,0:T(8,128)(2,1)S(1)} %get-tuple-element.17), channel_id=1, source_target_pairs={{0,2},{1,3},{2,0},{3,1},{4,6},{5,7},{6,4},{7,5},{8,10},{9,11},{10,... | collective-permute-start | bytes 393224 | tf_op jit(solution)/shard_map/ppermute | solution.py:27
  16.4 6.8 %collective-permute-start.3 = (bf16[64,1024]{1,0:T(8,128)(2,1)S(1)}, bf16[64,1024]{1,0:T(8,128)(2,1)S(1)}, u32[]{:S(2)}, u32[]{:S(2)}) collective-permute-start(bf16[64,1024]{1,0:T(8,128)(2,1)S(1)} %get-tuple-element.18), channel_id=1, source_target_pairs={{0,3},{1,2},{2,1},{3,0},{4,7},{5,6},{6,5},{7,4},{8,11},{9,10},{10,... | collective-permute-start | bytes 393224 | tf_op jit(solution)/shard_map/ppermute | solution.py:27
  18.4 5.6 %copy-start.9 = (bf16[64,1024]{1,0:T(8,128)(2,1)}, bf16[64,1024]{1,0:T(8,128)(2,1)S(1)}, u32[]{:S(2)}) copy-start(bf16[64,1024]{1,0:T(8,128)(2,1)S(1)} %collective-permute-done.1) | copy-start | bytes 393220
  21.2 2.7 %copy-start.10 = (bf16[64,1024]{1,0:T(8,128)(2,1)}, bf16[64,1024]{1,0:T(8,128)(2,1)S(1)}, u32[]{:S(2)}) copy-start(bf16[64,1024]{1,0:T(8,128)(2,1)S(1)} %collective-permute-done.2) | copy-start | bytes 393220
  23.9 3.7 %copy-start.1 = (bf16[128,1024]{1,0:T(8,128)(2,1)}, bf16[128,1024]{1,0:T(8,128)(2,1)S(1)}, u32[]{:S(2)}) copy-start(bf16[128,1024]{1,0:T(8,128)(2,1)S(1)} %collective-permute-done.7.refs_3_) | copy-start | bytes 786436
  23.9 37.4 %all-to-all-start = ((bf16[8,136,1024]{2,1,0:T(8,128)(2,1)}), bf16[8,136,1024]{2,1,0:T(8,128)(2,1)S(1)}, u32[]{:S(2)}, u32[]{:S(2)}) async-start(bf16[8,136,1024]{2,1,0:T(8,128)(2,1)} %outgoing_rows.1), calls=%async_computation | async-start | bytes 4456448 | tf_op jit(solution)/shard_map/all_to_all | solution.py:39
  27.7 11.0 %collective-permute-start.9 = (bf16[128,1024]{1,0:T(8,128)(2,1)S(1)}, bf16[128,1024]{1,0:T(8,128)(2,1)S(1)}, u32[]{:S(2)}, u32[]{:S(2)}) collective-permute-start(bf16[128,1024]{1,0:T(8,128)(2,1)S(1)} %collective-permute-done.7.refs_3_), channel_id=1, source_target_pairs={{0,4},{4,8},{8,12},{12,0},{1,5},{5,9},{9,13},{13,1},{2,6},{6,10},{... | collective-permute-start | bytes 786440 | tf_op jit(solution)/shard_map/ppermute | solution.py:31
  29.3 15.0 %collective-permute-start.8 = (bf16[128,1024]{1,0:T(8,128)(2,1)S(1)}, bf16[128,1024]{1,0:T(8,128)(2,1)}, u32[]{:S(2)}, u32[]{:S(2)}) collective-permute-start(bf16[128,1024]{1,0:T(8,128)(2,1)S(1)} %collective-permute-done.4.refs_2_), channel_id=1, source_target_pairs={{0,4},{4,8},{8,12},{12,0},{1,5},{5,9},{9,13},{13,1},{2,6},{6,10},{... | collective-permute-start | bytes 786440 | tf_op jit(solution)/shard_map/ppermute | solution.py:31
  38.6 11.3 %copy-start.3 = (bf16[128,1024]{1,0:T(8,128)(2,1)}, bf16[128,1024]{1,0:T(8,128)(2,1)S(1)}, u32[]{:S(2)}) copy-start(bf16[128,1024]{1,0:T(8,128)(2,1)S(1)} %collective-permute-done.9.refs_5_) | copy-start | bytes 786436
  38.6 11.3 %collective-permute-start.11 = (bf16[128,1024]{1,0:T(8,128)(2,1)S(1)}, bf16[128,1024]{1,0:T(8,128)(2,1)}, u32[]{:S(2)}, u32[]{:S(2)}) collective-permute-start(bf16[128,1024]{1,0:T(8,128)(2,1)S(1)} %collective-permute-done.9.refs_5_), channel_id=1, source_target_pairs={{0,4},{4,8},{8,12},{12,0},{1,5},{5,9},{9,13},{13,1},{2,6},{6,10},{... | collective-permute-start | bytes 786440 | tf_op jit(solution)/shard_map/ppermute | solution.py:31
  44.3 11.3 %collective-permute-start.10 = (bf16[128,1024]{1,0:T(8,128)(2,1)}, bf16[128,1024]{1,0:T(8,128)(2,1)S(1)}, u32[]{:S(2)}, u32[]{:S(2)}) collective-permute-start(bf16[128,1024]{1,0:T(8,128)(2,1)} %collective-permute-done.8.refs_4_), channel_id=1, source_target_pairs={{0,4},{4,8},{8,12},{12,0},{1,5},{5,9},{9,13},{13,1},{2,6},{6,10},{... | collective-permute-start | bytes 786440 | tf_op jit(solution)/shard_map/ppermute | solution.py:31
  50.0 11.4 %collective-permute-start.13 = (bf16[128,1024]{1,0:T(8,128)(2,1)S(1)}, bf16[128,1024]{1,0:T(8,128)(2,1)}, u32[]{:S(2)}, u32[]{:S(2)}) collective-permute-start(bf16[128,1024]{1,0:T(8,128)(2,1)S(1)} %pad_maximum_fusion.3.refs_1_), channel_id=1, source_target_pairs={{0,4},{4,8},{8,12},{12,0},{1,5},{5,9},{9,13},{13,1},{2,6},{6,10},{... | collective-permute-start | bytes 786440 | tf_op jit(solution)/shard_map/ppermute | solution.py:31
  56.3 13.1 %collective-permute-start.12 = (bf16[128,1024]{1,0:T(8,128)(2,1)S(1)}, bf16[128,1024]{1,0:T(8,128)(2,1)}, u32[]{:S(2)}, u32[]{:S(2)}) collective-permute-start(bf16[128,1024]{1,0:T(8,128)(2,1)S(1)} %pad_maximum_fusion.2.refs_0_), channel_id=1, source_target_pairs={{0,4},{4,8},{8,12},{12,0},{1,5},{5,9},{9,13},{13,1},{2,6},{6,10},{... | collective-permute-start | bytes 786440 | tf_op jit(solution)/shard_map/ppermute | solution.py:31
  61.3 13.6 %collective-permute-start.15 = (bf16[128,1024]{1,0:T(8,128)(2,1)}, bf16[128,1024]{1,0:T(8,128)(2,1)}, u32[]{:S(2)}, u32[]{:S(2)}) collective-permute-start(bf16[128,1024]{1,0:T(8,128)(2,1)} %collective-permute-done.13.refs_3_), channel_id=1, source_target_pairs={{0,4},{4,8},{8,12},{12,0},{1,5},{5,9},{9,13},{13,1},{2,6},{6,10},{... | collective-permute-start | bytes 786440 | tf_op jit(solution)/shard_map/ppermute | solution.py:31
  61.3 1.0 copy-start.2
  62.3 0.9 copy-start.4
  63.2 0.9 copy-start.6
  68.6 0.8 copy-start.7
  69.4 9.2 %collective-permute-start.14 = (bf16[128,1024]{1,0:T(8,128)(2,1)}, bf16[128,1024]{1,0:T(8,128)(2,1)S(1)}, u32[]{:S(2)}, u32[]{:S(2)}) collective-permute-start(bf16[128,1024]{1,0:T(8,128)(2,1)} %collective-permute-done.12.refs_2_), channel_id=1, source_target_pairs={{0,4},{4,8},{8,12},{12,0},{1,5},{5,9},{9,13},{13,1},{2,6},{6,10},{... | collective-permute-start | bytes 786440 | tf_op jit(solution)/shard_map/ppermute | solution.py:31
  70.7 10.2 %all-to-all-start.1 = ((f32[8,64,128]{2,1,0:T(8,128)}), f32[8,64,128]{2,1,0:T(8,128)S(1)}, u32[]{:S(2)}, u32[]{:S(2)}) async-start(f32[8,64,128]{2,1,0:T(8,128)} %get-tuple-element.22), calls=%async_computation.1 | async-start | bytes 524288 | tf_op jit(solution)/shard_map/all_to_all | solution.py:39
  74.9 11.2 %collective-permute-start.17 = (bf16[128,1024]{1,0:T(8,128)(2,1)}, bf16[128,1024]{1,0:T(8,128)(2,1)S(1)}, u32[]{:S(2)}, u32[]{:S(2)}) collective-permute-start(bf16[128,1024]{1,0:T(8,128)(2,1)} %collective-permute-done.15.refs_5_), channel_id=1, source_target_pairs={{0,4},{4,8},{8,12},{12,0},{1,5},{5,9},{9,13},{13,1},{2,6},{6,10},{... | collective-permute-start | bytes 786440 | tf_op jit(solution)/shard_map/ppermute | solution.py:31
  78.6 12.6 %collective-permute-start.16 = (bf16[128,1024]{1,0:T(8,128)(2,1)S(1)}, bf16[128,1024]{1,0:T(8,128)(2,1)S(1)}, u32[]{:S(2)}, u32[]{:S(2)}) collective-permute-start(bf16[128,1024]{1,0:T(8,128)(2,1)S(1)} %collective-permute-done.14.refs_4_), channel_id=1, source_target_pairs={{0,4},{4,8},{8,12},{12,0},{1,5},{5,9},{9,13},{13,1},{2,6},{6,10},{... | collective-permute-start | bytes 786440 | tf_op jit(solution)/shard_map/ppermute | solution.py:31
  81.6 8.5 %all-to-all-start.2 = ((bf16[8,64,128]{2,1,0:T(8,128)(2,1)}), bf16[8,64,128]{2,1,0:T(8,128)(2,1)S(1)}, u32[]{:S(2)}, u32[]{:S(2)}) async-start(bf16[8,64,128]{2,1,0:T(8,128)(2,1)} %summed_copies.1), calls=%async_computation.2 | async-start | bytes 262144 | tf_op jit(solution)/shard_map/all_to_all | solution.py:39
  91.2 1.0 copy-start.8
  (2 other events, 1.4 us)

commit v9 on v8

--- a/solution.py
+++ b/solution.py
@@ -39,6 +39,16 @@
     return lax.all_to_all(value, PLANE, split_axis=0, concat_axis=0, tiled=True)
 
 
+def load_maps(maps, map_buf, sems):
+    rows = maps[0].shape[0]
+    copies = [
+        pltpu.make_async_copy(m, map_buf.at[pl.ds(n * rows, rows)], sems.at[n]) for n, m in enumerate(maps)
+    ]
+    for copy in copies:
+        copy.start()
+    return copies
+
+
 def tile_labels(labels_ref, tile, rank, shape):
     per_tile = LANES // rank
     lane = lax.broadcasted_iota(jnp.int32, shape, 1)
@@ -71,7 +81,9 @@
 
 
 def down_kernel(map_count, rank, labels_ref, rows_ref, *refs):
-    maps, (packed_ref, ids_out, total_ref, ids_ref, sem) = refs[:map_count], refs[map_count:]
+    maps, (packed_ref, ids_out, total_ref, ids_ref, map_buf, sem, map_sems) = refs[:map_count], refs[map_count:]
+    copies = load_maps(maps, map_buf, map_sems)
+    map_rows = maps[0].shape[0]
     members, rows, share = rows_ref.shape
     tok = rows - ID_ROWS
     block = min(BLOCK, members)
@@ -90,7 +102,13 @@
         ids = ids_ref[here].reshape(block * tok, LANES)
         tile = 0
         for at in range(0, map_count, 2):
-            some = jnp.concatenate([m[...] for m in maps[at : at + 2]], axis=0)
+
+            @pl.when(step == 0)
+            def _():
+                for copy in copies[at : at + 2]:
+                    copy.wait()
+
+            some = map_buf[at * map_rows : (at + 2) * map_rows, :]
             product = lax.dot_general(
                 tokens, some, (((1,), (1,)), ((), ())), preferred_element_type=jnp.float32
             )
@@ -120,14 +138,16 @@
             jax.ShapeDtypeStruct((members, tok // 2, LANES), jnp.float32),
             jax.ShapeDtypeStruct((members, tok, LANES), jnp.float32),
         ],
-        in_specs=[IN_SMEM, IN_VMEM] + [IN_VMEM] * len(maps),
+        in_specs=[IN_SMEM, IN_VMEM] + [IN_HBM] * len(maps),
         out_specs=[IN_VMEM, IN_HBM],
         scratch_shapes=[
             pltpu.VMEM((min(BLOCK, members) * tok, LANES), jnp.float32),
             pltpu.VMEM((members, tok, LANES), jnp.float32),
+            pltpu.VMEM((map_rows, maps[0].shape[1]), jnp.bfloat16),
             pltpu.SemaphoreType.DMA,
+            pltpu.SemaphoreType.DMA((len(maps),)),
         ],
-        compiler_params=params(8 * members * tok * LANES),
+        compiler_params=params(8 * members * tok * LANES + 2 * map_rows * share),
         cost_estimate=pl.CostEstimate(
             flops=2 * map_rows * members * tok * share,
             bytes_accessed=2 * share * (map_rows + members * tok),
@@ -155,7 +175,8 @@
 
 
 def up_kernel(map_count, rank, labels_ref, ids_ref, shrunk_ref, *refs):
-    maps, (out_ref, spread_ref, ids_buf, sem) = refs[:map_count], refs[map_count:]
+    maps, (out_ref, spread_ref, ids_buf, map_buf, sem, map_sems) = refs[:map_count], refs[map_count:]
+    copies = load_maps(maps, map_buf, map_sems)
     kept = pltpu.make_async_copy(ids_ref, ids_buf, sem)
     kept.start()
     members, half, _ = shrunk_ref.shape
@@ -163,7 +184,6 @@
     block = min(BLOCK, members)
     tiles = spread_ref.shape[1] // LANES
     lane = lax.broadcasted_iota(jnp.int32, (half, LANES), 1)
-    held = jnp.concatenate([m[...] for m in maps], axis=0)
     kept.wait()
 
     def one(step, _):
@@ -180,7 +200,13 @@
                 spread_ref[n * tok : (n + 1) * tok, tile * LANES : (tile + 1) * LANES] = jnp.where(
                     named, shrunk, 0.0
                 ).astype(jnp.bfloat16)
-        product = jnp.dot(spread_ref[...], held, preferred_element_type=jnp.float32)
+
+        @pl.when(step == 0)
+        def _():
+            for copy in copies:
+                copy.wait()
+
+        product = jnp.dot(spread_ref[...], map_buf[...], preferred_element_type=jnp.float32)
         product = (adapter_scale * product).astype(jnp.bfloat16)
         out_ref[pl.ds(first, block)] = product.reshape(block, tok, product.shape[1])
         return 0
@@ -194,14 +220,16 @@
     return pl.pallas_call(
         functools.partial(up_kernel, len(maps), rank),
         out_shape=jax.ShapeDtypeStruct((members, tok, piece), jnp.bfloat16),
-        in_specs=[IN_SMEM, IN_HBM, IN_VMEM] + [IN_VMEM] * len(maps),
+        in_specs=[IN_SMEM, IN_HBM, IN_VMEM] + [IN_HBM] * len(maps),
         out_specs=IN_VMEM,
         scratch_shapes=[
             pltpu.VMEM((min(BLOCK, members) * tok, map_rows), jnp.bfloat16),
             pltpu.VMEM((members, tok, LANES), jnp.float32),
+            pltpu.VMEM((map_rows, maps[0].shape[1]), jnp.bfloat16),
             pltpu.SemaphoreType.DMA,
+            pltpu.SemaphoreType.DMA((len(maps),)),
         ],
-        compiler_params=params(2 * min(BLOCK, members) * tok * map_rows + 4 * members * tok * LANES),
+        compiler_params=params(2 * min(BLOCK, members) * tok * map_rows + 4 * members * tok * LANES + 2 * map_rows * piece),
         cost_estimate=pl.CostEstimate(
             flops=2 * map_rows * members * tok * piece,
             bytes_accessed=2 * piece * (map_rows + members * tok),
@@ -247,13 +275,17 @@
     rank = adapter_up_maps.shape[1]
     me = group * inner + place_in_group
 
-    def slices(array):
-        return [
-            lax.dynamic_slice_in_dim(array, (me ^ offset) * share, share, axis=1) for offset in range(inner)
-        ]
-
-    def exchanged(blocks):
-        return blocks[:1] + [to_partner(blocks[n], "inner", inner, n) for n in range(1, inner)]
+    def slices(offset):
+        start = (me ^ offset) * share
+        return jnp.concatenate(
+            [
+                lax.dynamic_slice_in_dim(adapter_down_maps[0].T, start, share, axis=1),
+                lax.dynamic_slice_in_dim(adapter_up_maps[0], start, share, axis=1),
+            ],
+            axis=0,
+        )
+
+    got = [slices(0)] + [to_partner(slices(n), "inner", inner, n) for n in range(1, inner)]
 
     def rings(blocks, near_after=(), far_after=(), second_after=()):
         near = [after(jnp.concatenate(blocks[: inner // 2], axis=0), *near_after)]
@@ -269,15 +301,13 @@
     )
     labels = labels.reshape(-1)
 
-    down = exchanged(slices(adapter_down_maps[0].T))
-    up = exchanged([after(block, down[1]) for block in slices(adapter_up_maps[0])])
-    down_near, down_far = rings(down, second_after=up[1:])
+    down_near, down_far = rings([g[:rank] for g in got])
     ids = token_adapter_index.astype(jnp.bfloat16).reshape(1, tok)
-    rows = swap(after(outgoing_rows(hidden, ids, members), *up[1:], down_near[1], down_far[1]))
+    rows = swap(after(outgoing_rows(hidden, ids, members), *got[1:], down_near[1]))
 
     down_maps = [m for pair in zip(down_near, down_far) for m in pair]
     packed, id_columns = down_product(labels, rows, down_maps, rank)
-    up_near, up_far = rings(up, [down_near[-1]], [down_far[-1]], second_after=[packed])
+    up_near, up_far = rings([g[rank:] for g in got], [down_near[-1]], [down_far[-1]], second_after=[packed])
     up_maps = [m for pair in zip(up_near, up_far) for m in pair]
     shrunk = swap(summed_copies(swap(packed)))
     return place([swap(up_product(labels, id_columns, shrunk, up_maps, rank))])

time: 128 us -> 136 us (1.062)
  waiting for transfers between devices: 49.2 us -> 56.9 us
  starting transfers between devices: 25 us -> 20.6 us
  Pallas kernels: 12.2 us -> 14.6 us
  local copies, waits for them, and re-layouts: 9.24 us -> 11.3 us
    ppermute x12, waiting for transfers between devices: 33.3 us -> 43.9 us  [next_on_ring(): lax.ppermute(block, 'outer', [(i, (i + 1) % outer) for i in range(outer)])]
    pallas_call x1, Pallas kernels: 4.46 us -> 6.87 us  [down_product(): pl.pallas_call(functools.partial(down_kernel, len(maps), rank), out_shape...]
    ppermute x12, starting transfers between devices: 8.63 us -> 6.28 us  [next_on_ring(): lax.ppermute(block, 'outer', [(i, (i + 1) % outer) for i in range(outer)])]
    slice x0 -> x3, local copies, waits for them, and re-layouts: none -> 2.01 us  [per_device(): g[rank:]]
    ppermute x6 -> x3, starting transfers between devices: 5.06 us -> 3.3 us  [to_partner(): return lax.ppermute(value, axes, [(i, i ^ offset) for i in range(size)])]
    ppermute x6 -> x3, waiting for transfers between devices: 9.57 us -> 8.04 us  [to_partner(): return lax.ppermute(value, axes, [(i, i ^ offset) for i in range(size)])]
    unnamed x26 -> x20, local copies, waits for them, and re-layouts: 6.07 us -> 6.09 us
  transfers between devices with their start and end apart: 21 -> 18, of which waited for: 14 -> 13; matrix products, arithmetic and copies ran while one was open for 3% -> 3% of each run, Pallas kernels for 5% -> 7%
where the time goes in v9:
time: 136 us; the launch traced here: 135 us
  waiting for transfers between devices  56.9 us (42%)
  blocking collectives  29.6 us (22%)
  starting transfers between devices  20.6 us (15%)
  Pallas kernels  14.6 us (11%)
  local copies, waits for them, and re-layouts  11.3 us (8%)
  other arithmetic  2.15 us (2%)
    ppermute x12, waiting for transfers between devices, next_on_ring(): lax.ppermute(block, 'outer', [(i, (i + 1) % outer) for i in range(outer)])  43.9 us
    all_to_all x1, blocking collectives, swap(): return lax.all_to_all(value, PLANE, split_axis=0, concat_axis=0, tiled=True)  29.6 us
    all_to_all x3, starting transfers between devices, swap(): return lax.all_to_all(value, PLANE, split_axis=0, concat_axis=0, tiled=True)  11 us
    ppermute x3, waiting for transfers between devices, to_partner(): return lax.ppermute(value, axes, [(i, i ^ offset) for i in range(size)])  8.04 us
    pallas_call x1, Pallas kernels, down_product(): pl.pallas_call(functools.partial(down_kernel, len(maps), rank), out_shape...  6.87 us
    ppermute x12, starting transfers between devices, next_on_ring(): lax.ppermute(block, 'outer', [(i, (i + 1) % outer) for i in range(outer)])  6.28 us
    unnamed x20, local copies, waits for them, and re-layouts  6.09 us
    all_to_all x3, waiting for transfers between devices, swap(): return lax.all_to_all(value, PLANE, split_axis=0, concat_axis=0, tiled=True)  4.99 us
  transfers between devices with their start and end apart: 18, of which 13 were waited for; matrix products, arithmetic and copies ran while one was open for 3% of the time, Pallas kernels for 7%

profile of v9, /device:TPU:0, one launch (start us, length us, event | category | flops | bytes accessed | tf_op | source)
XLA Modules:
  0.0 135.3 jit_solution(4979847636440176368)
XLA Ops:
  0.0 1.8 %dynamic-slice_bitcast_fusion = (bf16[64,1024]{1,0:T(8,128)(2,1)}, bf16[64,1024]{1,0:T(8,128)(2,1)S(1)}, bf16[64,1024]{1,0:T(8,128)(2,1)S(1)}, bf16[64,1024]{1,0:T(8,128)(2,1)S(1)}) fusion(bf16[1,64,8192]{2,1,0:T(8,128)(2,1)} %param.7, s32[]{:T(128)S(6)} %select_n.32, s32[]{:T(128)S(6)} %select_n.30, s32[]{:T(128)S(6)} %select_n.29, s32[]{:T(128)S(6)} %select_n.31), kind=kLoop, calls=%fused_computation.7 | loop fusion | bytes 1048592 | tf_op jit(solution)/shard_map/dynamic_slice | solution.py:283
  1.8 1.3 dynamic-slice_bitcast_fusion.1
  3.6 2.6 %collective-permute-start.1 = (bf16[128,1024]{1,0:T(8,128)(2,1)S(1)}, bf16[128,1024]{1,0:T(8,128)(2,1)S(1)}, u32[]{:S(2)}, u32[]{:S(2)}) collective-permute-start(bf16[128,1024]{1,0:T(8,128)(2,1)S(1)} %pad_maximum_fusion.1), channel_id=1, source_target_pairs={{0,2},{1,3},{2,0},{3,1},{4,6},{5,7},{6,4},{7,5},{8,10},{9,11},{10,... | collective-permute-start | bytes 786440 | tf_op jit(solution)/shard_map/ppermute | solution.py:27
  7.2 1.8 %collective-permute-start.3 = (bf16[128,1024]{1,0:T(8,128)(2,1)S(1)}, bf16[128,1024]{1,0:T(8,128)(2,1)S(1)}, u32[]{:S(2)}, u32[]{:S(2)}) collective-permute-start(bf16[128,1024]{1,0:T(8,128)(2,1)S(1)} %pad_maximum_fusion.3.refs_0_), channel_id=1, source_target_pairs={{0,4},{4,8},{8,12},{12,0},{1,5},{5,9},{9,13},{13,1},{2,6},{6,10},{... | collective-permute-start | bytes 786440 | tf_op jit(solution)/shard_map/ppermute | solution.py:31
  9.0 1.5 %outgoing_rows.1 = bf16[8,136,1024]{2,1,0:T(8,128)(2,1)} custom-call(bf16[128,8192]{1,0:T(8,128)(2,1)S(1)} %copy-done, bf16[8,1024]{1,0:T(8,128)(2,1)S(1)} %broadcast_in_dim.10.ids_ref), custom_call_target="tpu_custom_call" | custom-call | tf_op jit(solution)/shard_map/outgoing_rows/pallas_call | solution.py:73
  10.6 2.8 %collective-permute-done.1 = bf16[128,1024]{1,0:T(8,128)(2,1)S(1)} collective-permute-done((bf16[128,1024]{1,0:T(8,128)(2,1)S(1)}, bf16[128,1024]{1,0:T(8,128)(2,1)S(1)}, u32[]{:S(2)}, u32[]{:S(2)}) %collective-permute-start.1) | collective-permute-done | bytes 262176 | tf_op jit(solution)/shard_map/ppermute | solution.py:27
  13.4 5.2 %collective-permute-done.2 = bf16[128,1024]{1,0:T(8,128)(2,1)S(1)} collective-permute-done((bf16[128,1024]{1,0:T(8,128)(2,1)S(1)}, bf16[128,1024]{1,0:T(8,128)(2,1)S(1)}, u32[]{:S(2)}, u32[]{:S(2)}) %collective-permute-start.2) | collective-permute-done | bytes 262176 | tf_op jit(solution)/shard_map/ppermute | solution.py:27
  18.6 3.7 %all-to-all-start = ((bf16[8,136,1024]{2,1,0:T(8,128)(2,1)}), bf16[8,136,1024]{2,1,0:T(8,128)(2,1)S(1)}, u32[]{:S(2)}, u32[]{:S(2)}) async-start(bf16[8,136,1024]{2,1,0:T(8,128)(2,1)} %outgoing_rows.1), calls=%async_computation | async-start | bytes 4456448 | tf_op jit(solution)/shard_map/all_to_all | solution.py:39
  23.7 1.6 %collective-permute-start.4 = (bf16[128,1024]{1,0:T(8,128)(2,1)S(1)}, bf16[128,1024]{1,0:T(8,128)(2,1)S(1)}, u32[]{:S(2)}, u32[]{:S(2)}) collective-permute-start(bf16[128,1024]{1,0:T(8,128)(2,1)S(1)} %pad_maximum_fusion.4.refs_1_), channel_id=1, source_target_pairs={{0,4},{4,8},{8,12},{12,0},{1,5},{5,9},{9,13},{13,1},{2,6},{6,10},{... | collective-permute-start | bytes 786440 | tf_op jit(solution)/shard_map/ppermute | solution.py:31
  25.4 9.0 %collective-permute-done.4.refs_3_ = bf16[128,1024]{1,0:T(8,128)(2,1)S(1)} collective-permute-done((bf16[128,1024]{1,0:T(8,128)(2,1)S(1)}, bf16[128,1024]{1,0:T(8,128)(2,1)S(1)}, u32[]{:S(2)}, u32[]{:S(2)}) %collective-permute-start.4) | collective-permute-done | bytes 262176 | tf_op jit(solution)/shard_map/ppermute | solution.py:31
  35.1 1.3 collective-permute-start.5
  36.3 9.0 %collective-permute-done.6.refs_5_ = bf16[128,1024]{1,0:T(8,128)(2,1)S(1)} collective-permute-done((bf16[128,1024]{1,0:T(8,128)(2,1)S(1)}, bf16[128,1024]{1,0:T(8,128)(2,1)S(1)}, u32[]{:S(2)}, u32[]{:S(2)}) %collective-permute-start.6) | collective-permute-done | bytes 262176 | tf_op jit(solution)/shard_map/ppermute | solution.py:31
  45.4 5.7 %collective-permute-done.5.refs_4_ = bf16[128,1024]{1,0:T(8,128)(2,1)} collective-permute-done((bf16[128,1024]{1,0:T(8,128)(2,1)S(1)}, bf16[128,1024]{1,0:T(8,128)(2,1)}, u32[]{:S(2)}, u32[]{:S(2)}) %collective-permute-start.5) | collective-permute-done | bytes 262176 | tf_op jit(solution)/shard_map/ppermute | solution.py:31
  51.1 1.0 pad_maximum_fusion.6.refs_1_
  52.1 4.6 %collective-permute-done.8.refs_7_ = bf16[128,1024]{1,0:T(8,128)(2,1)} collective-permute-done((bf16[128,1024]{1,0:T(8,128)(2,1)S(1)}, bf16[128,1024]{1,0:T(8,128)(2,1)}, u32[]{:S(2)}, u32[]{:S(2)}) %collective-permute-start.8) | collective-permute-done | bytes 262176 | tf_op jit(solution)/shard_map/ppermute | solution.py:31
  56.7 1.0 pad_maximum_fusion.5.refs_0_
  57.7 4.6 %collective-permute-done.7.refs_6_ = bf16[128,1024]{1,0:T(8,128)(2,1)S(1)} collective-permute-done((bf16[128,1024]{1,0:T(8,128)(2,1)}, bf16[128,1024]{1,0:T(8,128)(2,1)S(1)}, u32[]{:S(2)}, u32[]{:S(2)}) %collective-permute-start.7) | collective-permute-done | bytes 262176 | tf_op jit(solution)/shard_map/ppermute | solution.py:31
  63.2 4.9 %collective-permute-done.10.refs_3_ = bf16[128,1024]{1,0:T(8,128)(2,1)} collective-permute-done((bf16[128,1024]{1,0:T(8,128)(2,1)S(1)}, bf16[128,1024]{1,0:T(8,128)(2,1)}, u32[]{:S(2)}, u32[]{:S(2)}) %collective-permute-start.10) | collective-permute-done | bytes 262176 | tf_op jit(solution)/shard_map/ppermute | solution.py:31
  69.0 0.9 copy-done.4
  70.9 6.9 %down_product.1 = (f32[8,64,128]{2,1,0:T(8,128)}, f32[8,128,128]{2,1,0:T(8,128)S(1)}) custom-call(s32[16]{0:T(128)S(1)} %add.62.labels_ref, bf16[8,136,1024]{2,1,0:T(8,128)(2,1)S(1)} %all-to-all-done.rows_ref, bf16[128,1024]{1,0:T(8,128)(2,1)S(1)} %pad_maximum_fusion.3.refs_0_, bf16[128,1024]{1,0:T(8,128)(2,1)S(1)} %pad_maximum_fusion.4.refs_1_, ...), custom_call_target="tpu_custom_call" | custom-call | flops 2147483648 | bytes 4194304 | tf_op jit(solution)/shard_map/down_product/pallas_call | solution.py:135
  78.6 3.9 %all-to-all-start.1 = ((f32[8,64,128]{2,1,0:T(8,128)}), f32[8,64,128]{2,1,0:T(8,128)S(1)}, u32[]{:S(2)}, u32[]{:S(2)}) async-start(f32[8,64,128]{2,1,0:T(8,128)} %get-tuple-element.13), calls=%async_computation.1 | async-start | bytes 524288 | tf_op jit(solution)/shard_map/all_to_all | solution.py:39
  82.5 1.0 collective-permute-start.14
  83.5 3.5 %collective-permute-done.11.refs_4_ = bf16[128,1024]{1,0:T(8,128)(2,1)S(1)} collective-permute-done((bf16[128,1024]{1,0:T(8,128)(2,1)}, bf16[128,1024]{1,0:T(8,128)(2,1)S(1)}, u32[]{:S(2)}, u32[]{:S(2)}) %collective-permute-start.11) | collective-permute-done | bytes 262176 | tf_op jit(solution)/shard_map/ppermute | solution.py:31
  87.5 1.0 all-to-all-done.1.terms_ref
  89.2 3.4 %all-to-all-start.2 = ((bf16[8,64,128]{2,1,0:T(8,128)(2,1)}), bf16[8,64,128]{2,1,0:T(8,128)(2,1)S(1)}, u32[]{:S(2)}, u32[]{:S(2)}) async-start(bf16[8,64,128]{2,1,0:T(8,128)(2,1)} %summed_copies.1), calls=%async_computation.2 | async-start | bytes 262144 | tf_op jit(solution)/shard_map/all_to_all | solution.py:39
  92.6 1.2 collective-permute-done.14.refs_7_
  93.7 3.9 %all-to-all-done.2.shrunk_ref = bf16[8,64,128]{2,1,0:T(8,128)(2,1)S(1)} async-done(((bf16[8,64,128]{2,1,0:T(8,128)(2,1)}), bf16[8,64,128]{2,1,0:T(8,128)(2,1)S(1)}, u32[]{:S(2)}, u32[]{:S(2)}) %all-to-all-start.2) | async-done | bytes 131104 | tf_op jit(solution)/shard_map/all_to_all | solution.py:39
  97.7 1.4 %collective-permute-done.13.refs_6_ = bf16[128,1024]{1,0:T(8,128)(2,1)S(1)} collective-permute-done((bf16[128,1024]{1,0:T(8,128)(2,1)S(1)}, bf16[128,1024]{1,0:T(8,128)(2,1)S(1)}, u32[]{:S(2)}, u32[]{:S(2)}) %collective-permute-start.13) | collective-permute-done | bytes 262176 | tf_op jit(solution)/shard_map/ppermute | solution.py:31
  99.1 1.0 copy-done.8
  100.1 4.1 %up_product.1 = bf16[8,128,1024]{2,1,0:T(8,128)(2,1)S(1)} custom-call(s32[16]{0:T(128)S(1)} %add.62.labels_ref, f32[8,128,128]{2,1,0:T(8,128)S(1)} %copy-done.8, bf16[8,64,128]{2,1,0:T(8,128)(2,1)S(1)} %all-to-all-done.2.shrunk_ref, bf16[128,1024]{1,0:T(8,128)(2,1)S(1)} %pad_maximum_fusion.5.refs_0_, bf16[128,1024]{1,0:T(8,128)(2,1)S(1)} %pad_maximum_fusion.6.refs_1_, ...), custom_call_target="tpu_custom_call" | custom-call | flops 2147483648 | bytes 4194304 | tf_op jit(solution)/shard_map/up_product/pallas_call | solution.py:220
  104.3 29.6 %all_to_all.20.refs_0_ = bf16[8,128,1024]{2,1,0:T(8,128)(2,1)S(1)} all-to-all(bf16[8,128,1024]{2,1,0:T(8,128)(2,1)S(1)} %up_product.1), channel_id=1, replica_groups=mesh['groups'=2,'outer'=4,'inner'=4] {'groups','inner'}, dimensions={0} | all-to-all | bytes 4194304 | tf_op jit(solution)/shard_map/all_to_all | solution.py:39
  133.9 1.4 %place_results.1 = bf16[128,8192]{1,0:T(8,128)(2,1)} custom-call(bf16[8,128,1024]{2,1,0:T(8,128)(2,1)S(1)} %all_to_all.20.refs_0_), custom_call_target="tpu_custom_call" | custom-call | tf_op jit(solution)/shard_map/place_results/pallas_call | solution.py:258
  (48 shorter events, 8.3 us)
Async XLA Ops:
  1.8 7.2 %copy-start.9 = (s32[128,1]{0,1:T(1,128)S(1)}, s32[128,1]{0,1:T(1,128)}, u32[]{:S(2)}) copy-start(s32[128,1]{0,1:T(1,128)} %param.4) | copy-start | bytes 1540
  1.8 7.2 %copy-start = (bf16[128,8192]{1,0:T(8,128)(2,1)S(1)}, bf16[128,8192]{1,0:T(8,128)(2,1)}, u32[]{:S(2)}) copy-start(bf16[128,8192]{1,0:T(8,128)(2,1)} %hidden_ref.1) | copy-start | bytes 6291460
  3.1 3.3 %collective-permute-start = (bf16[128,1024]{1,0:T(8,128)(2,1)S(1)}, bf16[128,1024]{1,0:T(8,128)(2,1)S(1)}, u32[]{:S(2)}, u32[]{:S(2)}) collective-permute-start(bf16[128,1024]{1,0:T(8,128)(2,1)S(1)} %pad_maximum_fusion), channel_id=1, source_target_pairs={{0,1},{1,0},{2,3},{3,2},{4,5},{5,4},{6,7},{7,6},{8,9},{9,8},{10,11... | collective-permute-start | bytes 786440 | tf_op jit(solution)/shard_map/ppermute | solution.py:27
  3.6 9.8 %collective-permute-start.1 = (bf16[128,1024]{1,0:T(8,128)(2,1)S(1)}, bf16[128,1024]{1,0:T(8,128)(2,1)S(1)}, u32[]{:S(2)}, u32[]{:S(2)}) collective-permute-start(bf16[128,1024]{1,0:T(8,128)(2,1)S(1)} %pad_maximum_fusion.1), channel_id=1, source_target_pairs={{0,2},{1,3},{2,0},{3,1},{4,6},{5,7},{6,4},{7,5},{8,10},{9,11},{10,... | collective-permute-start | bytes 786440 | tf_op jit(solution)/shard_map/ppermute | solution.py:27
  6.3 12.4 %collective-permute-start.2 = (bf16[128,1024]{1,0:T(8,128)(2,1)S(1)}, bf16[128,1024]{1,0:T(8,128)(2,1)S(1)}, u32[]{:S(2)}, u32[]{:S(2)}) collective-permute-start(bf16[128,1024]{1,0:T(8,128)(2,1)S(1)} %pad_maximum_fusion.2), channel_id=1, source_target_pairs={{0,3},{1,2},{2,1},{3,0},{4,7},{5,6},{6,5},{7,4},{8,11},{9,10},{10,... | collective-permute-start | bytes 786440 | tf_op jit(solution)/shard_map/ppermute | solution.py:27
  7.2 11.5 %collective-permute-start.3 = (bf16[128,1024]{1,0:T(8,128)(2,1)S(1)}, bf16[128,1024]{1,0:T(8,128)(2,1)S(1)}, u32[]{:S(2)}, u32[]{:S(2)}) collective-permute-start(bf16[128,1024]{1,0:T(8,128)(2,1)S(1)} %pad_maximum_fusion.3.refs_0_), channel_id=1, source_target_pairs={{0,4},{4,8},{8,12},{12,0},{1,5},{5,9},{9,13},{13,1},{2,6},{6,10},{... | collective-permute-start | bytes 786440 | tf_op jit(solution)/shard_map/ppermute | solution.py:31
  18.6 49.4 %all-to-all-start = ((bf16[8,136,1024]{2,1,0:T(8,128)(2,1)}), bf16[8,136,1024]{2,1,0:T(8,128)(2,1)S(1)}, u32[]{:S(2)}, u32[]{:S(2)}) async-start(bf16[8,136,1024]{2,1,0:T(8,128)(2,1)} %outgoing_rows.1), calls=%async_computation | async-start | bytes 4456448 | tf_op jit(solution)/shard_map/all_to_all | solution.py:39
  23.7 10.6 %collective-permute-start.4 = (bf16[128,1024]{1,0:T(8,128)(2,1)S(1)}, bf16[128,1024]{1,0:T(8,128)(2,1)S(1)}, u32[]{:S(2)}, u32[]{:S(2)}) collective-permute-start(bf16[128,1024]{1,0:T(8,128)(2,1)S(1)} %pad_maximum_fusion.4.refs_1_), channel_id=1, source_target_pairs={{0,4},{4,8},{8,12},{12,0},{1,5},{5,9},{9,13},{13,1},{2,6},{6,10},{... | collective-permute-start | bytes 786440 | tf_op jit(solution)/shard_map/ppermute | solution.py:31
  34.4 11.0 %collective-permute-start.6 = (bf16[128,1024]{1,0:T(8,128)(2,1)S(1)}, bf16[128,1024]{1,0:T(8,128)(2,1)S(1)}, u32[]{:S(2)}, u32[]{:S(2)}) collective-permute-start(bf16[128,1024]{1,0:T(8,128)(2,1)S(1)} %collective-permute-done.4.refs_3_), channel_id=1, source_target_pairs={{0,4},{4,8},{8,12},{12,0},{1,5},{5,9},{9,13},{13,1},{2,6},{6,10},{... | collective-permute-start | bytes 786440 | tf_op jit(solution)/shard_map/ppermute | solution.py:31
  34.4 0.7 copy-start.1
  35.1 16.0 %collective-permute-start.5 = (bf16[128,1024]{1,0:T(8,128)(2,1)S(1)}, bf16[128,1024]{1,0:T(8,128)(2,1)}, u32[]{:S(2)}, u32[]{:S(2)}) collective-permute-start(bf16[128,1024]{1,0:T(8,128)(2,1)S(1)} %collective-permute-done.3.refs_2_), channel_id=1, source_target_pairs={{0,4},{4,8},{8,12},{12,0},{1,5},{5,9},{9,13},{13,1},{2,6},{6,10},{... | collective-permute-start | bytes 786440 | tf_op jit(solution)/shard_map/ppermute | solution.py:31
  45.4 11.3 %copy-start.3 = (bf16[128,1024]{1,0:T(8,128)(2,1)}, bf16[128,1024]{1,0:T(8,128)(2,1)S(1)}, u32[]{:S(2)}) copy-start(bf16[128,1024]{1,0:T(8,128)(2,1)S(1)} %collective-permute-done.6.refs_5_) | copy-start | bytes 786436
  45.4 11.3 %collective-permute-start.8 = (bf16[128,1024]{1,0:T(8,128)(2,1)S(1)}, bf16[128,1024]{1,0:T(8,128)(2,1)}, u32[]{:S(2)}, u32[]{:S(2)}) collective-permute-start(bf16[128,1024]{1,0:T(8,128)(2,1)S(1)} %collective-permute-done.6.refs_5_), channel_id=1, source_target_pairs={{0,4},{4,8},{8,12},{12,0},{1,5},{5,9},{9,13},{13,1},{2,6},{6,10},{... | collective-permute-start | bytes 786440 | tf_op jit(solution)/shard_map/ppermute | solution.py:31
  51.1 11.2 %collective-permute-start.7 = (bf16[128,1024]{1,0:T(8,128)(2,1)}, bf16[128,1024]{1,0:T(8,128)(2,1)S(1)}, u32[]{:S(2)}, u32[]{:S(2)}) collective-permute-start(bf16[128,1024]{1,0:T(8,128)(2,1)} %collective-permute-done.5.refs_4_), channel_id=1, source_target_pairs={{0,4},{4,8},{8,12},{12,0},{1,5},{5,9},{9,13},{13,1},{2,6},{6,10},{... | collective-permute-start | bytes 786440 | tf_op jit(solution)/shard_map/ppermute | solution.py:31
  56.7 11.4 %collective-permute-start.10 = (bf16[128,1024]{1,0:T(8,128)(2,1)S(1)}, bf16[128,1024]{1,0:T(8,128)(2,1)}, u32[]{:S(2)}, u32[]{:S(2)}) collective-permute-start(bf16[128,1024]{1,0:T(8,128)(2,1)S(1)} %pad_maximum_fusion.6.refs_1_), channel_id=1, source_target_pairs={{0,4},{4,8},{8,12},{12,0},{1,5},{5,9},{9,13},{13,1},{2,6},{6,10},{... | collective-permute-start | bytes 786440 | tf_op jit(solution)/shard_map/ppermute | solution.py:31
  62.3 0.7 copy-start.5
  63.0 15.6 %collective-permute-start.9 = (bf16[128,1024]{1,0:T(8,128)(2,1)S(1)}, bf16[128,1024]{1,0:T(8,128)(2,1)}, u32[]{:S(2)}, u32[]{:S(2)}) collective-permute-start(bf16[128,1024]{1,0:T(8,128)(2,1)S(1)} %pad_maximum_fusion.5.refs_0_), channel_id=1, source_target_pairs={{0,4},{4,8},{8,12},{12,0},{1,5},{5,9},{9,13},{13,1},{2,6},{6,10},{... | collective-permute-start | bytes 786440 | tf_op jit(solution)/shard_map/ppermute | solution.py:31
  68.0 14.4 %collective-permute-start.12 = (bf16[128,1024]{1,0:T(8,128)(2,1)}, bf16[128,1024]{1,0:T(8,128)(2,1)}, u32[]{:S(2)}, u32[]{:S(2)}) collective-permute-start(bf16[128,1024]{1,0:T(8,128)(2,1)} %collective-permute-done.10.refs_3_), channel_id=1, source_target_pairs={{0,4},{4,8},{8,12},{12,0},{1,5},{5,9},{9,13},{13,1},{2,6},{6,10},{... | collective-permute-start | bytes 786440 | tf_op jit(solution)/shard_map/ppermute | solution.py:31
  68.1 1.0 copy-start.2
  69.0 0.9 copy-start.4
  70.0 0.9 copy-start.6
  77.8 0.8 copy-start.7
  78.6 8.4 %collective-permute-start.11 = (bf16[128,1024]{1,0:T(8,128)(2,1)}, bf16[128,1024]{1,0:T(8,128)(2,1)S(1)}, u32[]{:S(2)}, u32[]{:S(2)}) collective-permute-start(bf16[128,1024]{1,0:T(8,128)(2,1)} %collective-permute-done.9.refs_2_), channel_id=1, source_target_pairs={{0,4},{4,8},{8,12},{12,0},{1,5},{5,9},{9,13},{13,1},{2,6},{6,10},{... | collective-permute-start | bytes 786440 | tf_op jit(solution)/shard_map/ppermute | solution.py:31
  78.6 9.9 %all-to-all-start.1 = ((f32[8,64,128]{2,1,0:T(8,128)}), f32[8,64,128]{2,1,0:T(8,128)S(1)}, u32[]{:S(2)}, u32[]{:S(2)}) async-start(f32[8,64,128]{2,1,0:T(8,128)} %get-tuple-element.13), calls=%async_computation.1 | async-start | bytes 524288 | tf_op jit(solution)/shard_map/all_to_all | solution.py:39
  82.5 11.2 %collective-permute-start.14 = (bf16[128,1024]{1,0:T(8,128)(2,1)}, bf16[128,1024]{1,0:T(8,128)(2,1)S(1)}, u32[]{:S(2)}, u32[]{:S(2)}) collective-permute-start(bf16[128,1024]{1,0:T(8,128)(2,1)} %collective-permute-done.12.refs_5_), channel_id=1, source_target_pairs={{0,4},{4,8},{8,12},{12,0},{1,5},{5,9},{9,13},{13,1},{2,6},{6,10},{... | collective-permute-start | bytes 786440 | tf_op jit(solution)/shard_map/ppermute | solution.py:31
  87.0 12.1 %collective-permute-start.13 = (bf16[128,1024]{1,0:T(8,128)(2,1)S(1)}, bf16[128,1024]{1,0:T(8,128)(2,1)S(1)}, u32[]{:S(2)}, u32[]{:S(2)}) collective-permute-start(bf16[128,1024]{1,0:T(8,128)(2,1)S(1)} %collective-permute-done.11.refs_4_), channel_id=1, source_target_pairs={{0,4},{4,8},{8,12},{12,0},{1,5},{5,9},{9,13},{13,1},{2,6},{6,10},{... | collective-permute-start | bytes 786440 | tf_op jit(solution)/shard_map/ppermute | solution.py:31
  89.2 8.5 %all-to-all-start.2 = ((bf16[8,64,128]{2,1,0:T(8,128)(2,1)}), bf16[8,64,128]{2,1,0:T(8,128)(2,1)S(1)}, u32[]{:S(2)}, u32[]{:S(2)}) async-start(bf16[8,64,128]{2,1,0:T(8,128)(2,1)} %summed_copies.1), calls=%async_computation.2 | async-start | bytes 262144 | tf_op jit(solution)/shard_map/all_to_all | solution.py:39
  99.1 1.0 copy-start.8

commit v10 on v8

--- a/solution.py
+++ b/solution.py
@@ -260,7 +260,7 @@
         far = [after(jnp.concatenate(blocks[inner // 2 :], axis=0), *far_after)]
         for step in range(1, outer):
             near.append(next_on_ring(after(near[-1], *second_after) if step == 2 else near[-1], outer))
-            far.append(next_on_ring(far[-1], outer))
+            far.append(next_on_ring(after(far[-1], near[-1]), outer))
         return near, far
 
     steps_back = jnp.arange(outer, dtype=jnp.int32)[:, None]
@@ -270,10 +270,10 @@
     labels = labels.reshape(-1)
 
     down = exchanged(slices(adapter_down_maps[0].T))
-    up = exchanged([after(block, down[1]) for block in slices(adapter_up_maps[0])])
-    down_near, down_far = rings(down, second_after=up[1:])
+    down_near, down_far = rings(down)
     ids = token_adapter_index.astype(jnp.bfloat16).reshape(1, tok)
-    rows = swap(after(outgoing_rows(hidden, ids, members), *up[1:], down_near[1], down_far[1]))
+    rows = swap(after(outgoing_rows(hidden, ids, members), *down[1:], down_near[1]))
+    up = exchanged([after(block, down_near[1]) for block in slices(adapter_up_maps[0])])
 
     down_maps = [m for pair in zip(down_near, down_far) for m in pair]
     packed, id_columns = down_product(labels, rows, down_maps, rank)

time: 128 us -> 136 us (1.062)
  waiting for transfers between devices: 49.2 us -> 58.9 us
  starting transfers between devices: 25 us -> 18.1 us
  blocking collectives: 29.6 us -> 36.2 us
  local copies, waits for them, and re-layouts: 9.24 us -> 7.48 us
    ppermute x12, waiting for transfers between devices: 33.3 us -> 55.1 us  [next_on_ring(): lax.ppermute(block, 'outer', [(i, (i + 1) % outer) for i in range(outer)])]
    all_to_all x1 -> x2, blocking collectives: 29.6 us -> 36.2 us  [swap(): return lax.all_to_all(value, PLANE, split_axis=0, concat_axis=0, tiled=True)]
    all_to_all x3 -> x2, waiting for transfers between devices: 6.31 us -> 0.01 us  [swap(): return lax.all_to_all(value, PLANE, split_axis=0, concat_axis=0, tiled=True)]
    ppermute x6, waiting for transfers between devices: 9.57 us -> 3.85 us  [to_partner(): return lax.ppermute(value, axes, [(i, i ^ offset) for i in range(size)])]
    all_to_all x3 -> x2, starting transfers between devices: 11.3 us -> 7.15 us  [swap(): return lax.all_to_all(value, PLANE, split_axis=0, concat_axis=0, tiled=True)]
    ppermute x12, starting transfers between devices: 8.63 us -> 6.7 us  [next_on_ring(): lax.ppermute(block, 'outer', [(i, (i + 1) % outer) for i in range(outer)])]
    unnamed x26 -> x10, local copies, waits for them, and re-layouts: 6.07 us -> 4.37 us
  transfers between devices with their start and end apart: 21 -> 20, of which waited for: 14 -> 16; matrix products, arithmetic and copies ran while one was open for 3% -> 3% of each run, Pallas kernels for 5% -> 5%
where the time goes in v10:
time: 136 us; the launch traced here: 135 us
  waiting for transfers between devices  58.9 us (43%)
  blocking collectives  36.2 us (27%)
  starting transfers between devices  18.1 us (13%)
  Pallas kernels  11.6 us (9%)
  local copies, waits for them, and re-layouts  7.48 us (6%)
  other arithmetic  2.75 us (2%)
    ppermute x12, waiting for transfers between devices, next_on_ring(): lax.ppermute(block, 'outer', [(i, (i + 1) % outer) for i in range(outer)])  55.1 us
    all_to_all x2, blocking collectives, swap(): return lax.all_to_all(value, PLANE, split_axis=0, concat_axis=0, tiled=True)  36.2 us
    all_to_all x2, starting transfers between devices, swap(): return lax.all_to_all(value, PLANE, split_axis=0, concat_axis=0, tiled=True)  7.15 us
    ppermute x12, starting transfers between devices, next_on_ring(): lax.ppermute(block, 'outer', [(i, (i + 1) % outer) for i in range(outer)])  6.7 us
    pallas_call x1, Pallas kernels, down_product(): pl.pallas_call(functools.partial(down_kernel, len(maps), rank), out_shape...  4.63 us
    unnamed x10, local copies, waits for them, and re-layouts  4.37 us
    ppermute x6, starting transfers between devices, to_partner(): return lax.ppermute(value, axes, [(i, i ^ offset) for i in range(size)])  4.24 us
    pallas_call x1, Pallas kernels, up_product(): pl.pallas_call(functools.partial(up_kernel, len(maps), rank), out_shape=j...  4.06 us
  transfers between devices with their start and end apart: 20, of which 16 were waited for; matrix products, arithmetic and copies ran while one was open for 3% of the time, Pallas kernels for 5%

profile of v10, /device:TPU:0, one launch (start us, length us, event | category | flops | bytes accessed | tf_op | source)
XLA Modules:
  0.0 135.1 jit_solution(17438212467406494732)
XLA Ops:
  0.0 1.1 dynamic-slice_bitcast_fusion.4
  1.7 1.0 collective-permute-done
  2.7 3.0 %collective-permute-start.3 = (bf16[128,1024]{1,0:T(8,128)(2,1)S(1)}, bf16[128,1024]{1,0:T(8,128)(2,1)S(1)}, u32[]{:S(2)}, u32[]{:S(2)}) collective-permute-start(bf16[128,1024]{1,0:T(8,128)(2,1)S(1)} %pad_maximum_fusion.refs_0_), channel_id=1, source_target_pairs={{0,4},{4,8},{8,12},{12,0},{1,5},{5,9},{9,13},{13,1},{2,6},{6,10},{... | collective-permute-start | bytes 786440 | tf_op jit(solution)/shard_map/ppermute | solution.py:31
  5.6 1.5 %collective-permute-start.1 = (bf16[64,1024]{1,0:T(8,128)(2,1)S(1)}, bf16[64,1024]{1,0:T(8,128)(2,1)S(1)}, u32[]{:S(2)}, u32[]{:S(2)}) collective-permute-start(bf16[64,1024]{1,0:T(8,128)(2,1)S(1)} %get-tuple-element.42), channel_id=1, source_target_pairs={{0,2},{1,3},{2,0},{3,1},{4,6},{5,7},{6,4},{7,5},{8,10},{9,11},{10,... | collective-permute-start | bytes 393224 | tf_op jit(solution)/shard_map/ppermute | solution.py:27
  7.9 1.6 %copy-done = bf16[128,8192]{1,0:T(8,128)(2,1)S(1)} copy-done((bf16[128,8192]{1,0:T(8,128)(2,1)S(1)}, bf16[128,8192]{1,0:T(8,128)(2,1)}, u32[]{:S(2)}) %copy-start) | copy-done | bytes 2097176
  9.5 1.5 %outgoing_rows.1 = bf16[8,136,1024]{2,1,0:T(8,128)(2,1)} custom-call(bf16[128,8192]{1,0:T(8,128)(2,1)S(1)} %copy-done, bf16[8,1024]{1,0:T(8,128)(2,1)S(1)} %broadcast_in_dim.10.ids_ref), custom_call_target="tpu_custom_call" | custom-call | tf_op jit(solution)/shard_map/outgoing_rows/pallas_call | solution.py:63
  11.7 1.3 collective-permute-done.2
  13.0 1.3 collective-permute-done.3.refs_2_
  14.3 3.7 %all-to-all-start = ((bf16[8,136,1024]{2,1,0:T(8,128)(2,1)}), bf16[8,136,1024]{2,1,0:T(8,128)(2,1)S(1)}, u32[]{:S(2)}, u32[]{:S(2)}) async-start(bf16[8,136,1024]{2,1,0:T(8,128)(2,1)} %outgoing_rows.1), calls=%async_computation | async-start | bytes 4456448 | tf_op jit(solution)/shard_map/all_to_all | solution.py:39
  18.5 1.6 %collective-permute-start.5 = (bf16[128,1024]{1,0:T(8,128)(2,1)S(1)}, bf16[128,1024]{1,0:T(8,128)(2,1)}, u32[]{:S(2)}, u32[]{:S(2)}) collective-permute-start(bf16[128,1024]{1,0:T(8,128)(2,1)S(1)} %collective-permute-done.3.refs_2_), channel_id=1, source_target_pairs={{0,4},{4,8},{8,12},{12,0},{1,5},{5,9},{9,13},{13,1},{2,6},{6,10},{... | collective-permute-start | bytes 786440 | tf_op jit(solution)/shard_map/ppermute | solution.py:31
  20.1 8.9 %collective-permute-done.4.refs_3_ = bf16[128,1024]{1,0:T(8,128)(2,1)S(1)} collective-permute-done((bf16[128,1024]{1,0:T(8,128)(2,1)S(1)}, bf16[128,1024]{1,0:T(8,128)(2,1)S(1)}, u32[]{:S(2)}, u32[]{:S(2)}) %collective-permute-start.4) | collective-permute-done | bytes 262176 | tf_op jit(solution)/shard_map/ppermute | solution.py:31
  29.0 5.3 %collective-permute-done.5.refs_4_ = bf16[128,1024]{1,0:T(8,128)(2,1)} collective-permute-done((bf16[128,1024]{1,0:T(8,128)(2,1)S(1)}, bf16[128,1024]{1,0:T(8,128)(2,1)}, u32[]{:S(2)}, u32[]{:S(2)}) %collective-permute-start.5) | collective-permute-done | bytes 262176 | tf_op jit(solution)/shard_map/ppermute | solution.py:31
  34.5 1.9 %dynamic-slice_bitcast_fusion.1 = (bf16[64,1024]{1,0:T(8,128)(2,1)}, bf16[64,1024]{1,0:T(8,128)(2,1)S(1)}, bf16[64,1024]{1,0:T(8,128)(2,1)}, bf16[64,1024]{1,0:T(8,128)(2,1)}) fusion(bf16[1,64,8192]{2,1,0:T(8,128)(2,1)} %param.7, s32[]{:T(128)S(6)} %select_n.30, s32[]{:T(128)S(6)} %select_n.29, s32[]{:T(128)S(6)} %select_n.32, s32[]{:T(128)S(6)} %select_n.31), kind=kLoop, calls=%fused_computation.5 | loop fusion | bytes 1048592 | tf_op jit(solution)/shard_map/dynamic_slice | solution.py:252
  36.4 1.8 %collective-permute-start.11 = (bf16[64,1024]{1,0:T(8,128)(2,1)}, bf16[64,1024]{1,0:T(8,128)(2,1)}, u32[]{:S(2)}, u32[]{:S(2)}) collective-permute-start(bf16[64,1024]{1,0:T(8,128)(2,1)} %get-tuple-element.31), channel_id=1, source_target_pairs={{0,3},{1,2},{2,1},{3,0},{4,7},{5,6},{6,5},{7,4},{8,11},{9,10},{10,... | collective-permute-start | bytes 393224 | tf_op jit(solution)/shard_map/ppermute | solution.py:27
  38.6 1.0 pad_maximum_fusion.2.refs_0_
  39.6 5.8 %collective-permute-done.6.refs_5_ = bf16[128,1024]{1,0:T(8,128)(2,1)} collective-permute-done((bf16[128,1024]{1,0:T(8,128)(2,1)S(1)}, bf16[128,1024]{1,0:T(8,128)(2,1)}, u32[]{:S(2)}, u32[]{:S(2)}) %collective-permute-start.6) | collective-permute-done | bytes 262176 | tf_op jit(solution)/shard_map/ppermute | solution.py:31
  45.4 4.3 %collective-permute-done.7.refs_6_ = bf16[128,1024]{1,0:T(8,128)(2,1)} collective-permute-done((bf16[128,1024]{1,0:T(8,128)(2,1)}, bf16[128,1024]{1,0:T(8,128)(2,1)}, u32[]{:S(2)}, u32[]{:S(2)}) %collective-permute-start.7) | collective-permute-done | bytes 262176 | tf_op jit(solution)/shard_map/ppermute | solution.py:31
  50.8 1.0 pad_maximum_fusion.3.refs_1_
  51.8 9.3 %collective-permute-done.8.refs_7_ = bf16[128,1024]{1,0:T(8,128)(2,1)} collective-permute-done((bf16[128,1024]{1,0:T(8,128)(2,1)}, bf16[128,1024]{1,0:T(8,128)(2,1)}, u32[]{:S(2)}, u32[]{:S(2)}) %collective-permute-start.8) | collective-permute-done | bytes 262176 | tf_op jit(solution)/shard_map/ppermute | solution.py:31
  61.1 3.4 %collective-permute-done.12.refs_2_ = bf16[128,1024]{1,0:T(8,128)(2,1)} collective-permute-done((bf16[128,1024]{1,0:T(8,128)(2,1)S(1)}, bf16[128,1024]{1,0:T(8,128)(2,1)}, u32[]{:S(2)}, u32[]{:S(2)}) %collective-permute-start.12) | collective-permute-done | bytes 262176 | tf_op jit(solution)/shard_map/ppermute | solution.py:31
  65.5 4.6 %down_product.1 = (f32[8,64,128]{2,1,0:T(8,128)}, f32[8,128,128]{2,1,0:T(8,128)S(1)}) custom-call(s32[16]{0:T(128)S(1)} %add.62.labels_ref, bf16[8,136,1024]{2,1,0:T(8,128)(2,1)S(1)} %all-to-all-done.rows_ref, bf16[128,1024]{1,0:T(8,128)(2,1)S(1)} %pad_maximum_fusion.refs_0_, bf16[128,1024]{1,0:T(8,128)(2,1)S(1)} %pad_maximum_fusion.1.refs_1_, ...), custom_call_target="tpu_custom_call" | custom-call | flops 2147483648 | bytes 4194304 | tf_op jit(solution)/shard_map/down_product/pallas_call | solution.py:117
  71.0 1.9 %collective-permute-done.13.refs_3_ = bf16[128,1024]{1,0:T(8,128)(2,1)} collective-permute-done((bf16[128,1024]{1,0:T(8,128)(2,1)S(1)}, bf16[128,1024]{1,0:T(8,128)(2,1)}, u32[]{:S(2)}, u32[]{:S(2)}) %collective-permute-start.13) | collective-permute-done | bytes 262176 | tf_op jit(solution)/shard_map/ppermute | solution.py:31
  72.8 6.5 %collective-permute-done.14.refs_4_ = bf16[128,1024]{1,0:T(8,128)(2,1)S(1)} collective-permute-done((bf16[128,1024]{1,0:T(8,128)(2,1)}, bf16[128,1024]{1,0:T(8,128)(2,1)S(1)}, u32[]{:S(2)}, u32[]{:S(2)}) %collective-permute-start.14) | collective-permute-done | bytes 262176 | tf_op jit(solution)/shard_map/ppermute | solution.py:31
  79.3 1.4 %collective-permute-start.16 = (bf16[128,1024]{1,0:T(8,128)(2,1)S(1)}, bf16[128,1024]{1,0:T(8,128)(2,1)S(1)}, u32[]{:S(2)}, u32[]{:S(2)}) collective-permute-start(bf16[128,1024]{1,0:T(8,128)(2,1)S(1)} %collective-permute-done.14.refs_4_), channel_id=1, source_target_pairs={{0,4},{4,8},{8,12},{12,0},{1,5},{5,9},{9,13},{13,1},{2,6},{6,10},{... | collective-permute-start | bytes 786440 | tf_op jit(solution)/shard_map/ppermute | solution.py:31
  80.8 3.4 %all-to-all-start.1 = ((f32[8,64,128]{2,1,0:T(8,128)}), f32[8,64,128]{2,1,0:T(8,128)S(1)}, u32[]{:S(2)}, u32[]{:S(2)}) async-start(f32[8,64,128]{2,1,0:T(8,128)} %get-tuple-element.26), calls=%async_computation.1 | async-start | bytes 524288 | tf_op jit(solution)/shard_map/all_to_all | solution.py:39
  84.2 4.9 %collective-permute-done.15.refs_5_ = bf16[128,1024]{1,0:T(8,128)(2,1)S(1)} collective-permute-done((bf16[128,1024]{1,0:T(8,128)(2,1)}, bf16[128,1024]{1,0:T(8,128)(2,1)S(1)}, u32[]{:S(2)}, u32[]{:S(2)}) %collective-permute-start.15) | collective-permute-done | bytes 262176 | tf_op jit(solution)/shard_map/ppermute | solution.py:31
  89.1 2.8 %collective-permute-done.16.refs_6_ = bf16[128,1024]{1,0:T(8,128)(2,1)S(1)} collective-permute-done((bf16[128,1024]{1,0:T(8,128)(2,1)S(1)}, bf16[128,1024]{1,0:T(8,128)(2,1)S(1)}, u32[]{:S(2)}, u32[]{:S(2)}) %collective-permute-start.16) | collective-permute-done | bytes 262176 | tf_op jit(solution)/shard_map/ppermute | solution.py:31
  92.0 7.7 %all_to_all.20.shrunk_ref = bf16[8,64,128]{2,1,0:T(8,128)(2,1)S(1)} all-to-all(bf16[8,64,128]{2,1,0:T(8,128)(2,1)S(1)} %summed_copies.1), channel_id=1, replica_groups=mesh['groups'=2,'outer'=4,'inner'=4] {'groups','inner'}, dimensions={0} | all-to-all | bytes 262144 | tf_op jit(solution)/shard_map/all_to_all | solution.py:39
  100.1 1.0 copy-done.4
  101.2 4.1 %up_product.1 = bf16[8,128,1024]{2,1,0:T(8,128)(2,1)S(1)} custom-call(s32[16]{0:T(128)S(1)} %add.62.labels_ref, f32[8,128,128]{2,1,0:T(8,128)S(1)} %copy-done.4, bf16[8,64,128]{2,1,0:T(8,128)(2,1)S(1)} %all_to_all.20.shrunk_ref, bf16[128,1024]{1,0:T(8,128)(2,1)S(1)} %pad_maximum_fusion.2.refs_0_, bf16[128,1024]{1,0:T(8,128)(2,1)S(1)} %pad_maximum_fusion.3.refs_1_, ...), custom_call_target="tpu_custom_call" | custom-call | flops 2147483648 | bytes 4194304 | tf_op jit(solution)/shard_map/up_product/pallas_call | solution.py:194
  105.2 28.5 %all_to_all.21.refs_0_ = bf16[8,128,1024]{2,1,0:T(8,128)(2,1)S(1)} all-to-all(bf16[8,128,1024]{2,1,0:T(8,128)(2,1)S(1)} %up_product.1), channel_id=1, replica_groups=mesh['groups'=2,'outer'=4,'inner'=4] {'groups','inner'}, dimensions={0} | all-to-all | bytes 4194304 | tf_op jit(solution)/shard_map/all_to_all | solution.py:39
  133.7 1.4 %place_results.1 = bf16[128,8192]{1,0:T(8,128)(2,1)} custom-call(bf16[8,128,1024]{2,1,0:T(8,128)(2,1)S(1)} %all_to_all.21.refs_0_), custom_call_target="tpu_custom_call" | custom-call | tf_op jit(solution)/shard_map/place_results/pallas_call | solution.py:230
  (37 shorter events, 6.3 us)
Async XLA Ops:
  1.1 1.5 %collective-permute-start = (bf16[64,1024]{1,0:T(8,128)(2,1)S(1)}, bf16[64,1024]{1,0:T(8,128)(2,1)S(1)}, u32[]{:S(2)}, u32[]{:S(2)}) collective-permute-start(bf16[64,1024]{1,0:T(8,128)(2,1)S(1)} %get-tuple-element.43), channel_id=1, source_target_pairs={{0,1},{1,0},{2,3},{3,2},{4,5},{5,4},{6,7},{7,6},{8,9},{9,8},{10,11... | collective-permute-start | bytes 393224 | tf_op jit(solution)/shard_map/ppermute | solution.py:27
  2.7 11.6 %collective-permute-start.3 = (bf16[128,1024]{1,0:T(8,128)(2,1)S(1)}, bf16[128,1024]{1,0:T(8,128)(2,1)S(1)}, u32[]{:S(2)}, u32[]{:S(2)}) collective-permute-start(bf16[128,1024]{1,0:T(8,128)(2,1)S(1)} %pad_maximum_fusion.refs_0_), channel_id=1, source_target_pairs={{0,4},{4,8},{8,12},{12,0},{1,5},{5,9},{9,13},{13,1},{2,6},{6,10},{... | collective-permute-start | bytes 786440 | tf_op jit(solution)/shard_map/ppermute | solution.py:31
  5.6 6.0 %collective-permute-start.1 = (bf16[64,1024]{1,0:T(8,128)(2,1)S(1)}, bf16[64,1024]{1,0:T(8,128)(2,1)S(1)}, u32[]{:S(2)}, u32[]{:S(2)}) collective-permute-start(bf16[64,1024]{1,0:T(8,128)(2,1)S(1)} %get-tuple-element.42), channel_id=1, source_target_pairs={{0,2},{1,3},{2,0},{3,1},{4,6},{5,7},{6,4},{7,5},{8,10},{9,11},{10,... | collective-permute-start | bytes 393224 | tf_op jit(solution)/shard_map/ppermute | solution.py:27
  7.2 5.8 %collective-permute-start.2 = (bf16[64,1024]{1,0:T(8,128)(2,1)S(1)}, bf16[64,1024]{1,0:T(8,128)(2,1)S(1)}, u32[]{:S(2)}, u32[]{:S(2)}) collective-permute-start(bf16[64,1024]{1,0:T(8,128)(2,1)S(1)} %get-tuple-element.44), channel_id=1, source_target_pairs={{0,3},{1,2},{2,1},{3,0},{4,7},{5,6},{6,5},{7,4},{8,11},{9,10},{10,... | collective-permute-start | bytes 393224 | tf_op jit(solution)/shard_map/ppermute | solution.py:27
  7.9 1.6 %copy-start = (bf16[128,8192]{1,0:T(8,128)(2,1)S(1)}, bf16[128,8192]{1,0:T(8,128)(2,1)}, u32[]{:S(2)}) copy-start(bf16[128,8192]{1,0:T(8,128)(2,1)} %hidden_ref.1) | copy-start | bytes 6291460
  14.3 50.3 %all-to-all-start = ((bf16[8,136,1024]{2,1,0:T(8,128)(2,1)}), bf16[8,136,1024]{2,1,0:T(8,128)(2,1)S(1)}, u32[]{:S(2)}, u32[]{:S(2)}) async-start(bf16[8,136,1024]{2,1,0:T(8,128)(2,1)} %outgoing_rows.1), calls=%async_computation | async-start | bytes 4456448 | tf_op jit(solution)/shard_map/all_to_all | solution.py:39
  18.0 11.0 %collective-permute-start.4 = (bf16[128,1024]{1,0:T(8,128)(2,1)S(1)}, bf16[128,1024]{1,0:T(8,128)(2,1)S(1)}, u32[]{:S(2)}, u32[]{:S(2)}) collective-permute-start(bf16[128,1024]{1,0:T(8,128)(2,1)S(1)} %pad_maximum_fusion.1.refs_1_), channel_id=1, source_target_pairs={{0,4},{4,8},{8,12},{12,0},{1,5},{5,9},{9,13},{13,1},{2,6},{6,10},{... | collective-permute-start | bytes 786440 | tf_op jit(solution)/shard_map/ppermute | solution.py:31
  18.5 15.8 %collective-permute-start.5 = (bf16[128,1024]{1,0:T(8,128)(2,1)S(1)}, bf16[128,1024]{1,0:T(8,128)(2,1)}, u32[]{:S(2)}, u32[]{:S(2)}) collective-permute-start(bf16[128,1024]{1,0:T(8,128)(2,1)S(1)} %collective-permute-done.3.refs_2_), channel_id=1, source_target_pairs={{0,4},{4,8},{8,12},{12,0},{1,5},{5,9},{9,13},{13,1},{2,6},{6,10},{... | collective-permute-start | bytes 786440 | tf_op jit(solution)/shard_map/ppermute | solution.py:31
  29.0 21.0 %copy-start.1 = (bf16[128,1024]{1,0:T(8,128)(2,1)}, bf16[128,1024]{1,0:T(8,128)(2,1)S(1)}, u32[]{:S(2)}) copy-start(bf16[128,1024]{1,0:T(8,128)(2,1)S(1)} %collective-permute-done.4.refs_3_) | copy-start | bytes 786436
  34.3 11.1 %collective-permute-start.6 = (bf16[128,1024]{1,0:T(8,128)(2,1)S(1)}, bf16[128,1024]{1,0:T(8,128)(2,1)}, u32[]{:S(2)}, u32[]{:S(2)}) collective-permute-start(bf16[128,1024]{1,0:T(8,128)(2,1)S(1)} %collective-permute-done.4.refs_3_), channel_id=1, source_target_pairs={{0,4},{4,8},{8,12},{12,0},{1,5},{5,9},{9,13},{13,1},{2,6},{6,10},{... | collective-permute-start | bytes 786440 | tf_op jit(solution)/shard_map/ppermute | solution.py:31
  34.3 15.5 %collective-permute-start.7 = (bf16[128,1024]{1,0:T(8,128)(2,1)}, bf16[128,1024]{1,0:T(8,128)(2,1)}, u32[]{:S(2)}, u32[]{:S(2)}) collective-permute-start(bf16[128,1024]{1,0:T(8,128)(2,1)} %collective-permute-done.5.refs_4_), channel_id=1, source_target_pairs={{0,4},{4,8},{8,12},{12,0},{1,5},{5,9},{9,13},{13,1},{2,6},{6,10},{... | collective-permute-start | bytes 786440 | tf_op jit(solution)/shard_map/ppermute | solution.py:31
  36.4 2.2 %collective-permute-start.9 = (bf16[64,1024]{1,0:T(8,128)(2,1)S(1)}, bf16[64,1024]{1,0:T(8,128)(2,1)}, u32[]{:S(2)}, u32[]{:S(2)}) collective-permute-start(bf16[64,1024]{1,0:T(8,128)(2,1)S(1)} %get-tuple-element.28), channel_id=1, source_target_pairs={{0,1},{1,0},{2,3},{3,2},{4,5},{5,4},{6,7},{7,6},{8,9},{9,8},{10,11... | collective-permute-start | bytes 393224 | tf_op jit(solution)/shard_map/ppermute | solution.py:27
  36.4 13.5 %collective-permute-start.11 = (bf16[64,1024]{1,0:T(8,128)(2,1)}, bf16[64,1024]{1,0:T(8,128)(2,1)}, u32[]{:S(2)}, u32[]{:S(2)}) collective-permute-start(bf16[64,1024]{1,0:T(8,128)(2,1)} %get-tuple-element.31), channel_id=1, source_target_pairs={{0,3},{1,2},{2,1},{3,0},{4,7},{5,6},{6,5},{7,4},{8,11},{9,10},{10,... | collective-permute-start | bytes 393224 | tf_op jit(solution)/shard_map/ppermute | solution.py:27
  38.3 12.6 %collective-permute-start.10 = (bf16[64,1024]{1,0:T(8,128)(2,1)}, bf16[64,1024]{1,0:T(8,128)(2,1)}, u32[]{:S(2)}, u32[]{:S(2)}) collective-permute-start(bf16[64,1024]{1,0:T(8,128)(2,1)} %get-tuple-element.30), channel_id=1, source_target_pairs={{0,2},{1,3},{2,0},{3,1},{4,6},{5,7},{6,4},{7,5},{8,10},{9,11},{10,... | collective-permute-start | bytes 393224 | tf_op jit(solution)/shard_map/ppermute | solution.py:27
  49.8 11.4 %collective-permute-start.8 = (bf16[128,1024]{1,0:T(8,128)(2,1)}, bf16[128,1024]{1,0:T(8,128)(2,1)}, u32[]{:S(2)}, u32[]{:S(2)}) collective-permute-start(bf16[128,1024]{1,0:T(8,128)(2,1)} %collective-permute-done.6.refs_5_), channel_id=1, source_target_pairs={{0,4},{4,8},{8,12},{12,0},{1,5},{5,9},{9,13},{13,1},{2,6},{6,10},{... | collective-permute-start | bytes 786440 | tf_op jit(solution)/shard_map/ppermute | solution.py:31
  49.8 14.8 %collective-permute-start.12 = (bf16[128,1024]{1,0:T(8,128)(2,1)S(1)}, bf16[128,1024]{1,0:T(8,128)(2,1)}, u32[]{:S(2)}, u32[]{:S(2)}) collective-permute-start(bf16[128,1024]{1,0:T(8,128)(2,1)S(1)} %pad_maximum_fusion.2.refs_0_), channel_id=1, source_target_pairs={{0,4},{4,8},{8,12},{12,0},{1,5},{5,9},{9,13},{13,1},{2,6},{6,10},{... | collective-permute-start | bytes 786440 | tf_op jit(solution)/shard_map/ppermute | solution.py:31
  64.6 8.3 %collective-permute-start.13 = (bf16[128,1024]{1,0:T(8,128)(2,1)S(1)}, bf16[128,1024]{1,0:T(8,128)(2,1)}, u32[]{:S(2)}, u32[]{:S(2)}) collective-permute-start(bf16[128,1024]{1,0:T(8,128)(2,1)S(1)} %pad_maximum_fusion.3.refs_1_), channel_id=1, source_target_pairs={{0,4},{4,8},{8,12},{12,0},{1,5},{5,9},{9,13},{13,1},{2,6},{6,10},{... | collective-permute-start | bytes 786440 | tf_op jit(solution)/shard_map/ppermute | solution.py:31
  64.6 1.0 copy-start.2
  70.2 0.8 copy-start.3
  71.0 8.4 %collective-permute-start.14 = (bf16[128,1024]{1,0:T(8,128)(2,1)}, bf16[128,1024]{1,0:T(8,128)(2,1)S(1)}, u32[]{:S(2)}, u32[]{:S(2)}) collective-permute-start(bf16[128,1024]{1,0:T(8,128)(2,1)} %collective-permute-done.12.refs_2_), channel_id=1, source_target_pairs={{0,4},{4,8},{8,12},{12,0},{1,5},{5,9},{9,13},{13,1},{2,6},{6,10},{... | collective-permute-start | bytes 786440 | tf_op jit(solution)/shard_map/ppermute | solution.py:31
  79.3 9.8 %collective-permute-start.15 = (bf16[128,1024]{1,0:T(8,128)(2,1)}, bf16[128,1024]{1,0:T(8,128)(2,1)S(1)}, u32[]{:S(2)}, u32[]{:S(2)}) collective-permute-start(bf16[128,1024]{1,0:T(8,128)(2,1)} %collective-permute-done.13.refs_3_), channel_id=1, source_target_pairs={{0,4},{4,8},{8,12},{12,0},{1,5},{5,9},{9,13},{13,1},{2,6},{6,10},{... | collective-permute-start | bytes 786440 | tf_op jit(solution)/shard_map/ppermute | solution.py:31
  79.3 12.6 %collective-permute-start.16 = (bf16[128,1024]{1,0:T(8,128)(2,1)S(1)}, bf16[128,1024]{1,0:T(8,128)(2,1)S(1)}, u32[]{:S(2)}, u32[]{:S(2)}) collective-permute-start(bf16[128,1024]{1,0:T(8,128)(2,1)S(1)} %collective-permute-done.14.refs_4_), channel_id=1, source_target_pairs={{0,4},{4,8},{8,12},{12,0},{1,5},{5,9},{9,13},{13,1},{2,6},{6,10},{... | collective-permute-start | bytes 786440 | tf_op jit(solution)/shard_map/ppermute | solution.py:31
  80.8 11.2 %all-to-all-start.1 = ((f32[8,64,128]{2,1,0:T(8,128)}), f32[8,64,128]{2,1,0:T(8,128)S(1)}, u32[]{:S(2)}, u32[]{:S(2)}) async-start(f32[8,64,128]{2,1,0:T(8,128)} %get-tuple-element.26), calls=%async_computation.1 | async-start | bytes 524288 | tf_op jit(solution)/shard_map/all_to_all | solution.py:39
  91.9 8.2 %collective-permute-start.17 = (bf16[128,1024]{1,0:T(8,128)(2,1)S(1)}, bf16[128,1024]{1,0:T(8,128)(2,1)S(1)}, u32[]{:S(2)}, u32[]{:S(2)}) collective-permute-start(bf16[128,1024]{1,0:T(8,128)(2,1)S(1)} %collective-permute-done.15.refs_5_), channel_id=1, source_target_pairs={{0,4},{4,8},{8,12},{12,0},{1,5},{5,9},{9,13},{13,1},{2,6},{6,10},{... | collective-permute-start | bytes 786440 | tf_op jit(solution)/shard_map/ppermute | solution.py:31
  100.1 1.0 copy-start.4

commit v11 on v10

--- a/solution.py
+++ b/solution.py
@@ -48,23 +48,35 @@
     return label.astype(jnp.float32)
 
 
-def outgoing_kernel(hidden_ref, ids_ref, out_ref):
+def outgoing_kernel(hidden_ref, ids_ref, out_ref, sems):
     members, rows, share = out_ref.shape
     tok = rows - ID_ROWS
+    copies = [
+        pltpu.make_async_copy(
+            hidden_ref.at[:, pl.ds(member * share, share)], out_ref.at[member, pl.ds(0, tok)], sems.at[member]
+        )
+        for member in range(members)
+    ]
+    for copy in copies:
+        copy.start()
+    ids = jnp.broadcast_to(ids_ref[...].astype(jnp.float32).astype(jnp.bfloat16), (ID_ROWS, tok))
     for member in range(members):
-        out_ref[member, :tok, :] = hidden_ref[:, member * share : (member + 1) * share]
-        out_ref[member, tok:, :] = ids_ref[...]
+        out_ref[member, tok:, :tok] = ids
+        if share > tok:
+            out_ref[member, tok:, tok:] = jnp.zeros((ID_ROWS, share - tok), jnp.bfloat16)
+    for copy in copies:
+        copy.wait()
 
 
 def outgoing_rows(hidden, ids, members):
     tok, width = hidden.shape
     share = width // members
-    ids = jnp.broadcast_to(jnp.pad(ids, ((0, 0), (0, share - tok))), (ID_ROWS, share))
     return pl.pallas_call(
         outgoing_kernel,
         out_shape=jax.ShapeDtypeStruct((members, tok + ID_ROWS, share), jnp.bfloat16),
-        in_specs=[IN_VMEM, IN_VMEM],
+        in_specs=[IN_HBM, IN_VMEM],
         out_specs=IN_VMEM,
+        scratch_shapes=[pltpu.SemaphoreType.DMA((members,))],
         compiler_params=params(),
         name="outgoing_rows",
     )(hidden, ids)
@@ -260,7 +272,7 @@
         far = [after(jnp.concatenate(blocks[inner // 2 :], axis=0), *far_after)]
         for step in range(1, outer):
             near.append(next_on_ring(after(near[-1], *second_after) if step == 2 else near[-1], outer))
-            far.append(next_on_ring(after(far[-1], near[-1]), outer))
+            far.append(next_on_ring(far[-1], outer))
         return near, far
 
     steps_back = jnp.arange(outer, dtype=jnp.int32)[:, None]
@@ -271,8 +283,8 @@
 
     down = exchanged(slices(adapter_down_maps[0].T))
     down_near, down_far = rings(down)
-    ids = token_adapter_index.astype(jnp.bfloat16).reshape(1, tok)
-    rows = swap(after(outgoing_rows(hidden, ids, members), *down[1:], down_near[1]))
+    ids = token_adapter_index.reshape(1, tok)
+    rows = swap(after(outgoing_rows(hidden, ids, members), down[1]))
     up = exchanged([after(block, down_near[1]) for block in slices(adapter_up_maps[0])])
 
     down_maps = [m for pair in zip(down_near, down_far) for m in pair]

time: 136 us -> 154 us (1.13)
  waiting for transfers between devices: 58.9 us -> 75.3 us
  blocking collectives: 36.2 us -> 29.6 us
  starting transfers between devices: 18.1 us -> 22.7 us
  local copies, waits for them, and re-layouts: 7.48 us -> 10.9 us
    ppermute x6, waiting for transfers between devices: 3.85 us -> 33.6 us  [to_partner(): return lax.ppermute(value, axes, [(i, i ^ offset) for i in range(size)])]
    ppermute x12, waiting for transfers between devices: 55.1 us -> 35.6 us  [next_on_ring(): lax.ppermute(block, 'outer', [(i, (i + 1) % outer) for i in range(outer)])]
    all_to_all x2 -> x1, blocking collectives: 36.2 us -> 29.6 us  [swap(): return lax.all_to_all(value, PLANE, split_axis=0, concat_axis=0, tiled=True)]
    all_to_all x2 -> x3, waiting for transfers between devices: 0.01 us -> 6.14 us  [swap(): return lax.all_to_all(value, PLANE, split_axis=0, concat_axis=0, tiled=True)]
    all_to_all x2 -> x3, starting transfers between devices: 7.15 us -> 12.1 us  [swap(): return lax.all_to_all(value, PLANE, split_axis=0, concat_axis=0, tiled=True)]
    unnamed x10 -> x20, local copies, waits for them, and re-layouts: 4.37 us -> 7.63 us
  transfers between devices with their start and end apart: 20 -> 21, of which waited for: 16 -> 16; matrix products, arithmetic and copies ran while one was open for 3% -> 3% of each run, Pallas kernels for 5% -> 4%
where the time goes in v11:
time: 154 us; the launch traced here: 153 us
  waiting for transfers between devices  75.3 us (49%)
  blocking collectives  29.6 us (19%)
  starting transfers between devices  22.7 us (15%)
  Pallas kernels  12.3 us (8%)
  local copies, waits for them, and re-layouts  10.9 us (7%)
  other arithmetic  2.03 us (1%)
    ppermute x12, waiting for transfers between devices, next_on_ring(): lax.ppermute(block, 'outer', [(i, (i + 1) % outer) for i in range(outer)])  35.6 us
    ppermute x6, waiting for transfers between devices, to_partner(): return lax.ppermute(value, axes, [(i, i ^ offset) for i in range(size)])  33.6 us
    all_to_all x1, blocking collectives, swap(): return lax.all_to_all(value, PLANE, split_axis=0, concat_axis=0, tiled=True)  29.6 us
    all_to_all x3, starting transfers between devices, swap(): return lax.all_to_all(value, PLANE, split_axis=0, concat_axis=0, tiled=True)  12.1 us
    unnamed x20, local copies, waits for them, and re-layouts  7.63 us
    all_to_all x3, waiting for transfers between devices, swap(): return lax.all_to_all(value, PLANE, split_axis=0, concat_axis=0, tiled=True)  6.14 us
    ppermute x12, starting transfers between devices, next_on_ring(): lax.ppermute(block, 'outer', [(i, (i + 1) % outer) for i in range(outer)])  6.05 us
    ppermute x6, starting transfers between devices, to_partner(): return lax.ppermute(value, axes, [(i, i ^ offset) for i in range(size)])  4.51 us
  transfers between devices with their start and end apart: 21, of which 16 were waited for; matrix products, arithmetic and copies ran while one was open for 3% of the time, Pallas kernels for 4%

profile of v11, /device:TPU:0, one launch (start us, length us, event | category | flops | bytes accessed | tf_op | source)
XLA Modules:
  0.0 152.9 jit_solution(15227312466753415170)
XLA Ops:
  0.0 1.1 dynamic-slice_bitcast_fusion.5
  1.7 1.6 %copy-done = bf16[128,8192]{1,0:T(8,128)(2,1)S(1)} copy-done((bf16[128,8192]{1,0:T(8,128)(2,1)S(1)}, bf16[128,8192]{1,0:T(8,128)(2,1)}, u32[]{:S(2)}) %copy-start) | copy-done | bytes 2097176
  3.9 1.6 %outgoing_rows.1 = bf16[8,136,1024]{2,1,0:T(8,128)(2,1)} custom-call(bf16[128,8192]{1,0:T(8,128)(2,1)S(1)} %copy-done, s32[1,128]{1,0:T(1,128)S(1)} %bitcast.25), custom_call_target="tpu_custom_call" | custom-call | tf_op jit(solution)/shard_map/outgoing_rows/pallas_call | solution.py:74
  5.5 4.8 %all-to-all-start = ((bf16[8,136,1024]{2,1,0:T(8,128)(2,1)}), bf16[8,136,1024]{2,1,0:T(8,128)(2,1)S(1)}, u32[]{:S(2)}, u32[]{:S(2)}) async-start(bf16[8,136,1024]{2,1,0:T(8,128)(2,1)} %outgoing_rows.1), calls=%async_computation | async-start | bytes 4456448 | tf_op jit(solution)/shard_map/all_to_all | solution.py:39
  10.4 1.8 %collective-permute-start.2 = (bf16[64,1024]{1,0:T(8,128)(2,1)S(1)}, bf16[64,1024]{1,0:T(8,128)(2,1)S(1)}, u32[]{:S(2)}, u32[]{:S(2)}) collective-permute-start(bf16[64,1024]{1,0:T(8,128)(2,1)S(1)} %get-tuple-element.32), channel_id=1, source_target_pairs={{0,3},{1,2},{2,1},{3,0},{4,7},{5,6},{6,5},{7,4},{8,11},{9,10},{10,... | collective-permute-start | bytes 393224 | tf_op jit(solution)/shard_map/ppermute | solution.py:27
  12.5 27.3 %collective-permute-done.2 = bf16[64,1024]{1,0:T(8,128)(2,1)S(1)} collective-permute-done((bf16[64,1024]{1,0:T(8,128)(2,1)S(1)}, bf16[64,1024]{1,0:T(8,128)(2,1)S(1)}, u32[]{:S(2)}, u32[]{:S(2)}) %collective-permute-start.2) | collective-permute-done | bytes 131104 | tf_op jit(solution)/shard_map/ppermute | solution.py:27
  39.8 3.3 %collective-permute-done.1 = bf16[64,1024]{1,0:T(8,128)(2,1)S(1)} collective-permute-done((bf16[64,1024]{1,0:T(8,128)(2,1)S(1)}, bf16[64,1024]{1,0:T(8,128)(2,1)S(1)}, u32[]{:S(2)}, u32[]{:S(2)}) %collective-permute-start.1) | collective-permute-done | bytes 131104 | tf_op jit(solution)/shard_map/ppermute | solution.py:27
  43.1 1.6 %collective-permute-start.4 = (bf16[128,1024]{1,0:T(8,128)(2,1)S(1)}, bf16[128,1024]{1,0:T(8,128)(2,1)S(1)}, u32[]{:S(2)}, u32[]{:S(2)}) collective-permute-start(bf16[128,1024]{1,0:T(8,128)(2,1)S(1)} %pad_maximum_fusion.1.refs_1_), channel_id=1, source_target_pairs={{0,4},{4,8},{8,12},{12,0},{1,5},{5,9},{9,13},{13,1},{2,6},{6,10},{... | collective-permute-start | bytes 786440 | tf_op jit(solution)/shard_map/ppermute | solution.py:31
  44.8 1.6 %collective-permute-start.3 = (bf16[128,1024]{1,0:T(8,128)(2,1)S(1)}, bf16[128,1024]{1,0:T(8,128)(2,1)S(1)}, u32[]{:S(2)}, u32[]{:S(2)}) collective-permute-start(bf16[128,1024]{1,0:T(8,128)(2,1)S(1)} %pad_maximum_fusion.refs_0_), channel_id=1, source_target_pairs={{0,4},{4,8},{8,12},{12,0},{1,5},{5,9},{9,13},{13,1},{2,6},{6,10},{... | collective-permute-start | bytes 786440 | tf_op jit(solution)/shard_map/ppermute | solution.py:31
  46.4 7.8 %collective-permute-done.4.refs_3_ = bf16[128,1024]{1,0:T(8,128)(2,1)S(1)} collective-permute-done((bf16[128,1024]{1,0:T(8,128)(2,1)S(1)}, bf16[128,1024]{1,0:T(8,128)(2,1)S(1)}, u32[]{:S(2)}, u32[]{:S(2)}) %collective-permute-start.4) | collective-permute-done | bytes 262176 | tf_op jit(solution)/shard_map/ppermute | solution.py:31
  54.2 5.6 %collective-permute-done.3.refs_2_ = bf16[128,1024]{1,0:T(8,128)(2,1)S(1)} collective-permute-done((bf16[128,1024]{1,0:T(8,128)(2,1)S(1)}, bf16[128,1024]{1,0:T(8,128)(2,1)S(1)}, u32[]{:S(2)}, u32[]{:S(2)}) %collective-permute-start.3) | collective-permute-done | bytes 262176 | tf_op jit(solution)/shard_map/ppermute | solution.py:31
  59.8 5.6 %collective-permute-done.6.refs_5_ = bf16[128,1024]{1,0:T(8,128)(2,1)S(1)} collective-permute-done((bf16[128,1024]{1,0:T(8,128)(2,1)S(1)}, bf16[128,1024]{1,0:T(8,128)(2,1)S(1)}, u32[]{:S(2)}, u32[]{:S(2)}) %collective-permute-start.6) | collective-permute-done | bytes 262176 | tf_op jit(solution)/shard_map/ppermute | solution.py:31
  65.4 2.0 %dynamic-slice_bitcast_fusion.1 = (bf16[64,1024]{1,0:T(8,128)(2,1)}, bf16[64,1024]{1,0:T(8,128)(2,1)}, bf16[64,1024]{1,0:T(8,128)(2,1)}, bf16[64,1024]{1,0:T(8,128)(2,1)}) fusion(bf16[1,64,8192]{2,1,0:T(8,128)(2,1)} %param.7, s32[]{:T(128)S(6)} %select_n.31, s32[]{:T(128)S(6)} %select_n.29, s32[]{:T(128)S(6)} %select_n.30, s32[]{:T(128)S(6)} %select_n.32), kind=kLoop, calls=%fused_computation.5 | loop fusion | bytes 1048592 | tf_op jit(solution)/shard_map/dynamic_slice | solution.py:264
  67.8 1.5 collective-permute-start.9
  69.3 1.8 %collective-permute-done.5.refs_4_ = bf16[128,1024]{1,0:T(8,128)(2,1)} collective-permute-done((bf16[128,1024]{1,0:T(8,128)(2,1)S(1)}, bf16[128,1024]{1,0:T(8,128)(2,1)}, u32[]{:S(2)}, u32[]{:S(2)}) %collective-permute-start.5) | collective-permute-done | bytes 262176 | tf_op jit(solution)/shard_map/ppermute | solution.py:31
  71.2 2.3 %collective-permute-done.11 = bf16[64,1024]{1,0:T(8,128)(2,1)} collective-permute-done((bf16[64,1024]{1,0:T(8,128)(2,1)}, bf16[64,1024]{1,0:T(8,128)(2,1)}, u32[]{:S(2)}, u32[]{:S(2)}) %collective-permute-start.11) | collective-permute-done | bytes 131104 | tf_op jit(solution)/shard_map/ppermute | solution.py:27
  75.2 1.4 collective-permute-done.8.refs_7_
  77.6 3.4 %collective-permute-done.7.refs_6_ = bf16[128,1024]{1,0:T(8,128)(2,1)S(1)} collective-permute-done((bf16[128,1024]{1,0:T(8,128)(2,1)}, bf16[128,1024]{1,0:T(8,128)(2,1)S(1)}, u32[]{:S(2)}, u32[]{:S(2)}) %collective-permute-start.7) | collective-permute-done | bytes 262176 | tf_op jit(solution)/shard_map/ppermute | solution.py:31
  81.9 5.8 %collective-permute-done.13.refs_3_ = bf16[128,1024]{1,0:T(8,128)(2,1)} collective-permute-done((bf16[128,1024]{1,0:T(8,128)(2,1)S(1)}, bf16[128,1024]{1,0:T(8,128)(2,1)}, u32[]{:S(2)}, u32[]{:S(2)}) %collective-permute-start.13) | collective-permute-done | bytes 262176 | tf_op jit(solution)/shard_map/ppermute | solution.py:31
  90.6 4.5 %down_product.1 = (f32[8,64,128]{2,1,0:T(8,128)}, f32[8,128,128]{2,1,0:T(8,128)S(1)}) custom-call(s32[16]{0:T(128)S(1)} %add.60.labels_ref, bf16[8,136,1024]{2,1,0:T(8,128)(2,1)S(1)} %all-to-all-done.rows_ref, bf16[128,1024]{1,0:T(8,128)(2,1)S(1)} %pad_maximum_fusion.refs_0_, bf16[128,1024]{1,0:T(8,128)(2,1)S(1)} %pad_maximum_fusion.1.refs_1_, ...), custom_call_target="tpu_custom_call" | custom-call | flops 2147483648 | bytes 4194304 | tf_op jit(solution)/shard_map/down_product/pallas_call | solution.py:129
  96.5 3.9 %all-to-all-start.1 = ((f32[8,64,128]{2,1,0:T(8,128)}), f32[8,64,128]{2,1,0:T(8,128)S(1)}, u32[]{:S(2)}, u32[]{:S(2)}) async-start(f32[8,64,128]{2,1,0:T(8,128)} %get-tuple-element.17), calls=%async_computation.1 | async-start | bytes 524288 | tf_op jit(solution)/shard_map/all_to_all | solution.py:39
  100.4 2.1 %collective-permute-start.17 = (bf16[128,1024]{1,0:T(8,128)(2,1)}, bf16[128,1024]{1,0:T(8,128)(2,1)S(1)}, u32[]{:S(2)}, u32[]{:S(2)}) collective-permute-start(bf16[128,1024]{1,0:T(8,128)(2,1)} %collective-permute-done.15.refs_5_), channel_id=1, source_target_pairs={{0,4},{4,8},{8,12},{12,0},{1,5},{5,9},{9,13},{13,1},{2,6},{6,10},{... | collective-permute-start | bytes 786440 | tf_op jit(solution)/shard_map/ppermute | solution.py:31
  102.4 1.8 %collective-permute-done.14.refs_4_ = bf16[128,1024]{1,0:T(8,128)(2,1)S(1)} collective-permute-done((bf16[128,1024]{1,0:T(8,128)(2,1)}, bf16[128,1024]{1,0:T(8,128)(2,1)S(1)}, u32[]{:S(2)}, u32[]{:S(2)}) %collective-permute-start.14) | collective-permute-done | bytes 262176 | tf_op jit(solution)/shard_map/ppermute | solution.py:31
  104.3 2.1 %all-to-all-done.1.terms_ref = f32[8,64,128]{2,1,0:T(8,128)S(1)} async-done(((f32[8,64,128]{2,1,0:T(8,128)}), f32[8,64,128]{2,1,0:T(8,128)S(1)}, u32[]{:S(2)}, u32[]{:S(2)}) %all-to-all-start.1) | async-done | bytes 262176 | tf_op jit(solution)/shard_map/all_to_all | solution.py:39
  107.1 3.4 %all-to-all-start.2 = ((bf16[8,64,128]{2,1,0:T(8,128)(2,1)}), bf16[8,64,128]{2,1,0:T(8,128)(2,1)S(1)}, u32[]{:S(2)}, u32[]{:S(2)}) async-start(bf16[8,64,128]{2,1,0:T(8,128)(2,1)} %summed_copies.1), calls=%async_computation.2 | async-start | bytes 262144 | tf_op jit(solution)/shard_map/all_to_all | solution.py:39
  110.5 1.1 collective-permute-done.17.refs_7_
  111.5 4.0 %all-to-all-done.2.shrunk_ref = bf16[8,64,128]{2,1,0:T(8,128)(2,1)S(1)} async-done(((bf16[8,64,128]{2,1,0:T(8,128)(2,1)}), bf16[8,64,128]{2,1,0:T(8,128)(2,1)S(1)}, u32[]{:S(2)}, u32[]{:S(2)}) %all-to-all-start.2) | async-done | bytes 131104 | tf_op jit(solution)/shard_map/all_to_all | solution.py:39
  115.6 1.1 collective-permute-done.16.refs_6_
  116.7 1.0 copy-done.9
  117.8 4.1 %up_product.1 = bf16[8,128,1024]{2,1,0:T(8,128)(2,1)S(1)} custom-call(s32[16]{0:T(128)S(1)} %add.60.labels_ref, f32[8,128,128]{2,1,0:T(8,128)S(1)} %copy-done.9, bf16[8,64,128]{2,1,0:T(8,128)(2,1)S(1)} %all-to-all-done.2.shrunk_ref, bf16[128,1024]{1,0:T(8,128)(2,1)S(1)} %pad_maximum_fusion.2.refs_0_, bf16[128,1024]{1,0:T(8,128)(2,1)S(1)} %pad_maximum_fusion.3.refs_1_, ...), custom_call_target="tpu_custom_call" | custom-call | flops 2147483648 | bytes 4194304 | tf_op jit(solution)/shard_map/up_product/pallas_call | solution.py:206
  121.9 29.6 %all_to_all.20.refs_0_ = bf16[8,128,1024]{2,1,0:T(8,128)(2,1)S(1)} all-to-all(bf16[8,128,1024]{2,1,0:T(8,128)(2,1)S(1)} %up_product.1), channel_id=1, replica_groups=mesh['groups'=2,'outer'=4,'inner'=4] {'groups','inner'}, dimensions={0} | all-to-all | bytes 4194304 | tf_op jit(solution)/shard_map/all_to_all | solution.py:39
  151.6 1.4 place_results.1
  (45 shorter events, 10.5 us)
Async XLA Ops:
  1.1 4.4 %collective-permute-start = (bf16[64,1024]{1,0:T(8,128)(2,1)S(1)}, bf16[64,1024]{1,0:T(8,128)(2,1)S(1)}, u32[]{:S(2)}, u32[]{:S(2)}) collective-permute-start(bf16[64,1024]{1,0:T(8,128)(2,1)S(1)} %get-tuple-element.31), channel_id=1, source_target_pairs={{0,1},{1,0},{2,3},{3,2},{4,5},{5,4},{6,7},{7,6},{8,9},{9,8},{10,11... | collective-permute-start | bytes 393224 | tf_op jit(solution)/shard_map/ppermute | solution.py:27
  1.7 1.6 %copy-start = (bf16[128,8192]{1,0:T(8,128)(2,1)S(1)}, bf16[128,8192]{1,0:T(8,128)(2,1)}, u32[]{:S(2)}) copy-start(bf16[128,8192]{1,0:T(8,128)(2,1)} %hidden_ref.1) | copy-start | bytes 6291460
  3.2 0.7 copy-start.1
  5.5 82.2 %all-to-all-start = ((bf16[8,136,1024]{2,1,0:T(8,128)(2,1)}), bf16[8,136,1024]{2,1,0:T(8,128)(2,1)S(1)}, u32[]{:S(2)}, u32[]{:S(2)}) async-start(bf16[8,136,1024]{2,1,0:T(8,128)(2,1)} %outgoing_rows.1), calls=%async_computation | async-start | bytes 4456448 | tf_op jit(solution)/shard_map/all_to_all | solution.py:39
  10.4 29.4 %collective-permute-start.2 = (bf16[64,1024]{1,0:T(8,128)(2,1)S(1)}, bf16[64,1024]{1,0:T(8,128)(2,1)S(1)}, u32[]{:S(2)}, u32[]{:S(2)}) collective-permute-start(bf16[64,1024]{1,0:T(8,128)(2,1)S(1)} %get-tuple-element.32), channel_id=1, source_target_pairs={{0,3},{1,2},{2,1},{3,0},{4,7},{5,6},{6,5},{7,4},{8,11},{9,10},{10,... | collective-permute-start | bytes 393224 | tf_op jit(solution)/shard_map/ppermute | solution.py:27
  12.2 30.9 %collective-permute-start.1 = (bf16[64,1024]{1,0:T(8,128)(2,1)S(1)}, bf16[64,1024]{1,0:T(8,128)(2,1)S(1)}, u32[]{:S(2)}, u32[]{:S(2)}) collective-permute-start(bf16[64,1024]{1,0:T(8,128)(2,1)S(1)} %get-tuple-element.29), channel_id=1, source_target_pairs={{0,2},{1,3},{2,0},{3,1},{4,6},{5,7},{6,4},{7,5},{8,10},{9,11},{10,... | collective-permute-start | bytes 393224 | tf_op jit(solution)/shard_map/ppermute | solution.py:27
  43.1 11.1 %collective-permute-start.4 = (bf16[128,1024]{1,0:T(8,128)(2,1)S(1)}, bf16[128,1024]{1,0:T(8,128)(2,1)S(1)}, u32[]{:S(2)}, u32[]{:S(2)}) collective-permute-start(bf16[128,1024]{1,0:T(8,128)(2,1)S(1)} %pad_maximum_fusion.1.refs_1_), channel_id=1, source_target_pairs={{0,4},{4,8},{8,12},{12,0},{1,5},{5,9},{9,13},{13,1},{2,6},{6,10},{... | collective-permute-start | bytes 786440 | tf_op jit(solution)/shard_map/ppermute | solution.py:31
  44.8 15.0 %collective-permute-start.3 = (bf16[128,1024]{1,0:T(8,128)(2,1)S(1)}, bf16[128,1024]{1,0:T(8,128)(2,1)S(1)}, u32[]{:S(2)}, u32[]{:S(2)}) collective-permute-start(bf16[128,1024]{1,0:T(8,128)(2,1)S(1)} %pad_maximum_fusion.refs_0_), channel_id=1, source_target_pairs={{0,4},{4,8},{8,12},{12,0},{1,5},{5,9},{9,13},{13,1},{2,6},{6,10},{... | collective-permute-start | bytes 786440 | tf_op jit(solution)/shard_map/ppermute | solution.py:31
  54.2 11.2 %collective-permute-start.6 = (bf16[128,1024]{1,0:T(8,128)(2,1)S(1)}, bf16[128,1024]{1,0:T(8,128)(2,1)S(1)}, u32[]{:S(2)}, u32[]{:S(2)}) collective-permute-start(bf16[128,1024]{1,0:T(8,128)(2,1)S(1)} %collective-permute-done.4.refs_3_), channel_id=1, source_target_pairs={{0,4},{4,8},{8,12},{12,0},{1,5},{5,9},{9,13},{13,1},{2,6},{6,10},{... | collective-permute-start | bytes 786440 | tf_op jit(solution)/shard_map/ppermute | solution.py:31
  59.8 13.7 %copy-start.2 = (bf16[128,1024]{1,0:T(8,128)(2,1)}, bf16[128,1024]{1,0:T(8,128)(2,1)S(1)}, u32[]{:S(2)}) copy-start(bf16[128,1024]{1,0:T(8,128)(2,1)S(1)} %collective-permute-done.3.refs_2_) | copy-start | bytes 786436
  59.8 11.3 %collective-permute-start.5 = (bf16[128,1024]{1,0:T(8,128)(2,1)S(1)}, bf16[128,1024]{1,0:T(8,128)(2,1)}, u32[]{:S(2)}, u32[]{:S(2)}) collective-permute-start(bf16[128,1024]{1,0:T(8,128)(2,1)S(1)} %collective-permute-done.3.refs_2_), channel_id=1, source_target_pairs={{0,4},{4,8},{8,12},{12,0},{1,5},{5,9},{9,13},{13,1},{2,6},{6,10},{... | collective-permute-start | bytes 786440 | tf_op jit(solution)/shard_map/ppermute | solution.py:31
  65.4 11.2 %copy-start.4 = (bf16[128,1024]{1,0:T(8,128)(2,1)}, bf16[128,1024]{1,0:T(8,128)(2,1)S(1)}, u32[]{:S(2)}) copy-start(bf16[128,1024]{1,0:T(8,128)(2,1)S(1)} %collective-permute-done.6.refs_5_) | copy-start | bytes 786436
  65.4 11.2 %collective-permute-start.8 = (bf16[128,1024]{1,0:T(8,128)(2,1)S(1)}, bf16[128,1024]{1,0:T(8,128)(2,1)}, u32[]{:S(2)}, u32[]{:S(2)}) collective-permute-start(bf16[128,1024]{1,0:T(8,128)(2,1)S(1)} %collective-permute-done.6.refs_5_), channel_id=1, source_target_pairs={{0,4},{4,8},{8,12},{12,0},{1,5},{5,9},{9,13},{13,1},{2,6},{6,10},{... | collective-permute-start | bytes 786440 | tf_op jit(solution)/shard_map/ppermute | solution.py:31
  67.5 6.1 %collective-permute-start.11 = (bf16[64,1024]{1,0:T(8,128)(2,1)}, bf16[64,1024]{1,0:T(8,128)(2,1)}, u32[]{:S(2)}, u32[]{:S(2)}) collective-permute-start(bf16[64,1024]{1,0:T(8,128)(2,1)} %get-tuple-element.22), channel_id=1, source_target_pairs={{0,3},{1,2},{2,1},{3,0},{4,7},{5,6},{6,5},{7,4},{8,11},{9,10},{10,... | collective-permute-start | bytes 393224 | tf_op jit(solution)/shard_map/ppermute | solution.py:27
  67.5 6.8 %collective-permute-start.10 = (bf16[64,1024]{1,0:T(8,128)(2,1)}, bf16[64,1024]{1,0:T(8,128)(2,1)}, u32[]{:S(2)}, u32[]{:S(2)}) collective-permute-start(bf16[64,1024]{1,0:T(8,128)(2,1)} %get-tuple-element.21), channel_id=1, source_target_pairs={{0,2},{1,3},{2,0},{3,1},{4,6},{5,7},{6,4},{7,5},{8,10},{9,11},{10,... | collective-permute-start | bytes 393224 | tf_op jit(solution)/shard_map/ppermute | solution.py:27
  67.8 8.8 %collective-permute-start.9 = (bf16[64,1024]{1,0:T(8,128)(2,1)}, bf16[64,1024]{1,0:T(8,128)(2,1)S(1)}, u32[]{:S(2)}, u32[]{:S(2)}) collective-permute-start(bf16[64,1024]{1,0:T(8,128)(2,1)} %get-tuple-element.19), channel_id=1, source_target_pairs={{0,1},{1,0},{2,3},{3,2},{4,5},{5,4},{6,7},{7,6},{8,9},{9,8},{10,11... | collective-permute-start | bytes 393224 | tf_op jit(solution)/shard_map/ppermute | solution.py:27
  71.2 9.8 %collective-permute-start.7 = (bf16[128,1024]{1,0:T(8,128)(2,1)}, bf16[128,1024]{1,0:T(8,128)(2,1)S(1)}, u32[]{:S(2)}, u32[]{:S(2)}) collective-permute-start(bf16[128,1024]{1,0:T(8,128)(2,1)} %collective-permute-done.5.refs_4_), channel_id=1, source_target_pairs={{0,4},{4,8},{8,12},{12,0},{1,5},{5,9},{9,13},{13,1},{2,6},{6,10},{... | collective-permute-start | bytes 786440 | tf_op jit(solution)/shard_map/ppermute | solution.py:31
  76.7 11.1 %collective-permute-start.13 = (bf16[128,1024]{1,0:T(8,128)(2,1)S(1)}, bf16[128,1024]{1,0:T(8,128)(2,1)}, u32[]{:S(2)}, u32[]{:S(2)}) collective-permute-start(bf16[128,1024]{1,0:T(8,128)(2,1)S(1)} %pad_maximum_fusion.3.refs_1_), channel_id=1, source_target_pairs={{0,4},{4,8},{8,12},{12,0},{1,5},{5,9},{9,13},{13,1},{2,6},{6,10},{... | collective-permute-start | bytes 786440 | tf_op jit(solution)/shard_map/ppermute | solution.py:31
  81.0 0.7 copy-start.6
  81.7 14.2 %collective-permute-start.12 = (bf16[128,1024]{1,0:T(8,128)(2,1)S(1)}, bf16[128,1024]{1,0:T(8,128)(2,1)}, u32[]{:S(2)}, u32[]{:S(2)}) collective-permute-start(bf16[128,1024]{1,0:T(8,128)(2,1)S(1)} %pad_maximum_fusion.2.refs_0_), channel_id=1, source_target_pairs={{0,4},{4,8},{8,12},{12,0},{1,5},{5,9},{9,13},{13,1},{2,6},{6,10},{... | collective-permute-start | bytes 786440 | tf_op jit(solution)/shard_map/ppermute | solution.py:31
  87.7 12.6 %collective-permute-start.15 = (bf16[128,1024]{1,0:T(8,128)(2,1)}, bf16[128,1024]{1,0:T(8,128)(2,1)}, u32[]{:S(2)}, u32[]{:S(2)}) collective-permute-start(bf16[128,1024]{1,0:T(8,128)(2,1)} %collective-permute-done.13.refs_3_), channel_id=1, source_target_pairs={{0,4},{4,8},{8,12},{12,0},{1,5},{5,9},{9,13},{13,1},{2,6},{6,10},{... | collective-permute-start | bytes 786440 | tf_op jit(solution)/shard_map/ppermute | solution.py:31
  87.8 1.0 copy-start.3
  88.7 0.9 copy-start.5
  89.7 0.9 copy-start.7
  95.1 0.8 copy-start.8
  95.9 8.4 %collective-permute-start.14 = (bf16[128,1024]{1,0:T(8,128)(2,1)}, bf16[128,1024]{1,0:T(8,128)(2,1)S(1)}, u32[]{:S(2)}, u32[]{:S(2)}) collective-permute-start(bf16[128,1024]{1,0:T(8,128)(2,1)} %collective-permute-done.12.refs_2_), channel_id=1, source_target_pairs={{0,4},{4,8},{8,12},{12,0},{1,5},{5,9},{9,13},{13,1},{2,6},{6,10},{... | collective-permute-start | bytes 786440 | tf_op jit(solution)/shard_map/ppermute | solution.py:31
  96.5 9.9 %all-to-all-start.1 = ((f32[8,64,128]{2,1,0:T(8,128)}), f32[8,64,128]{2,1,0:T(8,128)S(1)}, u32[]{:S(2)}, u32[]{:S(2)}) async-start(f32[8,64,128]{2,1,0:T(8,128)} %get-tuple-element.17), calls=%async_computation.1 | async-start | bytes 524288 | tf_op jit(solution)/shard_map/all_to_all | solution.py:39
  100.4 11.2 %collective-permute-start.17 = (bf16[128,1024]{1,0:T(8,128)(2,1)}, bf16[128,1024]{1,0:T(8,128)(2,1)S(1)}, u32[]{:S(2)}, u32[]{:S(2)}) collective-permute-start(bf16[128,1024]{1,0:T(8,128)(2,1)} %collective-permute-done.15.refs_5_), channel_id=1, source_target_pairs={{0,4},{4,8},{8,12},{12,0},{1,5},{5,9},{9,13},{13,1},{2,6},{6,10},{... | collective-permute-start | bytes 786440 | tf_op jit(solution)/shard_map/ppermute | solution.py:31
  104.3 12.5 %collective-permute-start.16 = (bf16[128,1024]{1,0:T(8,128)(2,1)S(1)}, bf16[128,1024]{1,0:T(8,128)(2,1)S(1)}, u32[]{:S(2)}, u32[]{:S(2)}) collective-permute-start(bf16[128,1024]{1,0:T(8,128)(2,1)S(1)} %collective-permute-done.14.refs_4_), channel_id=1, source_target_pairs={{0,4},{4,8},{8,12},{12,0},{1,5},{5,9},{9,13},{13,1},{2,6},{6,10},{... | collective-permute-start | bytes 786440 | tf_op jit(solution)/shard_map/ppermute | solution.py:31
  107.1 8.5 %all-to-all-start.2 = ((bf16[8,64,128]{2,1,0:T(8,128)(2,1)}), bf16[8,64,128]{2,1,0:T(8,128)(2,1)S(1)}, u32[]{:S(2)}, u32[]{:S(2)}) async-start(bf16[8,64,128]{2,1,0:T(8,128)(2,1)} %summed_copies.1), calls=%async_computation.2 | async-start | bytes 262144 | tf_op jit(solution)/shard_map/all_to_all | solution.py:39
  116.7 1.0 copy-start.9

commit v12 on v11

--- a/solution.py
+++ b/solution.py
@@ -12,6 +12,7 @@
 PLANE = ("groups", "inner")
 LANES = 128
 ID_ROWS = 8
+RINGS = 3
 BLOCK = 8
 IN_VMEM = pl.BlockSpec(memory_space=pltpu.VMEM)
 IN_SMEM = pl.BlockSpec(memory_space=pltpu.SMEM)
@@ -74,12 +75,17 @@
     return pl.pallas_call(
         outgoing_kernel,
         out_shape=jax.ShapeDtypeStruct((members, tok + ID_ROWS, share), jnp.bfloat16),
-        in_specs=[IN_HBM, IN_VMEM],
+        in_specs=[ANYWHERE, IN_VMEM],
         out_specs=IN_VMEM,
         scratch_shapes=[pltpu.SemaphoreType.DMA((members,))],
         compiler_params=params(),
         name="outgoing_rows",
     )(hidden, ids)
+
+
+def held_maps(maps, step, first, rank):
+    own, *others = maps[step * RINGS : (step + 1) * RINGS]
+    return [own[first : first + rank, :]] + [other[...] for other in others]
 
 
 def down_kernel(map_count, rank, labels_ref, rows_ref, *refs):
@@ -101,17 +107,19 @@
         kept.start()
         ids = ids_ref[here].reshape(block * tok, LANES)
         tile = 0
-        for at in range(0, map_count, 2):
-            some = jnp.concatenate([m[...] for m in maps[at : at + 2]], axis=0)
-            product = lax.dot_general(
-                tokens, some, (((1,), (1,)), ((), ())), preferred_element_type=jnp.float32
-            )
-            total = jnp.zeros((block * tok, LANES), jnp.float32) if tile == 0 else total_ref[...]
-            for n in range(some.shape[0] // LANES):
-                named = ids == tile_labels(labels_ref, tile, rank, (1, LANES))
-                total += jnp.where(named, product[:, n * LANES : (n + 1) * LANES], 0.0)
-                tile += 1
-            total_ref[...] = total
+        for back in range(map_count // RINGS):
+            held = jnp.concatenate(held_maps(maps, back, 0, rank), axis=0)
+            for at in range(0, held.shape[0], 2 * LANES):
+                some = held[at : at + 2 * LANES]
+                product = lax.dot_general(
+                    tokens, some, (((1,), (1,)), ((), ())), preferred_element_type=jnp.float32
+                )
+                total = jnp.zeros((block * tok, LANES), jnp.float32) if tile == 0 else total_ref[...]
+                for n in range(some.shape[0] // LANES):
+                    named = ids == tile_labels(labels_ref, tile, rank, (1, LANES))
+                    total += jnp.where(named, product[:, n * LANES : (n + 1) * LANES], 0.0)
+                    tile += 1
+                total_ref[...] = total
         for n in range(block):
             total = total_ref[n * tok : (n + 1) * tok, :]
             total += pltpu.roll(total, LANES // 2, 1)
@@ -125,7 +133,7 @@
 def down_product(labels, rows, maps, rank):
     members, tok, share = rows.shape
     tok -= ID_ROWS
-    map_rows = sum(m.shape[0] for m in maps)
+    map_rows = labels.shape[0] * rank
     return pl.pallas_call(
         functools.partial(down_kernel, len(maps), rank),
         out_shape=[
@@ -175,7 +183,9 @@
     block = min(BLOCK, members)
     tiles = spread_ref.shape[1] // LANES
     lane = lax.broadcasted_iota(jnp.int32, (half, LANES), 1)
-    held = jnp.concatenate([m[...] for m in maps], axis=0)
+    held = jnp.concatenate(
+        [m for back in range(map_count // RINGS) for m in held_maps(maps, back, rank, rank)], axis=0
+    )
     kept.wait()
 
     def one(step, _):
@@ -202,7 +212,7 @@
 
 def up_product(labels, ids, shrunk, maps, rank):
     members, tok, _ = ids.shape
-    map_rows, piece = sum(m.shape[0] for m in maps), maps[0].shape[1]
+    map_rows, piece = labels.shape[0] * rank, maps[0].shape[1]
     return pl.pallas_call(
         functools.partial(up_kernel, len(maps), rank),
         out_shape=jax.ShapeDtypeStruct((members, tok, piece), jnp.bfloat16),
@@ -259,21 +269,24 @@
     rank = adapter_up_maps.shape[1]
     me = group * inner + place_in_group
 
-    def slices(array):
-        return [
-            lax.dynamic_slice_in_dim(array, (me ^ offset) * share, share, axis=1) for offset in range(inner)
-        ]
-
-    def exchanged(blocks):
-        return blocks[:1] + [to_partner(blocks[n], "inner", inner, n) for n in range(1, inner)]
-
-    def rings(blocks, near_after=(), far_after=(), second_after=()):
-        near = [after(jnp.concatenate(blocks[: inner // 2], axis=0), *near_after)]
-        far = [after(jnp.concatenate(blocks[inner // 2 :], axis=0), *far_after)]
+    def slices(offset):
+        start = (me ^ offset) * share
+        return jnp.concatenate(
+            [
+                lax.dynamic_slice_in_dim(adapter_down_maps[0].T, start, share, axis=1),
+                lax.dynamic_slice_in_dim(adapter_up_maps[0], start, share, axis=1),
+            ],
+            axis=0,
+        )
+
+    got = [slices(0)] + [to_partner(slices(n), "inner", inner, n) for n in range(1, inner)]
+
+    def ring(block, second_after=()):
+        blocks = [block]
         for step in range(1, outer):
-            near.append(next_on_ring(after(near[-1], *second_after) if step == 2 else near[-1], outer))
-            far.append(next_on_ring(far[-1], outer))
-        return near, far
+            block = next_on_ring(after(block, *second_after) if step == 2 else block, outer)
+            blocks.append(block)
+        return blocks
 
     steps_back = jnp.arange(outer, dtype=jnp.int32)[:, None]
     labels = ((level - steps_back + outer) % outer) * inner + (
@@ -281,18 +294,23 @@
     )
     labels = labels.reshape(-1)
 
-    down = exchanged(slices(adapter_down_maps[0].T))
-    down_near, down_far = rings(down)
+    own = ring(got[0])
+    down = [g[:rank] for g in got]
+    up = [g[rank:] for g in got]
+    middle = inner // 2
+    down_near = ring(jnp.concatenate(down[1:middle], axis=0))
+    down_far = ring(jnp.concatenate(down[middle:], axis=0))
     ids = token_adapter_index.reshape(1, tok)
-    rows = swap(after(outgoing_rows(hidden, ids, members), down[1]))
-    up = exchanged([after(block, down_near[1]) for block in slices(adapter_up_maps[0])])
-
-    down_maps = [m for pair in zip(down_near, down_far) for m in pair]
-    packed, id_columns = down_product(labels, rows, down_maps, rank)
-    up_near, up_far = rings(up, [down_near[-1]], [down_far[-1]], second_after=[packed])
-    up_maps = [m for pair in zip(up_near, up_far) for m in pair]
+    rows = swap(after(outgoing_rows(hidden, ids, members), *got[1:], own[2]))
+
+    packed, id_columns = down_product(
+        labels, rows, [m for step in zip(own, down_near, down_far) for m in step], rank
+    )
+    up_near = ring(after(jnp.concatenate(up[1:middle], axis=0), down_near[-1]))
+    up_far = ring(after(jnp.concatenate(up[middle:], axis=0), down_far[-1]), second_after=[packed])
     shrunk = swap(summed_copies(swap(packed)))
-    return place([swap(up_product(labels, id_columns, shrunk, up_maps, rank))])
+    delta = up_product(labels, id_columns, shrunk, [m for step in zip(own, up_near, up_far) for m in step], rank)
+    return place([swap(delta)])
 
 
 def solution(mesh):

time: 154 us -> 141 us (0.916)
  starting transfers between devices: 22.7 us -> 15.7 us
  local copies, waits for them, and re-layouts: 10.9 us -> 7.71 us
    ppermute x12 -> x15, waiting for transfers between devices: 35.6 us -> 68.2 us  [next_on_ring(): lax.ppermute(block, 'outer', [(i, (i + 1) % outer) for i in range(outer)])]
    ppermute x6 -> x3, waiting for transfers between devices: 33.6 us -> 4.1 us  [to_partner(): return lax.ppermute(value, axes, [(i, i ^ offset) for i in range(size)])]
    unnamed x20 -> x12, local copies, waits for them, and re-layouts: 7.63 us -> 2.79 us
    all_to_all x3, waiting for transfers between devices: 6.14 us -> 2.4 us  [swap(): return lax.all_to_all(value, PLANE, split_axis=0, concat_axis=0, tiled=True)]
    ppermute x12 -> x15, starting transfers between devices: 6.05 us -> 3.28 us  [next_on_ring(): lax.ppermute(block, 'outer', [(i, (i + 1) % outer) for i in range(outer)])]
    ppermute x6 -> x3, starting transfers between devices: 4.51 us -> 2.04 us  [to_partner(): return lax.ppermute(value, axes, [(i, i ^ offset) for i in range(size)])]
    slice x0 -> x3, local copies, waits for them, and re-layouts: none -> 2.42 us  [per_device(): up = [g[rank:] for g in got]]
    all_to_all x3, starting transfers between devices: 12.1 us -> 10.4 us  [swap(): return lax.all_to_all(value, PLANE, split_axis=0, concat_axis=0, tiled=True)]
  transfers between devices with their start and end apart: 21 -> 21, of which waited for: 16 -> 12; matrix products, arithmetic and copies ran while one was open for 3% -> 3% of each run, Pallas kernels for 4% -> 5%
where the time goes in v12:
time: 141 us
  waiting for transfers between devices  74.8 us (53%)
  blocking collectives  28.4 us (20%)
  starting transfers between devices  15.7 us (11%)
  Pallas kernels  12.6 us (9%)
  local copies, waits for them, and re-layouts  7.71 us (5%)
    ppermute x15, waiting for transfers between devices, next_on_ring(): lax.ppermute(block, 'outer', [(i, (i + 1) % outer) for i in range(outer)])  68.2 us
    all_to_all x1, blocking collectives, swap(): return lax.all_to_all(value, PLANE, split_axis=0, concat_axis=0, tiled=True)  28.4 us
    all_to_all x3, starting transfers between devices, swap(): return lax.all_to_all(value, PLANE, split_axis=0, concat_axis=0, tiled=True)  10.4 us
    pallas_call x1, Pallas kernels, down_product(): pl.pallas_call(functools.partial(down_kernel, len(maps), rank), out_shape...  4.73 us
    pallas_call x1, Pallas kernels, up_product(): pl.pallas_call(functools.partial(up_kernel, len(maps), rank), out_shape=j...  4.15 us
    ppermute x3, waiting for transfers between devices, to_partner(): return lax.ppermute(value, axes, [(i, i ^ offset) for i in range(size)])  4.1 us
    ppermute x15, starting transfers between devices, next_on_ring(): lax.ppermute(block, 'outer', [(i, (i + 1) % outer) for i in range(outer)])  3.28 us
  transfers between devices with their start and end apart: 21, of which 12 were waited for; matrix products, arithmetic and copies ran while one was open for 3% of the time, Pallas kernels for 5%

profile of v12, /device:TPU:0, one launch (start us, length us, event | category | flops | bytes accessed | tf_op | source)
XLA Modules:
  0.0 140.6 jit_solution(10142478011727607857)
XLA Ops:
  0.0 1.3 dynamic-slice_bitcast_fusion
  1.3 1.1 dynamic-slice_bitcast_fusion.1
  2.5 3.1 %collective-permute-start.3 = (bf16[128,1024]{1,0:T(8,128)(2,1)S(1)}, bf16[128,1024]{1,0:T(8,128)(2,1)S(1)}, u32[]{:S(2)}, u32[]{:S(2)}) collective-permute-start(bf16[128,1024]{1,0:T(8,128)(2,1)S(1)} %pad_maximum_fusion.3.refs_0_), channel_id=1, source_target_pairs={{0,4},{4,8},{8,12},{12,0},{1,5},{5,9},{9,13},{13,1},{2,6},{6,10},{... | collective-permute-start | bytes 786440 | tf_op jit(solution)/shard_map/ppermute | solution.py:32
  5.7 1.6 %collective-permute-start.1 = (bf16[128,1024]{1,0:T(8,128)(2,1)S(1)}, bf16[128,1024]{1,0:T(8,128)(2,1)S(1)}, u32[]{:S(2)}, u32[]{:S(2)}) collective-permute-start(bf16[128,1024]{1,0:T(8,128)(2,1)S(1)} %pad_maximum_fusion.1), channel_id=1, source_target_pairs={{0,2},{1,3},{2,0},{3,1},{4,6},{5,7},{6,4},{7,5},{8,10},{9,11},{10,... | collective-permute-start | bytes 786440 | tf_op jit(solution)/shard_map/ppermute | solution.py:28
  7.7 6.2 %collective-permute-done.3.refs_3_ = bf16[128,1024]{1,0:T(8,128)(2,1)S(1)} collective-permute-done((bf16[128,1024]{1,0:T(8,128)(2,1)S(1)}, bf16[128,1024]{1,0:T(8,128)(2,1)S(1)}, u32[]{:S(2)}, u32[]{:S(2)}) %collective-permute-start.3) | collective-permute-done | bytes 262176 | tf_op jit(solution)/shard_map/ppermute | solution.py:32
  13.9 1.6 %outgoing_rows.1 = bf16[8,136,1024]{2,1,0:T(8,128)(2,1)} custom-call(bf16[128,8192]{1,0:T(8,128)(2,1)S(1)} %copy-done, s32[1,128]{1,0:T(1,128)S(1)} %bitcast.25), custom_call_target="tpu_custom_call" | custom-call | tf_op jit(solution)/shard_map/outgoing_rows/pallas_call | solution.py:75
  15.5 4.1 %collective-permute-done.2 = bf16[128,1024]{1,0:T(8,128)(2,1)S(1)} collective-permute-done((bf16[128,1024]{1,0:T(8,128)(2,1)S(1)}, bf16[128,1024]{1,0:T(8,128)(2,1)S(1)}, u32[]{:S(2)}, u32[]{:S(2)}) %collective-permute-start.2) | collective-permute-done | bytes 262176 | tf_op jit(solution)/shard_map/ppermute | solution.py:28
  19.6 3.6 %collective-permute-done.4.refs_6_ = bf16[128,1024]{1,0:T(8,128)(2,1)} collective-permute-done((bf16[128,1024]{1,0:T(8,128)(2,1)S(1)}, bf16[128,1024]{1,0:T(8,128)(2,1)}, u32[]{:S(2)}, u32[]{:S(2)}) %collective-permute-start.4) | collective-permute-done | bytes 262176 | tf_op jit(solution)/shard_map/ppermute | solution.py:32
  23.3 3.6 %all-to-all-start = ((bf16[8,136,1024]{2,1,0:T(8,128)(2,1)}), bf16[8,136,1024]{2,1,0:T(8,128)(2,1)S(1)}, u32[]{:S(2)}, u32[]{:S(2)}) async-start(bf16[8,136,1024]{2,1,0:T(8,128)(2,1)} %outgoing_rows.1), calls=%async_computation | async-start | bytes 4456448 | tf_op jit(solution)/shard_map/all_to_all | solution.py:40
  26.9 0.7 fusion.3
  27.6 0.7 fusion.2
  28.3 10.4 %collective-permute-done.6.refs_5_ = bf16[128,1024]{1,0:T(8,128)(2,1)S(1)} collective-permute-done((bf16[128,1024]{1,0:T(8,128)(2,1)S(1)}, bf16[128,1024]{1,0:T(8,128)(2,1)S(1)}, u32[]{:S(2)}, u32[]{:S(2)}) %collective-permute-start.6) | collective-permute-done | bytes 262176 | tf_op jit(solution)/shard_map/ppermute | solution.py:32
  38.7 1.1 fusion.4
  39.9 10.0 %collective-permute-done.8.refs_8_ = bf16[128,1024]{1,0:T(8,128)(2,1)} collective-permute-done((bf16[128,1024]{1,0:T(8,128)(2,1)S(1)}, bf16[128,1024]{1,0:T(8,128)(2,1)}, u32[]{:S(2)}, u32[]{:S(2)}) %collective-permute-start.8) | collective-permute-done | bytes 262176 | tf_op jit(solution)/shard_map/ppermute | solution.py:32
  49.9 1.4 %collective-permute-done.5.refs_4_ = bf16[64,1024]{1,0:T(8,128)(2,1)} collective-permute-done((bf16[64,1024]{1,0:T(8,128)(2,1)S(1)}, bf16[64,1024]{1,0:T(8,128)(2,1)}, u32[]{:S(2)}, u32[]{:S(2)}) %collective-permute-start.5) | collective-permute-done | bytes 131104 | tf_op jit(solution)/shard_map/ppermute | solution.py:32
  51.4 1.0 pad_maximum_fusion.5.refs_2_
  52.4 11.5 %collective-permute-done.7.refs_7_ = bf16[64,1024]{1,0:T(8,128)(2,1)} collective-permute-done((bf16[64,1024]{1,0:T(8,128)(2,1)}, bf16[64,1024]{1,0:T(8,128)(2,1)}, u32[]{:S(2)}, u32[]{:S(2)}) %collective-permute-start.7) | collective-permute-done | bytes 131104 | tf_op jit(solution)/shard_map/ppermute | solution.py:32
  64.1 7.5 %collective-permute-done.10.refs_10_ = bf16[64,1024]{1,0:T(8,128)(2,1)} collective-permute-done((bf16[64,1024]{1,0:T(8,128)(2,1)}, bf16[64,1024]{1,0:T(8,128)(2,1)}, u32[]{:S(2)}, u32[]{:S(2)}) %collective-permute-start.10) | collective-permute-done | bytes 131104 | tf_op jit(solution)/shard_map/ppermute | solution.py:32
  71.6 0.9 copy-done.3
  72.6 4.7 %down_product.1 = (f32[8,64,128]{2,1,0:T(8,128)}, f32[8,128,128]{2,1,0:T(8,128)S(1)}) custom-call(s32[16]{0:T(128)S(1)} %add.60.labels_ref, bf16[8,136,1024]{2,1,0:T(8,128)(2,1)S(1)} %all-to-all-done.rows_ref, bf16[128,1024]{1,0:T(8,128)(2,1)S(1)} %pad_maximum_fusion.3.refs_0_, bf16[64,1024]{1,0:T(8,128)(2,1)S(1)} %get-tuple-element.30.refs_1_, ...), custom_call_target="tpu_custom_call" | custom-call | flops 2147483648 | bytes 4194304 | tf_op jit(solution)/shard_map/down_product/pallas_call | solution.py:137
  77.3 0.8 copy-done.4
  78.1 3.4 %all-to-all-start.1 = ((f32[8,64,128]{2,1,0:T(8,128)}), f32[8,64,128]{2,1,0:T(8,128)S(1)}, u32[]{:S(2)}, u32[]{:S(2)}) async-start(f32[8,64,128]{2,1,0:T(8,128)} %get-tuple-element.13), calls=%async_computation.1 | async-start | bytes 524288 | tf_op jit(solution)/shard_map/all_to_all | solution.py:40
  81.5 7.5 %collective-permute-done.12.refs_4_ = bf16[64,1024]{1,0:T(8,128)(2,1)S(1)} collective-permute-done((bf16[64,1024]{1,0:T(8,128)(2,1)S(1)}, bf16[64,1024]{1,0:T(8,128)(2,1)S(1)}, u32[]{:S(2)}, u32[]{:S(2)}) %collective-permute-start.12) | collective-permute-done | bytes 131104 | tf_op jit(solution)/shard_map/ppermute | solution.py:32
  89.1 7.3 %collective-permute-done.14.refs_7_ = bf16[64,1024]{1,0:T(8,128)(2,1)S(1)} collective-permute-done((bf16[64,1024]{1,0:T(8,128)(2,1)S(1)}, bf16[64,1024]{1,0:T(8,128)(2,1)S(1)}, u32[]{:S(2)}, u32[]{:S(2)}) %collective-permute-start.14) | collective-permute-done | bytes 131104 | tf_op jit(solution)/shard_map/ppermute | solution.py:32
  96.4 0.7 summed_copies.1
  97.0 3.4 %all-to-all-start.2 = ((bf16[8,64,128]{2,1,0:T(8,128)(2,1)}), bf16[8,64,128]{2,1,0:T(8,128)(2,1)S(1)}, u32[]{:S(2)}, u32[]{:S(2)}) async-start(bf16[8,64,128]{2,1,0:T(8,128)(2,1)} %summed_copies.1), calls=%async_computation.2 | async-start | bytes 262144 | tf_op jit(solution)/shard_map/all_to_all | solution.py:40
  100.4 2.7 %collective-permute-done.16.refs_10_ = bf16[64,1024]{1,0:T(8,128)(2,1)S(1)} collective-permute-done((bf16[64,1024]{1,0:T(8,128)(2,1)S(1)}, bf16[64,1024]{1,0:T(8,128)(2,1)S(1)}, u32[]{:S(2)}, u32[]{:S(2)}) %collective-permute-start.16) | collective-permute-done | bytes 131104 | tf_op jit(solution)/shard_map/ppermute | solution.py:32
  103.1 2.4 %all-to-all-done.2.shrunk_ref = bf16[8,64,128]{2,1,0:T(8,128)(2,1)S(1)} async-done(((bf16[8,64,128]{2,1,0:T(8,128)(2,1)}), bf16[8,64,128]{2,1,0:T(8,128)(2,1)S(1)}, u32[]{:S(2)}, u32[]{:S(2)}) %all-to-all-start.2) | async-done | bytes 131104 | tf_op jit(solution)/shard_map/all_to_all | solution.py:40
  105.5 1.0 copy-done.5
  106.6 4.1 %up_product.1 = bf16[8,128,1024]{2,1,0:T(8,128)(2,1)S(1)} custom-call(s32[16]{0:T(128)S(1)} %add.60.labels_ref, f32[8,128,128]{2,1,0:T(8,128)S(1)} %copy-done.5, bf16[8,64,128]{2,1,0:T(8,128)(2,1)S(1)} %all-to-all-done.2.shrunk_ref, bf16[128,1024]{1,0:T(8,128)(2,1)S(1)} %pad_maximum_fusion.3.refs_0_, bf16[64,1024]{1,0:T(8,128)(2,1)S(1)} %get-tuple-element.14.refs_1_, ...), custom_call_target="tpu_custom_call" | custom-call | flops 2147483648 | bytes 4194304 | tf_op jit(solution)/shard_map/up_product/pallas_call | solution.py:216
  110.7 28.4 %all_to_all.20.refs_0_ = bf16[8,128,1024]{2,1,0:T(8,128)(2,1)S(1)} all-to-all(bf16[8,128,1024]{2,1,0:T(8,128)(2,1)S(1)} %up_product.1), channel_id=1, replica_groups=mesh['groups'=2,'outer'=4,'inner'=4] {'groups','inner'}, dimensions={0} | all-to-all | bytes 4194304 | tf_op jit(solution)/shard_map/all_to_all | solution.py:40
  139.2 1.4 place_results.1
  (42 shorter events, 1.0 us)
Async XLA Ops:
  0.0 13.9 %copy-start = (bf16[128,8192]{1,0:T(8,128)(2,1)S(1)}, bf16[128,8192]{1,0:T(8,128)(2,1)}, u32[]{:S(2)}) copy-start(bf16[128,8192]{1,0:T(8,128)(2,1)} %hidden_ref.1) | copy-start | bytes 6291460
  0.0 13.9 %copy-start.1 = (s32[128,1]{0,1:T(1,128)S(1)}, s32[128,1]{0,1:T(1,128)}, u32[]{:S(2)}) copy-start(s32[128,1]{0,1:T(1,128)} %param.4) | copy-start | bytes 1540
  2.5 11.4 %collective-permute-start.3 = (bf16[128,1024]{1,0:T(8,128)(2,1)S(1)}, bf16[128,1024]{1,0:T(8,128)(2,1)S(1)}, u32[]{:S(2)}, u32[]{:S(2)}) collective-permute-start(bf16[128,1024]{1,0:T(8,128)(2,1)S(1)} %pad_maximum_fusion.3.refs_0_), channel_id=1, source_target_pairs={{0,4},{4,8},{8,12},{12,0},{1,5},{5,9},{9,13},{13,1},{2,6},{6,10},{... | collective-permute-start | bytes 786440 | tf_op jit(solution)/shard_map/ppermute | solution.py:32
  5.6 10.0 %collective-permute-start = (bf16[128,1024]{1,0:T(8,128)(2,1)S(1)}, bf16[128,1024]{1,0:T(8,128)(2,1)}, u32[]{:S(2)}, u32[]{:S(2)}) collective-permute-start(bf16[128,1024]{1,0:T(8,128)(2,1)S(1)} %pad_maximum_fusion), channel_id=1, source_target_pairs={{0,1},{1,0},{2,3},{3,2},{4,5},{5,4},{6,7},{7,6},{8,9},{9,8},{10,11... | collective-permute-start | bytes 786440 | tf_op jit(solution)/shard_map/ppermute | solution.py:28
  5.7 9.9 %collective-permute-start.1 = (bf16[128,1024]{1,0:T(8,128)(2,1)S(1)}, bf16[128,1024]{1,0:T(8,128)(2,1)S(1)}, u32[]{:S(2)}, u32[]{:S(2)}) collective-permute-start(bf16[128,1024]{1,0:T(8,128)(2,1)S(1)} %pad_maximum_fusion.1), channel_id=1, source_target_pairs={{0,2},{1,3},{2,0},{3,1},{4,6},{5,7},{6,4},{7,5},{8,10},{9,11},{10,... | collective-permute-start | bytes 786440 | tf_op jit(solution)/shard_map/ppermute | solution.py:28
  7.3 12.4 %collective-permute-start.2 = (bf16[128,1024]{1,0:T(8,128)(2,1)S(1)}, bf16[128,1024]{1,0:T(8,128)(2,1)S(1)}, u32[]{:S(2)}, u32[]{:S(2)}) collective-permute-start(bf16[128,1024]{1,0:T(8,128)(2,1)S(1)} %pad_maximum_fusion.2), channel_id=1, source_target_pairs={{0,3},{1,2},{2,1},{3,0},{4,7},{5,6},{6,5},{7,4},{8,11},{9,10},{10,... | collective-permute-start | bytes 786440 | tf_op jit(solution)/shard_map/ppermute | solution.py:28
  13.9 9.4 %collective-permute-start.4 = (bf16[128,1024]{1,0:T(8,128)(2,1)S(1)}, bf16[128,1024]{1,0:T(8,128)(2,1)}, u32[]{:S(2)}, u32[]{:S(2)}) collective-permute-start(bf16[128,1024]{1,0:T(8,128)(2,1)S(1)} %collective-permute-done.3.refs_3_), channel_id=1, source_target_pairs={{0,4},{4,8},{8,12},{12,0},{1,5},{5,9},{9,13},{13,1},{2,6},{6,10},{... | collective-permute-start | bytes 786440 | tf_op jit(solution)/shard_map/ppermute | solution.py:32
  23.3 48.3 %all-to-all-start = ((bf16[8,136,1024]{2,1,0:T(8,128)(2,1)}), bf16[8,136,1024]{2,1,0:T(8,128)(2,1)S(1)}, u32[]{:S(2)}, u32[]{:S(2)}) async-start(bf16[8,136,1024]{2,1,0:T(8,128)(2,1)} %outgoing_rows.1), calls=%async_computation | async-start | bytes 4456448 | tf_op jit(solution)/shard_map/all_to_all | solution.py:40
  28.2 10.5 %collective-permute-start.6 = (bf16[128,1024]{1,0:T(8,128)(2,1)S(1)}, bf16[128,1024]{1,0:T(8,128)(2,1)S(1)}, u32[]{:S(2)}, u32[]{:S(2)}) collective-permute-start(bf16[128,1024]{1,0:T(8,128)(2,1)S(1)} %pad_maximum_fusion.4.refs_2_), channel_id=1, source_target_pairs={{0,4},{4,8},{8,12},{12,0},{1,5},{5,9},{9,13},{13,1},{2,6},{6,10},{... | collective-permute-start | bytes 786440 | tf_op jit(solution)/shard_map/ppermute | solution.py:32
  38.7 12.6 %copy-start.2 = (bf16[128,1024]{1,0:T(8,128)(2,1)}, bf16[128,1024]{1,0:T(8,128)(2,1)S(1)}, u32[]{:S(2)}) copy-start(bf16[128,1024]{1,0:T(8,128)(2,1)S(1)} %collective-permute-done.6.refs_5_) | copy-start | bytes 786436
  38.7 11.1 %collective-permute-start.8 = (bf16[128,1024]{1,0:T(8,128)(2,1)S(1)}, bf16[128,1024]{1,0:T(8,128)(2,1)}, u32[]{:S(2)}, u32[]{:S(2)}) collective-permute-start(bf16[128,1024]{1,0:T(8,128)(2,1)S(1)} %collective-permute-done.6.refs_5_), channel_id=1, source_target_pairs={{0,4},{4,8},{8,12},{12,0},{1,5},{5,9},{9,13},{13,1},{2,6},{6,10},{... | collective-permute-start | bytes 786440 | tf_op jit(solution)/shard_map/ppermute | solution.py:32
  39.8 11.5 %collective-permute-start.5 = (bf16[64,1024]{1,0:T(8,128)(2,1)S(1)}, bf16[64,1024]{1,0:T(8,128)(2,1)}, u32[]{:S(2)}, u32[]{:S(2)}) collective-permute-start(bf16[64,1024]{1,0:T(8,128)(2,1)S(1)} %get-tuple-element.30.refs_1_), channel_id=1, source_target_pairs={{0,4},{4,8},{8,12},{12,0},{1,5},{5,9},{9,13},{13,1},{2,6},{6,10},{... | collective-permute-start | bytes 393224 | tf_op jit(solution)/shard_map/ppermute | solution.py:32
  49.9 14.1 %collective-permute-start.11 = (bf16[128,1024]{1,0:T(8,128)(2,1)}, bf16[128,1024]{1,0:T(8,128)(2,1)}, u32[]{:S(2)}, u32[]{:S(2)}) collective-permute-start(bf16[128,1024]{1,0:T(8,128)(2,1)} %collective-permute-done.8.refs_8_), channel_id=1, source_target_pairs={{0,4},{4,8},{8,12},{12,0},{1,5},{5,9},{9,13},{13,1},{2,6},{6,10},{... | collective-permute-start | bytes 786440 | tf_op jit(solution)/shard_map/ppermute | solution.py:32
  51.3 12.6 %collective-permute-start.7 = (bf16[64,1024]{1,0:T(8,128)(2,1)}, bf16[64,1024]{1,0:T(8,128)(2,1)}, u32[]{:S(2)}, u32[]{:S(2)}) collective-permute-start(bf16[64,1024]{1,0:T(8,128)(2,1)} %collective-permute-done.5.refs_4_), channel_id=1, source_target_pairs={{0,4},{4,8},{8,12},{12,0},{1,5},{5,9},{9,13},{13,1},{2,6},{6,10},{... | collective-permute-start | bytes 393224 | tf_op jit(solution)/shard_map/ppermute | solution.py:32
  51.3 20.3 %collective-permute-start.9 = (bf16[128,1024]{1,0:T(8,128)(2,1)}, bf16[128,1024]{1,0:T(8,128)(2,1)}, u32[]{:S(2)}, u32[]{:S(2)}) collective-permute-start(bf16[128,1024]{1,0:T(8,128)(2,1)} %collective-permute-done.4.refs_6_), channel_id=1, source_target_pairs={{0,4},{4,8},{8,12},{12,0},{1,5},{5,9},{9,13},{13,1},{2,6},{6,10},{... | collective-permute-start | bytes 786440 | tf_op jit(solution)/shard_map/ppermute | solution.py:32
  63.9 7.7 %collective-permute-start.10 = (bf16[64,1024]{1,0:T(8,128)(2,1)}, bf16[64,1024]{1,0:T(8,128)(2,1)}, u32[]{:S(2)}, u32[]{:S(2)}) collective-permute-start(bf16[64,1024]{1,0:T(8,128)(2,1)} %collective-permute-done.7.refs_7_), channel_id=1, source_target_pairs={{0,4},{4,8},{8,12},{12,0},{1,5},{5,9},{9,13},{13,1},{2,6},{6,10},{... | collective-permute-start | bytes 393224 | tf_op jit(solution)/shard_map/ppermute | solution.py:32
  63.9 14.2 %collective-permute-start.13 = (bf16[128,1024]{1,0:T(8,128)(2,1)S(1)}, bf16[128,1024]{1,0:T(8,128)(2,1)}, u32[]{:S(2)}, u32[]{:S(2)}) collective-permute-start(bf16[128,1024]{1,0:T(8,128)(2,1)S(1)} %pad_maximum_fusion.5.refs_2_), channel_id=1, source_target_pairs={{0,4},{4,8},{8,12},{12,0},{1,5},{5,9},{9,13},{13,1},{2,6},{6,10},{... | collective-permute-start | bytes 786440 | tf_op jit(solution)/shard_map/ppermute | solution.py:32
  71.6 1.0 copy-start.3
  77.3 0.8 copy-start.4
  78.1 11.0 %collective-permute-start.15 = (bf16[128,1024]{1,0:T(8,128)(2,1)}, bf16[128,1024]{1,0:T(8,128)(2,1)S(1)}, u32[]{:S(2)}, u32[]{:S(2)}) collective-permute-start(bf16[128,1024]{1,0:T(8,128)(2,1)} %collective-permute-done.13.refs_5_), channel_id=1, source_target_pairs={{0,4},{4,8},{8,12},{12,0},{1,5},{5,9},{9,13},{13,1},{2,6},{6,10},{... | collective-permute-start | bytes 786440 | tf_op jit(solution)/shard_map/ppermute | solution.py:32
  78.1 11.0 %collective-permute-start.12 = (bf16[64,1024]{1,0:T(8,128)(2,1)S(1)}, bf16[64,1024]{1,0:T(8,128)(2,1)S(1)}, u32[]{:S(2)}, u32[]{:S(2)}) collective-permute-start(bf16[64,1024]{1,0:T(8,128)(2,1)S(1)} %get-tuple-element.14.refs_1_), channel_id=1, source_target_pairs={{0,4},{4,8},{8,12},{12,0},{1,5},{5,9},{9,13},{13,1},{2,6},{6,10},{... | collective-permute-start | bytes 393224 | tf_op jit(solution)/shard_map/ppermute | solution.py:32
  78.1 18.3 %all-to-all-start.1 = ((f32[8,64,128]{2,1,0:T(8,128)}), f32[8,64,128]{2,1,0:T(8,128)S(1)}, u32[]{:S(2)}, u32[]{:S(2)}) async-start(f32[8,64,128]{2,1,0:T(8,128)} %get-tuple-element.13), calls=%async_computation.1 | async-start | bytes 524288 | tf_op jit(solution)/shard_map/all_to_all | solution.py:40
  89.1 7.3 %collective-permute-start.14 = (bf16[64,1024]{1,0:T(8,128)(2,1)S(1)}, bf16[64,1024]{1,0:T(8,128)(2,1)S(1)}, u32[]{:S(2)}, u32[]{:S(2)}) collective-permute-start(bf16[64,1024]{1,0:T(8,128)(2,1)S(1)} %collective-permute-done.12.refs_4_), channel_id=1, source_target_pairs={{0,4},{4,8},{8,12},{12,0},{1,5},{5,9},{9,13},{13,1},{2,6},{6,10},{... | collective-permute-start | bytes 393224 | tf_op jit(solution)/shard_map/ppermute | solution.py:32
  89.1 16.5 %collective-permute-start.17 = (bf16[128,1024]{1,0:T(8,128)(2,1)S(1)}, bf16[128,1024]{1,0:T(8,128)(2,1)S(1)}, u32[]{:S(2)}, u32[]{:S(2)}) collective-permute-start(bf16[128,1024]{1,0:T(8,128)(2,1)S(1)} %collective-permute-done.15.refs_8_), channel_id=1, source_target_pairs={{0,4},{4,8},{8,12},{12,0},{1,5},{5,9},{9,13},{13,1},{2,6},{6,10},{... | collective-permute-start | bytes 786440 | tf_op jit(solution)/shard_map/ppermute | solution.py:32
  96.4 6.8 %collective-permute-start.16 = (bf16[64,1024]{1,0:T(8,128)(2,1)S(1)}, bf16[64,1024]{1,0:T(8,128)(2,1)S(1)}, u32[]{:S(2)}, u32[]{:S(2)}) collective-permute-start(bf16[64,1024]{1,0:T(8,128)(2,1)S(1)} %collective-permute-done.14.refs_7_), channel_id=1, source_target_pairs={{0,4},{4,8},{8,12},{12,0},{1,5},{5,9},{9,13},{13,1},{2,6},{6,10},{... | collective-permute-start | bytes 393224 | tf_op jit(solution)/shard_map/ppermute | solution.py:32
  97.0 8.5 %all-to-all-start.2 = ((bf16[8,64,128]{2,1,0:T(8,128)(2,1)}), bf16[8,64,128]{2,1,0:T(8,128)(2,1)S(1)}, u32[]{:S(2)}, u32[]{:S(2)}) async-start(bf16[8,64,128]{2,1,0:T(8,128)(2,1)} %summed_copies.1), calls=%async_computation.2 | async-start | bytes 262144 | tf_op jit(solution)/shard_map/all_to_all | solution.py:40
  105.5 1.0 copy-start.5

commit v13 on v11

--- a/solution.py
+++ b/solution.py
@@ -46,6 +46,26 @@
     for n in range(1, per_tile):
         label = jnp.where(lane >= n * rank, labels_ref[tile * per_tile + n], label)
     return label.astype(jnp.float32)
+
+
+def join_kernel(*refs):
+    blocks, out_ref = refs[:-1], refs[-1]
+    rows = blocks[0].shape[0]
+    for n, block in enumerate(blocks):
+        out_ref[n * rows : (n + 1) * rows, :] = block[...]
+
+
+def joined(blocks):
+    rows, share = blocks[0].shape
+    return pl.pallas_call(
+        join_kernel,
+        out_shape=jax.ShapeDtypeStruct((len(blocks) * rows, share), jnp.bfloat16),
+        in_specs=[IN_VMEM] * len(blocks),
+        out_specs=IN_VMEM,
+        compiler_params=params(),
+        cost_estimate=pl.CostEstimate(flops=10**11, bytes_accessed=10**9, transcendentals=0),
+        name="join_blocks",
+    )(*blocks)
 
 
 def outgoing_kernel(hidden_ref, ids_ref, out_ref, sems):
@@ -74,7 +94,7 @@
     return pl.pallas_call(
         outgoing_kernel,
         out_shape=jax.ShapeDtypeStruct((members, tok + ID_ROWS, share), jnp.bfloat16),
-        in_specs=[IN_HBM, IN_VMEM],
+        in_specs=[ANYWHERE, IN_VMEM],
         out_specs=IN_VMEM,
         scratch_shapes=[pltpu.SemaphoreType.DMA((members,))],
         compiler_params=params(),
@@ -267,9 +287,8 @@
     def exchanged(blocks):
         return blocks[:1] + [to_partner(blocks[n], "inner", inner, n) for n in range(1, inner)]
 
-    def rings(blocks, near_after=(), far_after=(), second_after=()):
-        near = [after(jnp.concatenate(blocks[: inner // 2], axis=0), *near_after)]
-        far = [after(jnp.concatenate(blocks[inner // 2 :], axis=0), *far_after)]
+    def rings(near, far, second_after=()):
+        near, far = [near], [far]
         for step in range(1, outer):
             near.append(next_on_ring(after(near[-1], *second_after) if step == 2 else near[-1], outer))
             far.append(next_on_ring(far[-1], outer))
@@ -281,15 +300,20 @@
     )
     labels = labels.reshape(-1)
 
+    middle = inner // 2
     down = exchanged(slices(adapter_down_maps[0].T))
-    down_near, down_far = rings(down)
+    down_near, down_far = rings(joined(down[:middle]), joined(down[middle:]))
     ids = token_adapter_index.reshape(1, tok)
-    rows = swap(after(outgoing_rows(hidden, ids, members), down[1]))
+    rows = swap(after(outgoing_rows(hidden, ids, members), down_near[0]))
     up = exchanged([after(block, down_near[1]) for block in slices(adapter_up_maps[0])])
 
     down_maps = [m for pair in zip(down_near, down_far) for m in pair]
     packed, id_columns = down_product(labels, rows, down_maps, rank)
-    up_near, up_far = rings(up, [down_near[-1]], [down_far[-1]], second_after=[packed])
+    up_near, up_far = rings(
+        after(jnp.concatenate(up[:middle], axis=0), down_near[-1]),
+        after(jnp.concatenate(up[middle:], axis=0), down_far[-1]),
+        second_after=[packed],
+    )
     up_maps = [m for pair in zip(up_near, up_far) for m in pair]
     shrunk = swap(summed_copies(swap(packed)))
     return place([swap(up_product(labels, id_columns, shrunk, up_maps, rank))])

time: 154 us -> 124 us (0.81)
  waiting for transfers between devices: 75.3 us -> 44.9 us
  starting transfers between devices: 22.7 us -> 24.5 us
    ppermute x6, waiting for transfers between devices: 33.6 us -> 4.86 us  [to_partner(): return lax.ppermute(value, axes, [(i, i ^ offset) for i in range(size)])]
    ppermute x12, starting transfers between devices: 6.05 us -> 7.83 us  [next_on_ring(): lax.ppermute(block, 'outer', [(i, (i + 1) % outer) for i in range(outer)])]
    ppermute x12, waiting for transfers between devices: 35.6 us -> 33.8 us  [next_on_ring(): lax.ppermute(block, 'outer', [(i, (i + 1) % outer) for i in range(outer)])]
    unnamed x20 -> x22, local copies, waits for them, and re-layouts: 7.63 us -> 7.64 us
  transfers between devices with their start and end apart: 21 -> 21, of which waited for: 16 -> 13; matrix products, arithmetic and copies ran while one was open for 3% -> 2% of each run, Pallas kernels for 4% -> 6%
where the time goes in v13:
time: 124 us; the launch traced here: 123 us
  waiting for transfers between devices  44.9 us (36%)
  blocking collectives  29.6 us (24%)
  starting transfers between devices  24.5 us (20%)
  Pallas kernels  12.3 us (10%)
  local copies, waits for them, and re-layouts  9.75 us (8%)
  other arithmetic  1.99 us (2%)
    ppermute x12, waiting for transfers between devices, next_on_ring(): lax.ppermute(block, 'outer', [(i, (i + 1) % outer) for i in range(outer)])  33.8 us
    all_to_all x1, blocking collectives, swap(): return lax.all_to_all(value, PLANE, split_axis=0, concat_axis=0, tiled=True)  29.6 us
    all_to_all x3, starting transfers between devices, swap(): return lax.all_to_all(value, PLANE, split_axis=0, concat_axis=0, tiled=True)  11.3 us
    ppermute x12, starting transfers between devices, next_on_ring(): lax.ppermute(block, 'outer', [(i, (i + 1) % outer) for i in range(outer)])  7.83 us
    unnamed x22, local copies, waits for them, and re-layouts  7.64 us
    all_to_all x3, waiting for transfers between devices, swap(): return lax.all_to_all(value, PLANE, split_axis=0, concat_axis=0, tiled=True)  6.21 us
    ppermute x6, starting transfers between devices, to_partner(): return lax.ppermute(value, axes, [(i, i ^ offset) for i in range(size)])  5.36 us
    ppermute x6, waiting for transfers between devices, to_partner(): return lax.ppermute(value, axes, [(i, i ^ offset) for i in range(size)])  4.86 us
  transfers between devices with their start and end apart: 21, of which 13 were waited for; matrix products, arithmetic and copies ran while one was open for 2% of the time, Pallas kernels for 6%

profile of v13, /device:TPU:0, one launch (start us, length us, event | category | flops | bytes accessed | tf_op | source)
XLA Modules:
  0.0 123.3 jit_solution(16524794948250922048)
XLA Ops:
  0.0 1.1 dynamic-slice_bitcast_fusion.4
  1.7 2.6 %collective-permute-start.1 = (bf16[64,1024]{1,0:T(8,128)(2,1)S(1)}, bf16[64,1024]{1,0:T(8,128)(2,1)S(1)}, u32[]{:S(2)}, u32[]{:S(2)}) collective-permute-start(bf16[64,1024]{1,0:T(8,128)(2,1)S(1)} %get-tuple-element.32), channel_id=1, source_target_pairs={{0,2},{1,3},{2,0},{3,1},{4,6},{5,7},{6,4},{7,5},{8,10},{9,11},{10,... | collective-permute-start | bytes 393224 | tf_op jit(solution)/shard_map/ppermute | solution.py:27
  4.3 1.6 %copy-done = bf16[128,8192]{1,0:T(8,128)(2,1)S(1)} copy-done((bf16[128,8192]{1,0:T(8,128)(2,1)S(1)}, bf16[128,8192]{1,0:T(8,128)(2,1)}, u32[]{:S(2)}) %copy-start) | copy-done | bytes 2097176
  6.6 1.6 %outgoing_rows.1 = bf16[8,136,1024]{2,1,0:T(8,128)(2,1)} custom-call(bf16[128,8192]{1,0:T(8,128)(2,1)S(1)} %copy-done, s32[1,128]{1,0:T(1,128)S(1)} %bitcast.25), custom_call_target="tpu_custom_call" | custom-call | tf_op jit(solution)/shard_map/outgoing_rows/pallas_call | solution.py:94
  8.2 3.9 %all-to-all-start = ((bf16[8,136,1024]{2,1,0:T(8,128)(2,1)}), bf16[8,136,1024]{2,1,0:T(8,128)(2,1)S(1)}, u32[]{:S(2)}, u32[]{:S(2)}) async-start(bf16[8,136,1024]{2,1,0:T(8,128)(2,1)} %outgoing_rows.1), calls=%async_computation | async-start | bytes 4456448 | tf_op jit(solution)/shard_map/all_to_all | solution.py:39
  12.2 1.6 %collective-permute-start.4 = (bf16[128,1024]{1,0:T(8,128)(2,1)S(1)}, bf16[128,1024]{1,0:T(8,128)(2,1)S(1)}, u32[]{:S(2)}, u32[]{:S(2)}) collective-permute-start(bf16[128,1024]{1,0:T(8,128)(2,1)S(1)} %join_blocks.3.refs_1_), channel_id=1, source_target_pairs={{0,4},{4,8},{8,12},{12,0},{1,5},{5,9},{9,13},{13,1},{2,6},{6,10},{... | collective-permute-start | bytes 786440 | tf_op jit(solution)/shard_map/ppermute | solution.py:31
  13.9 1.6 %collective-permute-start.3 = (bf16[128,1024]{1,0:T(8,128)(2,1)S(1)}, bf16[128,1024]{1,0:T(8,128)(2,1)S(1)}, u32[]{:S(2)}, u32[]{:S(2)}) collective-permute-start(bf16[128,1024]{1,0:T(8,128)(2,1)S(1)} %join_blocks.2.refs_0_), channel_id=1, source_target_pairs={{0,4},{4,8},{8,12},{12,0},{1,5},{5,9},{9,13},{13,1},{2,6},{6,10},{... | collective-permute-start | bytes 786440 | tf_op jit(solution)/shard_map/ppermute | solution.py:31
  15.4 7.7 %collective-permute-done.4.refs_3_ = bf16[128,1024]{1,0:T(8,128)(2,1)S(1)} collective-permute-done((bf16[128,1024]{1,0:T(8,128)(2,1)S(1)}, bf16[128,1024]{1,0:T(8,128)(2,1)S(1)}, u32[]{:S(2)}, u32[]{:S(2)}) %collective-permute-start.4) | collective-permute-done | bytes 262176 | tf_op jit(solution)/shard_map/ppermute | solution.py:31
  23.2 5.6 %collective-permute-done.3.refs_2_ = bf16[128,1024]{1,0:T(8,128)(2,1)S(1)} collective-permute-done((bf16[128,1024]{1,0:T(8,128)(2,1)S(1)}, bf16[128,1024]{1,0:T(8,128)(2,1)S(1)}, u32[]{:S(2)}, u32[]{:S(2)}) %collective-permute-start.3) | collective-permute-done | bytes 262176 | tf_op jit(solution)/shard_map/ppermute | solution.py:31
  28.8 5.6 %collective-permute-done.6.refs_5_ = bf16[128,1024]{1,0:T(8,128)(2,1)S(1)} collective-permute-done((bf16[128,1024]{1,0:T(8,128)(2,1)S(1)}, bf16[128,1024]{1,0:T(8,128)(2,1)S(1)}, u32[]{:S(2)}, u32[]{:S(2)}) %collective-permute-start.6) | collective-permute-done | bytes 262176 | tf_op jit(solution)/shard_map/ppermute | solution.py:31
  35.7 1.8 %collective-permute-start.10 = (bf16[64,1024]{1,0:T(8,128)(2,1)}, bf16[64,1024]{1,0:T(8,128)(2,1)}, u32[]{:S(2)}, u32[]{:S(2)}) collective-permute-start(bf16[64,1024]{1,0:T(8,128)(2,1)} %get-tuple-element.21), channel_id=1, source_target_pairs={{0,2},{1,3},{2,0},{3,1},{4,6},{5,7},{6,4},{7,5},{8,10},{9,11},{10,... | collective-permute-start | bytes 393224 | tf_op jit(solution)/shard_map/ppermute | solution.py:27
  37.5 2.6 %collective-permute-done.5.refs_4_ = bf16[128,1024]{1,0:T(8,128)(2,1)} collective-permute-done((bf16[128,1024]{1,0:T(8,128)(2,1)S(1)}, bf16[128,1024]{1,0:T(8,128)(2,1)}, u32[]{:S(2)}, u32[]{:S(2)}) %collective-permute-start.5) | collective-permute-done | bytes 262176 | tf_op jit(solution)/shard_map/ppermute | solution.py:31
  40.2 1.6 %collective-permute-done.11 = bf16[64,1024]{1,0:T(8,128)(2,1)} collective-permute-done((bf16[64,1024]{1,0:T(8,128)(2,1)}, bf16[64,1024]{1,0:T(8,128)(2,1)}, u32[]{:S(2)}, u32[]{:S(2)}) %collective-permute-start.11) | collective-permute-done | bytes 131104 | tf_op jit(solution)/shard_map/ppermute | solution.py:27
  41.7 3.3 %collective-permute-done.10 = bf16[64,1024]{1,0:T(8,128)(2,1)} collective-permute-done((bf16[64,1024]{1,0:T(8,128)(2,1)}, bf16[64,1024]{1,0:T(8,128)(2,1)}, u32[]{:S(2)}, u32[]{:S(2)}) %collective-permute-start.10) | collective-permute-done | bytes 131104 | tf_op jit(solution)/shard_map/ppermute | solution.py:27
  45.0 1.0 pad_maximum_fusion.1.refs_1_
  46.0 1.6 %collective-permute-start.13 = (bf16[128,1024]{1,0:T(8,128)(2,1)S(1)}, bf16[128,1024]{1,0:T(8,128)(2,1)}, u32[]{:S(2)}, u32[]{:S(2)}) collective-permute-start(bf16[128,1024]{1,0:T(8,128)(2,1)S(1)} %pad_maximum_fusion.1.refs_1_), channel_id=1, source_target_pairs={{0,4},{4,8},{8,12},{12,0},{1,5},{5,9},{9,13},{13,1},{2,6},{6,10},{... | collective-permute-start | bytes 786440 | tf_op jit(solution)/shard_map/ppermute | solution.py:31
  48.6 2.8 %collective-permute-done.7.refs_6_ = bf16[128,1024]{1,0:T(8,128)(2,1)S(1)} collective-permute-done((bf16[128,1024]{1,0:T(8,128)(2,1)}, bf16[128,1024]{1,0:T(8,128)(2,1)S(1)}, u32[]{:S(2)}, u32[]{:S(2)}) %collective-permute-start.7) | collective-permute-done | bytes 262176 | tf_op jit(solution)/shard_map/ppermute | solution.py:31
  52.3 4.9 %collective-permute-done.13.refs_3_ = bf16[128,1024]{1,0:T(8,128)(2,1)} collective-permute-done((bf16[128,1024]{1,0:T(8,128)(2,1)S(1)}, bf16[128,1024]{1,0:T(8,128)(2,1)}, u32[]{:S(2)}, u32[]{:S(2)}) %collective-permute-start.13) | collective-permute-done | bytes 262176 | tf_op jit(solution)/shard_map/ppermute | solution.py:31
  60.1 4.5 %down_product.1 = (f32[8,64,128]{2,1,0:T(8,128)}, f32[8,128,128]{2,1,0:T(8,128)S(1)}) custom-call(s32[16]{0:T(128)S(1)} %add.60.labels_ref, bf16[8,136,1024]{2,1,0:T(8,128)(2,1)S(1)} %all-to-all-done.rows_ref, bf16[128,1024]{1,0:T(8,128)(2,1)S(1)} %join_blocks.2.refs_0_, bf16[128,1024]{1,0:T(8,128)(2,1)S(1)} %join_blocks.3.refs_1_, ...), custom_call_target="tpu_custom_call" | custom-call | flops 2147483648 | bytes 4194304 | tf_op jit(solution)/shard_map/down_product/pallas_call | solution.py:149
  65.3 1.3 %collective-permute-start.14 = (bf16[128,1024]{1,0:T(8,128)(2,1)}, bf16[128,1024]{1,0:T(8,128)(2,1)S(1)}, u32[]{:S(2)}, u32[]{:S(2)}) collective-permute-start(bf16[128,1024]{1,0:T(8,128)(2,1)} %collective-permute-done.12.refs_2_), channel_id=1, source_target_pairs={{0,4},{4,8},{8,12},{12,0},{1,5},{5,9},{9,13},{13,1},{2,6},{6,10},{... | collective-permute-start | bytes 786440 | tf_op jit(solution)/shard_map/ppermute | solution.py:31
  66.7 4.0 %all-to-all-start.1 = ((f32[8,64,128]{2,1,0:T(8,128)}), f32[8,64,128]{2,1,0:T(8,128)S(1)}, u32[]{:S(2)}, u32[]{:S(2)}) async-start(f32[8,64,128]{2,1,0:T(8,128)} %get-tuple-element.17), calls=%async_computation.1 | async-start | bytes 524288 | tf_op jit(solution)/shard_map/all_to_all | solution.py:39
  70.7 1.6 %collective-permute-start.17 = (bf16[128,1024]{1,0:T(8,128)(2,1)}, bf16[128,1024]{1,0:T(8,128)(2,1)S(1)}, u32[]{:S(2)}, u32[]{:S(2)}) collective-permute-start(bf16[128,1024]{1,0:T(8,128)(2,1)} %collective-permute-done.15.refs_5_), channel_id=1, source_target_pairs={{0,4},{4,8},{8,12},{12,0},{1,5},{5,9},{9,13},{13,1},{2,6},{6,10},{... | collective-permute-start | bytes 786440 | tf_op jit(solution)/shard_map/ppermute | solution.py:31
  72.4 2.2 %collective-permute-done.14.refs_4_ = bf16[128,1024]{1,0:T(8,128)(2,1)S(1)} collective-permute-done((bf16[128,1024]{1,0:T(8,128)(2,1)}, bf16[128,1024]{1,0:T(8,128)(2,1)S(1)}, u32[]{:S(2)}, u32[]{:S(2)}) %collective-permute-start.14) | collective-permute-done | bytes 262176 | tf_op jit(solution)/shard_map/ppermute | solution.py:31
  74.6 2.2 %all-to-all-done.1.terms_ref = f32[8,64,128]{2,1,0:T(8,128)S(1)} async-done(((f32[8,64,128]{2,1,0:T(8,128)}), f32[8,64,128]{2,1,0:T(8,128)S(1)}, u32[]{:S(2)}, u32[]{:S(2)}) %all-to-all-start.1) | async-done | bytes 262176 | tf_op jit(solution)/shard_map/all_to_all | solution.py:39
  77.4 3.4 %all-to-all-start.2 = ((bf16[8,64,128]{2,1,0:T(8,128)(2,1)}), bf16[8,64,128]{2,1,0:T(8,128)(2,1)S(1)}, u32[]{:S(2)}, u32[]{:S(2)}) async-start(bf16[8,64,128]{2,1,0:T(8,128)(2,1)} %summed_copies.1), calls=%async_computation.2 | async-start | bytes 262144 | tf_op jit(solution)/shard_map/all_to_all | solution.py:39
  80.8 1.1 collective-permute-done.17.refs_7_
  81.9 4.0 %all-to-all-done.2.shrunk_ref = bf16[8,64,128]{2,1,0:T(8,128)(2,1)S(1)} async-done(((bf16[8,64,128]{2,1,0:T(8,128)(2,1)}), bf16[8,64,128]{2,1,0:T(8,128)(2,1)S(1)}, u32[]{:S(2)}, u32[]{:S(2)}) %all-to-all-start.2) | async-done | bytes 131104 | tf_op jit(solution)/shard_map/all_to_all | solution.py:39
  85.9 1.1 collective-permute-done.16.refs_6_
  87.1 1.0 copy-done.9
  88.1 4.1 %up_product.1 = bf16[8,128,1024]{2,1,0:T(8,128)(2,1)S(1)} custom-call(s32[16]{0:T(128)S(1)} %add.60.labels_ref, f32[8,128,128]{2,1,0:T(8,128)S(1)} %copy-done.9, bf16[8,64,128]{2,1,0:T(8,128)(2,1)S(1)} %all-to-all-done.2.shrunk_ref, bf16[128,1024]{1,0:T(8,128)(2,1)S(1)} %pad_maximum_fusion.refs_0_, bf16[128,1024]{1,0:T(8,128)(2,1)S(1)} %pad_maximum_fusion.1.refs_1_, ...), custom_call_target="tpu_custom_call" | custom-call | flops 2147483648 | bytes 4194304 | tf_op jit(solution)/shard_map/up_product/pallas_call | solution.py:226
  92.3 29.6 %all_to_all.20.refs_0_ = bf16[8,128,1024]{2,1,0:T(8,128)(2,1)S(1)} all-to-all(bf16[8,128,1024]{2,1,0:T(8,128)(2,1)S(1)} %up_product.1), channel_id=1, replica_groups=mesh['groups'=2,'outer'=4,'inner'=4] {'groups','inner'}, dimensions={0} | all-to-all | bytes 4194304 | tf_op jit(solution)/shard_map/all_to_all | solution.py:39
  121.9 1.4 %place_results.1 = bf16[128,8192]{1,0:T(8,128)(2,1)} custom-call(bf16[8,128,1024]{2,1,0:T(8,128)(2,1)S(1)} %all_to_all.20.refs_0_), custom_call_target="tpu_custom_call" | custom-call | tf_op jit(solution)/shard_map/place_results/pallas_call | solution.py:262
  (47 shorter events, 8.7 us)
Async XLA Ops:
  1.1 7.1 %collective-permute-start = (bf16[64,1024]{1,0:T(8,128)(2,1)S(1)}, bf16[64,1024]{1,0:T(8,128)(2,1)S(1)}, u32[]{:S(2)}, u32[]{:S(2)}) collective-permute-start(bf16[64,1024]{1,0:T(8,128)(2,1)S(1)} %get-tuple-element.30), channel_id=1, source_target_pairs={{0,1},{1,0},{2,3},{3,2},{4,5},{5,4},{6,7},{7,6},{8,9},{9,8},{10,11... | collective-permute-start | bytes 393224 | tf_op jit(solution)/shard_map/ppermute | solution.py:27
  1.7 10.5 %collective-permute-start.1 = (bf16[64,1024]{1,0:T(8,128)(2,1)S(1)}, bf16[64,1024]{1,0:T(8,128)(2,1)S(1)}, u32[]{:S(2)}, u32[]{:S(2)}) collective-permute-start(bf16[64,1024]{1,0:T(8,128)(2,1)S(1)} %get-tuple-element.32), channel_id=1, source_target_pairs={{0,2},{1,3},{2,0},{3,1},{4,6},{5,7},{6,4},{7,5},{8,10},{9,11},{10,... | collective-permute-start | bytes 393224 | tf_op jit(solution)/shard_map/ppermute | solution.py:27
  4.3 7.9 %collective-permute-start.2 = (bf16[64,1024]{1,0:T(8,128)(2,1)S(1)}, bf16[64,1024]{1,0:T(8,128)(2,1)S(1)}, u32[]{:S(2)}, u32[]{:S(2)}) collective-permute-start(bf16[64,1024]{1,0:T(8,128)(2,1)S(1)} %get-tuple-element.29), channel_id=1, source_target_pairs={{0,3},{1,2},{2,1},{3,0},{4,7},{5,6},{6,5},{7,4},{8,11},{9,10},{10,... | collective-permute-start | bytes 393224 | tf_op jit(solution)/shard_map/ppermute | solution.py:27
  4.3 1.6 %copy-start = (bf16[128,8192]{1,0:T(8,128)(2,1)S(1)}, bf16[128,8192]{1,0:T(8,128)(2,1)}, u32[]{:S(2)}) copy-start(bf16[128,8192]{1,0:T(8,128)(2,1)} %hidden_ref.1) | copy-start | bytes 6291460
  5.9 0.7 copy-start.1
  8.2 49.0 %all-to-all-start = ((bf16[8,136,1024]{2,1,0:T(8,128)(2,1)}), bf16[8,136,1024]{2,1,0:T(8,128)(2,1)S(1)}, u32[]{:S(2)}, u32[]{:S(2)}) async-start(bf16[8,136,1024]{2,1,0:T(8,128)(2,1)} %outgoing_rows.1), calls=%async_computation | async-start | bytes 4456448 | tf_op jit(solution)/shard_map/all_to_all | solution.py:39
  12.2 22.2 %copy-start.10 = (bf16[1,64,8192]{2,1,0:T(8,128)(2,1)S(1)}, bf16[1,64,8192]{2,1,0:T(8,128)(2,1)}, u32[]{:S(2)}) copy-start(bf16[1,64,8192]{2,1,0:T(8,128)(2,1)} %param.7) | copy-start | bytes 3145732
  12.2 10.9 %collective-permute-start.4 = (bf16[128,1024]{1,0:T(8,128)(2,1)S(1)}, bf16[128,1024]{1,0:T(8,128)(2,1)S(1)}, u32[]{:S(2)}, u32[]{:S(2)}) collective-permute-start(bf16[128,1024]{1,0:T(8,128)(2,1)S(1)} %join_blocks.3.refs_1_), channel_id=1, source_target_pairs={{0,4},{4,8},{8,12},{12,0},{1,5},{5,9},{9,13},{13,1},{2,6},{6,10},{... | collective-permute-start | bytes 786440 | tf_op jit(solution)/shard_map/ppermute | solution.py:31
  13.9 14.9 %collective-permute-start.3 = (bf16[128,1024]{1,0:T(8,128)(2,1)S(1)}, bf16[128,1024]{1,0:T(8,128)(2,1)S(1)}, u32[]{:S(2)}, u32[]{:S(2)}) collective-permute-start(bf16[128,1024]{1,0:T(8,128)(2,1)S(1)} %join_blocks.2.refs_0_), channel_id=1, source_target_pairs={{0,4},{4,8},{8,12},{12,0},{1,5},{5,9},{9,13},{13,1},{2,6},{6,10},{... | collective-permute-start | bytes 786440 | tf_op jit(solution)/shard_map/ppermute | solution.py:31
  23.2 11.2 %collective-permute-start.6 = (bf16[128,1024]{1,0:T(8,128)(2,1)S(1)}, bf16[128,1024]{1,0:T(8,128)(2,1)S(1)}, u32[]{:S(2)}, u32[]{:S(2)}) collective-permute-start(bf16[128,1024]{1,0:T(8,128)(2,1)S(1)} %collective-permute-done.4.refs_3_), channel_id=1, source_target_pairs={{0,4},{4,8},{8,12},{12,0},{1,5},{5,9},{9,13},{13,1},{2,6},{6,10},{... | collective-permute-start | bytes 786440 | tf_op jit(solution)/shard_map/ppermute | solution.py:31
  28.8 12.9 %copy-start.2 = (bf16[128,1024]{1,0:T(8,128)(2,1)}, bf16[128,1024]{1,0:T(8,128)(2,1)S(1)}, u32[]{:S(2)}) copy-start(bf16[128,1024]{1,0:T(8,128)(2,1)S(1)} %collective-permute-done.3.refs_2_) | copy-start | bytes 786436
  28.8 11.3 %collective-permute-start.5 = (bf16[128,1024]{1,0:T(8,128)(2,1)S(1)}, bf16[128,1024]{1,0:T(8,128)(2,1)}, u32[]{:S(2)}, u32[]{:S(2)}) collective-permute-start(bf16[128,1024]{1,0:T(8,128)(2,1)S(1)} %collective-permute-done.3.refs_2_), channel_id=1, source_target_pairs={{0,4},{4,8},{8,12},{12,0},{1,5},{5,9},{9,13},{13,1},{2,6},{6,10},{... | collective-permute-start | bytes 786440 | tf_op jit(solution)/shard_map/ppermute | solution.py:31
  34.4 13.2 %copy-start.4 = (bf16[128,1024]{1,0:T(8,128)(2,1)}, bf16[128,1024]{1,0:T(8,128)(2,1)S(1)}, u32[]{:S(2)}) copy-start(bf16[128,1024]{1,0:T(8,128)(2,1)S(1)} %collective-permute-done.6.refs_5_) | copy-start | bytes 786436
  34.4 11.6 %collective-permute-start.8 = (bf16[128,1024]{1,0:T(8,128)(2,1)S(1)}, bf16[128,1024]{1,0:T(8,128)(2,1)}, u32[]{:S(2)}, u32[]{:S(2)}) collective-permute-start(bf16[128,1024]{1,0:T(8,128)(2,1)S(1)} %collective-permute-done.6.refs_5_), channel_id=1, source_target_pairs={{0,4},{4,8},{8,12},{12,0},{1,5},{5,9},{9,13},{13,1},{2,6},{6,10},{... | collective-permute-start | bytes 786440 | tf_op jit(solution)/shard_map/ppermute | solution.py:31
  35.3 6.4 %collective-permute-start.11 = (bf16[64,1024]{1,0:T(8,128)(2,1)}, bf16[64,1024]{1,0:T(8,128)(2,1)}, u32[]{:S(2)}, u32[]{:S(2)}) collective-permute-start(bf16[64,1024]{1,0:T(8,128)(2,1)} %get-tuple-element.22), channel_id=1, source_target_pairs={{0,3},{1,2},{2,1},{3,0},{4,7},{5,6},{6,5},{7,4},{8,11},{9,10},{10,... | collective-permute-start | bytes 393224 | tf_op jit(solution)/shard_map/ppermute | solution.py:27
  35.7 9.4 %collective-permute-start.10 = (bf16[64,1024]{1,0:T(8,128)(2,1)}, bf16[64,1024]{1,0:T(8,128)(2,1)}, u32[]{:S(2)}, u32[]{:S(2)}) collective-permute-start(bf16[64,1024]{1,0:T(8,128)(2,1)} %get-tuple-element.21), channel_id=1, source_target_pairs={{0,2},{1,3},{2,0},{3,1},{4,6},{5,7},{6,4},{7,5},{8,10},{9,11},{10,... | collective-permute-start | bytes 393224 | tf_op jit(solution)/shard_map/ppermute | solution.py:27
  37.4 10.2 %collective-permute-start.9 = (bf16[64,1024]{1,0:T(8,128)(2,1)}, bf16[64,1024]{1,0:T(8,128)(2,1)S(1)}, u32[]{:S(2)}, u32[]{:S(2)}) collective-permute-start(bf16[64,1024]{1,0:T(8,128)(2,1)} %get-tuple-element.19), channel_id=1, source_target_pairs={{0,1},{1,0},{2,3},{3,2},{4,5},{5,4},{6,7},{7,6},{8,9},{9,8},{10,11... | collective-permute-start | bytes 393224 | tf_op jit(solution)/shard_map/ppermute | solution.py:27
  40.1 11.2 %collective-permute-start.7 = (bf16[128,1024]{1,0:T(8,128)(2,1)}, bf16[128,1024]{1,0:T(8,128)(2,1)S(1)}, u32[]{:S(2)}, u32[]{:S(2)}) collective-permute-start(bf16[128,1024]{1,0:T(8,128)(2,1)} %collective-permute-done.5.refs_4_), channel_id=1, source_target_pairs={{0,4},{4,8},{8,12},{12,0},{1,5},{5,9},{9,13},{13,1},{2,6},{6,10},{... | collective-permute-start | bytes 786440 | tf_op jit(solution)/shard_map/ppermute | solution.py:31
  46.0 11.2 %collective-permute-start.13 = (bf16[128,1024]{1,0:T(8,128)(2,1)S(1)}, bf16[128,1024]{1,0:T(8,128)(2,1)}, u32[]{:S(2)}, u32[]{:S(2)}) collective-permute-start(bf16[128,1024]{1,0:T(8,128)(2,1)S(1)} %pad_maximum_fusion.1.refs_1_), channel_id=1, source_target_pairs={{0,4},{4,8},{8,12},{12,0},{1,5},{5,9},{9,13},{13,1},{2,6},{6,10},{... | collective-permute-start | bytes 786440 | tf_op jit(solution)/shard_map/ppermute | solution.py:31
  51.4 0.7 copy-start.6
  52.1 13.2 %collective-permute-start.12 = (bf16[128,1024]{1,0:T(8,128)(2,1)S(1)}, bf16[128,1024]{1,0:T(8,128)(2,1)}, u32[]{:S(2)}, u32[]{:S(2)}) collective-permute-start(bf16[128,1024]{1,0:T(8,128)(2,1)S(1)} %pad_maximum_fusion.refs_0_), channel_id=1, source_target_pairs={{0,4},{4,8},{8,12},{12,0},{1,5},{5,9},{9,13},{13,1},{2,6},{6,10},{... | collective-permute-start | bytes 786440 | tf_op jit(solution)/shard_map/ppermute | solution.py:31
  57.2 13.5 %collective-permute-start.15 = (bf16[128,1024]{1,0:T(8,128)(2,1)}, bf16[128,1024]{1,0:T(8,128)(2,1)}, u32[]{:S(2)}, u32[]{:S(2)}) collective-permute-start(bf16[128,1024]{1,0:T(8,128)(2,1)} %collective-permute-done.13.refs_3_), channel_id=1, source_target_pairs={{0,4},{4,8},{8,12},{12,0},{1,5},{5,9},{9,13},{13,1},{2,6},{6,10},{... | collective-permute-start | bytes 786440 | tf_op jit(solution)/shard_map/ppermute | solution.py:31
  57.2 1.0 copy-start.3
  58.2 0.9 copy-start.5
  59.1 0.9 copy-start.7
  64.5 0.8 copy-start.8
  65.3 9.3 %collective-permute-start.14 = (bf16[128,1024]{1,0:T(8,128)(2,1)}, bf16[128,1024]{1,0:T(8,128)(2,1)S(1)}, u32[]{:S(2)}, u32[]{:S(2)}) collective-permute-start(bf16[128,1024]{1,0:T(8,128)(2,1)} %collective-permute-done.12.refs_2_), channel_id=1, source_target_pairs={{0,4},{4,8},{8,12},{12,0},{1,5},{5,9},{9,13},{13,1},{2,6},{6,10},{... | collective-permute-start | bytes 786440 | tf_op jit(solution)/shard_map/ppermute | solution.py:31
  66.7 10.1 %all-to-all-start.1 = ((f32[8,64,128]{2,1,0:T(8,128)}), f32[8,64,128]{2,1,0:T(8,128)S(1)}, u32[]{:S(2)}, u32[]{:S(2)}) async-start(f32[8,64,128]{2,1,0:T(8,128)} %get-tuple-element.17), calls=%async_computation.1 | async-start | bytes 524288 | tf_op jit(solution)/shard_map/all_to_all | solution.py:39
  70.7 11.2 %collective-permute-start.17 = (bf16[128,1024]{1,0:T(8,128)(2,1)}, bf16[128,1024]{1,0:T(8,128)(2,1)S(1)}, u32[]{:S(2)}, u32[]{:S(2)}) collective-permute-start(bf16[128,1024]{1,0:T(8,128)(2,1)} %collective-permute-done.15.refs_5_), channel_id=1, source_target_pairs={{0,4},{4,8},{8,12},{12,0},{1,5},{5,9},{9,13},{13,1},{2,6},{6,10},{... | collective-permute-start | bytes 786440 | tf_op jit(solution)/shard_map/ppermute | solution.py:31
  74.6 12.5 %collective-permute-start.16 = (bf16[128,1024]{1,0:T(8,128)(2,1)S(1)}, bf16[128,1024]{1,0:T(8,128)(2,1)S(1)}, u32[]{:S(2)}, u32[]{:S(2)}) collective-permute-start(bf16[128,1024]{1,0:T(8,128)(2,1)S(1)} %collective-permute-done.14.refs_4_), channel_id=1, source_target_pairs={{0,4},{4,8},{8,12},{12,0},{1,5},{5,9},{9,13},{13,1},{2,6},{6,10},{... | collective-permute-start | bytes 786440 | tf_op jit(solution)/shard_map/ppermute | solution.py:31
  77.4 8.5 %all-to-all-start.2 = ((bf16[8,64,128]{2,1,0:T(8,128)(2,1)}), bf16[8,64,128]{2,1,0:T(8,128)(2,1)S(1)}, u32[]{:S(2)}, u32[]{:S(2)}) async-start(bf16[8,64,128]{2,1,0:T(8,128)(2,1)} %summed_copies.1), calls=%async_computation.2 | async-start | bytes 262144 | tf_op jit(solution)/shard_map/all_to_all | solution.py:39
  87.1 1.0 copy-start.9

commit v14 on v13

--- a/solution.py
+++ b/solution.py
@@ -12,6 +12,7 @@
 PLANE = ("groups", "inner")
 LANES = 128
 ID_ROWS = 8
+AHEAD, SLIGHTLY_AHEAD = 10**9, 15 * 10**6
 BLOCK = 8
 IN_VMEM = pl.BlockSpec(memory_space=pltpu.VMEM)
 IN_SMEM = pl.BlockSpec(memory_space=pltpu.SMEM)
@@ -55,7 +56,7 @@
         out_ref[n * rows : (n + 1) * rows, :] = block[...]
 
 
-def joined(blocks):
+def joined(blocks, cost_bytes):
     rows, share = blocks[0].shape
     return pl.pallas_call(
         join_kernel,
@@ -63,7 +64,7 @@
         in_specs=[IN_VMEM] * len(blocks),
         out_specs=IN_VMEM,
         compiler_params=params(),
-        cost_estimate=pl.CostEstimate(flops=10**11, bytes_accessed=10**9, transcendentals=0),
+        cost_estimate=pl.CostEstimate(flops=0, bytes_accessed=cost_bytes, transcendentals=0),
         name="join_blocks",
     )(*blocks)
 
@@ -287,11 +288,17 @@
     def exchanged(blocks):
         return blocks[:1] + [to_partner(blocks[n], "inner", inner, n) for n in range(1, inner)]
 
-    def rings(near, far, second_after=()):
+    def rings(near, far, first_cost=0, second_after=()):
         near, far = [near], [far]
         for step in range(1, outer):
-            near.append(next_on_ring(after(near[-1], *second_after) if step == 2 else near[-1], outer))
-            far.append(next_on_ring(far[-1], outer))
+            if step == 2:
+                near_block, far_block = after(near[-1], *second_after), after(far[-1], *second_after)
+                if first_cost:
+                    near_block = joined([near_block], first_cost)
+            else:
+                near_block, far_block = near[-1], far[-1]
+            near.append(next_on_ring(near_block, outer))
+            far.append(next_on_ring(far_block, outer))
         return near, far
 
     steps_back = jnp.arange(outer, dtype=jnp.int32)[:, None]
@@ -302,7 +309,7 @@
 
     middle = inner // 2
     down = exchanged(slices(adapter_down_maps[0].T))
-    down_near, down_far = rings(joined(down[:middle]), joined(down[middle:]))
+    down_near, down_far = rings(joined(down[:middle], AHEAD), joined(down[middle:], AHEAD), first_cost=SLIGHTLY_AHEAD)
     ids = token_adapter_index.reshape(1, tok)
     rows = swap(after(outgoing_rows(hidden, ids, members), down_near[0]))
     up = exchanged([after(block, down_near[1]) for block in slices(adapter_up_maps[0])])

time: 124 us -> 150 us (1.21)
  waiting for transfers between devices: 44.9 us -> 69.2 us
  blocking collectives: 29.6 us -> 36.2 us
  starting transfers between devices: 24.5 us -> 19.1 us
  local copies, waits for them, and re-layouts: 9.75 us -> 12.3 us
    ppermute x6, waiting for transfers between devices: 4.86 us -> 28.6 us  [to_partner(): return lax.ppermute(value, axes, [(i, i ^ offset) for i in range(size)])]
    ppermute x12, waiting for transfers between devices: 33.8 us -> 40.6 us  [next_on_ring(): lax.ppermute(block, 'outer', [(i, (i + 1) % outer) for i in range(outer)])]
    all_to_all x1 -> x2, blocking collectives: 29.6 us -> 36.2 us  [swap(): return lax.all_to_all(value, PLANE, split_axis=0, concat_axis=0, tiled=True)]
    all_to_all x3 -> x2, waiting for transfers between devices: 6.21 us -> 0.01 us  [swap(): return lax.all_to_all(value, PLANE, split_axis=0, concat_axis=0, tiled=True)]
    all_to_all x3 -> x2, starting transfers between devices: 11.3 us -> 8.26 us  [swap(): return lax.all_to_all(value, PLANE, split_axis=0, concat_axis=0, tiled=True)]
    ppermute x12, starting transfers between devices: 7.83 us -> 6.14 us  [next_on_ring(): lax.ppermute(block, 'outer', [(i, (i + 1) % outer) for i in range(outer)])]
  transfers between devices with their start and end apart: 21 -> 20, of which waited for: 13 -> 12; matrix products, arithmetic and copies ran while one was open for 2% -> 2% of each run, Pallas kernels for 6% -> 4%
where the time goes in v14:
time: 150 us; the launch traced here: 149 us
  waiting for transfers between devices  69.2 us (46%)
  blocking collectives  36.2 us (24%)
  starting transfers between devices  19.1 us (13%)
  local copies, waits for them, and re-layouts  12.3 us (8%)
  Pallas kernels  10.9 us (7%)
    ppermute x12, waiting for transfers between devices, next_on_ring(): lax.ppermute(block, 'outer', [(i, (i + 1) % outer) for i in range(outer)])  40.6 us
    all_to_all x2, blocking collectives, swap(): return lax.all_to_all(value, PLANE, split_axis=0, concat_axis=0, tiled=True)  36.2 us
    ppermute x6, waiting for transfers between devices, to_partner(): return lax.ppermute(value, axes, [(i, i ^ offset) for i in range(size)])  28.6 us
    unnamed x22, local copies, waits for them, and re-layouts  9.03 us
    all_to_all x2, starting transfers between devices, swap(): return lax.all_to_all(value, PLANE, split_axis=0, concat_axis=0, tiled=True)  8.26 us
    ppermute x12, starting transfers between devices, next_on_ring(): lax.ppermute(block, 'outer', [(i, (i + 1) % outer) for i in range(outer)])  6.14 us
    ppermute x6, starting transfers between devices, to_partner(): return lax.ppermute(value, axes, [(i, i ^ offset) for i in range(size)])  4.68 us
    pallas_call x1, Pallas kernels, up_product(): pl.pallas_call(functools.partial(up_kernel, len(maps), rank), out_shape=j...  4.06 us
  transfers between devices with their start and end apart: 20, of which 12 were waited for; matrix products, arithmetic and copies ran while one was open for 2% of the time, Pallas kernels for 4%

profile of v14, /device:TPU:0, one launch (start us, length us, event | category | flops | bytes accessed | tf_op | source)
XLA Modules:
  0.0 148.9 jit_solution(9756044693414466434)
XLA Ops:
  0.0 1.1 dynamic-slice_bitcast_fusion.4
  1.7 1.6 %copy-done = bf16[128,8192]{1,0:T(8,128)(2,1)S(1)} copy-done((bf16[128,8192]{1,0:T(8,128)(2,1)S(1)}, bf16[128,8192]{1,0:T(8,128)(2,1)}, u32[]{:S(2)}) %copy-start) | copy-done | bytes 2097176
  3.9 1.6 %outgoing_rows.1 = bf16[8,136,1024]{2,1,0:T(8,128)(2,1)} custom-call(bf16[128,8192]{1,0:T(8,128)(2,1)S(1)} %copy-done, s32[1,128]{1,0:T(1,128)S(1)} %bitcast.25), custom_call_target="tpu_custom_call" | custom-call | tf_op jit(solution)/shard_map/outgoing_rows/pallas_call | solution.py:95
  5.6 4.8 %all-to-all-start = ((bf16[8,136,1024]{2,1,0:T(8,128)(2,1)}), bf16[8,136,1024]{2,1,0:T(8,128)(2,1)S(1)}, u32[]{:S(2)}, u32[]{:S(2)}) async-start(bf16[8,136,1024]{2,1,0:T(8,128)(2,1)} %outgoing_rows.1), calls=%async_computation | async-start | bytes 4456448 | tf_op jit(solution)/shard_map/all_to_all | solution.py:40
  10.4 2.0 %collective-permute-start.1 = (bf16[64,1024]{1,0:T(8,128)(2,1)S(1)}, bf16[64,1024]{1,0:T(8,128)(2,1)S(1)}, u32[]{:S(2)}, u32[]{:S(2)}) collective-permute-start(bf16[64,1024]{1,0:T(8,128)(2,1)S(1)} %get-tuple-element.34), channel_id=1, source_target_pairs={{0,2},{1,3},{2,0},{3,1},{4,6},{5,7},{6,4},{7,5},{8,10},{9,11},{10,... | collective-permute-start | bytes 393224 | tf_op jit(solution)/shard_map/ppermute | solution.py:28
  12.4 1.6 %collective-permute-start.3 = (bf16[128,1024]{1,0:T(8,128)(2,1)S(1)}, bf16[128,1024]{1,0:T(8,128)(2,1)S(1)}, u32[]{:S(2)}, u32[]{:S(2)}) collective-permute-start(bf16[128,1024]{1,0:T(8,128)(2,1)S(1)} %join_blocks.3.refs_0_), channel_id=1, source_target_pairs={{0,4},{4,8},{8,12},{12,0},{1,5},{5,9},{9,13},{13,1},{2,6},{6,10},{... | collective-permute-start | bytes 786440 | tf_op jit(solution)/shard_map/ppermute | solution.py:32
  14.0 26.8 %collective-permute-done.1.refs_0_ = bf16[64,1024]{1,0:T(8,128)(2,1)S(1)} collective-permute-done((bf16[64,1024]{1,0:T(8,128)(2,1)S(1)}, bf16[64,1024]{1,0:T(8,128)(2,1)S(1)}, u32[]{:S(2)}, u32[]{:S(2)}) %collective-permute-start.1) | collective-permute-done | bytes 131104 | tf_op jit(solution)/shard_map/ppermute | solution.py:28
  40.8 1.9 %collective-permute-done.2.refs_1_ = bf16[64,1024]{1,0:T(8,128)(2,1)S(1)} collective-permute-done((bf16[64,1024]{1,0:T(8,128)(2,1)S(1)}, bf16[64,1024]{1,0:T(8,128)(2,1)S(1)}, u32[]{:S(2)}, u32[]{:S(2)}) %collective-permute-start.2) | collective-permute-done | bytes 131104 | tf_op jit(solution)/shard_map/ppermute | solution.py:28
  42.7 1.6 %collective-permute-start.4 = (bf16[128,1024]{1,0:T(8,128)(2,1)S(1)}, bf16[128,1024]{1,0:T(8,128)(2,1)S(1)}, u32[]{:S(2)}, u32[]{:S(2)}) collective-permute-start(bf16[128,1024]{1,0:T(8,128)(2,1)S(1)} %join_blocks.4.refs_1_), channel_id=1, source_target_pairs={{0,4},{4,8},{8,12},{12,0},{1,5},{5,9},{9,13},{13,1},{2,6},{6,10},{... | collective-permute-start | bytes 786440 | tf_op jit(solution)/shard_map/ppermute | solution.py:32
  44.3 1.6 %collective-permute-start.5 = (bf16[128,1024]{1,0:T(8,128)(2,1)S(1)}, bf16[128,1024]{1,0:T(8,128)(2,1)}, u32[]{:S(2)}, u32[]{:S(2)}) collective-permute-start(bf16[128,1024]{1,0:T(8,128)(2,1)S(1)} %join_blocks.5), channel_id=1, source_target_pairs={{0,4},{4,8},{8,12},{12,0},{1,5},{5,9},{9,13},{13,1},{2,6},{6,10},{... | collective-permute-start | bytes 786440 | tf_op jit(solution)/shard_map/ppermute | solution.py:32
  46.0 7.7 %collective-permute-done.4.refs_3_ = bf16[128,1024]{1,0:T(8,128)(2,1)S(1)} collective-permute-done((bf16[128,1024]{1,0:T(8,128)(2,1)S(1)}, bf16[128,1024]{1,0:T(8,128)(2,1)S(1)}, u32[]{:S(2)}, u32[]{:S(2)}) %collective-permute-start.4) | collective-permute-done | bytes 262176 | tf_op jit(solution)/shard_map/ppermute | solution.py:32
  53.7 2.0 %dynamic-slice_bitcast_fusion.1 = (bf16[64,1024]{1,0:T(8,128)(2,1)}, bf16[64,1024]{1,0:T(8,128)(2,1)}, bf16[64,1024]{1,0:T(8,128)(2,1)}, bf16[64,1024]{1,0:T(8,128)(2,1)}) fusion(bf16[1,64,8192]{2,1,0:T(8,128)(2,1)} %param.7, s32[]{:T(128)S(6)} %select_n.31, s32[]{:T(128)S(6)} %select_n.30, s32[]{:T(128)S(6)} %select_n.29, s32[]{:T(128)S(6)} %select_n.32), kind=kLoop, calls=%fused_computation.3 | loop fusion | bytes 1048592 | tf_op jit(solution)/shard_map/dynamic_slice | solution.py:285
  56.5 1.3 collective-permute-start.10
  57.8 1.6 %collective-permute-done.5.refs_4_ = bf16[128,1024]{1,0:T(8,128)(2,1)} collective-permute-done((bf16[128,1024]{1,0:T(8,128)(2,1)S(1)}, bf16[128,1024]{1,0:T(8,128)(2,1)}, u32[]{:S(2)}, u32[]{:S(2)}) %collective-permute-start.5) | collective-permute-done | bytes 262176 | tf_op jit(solution)/shard_map/ppermute | solution.py:32
  59.4 5.6 %collective-permute-done.6.refs_5_ = bf16[128,1024]{1,0:T(8,128)(2,1)} collective-permute-done((bf16[128,1024]{1,0:T(8,128)(2,1)S(1)}, bf16[128,1024]{1,0:T(8,128)(2,1)}, u32[]{:S(2)}, u32[]{:S(2)}) %collective-permute-start.6) | collective-permute-done | bytes 262176 | tf_op jit(solution)/shard_map/ppermute | solution.py:32
  65.0 1.0 pad_maximum_fusion.refs_0_
  66.1 4.6 %collective-permute-done.7.refs_6_ = bf16[128,1024]{1,0:T(8,128)(2,1)S(1)} collective-permute-done((bf16[128,1024]{1,0:T(8,128)(2,1)}, bf16[128,1024]{1,0:T(8,128)(2,1)S(1)}, u32[]{:S(2)}, u32[]{:S(2)}) %collective-permute-start.7) | collective-permute-done | bytes 262176 | tf_op jit(solution)/shard_map/ppermute | solution.py:32
  71.4 4.2 %collective-permute-done.8.refs_7_ = bf16[128,1024]{1,0:T(8,128)(2,1)S(1)} collective-permute-done((bf16[128,1024]{1,0:T(8,128)(2,1)}, bf16[128,1024]{1,0:T(8,128)(2,1)S(1)}, u32[]{:S(2)}, u32[]{:S(2)}) %collective-permute-start.8) | collective-permute-done | bytes 262176 | tf_op jit(solution)/shard_map/ppermute | solution.py:32
  76.3 1.3 collective-permute-start.13
  77.7 1.0 copy-done.4
  80.6 3.8 %down_product.1 = (f32[8,64,128]{2,1,0:T(8,128)S(1)}, f32[8,128,128]{2,1,0:T(8,128)S(1)}) custom-call(s32[16]{0:T(128)S(1)} %add.60.labels_ref, bf16[8,136,1024]{2,1,0:T(8,128)(2,1)S(1)} %all-to-all-done.rows_ref, bf16[128,1024]{1,0:T(8,128)(2,1)S(1)} %join_blocks.3.refs_0_, bf16[128,1024]{1,0:T(8,128)(2,1)S(1)} %join_blocks.4.refs_1_, ...), custom_call_target="tpu_custom_call" | custom-call | flops 2147483648 | bytes 4194304 | tf_op jit(solution)/shard_map/down_product/pallas_call | solution.py:150
  85.8 1.6 %collective-permute-done.12.refs_2_ = bf16[128,1024]{1,0:T(8,128)(2,1)} collective-permute-done((bf16[128,1024]{1,0:T(8,128)(2,1)S(1)}, bf16[128,1024]{1,0:T(8,128)(2,1)}, u32[]{:S(2)}, u32[]{:S(2)}) %collective-permute-start.12) | collective-permute-done | bytes 262176 | tf_op jit(solution)/shard_map/ppermute | solution.py:32
  87.4 5.6 %collective-permute-done.13.refs_3_ = bf16[128,1024]{1,0:T(8,128)(2,1)} collective-permute-done((bf16[128,1024]{1,0:T(8,128)(2,1)S(1)}, bf16[128,1024]{1,0:T(8,128)(2,1)}, u32[]{:S(2)}, u32[]{:S(2)}) %collective-permute-start.13) | collective-permute-done | bytes 262176 | tf_op jit(solution)/shard_map/ppermute | solution.py:32
  93.0 3.4 %all-to-all-start.1 = ((f32[8,64,128]{2,1,0:T(8,128)}), f32[8,64,128]{2,1,0:T(8,128)S(1)}, u32[]{:S(2)}, u32[]{:S(2)}) async-start(f32[8,64,128]{2,1,0:T(8,128)} %copy-done.1), calls=%async_computation.1 | async-start | bytes 524288 | tf_op jit(solution)/shard_map/all_to_all | solution.py:40
  96.5 2.2 %collective-permute-done.14.refs_4_ = bf16[128,1024]{1,0:T(8,128)(2,1)S(1)} collective-permute-done((bf16[128,1024]{1,0:T(8,128)(2,1)}, bf16[128,1024]{1,0:T(8,128)(2,1)S(1)}, u32[]{:S(2)}, u32[]{:S(2)}) %collective-permute-start.14) | collective-permute-done | bytes 262176 | tf_op jit(solution)/shard_map/ppermute | solution.py:32
  98.7 4.9 %collective-permute-done.15.refs_5_ = bf16[128,1024]{1,0:T(8,128)(2,1)S(1)} collective-permute-done((bf16[128,1024]{1,0:T(8,128)(2,1)}, bf16[128,1024]{1,0:T(8,128)(2,1)S(1)}, u32[]{:S(2)}, u32[]{:S(2)}) %collective-permute-start.15) | collective-permute-done | bytes 262176 | tf_op jit(solution)/shard_map/ppermute | solution.py:32
  103.6 7.6 %all_to_all.20.shrunk_ref = bf16[8,64,128]{2,1,0:T(8,128)(2,1)S(1)} all-to-all(bf16[8,64,128]{2,1,0:T(8,128)(2,1)S(1)} %summed_copies.1), channel_id=1, replica_groups=mesh['groups'=2,'outer'=4,'inner'=4] {'groups','inner'}, dimensions={0} | all-to-all | bytes 262144 | tf_op jit(solution)/shard_map/all_to_all | solution.py:40
  111.1 2.7 %collective-permute-done.17.refs_7_ = bf16[128,1024]{1,0:T(8,128)(2,1)S(1)} collective-permute-done((bf16[128,1024]{1,0:T(8,128)(2,1)S(1)}, bf16[128,1024]{1,0:T(8,128)(2,1)S(1)}, u32[]{:S(2)}, u32[]{:S(2)}) %collective-permute-start.17) | collective-permute-done | bytes 262176 | tf_op jit(solution)/shard_map/ppermute | solution.py:32
  113.8 1.0 copy-done.10
  114.8 4.1 %up_product.1 = bf16[8,128,1024]{2,1,0:T(8,128)(2,1)S(1)} custom-call(s32[16]{0:T(128)S(1)} %add.60.labels_ref, f32[8,128,128]{2,1,0:T(8,128)S(1)} %copy-done.10, bf16[8,64,128]{2,1,0:T(8,128)(2,1)S(1)} %all_to_all.20.shrunk_ref, bf16[128,1024]{1,0:T(8,128)(2,1)S(1)} %pad_maximum_fusion.refs_0_, bf16[128,1024]{1,0:T(8,128)(2,1)S(1)} %pad_maximum_fusion.1.refs_1_, ...), custom_call_target="tpu_custom_call" | custom-call | flops 2147483648 | bytes 4194304 | tf_op jit(solution)/shard_map/up_product/pallas_call | solution.py:227
  118.9 28.6 %all_to_all.21.refs_0_ = bf16[8,128,1024]{2,1,0:T(8,128)(2,1)S(1)} all-to-all(bf16[8,128,1024]{2,1,0:T(8,128)(2,1)S(1)} %up_product.1), channel_id=1, replica_groups=mesh['groups'=2,'outer'=4,'inner'=4] {'groups','inner'}, dimensions={0} | all-to-all | bytes 4194304 | tf_op jit(solution)/shard_map/all_to_all | solution.py:40
  147.6 1.4 place_results.1
  (47 shorter events, 7.1 us)
Async XLA Ops:
  1.1 4.4 %collective-permute-start = (bf16[64,1024]{1,0:T(8,128)(2,1)S(1)}, bf16[64,1024]{1,0:T(8,128)(2,1)S(1)}, u32[]{:S(2)}, u32[]{:S(2)}) collective-permute-start(bf16[64,1024]{1,0:T(8,128)(2,1)S(1)} %get-tuple-element.32), channel_id=1, source_target_pairs={{0,1},{1,0},{2,3},{3,2},{4,5},{5,4},{6,7},{7,6},{8,9},{9,8},{10,11... | collective-permute-start | bytes 393224 | tf_op jit(solution)/shard_map/ppermute | solution.py:28
  1.7 1.6 %copy-start = (bf16[128,8192]{1,0:T(8,128)(2,1)S(1)}, bf16[128,8192]{1,0:T(8,128)(2,1)}, u32[]{:S(2)}) copy-start(bf16[128,8192]{1,0:T(8,128)(2,1)} %hidden_ref.1) | copy-start | bytes 6291460
  3.2 0.7 copy-start.2
  5.6 72.1 %all-to-all-start = ((bf16[8,136,1024]{2,1,0:T(8,128)(2,1)}), bf16[8,136,1024]{2,1,0:T(8,128)(2,1)S(1)}, u32[]{:S(2)}, u32[]{:S(2)}) async-start(bf16[8,136,1024]{2,1,0:T(8,128)(2,1)} %outgoing_rows.1), calls=%async_computation | async-start | bytes 4456448 | tf_op jit(solution)/shard_map/all_to_all | solution.py:40
  10.4 30.4 %collective-permute-start.1 = (bf16[64,1024]{1,0:T(8,128)(2,1)S(1)}, bf16[64,1024]{1,0:T(8,128)(2,1)S(1)}, u32[]{:S(2)}, u32[]{:S(2)}) collective-permute-start(bf16[64,1024]{1,0:T(8,128)(2,1)S(1)} %get-tuple-element.34), channel_id=1, source_target_pairs={{0,2},{1,3},{2,0},{3,1},{4,6},{5,7},{6,4},{7,5},{8,10},{9,11},{10,... | collective-permute-start | bytes 393224 | tf_op jit(solution)/shard_map/ppermute | solution.py:28
  12.4 30.2 %collective-permute-start.2 = (bf16[64,1024]{1,0:T(8,128)(2,1)S(1)}, bf16[64,1024]{1,0:T(8,128)(2,1)S(1)}, u32[]{:S(2)}, u32[]{:S(2)}) collective-permute-start(bf16[64,1024]{1,0:T(8,128)(2,1)S(1)} %get-tuple-element.31), channel_id=1, source_target_pairs={{0,3},{1,2},{2,1},{3,0},{4,7},{5,6},{6,5},{7,4},{8,11},{9,10},{10,... | collective-permute-start | bytes 393224 | tf_op jit(solution)/shard_map/ppermute | solution.py:28
  12.4 31.9 %collective-permute-start.3 = (bf16[128,1024]{1,0:T(8,128)(2,1)S(1)}, bf16[128,1024]{1,0:T(8,128)(2,1)S(1)}, u32[]{:S(2)}, u32[]{:S(2)}) collective-permute-start(bf16[128,1024]{1,0:T(8,128)(2,1)S(1)} %join_blocks.3.refs_0_), channel_id=1, source_target_pairs={{0,4},{4,8},{8,12},{12,0},{1,5},{5,9},{9,13},{13,1},{2,6},{6,10},{... | collective-permute-start | bytes 786440 | tf_op jit(solution)/shard_map/ppermute | solution.py:32
  42.7 11.0 %collective-permute-start.4 = (bf16[128,1024]{1,0:T(8,128)(2,1)S(1)}, bf16[128,1024]{1,0:T(8,128)(2,1)S(1)}, u32[]{:S(2)}, u32[]{:S(2)}) collective-permute-start(bf16[128,1024]{1,0:T(8,128)(2,1)S(1)} %join_blocks.4.refs_1_), channel_id=1, source_target_pairs={{0,4},{4,8},{8,12},{12,0},{1,5},{5,9},{9,13},{13,1},{2,6},{6,10},{... | collective-permute-start | bytes 786440 | tf_op jit(solution)/shard_map/ppermute | solution.py:32
  44.3 15.0 %collective-permute-start.5 = (bf16[128,1024]{1,0:T(8,128)(2,1)S(1)}, bf16[128,1024]{1,0:T(8,128)(2,1)}, u32[]{:S(2)}, u32[]{:S(2)}) collective-permute-start(bf16[128,1024]{1,0:T(8,128)(2,1)S(1)} %join_blocks.5), channel_id=1, source_target_pairs={{0,4},{4,8},{8,12},{12,0},{1,5},{5,9},{9,13},{13,1},{2,6},{6,10},{... | collective-permute-start | bytes 786440 | tf_op jit(solution)/shard_map/ppermute | solution.py:32
  53.7 12.4 %copy-start.3 = (bf16[128,1024]{1,0:T(8,128)(2,1)}, bf16[128,1024]{1,0:T(8,128)(2,1)S(1)}, u32[]{:S(2)}) copy-start(bf16[128,1024]{1,0:T(8,128)(2,1)S(1)} %collective-permute-done.4.refs_3_) | copy-start | bytes 786436
  53.7 11.3 %collective-permute-start.6 = (bf16[128,1024]{1,0:T(8,128)(2,1)S(1)}, bf16[128,1024]{1,0:T(8,128)(2,1)}, u32[]{:S(2)}, u32[]{:S(2)}) collective-permute-start(bf16[128,1024]{1,0:T(8,128)(2,1)S(1)} %collective-permute-done.4.refs_3_), channel_id=1, source_target_pairs={{0,4},{4,8},{8,12},{12,0},{1,5},{5,9},{9,13},{13,1},{2,6},{6,10},{... | collective-permute-start | bytes 786440 | tf_op jit(solution)/shard_map/ppermute | solution.py:32
  55.7 9.3 %collective-permute-start.9 = (bf16[64,1024]{1,0:T(8,128)(2,1)}, bf16[64,1024]{1,0:T(8,128)(2,1)}, u32[]{:S(2)}, u32[]{:S(2)}) collective-permute-start(bf16[64,1024]{1,0:T(8,128)(2,1)} %get-tuple-element.20), channel_id=1, source_target_pairs={{0,1},{1,0},{2,3},{3,2},{4,5},{5,4},{6,7},{7,6},{8,9},{9,8},{10,11... | collective-permute-start | bytes 393224 | tf_op jit(solution)/shard_map/ppermute | solution.py:28
  55.7 10.3 %collective-permute-start.11 = (bf16[64,1024]{1,0:T(8,128)(2,1)}, bf16[64,1024]{1,0:T(8,128)(2,1)S(1)}, u32[]{:S(2)}, u32[]{:S(2)}) collective-permute-start(bf16[64,1024]{1,0:T(8,128)(2,1)} %get-tuple-element.23), channel_id=1, source_target_pairs={{0,3},{1,2},{2,1},{3,0},{4,7},{5,6},{6,5},{7,4},{8,11},{9,10},{10,... | collective-permute-start | bytes 393224 | tf_op jit(solution)/shard_map/ppermute | solution.py:28
  56.5 9.6 %collective-permute-start.10 = (bf16[64,1024]{1,0:T(8,128)(2,1)}, bf16[64,1024]{1,0:T(8,128)(2,1)S(1)}, u32[]{:S(2)}, u32[]{:S(2)}) collective-permute-start(bf16[64,1024]{1,0:T(8,128)(2,1)} %get-tuple-element.22), channel_id=1, source_target_pairs={{0,2},{1,3},{2,0},{3,1},{4,6},{5,7},{6,4},{7,5},{8,10},{9,11},{10,... | collective-permute-start | bytes 393224 | tf_op jit(solution)/shard_map/ppermute | solution.py:28
  59.4 11.3 %collective-permute-start.7 = (bf16[128,1024]{1,0:T(8,128)(2,1)}, bf16[128,1024]{1,0:T(8,128)(2,1)S(1)}, u32[]{:S(2)}, u32[]{:S(2)}) collective-permute-start(bf16[128,1024]{1,0:T(8,128)(2,1)} %collective-permute-done.5.refs_4_), channel_id=1, source_target_pairs={{0,4},{4,8},{8,12},{12,0},{1,5},{5,9},{9,13},{13,1},{2,6},{6,10},{... | collective-permute-start | bytes 786440 | tf_op jit(solution)/shard_map/ppermute | solution.py:32
  65.0 10.6 %collective-permute-start.8 = (bf16[128,1024]{1,0:T(8,128)(2,1)}, bf16[128,1024]{1,0:T(8,128)(2,1)S(1)}, u32[]{:S(2)}, u32[]{:S(2)}) collective-permute-start(bf16[128,1024]{1,0:T(8,128)(2,1)} %collective-permute-done.6.refs_5_), channel_id=1, source_target_pairs={{0,4},{4,8},{8,12},{12,0},{1,5},{5,9},{9,13},{13,1},{2,6},{6,10},{... | collective-permute-start | bytes 786440 | tf_op jit(solution)/shard_map/ppermute | solution.py:32
  70.6 0.7 copy-start.5
  75.6 0.7 copy-start.7
  76.3 11.1 %collective-permute-start.12 = (bf16[128,1024]{1,0:T(8,128)(2,1)S(1)}, bf16[128,1024]{1,0:T(8,128)(2,1)}, u32[]{:S(2)}, u32[]{:S(2)}) collective-permute-start(bf16[128,1024]{1,0:T(8,128)(2,1)S(1)} %pad_maximum_fusion.refs_0_), channel_id=1, source_target_pairs={{0,4},{4,8},{8,12},{12,0},{1,5},{5,9},{9,13},{13,1},{2,6},{6,10},{... | collective-permute-start | bytes 786440 | tf_op jit(solution)/shard_map/ppermute | solution.py:32
  76.3 16.8 %collective-permute-start.13 = (bf16[128,1024]{1,0:T(8,128)(2,1)S(1)}, bf16[128,1024]{1,0:T(8,128)(2,1)}, u32[]{:S(2)}, u32[]{:S(2)}) collective-permute-start(bf16[128,1024]{1,0:T(8,128)(2,1)S(1)} %pad_maximum_fusion.1.refs_1_), channel_id=1, source_target_pairs={{0,4},{4,8},{8,12},{12,0},{1,5},{5,9},{9,13},{13,1},{2,6},{6,10},{... | collective-permute-start | bytes 786440 | tf_op jit(solution)/shard_map/ppermute | solution.py:32
  77.7 1.0 copy-start.4
  78.7 0.9 copy-start.6
  79.6 0.9 copy-start.8
  84.3 0.7 copy-start.1
  85.0 0.8 copy-start.9
  87.4 11.2 %collective-permute-start.14 = (bf16[128,1024]{1,0:T(8,128)(2,1)}, bf16[128,1024]{1,0:T(8,128)(2,1)S(1)}, u32[]{:S(2)}, u32[]{:S(2)}) collective-permute-start(bf16[128,1024]{1,0:T(8,128)(2,1)} %collective-permute-done.12.refs_2_), channel_id=1, source_target_pairs={{0,4},{4,8},{8,12},{12,0},{1,5},{5,9},{9,13},{13,1},{2,6},{6,10},{... | collective-permute-start | bytes 786440 | tf_op jit(solution)/shard_map/ppermute | solution.py:32
  93.0 10.5 %collective-permute-start.15 = (bf16[128,1024]{1,0:T(8,128)(2,1)}, bf16[128,1024]{1,0:T(8,128)(2,1)S(1)}, u32[]{:S(2)}, u32[]{:S(2)}) collective-permute-start(bf16[128,1024]{1,0:T(8,128)(2,1)} %collective-permute-done.13.refs_3_), channel_id=1, source_target_pairs={{0,4},{4,8},{8,12},{12,0},{1,5},{5,9},{9,13},{13,1},{2,6},{6,10},{... | collective-permute-start | bytes 786440 | tf_op jit(solution)/shard_map/ppermute | solution.py:32
  93.0 10.5 %all-to-all-start.1 = ((f32[8,64,128]{2,1,0:T(8,128)}), f32[8,64,128]{2,1,0:T(8,128)S(1)}, u32[]{:S(2)}, u32[]{:S(2)}) async-start(f32[8,64,128]{2,1,0:T(8,128)} %copy-done.1), calls=%async_computation.1 | async-start | bytes 524288 | tf_op jit(solution)/shard_map/all_to_all | solution.py:40
  98.7 12.5 %collective-permute-start.16 = (bf16[128,1024]{1,0:T(8,128)(2,1)S(1)}, bf16[128,1024]{1,0:T(8,128)(2,1)S(1)}, u32[]{:S(2)}, u32[]{:S(2)}) collective-permute-start(bf16[128,1024]{1,0:T(8,128)(2,1)S(1)} %collective-permute-done.14.refs_4_), channel_id=1, source_target_pairs={{0,4},{4,8},{8,12},{12,0},{1,5},{5,9},{9,13},{13,1},{2,6},{6,10},{... | collective-permute-start | bytes 786440 | tf_op jit(solution)/shard_map/ppermute | solution.py:32
  103.5 10.3 %collective-permute-start.17 = (bf16[128,1024]{1,0:T(8,128)(2,1)S(1)}, bf16[128,1024]{1,0:T(8,128)(2,1)S(1)}, u32[]{:S(2)}, u32[]{:S(2)}) collective-permute-start(bf16[128,1024]{1,0:T(8,128)(2,1)S(1)} %collective-permute-done.15.refs_5_), channel_id=1, source_target_pairs={{0,4},{4,8},{8,12},{12,0},{1,5},{5,9},{9,13},{13,1},{2,6},{6,10},{... | collective-permute-start | bytes 786440 | tf_op jit(solution)/shard_map/ppermute | solution.py:32
  113.8 1.0 copy-start.10

commit v15 on v13

--- a/solution.py
+++ b/solution.py
@@ -12,6 +12,7 @@
 PLANE = ("groups", "inner")
 LANES = 128
 ID_ROWS = 8
+AHEAD, SLIGHTLY_AHEAD = 10**11, 5 * 10**9
 BLOCK = 8
 IN_VMEM = pl.BlockSpec(memory_space=pltpu.VMEM)
 IN_SMEM = pl.BlockSpec(memory_space=pltpu.SMEM)
@@ -55,7 +56,7 @@
         out_ref[n * rows : (n + 1) * rows, :] = block[...]
 
 
-def joined(blocks):
+def joined(blocks, cost):
     rows, share = blocks[0].shape
     return pl.pallas_call(
         join_kernel,
@@ -63,7 +64,7 @@
         in_specs=[IN_VMEM] * len(blocks),
         out_specs=IN_VMEM,
         compiler_params=params(),
-        cost_estimate=pl.CostEstimate(flops=10**11, bytes_accessed=10**9, transcendentals=0),
+        cost_estimate=pl.CostEstimate(flops=cost, bytes_accessed=10**6, transcendentals=0),
         name="join_blocks",
     )(*blocks)
 
@@ -186,27 +187,27 @@
     )(terms)
 
 
-def up_kernel(map_count, rank, labels_ref, ids_ref, shrunk_ref, *refs):
-    maps, (out_ref, spread_ref, ids_buf, sem) = refs[:map_count], refs[map_count:]
+def up_kernel(map_count, rank, labels_ref, me_ref, ids_ref, shrunk_ref, *refs):
+    members, half, _ = shrunk_ref.shape
+    maps, outs = refs[:map_count], refs[map_count : map_count + members]
+    spread_ref, ids_buf, sem = refs[map_count + members :]
     kept = pltpu.make_async_copy(ids_ref, ids_buf, sem)
     kept.start()
-    members, half, _ = shrunk_ref.shape
     tok = 2 * half
     block = min(BLOCK, members)
     tiles = spread_ref.shape[1] // LANES
     lane = lax.broadcasted_iota(jnp.int32, (half, LANES), 1)
     held = jnp.concatenate([m[...] for m in maps], axis=0)
     kept.wait()
-
-    def one(step, _):
-        first = step * block
+    for first in range(0, members, block):
         for n in range(block):
-            packed = shrunk_ref[first + n].astype(jnp.float32)
+            member = me_ref[0] ^ (first + n)
+            packed = shrunk_ref[member].astype(jnp.float32)
             turned = pltpu.roll(packed, LANES // 2, 1)
             shrunk = jnp.concatenate(
                 [jnp.where(lane < rank, packed, turned), jnp.where(lane < rank, turned, packed)], axis=0
             )
-            ids = ids_buf[first + n]
+            ids = ids_buf[member]
             for tile in range(tiles):
                 named = ids == tile_labels(labels_ref, tile, rank, (1, LANES))
                 spread_ref[n * tok : (n + 1) * tok, tile * LANES : (tile + 1) * LANES] = jnp.where(
@@ -214,20 +215,18 @@
                 ).astype(jnp.bfloat16)
         product = jnp.dot(spread_ref[...], held, preferred_element_type=jnp.float32)
         product = (adapter_scale * product).astype(jnp.bfloat16)
-        out_ref[pl.ds(first, block)] = product.reshape(block, tok, product.shape[1])
-        return 0
-
-    lax.fori_loop(0, members // block, one, 0)
-
-
-def up_product(labels, ids, shrunk, maps, rank):
+        for n in range(block):
+            outs[first + n][...] = product[n * tok : (n + 1) * tok, :]
+
+
+def up_product(labels, me, ids, shrunk, maps, rank):
     members, tok, _ = ids.shape
     map_rows, piece = sum(m.shape[0] for m in maps), maps[0].shape[1]
     return pl.pallas_call(
         functools.partial(up_kernel, len(maps), rank),
-        out_shape=jax.ShapeDtypeStruct((members, tok, piece), jnp.bfloat16),
-        in_specs=[IN_SMEM, IN_HBM, IN_VMEM] + [IN_VMEM] * len(maps),
-        out_specs=IN_VMEM,
+        out_shape=[jax.ShapeDtypeStruct((tok, piece), jnp.bfloat16)] * members,
+        in_specs=[IN_SMEM, IN_SMEM, IN_HBM, IN_VMEM] + [IN_VMEM] * len(maps),
+        out_specs=[IN_VMEM] * members,
         scratch_shapes=[
             pltpu.VMEM((min(BLOCK, members) * tok, map_rows), jnp.bfloat16),
             pltpu.VMEM((members, tok, LANES), jnp.float32),
@@ -240,34 +239,33 @@
             transcendentals=0,
         ),
         name="up_product",
-    )(labels, ids, shrunk, *maps)
-
-
-def place_kernel(pieces, *refs):
-    parts, out_ref, sems = refs[:pieces], refs[-2], refs[-1]
-    members, _, piece = parts[0].shape
+    )(labels, me, ids, shrunk, *maps)
+
+
+def place_kernel(me_ref, *refs):
+    blocks, out_ref, sems = refs[:-2], refs[-2], refs[-1]
+    share = blocks[0].shape[1]
     copies = []
-    for n in range(members * pieces):
-        member, part = n // pieces, n % pieces
-        target = out_ref.at[:, pl.ds(n * piece, piece)]
-        copies.append(pltpu.make_async_copy(parts[part].at[member], target, sems.at[n]))
+    for offset, block in enumerate(blocks):
+        at = pl.multiple_of((me_ref[0] ^ offset) * share, LANES)
+        copies.append(pltpu.make_async_copy(block, out_ref.at[:, pl.ds(at, share)], sems.at[offset]))
     for copy in copies:
         copy.start()
     for copy in copies:
         copy.wait()
 
 
-def place(parts):
-    members, tok, piece = parts[0].shape
-    return pl.pallas_call(
-        functools.partial(place_kernel, len(parts)),
-        out_shape=jax.ShapeDtypeStruct((tok, members * len(parts) * piece), jnp.bfloat16),
-        in_specs=[ANYWHERE] * len(parts),
+def place(me, blocks):
+    tok, share = blocks[0].shape
+    return pl.pallas_call(
+        place_kernel,
+        out_shape=jax.ShapeDtypeStruct((tok, len(blocks) * share), jnp.bfloat16),
+        in_specs=[IN_SMEM] + [ANYWHERE] * len(blocks),
         out_specs=ANYWHERE,
-        scratch_shapes=[pltpu.SemaphoreType.DMA((members * len(parts),))],
+        scratch_shapes=[pltpu.SemaphoreType.DMA((len(blocks),))],
         compiler_params=params(),
         name="place_results",
-    )(*parts)
+    )(me, *blocks)
 
 
 def per_device(token_adapter_index, hidden, adapter_down_maps, adapter_up_maps):
@@ -287,10 +285,15 @@
     def exchanged(blocks):
         return blocks[:1] + [to_partner(blocks[n], "inner", inner, n) for n in range(1, inner)]
 
-    def rings(near, far, second_after=()):
+    def rings(near, far, first_cost=0, second_after=()):
         near, far = [near], [far]
         for step in range(1, outer):
-            near.append(next_on_ring(after(near[-1], *second_after) if step == 2 else near[-1], outer))
+            block = near[-1]
+            if step == 2:
+                block = after(block, *second_after)
+                if first_cost:
+                    block = joined([block], first_cost)
+            near.append(next_on_ring(block, outer))
             far.append(next_on_ring(far[-1], outer))
         return near, far
 
@@ -302,7 +305,7 @@
 
     middle = inner // 2
     down = exchanged(slices(adapter_down_maps[0].T))
-    down_near, down_far = rings(joined(down[:middle]), joined(down[middle:]))
+    down_near, down_far = rings(joined(down[:middle], AHEAD), joined(down[middle:], AHEAD), first_cost=SLIGHTLY_AHEAD)
     ids = token_adapter_index.reshape(1, tok)
     rows = swap(after(outgoing_rows(hidden, ids, members), down_near[0]))
     up = exchanged([after(block, down_near[1]) for block in slices(adapter_up_maps[0])])
@@ -316,7 +319,9 @@
     )
     up_maps = [m for pair in zip(up_near, up_far) for m in pair]
     shrunk = swap(summed_copies(swap(packed)))
-    return place([swap(up_product(labels, id_columns, shrunk, up_maps, rank))])
+    results = list(up_product(labels, me.reshape(1), id_columns, shrunk, up_maps, rank))
+    returned = results[:1] + [to_partner(results[n], PLANE, members, n) for n in range(1, members)]
+    return place(me.reshape(1), returned)
 
 
 def solution(mesh):

time: 124 us -> 123 us (level)
  blocking collectives: 29.6 us -> 0 us
  waiting for transfers between devices: 44.9 us -> 66.1 us
  starting transfers between devices: 24.5 us -> 31.3 us
    all_to_all x1 -> x0, blocking collectives: 29.6 us -> none  [swap(): return lax.all_to_all(value, PLANE, split_axis=0, concat_axis=0, tiled=True)]
    ppermute x6 -> x13, waiting for transfers between devices: 4.86 us -> 25.6 us  [to_partner(): return lax.ppermute(value, axes, [(i, i ^ offset) for i in range(size)])]
    ppermute x6 -> x13, starting transfers between devices: 5.36 us -> 12.7 us  [to_partner(): return lax.ppermute(value, axes, [(i, i ^ offset) for i in range(size)])]
  transfers between devices with their start and end apart: 21 -> 28, of which waited for: 13 -> 18; matrix products, arithmetic and copies ran while one was open for 2% -> 2% of each run, Pallas kernels for 6% -> 6%
where the time goes in v15:
time: 123 us; the launch traced here: 122 us
  waiting for transfers between devices  66.1 us (54%)
  starting transfers between devices  31.3 us (25%)
  Pallas kernels  12.2 us (10%)
  local copies, waits for them, and re-layouts  10.4 us (8%)
  other arithmetic  1.99 us (2%)
    ppermute x12, waiting for transfers between devices, next_on_ring(): lax.ppermute(block, 'outer', [(i, (i + 1) % outer) for i in range(outer)])  34.3 us
    ppermute x13, waiting for transfers between devices, to_partner(): return lax.ppermute(value, axes, [(i, i ^ offset) for i in range(size)])  25.6 us
    ppermute x13, starting transfers between devices, to_partner(): return lax.ppermute(value, axes, [(i, i ^ offset) for i in range(size)])  12.7 us
    all_to_all x3, starting transfers between devices, swap(): return lax.all_to_all(value, PLANE, split_axis=0, concat_axis=0, tiled=True)  10.5 us
    unnamed x22, local copies, waits for them, and re-layouts  8.33 us
    ppermute x12, starting transfers between devices, next_on_ring(): lax.ppermute(block, 'outer', [(i, (i + 1) % outer) for i in range(outer)])  8.17 us
    all_to_all x3, waiting for transfers between devices, swap(): return lax.all_to_all(value, PLANE, split_axis=0, concat_axis=0, tiled=True)  6.26 us
    pallas_call x1, Pallas kernels, down_product(): pl.pallas_call(functools.partial(down_kernel, len(maps), rank), out_shape...  4.45 us
  transfers between devices with their start and end apart: 28, of which 18 were waited for; matrix products, arithmetic and copies ran while one was open for 2% of the time, Pallas kernels for 6%

profile of v15, /device:TPU:0, one launch (start us, length us, event | category | flops | bytes accessed | tf_op | source)
XLA Modules:
  0.0 122.3 jit_solution(18370836884373704429)
XLA Ops:
  1.7 2.6 %collective-permute-start.1 = (bf16[64,1024]{1,0:T(8,128)(2,1)S(1)}, bf16[64,1024]{1,0:T(8,128)(2,1)S(1)}, u32[]{:S(2)}, u32[]{:S(2)}) collective-permute-start(bf16[64,1024]{1,0:T(8,128)(2,1)S(1)} %get-tuple-element.48), channel_id=1, source_target_pairs={{0,2},{1,3},{2,0},{3,1},{4,6},{5,7},{6,4},{7,5},{8,10},{9,11},{10,... | collective-permute-start | bytes 393224 | tf_op jit(solution)/shard_map/ppermute | solution.py:28
  4.3 1.6 %copy-done = bf16[128,8192]{1,0:T(8,128)(2,1)S(1)} copy-done((bf16[128,8192]{1,0:T(8,128)(2,1)S(1)}, bf16[128,8192]{1,0:T(8,128)(2,1)}, u32[]{:S(2)}) %copy-start) | copy-done | bytes 2097176
  6.6 1.6 %outgoing_rows.1 = bf16[8,136,1024]{2,1,0:T(8,128)(2,1)} custom-call(bf16[128,8192]{1,0:T(8,128)(2,1)S(1)} %copy-done, s32[1,128]{1,0:T(1,128)S(1)} %bitcast.26), custom_call_target="tpu_custom_call" | custom-call | tf_op jit(solution)/shard_map/outgoing_rows/pallas_call | solution.py:95
  8.2 1.8 %collective-permute-start.3 = (bf16[128,1024]{1,0:T(8,128)(2,1)S(1)}, bf16[128,1024]{1,0:T(8,128)(2,1)S(1)}, u32[]{:S(2)}, u32[]{:S(2)}) collective-permute-start(bf16[128,1024]{1,0:T(8,128)(2,1)S(1)} %join_blocks.3.refs_0_), channel_id=1, source_target_pairs={{0,4},{4,8},{8,12},{12,0},{1,5},{5,9},{9,13},{13,1},{2,6},{6,10},{... | collective-permute-start | bytes 786440 | tf_op jit(solution)/shard_map/ppermute | solution.py:32
  10.1 3.7 %all-to-all-start = ((bf16[8,136,1024]{2,1,0:T(8,128)(2,1)}), bf16[8,136,1024]{2,1,0:T(8,128)(2,1)S(1)}, u32[]{:S(2)}, u32[]{:S(2)}) async-start(bf16[8,136,1024]{2,1,0:T(8,128)(2,1)} %outgoing_rows.1), calls=%async_computation | async-start | bytes 4456448 | tf_op jit(solution)/shard_map/all_to_all | solution.py:40
  13.9 1.6 %collective-permute-start.4 = (bf16[128,1024]{1,0:T(8,128)(2,1)S(1)}, bf16[128,1024]{1,0:T(8,128)(2,1)S(1)}, u32[]{:S(2)}, u32[]{:S(2)}) collective-permute-start(bf16[128,1024]{1,0:T(8,128)(2,1)S(1)} %join_blocks.4.refs_1_), channel_id=1, source_target_pairs={{0,4},{4,8},{8,12},{12,0},{1,5},{5,9},{9,13},{13,1},{2,6},{6,10},{... | collective-permute-start | bytes 786440 | tf_op jit(solution)/shard_map/ppermute | solution.py:32
  15.5 3.5 %collective-permute-done.3.refs_0_.refs_2_ = bf16[128,1024]{1,0:T(8,128)(2,1)S(1)} collective-permute-done((bf16[128,1024]{1,0:T(8,128)(2,1)S(1)}, bf16[128,1024]{1,0:T(8,128)(2,1)S(1)}, u32[]{:S(2)}, u32[]{:S(2)}) %collective-permute-start.3) | collective-permute-done | bytes 262176 | tf_op jit(solution)/shard_map/ppermute | solution.py:32
  19.0 5.6 %collective-permute-done.4.refs_3_ = bf16[128,1024]{1,0:T(8,128)(2,1)S(1)} collective-permute-done((bf16[128,1024]{1,0:T(8,128)(2,1)S(1)}, bf16[128,1024]{1,0:T(8,128)(2,1)S(1)}, u32[]{:S(2)}, u32[]{:S(2)}) %collective-permute-start.4) | collective-permute-done | bytes 262176 | tf_op jit(solution)/shard_map/ppermute | solution.py:32
  25.9 9.6 %collective-permute-done.6.refs_5_ = bf16[128,1024]{1,0:T(8,128)(2,1)S(1)} collective-permute-done((bf16[128,1024]{1,0:T(8,128)(2,1)S(1)}, bf16[128,1024]{1,0:T(8,128)(2,1)S(1)}, u32[]{:S(2)}, u32[]{:S(2)}) %collective-permute-start.6) | collective-permute-done | bytes 262176 | tf_op jit(solution)/shard_map/ppermute | solution.py:32
  36.4 1.6 %collective-permute-start.10 = (bf16[64,1024]{1,0:T(8,128)(2,1)}, bf16[64,1024]{1,0:T(8,128)(2,1)}, u32[]{:S(2)}, u32[]{:S(2)}) collective-permute-start(bf16[64,1024]{1,0:T(8,128)(2,1)} %get-tuple-element.29), channel_id=1, source_target_pairs={{0,2},{1,3},{2,0},{3,1},{4,6},{5,7},{6,4},{7,5},{8,10},{9,11},{10,... | collective-permute-start | bytes 393224 | tf_op jit(solution)/shard_map/ppermute | solution.py:28
  38.3 3.0 %collective-permute-done.5.refs_4_ = bf16[128,1024]{1,0:T(8,128)(2,1)} collective-permute-done((bf16[128,1024]{1,0:T(8,128)(2,1)S(1)}, bf16[128,1024]{1,0:T(8,128)(2,1)}, u32[]{:S(2)}, u32[]{:S(2)}) %collective-permute-start.5) | collective-permute-done | bytes 262176 | tf_op jit(solution)/shard_map/ppermute | solution.py:32
  41.3 2.1 %collective-permute-done.11 = bf16[64,1024]{1,0:T(8,128)(2,1)} collective-permute-done((bf16[64,1024]{1,0:T(8,128)(2,1)}, bf16[64,1024]{1,0:T(8,128)(2,1)}, u32[]{:S(2)}, u32[]{:S(2)}) %collective-permute-start.11) | collective-permute-done | bytes 131104 | tf_op jit(solution)/shard_map/ppermute | solution.py:28
  43.3 3.3 %collective-permute-done.10 = bf16[64,1024]{1,0:T(8,128)(2,1)} collective-permute-done((bf16[64,1024]{1,0:T(8,128)(2,1)}, bf16[64,1024]{1,0:T(8,128)(2,1)}, u32[]{:S(2)}, u32[]{:S(2)}) %collective-permute-start.10) | collective-permute-done | bytes 131104 | tf_op jit(solution)/shard_map/ppermute | solution.py:28
  47.6 1.6 %collective-permute-start.13 = (bf16[128,1024]{1,0:T(8,128)(2,1)S(1)}, bf16[128,1024]{1,0:T(8,128)(2,1)}, u32[]{:S(2)}, u32[]{:S(2)}) collective-permute-start(bf16[128,1024]{1,0:T(8,128)(2,1)S(1)} %pad_maximum_fusion.1.refs_1_), channel_id=1, source_target_pairs={{0,4},{4,8},{8,12},{12,0},{1,5},{5,9},{9,13},{13,1},{2,6},{6,10},{... | collective-permute-start | bytes 786440 | tf_op jit(solution)/shard_map/ppermute | solution.py:32
  52.6 6.2 %collective-permute-done.13.refs_3_ = bf16[128,1024]{1,0:T(8,128)(2,1)} collective-permute-done((bf16[128,1024]{1,0:T(8,128)(2,1)S(1)}, bf16[128,1024]{1,0:T(8,128)(2,1)}, u32[]{:S(2)}, u32[]{:S(2)}) %collective-permute-start.13) | collective-permute-done | bytes 262176 | tf_op jit(solution)/shard_map/ppermute | solution.py:32
  61.7 4.5 %down_product.1 = (f32[8,64,128]{2,1,0:T(8,128)}, f32[8,128,128]{2,1,0:T(8,128)S(1)}) custom-call(s32[16]{0:T(128)S(1)} %add.61.labels_ref, bf16[8,136,1024]{2,1,0:T(8,128)(2,1)S(1)} %all-to-all-done.rows_ref, bf16[128,1024]{1,0:T(8,128)(2,1)S(1)} %join_blocks.3.refs_0_, bf16[128,1024]{1,0:T(8,128)(2,1)S(1)} %join_blocks.4.refs_1_, ...), custom_call_target="tpu_custom_call" | custom-call | flops 2147483648 | bytes 4194304 | tf_op jit(solution)/shard_map/down_product/pallas_call | solution.py:150
  68.3 3.4 %all-to-all-start.1 = ((f32[8,64,128]{2,1,0:T(8,128)}), f32[8,64,128]{2,1,0:T(8,128)S(1)}, u32[]{:S(2)}, u32[]{:S(2)}) async-start(f32[8,64,128]{2,1,0:T(8,128)} %get-tuple-element.25), calls=%async_computation.1 | async-start | bytes 524288 | tf_op jit(solution)/shard_map/all_to_all | solution.py:40
  72.1 3.1 %collective-permute-done.14.refs_4_ = bf16[128,1024]{1,0:T(8,128)(2,1)S(1)} collective-permute-done((bf16[128,1024]{1,0:T(8,128)(2,1)}, bf16[128,1024]{1,0:T(8,128)(2,1)S(1)}, u32[]{:S(2)}, u32[]{:S(2)}) %collective-permute-start.14) | collective-permute-done | bytes 262176 | tf_op jit(solution)/shard_map/ppermute | solution.py:32
  75.4 2.3 %all-to-all-done.1.terms_ref = f32[8,64,128]{2,1,0:T(8,128)S(1)} async-done(((f32[8,64,128]{2,1,0:T(8,128)}), f32[8,64,128]{2,1,0:T(8,128)S(1)}, u32[]{:S(2)}, u32[]{:S(2)}) %all-to-all-start.1) | async-done | bytes 262176 | tf_op jit(solution)/shard_map/all_to_all | solution.py:40
  78.3 3.4 %all-to-all-start.2 = ((bf16[8,64,128]{2,1,0:T(8,128)(2,1)}), bf16[8,64,128]{2,1,0:T(8,128)(2,1)S(1)}, u32[]{:S(2)}, u32[]{:S(2)}) async-start(bf16[8,64,128]{2,1,0:T(8,128)(2,1)} %summed_copies.1), calls=%async_computation.2 | async-start | bytes 262144 | tf_op jit(solution)/shard_map/all_to_all | solution.py:40
  82.9 3.9 %all-to-all-done.2.shrunk_ref = bf16[8,64,128]{2,1,0:T(8,128)(2,1)S(1)} async-done(((bf16[8,64,128]{2,1,0:T(8,128)(2,1)}), bf16[8,64,128]{2,1,0:T(8,128)(2,1)S(1)}, u32[]{:S(2)}, u32[]{:S(2)}) %all-to-all-start.2) | async-done | bytes 131104 | tf_op jit(solution)/shard_map/all_to_all | solution.py:40
  89.0 4.0 %up_product.1 = (bf16[128,1024]{1,0:T(8,128)(2,1)S(1)}, bf16[128,1024]{1,0:T(8,128)(2,1)S(1)}, bf16[128,1024]{1,0:T(8,128)(2,1)S(1)}, bf16[128,1024]{1,0:T(8,128...) custom-call(s32[16]{0:T(128)S(1)} %add.61.labels_ref, ...), custom_call_target="tpu_custom_call" | custom-call | flops 2147483648 | bytes 4194304 | tf_op jit(solution)/shard_map/up_product/pallas_call | solution.py:225
  93.1 1.7 %collective-permute-start.19 = (bf16[128,1024]{1,0:T(8,128)(2,1)S(1)}, bf16[128,1024]{1,0:T(8,128)(2,1)S(1)}, u32[]{:S(2)}, u32[]{:S(2)}) collective-permute-start(bf16[128,1024]{1,0:T(8,128)(2,1)S(1)} %get-tuple-element.35), channel_id=1, source_target_pairs={{0,2},{1,3},{2,0},{3,1},{16,18},{17,19},{18,16},{19,17},{4,6},{5,7... | collective-permute-start | bytes 786440 | tf_op jit(solution)/shard_map/ppermute | solution.py:28
  94.9 1.7 %collective-permute-start.21 = (bf16[128,1024]{1,0:T(8,128)(2,1)S(1)}, bf16[128,1024]{1,0:T(8,128)(2,1)S(1)}, u32[]{:S(2)}, u32[]{:S(2)}) collective-permute-start(bf16[128,1024]{1,0:T(8,128)(2,1)S(1)} %get-tuple-element.37), channel_id=1, source_target_pairs={{0,16},{1,17},{2,18},{3,19},{16,0},{17,1},{18,2},{19,3},{4,20},{5,... | collective-permute-start | bytes 786440 | tf_op jit(solution)/shard_map/ppermute | solution.py:28
  96.7 2.6 %collective-permute-start.23 = (bf16[128,1024]{1,0:T(8,128)(2,1)S(1)}, bf16[128,1024]{1,0:T(8,128)(2,1)S(1)}, u32[]{:S(2)}, u32[]{:S(2)}) collective-permute-start(bf16[128,1024]{1,0:T(8,128)(2,1)S(1)} %get-tuple-element.39), channel_id=1, source_target_pairs={{0,18},{1,19},{2,16},{3,17},{16,2},{17,3},{18,0},{19,1},{4,22},{5,... | collective-permute-start | bytes 786440 | tf_op jit(solution)/shard_map/ppermute | solution.py:28
  99.2 3.0 %collective-permute-done.19.refs_2_ = bf16[128,1024]{1,0:T(8,128)(2,1)S(1)} collective-permute-done((bf16[128,1024]{1,0:T(8,128)(2,1)S(1)}, bf16[128,1024]{1,0:T(8,128)(2,1)S(1)}, u32[]{:S(2)}, u32[]{:S(2)}) %collective-permute-start.19) | collective-permute-done | bytes 262176 | tf_op jit(solution)/shard_map/ppermute | solution.py:28
  102.2 1.4 %collective-permute-start.24 = (bf16[128,1024]{1,0:T(8,128)(2,1)S(1)}, bf16[128,1024]{1,0:T(8,128)(2,1)S(1)}, u32[]{:S(2)}, u32[]{:S(2)}) collective-permute-start(bf16[128,1024]{1,0:T(8,128)(2,1)S(1)} %get-tuple-element.40), channel_id=1, source_target_pairs={{0,19},{1,18},{2,17},{3,16},{16,3},{17,2},{18,1},{19,0},{4,23},{5,... | collective-permute-start | bytes 786440 | tf_op jit(solution)/shard_map/ppermute | solution.py:28
  103.7 3.3 %collective-permute-done.20.refs_3_ = bf16[128,1024]{1,0:T(8,128)(2,1)S(1)} collective-permute-done((bf16[128,1024]{1,0:T(8,128)(2,1)S(1)}, bf16[128,1024]{1,0:T(8,128)(2,1)S(1)}, u32[]{:S(2)}, u32[]{:S(2)}) %collective-permute-start.20) | collective-permute-done | bytes 262176 | tf_op jit(solution)/shard_map/ppermute | solution.py:28
  107.0 1.9 %collective-permute-done.22.refs_5_ = bf16[128,1024]{1,0:T(8,128)(2,1)S(1)} collective-permute-done((bf16[128,1024]{1,0:T(8,128)(2,1)S(1)}, bf16[128,1024]{1,0:T(8,128)(2,1)S(1)}, u32[]{:S(2)}, u32[]{:S(2)}) %collective-permute-start.22) | collective-permute-done | bytes 262176 | tf_op jit(solution)/shard_map/ppermute | solution.py:28
  108.9 7.5 %collective-permute-done.23.refs_6_ = bf16[128,1024]{1,0:T(8,128)(2,1)S(1)} collective-permute-done((bf16[128,1024]{1,0:T(8,128)(2,1)S(1)}, bf16[128,1024]{1,0:T(8,128)(2,1)S(1)}, u32[]{:S(2)}, u32[]{:S(2)}) %collective-permute-start.23) | collective-permute-done | bytes 262176 | tf_op jit(solution)/shard_map/ppermute | solution.py:28
  116.4 4.5 %collective-permute-done.24.refs_7_ = bf16[128,1024]{1,0:T(8,128)(2,1)S(1)} collective-permute-done((bf16[128,1024]{1,0:T(8,128)(2,1)S(1)}, bf16[128,1024]{1,0:T(8,128)(2,1)S(1)}, u32[]{:S(2)}, u32[]{:S(2)}) %collective-permute-start.24) | collective-permute-done | bytes 262176 | tf_op jit(solution)/shard_map/ppermute | solution.py:28
  120.9 1.4 %place_results.1 = bf16[128,8192]{1,0:T(8,128)(2,1)} custom-call(s32[1]{0:T(128)} %bitcast.me_ref, bf16[128,1024]{1,0:T(8,128)(2,1)S(1)} %get-tuple-element.33.refs_0_, bf16[128,1024]{1,0:T(8,128)(2,1)S(1)} %collective-permute-done.18.refs_1_, bf16[128,1024]{1,0:T(8,128)(2,1)S(1)} %collective-permute-done.19.refs_2_, ...), custom_call_target="tpu_custom_call" | custom-call | tf_op jit(solution)/shard_map/place_results/pallas_call | solution.py:260
  (61 shorter events, 19.1 us)
Async XLA Ops:
  1.1 7.1 %collective-permute-start = (bf16[64,1024]{1,0:T(8,128)(2,1)S(1)}, bf16[64,1024]{1,0:T(8,128)(2,1)S(1)}, u32[]{:S(2)}, u32[]{:S(2)}) collective-permute-start(bf16[64,1024]{1,0:T(8,128)(2,1)S(1)} %get-tuple-element.46), channel_id=1, source_target_pairs={{0,1},{1,0},{2,3},{3,2},{4,5},{5,4},{6,7},{7,6},{8,9},{9,8},{10,11... | collective-permute-start | bytes 393224 | tf_op jit(solution)/shard_map/ppermute | solution.py:28
  1.7 12.1 %collective-permute-start.1 = (bf16[64,1024]{1,0:T(8,128)(2,1)S(1)}, bf16[64,1024]{1,0:T(8,128)(2,1)S(1)}, u32[]{:S(2)}, u32[]{:S(2)}) collective-permute-start(bf16[64,1024]{1,0:T(8,128)(2,1)S(1)} %get-tuple-element.48), channel_id=1, source_target_pairs={{0,2},{1,3},{2,0},{3,1},{4,6},{5,7},{6,4},{7,5},{8,10},{9,11},{10,... | collective-permute-start | bytes 393224 | tf_op jit(solution)/shard_map/ppermute | solution.py:28
  4.3 9.6 %collective-permute-start.2 = (bf16[64,1024]{1,0:T(8,128)(2,1)S(1)}, bf16[64,1024]{1,0:T(8,128)(2,1)S(1)}, u32[]{:S(2)}, u32[]{:S(2)}) collective-permute-start(bf16[64,1024]{1,0:T(8,128)(2,1)S(1)} %get-tuple-element.45), channel_id=1, source_target_pairs={{0,3},{1,2},{2,1},{3,0},{4,7},{5,6},{6,5},{7,4},{8,11},{9,10},{10,... | collective-permute-start | bytes 393224 | tf_op jit(solution)/shard_map/ppermute | solution.py:28
  4.3 1.6 %copy-start = (bf16[128,8192]{1,0:T(8,128)(2,1)S(1)}, bf16[128,8192]{1,0:T(8,128)(2,1)}, u32[]{:S(2)}) copy-start(bf16[128,8192]{1,0:T(8,128)(2,1)} %hidden_ref.1) | copy-start | bytes 6291460
  8.2 10.7 %collective-permute-start.3 = (bf16[128,1024]{1,0:T(8,128)(2,1)S(1)}, bf16[128,1024]{1,0:T(8,128)(2,1)S(1)}, u32[]{:S(2)}, u32[]{:S(2)}) collective-permute-start(bf16[128,1024]{1,0:T(8,128)(2,1)S(1)} %join_blocks.3.refs_0_), channel_id=1, source_target_pairs={{0,4},{4,8},{8,12},{12,0},{1,5},{5,9},{9,13},{13,1},{2,6},{6,10},{... | collective-permute-start | bytes 786440 | tf_op jit(solution)/shard_map/ppermute | solution.py:32
  10.1 48.7 %all-to-all-start = ((bf16[8,136,1024]{2,1,0:T(8,128)(2,1)}), bf16[8,136,1024]{2,1,0:T(8,128)(2,1)S(1)}, u32[]{:S(2)}, u32[]{:S(2)}) async-start(bf16[8,136,1024]{2,1,0:T(8,128)(2,1)} %outgoing_rows.1), calls=%async_computation | async-start | bytes 4456448 | tf_op jit(solution)/shard_map/all_to_all | solution.py:40
  13.8 21.7 %copy-start.10 = (bf16[1,64,8192]{2,1,0:T(8,128)(2,1)S(1)}, bf16[1,64,8192]{2,1,0:T(8,128)(2,1)}, u32[]{:S(2)}) copy-start(bf16[1,64,8192]{2,1,0:T(8,128)(2,1)} %param.7) | copy-start | bytes 3145732
  13.9 10.7 %collective-permute-start.4 = (bf16[128,1024]{1,0:T(8,128)(2,1)S(1)}, bf16[128,1024]{1,0:T(8,128)(2,1)S(1)}, u32[]{:S(2)}, u32[]{:S(2)}) collective-permute-start(bf16[128,1024]{1,0:T(8,128)(2,1)S(1)} %join_blocks.4.refs_1_), channel_id=1, source_target_pairs={{0,4},{4,8},{8,12},{12,0},{1,5},{5,9},{9,13},{13,1},{2,6},{6,10},{... | collective-permute-start | bytes 786440 | tf_op jit(solution)/shard_map/ppermute | solution.py:32
  24.5 11.0 %collective-permute-start.6 = (bf16[128,1024]{1,0:T(8,128)(2,1)S(1)}, bf16[128,1024]{1,0:T(8,128)(2,1)S(1)}, u32[]{:S(2)}, u32[]{:S(2)}) collective-permute-start(bf16[128,1024]{1,0:T(8,128)(2,1)S(1)} %collective-permute-done.4.refs_3_), channel_id=1, source_target_pairs={{0,4},{4,8},{8,12},{12,0},{1,5},{5,9},{9,13},{13,1},{2,6},{6,10},{... | collective-permute-start | bytes 786440 | tf_op jit(solution)/shard_map/ppermute | solution.py:32
  25.2 16.0 %collective-permute-start.5 = (bf16[128,1024]{1,0:T(8,128)(2,1)S(1)}, bf16[128,1024]{1,0:T(8,128)(2,1)}, u32[]{:S(2)}, u32[]{:S(2)}) collective-permute-start(bf16[128,1024]{1,0:T(8,128)(2,1)S(1)} %join_blocks.5), channel_id=1, source_target_pairs={{0,4},{4,8},{8,12},{12,0},{1,5},{5,9},{9,13},{13,1},{2,6},{6,10},{... | collective-permute-start | bytes 786440 | tf_op jit(solution)/shard_map/ppermute | solution.py:32
  35.5 13.7 %copy-start.4 = (bf16[128,1024]{1,0:T(8,128)(2,1)}, bf16[128,1024]{1,0:T(8,128)(2,1)S(1)}, u32[]{:S(2)}) copy-start(bf16[128,1024]{1,0:T(8,128)(2,1)S(1)} %collective-permute-done.6.refs_5_) | copy-start | bytes 786436
  35.5 12.1 %collective-permute-start.8 = (bf16[128,1024]{1,0:T(8,128)(2,1)S(1)}, bf16[128,1024]{1,0:T(8,128)(2,1)}, u32[]{:S(2)}, u32[]{:S(2)}) collective-permute-start(bf16[128,1024]{1,0:T(8,128)(2,1)S(1)} %collective-permute-done.6.refs_5_), channel_id=1, source_target_pairs={{0,4},{4,8},{8,12},{12,0},{1,5},{5,9},{9,13},{13,1},{2,6},{6,10},{... | collective-permute-start | bytes 786440 | tf_op jit(solution)/shard_map/ppermute | solution.py:32
  36.4 6.9 %collective-permute-start.11 = (bf16[64,1024]{1,0:T(8,128)(2,1)}, bf16[64,1024]{1,0:T(8,128)(2,1)}, u32[]{:S(2)}, u32[]{:S(2)}) collective-permute-start(bf16[64,1024]{1,0:T(8,128)(2,1)} %get-tuple-element.30), channel_id=1, source_target_pairs={{0,3},{1,2},{2,1},{3,0},{4,7},{5,6},{6,5},{7,4},{8,11},{9,10},{10,... | collective-permute-start | bytes 393224 | tf_op jit(solution)/shard_map/ppermute | solution.py:28
  36.4 10.2 %collective-permute-start.10 = (bf16[64,1024]{1,0:T(8,128)(2,1)}, bf16[64,1024]{1,0:T(8,128)(2,1)}, u32[]{:S(2)}, u32[]{:S(2)}) collective-permute-start(bf16[64,1024]{1,0:T(8,128)(2,1)} %get-tuple-element.29), channel_id=1, source_target_pairs={{0,2},{1,3},{2,0},{3,1},{4,6},{5,7},{6,4},{7,5},{8,10},{9,11},{10,... | collective-permute-start | bytes 393224 | tf_op jit(solution)/shard_map/ppermute | solution.py:28
  38.1 11.2 %collective-permute-start.9 = (bf16[64,1024]{1,0:T(8,128)(2,1)}, bf16[64,1024]{1,0:T(8,128)(2,1)S(1)}, u32[]{:S(2)}, u32[]{:S(2)}) collective-permute-start(bf16[64,1024]{1,0:T(8,128)(2,1)} %get-tuple-element.27), channel_id=1, source_target_pairs={{0,1},{1,0},{2,3},{3,2},{4,5},{5,4},{6,7},{7,6},{8,9},{9,8},{10,11... | collective-permute-start | bytes 393224 | tf_op jit(solution)/shard_map/ppermute | solution.py:28
  41.2 10.0 %collective-permute-start.7 = (bf16[128,1024]{1,0:T(8,128)(2,1)}, bf16[128,1024]{1,0:T(8,128)(2,1)S(1)}, u32[]{:S(2)}, u32[]{:S(2)}) collective-permute-start(bf16[128,1024]{1,0:T(8,128)(2,1)} %collective-permute-done.5.refs_4_), channel_id=1, source_target_pairs={{0,4},{4,8},{8,12},{12,0},{1,5},{5,9},{9,13},{13,1},{2,6},{6,10},{... | collective-permute-start | bytes 786440 | tf_op jit(solution)/shard_map/ppermute | solution.py:32
  47.6 11.2 %collective-permute-start.13 = (bf16[128,1024]{1,0:T(8,128)(2,1)S(1)}, bf16[128,1024]{1,0:T(8,128)(2,1)}, u32[]{:S(2)}, u32[]{:S(2)}) collective-permute-start(bf16[128,1024]{1,0:T(8,128)(2,1)S(1)} %pad_maximum_fusion.1.refs_1_), channel_id=1, source_target_pairs={{0,4},{4,8},{8,12},{12,0},{1,5},{5,9},{9,13},{13,1},{2,6},{6,10},{... | collective-permute-start | bytes 786440 | tf_op jit(solution)/shard_map/ppermute | solution.py:32
  52.0 15.0 %collective-permute-start.12 = (bf16[128,1024]{1,0:T(8,128)(2,1)S(1)}, bf16[128,1024]{1,0:T(8,128)(2,1)}, u32[]{:S(2)}, u32[]{:S(2)}) collective-permute-start(bf16[128,1024]{1,0:T(8,128)(2,1)S(1)} %pad_maximum_fusion.refs_0_), channel_id=1, source_target_pairs={{0,4},{4,8},{8,12},{12,0},{1,5},{5,9},{9,13},{13,1},{2,6},{6,10},{... | collective-permute-start | bytes 786440 | tf_op jit(solution)/shard_map/ppermute | solution.py:32
  58.8 12.9 %collective-permute-start.15 = (bf16[128,1024]{1,0:T(8,128)(2,1)}, bf16[128,1024]{1,0:T(8,128)(2,1)}, u32[]{:S(2)}, u32[]{:S(2)}) collective-permute-start(bf16[128,1024]{1,0:T(8,128)(2,1)} %collective-permute-done.13.refs_3_), channel_id=1, source_target_pairs={{0,4},{4,8},{8,12},{12,0},{1,5},{5,9},{9,13},{13,1},{2,6},{6,10},{... | collective-permute-start | bytes 786440 | tf_op jit(solution)/shard_map/ppermute | solution.py:32
  66.9 8.4 %collective-permute-start.14 = (bf16[128,1024]{1,0:T(8,128)(2,1)}, bf16[128,1024]{1,0:T(8,128)(2,1)S(1)}, u32[]{:S(2)}, u32[]{:S(2)}) collective-permute-start(bf16[128,1024]{1,0:T(8,128)(2,1)} %collective-permute-done.12.refs_2_), channel_id=1, source_target_pairs={{0,4},{4,8},{8,12},{12,0},{1,5},{5,9},{9,13},{13,1},{2,6},{6,10},{... | collective-permute-start | bytes 786440 | tf_op jit(solution)/shard_map/ppermute | solution.py:32
  68.3 9.4 %all-to-all-start.1 = ((f32[8,64,128]{2,1,0:T(8,128)}), f32[8,64,128]{2,1,0:T(8,128)S(1)}, u32[]{:S(2)}, u32[]{:S(2)}) async-start(f32[8,64,128]{2,1,0:T(8,128)} %get-tuple-element.25), calls=%async_computation.1 | async-start | bytes 524288 | tf_op jit(solution)/shard_map/all_to_all | solution.py:40
  71.7 11.2 %collective-permute-start.17 = (bf16[128,1024]{1,0:T(8,128)(2,1)}, bf16[128,1024]{1,0:T(8,128)(2,1)S(1)}, u32[]{:S(2)}, u32[]{:S(2)}) collective-permute-start(bf16[128,1024]{1,0:T(8,128)(2,1)} %collective-permute-done.15.refs_5_), channel_id=1, source_target_pairs={{0,4},{4,8},{8,12},{12,0},{1,5},{5,9},{9,13},{13,1},{2,6},{6,10},{... | collective-permute-start | bytes 786440 | tf_op jit(solution)/shard_map/ppermute | solution.py:32
  75.3 12.6 %collective-permute-start.16 = (bf16[128,1024]{1,0:T(8,128)(2,1)S(1)}, bf16[128,1024]{1,0:T(8,128)(2,1)S(1)}, u32[]{:S(2)}, u32[]{:S(2)}) collective-permute-start(bf16[128,1024]{1,0:T(8,128)(2,1)S(1)} %collective-permute-done.14.refs_4_), channel_id=1, source_target_pairs={{0,4},{4,8},{8,12},{12,0},{1,5},{5,9},{9,13},{13,1},{2,6},{6,10},{... | collective-permute-start | bytes 786440 | tf_op jit(solution)/shard_map/ppermute | solution.py:32
  78.3 8.5 %all-to-all-start.2 = ((bf16[8,64,128]{2,1,0:T(8,128)(2,1)}), bf16[8,64,128]{2,1,0:T(8,128)(2,1)S(1)}, u32[]{:S(2)}, u32[]{:S(2)}) async-start(bf16[8,64,128]{2,1,0:T(8,128)(2,1)} %summed_copies.1), calls=%async_computation.2 | async-start | bytes 262144 | tf_op jit(solution)/shard_map/all_to_all | solution.py:40
  87.9 1.0 copy-start.9
  93.0 3.7 %collective-permute-start.18 = (bf16[128,1024]{1,0:T(8,128)(2,1)S(1)}, bf16[128,1024]{1,0:T(8,128)(2,1)S(1)}, u32[]{:S(2)}, u32[]{:S(2)}) collective-permute-start(bf16[128,1024]{1,0:T(8,128)(2,1)S(1)} %get-tuple-element.34), channel_id=1, source_target_pairs={{0,1},{1,0},{2,3},{3,2},{16,17},{17,16},{18,19},{19,18},{4,5},{5,4... | collective-permute-start | bytes 786440 | tf_op jit(solution)/shard_map/ppermute | solution.py:28
  93.1 9.2 %collective-permute-start.19 = (bf16[128,1024]{1,0:T(8,128)(2,1)S(1)}, bf16[128,1024]{1,0:T(8,128)(2,1)S(1)}, u32[]{:S(2)}, u32[]{:S(2)}) collective-permute-start(bf16[128,1024]{1,0:T(8,128)(2,1)S(1)} %get-tuple-element.35), channel_id=1, source_target_pairs={{0,2},{1,3},{2,0},{3,1},{16,18},{17,19},{18,16},{19,17},{4,6},{5,7... | collective-permute-start | bytes 786440 | tf_op jit(solution)/shard_map/ppermute | solution.py:28
  94.8 12.2 %collective-permute-start.20 = (bf16[128,1024]{1,0:T(8,128)(2,1)S(1)}, bf16[128,1024]{1,0:T(8,128)(2,1)S(1)}, u32[]{:S(2)}, u32[]{:S(2)}) collective-permute-start(bf16[128,1024]{1,0:T(8,128)(2,1)S(1)} %get-tuple-element.36), channel_id=1, source_target_pairs={{0,3},{1,2},{2,1},{3,0},{16,19},{17,18},{18,17},{19,16},{4,7},{5,6... | collective-permute-start | bytes 786440 | tf_op jit(solution)/shard_map/ppermute | solution.py:28
  94.9 12.0 %collective-permute-start.21 = (bf16[128,1024]{1,0:T(8,128)(2,1)S(1)}, bf16[128,1024]{1,0:T(8,128)(2,1)S(1)}, u32[]{:S(2)}, u32[]{:S(2)}) collective-permute-start(bf16[128,1024]{1,0:T(8,128)(2,1)S(1)} %get-tuple-element.37), channel_id=1, source_target_pairs={{0,16},{1,17},{2,18},{3,19},{16,0},{17,1},{18,2},{19,3},{4,20},{5,... | collective-permute-start | bytes 786440 | tf_op jit(solution)/shard_map/ppermute | solution.py:28
  96.6 12.3 %collective-permute-start.22 = (bf16[128,1024]{1,0:T(8,128)(2,1)S(1)}, bf16[128,1024]{1,0:T(8,128)(2,1)S(1)}, u32[]{:S(2)}, u32[]{:S(2)}) collective-permute-start(bf16[128,1024]{1,0:T(8,128)(2,1)S(1)} %get-tuple-element.38), channel_id=1, source_target_pairs={{0,17},{1,16},{2,19},{3,18},{16,1},{17,0},{18,3},{19,2},{4,21},{5,... | collective-permute-start | bytes 786440 | tf_op jit(solution)/shard_map/ppermute | solution.py:28
  96.7 19.7 %collective-permute-start.23 = (bf16[128,1024]{1,0:T(8,128)(2,1)S(1)}, bf16[128,1024]{1,0:T(8,128)(2,1)S(1)}, u32[]{:S(2)}, u32[]{:S(2)}) collective-permute-start(bf16[128,1024]{1,0:T(8,128)(2,1)S(1)} %get-tuple-element.39), channel_id=1, source_target_pairs={{0,18},{1,19},{2,16},{3,17},{16,2},{17,3},{18,0},{19,1},{4,22},{5,... | collective-permute-start | bytes 786440 | tf_op jit(solution)/shard_map/ppermute | solution.py:28
  102.2 18.6 %collective-permute-start.24 = (bf16[128,1024]{1,0:T(8,128)(2,1)S(1)}, bf16[128,1024]{1,0:T(8,128)(2,1)S(1)}, u32[]{:S(2)}, u32[]{:S(2)}) collective-permute-start(bf16[128,1024]{1,0:T(8,128)(2,1)S(1)} %get-tuple-element.40), channel_id=1, source_target_pairs={{0,19},{1,18},{2,17},{3,16},{16,3},{17,2},{18,1},{19,0},{4,23},{5,... | collective-permute-start | bytes 786440 | tf_op jit(solution)/shard_map/ppermute | solution.py:28
  (7 other events, 5.7 us)

commit v16 on v15

--- a/solution.py
+++ b/solution.py
@@ -12,11 +12,10 @@
 PLANE = ("groups", "inner")
 LANES = 128
 ID_ROWS = 8
-AHEAD, SLIGHTLY_AHEAD = 10**11, 5 * 10**9
+AHEAD, SLIGHTLY_AHEAD, SUM_AHEAD = 10**11, 3 * 10**9, 4 * 10**9
 BLOCK = 8
 IN_VMEM = pl.BlockSpec(memory_space=pltpu.VMEM)
 IN_SMEM = pl.BlockSpec(memory_space=pltpu.SMEM)
-IN_HBM = pl.BlockSpec(memory_space=pltpu.HBM)
 ANYWHERE = pl.BlockSpec(memory_space=pl.ANY)
 
 
@@ -104,7 +103,7 @@
 
 
 def down_kernel(map_count, rank, labels_ref, rows_ref, *refs):
-    maps, (packed_ref, ids_out, total_ref, ids_ref, sem) = refs[:map_count], refs[map_count:]
+    maps, (packed_ref, id_rows_ref, total_ref, ids_ref) = refs[:map_count], refs[map_count:]
     members, rows, share = rows_ref.shape
     tok = rows - ID_ROWS
     block = min(BLOCK, members)
@@ -115,12 +114,10 @@
         first = step * block
         for n in range(block):
             row = rows_ref[first + n, tok : tok + 1, :LANES].astype(jnp.float32)
-            ids_ref[first + n] = jnp.broadcast_to(row, (LANES, tok)).T
+            id_rows_ref[pl.ds(first + n, 1), :] = row
+            ids_ref[n] = jnp.broadcast_to(row, (LANES, tok)).T
         tokens = rows_ref[pl.ds(first, block), :tok, :].reshape(block * tok, share)
-        here = pl.ds(first, block)
-        kept = pltpu.make_async_copy(ids_ref.at[here], ids_out.at[here], sem)
-        kept.start()
-        ids = ids_ref[here].reshape(block * tok, LANES)
+        ids = ids_ref[...].reshape(block * tok, LANES)
         tile = 0
         for at in range(0, map_count, 2):
             some = jnp.concatenate([m[...] for m in maps[at : at + 2]], axis=0)
@@ -137,7 +134,6 @@
             total = total_ref[n * tok : (n + 1) * tok, :]
             total += pltpu.roll(total, LANES // 2, 1)
             packed_ref[first + n] = jnp.where(lane < rank, total[:half], total[half:])
-        kept.wait()
         return 0
 
     lax.fori_loop(0, members // block, one, 0)
@@ -151,16 +147,15 @@
         functools.partial(down_kernel, len(maps), rank),
         out_shape=[
             jax.ShapeDtypeStruct((members, tok // 2, LANES), jnp.float32),
-            jax.ShapeDtypeStruct((members, tok, LANES), jnp.float32),
+            jax.ShapeDtypeStruct((members, tok), jnp.float32),
         ],
         in_specs=[IN_SMEM, IN_VMEM] + [IN_VMEM] * len(maps),
-        out_specs=[IN_VMEM, IN_HBM],
+        out_specs=[IN_VMEM, IN_VMEM],
         scratch_shapes=[
             pltpu.VMEM((min(BLOCK, members) * tok, LANES), jnp.float32),
-            pltpu.VMEM((members, tok, LANES), jnp.float32),
-            pltpu.SemaphoreType.DMA,
+            pltpu.VMEM((min(BLOCK, members), tok, LANES), jnp.float32),
         ],
-        compiler_params=params(8 * members * tok * LANES),
+        compiler_params=params(8 * min(BLOCK, members) * tok * LANES),
         cost_estimate=pl.CostEstimate(
             flops=2 * map_rows * members * tok * share,
             bytes_accessed=2 * share * (map_rows + members * tok),
@@ -183,6 +178,7 @@
         in_specs=[IN_VMEM],
         out_specs=IN_VMEM,
         compiler_params=params(),
+        cost_estimate=pl.CostEstimate(flops=SUM_AHEAD, bytes_accessed=10**6, transcendentals=0),
         name="summed_copies",
     )(terms)
 
@@ -190,15 +186,12 @@
 def up_kernel(map_count, rank, labels_ref, me_ref, ids_ref, shrunk_ref, *refs):
     members, half, _ = shrunk_ref.shape
     maps, outs = refs[:map_count], refs[map_count : map_count + members]
-    spread_ref, ids_buf, sem = refs[map_count + members :]
-    kept = pltpu.make_async_copy(ids_ref, ids_buf, sem)
-    kept.start()
+    spread_ref = refs[-1]
     tok = 2 * half
     block = min(BLOCK, members)
     tiles = spread_ref.shape[1] // LANES
     lane = lax.broadcasted_iota(jnp.int32, (half, LANES), 1)
     held = jnp.concatenate([m[...] for m in maps], axis=0)
-    kept.wait()
     for first in range(0, members, block):
         for n in range(block):
             member = me_ref[0] ^ (first + n)
@@ -207,7 +200,7 @@
             shrunk = jnp.concatenate(
                 [jnp.where(lane < rank, packed, turned), jnp.where(lane < rank, turned, packed)], axis=0
             )
-            ids = ids_buf[member]
+            ids = jnp.broadcast_to(ids_ref[pl.ds(member, 1), :], (LANES, tok)).T
             for tile in range(tiles):
                 named = ids == tile_labels(labels_ref, tile, rank, (1, LANES))
                 spread_ref[n * tok : (n + 1) * tok, tile * LANES : (tile + 1) * LANES] = jnp.where(
@@ -220,19 +213,15 @@
 
 
 def up_product(labels, me, ids, shrunk, maps, rank):
-    members, tok, _ = ids.shape
+    members, tok = ids.shape
     map_rows, piece = sum(m.shape[0] for m in maps), maps[0].shape[1]
     return pl.pallas_call(
         functools.partial(up_kernel, len(maps), rank),
         out_shape=[jax.ShapeDtypeStruct((tok, piece), jnp.bfloat16)] * members,
-        in_specs=[IN_SMEM, IN_SMEM, IN_HBM, IN_VMEM] + [IN_VMEM] * len(maps),
+        in_specs=[IN_SMEM, IN_SMEM, IN_VMEM, IN_VMEM] + [IN_VMEM] * len(maps),
         out_specs=[IN_VMEM] * members,
-        scratch_shapes=[
-            pltpu.VMEM((min(BLOCK, members) * tok, map_rows), jnp.bfloat16),
-            pltpu.VMEM((members, tok, LANES), jnp.float32),
-            pltpu.SemaphoreType.DMA,
-        ],
-        compiler_params=params(2 * min(BLOCK, members) * tok * map_rows + 4 * members * tok * LANES),
+        scratch_shapes=[pltpu.VMEM((min(BLOCK, members) * tok, map_rows), jnp.bfloat16)],
+        compiler_params=params(2 * min(BLOCK, members) * tok * map_rows),
         cost_estimate=pl.CostEstimate(
             flops=2 * map_rows * members * tok * piece,
             bytes_accessed=2 * piece * (map_rows + members * tok),
@@ -288,13 +277,13 @@
     def rings(near, far, first_cost=0, second_after=()):
         near, far = [near], [far]
         for step in range(1, outer):
-            block = near[-1]
-            if step == 2:
-                block = after(block, *second_after)
-                if first_cost:
-                    block = joined([block], first_cost)
-            near.append(next_on_ring(block, outer))
-            far.append(next_on_ring(far[-1], outer))
+            for blocks in near, far:
+                block = blocks[-1]
+                if step == 2:
+                    block = after(block, *second_after)
+                    if first_cost:
+                        block = joined([block], first_cost)
+                blocks.append(next_on_ring(block, outer))
         return near, far
 
     steps_back = jnp.arange(outer, dtype=jnp.int32)[:, None]
@@ -311,7 +300,7 @@
     up = exchanged([after(block, down_near[1]) for block in slices(adapter_up_maps[0])])
 
     down_maps = [m for pair in zip(down_near, down_far) for m in pair]
-    packed, id_columns = down_product(labels, rows, down_maps, rank)
+    packed, id_rows = down_product(labels, rows, down_maps, rank)
     up_near, up_far = rings(
         after(jnp.concatenate(up[:middle], axis=0), down_near[-1]),
         after(jnp.concatenate(up[middle:], axis=0), down_far[-1]),
@@ -319,9 +308,10 @@
     )
     up_maps = [m for pair in zip(up_near, up_far) for m in pair]
     shrunk = swap(summed_copies(swap(packed)))
-    results = list(up_product(labels, me.reshape(1), id_columns, shrunk, up_maps, rank))
-    returned = results[:1] + [to_partner(results[n], PLANE, members, n) for n in range(1, members)]
-    return place(me.reshape(1), returned)
+    results = list(up_product(labels, me.reshape(1), id_rows, shrunk, up_maps, rank))
+    order = sorted(range(1, members), key=lambda n: (-(n >= inner) - (n % inner >= 2), -(n >= inner), n))
+    returned = {n: to_partner(results[n], PLANE, members, n) for n in order}
+    return place(me.reshape(1), results[:1] + [returned[n] for n in range(1, members)])
 
 
 def solution(mesh):

time: 123 us -> 118 us (0.959)
  blocking collectives: 0 us -> 7.57 us
  starting transfers between devices: 31.3 us -> 24.9 us
  local copies, waits for them, and re-layouts: 10.4 us -> 8.5 us
  other arithmetic: 1.99 us -> 0.12 us
  waiting for transfers between devices: 66.1 us -> 64.6 us
    all_to_all x0 -> x1, blocking collectives: none -> 7.57 us  [swap(): return lax.all_to_all(value, PLANE, split_axis=0, concat_axis=0, tiled=True)]
    all_to_all x3 -> x2, waiting for transfers between devices: 6.26 us -> 0.01 us  [swap(): return lax.all_to_all(value, PLANE, split_axis=0, concat_axis=0, tiled=True)]
    ppermute x13, waiting for transfers between devices: 25.6 us -> 30.6 us  [to_partner(): return lax.ppermute(value, axes, [(i, i ^ offset) for i in range(size)])]
    all_to_all x3 -> x2, starting transfers between devices: 10.5 us -> 7.14 us  [swap(): return lax.all_to_all(value, PLANE, split_axis=0, concat_axis=0, tiled=True)]
    unnamed x22 -> x18, local copies, waits for them, and re-layouts: 8.33 us -> 6.51 us
    ppermute x13, starting transfers between devices: 12.7 us -> 11.1 us  [to_partner(): return lax.ppermute(value, axes, [(i, i ^ offset) for i in range(size)])]
    ppermute x12, starting transfers between devices: 8.17 us -> 6.7 us  [next_on_ring(): lax.ppermute(block, 'outer', [(i, (i + 1) % outer) for i in range(outer)])]
  transfers between devices with their start and end apart: 28 -> 27, of which waited for: 18 -> 16; matrix products, arithmetic and copies ran while one was open for 2% -> 1% of each run, Pallas kernels for 6% -> 6%
where the time goes in v16:
time: 118 us
  waiting for transfers between devices  64.6 us (55%)
  starting transfers between devices  24.9 us (21%)
  Pallas kernels  11.7 us (10%)
  local copies, waits for them, and re-layouts  8.5 us (7%)
  blocking collectives  7.57 us (6%)
    ppermute x12, waiting for transfers between devices, next_on_ring(): lax.ppermute(block, 'outer', [(i, (i + 1) % outer) for i in range(outer)])  34 us
    ppermute x13, waiting for transfers between devices, to_partner(): return lax.ppermute(value, axes, [(i, i ^ offset) for i in range(size)])  30.6 us
    ppermute x13, starting transfers between devices, to_partner(): return lax.ppermute(value, axes, [(i, i ^ offset) for i in range(size)])  11.1 us
    all_to_all x1, blocking collectives, swap(): return lax.all_to_all(value, PLANE, split_axis=0, concat_axis=0, tiled=True)  7.57 us
    all_to_all x2, starting transfers between devices, swap(): return lax.all_to_all(value, PLANE, split_axis=0, concat_axis=0, tiled=True)  7.14 us
    ppermute x12, starting transfers between devices, next_on_ring(): lax.ppermute(block, 'outer', [(i, (i + 1) % outer) for i in range(outer)])  6.7 us
    unnamed x18, local copies, waits for them, and re-layouts  6.51 us
    pallas_call x1, Pallas kernels, down_product(): pl.pallas_call(functools.partial(down_kernel, len(maps), rank), out_shape...  4.17 us
  transfers between devices with their start and end apart: 27, of which 16 were waited for; matrix products, arithmetic and copies ran while one was open for 1% of the time, Pallas kernels for 6%

profile of v16, /device:TPU:0, one launch (start us, length us, event | category | flops | bytes accessed | tf_op | source)
XLA Modules:
  0.0 117.7 jit_solution(12293451560993020102)
XLA Ops:
  1.7 2.6 %collective-permute-start.1 = (bf16[64,1024]{1,0:T(8,128)(2,1)S(1)}, bf16[64,1024]{1,0:T(8,128)(2,1)S(1)}, u32[]{:S(2)}, u32[]{:S(2)}) collective-permute-start(bf16[64,1024]{1,0:T(8,128)(2,1)S(1)} %get-tuple-element.50), channel_id=1, source_target_pairs={{0,2},{1,3},{2,0},{3,1},{4,6},{5,7},{6,4},{7,5},{8,10},{9,11},{10,... | collective-permute-start | bytes 393224 | tf_op jit(solution)/shard_map/ppermute | solution.py:27
  4.3 1.6 %copy-done = bf16[128,8192]{1,0:T(8,128)(2,1)S(1)} copy-done((bf16[128,8192]{1,0:T(8,128)(2,1)S(1)}, bf16[128,8192]{1,0:T(8,128)(2,1)}, u32[]{:S(2)}) %copy-start) | copy-done | bytes 2097176
  6.6 1.6 %outgoing_rows.1 = bf16[8,136,1024]{2,1,0:T(8,128)(2,1)} custom-call(bf16[128,8192]{1,0:T(8,128)(2,1)S(1)} %copy-done, s32[1,128]{1,0:T(1,128)S(1)} %bitcast.26), custom_call_target="tpu_custom_call" | custom-call | tf_op jit(solution)/shard_map/outgoing_rows/pallas_call | solution.py:94
  8.2 1.8 %collective-permute-start.3 = (bf16[128,1024]{1,0:T(8,128)(2,1)S(1)}, bf16[128,1024]{1,0:T(8,128)(2,1)S(1)}, u32[]{:S(2)}, u32[]{:S(2)}) collective-permute-start(bf16[128,1024]{1,0:T(8,128)(2,1)S(1)} %join_blocks.4.refs_0_), channel_id=1, source_target_pairs={{0,4},{4,8},{8,12},{12,0},{1,5},{5,9},{9,13},{13,1},{2,6},{6,10},{... | collective-permute-start | bytes 786440 | tf_op jit(solution)/shard_map/ppermute | solution.py:31
  10.1 3.7 %all-to-all-start = ((bf16[8,136,1024]{2,1,0:T(8,128)(2,1)}), bf16[8,136,1024]{2,1,0:T(8,128)(2,1)S(1)}, u32[]{:S(2)}, u32[]{:S(2)}) async-start(bf16[8,136,1024]{2,1,0:T(8,128)(2,1)} %outgoing_rows.1), calls=%async_computation | async-start | bytes 4456448 | tf_op jit(solution)/shard_map/all_to_all | solution.py:39
  13.8 1.6 %collective-permute-start.4 = (bf16[128,1024]{1,0:T(8,128)(2,1)S(1)}, bf16[128,1024]{1,0:T(8,128)(2,1)S(1)}, u32[]{:S(2)}, u32[]{:S(2)}) collective-permute-start(bf16[128,1024]{1,0:T(8,128)(2,1)S(1)} %join_blocks.5.refs_1_), channel_id=1, source_target_pairs={{0,4},{4,8},{8,12},{12,0},{1,5},{5,9},{9,13},{13,1},{2,6},{6,10},{... | collective-permute-start | bytes 786440 | tf_op jit(solution)/shard_map/ppermute | solution.py:31
  15.5 3.5 %collective-permute-done.3.refs_0_.refs_2_ = bf16[128,1024]{1,0:T(8,128)(2,1)S(1)} collective-permute-done((bf16[128,1024]{1,0:T(8,128)(2,1)S(1)}, bf16[128,1024]{1,0:T(8,128)(2,1)S(1)}, u32[]{:S(2)}, u32[]{:S(2)}) %collective-permute-start.3) | collective-permute-done | bytes 262176 | tf_op jit(solution)/shard_map/ppermute | solution.py:31
  19.1 5.8 %collective-permute-done.4.refs_0_.refs_3_ = bf16[128,1024]{1,0:T(8,128)(2,1)S(1)} collective-permute-done((bf16[128,1024]{1,0:T(8,128)(2,1)S(1)}, bf16[128,1024]{1,0:T(8,128)(2,1)S(1)}, u32[]{:S(2)}, u32[]{:S(2)}) %collective-permute-start.4) | collective-permute-done | bytes 262176 | tf_op jit(solution)/shard_map/ppermute | solution.py:31
  26.4 2.1 %collective-permute-start.11 = (bf16[64,1024]{1,0:T(8,128)(2,1)}, bf16[64,1024]{1,0:T(8,128)(2,1)S(1)}, u32[]{:S(2)}, u32[]{:S(2)}) collective-permute-start(bf16[64,1024]{1,0:T(8,128)(2,1)} %get-tuple-element.31), channel_id=1, source_target_pairs={{0,3},{1,2},{2,1},{3,0},{4,7},{5,6},{6,5},{7,4},{8,11},{9,10},{10,... | collective-permute-start | bytes 393224 | tf_op jit(solution)/shard_map/ppermute | solution.py:27
  28.6 2.0 %collective-permute-done.5.refs_4_ = bf16[128,1024]{1,0:T(8,128)(2,1)} collective-permute-done((bf16[128,1024]{1,0:T(8,128)(2,1)S(1)}, bf16[128,1024]{1,0:T(8,128)(2,1)}, u32[]{:S(2)}, u32[]{:S(2)}) %collective-permute-start.5) | collective-permute-done | bytes 262176 | tf_op jit(solution)/shard_map/ppermute | solution.py:31
  30.6 6.3 %collective-permute-done.6.refs_5_ = bf16[128,1024]{1,0:T(8,128)(2,1)} collective-permute-done((bf16[128,1024]{1,0:T(8,128)(2,1)}, bf16[128,1024]{1,0:T(8,128)(2,1)}, u32[]{:S(2)}, u32[]{:S(2)}) %collective-permute-start.6) | collective-permute-done | bytes 262176 | tf_op jit(solution)/shard_map/ppermute | solution.py:31
  37.0 6.2 %collective-permute-done.11 = bf16[64,1024]{1,0:T(8,128)(2,1)S(1)} collective-permute-done((bf16[64,1024]{1,0:T(8,128)(2,1)}, bf16[64,1024]{1,0:T(8,128)(2,1)S(1)}, u32[]{:S(2)}, u32[]{:S(2)}) %collective-permute-start.11) | collective-permute-done | bytes 131104 | tf_op jit(solution)/shard_map/ppermute | solution.py:27
  43.2 3.3 %collective-permute-done.10 = bf16[64,1024]{1,0:T(8,128)(2,1)S(1)} collective-permute-done((bf16[64,1024]{1,0:T(8,128)(2,1)}, bf16[64,1024]{1,0:T(8,128)(2,1)S(1)}, u32[]{:S(2)}, u32[]{:S(2)}) %collective-permute-start.10) | collective-permute-done | bytes 131104 | tf_op jit(solution)/shard_map/ppermute | solution.py:27
  48.0 1.6 %collective-permute-start.12 = (bf16[128,1024]{1,0:T(8,128)(2,1)S(1)}, bf16[128,1024]{1,0:T(8,128)(2,1)}, u32[]{:S(2)}, u32[]{:S(2)}) collective-permute-start(bf16[128,1024]{1,0:T(8,128)(2,1)S(1)} %pad_maximum_fusion.refs_0_), channel_id=1, source_target_pairs={{0,4},{4,8},{8,12},{12,0},{1,5},{5,9},{9,13},{13,1},{2,6},{6,10},{... | collective-permute-start | bytes 786440 | tf_op jit(solution)/shard_map/ppermute | solution.py:31
  49.5 1.6 %collective-permute-start.13 = (bf16[128,1024]{1,0:T(8,128)(2,1)S(1)}, bf16[128,1024]{1,0:T(8,128)(2,1)}, u32[]{:S(2)}, u32[]{:S(2)}) collective-permute-start(bf16[128,1024]{1,0:T(8,128)(2,1)S(1)} %pad_maximum_fusion.1.refs_1_), channel_id=1, source_target_pairs={{0,4},{4,8},{8,12},{12,0},{1,5},{5,9},{9,13},{13,1},{2,6},{6,10},{... | collective-permute-start | bytes 786440 | tf_op jit(solution)/shard_map/ppermute | solution.py:31
  54.1 4.2 %down_product.1 = (f32[8,64,128]{2,1,0:T(8,128)}, f32[8,128]{1,0:T(8,128)S(1)}) custom-call(s32[16]{0:T(128)S(1)} %add.61.labels_ref, bf16[8,136,1024]{2,1,0:T(8,128)(2,1)S(1)} %all-to-all-done.rows_ref, bf16[128,1024]{1,0:T(8,128)(2,1)S(1)} %join_blocks.4.refs_0_, bf16[128,1024]{1,0:T(8,128)(2,1)S(1)} %join_blocks.5.refs_1_, ...), custom_call_target="tpu_custom_call" | custom-call | flops 2147483648 | bytes 4194304 | tf_op jit(solution)/shard_map/down_product/pallas_call | solution.py:146
  59.1 5.4 %collective-permute-done.13.refs_3_ = bf16[128,1024]{1,0:T(8,128)(2,1)} collective-permute-done((bf16[128,1024]{1,0:T(8,128)(2,1)S(1)}, bf16[128,1024]{1,0:T(8,128)(2,1)}, u32[]{:S(2)}, u32[]{:S(2)}) %collective-permute-start.13) | collective-permute-done | bytes 262176 | tf_op jit(solution)/shard_map/ppermute | solution.py:31
  64.5 3.4 %all-to-all-start.1 = ((f32[8,64,128]{2,1,0:T(8,128)}), f32[8,64,128]{2,1,0:T(8,128)S(1)}, u32[]{:S(2)}, u32[]{:S(2)}) async-start(f32[8,64,128]{2,1,0:T(8,128)} %get-tuple-element.26), calls=%async_computation.1 | async-start | bytes 524288 | tf_op jit(solution)/shard_map/all_to_all | solution.py:39
  67.9 2.4 %collective-permute-done.14.refs_4_ = bf16[128,1024]{1,0:T(8,128)(2,1)S(1)} collective-permute-done((bf16[128,1024]{1,0:T(8,128)(2,1)}, bf16[128,1024]{1,0:T(8,128)(2,1)S(1)}, u32[]{:S(2)}, u32[]{:S(2)}) %collective-permute-start.14) | collective-permute-done | bytes 262176 | tf_op jit(solution)/shard_map/ppermute | solution.py:31
  70.3 5.5 %collective-permute-done.15.refs_5_ = bf16[128,1024]{1,0:T(8,128)(2,1)S(1)} collective-permute-done((bf16[128,1024]{1,0:T(8,128)(2,1)}, bf16[128,1024]{1,0:T(8,128)(2,1)S(1)}, u32[]{:S(2)}, u32[]{:S(2)}) %collective-permute-start.15) | collective-permute-done | bytes 262176 | tf_op jit(solution)/shard_map/ppermute | solution.py:31
  75.9 7.6 %all_to_all.15.shrunk_ref = bf16[8,64,128]{2,1,0:T(8,128)(2,1)S(1)} all-to-all(bf16[8,64,128]{2,1,0:T(8,128)(2,1)S(1)} %summed_copies.1), channel_id=1, replica_groups=mesh['groups'=2,'outer'=4,'inner'=4] {'groups','inner'}, dimensions={0} | all-to-all | bytes 262144 | tf_op jit(solution)/shard_map/all_to_all | solution.py:39
  83.5 2.2 %collective-permute-done.17.refs_7_ = bf16[128,1024]{1,0:T(8,128)(2,1)S(1)} collective-permute-done((bf16[128,1024]{1,0:T(8,128)(2,1)S(1)}, bf16[128,1024]{1,0:T(8,128)(2,1)S(1)}, u32[]{:S(2)}, u32[]{:S(2)}) %collective-permute-start.17) | collective-permute-done | bytes 262176 | tf_op jit(solution)/shard_map/ppermute | solution.py:31
  85.7 3.7 %up_product.1 = (bf16[128,1024]{1,0:T(8,128)(2,1)S(1)}, bf16[128,1024]{1,0:T(8,128)(2,1)S(1)}, bf16[128,1024]{1,0:T(8,128)(2,1)S(1)}, bf16[128,1024]{1,0:T(8,128...) custom-call(s32[16]{0:T(128)S(1)} %add.61.labels_ref, ...), custom_call_target="tpu_custom_call" | custom-call | flops 2147483648 | bytes 4194304 | tf_op jit(solution)/shard_map/up_product/pallas_call | solution.py:218
  90.2 1.1 collective-permute-start.20
  91.4 1.5 %collective-permute-start.21 = (bf16[128,1024]{1,0:T(8,128)(2,1)S(1)}, bf16[128,1024]{1,0:T(8,128)(2,1)S(1)}, u32[]{:S(2)}, u32[]{:S(2)}) collective-permute-start(bf16[128,1024]{1,0:T(8,128)(2,1)S(1)} %get-tuple-element.39), channel_id=1, source_target_pairs={{0,16},{1,17},{2,18},{3,19},{16,0},{17,1},{18,2},{19,3},{4,20},{5,... | collective-permute-start | bytes 786440 | tf_op jit(solution)/shard_map/ppermute | solution.py:27
  93.1 1.7 %collective-permute-start.23 = (bf16[128,1024]{1,0:T(8,128)(2,1)S(1)}, bf16[128,1024]{1,0:T(8,128)(2,1)S(1)}, u32[]{:S(2)}, u32[]{:S(2)}) collective-permute-start(bf16[128,1024]{1,0:T(8,128)(2,1)S(1)} %get-tuple-element.41), channel_id=1, source_target_pairs={{0,18},{1,19},{2,16},{3,17},{16,2},{17,3},{18,0},{19,1},{4,22},{5,... | collective-permute-start | bytes 786440 | tf_op jit(solution)/shard_map/ppermute | solution.py:27
  94.7 4.0 %collective-permute-done.19.refs_2_ = bf16[128,1024]{1,0:T(8,128)(2,1)S(1)} collective-permute-done((bf16[128,1024]{1,0:T(8,128)(2,1)S(1)}, bf16[128,1024]{1,0:T(8,128)(2,1)S(1)}, u32[]{:S(2)}, u32[]{:S(2)}) %collective-permute-start.19) | collective-permute-done | bytes 262176 | tf_op jit(solution)/shard_map/ppermute | solution.py:27
  99.1 4.2 %collective-permute-done.20.refs_3_ = bf16[128,1024]{1,0:T(8,128)(2,1)S(1)} collective-permute-done((bf16[128,1024]{1,0:T(8,128)(2,1)S(1)}, bf16[128,1024]{1,0:T(8,128)(2,1)S(1)}, u32[]{:S(2)}, u32[]{:S(2)}) %collective-permute-start.20) | collective-permute-done | bytes 262176 | tf_op jit(solution)/shard_map/ppermute | solution.py:27
  103.4 1.7 %collective-permute-done.22.refs_5_ = bf16[128,1024]{1,0:T(8,128)(2,1)S(1)} collective-permute-done((bf16[128,1024]{1,0:T(8,128)(2,1)S(1)}, bf16[128,1024]{1,0:T(8,128)(2,1)S(1)}, u32[]{:S(2)}, u32[]{:S(2)}) %collective-permute-start.22) | collective-permute-done | bytes 262176 | tf_op jit(solution)/shard_map/ppermute | solution.py:27
  105.1 6.7 %collective-permute-done.23.refs_6_ = bf16[128,1024]{1,0:T(8,128)(2,1)S(1)} collective-permute-done((bf16[128,1024]{1,0:T(8,128)(2,1)S(1)}, bf16[128,1024]{1,0:T(8,128)(2,1)S(1)}, u32[]{:S(2)}, u32[]{:S(2)}) %collective-permute-start.23) | collective-permute-done | bytes 262176 | tf_op jit(solution)/shard_map/ppermute | solution.py:27
  111.8 4.5 %collective-permute-done.24.refs_7_ = bf16[128,1024]{1,0:T(8,128)(2,1)S(1)} collective-permute-done((bf16[128,1024]{1,0:T(8,128)(2,1)S(1)}, bf16[128,1024]{1,0:T(8,128)(2,1)S(1)}, u32[]{:S(2)}, u32[]{:S(2)}) %collective-permute-start.24) | collective-permute-done | bytes 262176 | tf_op jit(solution)/shard_map/ppermute | solution.py:27
  116.3 1.4 %place_results.1 = bf16[128,8192]{1,0:T(8,128)(2,1)} custom-call(s32[1]{0:T(128)} %bitcast.me_ref, bf16[128,1024]{1,0:T(8,128)(2,1)S(1)} %get-tuple-element.35.refs_0_, bf16[128,1024]{1,0:T(8,128)(2,1)S(1)} %collective-permute-done.18.refs_1_, bf16[128,1024]{1,0:T(8,128)(2,1)S(1)} %collective-permute-done.19.refs_2_, ...), custom_call_target="tpu_custom_call" | custom-call | tf_op jit(solution)/shard_map/place_results/pallas_call | solution.py:249
  (57 shorter events, 10.9 us)
Async XLA Ops:
  1.1 7.1 %collective-permute-start = (bf16[64,1024]{1,0:T(8,128)(2,1)S(1)}, bf16[64,1024]{1,0:T(8,128)(2,1)S(1)}, u32[]{:S(2)}, u32[]{:S(2)}) collective-permute-start(bf16[64,1024]{1,0:T(8,128)(2,1)S(1)} %get-tuple-element.48), channel_id=1, source_target_pairs={{0,1},{1,0},{2,3},{3,2},{4,5},{5,4},{6,7},{7,6},{8,9},{9,8},{10,11... | collective-permute-start | bytes 393224 | tf_op jit(solution)/shard_map/ppermute | solution.py:27
  1.7 12.1 %collective-permute-start.1 = (bf16[64,1024]{1,0:T(8,128)(2,1)S(1)}, bf16[64,1024]{1,0:T(8,128)(2,1)S(1)}, u32[]{:S(2)}, u32[]{:S(2)}) collective-permute-start(bf16[64,1024]{1,0:T(8,128)(2,1)S(1)} %get-tuple-element.50), channel_id=1, source_target_pairs={{0,2},{1,3},{2,0},{3,1},{4,6},{5,7},{6,4},{7,5},{8,10},{9,11},{10,... | collective-permute-start | bytes 393224 | tf_op jit(solution)/shard_map/ppermute | solution.py:27
  4.3 9.6 %collective-permute-start.2 = (bf16[64,1024]{1,0:T(8,128)(2,1)S(1)}, bf16[64,1024]{1,0:T(8,128)(2,1)S(1)}, u32[]{:S(2)}, u32[]{:S(2)}) collective-permute-start(bf16[64,1024]{1,0:T(8,128)(2,1)S(1)} %get-tuple-element.47), channel_id=1, source_target_pairs={{0,3},{1,2},{2,1},{3,0},{4,7},{5,6},{6,5},{7,4},{8,11},{9,10},{10,... | collective-permute-start | bytes 393224 | tf_op jit(solution)/shard_map/ppermute | solution.py:27
  4.3 1.6 %copy-start = (bf16[128,8192]{1,0:T(8,128)(2,1)S(1)}, bf16[128,8192]{1,0:T(8,128)(2,1)}, u32[]{:S(2)}) copy-start(bf16[128,8192]{1,0:T(8,128)(2,1)} %hidden_ref.1) | copy-start | bytes 6291460
  8.2 10.7 %collective-permute-start.3 = (bf16[128,1024]{1,0:T(8,128)(2,1)S(1)}, bf16[128,1024]{1,0:T(8,128)(2,1)S(1)}, u32[]{:S(2)}, u32[]{:S(2)}) collective-permute-start(bf16[128,1024]{1,0:T(8,128)(2,1)S(1)} %join_blocks.4.refs_0_), channel_id=1, source_target_pairs={{0,4},{4,8},{8,12},{12,0},{1,5},{5,9},{9,13},{13,1},{2,6},{6,10},{... | collective-permute-start | bytes 786440 | tf_op jit(solution)/shard_map/ppermute | solution.py:31
  10.1 41.2 %all-to-all-start = ((bf16[8,136,1024]{2,1,0:T(8,128)(2,1)}), bf16[8,136,1024]{2,1,0:T(8,128)(2,1)S(1)}, u32[]{:S(2)}, u32[]{:S(2)}) async-start(bf16[8,136,1024]{2,1,0:T(8,128)(2,1)} %outgoing_rows.1), calls=%async_computation | async-start | bytes 4456448 | tf_op jit(solution)/shard_map/all_to_all | solution.py:39
  13.8 11.0 %collective-permute-start.4 = (bf16[128,1024]{1,0:T(8,128)(2,1)S(1)}, bf16[128,1024]{1,0:T(8,128)(2,1)S(1)}, u32[]{:S(2)}, u32[]{:S(2)}) collective-permute-start(bf16[128,1024]{1,0:T(8,128)(2,1)S(1)} %join_blocks.5.refs_1_), channel_id=1, source_target_pairs={{0,4},{4,8},{8,12},{12,0},{1,5},{5,9},{9,13},{13,1},{2,6},{6,10},{... | collective-permute-start | bytes 786440 | tf_op jit(solution)/shard_map/ppermute | solution.py:31
  19.0 6.7 %copy-start.8 = (bf16[1,64,8192]{2,1,0:T(8,128)(2,1)S(1)}, bf16[1,64,8192]{2,1,0:T(8,128)(2,1)}, u32[]{:S(2)}) copy-start(bf16[1,64,8192]{2,1,0:T(8,128)(2,1)} %param.7) | copy-start | bytes 3145732
  19.0 11.6 %collective-permute-start.5 = (bf16[128,1024]{1,0:T(8,128)(2,1)S(1)}, bf16[128,1024]{1,0:T(8,128)(2,1)}, u32[]{:S(2)}, u32[]{:S(2)}) collective-permute-start(bf16[128,1024]{1,0:T(8,128)(2,1)S(1)} %join_blocks.6), channel_id=1, source_target_pairs={{0,4},{4,8},{8,12},{12,0},{1,5},{5,9},{9,13},{13,1},{2,6},{6,10},{... | collective-permute-start | bytes 786440 | tf_op jit(solution)/shard_map/ppermute | solution.py:31
  25.7 11.3 %collective-permute-start.6 = (bf16[128,1024]{1,0:T(8,128)(2,1)}, bf16[128,1024]{1,0:T(8,128)(2,1)}, u32[]{:S(2)}, u32[]{:S(2)}) collective-permute-start(bf16[128,1024]{1,0:T(8,128)(2,1)} %join_blocks.7), channel_id=1, source_target_pairs={{0,4},{4,8},{8,12},{12,0},{1,5},{5,9},{9,13},{13,1},{2,6},{6,10},{... | collective-permute-start | bytes 786440 | tf_op jit(solution)/shard_map/ppermute | solution.py:31
  26.4 10.5 %collective-permute-start.9 = (bf16[64,1024]{1,0:T(8,128)(2,1)}, bf16[64,1024]{1,0:T(8,128)(2,1)S(1)}, u32[]{:S(2)}, u32[]{:S(2)}) collective-permute-start(bf16[64,1024]{1,0:T(8,128)(2,1)} %get-tuple-element.28), channel_id=1, source_target_pairs={{0,1},{1,0},{2,3},{3,2},{4,5},{5,4},{6,7},{7,6},{8,9},{9,8},{10,11... | collective-permute-start | bytes 393224 | tf_op jit(solution)/shard_map/ppermute | solution.py:27
  26.4 16.8 %collective-permute-start.11 = (bf16[64,1024]{1,0:T(8,128)(2,1)}, bf16[64,1024]{1,0:T(8,128)(2,1)S(1)}, u32[]{:S(2)}, u32[]{:S(2)}) collective-permute-start(bf16[64,1024]{1,0:T(8,128)(2,1)} %get-tuple-element.31), channel_id=1, source_target_pairs={{0,3},{1,2},{2,1},{3,0},{4,7},{5,6},{6,5},{7,4},{8,11},{9,10},{10,... | collective-permute-start | bytes 393224 | tf_op jit(solution)/shard_map/ppermute | solution.py:27
  28.5 18.0 %collective-permute-start.10 = (bf16[64,1024]{1,0:T(8,128)(2,1)}, bf16[64,1024]{1,0:T(8,128)(2,1)S(1)}, u32[]{:S(2)}, u32[]{:S(2)}) collective-permute-start(bf16[64,1024]{1,0:T(8,128)(2,1)} %get-tuple-element.30), channel_id=1, source_target_pairs={{0,2},{1,3},{2,0},{3,1},{4,6},{5,7},{6,4},{7,5},{8,10},{9,11},{10,... | collective-permute-start | bytes 393224 | tf_op jit(solution)/shard_map/ppermute | solution.py:27
  30.6 15.9 %collective-permute-start.7 = (bf16[128,1024]{1,0:T(8,128)(2,1)}, bf16[128,1024]{1,0:T(8,128)(2,1)S(1)}, u32[]{:S(2)}, u32[]{:S(2)}) collective-permute-start(bf16[128,1024]{1,0:T(8,128)(2,1)} %collective-permute-done.5.refs_4_), channel_id=1, source_target_pairs={{0,4},{4,8},{8,12},{12,0},{1,5},{5,9},{9,13},{13,1},{2,6},{6,10},{... | collective-permute-start | bytes 786440 | tf_op jit(solution)/shard_map/ppermute | solution.py:31
  36.9 10.3 %collective-permute-start.8 = (bf16[128,1024]{1,0:T(8,128)(2,1)}, bf16[128,1024]{1,0:T(8,128)(2,1)S(1)}, u32[]{:S(2)}, u32[]{:S(2)}) collective-permute-start(bf16[128,1024]{1,0:T(8,128)(2,1)} %collective-permute-done.6.refs_5_), channel_id=1, source_target_pairs={{0,4},{4,8},{8,12},{12,0},{1,5},{5,9},{9,13},{13,1},{2,6},{6,10},{... | collective-permute-start | bytes 786440 | tf_op jit(solution)/shard_map/ppermute | solution.py:31
  48.0 11.1 %collective-permute-start.12 = (bf16[128,1024]{1,0:T(8,128)(2,1)S(1)}, bf16[128,1024]{1,0:T(8,128)(2,1)}, u32[]{:S(2)}, u32[]{:S(2)}) collective-permute-start(bf16[128,1024]{1,0:T(8,128)(2,1)S(1)} %pad_maximum_fusion.refs_0_), channel_id=1, source_target_pairs={{0,4},{4,8},{8,12},{12,0},{1,5},{5,9},{9,13},{13,1},{2,6},{6,10},{... | collective-permute-start | bytes 786440 | tf_op jit(solution)/shard_map/ppermute | solution.py:31
  49.5 15.0 %collective-permute-start.13 = (bf16[128,1024]{1,0:T(8,128)(2,1)S(1)}, bf16[128,1024]{1,0:T(8,128)(2,1)}, u32[]{:S(2)}, u32[]{:S(2)}) collective-permute-start(bf16[128,1024]{1,0:T(8,128)(2,1)S(1)} %pad_maximum_fusion.1.refs_1_), channel_id=1, source_target_pairs={{0,4},{4,8},{8,12},{12,0},{1,5},{5,9},{9,13},{13,1},{2,6},{6,10},{... | collective-permute-start | bytes 786440 | tf_op jit(solution)/shard_map/ppermute | solution.py:31
  51.3 1.0 copy-start.3
  52.2 0.9 copy-start.5
  53.2 0.9 copy-start.7
  59.1 11.3 %collective-permute-start.14 = (bf16[128,1024]{1,0:T(8,128)(2,1)}, bf16[128,1024]{1,0:T(8,128)(2,1)S(1)}, u32[]{:S(2)}, u32[]{:S(2)}) collective-permute-start(bf16[128,1024]{1,0:T(8,128)(2,1)} %collective-permute-done.12.refs_2_), channel_id=1, source_target_pairs={{0,4},{4,8},{8,12},{12,0},{1,5},{5,9},{9,13},{13,1},{2,6},{6,10},{... | collective-permute-start | bytes 786440 | tf_op jit(solution)/shard_map/ppermute | solution.py:31
  64.5 11.3 %collective-permute-start.15 = (bf16[128,1024]{1,0:T(8,128)(2,1)}, bf16[128,1024]{1,0:T(8,128)(2,1)S(1)}, u32[]{:S(2)}, u32[]{:S(2)}) collective-permute-start(bf16[128,1024]{1,0:T(8,128)(2,1)} %collective-permute-done.13.refs_3_), channel_id=1, source_target_pairs={{0,4},{4,8},{8,12},{12,0},{1,5},{5,9},{9,13},{13,1},{2,6},{6,10},{... | collective-permute-start | bytes 786440 | tf_op jit(solution)/shard_map/ppermute | solution.py:31
  64.5 11.4 %all-to-all-start.1 = ((f32[8,64,128]{2,1,0:T(8,128)}), f32[8,64,128]{2,1,0:T(8,128)S(1)}, u32[]{:S(2)}, u32[]{:S(2)}) async-start(f32[8,64,128]{2,1,0:T(8,128)} %get-tuple-element.26), calls=%async_computation.1 | async-start | bytes 524288 | tf_op jit(solution)/shard_map/all_to_all | solution.py:39
  70.3 13.1 %collective-permute-start.16 = (bf16[128,1024]{1,0:T(8,128)(2,1)S(1)}, bf16[128,1024]{1,0:T(8,128)(2,1)S(1)}, u32[]{:S(2)}, u32[]{:S(2)}) collective-permute-start(bf16[128,1024]{1,0:T(8,128)(2,1)S(1)} %collective-permute-done.14.refs_4_), channel_id=1, source_target_pairs={{0,4},{4,8},{8,12},{12,0},{1,5},{5,9},{9,13},{13,1},{2,6},{6,10},{... | collective-permute-start | bytes 786440 | tf_op jit(solution)/shard_map/ppermute | solution.py:31
  75.8 9.8 %collective-permute-start.17 = (bf16[128,1024]{1,0:T(8,128)(2,1)S(1)}, bf16[128,1024]{1,0:T(8,128)(2,1)S(1)}, u32[]{:S(2)}, u32[]{:S(2)}) collective-permute-start(bf16[128,1024]{1,0:T(8,128)(2,1)S(1)} %collective-permute-done.15.refs_5_), channel_id=1, source_target_pairs={{0,4},{4,8},{8,12},{12,0},{1,5},{5,9},{9,13},{13,1},{2,6},{6,10},{... | collective-permute-start | bytes 786440 | tf_op jit(solution)/shard_map/ppermute | solution.py:31
  89.4 3.6 %collective-permute-start.18 = (bf16[128,1024]{1,0:T(8,128)(2,1)S(1)}, bf16[128,1024]{1,0:T(8,128)(2,1)S(1)}, u32[]{:S(2)}, u32[]{:S(2)}) collective-permute-start(bf16[128,1024]{1,0:T(8,128)(2,1)S(1)} %get-tuple-element.36), channel_id=1, source_target_pairs={{0,1},{1,0},{2,3},{3,2},{16,17},{17,16},{18,19},{19,18},{4,5},{5,4... | collective-permute-start | bytes 786440 | tf_op jit(solution)/shard_map/ppermute | solution.py:27
  89.5 9.2 %collective-permute-start.19 = (bf16[128,1024]{1,0:T(8,128)(2,1)S(1)}, bf16[128,1024]{1,0:T(8,128)(2,1)S(1)}, u32[]{:S(2)}, u32[]{:S(2)}) collective-permute-start(bf16[128,1024]{1,0:T(8,128)(2,1)S(1)} %get-tuple-element.37), channel_id=1, source_target_pairs={{0,2},{1,3},{2,0},{3,1},{16,18},{17,19},{18,16},{19,17},{4,6},{5,7... | collective-permute-start | bytes 786440 | tf_op jit(solution)/shard_map/ppermute | solution.py:27
  90.2 13.2 %collective-permute-start.20 = (bf16[128,1024]{1,0:T(8,128)(2,1)S(1)}, bf16[128,1024]{1,0:T(8,128)(2,1)S(1)}, u32[]{:S(2)}, u32[]{:S(2)}) collective-permute-start(bf16[128,1024]{1,0:T(8,128)(2,1)S(1)} %get-tuple-element.38), channel_id=1, source_target_pairs={{0,3},{1,2},{2,1},{3,0},{16,19},{17,18},{18,17},{19,16},{4,7},{5,6... | collective-permute-start | bytes 786440 | tf_op jit(solution)/shard_map/ppermute | solution.py:27
  91.4 12.0 %collective-permute-start.21 = (bf16[128,1024]{1,0:T(8,128)(2,1)S(1)}, bf16[128,1024]{1,0:T(8,128)(2,1)S(1)}, u32[]{:S(2)}, u32[]{:S(2)}) collective-permute-start(bf16[128,1024]{1,0:T(8,128)(2,1)S(1)} %get-tuple-element.39), channel_id=1, source_target_pairs={{0,16},{1,17},{2,18},{3,19},{16,0},{17,1},{18,2},{19,3},{4,20},{5,... | collective-permute-start | bytes 786440 | tf_op jit(solution)/shard_map/ppermute | solution.py:27
  92.8 12.3 %collective-permute-start.22 = (bf16[128,1024]{1,0:T(8,128)(2,1)S(1)}, bf16[128,1024]{1,0:T(8,128)(2,1)S(1)}, u32[]{:S(2)}, u32[]{:S(2)}) collective-permute-start(bf16[128,1024]{1,0:T(8,128)(2,1)S(1)} %get-tuple-element.40), channel_id=1, source_target_pairs={{0,17},{1,16},{2,19},{3,18},{16,1},{17,0},{18,3},{19,2},{4,21},{5,... | collective-permute-start | bytes 786440 | tf_op jit(solution)/shard_map/ppermute | solution.py:27
  93.1 18.7 %collective-permute-start.23 = (bf16[128,1024]{1,0:T(8,128)(2,1)S(1)}, bf16[128,1024]{1,0:T(8,128)(2,1)S(1)}, u32[]{:S(2)}, u32[]{:S(2)}) collective-permute-start(bf16[128,1024]{1,0:T(8,128)(2,1)S(1)} %get-tuple-element.41), channel_id=1, source_target_pairs={{0,18},{1,19},{2,16},{3,17},{16,2},{17,3},{18,0},{19,1},{4,22},{5,... | collective-permute-start | bytes 786440 | tf_op jit(solution)/shard_map/ppermute | solution.py:27
  98.7 17.6 %collective-permute-start.24 = (bf16[128,1024]{1,0:T(8,128)(2,1)S(1)}, bf16[128,1024]{1,0:T(8,128)(2,1)S(1)}, u32[]{:S(2)}, u32[]{:S(2)}) collective-permute-start(bf16[128,1024]{1,0:T(8,128)(2,1)S(1)} %get-tuple-element.42), channel_id=1, source_target_pairs={{0,19},{1,18},{2,17},{3,16},{16,3},{17,2},{18,1},{19,0},{4,23},{5,... | collective-permute-start | bytes 786440 | tf_op jit(solution)/shard_map/ppermute | solution.py:27
  (4 other events, 2.8 us)

commit v17 on v16

--- a/solution.py
+++ b/solution.py
@@ -12,7 +12,7 @@
 PLANE = ("groups", "inner")
 LANES = 128
 ID_ROWS = 8
-AHEAD, SLIGHTLY_AHEAD, SUM_AHEAD = 10**11, 3 * 10**9, 4 * 10**9
+AHEAD, SLIGHTLY_AHEAD, SUM_AHEAD = 10**11, 3 * 10**9, 8 * 10**9
 BLOCK = 8
 IN_VMEM = pl.BlockSpec(memory_space=pltpu.VMEM)
 IN_SMEM = pl.BlockSpec(memory_space=pltpu.SMEM)
@@ -48,17 +48,17 @@
     return label.astype(jnp.float32)
 
 
-def join_kernel(*refs):
+def join_kernel(first, *refs):
     blocks, out_ref = refs[:-1], refs[-1]
-    rows = blocks[0].shape[0]
+    rows = out_ref.shape[0] // len(blocks)
     for n, block in enumerate(blocks):
-        out_ref[n * rows : (n + 1) * rows, :] = block[...]
-
-
-def joined(blocks, cost):
-    rows, share = blocks[0].shape
-    return pl.pallas_call(
-        join_kernel,
+        out_ref[n * rows : (n + 1) * rows, :] = block[first : first + rows, :]
+
+
+def joined(blocks, first, rows, cost):
+    share = blocks[0].shape[1]
+    return pl.pallas_call(
+        functools.partial(join_kernel, first),
         out_shape=jax.ShapeDtypeStruct((len(blocks) * rows, share), jnp.bfloat16),
         in_specs=[IN_VMEM] * len(blocks),
         out_specs=IN_VMEM,
@@ -231,23 +231,23 @@
     )(labels, me, ids, shrunk, *maps)
 
 
-def place_kernel(me_ref, *refs):
+def place_kernel(offsets, me_ref, *refs):
     blocks, out_ref, sems = refs[:-2], refs[-2], refs[-1]
     share = blocks[0].shape[1]
     copies = []
-    for offset, block in enumerate(blocks):
-        at = pl.multiple_of((me_ref[0] ^ offset) * share, LANES)
-        copies.append(pltpu.make_async_copy(block, out_ref.at[:, pl.ds(at, share)], sems.at[offset]))
+    for n, block in enumerate(blocks):
+        at = pl.multiple_of((me_ref[0] ^ offsets[n]) * share, LANES)
+        copies.append(pltpu.make_async_copy(block, out_ref.at[:, pl.ds(at, share)], sems.at[n]))
     for copy in copies:
         copy.start()
     for copy in copies:
         copy.wait()
 
 
-def place(me, blocks):
+def place(me, offsets, blocks):
     tok, share = blocks[0].shape
     return pl.pallas_call(
-        place_kernel,
+        functools.partial(place_kernel, offsets),
         out_shape=jax.ShapeDtypeStruct((tok, len(blocks) * share), jnp.bfloat16),
         in_specs=[IN_SMEM] + [ANYWHERE] * len(blocks),
         out_specs=ANYWHERE,
@@ -266,13 +266,17 @@
     rank = adapter_up_maps.shape[1]
     me = group * inner + place_in_group
 
-    def slices(array):
-        return [
-            lax.dynamic_slice_in_dim(array, (me ^ offset) * share, share, axis=1) for offset in range(inner)
-        ]
-
-    def exchanged(blocks):
-        return blocks[:1] + [to_partner(blocks[n], "inner", inner, n) for n in range(1, inner)]
+    def slices(offset):
+        start = (me ^ offset) * share
+        return jnp.concatenate(
+            [
+                lax.dynamic_slice_in_dim(adapter_down_maps[0].T, start, share, axis=1),
+                lax.dynamic_slice_in_dim(adapter_up_maps[0], start, share, axis=1),
+            ],
+            axis=0,
+        )
+
+    got = [slices(0)] + [to_partner(slices(n), "inner", inner, n) for n in range(1, inner)]
 
     def rings(near, far, first_cost=0, second_after=()):
         near, far = [near], [far]
@@ -282,7 +286,7 @@
                 if step == 2:
                     block = after(block, *second_after)
                     if first_cost:
-                        block = joined([block], first_cost)
+                        block = joined([block], 0, block.shape[0], first_cost)
                 blocks.append(next_on_ring(block, outer))
         return near, far
 
@@ -293,25 +297,25 @@
     labels = labels.reshape(-1)
 
     middle = inner // 2
-    down = exchanged(slices(adapter_down_maps[0].T))
-    down_near, down_far = rings(joined(down[:middle], AHEAD), joined(down[middle:], AHEAD), first_cost=SLIGHTLY_AHEAD)
+    down_near, down_far = rings(
+        joined(got[:middle], 0, rank, AHEAD), joined(got[middle:], 0, rank, AHEAD), first_cost=SLIGHTLY_AHEAD
+    )
     ids = token_adapter_index.reshape(1, tok)
     rows = swap(after(outgoing_rows(hidden, ids, members), down_near[0]))
-    up = exchanged([after(block, down_near[1]) for block in slices(adapter_up_maps[0])])
 
     down_maps = [m for pair in zip(down_near, down_far) for m in pair]
     packed, id_rows = down_product(labels, rows, down_maps, rank)
     up_near, up_far = rings(
-        after(jnp.concatenate(up[:middle], axis=0), down_near[-1]),
-        after(jnp.concatenate(up[middle:], axis=0), down_far[-1]),
+        after(jnp.concatenate([g[rank:] for g in got[:middle]], axis=0), down_near[-1]),
+        after(jnp.concatenate([g[rank:] for g in got[middle:]], axis=0), down_far[-1]),
         second_after=[packed],
     )
     up_maps = [m for pair in zip(up_near, up_far) for m in pair]
     shrunk = swap(summed_copies(swap(packed)))
     results = list(up_product(labels, me.reshape(1), id_rows, shrunk, up_maps, rank))
-    order = sorted(range(1, members), key=lambda n: (-(n >= inner) - (n % inner >= 2), -(n >= inner), n))
-    returned = {n: to_partner(results[n], PLANE, members, n) for n in order}
-    return place(me.reshape(1), results[:1] + [returned[n] for n in range(1, members)])
+    offsets = sorted(range(1, members), key=lambda n: (-(n >= inner) - (n % inner >= 2), -(n >= inner), n))
+    returned = [to_partner(results[n], PLANE, members, n) for n in offsets]
+    return place(me.reshape(1), offsets + [0], returned + results[:1])
 
 
 def solution(mesh):

time: 118 us -> 126 us (1.068)
  waiting for transfers between devices: 64.6 us -> 72.2 us
  local copies, waits for them, and re-layouts: 8.5 us -> 5.15 us
  other arithmetic: 0.12 us -> 2.34 us
  starting transfers between devices: 24.9 us -> 27 us
    ppermute x12, waiting for transfers between devices: 34 us -> 44.5 us  [next_on_ring(): lax.ppermute(block, 'outer', [(i, (i + 1) % outer) for i in range(outer)])]
    ppermute x13 -> x10, waiting for transfers between devices: 30.6 us -> 23.2 us  [to_partner(): return lax.ppermute(value, axes, [(i, i ^ offset) for i in range(size)])]
    all_to_all x2, waiting for transfers between devices: 0.01 us -> 4.54 us  [swap(): return lax.all_to_all(value, PLANE, split_axis=0, concat_axis=0, tiled=True)]
    all_to_all x2, starting transfers between devices: 7.14 us -> 11.6 us  [swap(): return lax.all_to_all(value, PLANE, split_axis=0, concat_axis=0, tiled=True)]
    unnamed x18 -> x14, local copies, waits for them, and re-layouts: 6.51 us -> 2.61 us
    concatenate x2 -> x5, other arithmetic: 0.04 us -> 2.26 us  [the longest x3 1.48 us: slices(): jnp.concatenate([lax.dynamic_slice_in_dim(adapter_down_maps[0].T, start,...]
    ppermute x13 -> x10, starting transfers between devices: 11.1 us -> 9.88 us  [to_partner(): return lax.ppermute(value, axes, [(i, i ^ offset) for i in range(size)])]
  transfers between devices with their start and end apart: 27 -> 24, of which waited for: 16 -> 16; matrix products, arithmetic and copies ran while one was open for 1% -> 2% of each run, Pallas kernels for 6% -> 5%
where the time goes in v17:
time: 126 us
  waiting for transfers between devices  72.2 us (57%)
  starting transfers between devices  27 us (21%)
  Pallas kernels  11.2 us (9%)
  blocking collectives  7.75 us (6%)
  local copies, waits for them, and re-layouts  5.15 us (4%)
  other arithmetic  2.34 us (2%)
    ppermute x12, waiting for transfers between devices, next_on_ring(): lax.ppermute(block, 'outer', [(i, (i + 1) % outer) for i in range(outer)])  44.5 us
    ppermute x10, waiting for transfers between devices, to_partner(): return lax.ppermute(value, axes, [(i, i ^ offset) for i in range(size)])  23.2 us
    all_to_all x2, starting transfers between devices, swap(): return lax.all_to_all(value, PLANE, split_axis=0, concat_axis=0, tiled=True)  11.6 us
    ppermute x10, starting transfers between devices, to_partner(): return lax.ppermute(value, axes, [(i, i ^ offset) for i in range(size)])  9.88 us
    all_to_all x1, blocking collectives, swap(): return lax.all_to_all(value, PLANE, split_axis=0, concat_axis=0, tiled=True)  7.75 us
    ppermute x12, starting transfers between devices, next_on_ring(): lax.ppermute(block, 'outer', [(i, (i + 1) % outer) for i in range(outer)])  5.57 us
    all_to_all x2, waiting for transfers between devices, swap(): return lax.all_to_all(value, PLANE, split_axis=0, concat_axis=0, tiled=True)  4.54 us
    pallas_call x1, Pallas kernels, down_product(): pl.pallas_call(functools.partial(down_kernel, len(maps), rank), out_shape...  4.34 us
  transfers between devices with their start and end apart: 24, of which 16 were waited for; matrix products, arithmetic and copies ran while one was open for 2% of the time, Pallas kernels for 5%

profile of v17, /device:TPU:0, one launch (start us, length us, event | category | flops | bytes accessed | tf_op | source)
XLA Modules:
  0.0 125.8 jit_solution(871492765805043585)
XLA Ops:
  0.0 1.3 %dynamic-slice_bitcast_fusion = (bf16[64,1024]{1,0:T(8,128)(2,1)S(1)}, bf16[64,1024]{1,0:T(8,128)(2,1)S(1)}, bf16[64,1024]{1,0:T(8,128)(2,1)S(1)}, bf16[64,1024]{1,0:T(8,128)(2,1)S(1)}) fusion(bf16[1,64,8192]{2,1,0:T(8,128)(2,1)} %param.7, s32[]{:T(128)S(6)} %select_n.32, s32[]{:T(128)S(6)} %select_n.30, s32[]{:T(128)S(6)} %select_n.29, s32[]{:T(128)S(6)} %select_n.31), kind=kLoop, calls=%fused_computation.6 | loop fusion | bytes 1048592 | tf_op jit(solution)/shard_map/dynamic_slice | solution.py:274
  1.3 1.1 dynamic-slice_bitcast_fusion.1
  3.7 2.5 %collective-permute-start.1 = (bf16[128,1024]{1,0:T(8,128)(2,1)}, bf16[128,1024]{1,0:T(8,128)(2,1)S(1)}, u32[]{:S(2)}, u32[]{:S(2)}) collective-permute-start(bf16[128,1024]{1,0:T(8,128)(2,1)} %pad_maximum_fusion.2), channel_id=1, source_target_pairs={{0,2},{1,3},{2,0},{3,1},{4,6},{5,7},{6,4},{7,5},{8,10},{9,11},{10,... | collective-permute-start | bytes 786440 | tf_op jit(solution)/shard_map/ppermute | solution.py:27
  7.1 1.6 %outgoing_rows.1 = bf16[8,136,1024]{2,1,0:T(8,128)(2,1)} custom-call(bf16[128,8192]{1,0:T(8,128)(2,1)S(1)} %copy-done, s32[1,128]{1,0:T(1,128)S(1)} %bitcast.26), custom_call_target="tpu_custom_call" | custom-call | tf_op jit(solution)/shard_map/outgoing_rows/pallas_call | solution.py:94
  9.5 1.9 %collective-permute-start.3 = (bf16[128,1024]{1,0:T(8,128)(2,1)S(1)}, bf16[128,1024]{1,0:T(8,128)(2,1)S(1)}, u32[]{:S(2)}, u32[]{:S(2)}) collective-permute-start(bf16[128,1024]{1,0:T(8,128)(2,1)S(1)} %join_blocks.4.refs_0_), channel_id=1, source_target_pairs={{0,4},{4,8},{8,12},{12,0},{1,5},{5,9},{9,13},{13,1},{2,6},{6,10},{... | collective-permute-start | bytes 786440 | tf_op jit(solution)/shard_map/ppermute | solution.py:31
  11.4 3.7 %all-to-all-start = ((bf16[8,136,1024]{2,1,0:T(8,128)(2,1)}), bf16[8,136,1024]{2,1,0:T(8,128)(2,1)S(1)}, u32[]{:S(2)}, u32[]{:S(2)}) async-start(bf16[8,136,1024]{2,1,0:T(8,128)(2,1)} %outgoing_rows.1), calls=%async_computation | async-start | bytes 4456448 | tf_op jit(solution)/shard_map/all_to_all | solution.py:39
  15.1 4.1 %collective-permute-done.2.refs_1_ = bf16[128,1024]{1,0:T(8,128)(2,1)S(1)} collective-permute-done((bf16[128,1024]{1,0:T(8,128)(2,1)}, bf16[128,1024]{1,0:T(8,128)(2,1)S(1)}, u32[]{:S(2)}, u32[]{:S(2)}) %collective-permute-start.2) | collective-permute-done | bytes 262176 | tf_op jit(solution)/shard_map/ppermute | solution.py:27
  19.2 1.6 %collective-permute-start.4 = (bf16[128,1024]{1,0:T(8,128)(2,1)S(1)}, bf16[128,1024]{1,0:T(8,128)(2,1)S(1)}, u32[]{:S(2)}, u32[]{:S(2)}) collective-permute-start(bf16[128,1024]{1,0:T(8,128)(2,1)S(1)} %join_blocks.5.refs_1_), channel_id=1, source_target_pairs={{0,4},{4,8},{8,12},{12,0},{1,5},{5,9},{9,13},{13,1},{2,6},{6,10},{... | collective-permute-start | bytes 786440 | tf_op jit(solution)/shard_map/ppermute | solution.py:31
  20.9 1.6 %collective-permute-start.5 = (bf16[128,1024]{1,0:T(8,128)(2,1)S(1)}, bf16[128,1024]{1,0:T(8,128)(2,1)}, u32[]{:S(2)}, u32[]{:S(2)}) collective-permute-start(bf16[128,1024]{1,0:T(8,128)(2,1)S(1)} %join_blocks.6), channel_id=1, source_target_pairs={{0,4},{4,8},{8,12},{12,0},{1,5},{5,9},{9,13},{13,1},{2,6},{6,10},{... | collective-permute-start | bytes 786440 | tf_op jit(solution)/shard_map/ppermute | solution.py:31
  22.5 8.9 %collective-permute-done.4.refs_0_.refs_3_ = bf16[128,1024]{1,0:T(8,128)(2,1)S(1)} collective-permute-done((bf16[128,1024]{1,0:T(8,128)(2,1)S(1)}, bf16[128,1024]{1,0:T(8,128)(2,1)S(1)}, u32[]{:S(2)}, u32[]{:S(2)}) %collective-permute-start.4) | collective-permute-done | bytes 262176 | tf_op jit(solution)/shard_map/ppermute | solution.py:31
  32.1 5.0 %collective-permute-done.5.refs_4_ = bf16[128,1024]{1,0:T(8,128)(2,1)} collective-permute-done((bf16[128,1024]{1,0:T(8,128)(2,1)S(1)}, bf16[128,1024]{1,0:T(8,128)(2,1)}, u32[]{:S(2)}, u32[]{:S(2)}) %collective-permute-start.5) | collective-permute-done | bytes 262176 | tf_op jit(solution)/shard_map/ppermute | solution.py:31
  37.1 6.1 %collective-permute-done.6.refs_5_ = bf16[128,1024]{1,0:T(8,128)(2,1)} collective-permute-done((bf16[128,1024]{1,0:T(8,128)(2,1)S(1)}, bf16[128,1024]{1,0:T(8,128)(2,1)}, u32[]{:S(2)}, u32[]{:S(2)}) %collective-permute-start.6) | collective-permute-done | bytes 262176 | tf_op jit(solution)/shard_map/ppermute | solution.py:31
  43.3 5.5 %collective-permute-done.7.refs_6_ = bf16[128,1024]{1,0:T(8,128)(2,1)} collective-permute-done((bf16[128,1024]{1,0:T(8,128)(2,1)}, bf16[128,1024]{1,0:T(8,128)(2,1)}, u32[]{:S(2)}, u32[]{:S(2)}) %collective-permute-start.7) | collective-permute-done | bytes 262176 | tf_op jit(solution)/shard_map/ppermute | solution.py:31
  48.9 4.9 %collective-permute-done.8.refs_7_ = bf16[128,1024]{1,0:T(8,128)(2,1)} collective-permute-done((bf16[128,1024]{1,0:T(8,128)(2,1)}, bf16[128,1024]{1,0:T(8,128)(2,1)}, u32[]{:S(2)}, u32[]{:S(2)}) %collective-permute-start.8) | collective-permute-done | bytes 262176 | tf_op jit(solution)/shard_map/ppermute | solution.py:31
  54.3 1.0 copy-done.4
  56.2 4.3 %down_product.1 = (f32[8,64,128]{2,1,0:T(8,128)}, f32[8,128]{1,0:T(8,128)S(1)}) custom-call(s32[16]{0:T(128)S(1)} %add.61.labels_ref, bf16[8,136,1024]{2,1,0:T(8,128)(2,1)S(1)} %all-to-all-done.rows_ref, bf16[128,1024]{1,0:T(8,128)(2,1)S(1)} %join_blocks.4.refs_0_, bf16[128,1024]{1,0:T(8,128)(2,1)S(1)} %copy-done.4, ...), custom_call_target="tpu_custom_call" | custom-call | flops 2147483648 | bytes 4194304 | tf_op jit(solution)/shard_map/down_product/pallas_call | solution.py:146
  60.6 4.4 %collective-permute-done.9.refs_2_ = bf16[128,1024]{1,0:T(8,128)(2,1)} collective-permute-done((bf16[128,1024]{1,0:T(8,128)(2,1)S(1)}, bf16[128,1024]{1,0:T(8,128)(2,1)}, u32[]{:S(2)}, u32[]{:S(2)}) %collective-permute-start.9) | collective-permute-done | bytes 262176 | tf_op jit(solution)/shard_map/ppermute | solution.py:31
  64.9 5.6 %collective-permute-done.10.refs_3_ = bf16[128,1024]{1,0:T(8,128)(2,1)} collective-permute-done((bf16[128,1024]{1,0:T(8,128)(2,1)S(1)}, bf16[128,1024]{1,0:T(8,128)(2,1)}, u32[]{:S(2)}, u32[]{:S(2)}) %collective-permute-start.10) | collective-permute-done | bytes 262176 | tf_op jit(solution)/shard_map/ppermute | solution.py:31
  70.5 7.9 %all-to-all-start.1 = ((f32[8,64,128]{2,1,0:T(8,128)}), f32[8,64,128]{2,1,0:T(8,128)S(1)}, u32[]{:S(2)}, u32[]{:S(2)}) async-start(f32[8,64,128]{2,1,0:T(8,128)} %get-tuple-element.22), calls=%async_computation.1 | async-start | bytes 524288 | tf_op jit(solution)/shard_map/all_to_all | solution.py:39
  78.5 1.4 %collective-permute-done.12.refs_5_ = bf16[128,1024]{1,0:T(8,128)(2,1)S(1)} collective-permute-done((bf16[128,1024]{1,0:T(8,128)(2,1)}, bf16[128,1024]{1,0:T(8,128)(2,1)S(1)}, u32[]{:S(2)}, u32[]{:S(2)}) %collective-permute-start.12) | collective-permute-done | bytes 262176 | tf_op jit(solution)/shard_map/ppermute | solution.py:31
  79.9 4.5 %all-to-all-done.1.terms_ref = f32[8,64,128]{2,1,0:T(8,128)S(1)} async-done(((f32[8,64,128]{2,1,0:T(8,128)}), f32[8,64,128]{2,1,0:T(8,128)S(1)}, u32[]{:S(2)}, u32[]{:S(2)}) %all-to-all-start.1) | async-done | bytes 262176 | tf_op jit(solution)/shard_map/all_to_all | solution.py:39
  84.5 7.8 %all_to_all.15.shrunk_ref = bf16[8,64,128]{2,1,0:T(8,128)(2,1)S(1)} all-to-all(bf16[8,64,128]{2,1,0:T(8,128)(2,1)S(1)} %summed_copies.1), channel_id=1, replica_groups=mesh['groups'=2,'outer'=4,'inner'=4] {'groups','inner'}, dimensions={0} | all-to-all | bytes 262144 | tf_op jit(solution)/shard_map/all_to_all | solution.py:39
  92.2 2.6 %collective-permute-done.14.refs_7_ = bf16[128,1024]{1,0:T(8,128)(2,1)S(1)} collective-permute-done((bf16[128,1024]{1,0:T(8,128)(2,1)S(1)}, bf16[128,1024]{1,0:T(8,128)(2,1)S(1)}, u32[]{:S(2)}, u32[]{:S(2)}) %collective-permute-start.14) | collective-permute-done | bytes 262176 | tf_op jit(solution)/shard_map/ppermute | solution.py:31
  94.8 3.7 %up_product.1 = (bf16[128,1024]{1,0:T(8,128)(2,1)S(1)}, bf16[128,1024]{1,0:T(8,128)(2,1)S(1)}, bf16[128,1024]{1,0:T(8,128)(2,1)S(1)}, bf16[128,1024]{1,0:T(8,128...) custom-call(s32[16]{0:T(128)S(1)} %add.61.labels_ref, ...), custom_call_target="tpu_custom_call" | custom-call | flops 2147483648 | bytes 4194304 | tf_op jit(solution)/shard_map/up_product/pallas_call | solution.py:218
  98.6 2.6 %collective-permute-start.15 = (bf16[128,1024]{1,0:T(8,128)(2,1)S(1)}, bf16[128,1024]{1,0:T(8,128)(2,1)S(1)}, u32[]{:S(2)}, u32[]{:S(2)}) collective-permute-start(bf16[128,1024]{1,0:T(8,128)(2,1)S(1)} %get-tuple-element.27), channel_id=1, source_target_pairs={{0,18},{1,19},{2,16},{3,17},{16,2},{17,3},{18,0},{19,1},{4,22},{5,... | collective-permute-start | bytes 786440 | tf_op jit(solution)/shard_map/ppermute | solution.py:27
  101.8 1.5 %collective-permute-start.18 = (bf16[128,1024]{1,0:T(8,128)(2,1)S(1)}, bf16[128,1024]{1,0:T(8,128)(2,1)S(1)}, u32[]{:S(2)}, u32[]{:S(2)}) collective-permute-start(bf16[128,1024]{1,0:T(8,128)(2,1)S(1)} %get-tuple-element.30), channel_id=1, source_target_pairs={{0,17},{1,16},{2,19},{3,18},{16,1},{17,0},{18,3},{19,2},{4,21},{5,... | collective-permute-start | bytes 786440 | tf_op jit(solution)/shard_map/ppermute | solution.py:27
  103.2 1.5 %collective-permute-start.19 = (bf16[128,1024]{1,0:T(8,128)(2,1)S(1)}, bf16[128,1024]{1,0:T(8,128)(2,1)S(1)}, u32[]{:S(2)}, u32[]{:S(2)}) collective-permute-start(bf16[128,1024]{1,0:T(8,128)(2,1)S(1)} %get-tuple-element.31), channel_id=1, source_target_pairs={{0,2},{1,3},{2,0},{3,1},{16,18},{17,19},{18,16},{19,17},{4,6},{5,7... | collective-permute-start | bytes 786440 | tf_op jit(solution)/shard_map/ppermute | solution.py:27
  104.7 4.1 %collective-permute-done.15.refs_0_ = bf16[128,1024]{1,0:T(8,128)(2,1)S(1)} collective-permute-done((bf16[128,1024]{1,0:T(8,128)(2,1)S(1)}, bf16[128,1024]{1,0:T(8,128)(2,1)S(1)}, u32[]{:S(2)}, u32[]{:S(2)}) %collective-permute-start.15) | collective-permute-done | bytes 262176 | tf_op jit(solution)/shard_map/ppermute | solution.py:27
  108.8 4.8 %collective-permute-done.16.refs_1_ = bf16[128,1024]{1,0:T(8,128)(2,1)S(1)} collective-permute-done((bf16[128,1024]{1,0:T(8,128)(2,1)S(1)}, bf16[128,1024]{1,0:T(8,128)(2,1)S(1)}, u32[]{:S(2)}, u32[]{:S(2)}) %collective-permute-start.16) | collective-permute-done | bytes 262176 | tf_op jit(solution)/shard_map/ppermute | solution.py:27
  114.2 6.0 %collective-permute-done.17.refs_2_ = bf16[128,1024]{1,0:T(8,128)(2,1)S(1)} collective-permute-done((bf16[128,1024]{1,0:T(8,128)(2,1)S(1)}, bf16[128,1024]{1,0:T(8,128)(2,1)S(1)}, u32[]{:S(2)}, u32[]{:S(2)}) %collective-permute-start.17) | collective-permute-done | bytes 262176 | tf_op jit(solution)/shard_map/ppermute | solution.py:27
  120.2 3.2 %collective-permute-done.18.refs_3_ = bf16[128,1024]{1,0:T(8,128)(2,1)S(1)} collective-permute-done((bf16[128,1024]{1,0:T(8,128)(2,1)S(1)}, bf16[128,1024]{1,0:T(8,128)(2,1)S(1)}, u32[]{:S(2)}, u32[]{:S(2)}) %collective-permute-start.18) | collective-permute-done | bytes 262176 | tf_op jit(solution)/shard_map/ppermute | solution.py:27
  124.4 1.4 %place_results.1 = bf16[128,8192]{1,0:T(8,128)(2,1)} custom-call(s32[1]{0:T(128)} %bitcast.me_ref, bf16[128,1024]{1,0:T(8,128)(2,1)S(1)} %collective-permute-done.15.refs_0_, bf16[128,1024]{1,0:T(8,128)(2,1)S(1)} %collective-permute-done.16.refs_1_, bf16[128,1024]{1,0:T(8,128)(2,1)S(1)} %collective-permute-done.17.refs_2_, ...), custom_call_target="tpu_custom_call" | custom-call | tf_op jit(solution)/shard_map/place_results/pallas_call | solution.py:249
  (53 shorter events, 7.4 us)
Async XLA Ops:
  0.0 7.1 %copy-start = (bf16[128,8192]{1,0:T(8,128)(2,1)S(1)}, bf16[128,8192]{1,0:T(8,128)(2,1)}, u32[]{:S(2)}) copy-start(bf16[128,8192]{1,0:T(8,128)(2,1)} %hidden_ref.1) | copy-start | bytes 6291460
  0.0 7.1 %copy-start.2 = (s32[128,1]{0,1:T(1,128)S(1)}, s32[128,1]{0,1:T(1,128)}, u32[]{:S(2)}) copy-start(s32[128,1]{0,1:T(1,128)} %param.4) | copy-start | bytes 1540
  2.5 6.3 %collective-permute-start = (bf16[128,1024]{1,0:T(8,128)(2,1)S(1)}, bf16[128,1024]{1,0:T(8,128)(2,1)S(1)}, u32[]{:S(2)}, u32[]{:S(2)}) collective-permute-start(bf16[128,1024]{1,0:T(8,128)(2,1)S(1)} %pad_maximum_fusion.1), channel_id=1, source_target_pairs={{0,1},{1,0},{2,3},{3,2},{4,5},{5,4},{6,7},{7,6},{8,9},{9,8},{10,11... | collective-permute-start | bytes 786440 | tf_op jit(solution)/shard_map/ppermute | solution.py:27
  3.7 11.4 %collective-permute-start.1 = (bf16[128,1024]{1,0:T(8,128)(2,1)}, bf16[128,1024]{1,0:T(8,128)(2,1)S(1)}, u32[]{:S(2)}, u32[]{:S(2)}) collective-permute-start(bf16[128,1024]{1,0:T(8,128)(2,1)} %pad_maximum_fusion.2), channel_id=1, source_target_pairs={{0,2},{1,3},{2,0},{3,1},{4,6},{5,7},{6,4},{7,5},{8,10},{9,11},{10,... | collective-permute-start | bytes 786440 | tf_op jit(solution)/shard_map/ppermute | solution.py:27
  7.0 12.2 %collective-permute-start.2 = (bf16[128,1024]{1,0:T(8,128)(2,1)}, bf16[128,1024]{1,0:T(8,128)(2,1)S(1)}, u32[]{:S(2)}, u32[]{:S(2)}) collective-permute-start(bf16[128,1024]{1,0:T(8,128)(2,1)} %pad_maximum_fusion.3), channel_id=1, source_target_pairs={{0,3},{1,2},{2,1},{3,0},{4,7},{5,6},{6,5},{7,4},{8,11},{9,10},{10,... | collective-permute-start | bytes 786440 | tf_op jit(solution)/shard_map/ppermute | solution.py:27
  9.5 11.3 %collective-permute-start.3 = (bf16[128,1024]{1,0:T(8,128)(2,1)S(1)}, bf16[128,1024]{1,0:T(8,128)(2,1)S(1)}, u32[]{:S(2)}, u32[]{:S(2)}) collective-permute-start(bf16[128,1024]{1,0:T(8,128)(2,1)S(1)} %join_blocks.4.refs_0_), channel_id=1, source_target_pairs={{0,4},{4,8},{8,12},{12,0},{1,5},{5,9},{9,13},{13,1},{2,6},{6,10},{... | collective-permute-start | bytes 786440 | tf_op jit(solution)/shard_map/ppermute | solution.py:31
  11.4 43.0 %all-to-all-start = ((bf16[8,136,1024]{2,1,0:T(8,128)(2,1)}), bf16[8,136,1024]{2,1,0:T(8,128)(2,1)S(1)}, u32[]{:S(2)}, u32[]{:S(2)}) async-start(bf16[8,136,1024]{2,1,0:T(8,128)(2,1)} %outgoing_rows.1), calls=%async_computation | async-start | bytes 4456448 | tf_op jit(solution)/shard_map/all_to_all | solution.py:39
  19.2 1.7 %copy-start.3 = (bf16[128,1024]{1,0:T(8,128)(2,1)}, bf16[128,1024]{1,0:T(8,128)(2,1)S(1)}, u32[]{:S(2)}) copy-start(bf16[128,1024]{1,0:T(8,128)(2,1)S(1)} %join_blocks.5.refs_1_) | copy-start | bytes 786436
  19.2 12.2 %collective-permute-start.4 = (bf16[128,1024]{1,0:T(8,128)(2,1)S(1)}, bf16[128,1024]{1,0:T(8,128)(2,1)S(1)}, u32[]{:S(2)}, u32[]{:S(2)}) collective-permute-start(bf16[128,1024]{1,0:T(8,128)(2,1)S(1)} %join_blocks.5.refs_1_), channel_id=1, source_target_pairs={{0,4},{4,8},{8,12},{12,0},{1,5},{5,9},{9,13},{13,1},{2,6},{6,10},{... | collective-permute-start | bytes 786440 | tf_op jit(solution)/shard_map/ppermute | solution.py:31
  20.9 32.9 %copy-start.1 = (bf16[128,1024]{1,0:T(8,128)(2,1)S(1)}, bf16[128,1024]{1,0:T(8,128)(2,1)}, u32[]{:S(2)}) copy-start(bf16[128,1024]{1,0:T(8,128)(2,1)} %get-tuple-element.23.refs_0_) | copy-start | bytes 786436
  20.9 16.2 %collective-permute-start.5 = (bf16[128,1024]{1,0:T(8,128)(2,1)S(1)}, bf16[128,1024]{1,0:T(8,128)(2,1)}, u32[]{:S(2)}, u32[]{:S(2)}) collective-permute-start(bf16[128,1024]{1,0:T(8,128)(2,1)S(1)} %join_blocks.6), channel_id=1, source_target_pairs={{0,4},{4,8},{8,12},{12,0},{1,5},{5,9},{9,13},{13,1},{2,6},{6,10},{... | collective-permute-start | bytes 786440 | tf_op jit(solution)/shard_map/ppermute | solution.py:31
  31.4 0.7 copy-start.5
  32.1 11.2 %collective-permute-start.6 = (bf16[128,1024]{1,0:T(8,128)(2,1)S(1)}, bf16[128,1024]{1,0:T(8,128)(2,1)}, u32[]{:S(2)}, u32[]{:S(2)}) collective-permute-start(bf16[128,1024]{1,0:T(8,128)(2,1)S(1)} %join_blocks.7), channel_id=1, source_target_pairs={{0,4},{4,8},{8,12},{12,0},{1,5},{5,9},{9,13},{13,1},{2,6},{6,10},{... | collective-permute-start | bytes 786440 | tf_op jit(solution)/shard_map/ppermute | solution.py:31
  37.1 11.8 %collective-permute-start.7 = (bf16[128,1024]{1,0:T(8,128)(2,1)}, bf16[128,1024]{1,0:T(8,128)(2,1)}, u32[]{:S(2)}, u32[]{:S(2)}) collective-permute-start(bf16[128,1024]{1,0:T(8,128)(2,1)} %collective-permute-done.5.refs_4_), channel_id=1, source_target_pairs={{0,4},{4,8},{8,12},{12,0},{1,5},{5,9},{9,13},{13,1},{2,6},{6,10},{... | collective-permute-start | bytes 786440 | tf_op jit(solution)/shard_map/ppermute | solution.py:31
  43.3 10.5 %collective-permute-start.8 = (bf16[128,1024]{1,0:T(8,128)(2,1)}, bf16[128,1024]{1,0:T(8,128)(2,1)}, u32[]{:S(2)}, u32[]{:S(2)}) collective-permute-start(bf16[128,1024]{1,0:T(8,128)(2,1)} %collective-permute-done.6.refs_5_), channel_id=1, source_target_pairs={{0,4},{4,8},{8,12},{12,0},{1,5},{5,9},{9,13},{13,1},{2,6},{6,10},{... | collective-permute-start | bytes 786440 | tf_op jit(solution)/shard_map/ppermute | solution.py:31
  53.8 11.1 %collective-permute-start.9 = (bf16[128,1024]{1,0:T(8,128)(2,1)S(1)}, bf16[128,1024]{1,0:T(8,128)(2,1)}, u32[]{:S(2)}, u32[]{:S(2)}) collective-permute-start(bf16[128,1024]{1,0:T(8,128)(2,1)S(1)} %copy-done.1), channel_id=1, source_target_pairs={{0,4},{4,8},{8,12},{12,0},{1,5},{5,9},{9,13},{13,1},{2,6},{6,10},{... | collective-permute-start | bytes 786440 | tf_op jit(solution)/shard_map/ppermute | solution.py:31
  53.8 16.8 %collective-permute-start.10 = (bf16[128,1024]{1,0:T(8,128)(2,1)S(1)}, bf16[128,1024]{1,0:T(8,128)(2,1)}, u32[]{:S(2)}, u32[]{:S(2)}) collective-permute-start(bf16[128,1024]{1,0:T(8,128)(2,1)S(1)} %pad_maximum_fusion.5.refs_1_), channel_id=1, source_target_pairs={{0,4},{4,8},{8,12},{12,0},{1,5},{5,9},{9,13},{13,1},{2,6},{6,10},{... | collective-permute-start | bytes 786440 | tf_op jit(solution)/shard_map/ppermute | solution.py:31
  54.3 1.0 copy-start.4
  55.3 0.9 copy-start.6
  64.9 13.5 %collective-permute-start.11 = (bf16[128,1024]{1,0:T(8,128)(2,1)}, bf16[128,1024]{1,0:T(8,128)(2,1)S(1)}, u32[]{:S(2)}, u32[]{:S(2)}) collective-permute-start(bf16[128,1024]{1,0:T(8,128)(2,1)} %collective-permute-done.9.refs_2_), channel_id=1, source_target_pairs={{0,4},{4,8},{8,12},{12,0},{1,5},{5,9},{9,13},{13,1},{2,6},{6,10},{... | collective-permute-start | bytes 786440 | tf_op jit(solution)/shard_map/ppermute | solution.py:31
  70.5 9.4 %collective-permute-start.12 = (bf16[128,1024]{1,0:T(8,128)(2,1)}, bf16[128,1024]{1,0:T(8,128)(2,1)S(1)}, u32[]{:S(2)}, u32[]{:S(2)}) collective-permute-start(bf16[128,1024]{1,0:T(8,128)(2,1)} %collective-permute-done.10.refs_3_), channel_id=1, source_target_pairs={{0,4},{4,8},{8,12},{12,0},{1,5},{5,9},{9,13},{13,1},{2,6},{6,10},{... | collective-permute-start | bytes 786440 | tf_op jit(solution)/shard_map/ppermute | solution.py:31
  70.5 13.9 %all-to-all-start.1 = ((f32[8,64,128]{2,1,0:T(8,128)}), f32[8,64,128]{2,1,0:T(8,128)S(1)}, u32[]{:S(2)}, u32[]{:S(2)}) async-start(f32[8,64,128]{2,1,0:T(8,128)} %get-tuple-element.22), calls=%async_computation.1 | async-start | bytes 524288 | tf_op jit(solution)/shard_map/all_to_all | solution.py:39
  78.4 13.8 %collective-permute-start.13 = (bf16[128,1024]{1,0:T(8,128)(2,1)S(1)}, bf16[128,1024]{1,0:T(8,128)(2,1)S(1)}, u32[]{:S(2)}, u32[]{:S(2)}) collective-permute-start(bf16[128,1024]{1,0:T(8,128)(2,1)S(1)} %collective-permute-done.11.refs_4_), channel_id=1, source_target_pairs={{0,4},{4,8},{8,12},{12,0},{1,5},{5,9},{9,13},{13,1},{2,6},{6,10},{... | collective-permute-start | bytes 786440 | tf_op jit(solution)/shard_map/ppermute | solution.py:31
  79.9 14.9 %collective-permute-start.14 = (bf16[128,1024]{1,0:T(8,128)(2,1)S(1)}, bf16[128,1024]{1,0:T(8,128)(2,1)S(1)}, u32[]{:S(2)}, u32[]{:S(2)}) collective-permute-start(bf16[128,1024]{1,0:T(8,128)(2,1)S(1)} %collective-permute-done.12.refs_5_), channel_id=1, source_target_pairs={{0,4},{4,8},{8,12},{12,0},{1,5},{5,9},{9,13},{13,1},{2,6},{6,10},{... | collective-permute-start | bytes 786440 | tf_op jit(solution)/shard_map/ppermute | solution.py:31
  98.6 10.2 %collective-permute-start.15 = (bf16[128,1024]{1,0:T(8,128)(2,1)S(1)}, bf16[128,1024]{1,0:T(8,128)(2,1)S(1)}, u32[]{:S(2)}, u32[]{:S(2)}) collective-permute-start(bf16[128,1024]{1,0:T(8,128)(2,1)S(1)} %get-tuple-element.27), channel_id=1, source_target_pairs={{0,18},{1,19},{2,16},{3,17},{16,2},{17,3},{18,0},{19,1},{4,22},{5,... | collective-permute-start | bytes 786440 | tf_op jit(solution)/shard_map/ppermute | solution.py:27
  101.2 12.4 %collective-permute-start.16 = (bf16[128,1024]{1,0:T(8,128)(2,1)S(1)}, bf16[128,1024]{1,0:T(8,128)(2,1)S(1)}, u32[]{:S(2)}, u32[]{:S(2)}) collective-permute-start(bf16[128,1024]{1,0:T(8,128)(2,1)S(1)} %get-tuple-element.28), channel_id=1, source_target_pairs={{0,19},{1,18},{2,17},{3,16},{16,3},{17,2},{18,1},{19,0},{4,23},{5,... | collective-permute-start | bytes 786440 | tf_op jit(solution)/shard_map/ppermute | solution.py:27
  101.2 19.0 %collective-permute-start.17 = (bf16[128,1024]{1,0:T(8,128)(2,1)S(1)}, bf16[128,1024]{1,0:T(8,128)(2,1)S(1)}, u32[]{:S(2)}, u32[]{:S(2)}) collective-permute-start(bf16[128,1024]{1,0:T(8,128)(2,1)S(1)} %get-tuple-element.29), channel_id=1, source_target_pairs={{0,16},{1,17},{2,18},{3,19},{16,0},{17,1},{18,2},{19,3},{4,20},{5,... | collective-permute-start | bytes 786440 | tf_op jit(solution)/shard_map/ppermute | solution.py:27
  101.8 21.7 %collective-permute-start.18 = (bf16[128,1024]{1,0:T(8,128)(2,1)S(1)}, bf16[128,1024]{1,0:T(8,128)(2,1)S(1)}, u32[]{:S(2)}, u32[]{:S(2)}) collective-permute-start(bf16[128,1024]{1,0:T(8,128)(2,1)S(1)} %get-tuple-element.30), channel_id=1, source_target_pairs={{0,17},{1,16},{2,19},{3,18},{16,1},{17,0},{18,3},{19,2},{4,21},{5,... | collective-permute-start | bytes 786440 | tf_op jit(solution)/shard_map/ppermute | solution.py:27
  103.2 20.2 %collective-permute-start.19 = (bf16[128,1024]{1,0:T(8,128)(2,1)S(1)}, bf16[128,1024]{1,0:T(8,128)(2,1)S(1)}, u32[]{:S(2)}, u32[]{:S(2)}) collective-permute-start(bf16[128,1024]{1,0:T(8,128)(2,1)S(1)} %get-tuple-element.31), channel_id=1, source_target_pairs={{0,2},{1,3},{2,0},{3,1},{16,18},{17,19},{18,16},{19,17},{4,6},{5,7... | collective-permute-start | bytes 786440 | tf_op jit(solution)/shard_map/ppermute | solution.py:27
  108.8 15.6 %collective-permute-start.20 = (bf16[128,1024]{1,0:T(8,128)(2,1)S(1)}, bf16[128,1024]{1,0:T(8,128)(2,1)S(1)}, u32[]{:S(2)}, u32[]{:S(2)}) collective-permute-start(bf16[128,1024]{1,0:T(8,128)(2,1)S(1)} %get-tuple-element.32), channel_id=1, source_target_pairs={{0,3},{1,2},{2,1},{3,0},{16,19},{17,18},{18,17},{19,16},{4,7},{5,6... | collective-permute-start | bytes 786440 | tf_op jit(solution)/shard_map/ppermute | solution.py:27
  113.6 10.8 %collective-permute-start.21 = (bf16[128,1024]{1,0:T(8,128)(2,1)S(1)}, bf16[128,1024]{1,0:T(8,128)(2,1)S(1)}, u32[]{:S(2)}, u32[]{:S(2)}) collective-permute-start(bf16[128,1024]{1,0:T(8,128)(2,1)S(1)} %get-tuple-element.33), channel_id=1, source_target_pairs={{0,1},{1,0},{2,3},{3,2},{16,17},{17,16},{18,19},{19,18},{4,5},{5,4... | collective-permute-start | bytes 786440 | tf_op jit(solution)/shard_map/ppermute | solution.py:27

commit v18 on v16

--- a/solution.py
+++ b/solution.py
@@ -12,7 +12,7 @@
 PLANE = ("groups", "inner")
 LANES = 128
 ID_ROWS = 8
-AHEAD, SLIGHTLY_AHEAD, SUM_AHEAD = 10**11, 3 * 10**9, 4 * 10**9
+AHEAD, SLIGHTLY_AHEAD = 10**11, 6 * 10**9
 BLOCK = 8
 IN_VMEM = pl.BlockSpec(memory_space=pltpu.VMEM)
 IN_SMEM = pl.BlockSpec(memory_space=pltpu.SMEM)
@@ -178,7 +178,6 @@
         in_specs=[IN_VMEM],
         out_specs=IN_VMEM,
         compiler_params=params(),
-        cost_estimate=pl.CostEstimate(flops=SUM_AHEAD, bytes_accessed=10**6, transcendentals=0),
         name="summed_copies",
     )(terms)
 
@@ -231,23 +230,23 @@
     )(labels, me, ids, shrunk, *maps)
 
 
-def place_kernel(me_ref, *refs):
+def place_kernel(offsets, me_ref, *refs):
     blocks, out_ref, sems = refs[:-2], refs[-2], refs[-1]
     share = blocks[0].shape[1]
     copies = []
-    for offset, block in enumerate(blocks):
-        at = pl.multiple_of((me_ref[0] ^ offset) * share, LANES)
-        copies.append(pltpu.make_async_copy(block, out_ref.at[:, pl.ds(at, share)], sems.at[offset]))
+    for n, block in enumerate(blocks):
+        at = pl.multiple_of((me_ref[0] ^ offsets[n]) * share, LANES)
+        copies.append(pltpu.make_async_copy(block, out_ref.at[:, pl.ds(at, share)], sems.at[n]))
     for copy in copies:
         copy.start()
     for copy in copies:
         copy.wait()
 
 
-def place(me, blocks):
+def place(me, offsets, blocks):
     tok, share = blocks[0].shape
     return pl.pallas_call(
-        place_kernel,
+        functools.partial(place_kernel, offsets),
         out_shape=jax.ShapeDtypeStruct((tok, len(blocks) * share), jnp.bfloat16),
         in_specs=[IN_SMEM] + [ANYWHERE] * len(blocks),
         out_specs=ANYWHERE,
@@ -274,15 +273,13 @@
     def exchanged(blocks):
         return blocks[:1] + [to_partner(blocks[n], "inner", inner, n) for n in range(1, inner)]
 
-    def rings(near, far, first_cost=0, second_after=()):
+    def rings(near, far, first_cost=0):
         near, far = [near], [far]
         for step in range(1, outer):
             for blocks in near, far:
                 block = blocks[-1]
-                if step == 2:
-                    block = after(block, *second_after)
-                    if first_cost:
-                        block = joined([block], first_cost)
+                if step == 2 and first_cost:
+                    block = joined([block], first_cost)
                 blocks.append(next_on_ring(block, outer))
         return near, far
 
@@ -296,22 +293,21 @@
     down = exchanged(slices(adapter_down_maps[0].T))
     down_near, down_far = rings(joined(down[:middle], AHEAD), joined(down[middle:], AHEAD), first_cost=SLIGHTLY_AHEAD)
     ids = token_adapter_index.reshape(1, tok)
-    rows = swap(after(outgoing_rows(hidden, ids, members), down_near[0]))
+    rows = swap(outgoing_rows(after(hidden, down_near[0]), ids, members))
     up = exchanged([after(block, down_near[1]) for block in slices(adapter_up_maps[0])])
 
     down_maps = [m for pair in zip(down_near, down_far) for m in pair]
     packed, id_rows = down_product(labels, rows, down_maps, rank)
     up_near, up_far = rings(
         after(jnp.concatenate(up[:middle], axis=0), down_near[-1]),
-        after(jnp.concatenate(up[middle:], axis=0), down_far[-1]),
-        second_after=[packed],
+        after(jnp.concatenate(up[middle:], axis=0), down_far[-1], packed),
     )
     up_maps = [m for pair in zip(up_near, up_far) for m in pair]
     shrunk = swap(summed_copies(swap(packed)))
     results = list(up_product(labels, me.reshape(1), id_rows, shrunk, up_maps, rank))
-    order = sorted(range(1, members), key=lambda n: (-(n >= inner) - (n % inner >= 2), -(n >= inner), n))
-    returned = {n: to_partner(results[n], PLANE, members, n) for n in order}
-    return place(me.reshape(1), results[:1] + [returned[n] for n in range(1, members)])
+    offsets = sorted(range(1, members), key=lambda n: (-(n >= inner) - (n % inner >= 2), -(n >= inner), n))
+    returned = [to_partner(results[n], PLANE, members, n) for n in offsets]
+    return place(me.reshape(1), offsets + [0], returned + results[:1])
 
 
 def solution(mesh):

time: 118 us -> 115 us (0.975)
  blocking collectives: 7.57 us -> 0 us
  starting transfers between devices: 24.9 us -> 30.4 us
  local copies, waits for them, and re-layouts: 8.5 us -> 4.72 us
  other arithmetic: 0.12 us -> 1.99 us
    all_to_all x1 -> x0, blocking collectives: 7.57 us -> none  [swap(): return lax.all_to_all(value, PLANE, split_axis=0, concat_axis=0, tiled=True)]
    unnamed x18 -> x10, local copies, waits for them, and re-layouts: 6.51 us -> 1.63 us
    ppermute x13, waiting for transfers between devices: 30.6 us -> 26.7 us  [to_partner(): return lax.ppermute(value, axes, [(i, i ^ offset) for i in range(size)])]
    all_to_all x2 -> x3, waiting for transfers between devices: 0.01 us -> 3.4 us  [swap(): return lax.all_to_all(value, PLANE, split_axis=0, concat_axis=0, tiled=True)]
    all_to_all x2 -> x3, starting transfers between devices: 7.14 us -> 10.5 us  [swap(): return lax.all_to_all(value, PLANE, split_axis=0, concat_axis=0, tiled=True)]
  transfers between devices with their start and end apart: 27 -> 28, of which waited for: 16 -> 18; matrix products, arithmetic and copies ran while one was open for 1% -> 3% of each run, Pallas kernels for 6% -> 7%
where the time goes in v18:
time: 115 us; the launch traced here: 114 us
  waiting for transfers between devices  64.6 us (56%)
  starting transfers between devices  30.4 us (26%)
  Pallas kernels  12.5 us (11%)
  local copies, waits for them, and re-layouts  4.72 us (4%)
  other arithmetic  1.99 us (2%)
    ppermute x12, waiting for transfers between devices, next_on_ring(): lax.ppermute(block, 'outer', [(i, (i + 1) % outer) for i in range(outer)])  34.5 us
    ppermute x13, waiting for transfers between devices, to_partner(): return lax.ppermute(value, axes, [(i, i ^ offset) for i in range(size)])  26.7 us
    ppermute x13, starting transfers between devices, to_partner(): return lax.ppermute(value, axes, [(i, i ^ offset) for i in range(size)])  12 us
    all_to_all x3, starting transfers between devices, swap(): return lax.all_to_all(value, PLANE, split_axis=0, concat_axis=0, tiled=True)  10.5 us
    ppermute x12, starting transfers between devices, next_on_ring(): lax.ppermute(block, 'outer', [(i, (i + 1) % outer) for i in range(outer)])  7.81 us
    pallas_call x1, Pallas kernels, down_product(): pl.pallas_call(functools.partial(down_kernel, len(maps), rank), out_shape...  4.34 us
    pallas_call x1, Pallas kernels, up_product(): pl.pallas_call(functools.partial(up_kernel, len(maps), rank), out_shape=[...  3.65 us
    all_to_all x3, waiting for transfers between devices, swap(): return lax.all_to_all(value, PLANE, split_axis=0, concat_axis=0, tiled=True)  3.4 us
  transfers between devices with their start and end apart: 28, of which 18 were waited for; matrix products, arithmetic and copies ran while one was open for 3% of the time, Pallas kernels for 7%

profile of v18, /device:TPU:0, one launch (start us, length us, event | category | flops | bytes accessed | tf_op | source)
XLA Modules:
  0.0 114.3 jit_solution(6374336105948519034)
XLA Ops:
  1.7 2.6 %collective-permute-start.1 = (bf16[64,1024]{1,0:T(8,128)(2,1)S(1)}, bf16[64,1024]{1,0:T(8,128)(2,1)S(1)}, u32[]{:S(2)}, u32[]{:S(2)}) collective-permute-start(bf16[64,1024]{1,0:T(8,128)(2,1)S(1)} %get-tuple-element.46), channel_id=1, source_target_pairs={{0,2},{1,3},{2,0},{3,1},{4,6},{5,7},{6,4},{7,5},{8,10},{9,11},{10,... | collective-permute-start | bytes 393224 | tf_op jit(solution)/shard_map/ppermute | solution.py:27
  4.3 1.8 %collective-permute-start.3 = (bf16[128,1024]{1,0:T(8,128)(2,1)S(1)}, bf16[128,1024]{1,0:T(8,128)(2,1)S(1)}, u32[]{:S(2)}, u32[]{:S(2)}) collective-permute-start(bf16[128,1024]{1,0:T(8,128)(2,1)S(1)} %join_blocks.4.refs_0_), channel_id=1, source_target_pairs={{0,4},{4,8},{8,12},{12,0},{1,5},{5,9},{9,13},{13,1},{2,6},{6,10},{... | collective-permute-start | bytes 786440 | tf_op jit(solution)/shard_map/ppermute | solution.py:31
  6.2 1.6 %outgoing_rows.1 = bf16[8,136,1024]{2,1,0:T(8,128)(2,1)} custom-call(bf16[128,8192]{1,0:T(8,128)(2,1)S(1)} %copy-done, s32[1,128]{1,0:T(1,128)S(1)} %bitcast.26), custom_call_target="tpu_custom_call" | custom-call | tf_op jit(solution)/shard_map/outgoing_rows/pallas_call | solution.py:94
  7.8 3.7 %all-to-all-start = ((bf16[8,136,1024]{2,1,0:T(8,128)(2,1)}), bf16[8,136,1024]{2,1,0:T(8,128)(2,1)S(1)}, u32[]{:S(2)}, u32[]{:S(2)}) async-start(bf16[8,136,1024]{2,1,0:T(8,128)(2,1)} %outgoing_rows.1), calls=%async_computation | async-start | bytes 4456448 | tf_op jit(solution)/shard_map/all_to_all | solution.py:39
  11.6 1.6 %collective-permute-start.4 = (bf16[128,1024]{1,0:T(8,128)(2,1)S(1)}, bf16[128,1024]{1,0:T(8,128)(2,1)S(1)}, u32[]{:S(2)}, u32[]{:S(2)}) collective-permute-start(bf16[128,1024]{1,0:T(8,128)(2,1)S(1)} %join_blocks.5.refs_1_), channel_id=1, source_target_pairs={{0,4},{4,8},{8,12},{12,0},{1,5},{5,9},{9,13},{13,1},{2,6},{6,10},{... | collective-permute-start | bytes 786440 | tf_op jit(solution)/shard_map/ppermute | solution.py:31
  13.2 1.8 %collective-permute-done.3.refs_0_.refs_2_ = bf16[128,1024]{1,0:T(8,128)(2,1)S(1)} collective-permute-done((bf16[128,1024]{1,0:T(8,128)(2,1)S(1)}, bf16[128,1024]{1,0:T(8,128)(2,1)S(1)}, u32[]{:S(2)}, u32[]{:S(2)}) %collective-permute-start.3) | collective-permute-done | bytes 262176 | tf_op jit(solution)/shard_map/ppermute | solution.py:31
  15.1 7.4 %collective-permute-done.4.refs_0_.refs_3_ = bf16[128,1024]{1,0:T(8,128)(2,1)S(1)} collective-permute-done((bf16[128,1024]{1,0:T(8,128)(2,1)S(1)}, bf16[128,1024]{1,0:T(8,128)(2,1)S(1)}, u32[]{:S(2)}, u32[]{:S(2)}) %collective-permute-start.4) | collective-permute-done | bytes 262176 | tf_op jit(solution)/shard_map/ppermute | solution.py:31
  23.3 1.9 %dynamic-slice_bitcast_fusion.1 = (bf16[64,1024]{1,0:T(8,128)(2,1)}, bf16[64,1024]{1,0:T(8,128)(2,1)}, bf16[64,1024]{1,0:T(8,128)(2,1)S(1)}, bf16[64,1024]{1,0:T(8,128)(2,1)}) fusion(bf16[1,64,8192]{2,1,0:T(8,128)(2,1)} %param.7, s32[]{:T(128)S(6)} %select_n.31, s32[]{:T(128)S(6)} %select_n.30, s32[]{:T(128)S(6)} %select_n.29, s32[]{:T(128)S(6)} %select_n.32), kind=kLoop, calls=%fused_computation.3 | loop fusion | bytes 1048592 | tf_op jit(solution)/shard_map/dynamic_slice | solution.py:270
  25.2 2.2 %collective-permute-start.11 = (bf16[64,1024]{1,0:T(8,128)(2,1)}, bf16[64,1024]{1,0:T(8,128)(2,1)S(1)}, u32[]{:S(2)}, u32[]{:S(2)}) collective-permute-start(bf16[64,1024]{1,0:T(8,128)(2,1)} %get-tuple-element.29), channel_id=1, source_target_pairs={{0,3},{1,2},{2,1},{3,0},{4,7},{5,6},{6,5},{7,4},{8,11},{9,10},{10,... | collective-permute-start | bytes 393224 | tf_op jit(solution)/shard_map/ppermute | solution.py:27
  28.8 5.6 %collective-permute-done.6.refs_5_ = bf16[128,1024]{1,0:T(8,128)(2,1)} collective-permute-done((bf16[128,1024]{1,0:T(8,128)(2,1)}, bf16[128,1024]{1,0:T(8,128)(2,1)}, u32[]{:S(2)}, u32[]{:S(2)}) %collective-permute-start.6) | collective-permute-done | bytes 262176 | tf_op jit(solution)/shard_map/ppermute | solution.py:31
  35.5 5.5 %collective-permute-done.11 = bf16[64,1024]{1,0:T(8,128)(2,1)S(1)} collective-permute-done((bf16[64,1024]{1,0:T(8,128)(2,1)}, bf16[64,1024]{1,0:T(8,128)(2,1)S(1)}, u32[]{:S(2)}, u32[]{:S(2)}) %collective-permute-start.11) | collective-permute-done | bytes 131104 | tf_op jit(solution)/shard_map/ppermute | solution.py:27
  41.6 2.7 %collective-permute-done.10 = bf16[64,1024]{1,0:T(8,128)(2,1)} collective-permute-done((bf16[64,1024]{1,0:T(8,128)(2,1)}, bf16[64,1024]{1,0:T(8,128)(2,1)}, u32[]{:S(2)}, u32[]{:S(2)}) %collective-permute-start.10) | collective-permute-done | bytes 131104 | tf_op jit(solution)/shard_map/ppermute | solution.py:27
  45.4 1.6 %collective-permute-start.12 = (bf16[128,1024]{1,0:T(8,128)(2,1)S(1)}, bf16[128,1024]{1,0:T(8,128)(2,1)}, u32[]{:S(2)}, u32[]{:S(2)}) collective-permute-start(bf16[128,1024]{1,0:T(8,128)(2,1)S(1)} %pad_maximum_fusion.refs_0_), channel_id=1, source_target_pairs={{0,4},{4,8},{8,12},{12,0},{1,5},{5,9},{9,13},{13,1},{2,6},{6,10},{... | collective-permute-start | bytes 786440 | tf_op jit(solution)/shard_map/ppermute | solution.py:31
  48.0 4.3 %down_product.1 = (f32[8,64,128]{2,1,0:T(8,128)}, f32[8,128]{1,0:T(8,128)S(1)}) custom-call(s32[16]{0:T(128)S(1)} %add.61.labels_ref, bf16[8,136,1024]{2,1,0:T(8,128)(2,1)S(1)} %all-to-all-done.rows_ref, bf16[128,1024]{1,0:T(8,128)(2,1)S(1)} %join_blocks.4.refs_0_, bf16[128,1024]{1,0:T(8,128)(2,1)S(1)} %join_blocks.5.refs_1_, ...), custom_call_target="tpu_custom_call" | custom-call | flops 2147483648 | bytes 4194304 | tf_op jit(solution)/shard_map/down_product/pallas_call | solution.py:146
  52.3 1.6 %collective-permute-start.13 = (bf16[128,1024]{1,0:T(8,128)(2,1)S(1)}, bf16[128,1024]{1,0:T(8,128)(2,1)S(1)}, u32[]{:S(2)}, u32[]{:S(2)}) collective-permute-start(bf16[128,1024]{1,0:T(8,128)(2,1)S(1)} %pad_maximum_fusion.1.refs_1_), channel_id=1, source_target_pairs={{0,4},{4,8},{8,12},{12,0},{1,5},{5,9},{9,13},{13,1},{2,6},{6,10},{... | collective-permute-start | bytes 786440 | tf_op jit(solution)/shard_map/ppermute | solution.py:31
  55.4 8.0 %collective-permute-done.13.refs_3_ = bf16[128,1024]{1,0:T(8,128)(2,1)S(1)} collective-permute-done((bf16[128,1024]{1,0:T(8,128)(2,1)S(1)}, bf16[128,1024]{1,0:T(8,128)(2,1)S(1)}, u32[]{:S(2)}, u32[]{:S(2)}) %collective-permute-start.13) | collective-permute-done | bytes 262176 | tf_op jit(solution)/shard_map/ppermute | solution.py:31
  63.3 3.4 %all-to-all-start.1 = ((f32[8,64,128]{2,1,0:T(8,128)}), f32[8,64,128]{2,1,0:T(8,128)S(1)}, u32[]{:S(2)}, u32[]{:S(2)}) async-start(f32[8,64,128]{2,1,0:T(8,128)} %get-tuple-element.24), calls=%async_computation.1 | async-start | bytes 524288 | tf_op jit(solution)/shard_map/all_to_all | solution.py:39
  66.8 2.2 %collective-permute-done.14.refs_4_ = bf16[128,1024]{1,0:T(8,128)(2,1)S(1)} collective-permute-done((bf16[128,1024]{1,0:T(8,128)(2,1)}, bf16[128,1024]{1,0:T(8,128)(2,1)S(1)}, u32[]{:S(2)}, u32[]{:S(2)}) %collective-permute-start.14) | collective-permute-done | bytes 262176 | tf_op jit(solution)/shard_map/ppermute | solution.py:31
  69.0 4.9 %collective-permute-done.15.refs_5_ = bf16[128,1024]{1,0:T(8,128)(2,1)S(1)} collective-permute-done((bf16[128,1024]{1,0:T(8,128)(2,1)S(1)}, bf16[128,1024]{1,0:T(8,128)(2,1)S(1)}, u32[]{:S(2)}, u32[]{:S(2)}) %collective-permute-start.15) | collective-permute-done | bytes 262176 | tf_op jit(solution)/shard_map/ppermute | solution.py:31
  74.9 3.4 %all-to-all-start.2 = ((bf16[8,64,128]{2,1,0:T(8,128)(2,1)}), bf16[8,64,128]{2,1,0:T(8,128)(2,1)S(1)}, u32[]{:S(2)}, u32[]{:S(2)}) async-start(bf16[8,64,128]{2,1,0:T(8,128)(2,1)} %summed_copies.1), calls=%async_computation.2 | async-start | bytes 262144 | tf_op jit(solution)/shard_map/all_to_all | solution.py:39
  78.3 1.7 %collective-permute-done.16.refs_6_ = bf16[128,1024]{1,0:T(8,128)(2,1)S(1)} collective-permute-done((bf16[128,1024]{1,0:T(8,128)(2,1)S(1)}, bf16[128,1024]{1,0:T(8,128)(2,1)S(1)}, u32[]{:S(2)}, u32[]{:S(2)}) %collective-permute-start.16) | collective-permute-done | bytes 262176 | tf_op jit(solution)/shard_map/ppermute | solution.py:31
  80.0 3.4 %all-to-all-done.2.shrunk_ref = bf16[8,64,128]{2,1,0:T(8,128)(2,1)S(1)} async-done(((bf16[8,64,128]{2,1,0:T(8,128)(2,1)}), bf16[8,64,128]{2,1,0:T(8,128)(2,1)S(1)}, u32[]{:S(2)}, u32[]{:S(2)}) %all-to-all-start.2) | async-done | bytes 131104 | tf_op jit(solution)/shard_map/all_to_all | solution.py:39
  84.1 3.6 %up_product.1 = (bf16[128,1024]{1,0:T(8,128)(2,1)S(1)}, bf16[128,1024]{1,0:T(8,128)(2,1)S(1)}, bf16[128,1024]{1,0:T(8,128)(2,1)S(1)}, bf16[128,1024]{1,0:T(8,128...) custom-call(s32[16]{0:T(128)S(1)} %add.61.labels_ref, ...), custom_call_target="tpu_custom_call" | custom-call | flops 2147483648 | bytes 4194304 | tf_op jit(solution)/shard_map/up_product/pallas_call | solution.py:217
  87.8 1.7 %collective-permute-start.18 = (bf16[128,1024]{1,0:T(8,128)(2,1)S(1)}, bf16[128,1024]{1,0:T(8,128)(2,1)S(1)}, u32[]{:S(2)}, u32[]{:S(2)}) collective-permute-start(bf16[128,1024]{1,0:T(8,128)(2,1)S(1)} %get-tuple-element.31), channel_id=1, source_target_pairs={{0,18},{1,19},{2,16},{3,17},{16,2},{17,3},{18,0},{19,1},{4,22},{5,... | collective-permute-start | bytes 786440 | tf_op jit(solution)/shard_map/ppermute | solution.py:27
  90.2 2.0 %collective-permute-start.21 = (bf16[128,1024]{1,0:T(8,128)(2,1)S(1)}, bf16[128,1024]{1,0:T(8,128)(2,1)S(1)}, u32[]{:S(2)}, u32[]{:S(2)}) collective-permute-start(bf16[128,1024]{1,0:T(8,128)(2,1)S(1)} %get-tuple-element.34), channel_id=1, source_target_pairs={{0,17},{1,16},{2,19},{3,18},{16,1},{17,0},{18,3},{19,2},{4,21},{5,... | collective-permute-start | bytes 786440 | tf_op jit(solution)/shard_map/ppermute | solution.py:27
  92.9 5.2 %collective-permute-done.18.refs_0_ = bf16[128,1024]{1,0:T(8,128)(2,1)S(1)} collective-permute-done((bf16[128,1024]{1,0:T(8,128)(2,1)S(1)}, bf16[128,1024]{1,0:T(8,128)(2,1)S(1)}, u32[]{:S(2)}, u32[]{:S(2)}) %collective-permute-start.18) | collective-permute-done | bytes 262176 | tf_op jit(solution)/shard_map/ppermute | solution.py:27
  98.1 3.8 %collective-permute-done.19.refs_1_ = bf16[128,1024]{1,0:T(8,128)(2,1)S(1)} collective-permute-done((bf16[128,1024]{1,0:T(8,128)(2,1)S(1)}, bf16[128,1024]{1,0:T(8,128)(2,1)S(1)}, u32[]{:S(2)}, u32[]{:S(2)}) %collective-permute-start.19) | collective-permute-done | bytes 262176 | tf_op jit(solution)/shard_map/ppermute | solution.py:27
  101.9 1.5 %collective-permute-start.24 = (bf16[128,1024]{1,0:T(8,128)(2,1)S(1)}, bf16[128,1024]{1,0:T(8,128)(2,1)S(1)}, u32[]{:S(2)}, u32[]{:S(2)}) collective-permute-start(bf16[128,1024]{1,0:T(8,128)(2,1)S(1)} %get-tuple-element.37), channel_id=1, source_target_pairs={{0,1},{1,0},{2,3},{3,2},{16,17},{17,16},{18,19},{19,18},{4,5},{5,4... | collective-permute-start | bytes 786440 | tf_op jit(solution)/shard_map/ppermute | solution.py:27
  103.5 5.0 %collective-permute-done.20.refs_2_ = bf16[128,1024]{1,0:T(8,128)(2,1)S(1)} collective-permute-done((bf16[128,1024]{1,0:T(8,128)(2,1)S(1)}, bf16[128,1024]{1,0:T(8,128)(2,1)S(1)}, u32[]{:S(2)}, u32[]{:S(2)}) %collective-permute-start.20) | collective-permute-done | bytes 262176 | tf_op jit(solution)/shard_map/ppermute | solution.py:27
  108.5 2.5 %collective-permute-done.21.refs_3_ = bf16[128,1024]{1,0:T(8,128)(2,1)S(1)} collective-permute-done((bf16[128,1024]{1,0:T(8,128)(2,1)S(1)}, bf16[128,1024]{1,0:T(8,128)(2,1)S(1)}, u32[]{:S(2)}, u32[]{:S(2)}) %collective-permute-start.21) | collective-permute-done | bytes 262176 | tf_op jit(solution)/shard_map/ppermute | solution.py:27
  111.0 1.9 %collective-permute-done.23.refs_5_ = bf16[128,1024]{1,0:T(8,128)(2,1)S(1)} collective-permute-done((bf16[128,1024]{1,0:T(8,128)(2,1)S(1)}, bf16[128,1024]{1,0:T(8,128)(2,1)S(1)}, u32[]{:S(2)}, u32[]{:S(2)}) %collective-permute-start.23) | collective-permute-done | bytes 262176 | tf_op jit(solution)/shard_map/ppermute | solution.py:27
  112.9 1.4 %place_results.1 = bf16[128,8192]{1,0:T(8,128)(2,1)} custom-call(s32[1]{0:T(128)} %bitcast.me_ref, bf16[128,1024]{1,0:T(8,128)(2,1)S(1)} %collective-permute-done.18.refs_0_, bf16[128,1024]{1,0:T(8,128)(2,1)S(1)} %collective-permute-done.19.refs_1_, bf16[128,1024]{1,0:T(8,128)(2,1)S(1)} %collective-permute-done.20.refs_2_, ...), custom_call_target="tpu_custom_call" | custom-call | tf_op jit(solution)/shard_map/place_results/pallas_call | solution.py:248
  (50 shorter events, 12.4 us)
Async XLA Ops:
  1.1 3.2 %collective-permute-start = (bf16[64,1024]{1,0:T(8,128)(2,1)S(1)}, bf16[64,1024]{1,0:T(8,128)(2,1)S(1)}, u32[]{:S(2)}, u32[]{:S(2)}) collective-permute-start(bf16[64,1024]{1,0:T(8,128)(2,1)S(1)} %get-tuple-element.44), channel_id=1, source_target_pairs={{0,1},{1,0},{2,3},{3,2},{4,5},{5,4},{6,7},{7,6},{8,9},{9,8},{10,11... | collective-permute-start | bytes 393224 | tf_op jit(solution)/shard_map/ppermute | solution.py:27
  1.7 9.9 %collective-permute-start.1 = (bf16[64,1024]{1,0:T(8,128)(2,1)S(1)}, bf16[64,1024]{1,0:T(8,128)(2,1)S(1)}, u32[]{:S(2)}, u32[]{:S(2)}) collective-permute-start(bf16[64,1024]{1,0:T(8,128)(2,1)S(1)} %get-tuple-element.46), channel_id=1, source_target_pairs={{0,2},{1,3},{2,0},{3,1},{4,6},{5,7},{6,4},{7,5},{8,10},{9,11},{10,... | collective-permute-start | bytes 393224 | tf_op jit(solution)/shard_map/ppermute | solution.py:27
  4.2 7.3 %collective-permute-start.2 = (bf16[64,1024]{1,0:T(8,128)(2,1)S(1)}, bf16[64,1024]{1,0:T(8,128)(2,1)S(1)}, u32[]{:S(2)}, u32[]{:S(2)}) collective-permute-start(bf16[64,1024]{1,0:T(8,128)(2,1)S(1)} %get-tuple-element.43), channel_id=1, source_target_pairs={{0,3},{1,2},{2,1},{3,0},{4,7},{5,6},{6,5},{7,4},{8,11},{9,10},{10,... | collective-permute-start | bytes 393224 | tf_op jit(solution)/shard_map/ppermute | solution.py:27
  4.3 1.9 %copy-start = (bf16[128,8192]{1,0:T(8,128)(2,1)S(1)}, bf16[128,8192]{1,0:T(8,128)(2,1)}, u32[]{:S(2)}) copy-start(bf16[128,8192]{1,0:T(8,128)(2,1)} %hidden_ref) | copy-start | bytes 6291460
  4.3 1.9 %copy-start.1 = (s32[128,1]{0,1:T(1,128)S(1)}, s32[128,1]{0,1:T(1,128)}, u32[]{:S(2)}) copy-start(s32[128,1]{0,1:T(1,128)} %param.4) | copy-start | bytes 1540
  4.3 10.7 %collective-permute-start.3 = (bf16[128,1024]{1,0:T(8,128)(2,1)S(1)}, bf16[128,1024]{1,0:T(8,128)(2,1)S(1)}, u32[]{:S(2)}, u32[]{:S(2)}) collective-permute-start(bf16[128,1024]{1,0:T(8,128)(2,1)S(1)} %join_blocks.4.refs_0_), channel_id=1, source_target_pairs={{0,4},{4,8},{8,12},{12,0},{1,5},{5,9},{9,13},{13,1},{2,6},{6,10},{... | collective-permute-start | bytes 786440 | tf_op jit(solution)/shard_map/ppermute | solution.py:31
  7.8 39.2 %all-to-all-start = ((bf16[8,136,1024]{2,1,0:T(8,128)(2,1)}), bf16[8,136,1024]{2,1,0:T(8,128)(2,1)S(1)}, u32[]{:S(2)}, u32[]{:S(2)}) async-start(bf16[8,136,1024]{2,1,0:T(8,128)(2,1)} %outgoing_rows.1), calls=%async_computation | async-start | bytes 4456448 | tf_op jit(solution)/shard_map/all_to_all | solution.py:39
  11.6 11.0 %collective-permute-start.4 = (bf16[128,1024]{1,0:T(8,128)(2,1)S(1)}, bf16[128,1024]{1,0:T(8,128)(2,1)S(1)}, u32[]{:S(2)}, u32[]{:S(2)}) collective-permute-start(bf16[128,1024]{1,0:T(8,128)(2,1)S(1)} %join_blocks.5.refs_1_), channel_id=1, source_target_pairs={{0,4},{4,8},{8,12},{12,0},{1,5},{5,9},{9,13},{13,1},{2,6},{6,10},{... | collective-permute-start | bytes 786440 | tf_op jit(solution)/shard_map/ppermute | solution.py:31
  15.0 13.2 %collective-permute-start.5 = (bf16[128,1024]{1,0:T(8,128)(2,1)S(1)}, bf16[128,1024]{1,0:T(8,128)(2,1)}, u32[]{:S(2)}, u32[]{:S(2)}) collective-permute-start(bf16[128,1024]{1,0:T(8,128)(2,1)S(1)} %join_blocks.6), channel_id=1, source_target_pairs={{0,4},{4,8},{8,12},{12,0},{1,5},{5,9},{9,13},{13,1},{2,6},{6,10},{... | collective-permute-start | bytes 786440 | tf_op jit(solution)/shard_map/ppermute | solution.py:31
  22.5 0.8 copy-start.2
  23.3 11.0 %collective-permute-start.6 = (bf16[128,1024]{1,0:T(8,128)(2,1)}, bf16[128,1024]{1,0:T(8,128)(2,1)}, u32[]{:S(2)}, u32[]{:S(2)}) collective-permute-start(bf16[128,1024]{1,0:T(8,128)(2,1)} %join_blocks.7), channel_id=1, source_target_pairs={{0,4},{4,8},{8,12},{12,0},{1,5},{5,9},{9,13},{13,1},{2,6},{6,10},{... | collective-permute-start | bytes 786440 | tf_op jit(solution)/shard_map/ppermute | solution.py:31
  25.2 9.3 %collective-permute-start.9 = (bf16[64,1024]{1,0:T(8,128)(2,1)}, bf16[64,1024]{1,0:T(8,128)(2,1)}, u32[]{:S(2)}, u32[]{:S(2)}) collective-permute-start(bf16[64,1024]{1,0:T(8,128)(2,1)} %get-tuple-element.26), channel_id=1, source_target_pairs={{0,1},{1,0},{2,3},{3,2},{4,5},{5,4},{6,7},{7,6},{8,9},{9,8},{10,11... | collective-permute-start | bytes 393224 | tf_op jit(solution)/shard_map/ppermute | solution.py:27
  25.2 15.8 %collective-permute-start.11 = (bf16[64,1024]{1,0:T(8,128)(2,1)}, bf16[64,1024]{1,0:T(8,128)(2,1)S(1)}, u32[]{:S(2)}, u32[]{:S(2)}) collective-permute-start(bf16[64,1024]{1,0:T(8,128)(2,1)} %get-tuple-element.29), channel_id=1, source_target_pairs={{0,3},{1,2},{2,1},{3,0},{4,7},{5,6},{6,5},{7,4},{8,11},{9,10},{10,... | collective-permute-start | bytes 393224 | tf_op jit(solution)/shard_map/ppermute | solution.py:27
  27.4 17.0 %collective-permute-start.10 = (bf16[64,1024]{1,0:T(8,128)(2,1)}, bf16[64,1024]{1,0:T(8,128)(2,1)}, u32[]{:S(2)}, u32[]{:S(2)}) collective-permute-start(bf16[64,1024]{1,0:T(8,128)(2,1)} %get-tuple-element.28), channel_id=1, source_target_pairs={{0,2},{1,3},{2,0},{3,1},{4,6},{5,7},{6,4},{7,5},{8,10},{9,11},{10,... | collective-permute-start | bytes 393224 | tf_op jit(solution)/shard_map/ppermute | solution.py:27
  28.3 17.1 %collective-permute-start.7 = (bf16[128,1024]{1,0:T(8,128)(2,1)}, bf16[128,1024]{1,0:T(8,128)(2,1)}, u32[]{:S(2)}, u32[]{:S(2)}) collective-permute-start(bf16[128,1024]{1,0:T(8,128)(2,1)} %collective-permute-done.5.refs_4_), channel_id=1, source_target_pairs={{0,4},{4,8},{8,12},{12,0},{1,5},{5,9},{9,13},{13,1},{2,6},{6,10},{... | collective-permute-start | bytes 786440 | tf_op jit(solution)/shard_map/ppermute | solution.py:31
  34.4 12.6 %collective-permute-start.8 = (bf16[128,1024]{1,0:T(8,128)(2,1)}, bf16[128,1024]{1,0:T(8,128)(2,1)}, u32[]{:S(2)}, u32[]{:S(2)}) collective-permute-start(bf16[128,1024]{1,0:T(8,128)(2,1)} %collective-permute-done.6.refs_5_), channel_id=1, source_target_pairs={{0,4},{4,8},{8,12},{12,0},{1,5},{5,9},{9,13},{13,1},{2,6},{6,10},{... | collective-permute-start | bytes 786440 | tf_op jit(solution)/shard_map/ppermute | solution.py:31
  45.4 9.8 %collective-permute-start.12 = (bf16[128,1024]{1,0:T(8,128)(2,1)S(1)}, bf16[128,1024]{1,0:T(8,128)(2,1)}, u32[]{:S(2)}, u32[]{:S(2)}) collective-permute-start(bf16[128,1024]{1,0:T(8,128)(2,1)S(1)} %pad_maximum_fusion.refs_0_), channel_id=1, source_target_pairs={{0,4},{4,8},{8,12},{12,0},{1,5},{5,9},{9,13},{13,1},{2,6},{6,10},{... | collective-permute-start | bytes 786440 | tf_op jit(solution)/shard_map/ppermute | solution.py:31
  47.0 1.0 copy-start.3
  52.3 11.0 %collective-permute-start.13 = (bf16[128,1024]{1,0:T(8,128)(2,1)S(1)}, bf16[128,1024]{1,0:T(8,128)(2,1)S(1)}, u32[]{:S(2)}, u32[]{:S(2)}) collective-permute-start(bf16[128,1024]{1,0:T(8,128)(2,1)S(1)} %pad_maximum_fusion.1.refs_1_), channel_id=1, source_target_pairs={{0,4},{4,8},{8,12},{12,0},{1,5},{5,9},{9,13},{13,1},{2,6},{6,10},{... | collective-permute-start | bytes 786440 | tf_op jit(solution)/shard_map/ppermute | solution.py:31
  55.2 13.8 %collective-permute-start.14 = (bf16[128,1024]{1,0:T(8,128)(2,1)}, bf16[128,1024]{1,0:T(8,128)(2,1)S(1)}, u32[]{:S(2)}, u32[]{:S(2)}) collective-permute-start(bf16[128,1024]{1,0:T(8,128)(2,1)} %collective-permute-done.12.refs_2_), channel_id=1, source_target_pairs={{0,4},{4,8},{8,12},{12,0},{1,5},{5,9},{9,13},{13,1},{2,6},{6,10},{... | collective-permute-start | bytes 786440 | tf_op jit(solution)/shard_map/ppermute | solution.py:31
  63.3 10.5 %collective-permute-start.15 = (bf16[128,1024]{1,0:T(8,128)(2,1)S(1)}, bf16[128,1024]{1,0:T(8,128)(2,1)S(1)}, u32[]{:S(2)}, u32[]{:S(2)}) collective-permute-start(bf16[128,1024]{1,0:T(8,128)(2,1)S(1)} %collective-permute-done.13.refs_3_), channel_id=1, source_target_pairs={{0,4},{4,8},{8,12},{12,0},{1,5},{5,9},{9,13},{13,1},{2,6},{6,10},{... | collective-permute-start | bytes 786440 | tf_op jit(solution)/shard_map/ppermute | solution.py:31
  63.3 10.9 %all-to-all-start.1 = ((f32[8,64,128]{2,1,0:T(8,128)}), f32[8,64,128]{2,1,0:T(8,128)S(1)}, u32[]{:S(2)}, u32[]{:S(2)}) async-start(f32[8,64,128]{2,1,0:T(8,128)} %get-tuple-element.24), calls=%async_computation.1 | async-start | bytes 524288 | tf_op jit(solution)/shard_map/all_to_all | solution.py:39
  69.0 11.0 %collective-permute-start.16 = (bf16[128,1024]{1,0:T(8,128)(2,1)S(1)}, bf16[128,1024]{1,0:T(8,128)(2,1)S(1)}, u32[]{:S(2)}, u32[]{:S(2)}) collective-permute-start(bf16[128,1024]{1,0:T(8,128)(2,1)S(1)} %collective-permute-done.14.refs_4_), channel_id=1, source_target_pairs={{0,4},{4,8},{8,12},{12,0},{1,5},{5,9},{9,13},{13,1},{2,6},{6,10},{... | collective-permute-start | bytes 786440 | tf_op jit(solution)/shard_map/ppermute | solution.py:31
  73.9 10.3 %collective-permute-start.17 = (bf16[128,1024]{1,0:T(8,128)(2,1)S(1)}, bf16[128,1024]{1,0:T(8,128)(2,1)S(1)}, u32[]{:S(2)}, u32[]{:S(2)}) collective-permute-start(bf16[128,1024]{1,0:T(8,128)(2,1)S(1)} %collective-permute-done.15.refs_5_), channel_id=1, source_target_pairs={{0,4},{4,8},{8,12},{12,0},{1,5},{5,9},{9,13},{13,1},{2,6},{6,10},{... | collective-permute-start | bytes 786440 | tf_op jit(solution)/shard_map/ppermute | solution.py:31
  74.9 8.5 %all-to-all-start.2 = ((bf16[8,64,128]{2,1,0:T(8,128)(2,1)}), bf16[8,64,128]{2,1,0:T(8,128)(2,1)S(1)}, u32[]{:S(2)}, u32[]{:S(2)}) async-start(bf16[8,64,128]{2,1,0:T(8,128)(2,1)} %summed_copies.1), calls=%async_computation.2 | async-start | bytes 262144 | tf_op jit(solution)/shard_map/all_to_all | solution.py:39
  87.8 10.3 %collective-permute-start.18 = (bf16[128,1024]{1,0:T(8,128)(2,1)S(1)}, bf16[128,1024]{1,0:T(8,128)(2,1)S(1)}, u32[]{:S(2)}, u32[]{:S(2)}) collective-permute-start(bf16[128,1024]{1,0:T(8,128)(2,1)S(1)} %get-tuple-element.31), channel_id=1, source_target_pairs={{0,18},{1,19},{2,16},{3,17},{16,2},{17,3},{18,0},{19,1},{4,22},{5,... | collective-permute-start | bytes 786440 | tf_op jit(solution)/shard_map/ppermute | solution.py:27
  89.5 12.4 %collective-permute-start.19 = (bf16[128,1024]{1,0:T(8,128)(2,1)S(1)}, bf16[128,1024]{1,0:T(8,128)(2,1)S(1)}, u32[]{:S(2)}, u32[]{:S(2)}) collective-permute-start(bf16[128,1024]{1,0:T(8,128)(2,1)S(1)} %get-tuple-element.32), channel_id=1, source_target_pairs={{0,19},{1,18},{2,17},{3,16},{16,3},{17,2},{18,1},{19,0},{4,23},{5,... | collective-permute-start | bytes 786440 | tf_op jit(solution)/shard_map/ppermute | solution.py:27
  89.5 19.0 %collective-permute-start.20 = (bf16[128,1024]{1,0:T(8,128)(2,1)S(1)}, bf16[128,1024]{1,0:T(8,128)(2,1)S(1)}, u32[]{:S(2)}, u32[]{:S(2)}) collective-permute-start(bf16[128,1024]{1,0:T(8,128)(2,1)S(1)} %get-tuple-element.33), channel_id=1, source_target_pairs={{0,16},{1,17},{2,18},{3,19},{16,0},{17,1},{18,2},{19,3},{4,20},{5,... | collective-permute-start | bytes 786440 | tf_op jit(solution)/shard_map/ppermute | solution.py:27
  90.2 20.8 %collective-permute-start.21 = (bf16[128,1024]{1,0:T(8,128)(2,1)S(1)}, bf16[128,1024]{1,0:T(8,128)(2,1)S(1)}, u32[]{:S(2)}, u32[]{:S(2)}) collective-permute-start(bf16[128,1024]{1,0:T(8,128)(2,1)S(1)} %get-tuple-element.34), channel_id=1, source_target_pairs={{0,17},{1,16},{2,19},{3,18},{16,1},{17,0},{18,3},{19,2},{4,21},{5,... | collective-permute-start | bytes 786440 | tf_op jit(solution)/shard_map/ppermute | solution.py:27
  92.2 18.7 %collective-permute-start.22 = (bf16[128,1024]{1,0:T(8,128)(2,1)S(1)}, bf16[128,1024]{1,0:T(8,128)(2,1)S(1)}, u32[]{:S(2)}, u32[]{:S(2)}) collective-permute-start(bf16[128,1024]{1,0:T(8,128)(2,1)S(1)} %get-tuple-element.35), channel_id=1, source_target_pairs={{0,2},{1,3},{2,0},{3,1},{16,18},{17,19},{18,16},{19,17},{4,6},{5,7... | collective-permute-start | bytes 786440 | tf_op jit(solution)/shard_map/ppermute | solution.py:27
  98.1 14.8 %collective-permute-start.23 = (bf16[128,1024]{1,0:T(8,128)(2,1)S(1)}, bf16[128,1024]{1,0:T(8,128)(2,1)S(1)}, u32[]{:S(2)}, u32[]{:S(2)}) collective-permute-start(bf16[128,1024]{1,0:T(8,128)(2,1)S(1)} %get-tuple-element.36), channel_id=1, source_target_pairs={{0,3},{1,2},{2,1},{3,0},{16,19},{17,18},{18,17},{19,16},{4,7},{5,6... | collective-permute-start | bytes 786440 | tf_op jit(solution)/shard_map/ppermute | solution.py:27
  101.9 10.9 %collective-permute-start.24 = (bf16[128,1024]{1,0:T(8,128)(2,1)S(1)}, bf16[128,1024]{1,0:T(8,128)(2,1)S(1)}, u32[]{:S(2)}, u32[]{:S(2)}) collective-permute-start(bf16[128,1024]{1,0:T(8,128)(2,1)S(1)} %get-tuple-element.37), channel_id=1, source_target_pairs={{0,1},{1,0},{2,3},{3,2},{16,17},{17,16},{18,19},{19,18},{4,5},{5,4... | collective-permute-start | bytes 786440 | tf_op jit(solution)/shard_map/ppermute | solution.py:27
  (1 other events, 0.7 us)

commit v19 on v18

--- a/solution.py
+++ b/solution.py
@@ -182,8 +182,8 @@
     )(terms)
 
 
-def up_kernel(map_count, rank, labels_ref, me_ref, ids_ref, shrunk_ref, *refs):
-    members, half, _ = shrunk_ref.shape
+def up_kernel(map_count, rank, offsets, labels_ref, me_ref, ids_ref, shrunk_ref, *refs):
+    half, members = shrunk_ref.shape[1], len(offsets)
     maps, outs = refs[:map_count], refs[map_count : map_count + members]
     spread_ref = refs[-1]
     tok = 2 * half
@@ -193,7 +193,7 @@
     held = jnp.concatenate([m[...] for m in maps], axis=0)
     for first in range(0, members, block):
         for n in range(block):
-            member = me_ref[0] ^ (first + n)
+            member = me_ref[0] ^ offsets[first + n]
             packed = shrunk_ref[member].astype(jnp.float32)
             turned = pltpu.roll(packed, LANES // 2, 1)
             shrunk = jnp.concatenate(
@@ -211,11 +211,11 @@
             outs[first + n][...] = product[n * tok : (n + 1) * tok, :]
 
 
-def up_product(labels, me, ids, shrunk, maps, rank):
-    members, tok = ids.shape
+def up_product(labels, me, ids, shrunk, maps, rank, offsets):
+    members, tok = len(offsets), ids.shape[1]
     map_rows, piece = sum(m.shape[0] for m in maps), maps[0].shape[1]
     return pl.pallas_call(
-        functools.partial(up_kernel, len(maps), rank),
+        functools.partial(up_kernel, len(maps), rank, offsets),
         out_shape=[jax.ShapeDtypeStruct((tok, piece), jnp.bfloat16)] * members,
         in_specs=[IN_SMEM, IN_SMEM, IN_VMEM, IN_VMEM] + [IN_VMEM] * len(maps),
         out_specs=[IN_VMEM] * members,
@@ -273,13 +273,15 @@
     def exchanged(blocks):
         return blocks[:1] + [to_partner(blocks[n], "inner", inner, n) for n in range(1, inner)]
 
-    def rings(near, far, first_cost=0):
+    def rings(near, far, first_cost=0, third_after=()):
         near, far = [near], [far]
         for step in range(1, outer):
             for blocks in near, far:
                 block = blocks[-1]
                 if step == 2 and first_cost:
                     block = joined([block], first_cost)
+                if step == 3:
+                    block = after(block, *third_after)
                 blocks.append(next_on_ring(block, outer))
         return near, far
 
@@ -298,16 +300,20 @@
 
     down_maps = [m for pair in zip(down_near, down_far) for m in pair]
     packed, id_rows = down_product(labels, rows, down_maps, rank)
+    terms = swap(packed)
     up_near, up_far = rings(
         after(jnp.concatenate(up[:middle], axis=0), down_near[-1]),
-        after(jnp.concatenate(up[middle:], axis=0), down_far[-1], packed),
+        jnp.concatenate([after(block, packed) for block in up[middle:]], axis=0),
+        third_after=[terms],
     )
     up_maps = [m for pair in zip(up_near, up_far) for m in pair]
-    shrunk = swap(summed_copies(swap(packed)))
-    results = list(up_product(labels, me.reshape(1), id_rows, shrunk, up_maps, rank))
-    offsets = sorted(range(1, members), key=lambda n: (-(n >= inner) - (n % inner >= 2), -(n >= inner), n))
-    returned = [to_partner(results[n], PLANE, members, n) for n in offsets]
-    return place(me.reshape(1), offsets + [0], returned + results[:1])
+    shrunk = swap(summed_copies(terms))
+    offsets = sorted(range(1, members), key=lambda n: (-(n >= inner) - (n % inner >= 2), -(n >= inner), n)) + [0]
+    results = []
+    for some in offsets[: members // 2], offsets[members // 2 :]:
+        results += up_product(labels, me.reshape(1), id_rows, shrunk, up_maps, rank, some)
+    returned = [to_partner(r, PLANE, members, n) for r, n in zip(results[:-1], offsets)]
+    return place(me.reshape(1), offsets, returned + results[-1:])
 
 
 def solution(mesh):

time: 115 us -> 119 us (1.035)
  blocking collectives: 0 us -> 7.75 us
  starting transfers between devices: 30.4 us -> 25.1 us
  local copies, waits for them, and re-layouts: 4.72 us -> 7.59 us
    ppermute x13, waiting for transfers between devices: 26.7 us -> 15.7 us  [to_partner(): return lax.ppermute(value, axes, [(i, i ^ offset) for i in range(size)])]
    ppermute x12, waiting for transfers between devices: 34.5 us -> 44.8 us  [next_on_ring(): lax.ppermute(block, 'outer', [(i, (i + 1) % outer) for i in range(outer)])]
    all_to_all x0 -> x1, blocking collectives: none -> 7.75 us  [swap(): return lax.all_to_all(value, PLANE, split_axis=0, concat_axis=0, tiled=True)]
    all_to_all x3 -> x2, starting transfers between devices: 10.5 us -> 7.28 us  [swap(): return lax.all_to_all(value, PLANE, split_axis=0, concat_axis=0, tiled=True)]
    ppermute x12, starting transfers between devices: 7.81 us -> 5.14 us  [next_on_ring(): lax.ppermute(block, 'outer', [(i, (i + 1) % outer) for i in range(outer)])]
    unnamed x10 -> x13, local copies, waits for them, and re-layouts: 1.63 us -> 3.53 us
    all_to_all x3 -> x2, waiting for transfers between devices: 3.4 us -> 4.52 us  [swap(): return lax.all_to_all(value, PLANE, split_axis=0, concat_axis=0, tiled=True)]
    pallas_call x1 -> x2, Pallas kernels: 3.65 us -> 3.94 us  [up_product(): pl.pallas_call(functools.partial(up_kernel, len(maps), rank, offsets), ou...]
  transfers between devices with their start and end apart: 28 -> 27, of which waited for: 18 -> 16; matrix products, arithmetic and copies ran while one was open for 3% -> 4% of each run, Pallas kernels for 7% -> 7%
where the time goes in v19:
time: 119 us
  waiting for transfers between devices  65.1 us (55%)
  starting transfers between devices  25.1 us (21%)
  Pallas kernels  12 us (10%)
  blocking collectives  7.75 us (7%)
  local copies, waits for them, and re-layouts  7.59 us (6%)
    ppermute x12, waiting for transfers between devices, next_on_ring(): lax.ppermute(block, 'outer', [(i, (i + 1) % outer) for i in range(outer)])  44.8 us
    ppermute x13, waiting for transfers between devices, to_partner(): return lax.ppermute(value, axes, [(i, i ^ offset) for i in range(size)])  15.7 us
    ppermute x13, starting transfers between devices, to_partner(): return lax.ppermute(value, axes, [(i, i ^ offset) for i in range(size)])  12.7 us
    all_to_all x1, blocking collectives, swap(): return lax.all_to_all(value, PLANE, split_axis=0, concat_axis=0, tiled=True)  7.75 us
    all_to_all x2, starting transfers between devices, swap(): return lax.all_to_all(value, PLANE, split_axis=0, concat_axis=0, tiled=True)  7.28 us
    ppermute x12, starting transfers between devices, next_on_ring(): lax.ppermute(block, 'outer', [(i, (i + 1) % outer) for i in range(outer)])  5.14 us
    all_to_all x2, waiting for transfers between devices, swap(): return lax.all_to_all(value, PLANE, split_axis=0, concat_axis=0, tiled=True)  4.52 us
    pallas_call x1, Pallas kernels, down_product(): pl.pallas_call(functools.partial(down_kernel, len(maps), rank), out_shape...  4.26 us
  transfers between devices with their start and end apart: 27, of which 16 were waited for; matrix products, arithmetic and copies ran while one was open for 4% of the time, Pallas kernels for 7%

profile of v19, /device:TPU:0, one launch (start us, length us, event | category | flops | bytes accessed | tf_op | source)
XLA Modules:
  0.0 118.7 jit_solution(2578323941634068655)
XLA Ops:
  1.7 2.6 %collective-permute-start.1 = (bf16[64,1024]{1,0:T(8,128)(2,1)S(1)}, bf16[64,1024]{1,0:T(8,128)(2,1)S(1)}, u32[]{:S(2)}, u32[]{:S(2)}) collective-permute-start(bf16[64,1024]{1,0:T(8,128)(2,1)S(1)} %get-tuple-element.52), channel_id=1, source_target_pairs={{0,2},{1,3},{2,0},{3,1},{4,6},{5,7},{6,4},{7,5},{8,10},{9,11},{10,... | collective-permute-start | bytes 393224 | tf_op jit(solution)/shard_map/ppermute | solution.py:27
  4.3 1.8 %collective-permute-start.3 = (bf16[128,1024]{1,0:T(8,128)(2,1)S(1)}, bf16[128,1024]{1,0:T(8,128)(2,1)S(1)}, u32[]{:S(2)}, u32[]{:S(2)}) collective-permute-start(bf16[128,1024]{1,0:T(8,128)(2,1)S(1)} %join_blocks.4.refs_0_), channel_id=1, source_target_pairs={{0,4},{4,8},{8,12},{12,0},{1,5},{5,9},{9,13},{13,1},{2,6},{6,10},{... | collective-permute-start | bytes 786440 | tf_op jit(solution)/shard_map/ppermute | solution.py:31
  6.2 1.6 %outgoing_rows.1 = bf16[8,136,1024]{2,1,0:T(8,128)(2,1)} custom-call(bf16[128,8192]{1,0:T(8,128)(2,1)S(1)} %copy-done, s32[1,128]{1,0:T(1,128)S(1)} %bitcast.26), custom_call_target="tpu_custom_call" | custom-call | tf_op jit(solution)/shard_map/outgoing_rows/pallas_call | solution.py:94
  7.8 3.7 %all-to-all-start = ((bf16[8,136,1024]{2,1,0:T(8,128)(2,1)}), bf16[8,136,1024]{2,1,0:T(8,128)(2,1)S(1)}, u32[]{:S(2)}, u32[]{:S(2)}) async-start(bf16[8,136,1024]{2,1,0:T(8,128)(2,1)} %outgoing_rows.1), calls=%async_computation | async-start | bytes 4456448 | tf_op jit(solution)/shard_map/all_to_all | solution.py:39
  11.6 1.6 %collective-permute-start.4 = (bf16[128,1024]{1,0:T(8,128)(2,1)S(1)}, bf16[128,1024]{1,0:T(8,128)(2,1)S(1)}, u32[]{:S(2)}, u32[]{:S(2)}) collective-permute-start(bf16[128,1024]{1,0:T(8,128)(2,1)S(1)} %join_blocks.5.refs_1_), channel_id=1, source_target_pairs={{0,4},{4,8},{8,12},{12,0},{1,5},{5,9},{9,13},{13,1},{2,6},{6,10},{... | collective-permute-start | bytes 786440 | tf_op jit(solution)/shard_map/ppermute | solution.py:31
  13.2 1.8 %collective-permute-done.3.refs_0_.refs_2_ = bf16[128,1024]{1,0:T(8,128)(2,1)S(1)} collective-permute-done((bf16[128,1024]{1,0:T(8,128)(2,1)S(1)}, bf16[128,1024]{1,0:T(8,128)(2,1)S(1)}, u32[]{:S(2)}, u32[]{:S(2)}) %collective-permute-start.3) | collective-permute-done | bytes 262176 | tf_op jit(solution)/shard_map/ppermute | solution.py:31
  15.1 7.4 %collective-permute-done.4.refs_0_.refs_3_ = bf16[128,1024]{1,0:T(8,128)(2,1)S(1)} collective-permute-done((bf16[128,1024]{1,0:T(8,128)(2,1)S(1)}, bf16[128,1024]{1,0:T(8,128)(2,1)S(1)}, u32[]{:S(2)}, u32[]{:S(2)}) %collective-permute-start.4) | collective-permute-done | bytes 262176 | tf_op jit(solution)/shard_map/ppermute | solution.py:31
  23.3 1.9 %dynamic-slice_bitcast_fusion = (bf16[64,1024]{1,0:T(8,128)(2,1)}, bf16[64,1024]{1,0:T(8,128)(2,1)}, bf16[64,1024]{1,0:T(8,128)(2,1)}, bf16[64,1024]{1,0:T(8,128)(2,1)}) fusion(bf16[1,64,8192]{2,1,0:T(8,128)(2,1)} %param.7, s32[]{:T(128)S(6)} %select_n.32, s32[]{:T(128)S(6)} %select_n.30, s32[]{:T(128)S(6)} %select_n.29, s32[]{:T(128)S(6)} %select_n.31), kind=kLoop, calls=%fused_computation.1 | loop fusion | bytes 1048592 | tf_op jit(solution)/shard_map/dynamic_slice | solution.py:270
  25.3 3.0 %collective-permute-done.5.refs_4_ = bf16[128,1024]{1,0:T(8,128)(2,1)} collective-permute-done((bf16[128,1024]{1,0:T(8,128)(2,1)S(1)}, bf16[128,1024]{1,0:T(8,128)(2,1)}, u32[]{:S(2)}, u32[]{:S(2)}) %collective-permute-start.5) | collective-permute-done | bytes 262176 | tf_op jit(solution)/shard_map/ppermute | solution.py:31
  28.3 6.3 %collective-permute-done.6.refs_5_ = bf16[128,1024]{1,0:T(8,128)(2,1)} collective-permute-done((bf16[128,1024]{1,0:T(8,128)(2,1)}, bf16[128,1024]{1,0:T(8,128)(2,1)}, u32[]{:S(2)}, u32[]{:S(2)}) %collective-permute-start.6) | collective-permute-done | bytes 262176 | tf_op jit(solution)/shard_map/ppermute | solution.py:31
  34.8 2.1 %collective-permute-start.10 = (bf16[64,1024]{1,0:T(8,128)(2,1)}, bf16[64,1024]{1,0:T(8,128)(2,1)}, u32[]{:S(2)}, u32[]{:S(2)}) collective-permute-start(bf16[64,1024]{1,0:T(8,128)(2,1)} %get-tuple-element.31), channel_id=1, source_target_pairs={{0,2},{1,3},{2,0},{3,1},{4,6},{5,7},{6,4},{7,5},{8,10},{9,11},{10,... | collective-permute-start | bytes 393224 | tf_op jit(solution)/shard_map/ppermute | solution.py:27
  37.8 2.3 %collective-permute-done.7.refs_6_ = bf16[128,1024]{1,0:T(8,128)(2,1)S(1)} collective-permute-done((bf16[128,1024]{1,0:T(8,128)(2,1)}, bf16[128,1024]{1,0:T(8,128)(2,1)S(1)}, u32[]{:S(2)}, u32[]{:S(2)}) %collective-permute-start.7) | collective-permute-done | bytes 262176 | tf_op jit(solution)/shard_map/ppermute | solution.py:31
  40.8 5.1 %collective-permute-done.8.refs_7_ = bf16[128,1024]{1,0:T(8,128)(2,1)} collective-permute-done((bf16[128,1024]{1,0:T(8,128)(2,1)}, bf16[128,1024]{1,0:T(8,128)(2,1)}, u32[]{:S(2)}, u32[]{:S(2)}) %collective-permute-start.8) | collective-permute-done | bytes 262176 | tf_op jit(solution)/shard_map/ppermute | solution.py:31
  47.8 4.3 %down_product.1 = (f32[8,64,128]{2,1,0:T(8,128)}, f32[8,128]{1,0:T(8,128)S(1)}) custom-call(s32[16]{0:T(128)S(1)} %add.61.labels_ref, bf16[8,136,1024]{2,1,0:T(8,128)(2,1)S(1)} %all-to-all-done.rows_ref, bf16[128,1024]{1,0:T(8,128)(2,1)S(1)} %join_blocks.4.refs_0_, bf16[128,1024]{1,0:T(8,128)(2,1)S(1)} %join_blocks.5.refs_1_, ...), custom_call_target="tpu_custom_call" | custom-call | flops 2147483648 | bytes 4194304 | tf_op jit(solution)/shard_map/down_product/pallas_call | solution.py:146
  54.5 10.5 %collective-permute-done.13.refs_3_ = bf16[128,1024]{1,0:T(8,128)(2,1)S(1)} collective-permute-done((bf16[128,1024]{1,0:T(8,128)(2,1)S(1)}, bf16[128,1024]{1,0:T(8,128)(2,1)S(1)}, u32[]{:S(2)}, u32[]{:S(2)}) %collective-permute-start.13) | collective-permute-done | bytes 262176 | tf_op jit(solution)/shard_map/ppermute | solution.py:31
  65.0 3.5 %all-to-all-start.1 = ((f32[8,64,128]{2,1,0:T(8,128)}), f32[8,64,128]{2,1,0:T(8,128)S(1)}, u32[]{:S(2)}, u32[]{:S(2)}) async-start(f32[8,64,128]{2,1,0:T(8,128)} %get-tuple-element.27), calls=%async_computation.1 | async-start | bytes 524288 | tf_op jit(solution)/shard_map/all_to_all | solution.py:39
  68.6 1.5 %collective-permute-done.14.refs_4_ = bf16[128,1024]{1,0:T(8,128)(2,1)S(1)} collective-permute-done((bf16[128,1024]{1,0:T(8,128)(2,1)S(1)}, bf16[128,1024]{1,0:T(8,128)(2,1)S(1)}, u32[]{:S(2)}, u32[]{:S(2)}) %collective-permute-start.14) | collective-permute-done | bytes 262176 | tf_op jit(solution)/shard_map/ppermute | solution.py:31
  70.1 4.5 %all-to-all-done.1.terms_ref = f32[8,64,128]{2,1,0:T(8,128)S(1)} async-done(((f32[8,64,128]{2,1,0:T(8,128)}), f32[8,64,128]{2,1,0:T(8,128)S(1)}, u32[]{:S(2)}, u32[]{:S(2)}) %all-to-all-start.1) | async-done | bytes 262176 | tf_op jit(solution)/shard_map/all_to_all | solution.py:39
  75.6 7.8 %all_to_all.15.shrunk_ref = bf16[8,64,128]{2,1,0:T(8,128)(2,1)S(1)} all-to-all(bf16[8,64,128]{2,1,0:T(8,128)(2,1)S(1)} %summed_copies.1), channel_id=1, replica_groups=mesh['groups'=2,'outer'=4,'inner'=4] {'groups','inner'}, dimensions={0} | all-to-all | bytes 262144 | tf_op jit(solution)/shard_map/all_to_all | solution.py:39
  83.4 2.2 %collective-permute-done.16.refs_6_ = bf16[128,1024]{1,0:T(8,128)(2,1)S(1)} collective-permute-done((bf16[128,1024]{1,0:T(8,128)(2,1)S(1)}, bf16[128,1024]{1,0:T(8,128)(2,1)S(1)}, u32[]{:S(2)}, u32[]{:S(2)}) %collective-permute-start.16) | collective-permute-done | bytes 262176 | tf_op jit(solution)/shard_map/ppermute | solution.py:31
  85.6 4.7 %collective-permute-done.17.refs_7_ = bf16[128,1024]{1,0:T(8,128)(2,1)S(1)} collective-permute-done((bf16[128,1024]{1,0:T(8,128)(2,1)S(1)}, bf16[128,1024]{1,0:T(8,128)(2,1)S(1)}, u32[]{:S(2)}, u32[]{:S(2)}) %collective-permute-start.17) | collective-permute-done | bytes 262176 | tf_op jit(solution)/shard_map/ppermute | solution.py:31
  90.3 2.0 %up_product.2 = (bf16[128,1024]{1,0:T(8,128)(2,1)S(1)}, bf16[128,1024]{1,0:T(8,128)(2,1)S(1)}, bf16[128,1024]{1,0:T(8,128)(2,1)S(1)}, bf16[128,1024]{1,0:T(8,128)(2,1)S(1)}) custom-call(s32[16]{0:T(128)S(1)} %add.61.labels_ref, s32[1]{0:T(128)} %bitcast.me_ref, f32[8,128]{1,0:T(8,128)S(1)} %get-tuple-element.26.ids_ref, ...), custom_call_target="tpu_custom_call" | custom-call | flops 1073741824 | bytes 3145728 | tf_op jit(solution)/shard_map/up_product/pallas_call | solution.py:217
  92.2 1.6 %collective-permute-start.18 = (bf16[128,1024]{1,0:T(8,128)(2,1)S(1)}, bf16[128,1024]{1,0:T(8,128)(2,1)S(1)}, u32[]{:S(2)}, u32[]{:S(2)}) collective-permute-start(bf16[128,1024]{1,0:T(8,128)(2,1)S(1)} %get-tuple-element.37), channel_id=1, source_target_pairs={{0,18},{1,19},{2,16},{3,17},{16,2},{17,3},{18,0},{19,1},{4,22},{5,... | collective-permute-start | bytes 786440 | tf_op jit(solution)/shard_map/ppermute | solution.py:27
  95.1 1.5 %collective-permute-start.21 = (bf16[128,1024]{1,0:T(8,128)(2,1)S(1)}, bf16[128,1024]{1,0:T(8,128)(2,1)S(1)}, u32[]{:S(2)}, u32[]{:S(2)}) collective-permute-start(bf16[128,1024]{1,0:T(8,128)(2,1)S(1)} %get-tuple-element.40), channel_id=1, source_target_pairs={{0,17},{1,16},{2,19},{3,18},{16,1},{17,0},{18,3},{19,2},{4,21},{5,... | collective-permute-start | bytes 786440 | tf_op jit(solution)/shard_map/ppermute | solution.py:27
  96.7 2.0 %up_product.3 = (bf16[128,1024]{1,0:T(8,128)(2,1)S(1)}, bf16[128,1024]{1,0:T(8,128)(2,1)S(1)}, bf16[128,1024]{1,0:T(8,128)(2,1)S(1)}, bf16[128,1024]{1,0:T(8,128)(2,1)S(1)}) custom-call(s32[16]{0:T(128)S(1)} %add.61.labels_ref, s32[1]{0:T(128)} %bitcast.me_ref, f32[8,128]{1,0:T(8,128)S(1)} %get-tuple-element.26.ids_ref, ...), custom_call_target="tpu_custom_call" | custom-call | flops 1073741824 | bytes 3145728 | tf_op jit(solution)/shard_map/up_product/pallas_call | solution.py:217
  100.0 2.6 %collective-permute-done.18.refs_0_ = bf16[128,1024]{1,0:T(8,128)(2,1)S(1)} collective-permute-done((bf16[128,1024]{1,0:T(8,128)(2,1)S(1)}, bf16[128,1024]{1,0:T(8,128)(2,1)S(1)}, u32[]{:S(2)}, u32[]{:S(2)}) %collective-permute-start.18) | collective-permute-done | bytes 262176 | tf_op jit(solution)/shard_map/ppermute | solution.py:27
  102.5 3.7 %collective-permute-done.19.refs_1_ = bf16[128,1024]{1,0:T(8,128)(2,1)S(1)} collective-permute-done((bf16[128,1024]{1,0:T(8,128)(2,1)S(1)}, bf16[128,1024]{1,0:T(8,128)(2,1)S(1)}, u32[]{:S(2)}, u32[]{:S(2)}) %collective-permute-start.19) | collective-permute-done | bytes 262176 | tf_op jit(solution)/shard_map/ppermute | solution.py:27
  106.2 1.7 %collective-permute-start.24 = (bf16[128,1024]{1,0:T(8,128)(2,1)S(1)}, bf16[128,1024]{1,0:T(8,128)(2,1)S(1)}, u32[]{:S(2)}, u32[]{:S(2)}) collective-permute-start(bf16[128,1024]{1,0:T(8,128)(2,1)S(1)} %get-tuple-element.43), channel_id=1, source_target_pairs={{0,1},{1,0},{2,3},{3,2},{16,17},{17,16},{18,19},{19,18},{4,5},{5,4... | collective-permute-start | bytes 786440 | tf_op jit(solution)/shard_map/ppermute | solution.py:27
  107.9 5.6 %collective-permute-done.20.refs_2_ = bf16[128,1024]{1,0:T(8,128)(2,1)S(1)} collective-permute-done((bf16[128,1024]{1,0:T(8,128)(2,1)S(1)}, bf16[128,1024]{1,0:T(8,128)(2,1)S(1)}, u32[]{:S(2)}, u32[]{:S(2)}) %collective-permute-start.20) | collective-permute-done | bytes 262176 | tf_op jit(solution)/shard_map/ppermute | solution.py:27
  113.5 2.2 %collective-permute-done.21.refs_3_ = bf16[128,1024]{1,0:T(8,128)(2,1)S(1)} collective-permute-done((bf16[128,1024]{1,0:T(8,128)(2,1)S(1)}, bf16[128,1024]{1,0:T(8,128)(2,1)S(1)}, u32[]{:S(2)}, u32[]{:S(2)}) %collective-permute-start.21) | collective-permute-done | bytes 262176 | tf_op jit(solution)/shard_map/ppermute | solution.py:27
  115.6 1.7 %collective-permute-done.23.refs_5_ = bf16[128,1024]{1,0:T(8,128)(2,1)S(1)} collective-permute-done((bf16[128,1024]{1,0:T(8,128)(2,1)S(1)}, bf16[128,1024]{1,0:T(8,128)(2,1)S(1)}, u32[]{:S(2)}, u32[]{:S(2)}) %collective-permute-start.23) | collective-permute-done | bytes 262176 | tf_op jit(solution)/shard_map/ppermute | solution.py:27
  117.4 1.4 %place_results.1 = bf16[128,8192]{1,0:T(8,128)(2,1)} custom-call(s32[1]{0:T(128)} %bitcast.me_ref, bf16[128,1024]{1,0:T(8,128)(2,1)S(1)} %collective-permute-done.18.refs_0_, bf16[128,1024]{1,0:T(8,128)(2,1)S(1)} %collective-permute-done.19.refs_1_, bf16[128,1024]{1,0:T(8,128)(2,1)S(1)} %collective-permute-done.20.refs_2_, ...), custom_call_target="tpu_custom_call" | custom-call | tf_op jit(solution)/shard_map/place_results/pallas_call | solution.py:248
  (53 shorter events, 12.5 us)
Async XLA Ops:
  1.1 3.2 %collective-permute-start = (bf16[64,1024]{1,0:T(8,128)(2,1)S(1)}, bf16[64,1024]{1,0:T(8,128)(2,1)S(1)}, u32[]{:S(2)}, u32[]{:S(2)}) collective-permute-start(bf16[64,1024]{1,0:T(8,128)(2,1)S(1)} %get-tuple-element.50), channel_id=1, source_target_pairs={{0,1},{1,0},{2,3},{3,2},{4,5},{5,4},{6,7},{7,6},{8,9},{9,8},{10,11... | collective-permute-start | bytes 393224 | tf_op jit(solution)/shard_map/ppermute | solution.py:27
  1.7 9.9 %collective-permute-start.1 = (bf16[64,1024]{1,0:T(8,128)(2,1)S(1)}, bf16[64,1024]{1,0:T(8,128)(2,1)S(1)}, u32[]{:S(2)}, u32[]{:S(2)}) collective-permute-start(bf16[64,1024]{1,0:T(8,128)(2,1)S(1)} %get-tuple-element.52), channel_id=1, source_target_pairs={{0,2},{1,3},{2,0},{3,1},{4,6},{5,7},{6,4},{7,5},{8,10},{9,11},{10,... | collective-permute-start | bytes 393224 | tf_op jit(solution)/shard_map/ppermute | solution.py:27
  4.2 7.3 %collective-permute-start.2 = (bf16[64,1024]{1,0:T(8,128)(2,1)S(1)}, bf16[64,1024]{1,0:T(8,128)(2,1)S(1)}, u32[]{:S(2)}, u32[]{:S(2)}) collective-permute-start(bf16[64,1024]{1,0:T(8,128)(2,1)S(1)} %get-tuple-element.49), channel_id=1, source_target_pairs={{0,3},{1,2},{2,1},{3,0},{4,7},{5,6},{6,5},{7,4},{8,11},{9,10},{10,... | collective-permute-start | bytes 393224 | tf_op jit(solution)/shard_map/ppermute | solution.py:27
  4.3 1.9 %copy-start = (bf16[128,8192]{1,0:T(8,128)(2,1)S(1)}, bf16[128,8192]{1,0:T(8,128)(2,1)}, u32[]{:S(2)}) copy-start(bf16[128,8192]{1,0:T(8,128)(2,1)} %hidden_ref) | copy-start | bytes 6291460
  4.3 1.9 %copy-start.1 = (s32[128,1]{0,1:T(1,128)S(1)}, s32[128,1]{0,1:T(1,128)}, u32[]{:S(2)}) copy-start(s32[128,1]{0,1:T(1,128)} %param.4) | copy-start | bytes 1540
  4.3 10.7 %collective-permute-start.3 = (bf16[128,1024]{1,0:T(8,128)(2,1)S(1)}, bf16[128,1024]{1,0:T(8,128)(2,1)S(1)}, u32[]{:S(2)}, u32[]{:S(2)}) collective-permute-start(bf16[128,1024]{1,0:T(8,128)(2,1)S(1)} %join_blocks.4.refs_0_), channel_id=1, source_target_pairs={{0,4},{4,8},{8,12},{12,0},{1,5},{5,9},{9,13},{13,1},{2,6},{6,10},{... | collective-permute-start | bytes 786440 | tf_op jit(solution)/shard_map/ppermute | solution.py:31
  7.8 38.1 %all-to-all-start = ((bf16[8,136,1024]{2,1,0:T(8,128)(2,1)}), bf16[8,136,1024]{2,1,0:T(8,128)(2,1)S(1)}, u32[]{:S(2)}, u32[]{:S(2)}) async-start(bf16[8,136,1024]{2,1,0:T(8,128)(2,1)} %outgoing_rows.1), calls=%async_computation | async-start | bytes 4456448 | tf_op jit(solution)/shard_map/all_to_all | solution.py:39
  11.6 11.0 %collective-permute-start.4 = (bf16[128,1024]{1,0:T(8,128)(2,1)S(1)}, bf16[128,1024]{1,0:T(8,128)(2,1)S(1)}, u32[]{:S(2)}, u32[]{:S(2)}) collective-permute-start(bf16[128,1024]{1,0:T(8,128)(2,1)S(1)} %join_blocks.5.refs_1_), channel_id=1, source_target_pairs={{0,4},{4,8},{8,12},{12,0},{1,5},{5,9},{9,13},{13,1},{2,6},{6,10},{... | collective-permute-start | bytes 786440 | tf_op jit(solution)/shard_map/ppermute | solution.py:31
  15.0 13.2 %collective-permute-start.5 = (bf16[128,1024]{1,0:T(8,128)(2,1)S(1)}, bf16[128,1024]{1,0:T(8,128)(2,1)}, u32[]{:S(2)}, u32[]{:S(2)}) collective-permute-start(bf16[128,1024]{1,0:T(8,128)(2,1)S(1)} %join_blocks.6), channel_id=1, source_target_pairs={{0,4},{4,8},{8,12},{12,0},{1,5},{5,9},{9,13},{13,1},{2,6},{6,10},{... | collective-permute-start | bytes 786440 | tf_op jit(solution)/shard_map/ppermute | solution.py:31
  22.5 0.8 copy-start.2
  23.3 11.3 %collective-permute-start.6 = (bf16[128,1024]{1,0:T(8,128)(2,1)}, bf16[128,1024]{1,0:T(8,128)(2,1)}, u32[]{:S(2)}, u32[]{:S(2)}) collective-permute-start(bf16[128,1024]{1,0:T(8,128)(2,1)} %join_blocks.7), channel_id=1, source_target_pairs={{0,4},{4,8},{8,12},{12,0},{1,5},{5,9},{9,13},{13,1},{2,6},{6,10},{... | collective-permute-start | bytes 786440 | tf_op jit(solution)/shard_map/ppermute | solution.py:31
  25.3 11.6 %collective-permute-start.9 = (bf16[64,1024]{1,0:T(8,128)(2,1)}, bf16[64,1024]{1,0:T(8,128)(2,1)}, u32[]{:S(2)}, u32[]{:S(2)}) collective-permute-start(bf16[64,1024]{1,0:T(8,128)(2,1)} %get-tuple-element.29), channel_id=1, source_target_pairs={{0,1},{1,0},{2,3},{3,2},{4,5},{5,4},{6,7},{7,6},{8,9},{9,8},{10,11... | collective-permute-start | bytes 393224 | tf_op jit(solution)/shard_map/ppermute | solution.py:27
  28.3 11.9 %collective-permute-start.7 = (bf16[128,1024]{1,0:T(8,128)(2,1)}, bf16[128,1024]{1,0:T(8,128)(2,1)S(1)}, u32[]{:S(2)}, u32[]{:S(2)}) collective-permute-start(bf16[128,1024]{1,0:T(8,128)(2,1)} %collective-permute-done.5.refs_4_), channel_id=1, source_target_pairs={{0,4},{4,8},{8,12},{12,0},{1,5},{5,9},{9,13},{13,1},{2,6},{6,10},{... | collective-permute-start | bytes 786440 | tf_op jit(solution)/shard_map/ppermute | solution.py:31
  34.6 11.3 %collective-permute-start.8 = (bf16[128,1024]{1,0:T(8,128)(2,1)}, bf16[128,1024]{1,0:T(8,128)(2,1)}, u32[]{:S(2)}, u32[]{:S(2)}) collective-permute-start(bf16[128,1024]{1,0:T(8,128)(2,1)} %collective-permute-done.6.refs_5_), channel_id=1, source_target_pairs={{0,4},{4,8},{8,12},{12,0},{1,5},{5,9},{9,13},{13,1},{2,6},{6,10},{... | collective-permute-start | bytes 786440 | tf_op jit(solution)/shard_map/ppermute | solution.py:31
  34.8 17.3 %collective-permute-start.10 = (bf16[64,1024]{1,0:T(8,128)(2,1)}, bf16[64,1024]{1,0:T(8,128)(2,1)}, u32[]{:S(2)}, u32[]{:S(2)}) collective-permute-start(bf16[64,1024]{1,0:T(8,128)(2,1)} %get-tuple-element.31), channel_id=1, source_target_pairs={{0,2},{1,3},{2,0},{3,1},{4,6},{5,7},{6,4},{7,5},{8,10},{9,11},{10,... | collective-permute-start | bytes 393224 | tf_op jit(solution)/shard_map/ppermute | solution.py:27
  36.8 16.1 %collective-permute-start.11 = (bf16[64,1024]{1,0:T(8,128)(2,1)}, bf16[64,1024]{1,0:T(8,128)(2,1)}, u32[]{:S(2)}, u32[]{:S(2)}) collective-permute-start(bf16[64,1024]{1,0:T(8,128)(2,1)} %get-tuple-element.33), channel_id=1, source_target_pairs={{0,3},{1,2},{2,1},{3,0},{4,7},{5,6},{6,5},{7,4},{8,11},{9,10},{10,... | collective-permute-start | bytes 393224 | tf_op jit(solution)/shard_map/ppermute | solution.py:27
  40.8 13.2 %collective-permute-start.12 = (bf16[128,1024]{1,0:T(8,128)(2,1)S(1)}, bf16[128,1024]{1,0:T(8,128)(2,1)S(1)}, u32[]{:S(2)}, u32[]{:S(2)}) collective-permute-start(bf16[128,1024]{1,0:T(8,128)(2,1)S(1)} %pad_maximum_fusion.refs_0_), channel_id=1, source_target_pairs={{0,4},{4,8},{8,12},{12,0},{1,5},{5,9},{9,13},{13,1},{2,6},{6,10},{... | collective-permute-start | bytes 786440 | tf_op jit(solution)/shard_map/ppermute | solution.py:31
  45.9 1.0 copy-start.3
  46.8 0.9 copy-start.5
  53.9 11.1 %collective-permute-start.13 = (bf16[128,1024]{1,0:T(8,128)(2,1)S(1)}, bf16[128,1024]{1,0:T(8,128)(2,1)S(1)}, u32[]{:S(2)}, u32[]{:S(2)}) collective-permute-start(bf16[128,1024]{1,0:T(8,128)(2,1)S(1)} %constant_dynamic-update-slice_fusion.refs_1_), channel_id=1, source_target_pairs={{0,4},{4,8},{8,12},{12,0},{1,5},{5,9},{9,13},{13,1},{2,6},{6,10},{... | collective-permute-start | bytes 786440 | tf_op jit(solution)/shard_map/ppermute | solution.py:31
  54.0 16.1 %collective-permute-start.14 = (bf16[128,1024]{1,0:T(8,128)(2,1)S(1)}, bf16[128,1024]{1,0:T(8,128)(2,1)S(1)}, u32[]{:S(2)}, u32[]{:S(2)}) collective-permute-start(bf16[128,1024]{1,0:T(8,128)(2,1)S(1)} %collective-permute-done.12.refs_2_), channel_id=1, source_target_pairs={{0,4},{4,8},{8,12},{12,0},{1,5},{5,9},{9,13},{13,1},{2,6},{6,10},{... | collective-permute-start | bytes 786440 | tf_op jit(solution)/shard_map/ppermute | solution.py:31
  65.0 9.6 %collective-permute-start.15 = (bf16[128,1024]{1,0:T(8,128)(2,1)S(1)}, bf16[128,1024]{1,0:T(8,128)(2,1)S(1)}, u32[]{:S(2)}, u32[]{:S(2)}) collective-permute-start(bf16[128,1024]{1,0:T(8,128)(2,1)S(1)} %collective-permute-done.13.refs_3_), channel_id=1, source_target_pairs={{0,4},{4,8},{8,12},{12,0},{1,5},{5,9},{9,13},{13,1},{2,6},{6,10},{... | collective-permute-start | bytes 786440 | tf_op jit(solution)/shard_map/ppermute | solution.py:31
  65.0 9.6 %all-to-all-start.1 = ((f32[8,64,128]{2,1,0:T(8,128)}), f32[8,64,128]{2,1,0:T(8,128)S(1)}, u32[]{:S(2)}, u32[]{:S(2)}) async-start(f32[8,64,128]{2,1,0:T(8,128)} %get-tuple-element.27), calls=%async_computation.1 | async-start | bytes 524288 | tf_op jit(solution)/shard_map/all_to_all | solution.py:39
  74.6 11.0 %collective-permute-start.16 = (bf16[128,1024]{1,0:T(8,128)(2,1)S(1)}, bf16[128,1024]{1,0:T(8,128)(2,1)S(1)}, u32[]{:S(2)}, u32[]{:S(2)}) collective-permute-start(bf16[128,1024]{1,0:T(8,128)(2,1)S(1)} %collective-permute-done.14.refs_4_), channel_id=1, source_target_pairs={{0,4},{4,8},{8,12},{12,0},{1,5},{5,9},{9,13},{13,1},{2,6},{6,10},{... | collective-permute-start | bytes 786440 | tf_op jit(solution)/shard_map/ppermute | solution.py:31
  74.6 15.6 %collective-permute-start.17 = (bf16[128,1024]{1,0:T(8,128)(2,1)S(1)}, bf16[128,1024]{1,0:T(8,128)(2,1)S(1)}, u32[]{:S(2)}, u32[]{:S(2)}) collective-permute-start(bf16[128,1024]{1,0:T(8,128)(2,1)S(1)} %collective-permute-done.15.refs_5_), channel_id=1, source_target_pairs={{0,4},{4,8},{8,12},{12,0},{1,5},{5,9},{9,13},{13,1},{2,6},{6,10},{... | collective-permute-start | bytes 786440 | tf_op jit(solution)/shard_map/ppermute | solution.py:31
  92.2 10.3 %collective-permute-start.18 = (bf16[128,1024]{1,0:T(8,128)(2,1)S(1)}, bf16[128,1024]{1,0:T(8,128)(2,1)S(1)}, u32[]{:S(2)}, u32[]{:S(2)}) collective-permute-start(bf16[128,1024]{1,0:T(8,128)(2,1)S(1)} %get-tuple-element.37), channel_id=1, source_target_pairs={{0,18},{1,19},{2,16},{3,17},{16,2},{17,3},{18,0},{19,1},{4,22},{5,... | collective-permute-start | bytes 786440 | tf_op jit(solution)/shard_map/ppermute | solution.py:27
  93.8 12.4 %collective-permute-start.19 = (bf16[128,1024]{1,0:T(8,128)(2,1)S(1)}, bf16[128,1024]{1,0:T(8,128)(2,1)S(1)}, u32[]{:S(2)}, u32[]{:S(2)}) collective-permute-start(bf16[128,1024]{1,0:T(8,128)(2,1)S(1)} %get-tuple-element.38), channel_id=1, source_target_pairs={{0,19},{1,18},{2,17},{3,16},{16,3},{17,2},{18,1},{19,0},{4,23},{5,... | collective-permute-start | bytes 786440 | tf_op jit(solution)/shard_map/ppermute | solution.py:27
  93.8 19.7 %collective-permute-start.20 = (bf16[128,1024]{1,0:T(8,128)(2,1)S(1)}, bf16[128,1024]{1,0:T(8,128)(2,1)S(1)}, u32[]{:S(2)}, u32[]{:S(2)}) collective-permute-start(bf16[128,1024]{1,0:T(8,128)(2,1)S(1)} %get-tuple-element.39), channel_id=1, source_target_pairs={{0,16},{1,17},{2,18},{3,19},{16,0},{17,1},{18,2},{19,3},{4,20},{5,... | collective-permute-start | bytes 786440 | tf_op jit(solution)/shard_map/ppermute | solution.py:27
  95.1 20.5 %collective-permute-start.21 = (bf16[128,1024]{1,0:T(8,128)(2,1)S(1)}, bf16[128,1024]{1,0:T(8,128)(2,1)S(1)}, u32[]{:S(2)}, u32[]{:S(2)}) collective-permute-start(bf16[128,1024]{1,0:T(8,128)(2,1)S(1)} %get-tuple-element.40), channel_id=1, source_target_pairs={{0,17},{1,16},{2,19},{3,18},{16,1},{17,0},{18,3},{19,2},{4,21},{5,... | collective-permute-start | bytes 786440 | tf_op jit(solution)/shard_map/ppermute | solution.py:27
  98.7 17.0 %collective-permute-start.22 = (bf16[128,1024]{1,0:T(8,128)(2,1)S(1)}, bf16[128,1024]{1,0:T(8,128)(2,1)S(1)}, u32[]{:S(2)}, u32[]{:S(2)}) collective-permute-start(bf16[128,1024]{1,0:T(8,128)(2,1)S(1)} %get-tuple-element.41), channel_id=1, source_target_pairs={{0,2},{1,3},{2,0},{3,1},{16,18},{17,19},{18,16},{19,17},{4,6},{5,7... | collective-permute-start | bytes 786440 | tf_op jit(solution)/shard_map/ppermute | solution.py:27
  102.5 14.8 %collective-permute-start.23 = (bf16[128,1024]{1,0:T(8,128)(2,1)S(1)}, bf16[128,1024]{1,0:T(8,128)(2,1)S(1)}, u32[]{:S(2)}, u32[]{:S(2)}) collective-permute-start(bf16[128,1024]{1,0:T(8,128)(2,1)S(1)} %get-tuple-element.42), channel_id=1, source_target_pairs={{0,3},{1,2},{2,1},{3,0},{16,19},{17,18},{18,17},{19,16},{4,7},{5,6... | collective-permute-start | bytes 786440 | tf_op jit(solution)/shard_map/ppermute | solution.py:27
  106.2 11.1 %collective-permute-start.24 = (bf16[128,1024]{1,0:T(8,128)(2,1)S(1)}, bf16[128,1024]{1,0:T(8,128)(2,1)S(1)}, u32[]{:S(2)}, u32[]{:S(2)}) collective-permute-start(bf16[128,1024]{1,0:T(8,128)(2,1)S(1)} %get-tuple-element.43), channel_id=1, source_target_pairs={{0,1},{1,0},{2,3},{3,2},{16,17},{17,16},{18,19},{19,18},{4,5},{5,4... | collective-permute-start | bytes 786440 | tf_op jit(solution)/shard_map/ppermute | solution.py:27
  (1 other events, 0.7 us)

commit v20 on v19

--- a/solution.py
+++ b/solution.py
@@ -273,15 +273,15 @@
     def exchanged(blocks):
         return blocks[:1] + [to_partner(blocks[n], "inner", inner, n) for n in range(1, inner)]
 
-    def rings(near, far, first_cost=0, third_after=()):
+    def rings(near, far, first_cost=0, second_after=()):
         near, far = [near], [far]
         for step in range(1, outer):
             for blocks in near, far:
                 block = blocks[-1]
-                if step == 2 and first_cost:
-                    block = joined([block], first_cost)
-                if step == 3:
-                    block = after(block, *third_after)
+                if step == 2:
+                    block = after(block, *second_after)
+                    if first_cost:
+                        block = joined([block], first_cost)
                 blocks.append(next_on_ring(block, outer))
         return near, far
 
@@ -300,14 +300,14 @@
 
     down_maps = [m for pair in zip(down_near, down_far) for m in pair]
     packed, id_rows = down_product(labels, rows, down_maps, rank)
-    terms = swap(packed)
     up_near, up_far = rings(
         after(jnp.concatenate(up[:middle], axis=0), down_near[-1]),
-        jnp.concatenate([after(block, packed) for block in up[middle:]], axis=0),
-        third_after=[terms],
+        jnp.concatenate([after(block, down_far[-1]) for block in up[middle:]], axis=0),
+        second_after=[packed],
     )
     up_maps = [m for pair in zip(up_near, up_far) for m in pair]
-    shrunk = swap(summed_copies(terms))
+    shrunk = swap(summed_copies(swap(packed)))
+    shrunk = after(shrunk, to_partner(after(id_rows, shrunk), "inner", inner, 1))
     offsets = sorted(range(1, members), key=lambda n: (-(n >= inner) - (n % inner >= 2), -(n >= inner), n)) + [0]
     results = []
     for some in offsets[: members // 2], offsets[members // 2 :]:

time: 119 us -> 112 us (0.941)
  waiting for transfers between devices: 65.1 us -> 59.3 us
  local copies, waits for them, and re-layouts: 7.59 us -> 4.59 us
  blocking collectives: 7.75 us -> 8.97 us
    all_to_all x2, waiting for transfers between devices: 4.52 us -> 0.01 us  [swap(): return lax.all_to_all(value, PLANE, split_axis=0, concat_axis=0, tiled=True)]
    ppermute x12, waiting for transfers between devices: 44.8 us -> 41.5 us  [next_on_ring(): lax.ppermute(block, 'outer', [(i, (i + 1) % outer) for i in range(outer)])]
    ppermute x13, waiting for transfers between devices: 15.7 us -> 17.8 us  [to_partner(): return lax.ppermute(value, axes, [(i, i ^ offset) for i in range(size)])]
    all_to_all x1, blocking collectives: 7.75 us -> 8.97 us  [swap(): return lax.all_to_all(value, PLANE, split_axis=0, concat_axis=0, tiled=True)]
    unnamed x13 -> x15, local copies, waits for them, and re-layouts: 3.53 us -> 2.61 us
  transfers between devices with their start and end apart: 27 -> 27, of which waited for: 16 -> 17; matrix products, arithmetic and copies ran while one was open for 4% -> 2% of each run, Pallas kernels for 7% -> 8%
where the time goes in v20:
time: 112 us
  waiting for transfers between devices  59.3 us (53%)
  starting transfers between devices  25.3 us (23%)
  Pallas kernels  12.3 us (11%)
  blocking collectives  8.97 us (8%)
  local copies, waits for them, and re-layouts  4.59 us (4%)
    ppermute x12, waiting for transfers between devices, next_on_ring(): lax.ppermute(block, 'outer', [(i, (i + 1) % outer) for i in range(outer)])  41.5 us
    ppermute x13, waiting for transfers between devices, to_partner(): return lax.ppermute(value, axes, [(i, i ^ offset) for i in range(size)])  17.8 us
    ppermute x13, starting transfers between devices, to_partner(): return lax.ppermute(value, axes, [(i, i ^ offset) for i in range(size)])  12 us
    all_to_all x1, blocking collectives, swap(): return lax.all_to_all(value, PLANE, split_axis=0, concat_axis=0, tiled=True)  8.97 us
    all_to_all x2, starting transfers between devices, swap(): return lax.all_to_all(value, PLANE, split_axis=0, concat_axis=0, tiled=True)  7.56 us
    ppermute x12, starting transfers between devices, next_on_ring(): lax.ppermute(block, 'outer', [(i, (i + 1) % outer) for i in range(outer)])  5.81 us
    pallas_call x2, Pallas kernels, up_product(): pl.pallas_call(functools.partial(up_kernel, len(maps), rank, offsets), ou...  4.93 us
    pallas_call x1, Pallas kernels, down_product(): pl.pallas_call(functools.partial(down_kernel, len(maps), rank), out_shape...  4.25 us
  transfers between devices with their start and end apart: 27, of which 17 were waited for; matrix products, arithmetic and copies ran while one was open for 2% of the time, Pallas kernels for 8%

profile of v20, /device:TPU:0, one launch (start us, length us, event | category | flops | bytes accessed | tf_op | source)
XLA Modules:
  0.0 111.7 jit_solution(2421474778050169449)
XLA Ops:
  1.7 2.6 %collective-permute-start.1 = (bf16[64,1024]{1,0:T(8,128)(2,1)S(1)}, bf16[64,1024]{1,0:T(8,128)(2,1)S(1)}, u32[]{:S(2)}, u32[]{:S(2)}) collective-permute-start(bf16[64,1024]{1,0:T(8,128)(2,1)S(1)} %get-tuple-element.52), channel_id=1, source_target_pairs={{0,2},{1,3},{2,0},{3,1},{4,6},{5,7},{6,4},{7,5},{8,10},{9,11},{10,... | collective-permute-start | bytes 393224 | tf_op jit(solution)/shard_map/ppermute | solution.py:27
  4.3 1.8 %collective-permute-start.3 = (bf16[128,1024]{1,0:T(8,128)(2,1)S(1)}, bf16[128,1024]{1,0:T(8,128)(2,1)S(1)}, u32[]{:S(2)}, u32[]{:S(2)}) collective-permute-start(bf16[128,1024]{1,0:T(8,128)(2,1)S(1)} %join_blocks.4.refs_0_), channel_id=1, source_target_pairs={{0,4},{4,8},{8,12},{12,0},{1,5},{5,9},{9,13},{13,1},{2,6},{6,10},{... | collective-permute-start | bytes 786440 | tf_op jit(solution)/shard_map/ppermute | solution.py:31
  6.2 1.6 %outgoing_rows.1 = bf16[8,136,1024]{2,1,0:T(8,128)(2,1)} custom-call(bf16[128,8192]{1,0:T(8,128)(2,1)S(1)} %copy-done, s32[1,128]{1,0:T(1,128)S(1)} %bitcast.26), custom_call_target="tpu_custom_call" | custom-call | tf_op jit(solution)/shard_map/outgoing_rows/pallas_call | solution.py:94
  7.8 3.7 %all-to-all-start = ((bf16[8,136,1024]{2,1,0:T(8,128)(2,1)}), bf16[8,136,1024]{2,1,0:T(8,128)(2,1)S(1)}, u32[]{:S(2)}, u32[]{:S(2)}) async-start(bf16[8,136,1024]{2,1,0:T(8,128)(2,1)} %outgoing_rows.1), calls=%async_computation | async-start | bytes 4456448 | tf_op jit(solution)/shard_map/all_to_all | solution.py:39
  11.6 1.6 %collective-permute-start.4 = (bf16[128,1024]{1,0:T(8,128)(2,1)S(1)}, bf16[128,1024]{1,0:T(8,128)(2,1)S(1)}, u32[]{:S(2)}, u32[]{:S(2)}) collective-permute-start(bf16[128,1024]{1,0:T(8,128)(2,1)S(1)} %join_blocks.5.refs_1_), channel_id=1, source_target_pairs={{0,4},{4,8},{8,12},{12,0},{1,5},{5,9},{9,13},{13,1},{2,6},{6,10},{... | collective-permute-start | bytes 786440 | tf_op jit(solution)/shard_map/ppermute | solution.py:31
  13.2 1.8 %collective-permute-done.3.refs_0_.refs_2_ = bf16[128,1024]{1,0:T(8,128)(2,1)S(1)} collective-permute-done((bf16[128,1024]{1,0:T(8,128)(2,1)S(1)}, bf16[128,1024]{1,0:T(8,128)(2,1)S(1)}, u32[]{:S(2)}, u32[]{:S(2)}) %collective-permute-start.3) | collective-permute-done | bytes 262176 | tf_op jit(solution)/shard_map/ppermute | solution.py:31
  15.1 7.4 %collective-permute-done.4.refs_0_.refs_3_ = bf16[128,1024]{1,0:T(8,128)(2,1)S(1)} collective-permute-done((bf16[128,1024]{1,0:T(8,128)(2,1)S(1)}, bf16[128,1024]{1,0:T(8,128)(2,1)S(1)}, u32[]{:S(2)}, u32[]{:S(2)}) %collective-permute-start.4) | collective-permute-done | bytes 262176 | tf_op jit(solution)/shard_map/ppermute | solution.py:31
  23.2 4.9 %collective-permute-done.5.refs_4_ = bf16[128,1024]{1,0:T(8,128)(2,1)S(1)} collective-permute-done((bf16[128,1024]{1,0:T(8,128)(2,1)S(1)}, bf16[128,1024]{1,0:T(8,128)(2,1)S(1)}, u32[]{:S(2)}, u32[]{:S(2)}) %collective-permute-start.5) | collective-permute-done | bytes 262176 | tf_op jit(solution)/shard_map/ppermute | solution.py:31
  28.2 6.2 %collective-permute-done.6.refs_5_ = bf16[128,1024]{1,0:T(8,128)(2,1)} collective-permute-done((bf16[128,1024]{1,0:T(8,128)(2,1)S(1)}, bf16[128,1024]{1,0:T(8,128)(2,1)}, u32[]{:S(2)}, u32[]{:S(2)}) %collective-permute-start.6) | collective-permute-done | bytes 262176 | tf_op jit(solution)/shard_map/ppermute | solution.py:31
  35.2 2.1 %collective-permute-start.10 = (bf16[64,1024]{1,0:T(8,128)(2,1)}, bf16[64,1024]{1,0:T(8,128)(2,1)S(1)}, u32[]{:S(2)}, u32[]{:S(2)}) collective-permute-start(bf16[64,1024]{1,0:T(8,128)(2,1)} %get-tuple-element.31), channel_id=1, source_target_pairs={{0,2},{1,3},{2,0},{3,1},{4,6},{5,7},{6,4},{7,5},{8,10},{9,11},{10,... | collective-permute-start | bytes 393224 | tf_op jit(solution)/shard_map/ppermute | solution.py:27
  38.4 1.6 %collective-permute-done.7.refs_6_ = bf16[128,1024]{1,0:T(8,128)(2,1)} collective-permute-done((bf16[128,1024]{1,0:T(8,128)(2,1)S(1)}, bf16[128,1024]{1,0:T(8,128)(2,1)}, u32[]{:S(2)}, u32[]{:S(2)}) %collective-permute-start.7) | collective-permute-done | bytes 262176 | tf_op jit(solution)/shard_map/ppermute | solution.py:31
  40.0 1.8 %collective-permute-done.10 = bf16[64,1024]{1,0:T(8,128)(2,1)S(1)} collective-permute-done((bf16[64,1024]{1,0:T(8,128)(2,1)}, bf16[64,1024]{1,0:T(8,128)(2,1)S(1)}, u32[]{:S(2)}, u32[]{:S(2)}) %collective-permute-start.10) | collective-permute-done | bytes 131104 | tf_op jit(solution)/shard_map/ppermute | solution.py:27
  41.8 2.9 %collective-permute-done.8.refs_7_ = bf16[128,1024]{1,0:T(8,128)(2,1)} collective-permute-done((bf16[128,1024]{1,0:T(8,128)(2,1)}, bf16[128,1024]{1,0:T(8,128)(2,1)}, u32[]{:S(2)}, u32[]{:S(2)}) %collective-permute-start.8) | collective-permute-done | bytes 262176 | tf_op jit(solution)/shard_map/ppermute | solution.py:31
  45.4 1.6 %collective-permute-start.13 = (bf16[128,1024]{1,0:T(8,128)(2,1)S(1)}, bf16[128,1024]{1,0:T(8,128)(2,1)}, u32[]{:S(2)}, u32[]{:S(2)}) collective-permute-start(bf16[128,1024]{1,0:T(8,128)(2,1)S(1)} %constant_dynamic-update-slice_fusion.refs_1_), channel_id=1, source_target_pairs={{0,4},{4,8},{8,12},{12,0},{1,5},{5,9},{9,13},{13,1},{2,6},{6,10},{... | collective-permute-start | bytes 786440 | tf_op jit(solution)/shard_map/ppermute | solution.py:31
  49.1 4.3 %down_product.1 = (f32[8,64,128]{2,1,0:T(8,128)}, f32[8,128]{1,0:T(8,128)S(1)}) custom-call(s32[16]{0:T(128)S(1)} %add.61.labels_ref, bf16[8,136,1024]{2,1,0:T(8,128)(2,1)S(1)} %all-to-all-done.rows_ref, bf16[128,1024]{1,0:T(8,128)(2,1)S(1)} %join_blocks.4.refs_0_, bf16[128,1024]{1,0:T(8,128)(2,1)S(1)} %join_blocks.5.refs_1_, ...), custom_call_target="tpu_custom_call" | custom-call | flops 2147483648 | bytes 4194304 | tf_op jit(solution)/shard_map/down_product/pallas_call | solution.py:146
  53.3 2.5 %collective-permute-done.12.refs_2_ = bf16[128,1024]{1,0:T(8,128)(2,1)} collective-permute-done((bf16[128,1024]{1,0:T(8,128)(2,1)S(1)}, bf16[128,1024]{1,0:T(8,128)(2,1)}, u32[]{:S(2)}, u32[]{:S(2)}) %collective-permute-start.12) | collective-permute-done | bytes 262176 | tf_op jit(solution)/shard_map/ppermute | solution.py:31
  55.8 5.6 %collective-permute-done.13.refs_3_ = bf16[128,1024]{1,0:T(8,128)(2,1)} collective-permute-done((bf16[128,1024]{1,0:T(8,128)(2,1)S(1)}, bf16[128,1024]{1,0:T(8,128)(2,1)}, u32[]{:S(2)}, u32[]{:S(2)}) %collective-permute-start.13) | collective-permute-done | bytes 262176 | tf_op jit(solution)/shard_map/ppermute | solution.py:31
  61.4 3.8 %all-to-all-start.1 = ((f32[8,64,128]{2,1,0:T(8,128)}), f32[8,64,128]{2,1,0:T(8,128)S(1)}, u32[]{:S(2)}, u32[]{:S(2)}) async-start(f32[8,64,128]{2,1,0:T(8,128)} %get-tuple-element.27), calls=%async_computation.1 | async-start | bytes 524288 | tf_op jit(solution)/shard_map/all_to_all | solution.py:39
  65.3 1.8 %collective-permute-done.14.refs_4_ = bf16[128,1024]{1,0:T(8,128)(2,1)S(1)} collective-permute-done((bf16[128,1024]{1,0:T(8,128)(2,1)}, bf16[128,1024]{1,0:T(8,128)(2,1)S(1)}, u32[]{:S(2)}, u32[]{:S(2)}) %collective-permute-start.14) | collective-permute-done | bytes 262176 | tf_op jit(solution)/shard_map/ppermute | solution.py:31
  67.1 5.4 %collective-permute-done.15.refs_5_ = bf16[128,1024]{1,0:T(8,128)(2,1)S(1)} collective-permute-done((bf16[128,1024]{1,0:T(8,128)(2,1)}, bf16[128,1024]{1,0:T(8,128)(2,1)S(1)}, u32[]{:S(2)}, u32[]{:S(2)}) %collective-permute-start.15) | collective-permute-done | bytes 262176 | tf_op jit(solution)/shard_map/ppermute | solution.py:31
  72.5 9.0 %all_to_all.15.shrunk_ref = bf16[8,64,128]{2,1,0:T(8,128)(2,1)S(1)} all-to-all(bf16[8,64,128]{2,1,0:T(8,128)(2,1)S(1)} %summed_copies.1), channel_id=1, replica_groups=mesh['groups'=2,'outer'=4,'inner'=4] {'groups','inner'}, dimensions={0} | all-to-all | bytes 262144 | tf_op jit(solution)/shard_map/all_to_all | solution.py:39
  81.5 1.3 %collective-permute-done.17.refs_7_ = bf16[128,1024]{1,0:T(8,128)(2,1)S(1)} collective-permute-done((bf16[128,1024]{1,0:T(8,128)(2,1)S(1)}, bf16[128,1024]{1,0:T(8,128)(2,1)S(1)}, u32[]{:S(2)}, u32[]{:S(2)}) %collective-permute-start.17) | collective-permute-done | bytes 262176 | tf_op jit(solution)/shard_map/ppermute | solution.py:31
  82.7 2.5 %up_product.2 = (bf16[128,1024]{1,0:T(8,128)(2,1)S(1)}, bf16[128,1024]{1,0:T(8,128)(2,1)S(1)}, bf16[128,1024]{1,0:T(8,128)(2,1)S(1)}, bf16[128,1024]{1,0:T(8,128)(2,1)S(1)}) custom-call(s32[16]{0:T(128)S(1)} %add.61.labels_ref, s32[1]{0:T(128)} %bitcast.me_ref, f32[8,128]{1,0:T(8,128)S(1)} %get-tuple-element.26.ids_ref, ...), custom_call_target="tpu_custom_call" | custom-call | flops 1073741824 | bytes 3145728 | tf_op jit(solution)/shard_map/up_product/pallas_call | solution.py:217
  85.2 2.7 %collective-permute-start.18 = (bf16[128,1024]{1,0:T(8,128)(2,1)S(1)}, bf16[128,1024]{1,0:T(8,128)(2,1)S(1)}, u32[]{:S(2)}, u32[]{:S(2)}) collective-permute-start(bf16[128,1024]{1,0:T(8,128)(2,1)S(1)} %get-tuple-element.37), channel_id=1, source_target_pairs={{0,18},{1,19},{2,16},{3,17},{16,2},{17,3},{18,0},{19,1},{4,22},{5,... | collective-permute-start | bytes 786440 | tf_op jit(solution)/shard_map/ppermute | solution.py:27
  88.5 1.2 %collective-permute-start.21 = (bf16[128,1024]{1,0:T(8,128)(2,1)S(1)}, bf16[128,1024]{1,0:T(8,128)(2,1)S(1)}, u32[]{:S(2)}, u32[]{:S(2)}) collective-permute-start(bf16[128,1024]{1,0:T(8,128)(2,1)S(1)} %get-tuple-element.40), channel_id=1, source_target_pairs={{0,17},{1,16},{2,19},{3,18},{16,1},{17,0},{18,3},{19,2},{4,21},{5,... | collective-permute-start | bytes 786440 | tf_op jit(solution)/shard_map/ppermute | solution.py:27
  89.7 2.5 %up_product.3 = (bf16[128,1024]{1,0:T(8,128)(2,1)S(1)}, bf16[128,1024]{1,0:T(8,128)(2,1)S(1)}, bf16[128,1024]{1,0:T(8,128)(2,1)S(1)}, bf16[128,1024]{1,0:T(8,128)(2,1)S(1)}) custom-call(s32[16]{0:T(128)S(1)} %add.61.labels_ref, s32[1]{0:T(128)} %bitcast.me_ref, f32[8,128]{1,0:T(8,128)S(1)} %get-tuple-element.26.ids_ref, ...), custom_call_target="tpu_custom_call" | custom-call | flops 1073741824 | bytes 3145728 | tf_op jit(solution)/shard_map/up_product/pallas_call | solution.py:217
  92.2 1.8 %collective-permute-start.22 = (bf16[128,1024]{1,0:T(8,128)(2,1)S(1)}, bf16[128,1024]{1,0:T(8,128)(2,1)S(1)}, u32[]{:S(2)}, u32[]{:S(2)}) collective-permute-start(bf16[128,1024]{1,0:T(8,128)(2,1)S(1)} %get-tuple-element.41), channel_id=1, source_target_pairs={{0,2},{1,3},{2,0},{3,1},{16,18},{17,19},{18,16},{19,17},{4,6},{5,7... | collective-permute-start | bytes 786440 | tf_op jit(solution)/shard_map/ppermute | solution.py:27
  93.9 1.2 %collective-permute-done.18.refs_0_ = bf16[128,1024]{1,0:T(8,128)(2,1)S(1)} collective-permute-done((bf16[128,1024]{1,0:T(8,128)(2,1)S(1)}, bf16[128,1024]{1,0:T(8,128)(2,1)S(1)}, u32[]{:S(2)}, u32[]{:S(2)}) %collective-permute-start.18) | collective-permute-done | bytes 262176 | tf_op jit(solution)/shard_map/ppermute | solution.py:27
  95.2 5.2 %collective-permute-done.19.refs_1_ = bf16[128,1024]{1,0:T(8,128)(2,1)S(1)} collective-permute-done((bf16[128,1024]{1,0:T(8,128)(2,1)S(1)}, bf16[128,1024]{1,0:T(8,128)(2,1)S(1)}, u32[]{:S(2)}, u32[]{:S(2)}) %collective-permute-start.19) | collective-permute-done | bytes 262176 | tf_op jit(solution)/shard_map/ppermute | solution.py:27
  100.6 6.3 %collective-permute-done.20.refs_2_ = bf16[128,1024]{1,0:T(8,128)(2,1)S(1)} collective-permute-done((bf16[128,1024]{1,0:T(8,128)(2,1)S(1)}, bf16[128,1024]{1,0:T(8,128)(2,1)S(1)}, u32[]{:S(2)}, u32[]{:S(2)}) %collective-permute-start.20) | collective-permute-done | bytes 262176 | tf_op jit(solution)/shard_map/ppermute | solution.py:27
  107.0 2.6 %collective-permute-done.21.refs_3_ = bf16[128,1024]{1,0:T(8,128)(2,1)S(1)} collective-permute-done((bf16[128,1024]{1,0:T(8,128)(2,1)S(1)}, bf16[128,1024]{1,0:T(8,128)(2,1)S(1)}, u32[]{:S(2)}, u32[]{:S(2)}) %collective-permute-start.21) | collective-permute-done | bytes 262176 | tf_op jit(solution)/shard_map/ppermute | solution.py:27
  110.3 1.4 %place_results.1 = bf16[128,8192]{1,0:T(8,128)(2,1)} custom-call(s32[1]{0:T(128)} %bitcast.me_ref, bf16[128,1024]{1,0:T(8,128)(2,1)S(1)} %collective-permute-done.18.refs_0_, bf16[128,1024]{1,0:T(8,128)(2,1)S(1)} %collective-permute-done.19.refs_1_, bf16[128,1024]{1,0:T(8,128)(2,1)S(1)} %collective-permute-done.20.refs_2_, ...), custom_call_target="tpu_custom_call" | custom-call | tf_op jit(solution)/shard_map/place_results/pallas_call | solution.py:248
  (55 shorter events, 8.8 us)
Async XLA Ops:
  1.1 3.2 %collective-permute-start = (bf16[64,1024]{1,0:T(8,128)(2,1)S(1)}, bf16[64,1024]{1,0:T(8,128)(2,1)S(1)}, u32[]{:S(2)}, u32[]{:S(2)}) collective-permute-start(bf16[64,1024]{1,0:T(8,128)(2,1)S(1)} %get-tuple-element.50), channel_id=1, source_target_pairs={{0,1},{1,0},{2,3},{3,2},{4,5},{5,4},{6,7},{7,6},{8,9},{9,8},{10,11... | collective-permute-start | bytes 393224 | tf_op jit(solution)/shard_map/ppermute | solution.py:27
  1.7 9.9 %collective-permute-start.1 = (bf16[64,1024]{1,0:T(8,128)(2,1)S(1)}, bf16[64,1024]{1,0:T(8,128)(2,1)S(1)}, u32[]{:S(2)}, u32[]{:S(2)}) collective-permute-start(bf16[64,1024]{1,0:T(8,128)(2,1)S(1)} %get-tuple-element.52), channel_id=1, source_target_pairs={{0,2},{1,3},{2,0},{3,1},{4,6},{5,7},{6,4},{7,5},{8,10},{9,11},{10,... | collective-permute-start | bytes 393224 | tf_op jit(solution)/shard_map/ppermute | solution.py:27
  4.2 7.3 %collective-permute-start.2 = (bf16[64,1024]{1,0:T(8,128)(2,1)S(1)}, bf16[64,1024]{1,0:T(8,128)(2,1)S(1)}, u32[]{:S(2)}, u32[]{:S(2)}) collective-permute-start(bf16[64,1024]{1,0:T(8,128)(2,1)S(1)} %get-tuple-element.49), channel_id=1, source_target_pairs={{0,3},{1,2},{2,1},{3,0},{4,7},{5,6},{6,5},{7,4},{8,11},{9,10},{10,... | collective-permute-start | bytes 393224 | tf_op jit(solution)/shard_map/ppermute | solution.py:27
  4.3 1.9 %copy-start = (bf16[128,8192]{1,0:T(8,128)(2,1)S(1)}, bf16[128,8192]{1,0:T(8,128)(2,1)}, u32[]{:S(2)}) copy-start(bf16[128,8192]{1,0:T(8,128)(2,1)} %hidden_ref) | copy-start | bytes 6291460
  4.3 1.9 %copy-start.1 = (s32[128,1]{0,1:T(1,128)S(1)}, s32[128,1]{0,1:T(1,128)}, u32[]{:S(2)}) copy-start(s32[128,1]{0,1:T(1,128)} %param.4) | copy-start | bytes 1540
  4.3 10.7 %collective-permute-start.3 = (bf16[128,1024]{1,0:T(8,128)(2,1)S(1)}, bf16[128,1024]{1,0:T(8,128)(2,1)S(1)}, u32[]{:S(2)}, u32[]{:S(2)}) collective-permute-start(bf16[128,1024]{1,0:T(8,128)(2,1)S(1)} %join_blocks.4.refs_0_), channel_id=1, source_target_pairs={{0,4},{4,8},{8,12},{12,0},{1,5},{5,9},{9,13},{13,1},{2,6},{6,10},{... | collective-permute-start | bytes 786440 | tf_op jit(solution)/shard_map/ppermute | solution.py:31
  7.8 39.4 %all-to-all-start = ((bf16[8,136,1024]{2,1,0:T(8,128)(2,1)}), bf16[8,136,1024]{2,1,0:T(8,128)(2,1)S(1)}, u32[]{:S(2)}, u32[]{:S(2)}) async-start(bf16[8,136,1024]{2,1,0:T(8,128)(2,1)} %outgoing_rows.1), calls=%async_computation | async-start | bytes 4456448 | tf_op jit(solution)/shard_map/all_to_all | solution.py:39
  11.6 11.0 %collective-permute-start.4 = (bf16[128,1024]{1,0:T(8,128)(2,1)S(1)}, bf16[128,1024]{1,0:T(8,128)(2,1)S(1)}, u32[]{:S(2)}, u32[]{:S(2)}) collective-permute-start(bf16[128,1024]{1,0:T(8,128)(2,1)S(1)} %join_blocks.5.refs_1_), channel_id=1, source_target_pairs={{0,4},{4,8},{8,12},{12,0},{1,5},{5,9},{9,13},{13,1},{2,6},{6,10},{... | collective-permute-start | bytes 786440 | tf_op jit(solution)/shard_map/ppermute | solution.py:31
  15.0 19.4 %copy-start.6 = (bf16[1,64,8192]{2,1,0:T(8,128)(2,1)S(1)}, bf16[1,64,8192]{2,1,0:T(8,128)(2,1)}, u32[]{:S(2)}) copy-start(bf16[1,64,8192]{2,1,0:T(8,128)(2,1)} %param.7) | copy-start | bytes 3145732
  15.1 13.1 %collective-permute-start.5 = (bf16[128,1024]{1,0:T(8,128)(2,1)S(1)}, bf16[128,1024]{1,0:T(8,128)(2,1)S(1)}, u32[]{:S(2)}, u32[]{:S(2)}) collective-permute-start(bf16[128,1024]{1,0:T(8,128)(2,1)S(1)} %join_blocks.6), channel_id=1, source_target_pairs={{0,4},{4,8},{8,12},{12,0},{1,5},{5,9},{9,13},{13,1},{2,6},{6,10},{... | collective-permute-start | bytes 786440 | tf_op jit(solution)/shard_map/ppermute | solution.py:31
  23.2 11.1 %collective-permute-start.6 = (bf16[128,1024]{1,0:T(8,128)(2,1)S(1)}, bf16[128,1024]{1,0:T(8,128)(2,1)}, u32[]{:S(2)}, u32[]{:S(2)}) collective-permute-start(bf16[128,1024]{1,0:T(8,128)(2,1)S(1)} %join_blocks.7), channel_id=1, source_target_pairs={{0,4},{4,8},{8,12},{12,0},{1,5},{5,9},{9,13},{13,1},{2,6},{6,10},{... | collective-permute-start | bytes 786440 | tf_op jit(solution)/shard_map/ppermute | solution.py:31
  28.2 16.6 %copy-start.4 = (bf16[128,1024]{1,0:T(8,128)(2,1)}, bf16[128,1024]{1,0:T(8,128)(2,1)S(1)}, u32[]{:S(2)}) copy-start(bf16[128,1024]{1,0:T(8,128)(2,1)S(1)} %collective-permute-done.5.refs_4_) | copy-start | bytes 786436
  28.2 11.8 %collective-permute-start.7 = (bf16[128,1024]{1,0:T(8,128)(2,1)S(1)}, bf16[128,1024]{1,0:T(8,128)(2,1)}, u32[]{:S(2)}, u32[]{:S(2)}) collective-permute-start(bf16[128,1024]{1,0:T(8,128)(2,1)S(1)} %collective-permute-done.5.refs_4_), channel_id=1, source_target_pairs={{0,4},{4,8},{8,12},{12,0},{1,5},{5,9},{9,13},{13,1},{2,6},{6,10},{... | collective-permute-start | bytes 786440 | tf_op jit(solution)/shard_map/ppermute | solution.py:31
  34.4 10.3 %collective-permute-start.8 = (bf16[128,1024]{1,0:T(8,128)(2,1)}, bf16[128,1024]{1,0:T(8,128)(2,1)}, u32[]{:S(2)}, u32[]{:S(2)}) collective-permute-start(bf16[128,1024]{1,0:T(8,128)(2,1)} %collective-permute-done.6.refs_5_), channel_id=1, source_target_pairs={{0,4},{4,8},{8,12},{12,0},{1,5},{5,9},{9,13},{13,1},{2,6},{6,10},{... | collective-permute-start | bytes 786440 | tf_op jit(solution)/shard_map/ppermute | solution.py:31
  35.1 2.2 %collective-permute-start.9 = (bf16[64,1024]{1,0:T(8,128)(2,1)S(1)}, bf16[64,1024]{1,0:T(8,128)(2,1)}, u32[]{:S(2)}, u32[]{:S(2)}) collective-permute-start(bf16[64,1024]{1,0:T(8,128)(2,1)S(1)} %get-tuple-element.29), channel_id=1, source_target_pairs={{0,1},{1,0},{2,3},{3,2},{4,5},{5,4},{6,7},{7,6},{8,9},{9,8},{10,11... | collective-permute-start | bytes 393224 | tf_op jit(solution)/shard_map/ppermute | solution.py:27
  35.2 6.6 %collective-permute-start.10 = (bf16[64,1024]{1,0:T(8,128)(2,1)}, bf16[64,1024]{1,0:T(8,128)(2,1)S(1)}, u32[]{:S(2)}, u32[]{:S(2)}) collective-permute-start(bf16[64,1024]{1,0:T(8,128)(2,1)} %get-tuple-element.31), channel_id=1, source_target_pairs={{0,2},{1,3},{2,0},{3,1},{4,6},{5,7},{6,4},{7,5},{8,10},{9,11},{10,... | collective-permute-start | bytes 393224 | tf_op jit(solution)/shard_map/ppermute | solution.py:27
  37.2 7.5 %collective-permute-start.11 = (bf16[64,1024]{1,0:T(8,128)(2,1)}, bf16[64,1024]{1,0:T(8,128)(2,1)S(1)}, u32[]{:S(2)}, u32[]{:S(2)}) collective-permute-start(bf16[64,1024]{1,0:T(8,128)(2,1)} %get-tuple-element.33), channel_id=1, source_target_pairs={{0,3},{1,2},{2,1},{3,0},{4,7},{5,6},{6,5},{7,4},{8,11},{9,10},{10,... | collective-permute-start | bytes 393224 | tf_op jit(solution)/shard_map/ppermute | solution.py:27
  44.7 11.1 %collective-permute-start.12 = (bf16[128,1024]{1,0:T(8,128)(2,1)S(1)}, bf16[128,1024]{1,0:T(8,128)(2,1)}, u32[]{:S(2)}, u32[]{:S(2)}) collective-permute-start(bf16[128,1024]{1,0:T(8,128)(2,1)S(1)} %pad_maximum_fusion.refs_0_), channel_id=1, source_target_pairs={{0,4},{4,8},{8,12},{12,0},{1,5},{5,9},{9,13},{13,1},{2,6},{6,10},{... | collective-permute-start | bytes 786440 | tf_op jit(solution)/shard_map/ppermute | solution.py:31
  45.4 16.0 %collective-permute-start.13 = (bf16[128,1024]{1,0:T(8,128)(2,1)S(1)}, bf16[128,1024]{1,0:T(8,128)(2,1)}, u32[]{:S(2)}, u32[]{:S(2)}) collective-permute-start(bf16[128,1024]{1,0:T(8,128)(2,1)S(1)} %constant_dynamic-update-slice_fusion.refs_1_), channel_id=1, source_target_pairs={{0,4},{4,8},{8,12},{12,0},{1,5},{5,9},{9,13},{13,1},{2,6},{6,10},{... | collective-permute-start | bytes 786440 | tf_op jit(solution)/shard_map/ppermute | solution.py:31
  47.2 1.0 copy-start.3
  55.8 11.3 %collective-permute-start.14 = (bf16[128,1024]{1,0:T(8,128)(2,1)}, bf16[128,1024]{1,0:T(8,128)(2,1)S(1)}, u32[]{:S(2)}, u32[]{:S(2)}) collective-permute-start(bf16[128,1024]{1,0:T(8,128)(2,1)} %collective-permute-done.12.refs_2_), channel_id=1, source_target_pairs={{0,4},{4,8},{8,12},{12,0},{1,5},{5,9},{9,13},{13,1},{2,6},{6,10},{... | collective-permute-start | bytes 786440 | tf_op jit(solution)/shard_map/ppermute | solution.py:31
  61.4 11.0 %collective-permute-start.15 = (bf16[128,1024]{1,0:T(8,128)(2,1)}, bf16[128,1024]{1,0:T(8,128)(2,1)S(1)}, u32[]{:S(2)}, u32[]{:S(2)}) collective-permute-start(bf16[128,1024]{1,0:T(8,128)(2,1)} %collective-permute-done.13.refs_3_), channel_id=1, source_target_pairs={{0,4},{4,8},{8,12},{12,0},{1,5},{5,9},{9,13},{13,1},{2,6},{6,10},{... | collective-permute-start | bytes 786440 | tf_op jit(solution)/shard_map/ppermute | solution.py:31
  61.4 11.0 %all-to-all-start.1 = ((f32[8,64,128]{2,1,0:T(8,128)}), f32[8,64,128]{2,1,0:T(8,128)S(1)}, u32[]{:S(2)}, u32[]{:S(2)}) async-start(f32[8,64,128]{2,1,0:T(8,128)} %get-tuple-element.27), calls=%async_computation.1 | async-start | bytes 524288 | tf_op jit(solution)/shard_map/all_to_all | solution.py:39
  67.1 14.4 %collective-permute-start.16 = (bf16[128,1024]{1,0:T(8,128)(2,1)S(1)}, bf16[128,1024]{1,0:T(8,128)(2,1)S(1)}, u32[]{:S(2)}, u32[]{:S(2)}) collective-permute-start(bf16[128,1024]{1,0:T(8,128)(2,1)S(1)} %collective-permute-done.14.refs_4_), channel_id=1, source_target_pairs={{0,4},{4,8},{8,12},{12,0},{1,5},{5,9},{9,13},{13,1},{2,6},{6,10},{... | collective-permute-start | bytes 786440 | tf_op jit(solution)/shard_map/ppermute | solution.py:31
  72.4 10.3 %collective-permute-start.17 = (bf16[128,1024]{1,0:T(8,128)(2,1)S(1)}, bf16[128,1024]{1,0:T(8,128)(2,1)S(1)}, u32[]{:S(2)}, u32[]{:S(2)}) collective-permute-start(bf16[128,1024]{1,0:T(8,128)(2,1)S(1)} %collective-permute-done.15.refs_5_), channel_id=1, source_target_pairs={{0,4},{4,8},{8,12},{12,0},{1,5},{5,9},{9,13},{13,1},{2,6},{6,10},{... | collective-permute-start | bytes 786440 | tf_op jit(solution)/shard_map/ppermute | solution.py:31
  85.2 10.0 %collective-permute-start.18 = (bf16[128,1024]{1,0:T(8,128)(2,1)S(1)}, bf16[128,1024]{1,0:T(8,128)(2,1)S(1)}, u32[]{:S(2)}, u32[]{:S(2)}) collective-permute-start(bf16[128,1024]{1,0:T(8,128)(2,1)S(1)} %get-tuple-element.37), channel_id=1, source_target_pairs={{0,18},{1,19},{2,16},{3,17},{16,2},{17,3},{18,0},{19,1},{4,22},{5,... | collective-permute-start | bytes 786440 | tf_op jit(solution)/shard_map/ppermute | solution.py:27
  87.9 12.4 %collective-permute-start.19 = (bf16[128,1024]{1,0:T(8,128)(2,1)S(1)}, bf16[128,1024]{1,0:T(8,128)(2,1)S(1)}, u32[]{:S(2)}, u32[]{:S(2)}) collective-permute-start(bf16[128,1024]{1,0:T(8,128)(2,1)S(1)} %get-tuple-element.38), channel_id=1, source_target_pairs={{0,19},{1,18},{2,17},{3,16},{16,3},{17,2},{18,1},{19,0},{4,23},{5,... | collective-permute-start | bytes 786440 | tf_op jit(solution)/shard_map/ppermute | solution.py:27
  87.9 19.1 %collective-permute-start.20 = (bf16[128,1024]{1,0:T(8,128)(2,1)S(1)}, bf16[128,1024]{1,0:T(8,128)(2,1)S(1)}, u32[]{:S(2)}, u32[]{:S(2)}) collective-permute-start(bf16[128,1024]{1,0:T(8,128)(2,1)S(1)} %get-tuple-element.39), channel_id=1, source_target_pairs={{0,16},{1,17},{2,18},{3,19},{16,0},{17,1},{18,2},{19,3},{4,20},{5,... | collective-permute-start | bytes 786440 | tf_op jit(solution)/shard_map/ppermute | solution.py:27
  88.5 21.1 %collective-permute-start.21 = (bf16[128,1024]{1,0:T(8,128)(2,1)S(1)}, bf16[128,1024]{1,0:T(8,128)(2,1)S(1)}, u32[]{:S(2)}, u32[]{:S(2)}) collective-permute-start(bf16[128,1024]{1,0:T(8,128)(2,1)S(1)} %get-tuple-element.40), channel_id=1, source_target_pairs={{0,17},{1,16},{2,19},{3,18},{16,1},{17,0},{18,3},{19,2},{4,21},{5,... | collective-permute-start | bytes 786440 | tf_op jit(solution)/shard_map/ppermute | solution.py:27
  92.2 17.4 %collective-permute-start.22 = (bf16[128,1024]{1,0:T(8,128)(2,1)S(1)}, bf16[128,1024]{1,0:T(8,128)(2,1)S(1)}, u32[]{:S(2)}, u32[]{:S(2)}) collective-permute-start(bf16[128,1024]{1,0:T(8,128)(2,1)S(1)} %get-tuple-element.41), channel_id=1, source_target_pairs={{0,2},{1,3},{2,0},{3,1},{16,18},{17,19},{18,16},{19,17},{4,6},{5,7... | collective-permute-start | bytes 786440 | tf_op jit(solution)/shard_map/ppermute | solution.py:27
  95.2 15.1 %collective-permute-start.23 = (bf16[128,1024]{1,0:T(8,128)(2,1)S(1)}, bf16[128,1024]{1,0:T(8,128)(2,1)S(1)}, u32[]{:S(2)}, u32[]{:S(2)}) collective-permute-start(bf16[128,1024]{1,0:T(8,128)(2,1)S(1)} %get-tuple-element.42), channel_id=1, source_target_pairs={{0,3},{1,2},{2,1},{3,0},{16,19},{17,18},{18,17},{19,16},{4,7},{5,6... | collective-permute-start | bytes 786440 | tf_op jit(solution)/shard_map/ppermute | solution.py:27
  100.3 10.0 %collective-permute-start.24 = (bf16[128,1024]{1,0:T(8,128)(2,1)S(1)}, bf16[128,1024]{1,0:T(8,128)(2,1)S(1)}, u32[]{:S(2)}, u32[]{:S(2)}) collective-permute-start(bf16[128,1024]{1,0:T(8,128)(2,1)S(1)} %get-tuple-element.43), channel_id=1, source_target_pairs={{0,1},{1,0},{2,3},{3,2},{16,17},{17,16},{18,19},{19,18},{4,5},{5,4... | collective-permute-start | bytes 786440 | tf_op jit(solution)/shard_map/ppermute | solution.py:27
  (2 other events, 1.7 us)

commit v21 on v20

--- a/solution.py
+++ b/solution.py
@@ -273,16 +273,18 @@
     def exchanged(blocks):
         return blocks[:1] + [to_partner(blocks[n], "inner", inner, n) for n in range(1, inner)]
 
-    def rings(near, far, first_cost=0, second_after=()):
+    def rings(near, far, near_cost, far_cost, far_second_after=()):
         near, far = [near], [far]
         for step in range(1, outer):
-            for blocks in near, far:
-                block = blocks[-1]
-                if step == 2:
-                    block = after(block, *second_after)
-                    if first_cost:
-                        block = joined([block], first_cost)
-                blocks.append(next_on_ring(block, outer))
+            near_block, far_block = near[-1], far[-1]
+            if step == 2:
+                far_block = after(far_block, *far_second_after)
+                if near_cost:
+                    near_block = joined([near_block], near_cost)
+                if far_cost:
+                    far_block = joined([far_block], far_cost)
+            near.append(next_on_ring(near_block, outer))
+            far.append(next_on_ring(far_block, outer))
         return near, far
 
     steps_back = jnp.arange(outer, dtype=jnp.int32)[:, None]
@@ -293,7 +295,7 @@
 
     middle = inner // 2
     down = exchanged(slices(adapter_down_maps[0].T))
-    down_near, down_far = rings(joined(down[:middle], AHEAD), joined(down[middle:], AHEAD), first_cost=SLIGHTLY_AHEAD)
+    down_near, down_far = rings(joined(down[:middle], AHEAD), joined(down[middle:], AHEAD), SLIGHTLY_AHEAD, SLIGHTLY_AHEAD)
     ids = token_adapter_index.reshape(1, tok)
     rows = swap(outgoing_rows(after(hidden, down_near[0]), ids, members))
     up = exchanged([after(block, down_near[1]) for block in slices(adapter_up_maps[0])])
@@ -303,11 +305,12 @@
     up_near, up_far = rings(
         after(jnp.concatenate(up[:middle], axis=0), down_near[-1]),
         jnp.concatenate([after(block, down_far[-1]) for block in up[middle:]], axis=0),
-        second_after=[packed],
+        SLIGHTLY_AHEAD,
+        0,
+        far_second_after=[packed],
     )
     up_maps = [m for pair in zip(up_near, up_far) for m in pair]
     shrunk = swap(summed_copies(swap(packed)))
-    shrunk = after(shrunk, to_partner(after(id_rows, shrunk), "inner", inner, 1))
     offsets = sorted(range(1, members), key=lambda n: (-(n >= inner) - (n % inner >= 2), -(n >= inner), n)) + [0]
     results = []
     for some in offsets[: members // 2], offsets[members // 2 :]:

time: 112 us -> 110 us (0.982)
  blocking collectives: 8.97 us -> 0 us
  starting transfers between devices: 25.3 us -> 30.3 us
  Pallas kernels: 12.3 us -> 15.5 us
  waiting for transfers between devices: 59.3 us -> 57 us
  local copies, waits for them, and re-layouts: 4.59 us -> 5.84 us
    all_to_all x1 -> x0, blocking collectives: 8.97 us -> none  [swap(): return lax.all_to_all(value, PLANE, split_axis=0, concat_axis=0, tiled=True)]
    ppermute x12, waiting for transfers between devices: 41.5 us -> 32.7 us  [next_on_ring(): lax.ppermute(block, 'outer', [(i, (i + 1) % outer) for i in range(outer)])]
    all_to_all x2 -> x3, waiting for transfers between devices: 0.01 us -> 6.38 us  [swap(): return lax.all_to_all(value, PLANE, split_axis=0, concat_axis=0, tiled=True)]
    all_to_all x2 -> x3, starting transfers between devices: 7.56 us -> 11.5 us  [swap(): return lax.all_to_all(value, PLANE, split_axis=0, concat_axis=0, tiled=True)]
    pallas_call x4 -> x5, Pallas kernels: 0.07 us -> 2.49 us  [joined(): pl.pallas_call(join_kernel, out_shape=jax.ShapeDtypeStruct((len(blocks) *...]
  transfers between devices with their start and end apart: 27 -> 28, of which waited for: 17 -> 18; matrix products, arithmetic and copies ran while one was open for 2% -> 3% of each run, Pallas kernels for 8% -> 11%
where the time goes in v21:
time: 110 us
  waiting for transfers between devices  57 us (52%)
  starting transfers between devices  30.3 us (28%)
  Pallas kernels  15.5 us (14%)
  local copies, waits for them, and re-layouts  5.84 us (5%)
    ppermute x12, waiting for transfers between devices, next_on_ring(): lax.ppermute(block, 'outer', [(i, (i + 1) % outer) for i in range(outer)])  32.7 us
    ppermute x13, waiting for transfers between devices, to_partner(): return lax.ppermute(value, axes, [(i, i ^ offset) for i in range(size)])  17.9 us
    ppermute x13, starting transfers between devices, to_partner(): return lax.ppermute(value, axes, [(i, i ^ offset) for i in range(size)])  12.3 us
    all_to_all x3, starting transfers between devices, swap(): return lax.all_to_all(value, PLANE, split_axis=0, concat_axis=0, tiled=True)  11.5 us
    ppermute x12, starting transfers between devices, next_on_ring(): lax.ppermute(block, 'outer', [(i, (i + 1) % outer) for i in range(outer)])  6.52 us
    all_to_all x3, waiting for transfers between devices, swap(): return lax.all_to_all(value, PLANE, split_axis=0, concat_axis=0, tiled=True)  6.38 us
    pallas_call x2, Pallas kernels, up_product(): pl.pallas_call(functools.partial(up_kernel, len(maps), rank, offsets), ou...  5.09 us
    pallas_call x1, Pallas kernels, down_product(): pl.pallas_call(functools.partial(down_kernel, len(maps), rank), out_shape...  4.25 us
  transfers between devices with their start and end apart: 28, of which 18 were waited for; matrix products, arithmetic and copies ran while one was open for 3% of the time, Pallas kernels for 11%

profile of v21, /device:TPU:0, one launch (start us, length us, event | category | flops | bytes accessed | tf_op | source)
XLA Modules:
  0.0 109.8 jit_solution(11982252966616896872)
XLA Ops:
  1.7 2.6 %collective-permute-start.1 = (bf16[64,1024]{1,0:T(8,128)(2,1)S(1)}, bf16[64,1024]{1,0:T(8,128)(2,1)S(1)}, u32[]{:S(2)}, u32[]{:S(2)}) collective-permute-start(bf16[64,1024]{1,0:T(8,128)(2,1)S(1)} %get-tuple-element.50), channel_id=1, source_target_pairs={{0,2},{1,3},{2,0},{3,1},{4,6},{5,7},{6,4},{7,5},{8,10},{9,11},{10,... | collective-permute-start | bytes 393224 | tf_op jit(solution)/shard_map/ppermute | solution.py:27
  4.3 1.8 %collective-permute-start.3 = (bf16[128,1024]{1,0:T(8,128)(2,1)S(1)}, bf16[128,1024]{1,0:T(8,128)(2,1)S(1)}, u32[]{:S(2)}, u32[]{:S(2)}) collective-permute-start(bf16[128,1024]{1,0:T(8,128)(2,1)S(1)} %join_blocks.5.refs_0_), channel_id=1, source_target_pairs={{0,4},{4,8},{8,12},{12,0},{1,5},{5,9},{9,13},{13,1},{2,6},{6,10},{... | collective-permute-start | bytes 786440 | tf_op jit(solution)/shard_map/ppermute | solution.py:31
  6.2 1.6 %outgoing_rows.1 = bf16[8,136,1024]{2,1,0:T(8,128)(2,1)} custom-call(bf16[128,8192]{1,0:T(8,128)(2,1)S(1)} %copy-done, s32[1,128]{1,0:T(1,128)S(1)} %bitcast.26), custom_call_target="tpu_custom_call" | custom-call | tf_op jit(solution)/shard_map/outgoing_rows/pallas_call | solution.py:94
  7.8 3.7 %all-to-all-start = ((bf16[8,136,1024]{2,1,0:T(8,128)(2,1)}), bf16[8,136,1024]{2,1,0:T(8,128)(2,1)S(1)}, u32[]{:S(2)}, u32[]{:S(2)}) async-start(bf16[8,136,1024]{2,1,0:T(8,128)(2,1)} %outgoing_rows.1), calls=%async_computation | async-start | bytes 4456448 | tf_op jit(solution)/shard_map/all_to_all | solution.py:39
  11.6 1.6 %collective-permute-start.4 = (bf16[128,1024]{1,0:T(8,128)(2,1)S(1)}, bf16[128,1024]{1,0:T(8,128)(2,1)S(1)}, u32[]{:S(2)}, u32[]{:S(2)}) collective-permute-start(bf16[128,1024]{1,0:T(8,128)(2,1)S(1)} %join_blocks.6.refs_1_), channel_id=1, source_target_pairs={{0,4},{4,8},{8,12},{12,0},{1,5},{5,9},{9,13},{13,1},{2,6},{6,10},{... | collective-permute-start | bytes 786440 | tf_op jit(solution)/shard_map/ppermute | solution.py:31
  13.2 1.8 %collective-permute-done.3.refs_0_.refs_2_ = bf16[128,1024]{1,0:T(8,128)(2,1)S(1)} collective-permute-done((bf16[128,1024]{1,0:T(8,128)(2,1)S(1)}, bf16[128,1024]{1,0:T(8,128)(2,1)S(1)}, u32[]{:S(2)}, u32[]{:S(2)}) %collective-permute-start.3) | collective-permute-done | bytes 262176 | tf_op jit(solution)/shard_map/ppermute | solution.py:31
  15.1 7.4 %collective-permute-done.4.refs_0_.refs_3_ = bf16[128,1024]{1,0:T(8,128)(2,1)S(1)} collective-permute-done((bf16[128,1024]{1,0:T(8,128)(2,1)S(1)}, bf16[128,1024]{1,0:T(8,128)(2,1)S(1)}, u32[]{:S(2)}, u32[]{:S(2)}) %collective-permute-start.4) | collective-permute-done | bytes 262176 | tf_op jit(solution)/shard_map/ppermute | solution.py:31
  23.3 4.8 %collective-permute-done.5.refs_4_ = bf16[128,1024]{1,0:T(8,128)(2,1)S(1)} collective-permute-done((bf16[128,1024]{1,0:T(8,128)(2,1)S(1)}, bf16[128,1024]{1,0:T(8,128)(2,1)S(1)}, u32[]{:S(2)}, u32[]{:S(2)}) %collective-permute-start.5) | collective-permute-done | bytes 262176 | tf_op jit(solution)/shard_map/ppermute | solution.py:31
  29.0 2.1 %collective-permute-start.10 = (bf16[64,1024]{1,0:T(8,128)(2,1)}, bf16[64,1024]{1,0:T(8,128)(2,1)}, u32[]{:S(2)}, u32[]{:S(2)}) collective-permute-start(bf16[64,1024]{1,0:T(8,128)(2,1)} %get-tuple-element.30), channel_id=1, source_target_pairs={{0,2},{1,3},{2,0},{3,1},{4,6},{5,7},{6,4},{7,5},{8,10},{9,11},{10,... | collective-permute-start | bytes 393224 | tf_op jit(solution)/shard_map/ppermute | solution.py:27
  31.4 3.3 %collective-permute-done.6.refs_5_ = bf16[128,1024]{1,0:T(8,128)(2,1)} collective-permute-done((bf16[128,1024]{1,0:T(8,128)(2,1)}, bf16[128,1024]{1,0:T(8,128)(2,1)}, u32[]{:S(2)}, u32[]{:S(2)}) %collective-permute-start.6) | collective-permute-done | bytes 262176 | tf_op jit(solution)/shard_map/ppermute | solution.py:31
  35.7 4.6 %collective-permute-done.7.refs_6_ = bf16[128,1024]{1,0:T(8,128)(2,1)} collective-permute-done((bf16[128,1024]{1,0:T(8,128)(2,1)S(1)}, bf16[128,1024]{1,0:T(8,128)(2,1)}, u32[]{:S(2)}, u32[]{:S(2)}) %collective-permute-start.7) | collective-permute-done | bytes 262176 | tf_op jit(solution)/shard_map/ppermute | solution.py:31
  40.5 1.6 %collective-permute-done.10 = bf16[64,1024]{1,0:T(8,128)(2,1)} collective-permute-done((bf16[64,1024]{1,0:T(8,128)(2,1)}, bf16[64,1024]{1,0:T(8,128)(2,1)}, u32[]{:S(2)}, u32[]{:S(2)}) %collective-permute-start.10) | collective-permute-done | bytes 131104 | tf_op jit(solution)/shard_map/ppermute | solution.py:27
  42.0 4.0 %collective-permute-done.8.refs_7_ = bf16[128,1024]{1,0:T(8,128)(2,1)} collective-permute-done((bf16[128,1024]{1,0:T(8,128)(2,1)}, bf16[128,1024]{1,0:T(8,128)(2,1)}, u32[]{:S(2)}, u32[]{:S(2)}) %collective-permute-start.8) | collective-permute-done | bytes 262176 | tf_op jit(solution)/shard_map/ppermute | solution.py:31
  48.0 2.4 %collective-permute-done.12.refs_0_.refs_2_ = bf16[128,1024]{1,0:T(8,128)(2,1)} collective-permute-done((bf16[128,1024]{1,0:T(8,128)(2,1)S(1)}, bf16[128,1024]{1,0:T(8,128)(2,1)}, u32[]{:S(2)}, u32[]{:S(2)}) %collective-permute-start.12) | collective-permute-done | bytes 262176 | tf_op jit(solution)/shard_map/ppermute | solution.py:31
  50.3 1.7 %join_blocks.9 = bf16[128,1024]{1,0:T(8,128)(2,1)} custom-call(bf16[128,1024]{1,0:T(8,128)(2,1)} %collective-permute-done.12.refs_0_.refs_2_), custom_call_target="tpu_custom_call" | custom-call | flops 6000000000 | bytes 1000000 | tf_op jit(solution)/shard_map/join_blocks/pallas_call | solution.py:60
  53.9 4.3 %down_product.1 = (f32[8,64,128]{2,1,0:T(8,128)}, f32[8,128]{1,0:T(8,128)S(1)}) custom-call(s32[16]{0:T(128)S(1)} %add.61.labels_ref, bf16[8,136,1024]{2,1,0:T(8,128)(2,1)S(1)} %all-to-all-done.rows_ref, bf16[128,1024]{1,0:T(8,128)(2,1)S(1)} %join_blocks.5.refs_0_, bf16[128,1024]{1,0:T(8,128)(2,1)S(1)} %join_blocks.6.refs_1_, ...), custom_call_target="tpu_custom_call" | custom-call | flops 2147483648 | bytes 4194304 | tf_op jit(solution)/shard_map/down_product/pallas_call | solution.py:146
  58.2 1.4 %collective-permute-start.15 = (bf16[128,1024]{1,0:T(8,128)(2,1)}, bf16[128,1024]{1,0:T(8,128)(2,1)S(1)}, u32[]{:S(2)}, u32[]{:S(2)}) collective-permute-start(bf16[128,1024]{1,0:T(8,128)(2,1)} %collective-permute-done.13.refs_3_), channel_id=1, source_target_pairs={{0,4},{4,8},{8,12},{12,0},{1,5},{5,9},{9,13},{13,1},{2,6},{6,10},{... | collective-permute-start | bytes 786440 | tf_op jit(solution)/shard_map/ppermute | solution.py:31
  59.5 4.4 %all-to-all-start.1 = ((f32[8,64,128]{2,1,0:T(8,128)}), f32[8,64,128]{2,1,0:T(8,128)S(1)}, u32[]{:S(2)}, u32[]{:S(2)}) async-start(f32[8,64,128]{2,1,0:T(8,128)} %get-tuple-element.26), calls=%async_computation.1 | async-start | bytes 524288 | tf_op jit(solution)/shard_map/all_to_all | solution.py:39
  63.9 1.6 %collective-permute-start.16 = (bf16[128,1024]{1,0:T(8,128)(2,1)}, bf16[128,1024]{1,0:T(8,128)(2,1)S(1)}, u32[]{:S(2)}, u32[]{:S(2)}) collective-permute-start(bf16[128,1024]{1,0:T(8,128)(2,1)} %collective-permute-done.14.refs_4_), channel_id=1, source_target_pairs={{0,4},{4,8},{8,12},{12,0},{1,5},{5,9},{9,13},{13,1},{2,6},{6,10},{... | collective-permute-start | bytes 786440 | tf_op jit(solution)/shard_map/ppermute | solution.py:31
  65.5 2.1 %collective-permute-done.15.refs_5_ = bf16[128,1024]{1,0:T(8,128)(2,1)S(1)} collective-permute-done((bf16[128,1024]{1,0:T(8,128)(2,1)}, bf16[128,1024]{1,0:T(8,128)(2,1)S(1)}, u32[]{:S(2)}, u32[]{:S(2)}) %collective-permute-start.15) | collective-permute-done | bytes 262176 | tf_op jit(solution)/shard_map/ppermute | solution.py:31
  67.6 2.3 %all-to-all-done.1.terms_ref = f32[8,64,128]{2,1,0:T(8,128)S(1)} async-done(((f32[8,64,128]{2,1,0:T(8,128)}), f32[8,64,128]{2,1,0:T(8,128)S(1)}, u32[]{:S(2)}, u32[]{:S(2)}) %all-to-all-start.1) | async-done | bytes 262176 | tf_op jit(solution)/shard_map/all_to_all | solution.py:39
  70.6 3.4 %all-to-all-start.2 = ((bf16[8,64,128]{2,1,0:T(8,128)(2,1)}), bf16[8,64,128]{2,1,0:T(8,128)(2,1)S(1)}, u32[]{:S(2)}, u32[]{:S(2)}) async-start(bf16[8,64,128]{2,1,0:T(8,128)(2,1)} %summed_copies.1), calls=%async_computation.2 | async-start | bytes 262144 | tf_op jit(solution)/shard_map/all_to_all | solution.py:39
  75.1 4.0 %all-to-all-done.2.shrunk_ref = bf16[8,64,128]{2,1,0:T(8,128)(2,1)S(1)} async-done(((bf16[8,64,128]{2,1,0:T(8,128)(2,1)}), bf16[8,64,128]{2,1,0:T(8,128)(2,1)S(1)}, u32[]{:S(2)}, u32[]{:S(2)}) %all-to-all-start.2) | async-done | bytes 131104 | tf_op jit(solution)/shard_map/all_to_all | solution.py:39
  80.3 2.5 %up_product.2 = (bf16[128,1024]{1,0:T(8,128)(2,1)S(1)}, bf16[128,1024]{1,0:T(8,128)(2,1)S(1)}, bf16[128,1024]{1,0:T(8,128)(2,1)S(1)}, bf16[128,1024]{1,0:T(8,128)(2,1)S(1)}) custom-call(s32[16]{0:T(128)S(1)} %add.61.labels_ref, s32[1]{0:T(128)} %bitcast.me_ref, f32[8,128]{1,0:T(8,128)S(1)} %get-tuple-element.25.ids_ref, ...), custom_call_target="tpu_custom_call" | custom-call | flops 1073741824 | bytes 3145728 | tf_op jit(solution)/shard_map/up_product/pallas_call | solution.py:217
  82.8 2.6 %collective-permute-start.18 = (bf16[128,1024]{1,0:T(8,128)(2,1)S(1)}, bf16[128,1024]{1,0:T(8,128)(2,1)S(1)}, u32[]{:S(2)}, u32[]{:S(2)}) collective-permute-start(bf16[128,1024]{1,0:T(8,128)(2,1)S(1)} %get-tuple-element.35), channel_id=1, source_target_pairs={{0,18},{1,19},{2,16},{3,17},{16,2},{17,3},{18,0},{19,1},{4,22},{5,... | collective-permute-start | bytes 786440 | tf_op jit(solution)/shard_map/ppermute | solution.py:27
  87.3 2.5 %up_product.3 = (bf16[128,1024]{1,0:T(8,128)(2,1)S(1)}, bf16[128,1024]{1,0:T(8,128)(2,1)S(1)}, bf16[128,1024]{1,0:T(8,128)(2,1)S(1)}, bf16[128,1024]{1,0:T(8,128)(2,1)S(1)}) custom-call(s32[16]{0:T(128)S(1)} %add.61.labels_ref, s32[1]{0:T(128)} %bitcast.me_ref, f32[8,128]{1,0:T(8,128)S(1)} %get-tuple-element.25.ids_ref, ...), custom_call_target="tpu_custom_call" | custom-call | flops 1073741824 | bytes 3145728 | tf_op jit(solution)/shard_map/up_product/pallas_call | solution.py:217
  89.8 1.7 %collective-permute-start.22 = (bf16[128,1024]{1,0:T(8,128)(2,1)S(1)}, bf16[128,1024]{1,0:T(8,128)(2,1)S(1)}, u32[]{:S(2)}, u32[]{:S(2)}) collective-permute-start(bf16[128,1024]{1,0:T(8,128)(2,1)S(1)} %get-tuple-element.39), channel_id=1, source_target_pairs={{0,2},{1,3},{2,0},{3,1},{16,18},{17,19},{18,16},{19,17},{4,6},{5,7... | collective-permute-start | bytes 786440 | tf_op jit(solution)/shard_map/ppermute | solution.py:27
  91.5 1.5 %collective-permute-done.18.refs_0_ = bf16[128,1024]{1,0:T(8,128)(2,1)S(1)} collective-permute-done((bf16[128,1024]{1,0:T(8,128)(2,1)S(1)}, bf16[128,1024]{1,0:T(8,128)(2,1)S(1)}, u32[]{:S(2)}, u32[]{:S(2)}) %collective-permute-start.18) | collective-permute-done | bytes 262176 | tf_op jit(solution)/shard_map/ppermute | solution.py:27
  93.0 4.8 %collective-permute-done.19.refs_1_ = bf16[128,1024]{1,0:T(8,128)(2,1)S(1)} collective-permute-done((bf16[128,1024]{1,0:T(8,128)(2,1)S(1)}, bf16[128,1024]{1,0:T(8,128)(2,1)S(1)}, u32[]{:S(2)}, u32[]{:S(2)}) %collective-permute-start.19) | collective-permute-done | bytes 262176 | tf_op jit(solution)/shard_map/ppermute | solution.py:27
  98.5 6.0 %collective-permute-done.20.refs_2_ = bf16[128,1024]{1,0:T(8,128)(2,1)S(1)} collective-permute-done((bf16[128,1024]{1,0:T(8,128)(2,1)S(1)}, bf16[128,1024]{1,0:T(8,128)(2,1)S(1)}, u32[]{:S(2)}, u32[]{:S(2)}) %collective-permute-start.20) | collective-permute-done | bytes 262176 | tf_op jit(solution)/shard_map/ppermute | solution.py:27
  104.5 2.9 %collective-permute-done.21.refs_3_ = bf16[128,1024]{1,0:T(8,128)(2,1)S(1)} collective-permute-done((bf16[128,1024]{1,0:T(8,128)(2,1)S(1)}, bf16[128,1024]{1,0:T(8,128)(2,1)S(1)}, u32[]{:S(2)}, u32[]{:S(2)}) %collective-permute-start.21) | collective-permute-done | bytes 262176 | tf_op jit(solution)/shard_map/ppermute | solution.py:27
  108.4 1.4 %place_results.1 = bf16[128,8192]{1,0:T(8,128)(2,1)} custom-call(s32[1]{0:T(128)} %bitcast.me_ref, bf16[128,1024]{1,0:T(8,128)(2,1)S(1)} %collective-permute-done.18.refs_0_, bf16[128,1024]{1,0:T(8,128)(2,1)S(1)} %collective-permute-done.19.refs_1_, bf16[128,1024]{1,0:T(8,128)(2,1)S(1)} %collective-permute-done.20.refs_2_, ...), custom_call_target="tpu_custom_call" | custom-call | tf_op jit(solution)/shard_map/place_results/pallas_call | solution.py:248
  (57 shorter events, 15.0 us)
Async XLA Ops:
  1.1 3.2 %collective-permute-start = (bf16[64,1024]{1,0:T(8,128)(2,1)S(1)}, bf16[64,1024]{1,0:T(8,128)(2,1)S(1)}, u32[]{:S(2)}, u32[]{:S(2)}) collective-permute-start(bf16[64,1024]{1,0:T(8,128)(2,1)S(1)} %get-tuple-element.48), channel_id=1, source_target_pairs={{0,1},{1,0},{2,3},{3,2},{4,5},{5,4},{6,7},{7,6},{8,9},{9,8},{10,11... | collective-permute-start | bytes 393224 | tf_op jit(solution)/shard_map/ppermute | solution.py:27
  1.7 9.9 %collective-permute-start.1 = (bf16[64,1024]{1,0:T(8,128)(2,1)S(1)}, bf16[64,1024]{1,0:T(8,128)(2,1)S(1)}, u32[]{:S(2)}, u32[]{:S(2)}) collective-permute-start(bf16[64,1024]{1,0:T(8,128)(2,1)S(1)} %get-tuple-element.50), channel_id=1, source_target_pairs={{0,2},{1,3},{2,0},{3,1},{4,6},{5,7},{6,4},{7,5},{8,10},{9,11},{10,... | collective-permute-start | bytes 393224 | tf_op jit(solution)/shard_map/ppermute | solution.py:27
  4.2 7.3 %collective-permute-start.2 = (bf16[64,1024]{1,0:T(8,128)(2,1)S(1)}, bf16[64,1024]{1,0:T(8,128)(2,1)S(1)}, u32[]{:S(2)}, u32[]{:S(2)}) collective-permute-start(bf16[64,1024]{1,0:T(8,128)(2,1)S(1)} %get-tuple-element.47), channel_id=1, source_target_pairs={{0,3},{1,2},{2,1},{3,0},{4,7},{5,6},{6,5},{7,4},{8,11},{9,10},{10,... | collective-permute-start | bytes 393224 | tf_op jit(solution)/shard_map/ppermute | solution.py:27
  4.3 1.9 %copy-start = (bf16[128,8192]{1,0:T(8,128)(2,1)S(1)}, bf16[128,8192]{1,0:T(8,128)(2,1)}, u32[]{:S(2)}) copy-start(bf16[128,8192]{1,0:T(8,128)(2,1)} %hidden_ref) | copy-start | bytes 6291460
  4.3 1.9 %copy-start.1 = (s32[128,1]{0,1:T(1,128)S(1)}, s32[128,1]{0,1:T(1,128)}, u32[]{:S(2)}) copy-start(s32[128,1]{0,1:T(1,128)} %param.4) | copy-start | bytes 1540
  4.3 10.7 %collective-permute-start.3 = (bf16[128,1024]{1,0:T(8,128)(2,1)S(1)}, bf16[128,1024]{1,0:T(8,128)(2,1)S(1)}, u32[]{:S(2)}, u32[]{:S(2)}) collective-permute-start(bf16[128,1024]{1,0:T(8,128)(2,1)S(1)} %join_blocks.5.refs_0_), channel_id=1, source_target_pairs={{0,4},{4,8},{8,12},{12,0},{1,5},{5,9},{9,13},{13,1},{2,6},{6,10},{... | collective-permute-start | bytes 786440 | tf_op jit(solution)/shard_map/ppermute | solution.py:31
  7.8 44.2 %all-to-all-start = ((bf16[8,136,1024]{2,1,0:T(8,128)(2,1)}), bf16[8,136,1024]{2,1,0:T(8,128)(2,1)S(1)}, u32[]{:S(2)}, u32[]{:S(2)}) async-start(bf16[8,136,1024]{2,1,0:T(8,128)(2,1)} %outgoing_rows.1), calls=%async_computation | async-start | bytes 4456448 | tf_op jit(solution)/shard_map/all_to_all | solution.py:39
  11.6 11.0 %collective-permute-start.4 = (bf16[128,1024]{1,0:T(8,128)(2,1)S(1)}, bf16[128,1024]{1,0:T(8,128)(2,1)S(1)}, u32[]{:S(2)}, u32[]{:S(2)}) collective-permute-start(bf16[128,1024]{1,0:T(8,128)(2,1)S(1)} %join_blocks.6.refs_1_), channel_id=1, source_target_pairs={{0,4},{4,8},{8,12},{12,0},{1,5},{5,9},{9,13},{13,1},{2,6},{6,10},{... | collective-permute-start | bytes 786440 | tf_op jit(solution)/shard_map/ppermute | solution.py:31
  15.0 13.1 %copy-start.6 = (bf16[1,64,8192]{2,1,0:T(8,128)(2,1)S(1)}, bf16[1,64,8192]{2,1,0:T(8,128)(2,1)}, u32[]{:S(2)}) copy-start(bf16[1,64,8192]{2,1,0:T(8,128)(2,1)} %param.7) | copy-start | bytes 3145732
  15.1 13.1 %collective-permute-start.5 = (bf16[128,1024]{1,0:T(8,128)(2,1)S(1)}, bf16[128,1024]{1,0:T(8,128)(2,1)S(1)}, u32[]{:S(2)}, u32[]{:S(2)}) collective-permute-start(bf16[128,1024]{1,0:T(8,128)(2,1)S(1)} %join_blocks.7), channel_id=1, source_target_pairs={{0,4},{4,8},{8,12},{12,0},{1,5},{5,9},{9,13},{13,1},{2,6},{6,10},{... | collective-permute-start | bytes 786440 | tf_op jit(solution)/shard_map/ppermute | solution.py:31
  23.3 11.4 %collective-permute-start.6 = (bf16[128,1024]{1,0:T(8,128)(2,1)}, bf16[128,1024]{1,0:T(8,128)(2,1)}, u32[]{:S(2)}, u32[]{:S(2)}) collective-permute-start(bf16[128,1024]{1,0:T(8,128)(2,1)} %join_blocks.8), channel_id=1, source_target_pairs={{0,4},{4,8},{8,12},{12,0},{1,5},{5,9},{9,13},{13,1},{2,6},{6,10},{... | collective-permute-start | bytes 786440 | tf_op jit(solution)/shard_map/ppermute | solution.py:31
  28.2 17.9 %copy-start.4 = (bf16[128,1024]{1,0:T(8,128)(2,1)}, bf16[128,1024]{1,0:T(8,128)(2,1)S(1)}, u32[]{:S(2)}) copy-start(bf16[128,1024]{1,0:T(8,128)(2,1)S(1)} %collective-permute-done.5.refs_4_) | copy-start | bytes 786436
  28.2 12.1 %collective-permute-start.7 = (bf16[128,1024]{1,0:T(8,128)(2,1)S(1)}, bf16[128,1024]{1,0:T(8,128)(2,1)}, u32[]{:S(2)}, u32[]{:S(2)}) collective-permute-start(bf16[128,1024]{1,0:T(8,128)(2,1)S(1)} %collective-permute-done.5.refs_4_), channel_id=1, source_target_pairs={{0,4},{4,8},{8,12},{12,0},{1,5},{5,9},{9,13},{13,1},{2,6},{6,10},{... | collective-permute-start | bytes 786440 | tf_op jit(solution)/shard_map/ppermute | solution.py:31
  29.0 5.7 %collective-permute-start.9 = (bf16[64,1024]{1,0:T(8,128)(2,1)S(1)}, bf16[64,1024]{1,0:T(8,128)(2,1)}, u32[]{:S(2)}, u32[]{:S(2)}) collective-permute-start(bf16[64,1024]{1,0:T(8,128)(2,1)S(1)} %get-tuple-element.28), channel_id=1, source_target_pairs={{0,1},{1,0},{2,3},{3,2},{4,5},{5,4},{6,7},{7,6},{8,9},{9,8},{10,11... | collective-permute-start | bytes 393224 | tf_op jit(solution)/shard_map/ppermute | solution.py:27
  29.0 13.0 %collective-permute-start.10 = (bf16[64,1024]{1,0:T(8,128)(2,1)}, bf16[64,1024]{1,0:T(8,128)(2,1)}, u32[]{:S(2)}, u32[]{:S(2)}) collective-permute-start(bf16[64,1024]{1,0:T(8,128)(2,1)} %get-tuple-element.30), channel_id=1, source_target_pairs={{0,2},{1,3},{2,0},{3,1},{4,6},{5,7},{6,4},{7,5},{8,10},{9,11},{10,... | collective-permute-start | bytes 393224 | tf_op jit(solution)/shard_map/ppermute | solution.py:27
  31.2 14.9 %collective-permute-start.11 = (bf16[64,1024]{1,0:T(8,128)(2,1)}, bf16[64,1024]{1,0:T(8,128)(2,1)}, u32[]{:S(2)}, u32[]{:S(2)}) collective-permute-start(bf16[64,1024]{1,0:T(8,128)(2,1)} %get-tuple-element.32), channel_id=1, source_target_pairs={{0,3},{1,2},{2,1},{3,0},{4,7},{5,6},{6,5},{7,4},{8,11},{9,10},{10,... | collective-permute-start | bytes 393224 | tf_op jit(solution)/shard_map/ppermute | solution.py:27
  34.7 11.4 %collective-permute-start.8 = (bf16[128,1024]{1,0:T(8,128)(2,1)}, bf16[128,1024]{1,0:T(8,128)(2,1)}, u32[]{:S(2)}, u32[]{:S(2)}) collective-permute-start(bf16[128,1024]{1,0:T(8,128)(2,1)} %collective-permute-done.6.refs_5_), channel_id=1, source_target_pairs={{0,4},{4,8},{8,12},{12,0},{1,5},{5,9},{9,13},{13,1},{2,6},{6,10},{... | collective-permute-start | bytes 786440 | tf_op jit(solution)/shard_map/ppermute | solution.py:31
  40.3 10.0 %collective-permute-start.12 = (bf16[128,1024]{1,0:T(8,128)(2,1)S(1)}, bf16[128,1024]{1,0:T(8,128)(2,1)}, u32[]{:S(2)}, u32[]{:S(2)}) collective-permute-start(bf16[128,1024]{1,0:T(8,128)(2,1)S(1)} %pad_maximum_fusion.refs_0_), channel_id=1, source_target_pairs={{0,4},{4,8},{8,12},{12,0},{1,5},{5,9},{9,13},{13,1},{2,6},{6,10},{... | collective-permute-start | bytes 786440 | tf_op jit(solution)/shard_map/ppermute | solution.py:31
  47.9 10.3 %collective-permute-start.13 = (bf16[128,1024]{1,0:T(8,128)(2,1)S(1)}, bf16[128,1024]{1,0:T(8,128)(2,1)}, u32[]{:S(2)}, u32[]{:S(2)}) collective-permute-start(bf16[128,1024]{1,0:T(8,128)(2,1)S(1)} %constant_dynamic-update-slice_fusion.refs_1_), channel_id=1, source_target_pairs={{0,4},{4,8},{8,12},{12,0},{1,5},{5,9},{9,13},{13,1},{2,6},{6,10},{... | collective-permute-start | bytes 786440 | tf_op jit(solution)/shard_map/ppermute | solution.py:31
  52.0 11.9 %collective-permute-start.14 = (bf16[128,1024]{1,0:T(8,128)(2,1)}, bf16[128,1024]{1,0:T(8,128)(2,1)}, u32[]{:S(2)}, u32[]{:S(2)}) collective-permute-start(bf16[128,1024]{1,0:T(8,128)(2,1)} %join_blocks.9), channel_id=1, source_target_pairs={{0,4},{4,8},{8,12},{12,0},{1,5},{5,9},{9,13},{13,1},{2,6},{6,10},{... | collective-permute-start | bytes 786440 | tf_op jit(solution)/shard_map/ppermute | solution.py:31
  58.2 9.4 %collective-permute-start.15 = (bf16[128,1024]{1,0:T(8,128)(2,1)}, bf16[128,1024]{1,0:T(8,128)(2,1)S(1)}, u32[]{:S(2)}, u32[]{:S(2)}) collective-permute-start(bf16[128,1024]{1,0:T(8,128)(2,1)} %collective-permute-done.13.refs_3_), channel_id=1, source_target_pairs={{0,4},{4,8},{8,12},{12,0},{1,5},{5,9},{9,13},{13,1},{2,6},{6,10},{... | collective-permute-start | bytes 786440 | tf_op jit(solution)/shard_map/ppermute | solution.py:31
  59.5 10.4 %all-to-all-start.1 = ((f32[8,64,128]{2,1,0:T(8,128)}), f32[8,64,128]{2,1,0:T(8,128)S(1)}, u32[]{:S(2)}, u32[]{:S(2)}) async-start(f32[8,64,128]{2,1,0:T(8,128)} %get-tuple-element.26), calls=%async_computation.1 | async-start | bytes 524288 | tf_op jit(solution)/shard_map/all_to_all | solution.py:39
  63.9 11.2 %collective-permute-start.16 = (bf16[128,1024]{1,0:T(8,128)(2,1)}, bf16[128,1024]{1,0:T(8,128)(2,1)S(1)}, u32[]{:S(2)}, u32[]{:S(2)}) collective-permute-start(bf16[128,1024]{1,0:T(8,128)(2,1)} %collective-permute-done.14.refs_4_), channel_id=1, source_target_pairs={{0,4},{4,8},{8,12},{12,0},{1,5},{5,9},{9,13},{13,1},{2,6},{6,10},{... | collective-permute-start | bytes 786440 | tf_op jit(solution)/shard_map/ppermute | solution.py:31
  67.6 12.6 %collective-permute-start.17 = (bf16[128,1024]{1,0:T(8,128)(2,1)S(1)}, bf16[128,1024]{1,0:T(8,128)(2,1)S(1)}, u32[]{:S(2)}, u32[]{:S(2)}) collective-permute-start(bf16[128,1024]{1,0:T(8,128)(2,1)S(1)} %collective-permute-done.15.refs_5_), channel_id=1, source_target_pairs={{0,4},{4,8},{8,12},{12,0},{1,5},{5,9},{9,13},{13,1},{2,6},{6,10},{... | collective-permute-start | bytes 786440 | tf_op jit(solution)/shard_map/ppermute | solution.py:31
  70.6 8.5 %all-to-all-start.2 = ((bf16[8,64,128]{2,1,0:T(8,128)(2,1)}), bf16[8,64,128]{2,1,0:T(8,128)(2,1)S(1)}, u32[]{:S(2)}, u32[]{:S(2)}) async-start(bf16[8,64,128]{2,1,0:T(8,128)(2,1)} %summed_copies.1), calls=%async_computation.2 | async-start | bytes 262144 | tf_op jit(solution)/shard_map/all_to_all | solution.py:39
  82.8 10.2 %collective-permute-start.18 = (bf16[128,1024]{1,0:T(8,128)(2,1)S(1)}, bf16[128,1024]{1,0:T(8,128)(2,1)S(1)}, u32[]{:S(2)}, u32[]{:S(2)}) collective-permute-start(bf16[128,1024]{1,0:T(8,128)(2,1)S(1)} %get-tuple-element.35), channel_id=1, source_target_pairs={{0,18},{1,19},{2,16},{3,17},{16,2},{17,3},{18,0},{19,1},{4,22},{5,... | collective-permute-start | bytes 786440 | tf_op jit(solution)/shard_map/ppermute | solution.py:27
  85.4 12.4 %collective-permute-start.19 = (bf16[128,1024]{1,0:T(8,128)(2,1)S(1)}, bf16[128,1024]{1,0:T(8,128)(2,1)S(1)}, u32[]{:S(2)}, u32[]{:S(2)}) collective-permute-start(bf16[128,1024]{1,0:T(8,128)(2,1)S(1)} %get-tuple-element.36), channel_id=1, source_target_pairs={{0,19},{1,18},{2,17},{3,16},{16,3},{17,2},{18,1},{19,0},{4,23},{5,... | collective-permute-start | bytes 786440 | tf_op jit(solution)/shard_map/ppermute | solution.py:27
  85.4 19.1 %collective-permute-start.20 = (bf16[128,1024]{1,0:T(8,128)(2,1)S(1)}, bf16[128,1024]{1,0:T(8,128)(2,1)S(1)}, u32[]{:S(2)}, u32[]{:S(2)}) collective-permute-start(bf16[128,1024]{1,0:T(8,128)(2,1)S(1)} %get-tuple-element.37), channel_id=1, source_target_pairs={{0,16},{1,17},{2,18},{3,19},{16,0},{17,1},{18,2},{19,3},{4,20},{5,... | collective-permute-start | bytes 786440 | tf_op jit(solution)/shard_map/ppermute | solution.py:27
  86.1 21.3 %collective-permute-start.21 = (bf16[128,1024]{1,0:T(8,128)(2,1)S(1)}, bf16[128,1024]{1,0:T(8,128)(2,1)S(1)}, u32[]{:S(2)}, u32[]{:S(2)}) collective-permute-start(bf16[128,1024]{1,0:T(8,128)(2,1)S(1)} %get-tuple-element.38), channel_id=1, source_target_pairs={{0,17},{1,16},{2,19},{3,18},{16,1},{17,0},{18,3},{19,2},{4,21},{5,... | collective-permute-start | bytes 786440 | tf_op jit(solution)/shard_map/ppermute | solution.py:27
  89.8 17.6 %collective-permute-start.22 = (bf16[128,1024]{1,0:T(8,128)(2,1)S(1)}, bf16[128,1024]{1,0:T(8,128)(2,1)S(1)}, u32[]{:S(2)}, u32[]{:S(2)}) collective-permute-start(bf16[128,1024]{1,0:T(8,128)(2,1)S(1)} %get-tuple-element.39), channel_id=1, source_target_pairs={{0,2},{1,3},{2,0},{3,1},{16,18},{17,19},{18,16},{19,17},{4,6},{5,7... | collective-permute-start | bytes 786440 | tf_op jit(solution)/shard_map/ppermute | solution.py:27
  93.0 15.4 %collective-permute-start.23 = (bf16[128,1024]{1,0:T(8,128)(2,1)S(1)}, bf16[128,1024]{1,0:T(8,128)(2,1)S(1)}, u32[]{:S(2)}, u32[]{:S(2)}) collective-permute-start(bf16[128,1024]{1,0:T(8,128)(2,1)S(1)} %get-tuple-element.40), channel_id=1, source_target_pairs={{0,3},{1,2},{2,1},{3,0},{16,19},{17,18},{18,17},{19,16},{4,7},{5,6... | collective-permute-start | bytes 786440 | tf_op jit(solution)/shard_map/ppermute | solution.py:27
  97.9 10.6 %collective-permute-start.24 = (bf16[128,1024]{1,0:T(8,128)(2,1)S(1)}, bf16[128,1024]{1,0:T(8,128)(2,1)S(1)}, u32[]{:S(2)}, u32[]{:S(2)}) collective-permute-start(bf16[128,1024]{1,0:T(8,128)(2,1)S(1)} %get-tuple-element.41), channel_id=1, source_target_pairs={{0,1},{1,0},{2,3},{3,2},{16,17},{17,16},{18,19},{19,18},{4,5},{5,4... | collective-permute-start | bytes 786440 | tf_op jit(solution)/shard_map/ppermute | solution.py:27
  (3 other events, 2.7 us)

commit v22 on v21

--- a/solution.py
+++ b/solution.py
@@ -1,4 +1,5 @@
 import functools
+import math
 
 import jax
 import jax.numpy as jnp
@@ -66,6 +67,23 @@
         cost_estimate=pl.CostEstimate(flops=cost, bytes_accessed=10**6, transcendentals=0),
         name="join_blocks",
     )(*blocks)
+
+
+def pass_kernel(block_ref, out_ref):
+    del block_ref, out_ref
+
+
+def passed(block, cost):
+    return pl.pallas_call(
+        pass_kernel,
+        out_shape=jax.ShapeDtypeStruct(block.shape, block.dtype),
+        in_specs=[ANYWHERE],
+        out_specs=ANYWHERE,
+        input_output_aliases={0: 0},
+        compiler_params=params(),
+        cost_estimate=pl.CostEstimate(flops=cost, bytes_accessed=10**6, transcendentals=0),
+        name="pass_block",
+    )(block)
 
 
 def outgoing_kernel(hidden_ref, ids_ref, out_ref, sems):
@@ -182,12 +200,16 @@
     )(terms)
 
 
+def rows_at_once(members):
+    return members if members <= BLOCK else math.gcd(BLOCK, members)
+
+
 def up_kernel(map_count, rank, offsets, labels_ref, me_ref, ids_ref, shrunk_ref, *refs):
     half, members = shrunk_ref.shape[1], len(offsets)
     maps, outs = refs[:map_count], refs[map_count : map_count + members]
     spread_ref = refs[-1]
     tok = 2 * half
-    block = min(BLOCK, members)
+    block = rows_at_once(members)
     tiles = spread_ref.shape[1] // LANES
     lane = lax.broadcasted_iota(jnp.int32, (half, LANES), 1)
     held = jnp.concatenate([m[...] for m in maps], axis=0)
@@ -219,8 +241,8 @@
         out_shape=[jax.ShapeDtypeStruct((tok, piece), jnp.bfloat16)] * members,
         in_specs=[IN_SMEM, IN_SMEM, IN_VMEM, IN_VMEM] + [IN_VMEM] * len(maps),
         out_specs=[IN_VMEM] * members,
-        scratch_shapes=[pltpu.VMEM((min(BLOCK, members) * tok, map_rows), jnp.bfloat16)],
-        compiler_params=params(2 * min(BLOCK, members) * tok * map_rows),
+        scratch_shapes=[pltpu.VMEM((rows_at_once(members) * tok, map_rows), jnp.bfloat16)],
+        compiler_params=params(2 * rows_at_once(members) * tok * map_rows),
         cost_estimate=pl.CostEstimate(
             flops=2 * map_rows * members * tok * piece,
             bytes_accessed=2 * piece * (map_rows + members * tok),
@@ -276,15 +298,14 @@
     def rings(near, far, near_cost, far_cost, far_second_after=()):
         near, far = [near], [far]
         for step in range(1, outer):
-            near_block, far_block = near[-1], far[-1]
             if step == 2:
-                far_block = after(far_block, *far_second_after)
                 if near_cost:
-                    near_block = joined([near_block], near_cost)
+                    near[-1] = passed(near[-1], near_cost)
                 if far_cost:
-                    far_block = joined([far_block], far_cost)
-            near.append(next_on_ring(near_block, outer))
-            far.append(next_on_ring(far_block, outer))
+                    far[-1] = passed(far[-1], far_cost)
+                far[-1] = after(far[-1], *far_second_after)
+            near.append(next_on_ring(near[-1], outer))
+            far.append(next_on_ring(far[-1], outer))
         return near, far
 
     steps_back = jnp.arange(outer, dtype=jnp.int32)[:, None]
@@ -304,7 +325,7 @@
     packed, id_rows = down_product(labels, rows, down_maps, rank)
     up_near, up_far = rings(
         after(jnp.concatenate(up[:middle], axis=0), down_near[-1]),
-        jnp.concatenate([after(block, down_far[-1]) for block in up[middle:]], axis=0),
+        joined([after(block, down_far[-1]) for block in up[middle:]], 0),
         SLIGHTLY_AHEAD,
         0,
         far_second_after=[packed],
@@ -313,7 +334,7 @@
     shrunk = swap(summed_copies(swap(packed)))
     offsets = sorted(range(1, members), key=lambda n: (-(n >= inner) - (n % inner >= 2), -(n >= inner), n)) + [0]
     results = []
-    for some in offsets[: members // 2], offsets[members // 2 :]:
+    for some in offsets[: members // 4], offsets[members // 4 :]:
         results += up_product(labels, me.reshape(1), id_rows, shrunk, up_maps, rank, some)
     returned = [to_partner(r, PLANE, members, n) for r, n in zip(results[:-1], offsets)]
     return place(me.reshape(1), offsets, returned + results[-1:])

time: 110 us -> 112 us (1.018)
  Pallas kernels: 15.5 us -> 11.8 us
  local copies, waits for them, and re-layouts: 5.84 us -> 9.43 us
  starting transfers between devices: 30.3 us -> 31.8 us
    ppermute x13, waiting for transfers between devices: 17.9 us -> 23.4 us  [to_partner(): return lax.ppermute(value, axes, [(i, i ^ offset) for i in range(size)])]
    unnamed x15 -> x34, local copies, waits for them, and re-layouts: 2.86 us -> 7.38 us
    ppermute x12, waiting for transfers between devices: 32.7 us -> 28.9 us  [next_on_ring(): lax.ppermute(block, 'outer', [(i, (i + 1) % outer) for i in range(outer)])]
    ppermute x12, starting transfers between devices: 6.52 us -> 9.21 us  [next_on_ring(): lax.ppermute(block, 'outer', [(i, (i + 1) % outer) for i in range(outer)])]
    pallas_call x5 -> x3, Pallas kernels: 2.49 us -> 0.06 us  [joined(): pl.pallas_call(join_kernel, out_shape=jax.ShapeDtypeStruct((len(blocks) *...]
    all_to_all x3, waiting for transfers between devices: 6.38 us -> 5.2 us  [swap(): return lax.all_to_all(value, PLANE, split_axis=0, concat_axis=0, tiled=True)]
  transfers between devices with their start and end apart: 28 -> 28, of which waited for: 18 -> 19; matrix products, arithmetic and copies ran while one was open for 3% -> 2% of each run, Pallas kernels for 11% -> 8%
where the time goes in v22:
time: 112 us
  waiting for transfers between devices  57.4 us (51%)
  starting transfers between devices  31.8 us (28%)
  Pallas kernels  11.8 us (11%)
  local copies, waits for them, and re-layouts  9.43 us (8%)
    ppermute x12, waiting for transfers between devices, next_on_ring(): lax.ppermute(block, 'outer', [(i, (i + 1) % outer) for i in range(outer)])  28.9 us
    ppermute x13, waiting for transfers between devices, to_partner(): return lax.ppermute(value, axes, [(i, i ^ offset) for i in range(size)])  23.4 us
    ppermute x13, starting transfers between devices, to_partner(): return lax.ppermute(value, axes, [(i, i ^ offset) for i in range(size)])  12.1 us
    all_to_all x3, starting transfers between devices, swap(): return lax.all_to_all(value, PLANE, split_axis=0, concat_axis=0, tiled=True)  10.5 us
    ppermute x12, starting transfers between devices, next_on_ring(): lax.ppermute(block, 'outer', [(i, (i + 1) % outer) for i in range(outer)])  9.21 us
    unnamed x34, local copies, waits for them, and re-layouts  7.38 us
    all_to_all x3, waiting for transfers between devices, swap(): return lax.all_to_all(value, PLANE, split_axis=0, concat_axis=0, tiled=True)  5.2 us
    pallas_call x1, Pallas kernels, down_product(): pl.pallas_call(functools.partial(down_kernel, len(maps), rank), out_shape...  4.1 us
  transfers between devices with their start and end apart: 28, of which 19 were waited for; matrix products, arithmetic and copies ran while one was open for 2% of the time, Pallas kernels for 8%

profile of v22, /device:TPU:0, one launch (start us, length us, event | category | flops | bytes accessed | tf_op | source)
XLA Modules:
  0.0 111.8 jit_solution(1667099191891209354)
XLA Ops:
  0.0 1.1 %dynamic-slice_bitcast_fusion.4 = (bf16[64,1024]{1,0:T(8,128)(2,1)S(1)}, bf16[64,1024]{1,0:T(8,128)(2,1)S(1)}, bf16[64,1024]{1,0:T(8,128)(2,1)S(1)}, bf16[64,1024]{1,0:T(8,128)(2,1)S(1)}) fusion(bf16[1,8192,64]{1,2,0:T(8,128)(2,1)} %param.6, s32[]{:T(128)S(6)} %select_n.32, s32[]{:T(128)S(6)} %select_n.30, s32[]{:T(128)S(6)} %select_n.29, s32[]{:T(128)S(6)} %select_n.31), kind=kLoop, calls=%fused_computation.5 | loop fusion | bytes 1048592 | tf_op jit(solution)/shard_map/dynamic_slice | solution.py:292
  1.7 2.6 %collective-permute-start.1 = (bf16[64,1024]{1,0:T(8,128)(2,1)S(1)}, bf16[64,1024]{1,0:T(8,128)(2,1)S(1)}, u32[]{:S(2)}, u32[]{:S(2)}) collective-permute-start(bf16[64,1024]{1,0:T(8,128)(2,1)S(1)} %get-tuple-element.50), channel_id=1, source_target_pairs={{0,2},{1,3},{2,0},{3,1},{4,6},{5,7},{6,4},{7,5},{8,10},{9,11},{10,... | collective-permute-start | bytes 393224 | tf_op jit(solution)/shard_map/ppermute | solution.py:28
  4.4 1.8 %collective-permute-start.3 = (bf16[128,1024]{1,0:T(8,128)(2,1)S(1)}, bf16[128,1024]{1,0:T(8,128)(2,1)S(1)}, u32[]{:S(2)}, u32[]{:S(2)}) collective-permute-start(bf16[128,1024]{1,0:T(8,128)(2,1)S(1)} %join_blocks.3.refs_0_), channel_id=1, source_target_pairs={{0,4},{4,8},{8,12},{12,0},{1,5},{5,9},{9,13},{13,1},{2,6},{6,10},{... | collective-permute-start | bytes 786440 | tf_op jit(solution)/shard_map/ppermute | solution.py:32
  6.2 1.6 %outgoing_rows.1 = bf16[8,136,1024]{2,1,0:T(8,128)(2,1)} custom-call(bf16[128,8192]{1,0:T(8,128)(2,1)S(1)} %copy-done, s32[1,128]{1,0:T(1,128)S(1)} %bitcast.26), custom_call_target="tpu_custom_call" | custom-call | tf_op jit(solution)/shard_map/outgoing_rows/pallas_call | solution.py:112
  7.9 3.8 %all-to-all-start = ((bf16[8,136,1024]{2,1,0:T(8,128)(2,1)}), bf16[8,136,1024]{2,1,0:T(8,128)(2,1)S(1)}, u32[]{:S(2)}, u32[]{:S(2)}) async-start(bf16[8,136,1024]{2,1,0:T(8,128)(2,1)} %outgoing_rows.1), calls=%async_computation | async-start | bytes 4456448 | tf_op jit(solution)/shard_map/all_to_all | solution.py:40
  11.7 1.6 %collective-permute-start.4 = (bf16[128,1024]{1,0:T(8,128)(2,1)S(1)}, bf16[128,1024]{1,0:T(8,128)(2,1)S(1)}, u32[]{:S(2)}, u32[]{:S(2)}) collective-permute-start(bf16[128,1024]{1,0:T(8,128)(2,1)S(1)} %join_blocks.4.refs_1_), channel_id=1, source_target_pairs={{0,4},{4,8},{8,12},{12,0},{1,5},{5,9},{9,13},{13,1},{2,6},{6,10},{... | collective-permute-start | bytes 786440 | tf_op jit(solution)/shard_map/ppermute | solution.py:32
  13.3 1.7 %collective-permute-done.3.block_ref = bf16[128,1024]{1,0:T(8,128)(2,1)S(1)} collective-permute-done((bf16[128,1024]{1,0:T(8,128)(2,1)S(1)}, bf16[128,1024]{1,0:T(8,128)(2,1)S(1)}, u32[]{:S(2)}, u32[]{:S(2)}) %collective-permute-start.3) | collective-permute-done | bytes 262176 | tf_op jit(solution)/shard_map/ppermute | solution.py:32
  15.1 7.5 %collective-permute-done.4.block_ref = bf16[128,1024]{1,0:T(8,128)(2,1)S(1)} collective-permute-done((bf16[128,1024]{1,0:T(8,128)(2,1)S(1)}, bf16[128,1024]{1,0:T(8,128)(2,1)S(1)}, u32[]{:S(2)}, u32[]{:S(2)}) %collective-permute-start.4) | collective-permute-done | bytes 262176 | tf_op jit(solution)/shard_map/ppermute | solution.py:32
  22.6 5.6 %collective-permute-done.5.refs_4_ = bf16[128,1024]{1,0:T(8,128)(2,1)S(1)} collective-permute-done((bf16[128,1024]{1,0:T(8,128)(2,1)S(1)}, bf16[128,1024]{1,0:T(8,128)(2,1)S(1)}, u32[]{:S(2)}, u32[]{:S(2)}) %collective-permute-start.5) | collective-permute-done | bytes 262176 | tf_op jit(solution)/shard_map/ppermute | solution.py:32
  29.1 1.5 %collective-permute-done.9 = bf16[64,1024]{1,0:T(8,128)(2,1)} collective-permute-done((bf16[64,1024]{1,0:T(8,128)(2,1)S(1)}, bf16[64,1024]{1,0:T(8,128)(2,1)}, u32[]{:S(2)}, u32[]{:S(2)}) %collective-permute-start.9) | collective-permute-done | bytes 131104 | tf_op jit(solution)/shard_map/ppermute | solution.py:28
  31.5 2.3 %collective-permute-done.6.refs_5_ = bf16[128,1024]{1,0:T(8,128)(2,1)S(1)} collective-permute-done((bf16[128,1024]{1,0:T(8,128)(2,1)S(1)}, bf16[128,1024]{1,0:T(8,128)(2,1)S(1)}, u32[]{:S(2)}, u32[]{:S(2)}) %collective-permute-start.6) | collective-permute-done | bytes 262176 | tf_op jit(solution)/shard_map/ppermute | solution.py:32
  33.8 5.6 %collective-permute-done.7.refs_6_ = bf16[128,1024]{1,0:T(8,128)(2,1)S(1)} collective-permute-done((bf16[128,1024]{1,0:T(8,128)(2,1)S(1)}, bf16[128,1024]{1,0:T(8,128)(2,1)S(1)}, u32[]{:S(2)}, u32[]{:S(2)}) %collective-permute-start.7) | collective-permute-done | bytes 262176 | tf_op jit(solution)/shard_map/ppermute | solution.py:32
  40.2 2.1 %collective-permute-start.10 = (bf16[64,1024]{1,0:T(8,128)(2,1)}, bf16[64,1024]{1,0:T(8,128)(2,1)S(1)}, u32[]{:S(2)}, u32[]{:S(2)}) collective-permute-start(bf16[64,1024]{1,0:T(8,128)(2,1)} %get-tuple-element.30), channel_id=1, source_target_pairs={{0,2},{1,3},{2,0},{3,1},{4,6},{5,7},{6,4},{7,5},{8,10},{9,11},{10,... | collective-permute-start | bytes 393224 | tf_op jit(solution)/shard_map/ppermute | solution.py:28
  42.5 3.6 %collective-permute-done.10.refs_0_ = bf16[64,1024]{1,0:T(8,128)(2,1)S(1)} collective-permute-done((bf16[64,1024]{1,0:T(8,128)(2,1)}, bf16[64,1024]{1,0:T(8,128)(2,1)S(1)}, u32[]{:S(2)}, u32[]{:S(2)}) %collective-permute-start.10) | collective-permute-done | bytes 131104 | tf_op jit(solution)/shard_map/ppermute | solution.py:28
  46.0 2.2 %collective-permute-done.11.refs_1_ = bf16[64,1024]{1,0:T(8,128)(2,1)S(1)} collective-permute-done((bf16[64,1024]{1,0:T(8,128)(2,1)}, bf16[64,1024]{1,0:T(8,128)(2,1)S(1)}, u32[]{:S(2)}, u32[]{:S(2)}) %collective-permute-start.11) | collective-permute-done | bytes 131104 | tf_op jit(solution)/shard_map/ppermute | solution.py:28
  48.3 1.4 %collective-permute-start.13 = (bf16[128,1024]{1,0:T(8,128)(2,1)S(1)}, bf16[128,1024]{1,0:T(8,128)(2,1)S(1)}, u32[]{:S(2)}, u32[]{:S(2)}) collective-permute-start(bf16[128,1024]{1,0:T(8,128)(2,1)S(1)} %join_blocks.5.refs_1_), channel_id=1, source_target_pairs={{0,4},{4,8},{8,12},{12,0},{1,5},{5,9},{9,13},{13,1},{2,6},{6,10},{... | collective-permute-start | bytes 786440 | tf_op jit(solution)/shard_map/ppermute | solution.py:32
  57.9 4.1 %down_product.1 = (f32[8,64,128]{2,1,0:T(8,128)}, f32[8,128]{1,0:T(8,128)S(1)}) custom-call(s32[16]{0:T(128)S(1)} %add.61.labels_ref, bf16[8,136,1024]{2,1,0:T(8,128)(2,1)S(1)} %all-to-all-done.rows_ref, bf16[128,1024]{1,0:T(8,128)(2,1)S(1)} %copy-done.3, bf16[128,1024]{1,0:T(8,128)(2,1)S(1)} %copy-done.5, bf16[128,1024]{1,0:T(8,128)(2,1)S(1)} %copy-done.13, ...), custom_call_target="tpu_custom_call" | custom-call | flops 2147483648 | bytes 4194304 | tf_op jit(solution)/shard_map/down_product/pallas_call | solution.py:164
  62.0 2.0 %collective-permute-start.15 = (bf16[128,1024]{1,0:T(8,128)(2,1)S(1)}, bf16[128,1024]{1,0:T(8,128)(2,1)S(1)}, u32[]{:S(2)}, u32[]{:S(2)}) collective-permute-start(bf16[128,1024]{1,0:T(8,128)(2,1)S(1)} %collective-permute-done.13.refs_3_), channel_id=1, source_target_pairs={{0,4},{4,8},{8,12},{12,0},{1,5},{5,9},{9,13},{13,1},{2,6},{6,10},{... | collective-permute-start | bytes 786440 | tf_op jit(solution)/shard_map/ppermute | solution.py:32
  64.1 3.4 %all-to-all-start.1 = ((f32[8,64,128]{2,1,0:T(8,128)}), f32[8,64,128]{2,1,0:T(8,128)S(1)}, u32[]{:S(2)}, u32[]{:S(2)}) async-start(f32[8,64,128]{2,1,0:T(8,128)} %get-tuple-element.26), calls=%async_computation.1 | async-start | bytes 524288 | tf_op jit(solution)/shard_map/all_to_all | solution.py:40
  67.9 3.6 %collective-permute-done.15.refs_5_ = bf16[128,1024]{1,0:T(8,128)(2,1)S(1)} collective-permute-done((bf16[128,1024]{1,0:T(8,128)(2,1)S(1)}, bf16[128,1024]{1,0:T(8,128)(2,1)S(1)}, u32[]{:S(2)}, u32[]{:S(2)}) %collective-permute-start.15) | collective-permute-done | bytes 262176 | tf_op jit(solution)/shard_map/ppermute | solution.py:32
  74.1 3.4 %all-to-all-start.2 = ((bf16[8,64,128]{2,1,0:T(8,128)(2,1)}), bf16[8,64,128]{2,1,0:T(8,128)(2,1)S(1)}, u32[]{:S(2)}, u32[]{:S(2)}) async-start(bf16[8,64,128]{2,1,0:T(8,128)(2,1)} %summed_copies.1), calls=%async_computation.2 | async-start | bytes 262144 | tf_op jit(solution)/shard_map/all_to_all | solution.py:40
  78.5 4.2 %all-to-all-done.2.shrunk_ref = bf16[8,64,128]{2,1,0:T(8,128)(2,1)S(1)} async-done(((bf16[8,64,128]{2,1,0:T(8,128)(2,1)}), bf16[8,64,128]{2,1,0:T(8,128)(2,1)S(1)}, u32[]{:S(2)}, u32[]{:S(2)}) %all-to-all-start.2) | async-done | bytes 131104 | tf_op jit(solution)/shard_map/all_to_all | solution.py:40
  83.5 1.4 %up_product.2 = (bf16[128,1024]{1,0:T(8,128)(2,1)S(1)}, bf16[128,1024]{1,0:T(8,128)(2,1)S(1)}) custom-call(s32[16]{0:T(128)S(1)} %add.61.labels_ref, s32[1]{0:T(128)} %bitcast.me_ref, f32[8,128]{1,0:T(8,128)S(1)} %get-tuple-element.25.ids_ref, bf16[8,64,128]{2,1,0:T(8,128)(2,1)S(1)} %all-to-all-done.2.shrunk_ref, ...), custom_call_target="tpu_custom_call" | custom-call | flops 536870912 | bytes 2621440 | tf_op jit(solution)/shard_map/up_product/pallas_call | solution.py:239
  84.9 2.7 %collective-permute-start.18 = (bf16[128,1024]{1,0:T(8,128)(2,1)S(1)}, bf16[128,1024]{1,0:T(8,128)(2,1)S(1)}, u32[]{:S(2)}, u32[]{:S(2)}) collective-permute-start(bf16[128,1024]{1,0:T(8,128)(2,1)S(1)} %get-tuple-element.35), channel_id=1, source_target_pairs={{0,18},{1,19},{2,16},{3,17},{16,2},{17,3},{18,0},{19,1},{4,22},{5,... | collective-permute-start | bytes 786440 | tf_op jit(solution)/shard_map/ppermute | solution.py:28
  87.6 2.6 %up_product.3 = (bf16[128,1024]{1,0:T(8,128)(2,1)S(1)}, bf16[128,1024]{1,0:T(8,128)(2,1)S(1)}, bf16[128,1024]{1,0:T(8,128)(2,1)S(1)}, bf16[128,1024]{1,0:T(8,128...) custom-call(s32[16]{0:T(128)S(1)} %add.61.labels_ref, s32[1]{0:T(128)} %bitcast.me_ref, ...), custom_call_target="tpu_custom_call" | custom-call | flops 1610612736 | bytes 3670016 | tf_op jit(solution)/shard_map/up_product/pallas_call | solution.py:239
  90.9 1.2 %collective-permute-start.21 = (bf16[128,1024]{1,0:T(8,128)(2,1)S(1)}, bf16[128,1024]{1,0:T(8,128)(2,1)S(1)}, u32[]{:S(2)}, u32[]{:S(2)}) collective-permute-start(bf16[128,1024]{1,0:T(8,128)(2,1)S(1)} %get-tuple-element.38), channel_id=1, source_target_pairs={{0,17},{1,16},{2,19},{3,18},{16,1},{17,0},{18,3},{19,2},{4,21},{5,... | collective-permute-start | bytes 786440 | tf_op jit(solution)/shard_map/ppermute | solution.py:28
  92.1 1.7 %collective-permute-start.22 = (bf16[128,1024]{1,0:T(8,128)(2,1)S(1)}, bf16[128,1024]{1,0:T(8,128)(2,1)S(1)}, u32[]{:S(2)}, u32[]{:S(2)}) collective-permute-start(bf16[128,1024]{1,0:T(8,128)(2,1)S(1)} %get-tuple-element.39), channel_id=1, source_target_pairs={{0,2},{1,3},{2,0},{3,1},{16,18},{17,19},{18,16},{19,17},{4,6},{5,7... | collective-permute-start | bytes 786440 | tf_op jit(solution)/shard_map/ppermute | solution.py:28
  93.7 1.4 %collective-permute-done.18.refs_0_ = bf16[128,1024]{1,0:T(8,128)(2,1)S(1)} collective-permute-done((bf16[128,1024]{1,0:T(8,128)(2,1)S(1)}, bf16[128,1024]{1,0:T(8,128)(2,1)S(1)}, u32[]{:S(2)}, u32[]{:S(2)}) %collective-permute-start.18) | collective-permute-done | bytes 262176 | tf_op jit(solution)/shard_map/ppermute | solution.py:28
  95.1 4.9 %collective-permute-done.19.refs_1_ = bf16[128,1024]{1,0:T(8,128)(2,1)S(1)} collective-permute-done((bf16[128,1024]{1,0:T(8,128)(2,1)S(1)}, bf16[128,1024]{1,0:T(8,128)(2,1)S(1)}, u32[]{:S(2)}, u32[]{:S(2)}) %collective-permute-start.19) | collective-permute-done | bytes 262176 | tf_op jit(solution)/shard_map/ppermute | solution.py:28
  100.6 6.0 %collective-permute-done.20.refs_2_ = bf16[128,1024]{1,0:T(8,128)(2,1)S(1)} collective-permute-done((bf16[128,1024]{1,0:T(8,128)(2,1)S(1)}, bf16[128,1024]{1,0:T(8,128)(2,1)S(1)}, u32[]{:S(2)}, u32[]{:S(2)}) %collective-permute-start.20) | collective-permute-done | bytes 262176 | tf_op jit(solution)/shard_map/ppermute | solution.py:28
  106.6 2.9 %collective-permute-done.21.refs_3_ = bf16[128,1024]{1,0:T(8,128)(2,1)S(1)} collective-permute-done((bf16[128,1024]{1,0:T(8,128)(2,1)S(1)}, bf16[128,1024]{1,0:T(8,128)(2,1)S(1)}, u32[]{:S(2)}, u32[]{:S(2)}) %collective-permute-start.21) | collective-permute-done | bytes 262176 | tf_op jit(solution)/shard_map/ppermute | solution.py:28
  110.4 1.4 %place_results.1 = bf16[128,8192]{1,0:T(8,128)(2,1)} custom-call(s32[1]{0:T(128)} %bitcast.me_ref, bf16[128,1024]{1,0:T(8,128)(2,1)S(1)} %collective-permute-done.18.refs_0_, bf16[128,1024]{1,0:T(8,128)(2,1)S(1)} %collective-permute-done.19.refs_1_, bf16[128,1024]{1,0:T(8,128)(2,1)S(1)} %collective-permute-done.20.refs_2_, ...), custom_call_target="tpu_custom_call" | custom-call | tf_op jit(solution)/shard_map/place_results/pallas_call | solution.py:270
  (76 shorter events, 18.8 us)
Async XLA Ops:
  1.1 3.2 %collective-permute-start = (bf16[64,1024]{1,0:T(8,128)(2,1)S(1)}, bf16[64,1024]{1,0:T(8,128)(2,1)S(1)}, u32[]{:S(2)}, u32[]{:S(2)}) collective-permute-start(bf16[64,1024]{1,0:T(8,128)(2,1)S(1)} %get-tuple-element.48), channel_id=1, source_target_pairs={{0,1},{1,0},{2,3},{3,2},{4,5},{5,4},{6,7},{7,6},{8,9},{9,8},{10,11... | collective-permute-start | bytes 393224 | tf_op jit(solution)/shard_map/ppermute | solution.py:28
  1.7 10.0 %collective-permute-start.1 = (bf16[64,1024]{1,0:T(8,128)(2,1)S(1)}, bf16[64,1024]{1,0:T(8,128)(2,1)S(1)}, u32[]{:S(2)}, u32[]{:S(2)}) collective-permute-start(bf16[64,1024]{1,0:T(8,128)(2,1)S(1)} %get-tuple-element.50), channel_id=1, source_target_pairs={{0,2},{1,3},{2,0},{3,1},{4,6},{5,7},{6,4},{7,5},{8,10},{9,11},{10,... | collective-permute-start | bytes 393224 | tf_op jit(solution)/shard_map/ppermute | solution.py:28
  4.2 7.4 %collective-permute-start.2 = (bf16[64,1024]{1,0:T(8,128)(2,1)S(1)}, bf16[64,1024]{1,0:T(8,128)(2,1)S(1)}, u32[]{:S(2)}, u32[]{:S(2)}) collective-permute-start(bf16[64,1024]{1,0:T(8,128)(2,1)S(1)} %get-tuple-element.47), channel_id=1, source_target_pairs={{0,3},{1,2},{2,1},{3,0},{4,7},{5,6},{6,5},{7,4},{8,11},{9,10},{10,... | collective-permute-start | bytes 393224 | tf_op jit(solution)/shard_map/ppermute | solution.py:28
  4.4 10.7 %collective-permute-start.3 = (bf16[128,1024]{1,0:T(8,128)(2,1)S(1)}, bf16[128,1024]{1,0:T(8,128)(2,1)S(1)}, u32[]{:S(2)}, u32[]{:S(2)}) collective-permute-start(bf16[128,1024]{1,0:T(8,128)(2,1)S(1)} %join_blocks.3.refs_0_), channel_id=1, source_target_pairs={{0,4},{4,8},{8,12},{12,0},{1,5},{5,9},{9,13},{13,1},{2,6},{6,10},{... | collective-permute-start | bytes 786440 | tf_op jit(solution)/shard_map/ppermute | solution.py:32
  7.9 43.4 %all-to-all-start = ((bf16[8,136,1024]{2,1,0:T(8,128)(2,1)}), bf16[8,136,1024]{2,1,0:T(8,128)(2,1)S(1)}, u32[]{:S(2)}, u32[]{:S(2)}) async-start(bf16[8,136,1024]{2,1,0:T(8,128)(2,1)} %outgoing_rows.1), calls=%async_computation | async-start | bytes 4456448 | tf_op jit(solution)/shard_map/all_to_all | solution.py:40
  11.7 10.9 %collective-permute-start.4 = (bf16[128,1024]{1,0:T(8,128)(2,1)S(1)}, bf16[128,1024]{1,0:T(8,128)(2,1)S(1)}, u32[]{:S(2)}, u32[]{:S(2)}) collective-permute-start(bf16[128,1024]{1,0:T(8,128)(2,1)S(1)} %join_blocks.4.refs_1_), channel_id=1, source_target_pairs={{0,4},{4,8},{8,12},{12,0},{1,5},{5,9},{9,13},{13,1},{2,6},{6,10},{... | collective-permute-start | bytes 786440 | tf_op jit(solution)/shard_map/ppermute | solution.py:32
  15.0 13.2 %copy-start.16 = (bf16[1,64,8192]{2,1,0:T(8,128)(2,1)S(1)}, bf16[1,64,8192]{2,1,0:T(8,128)(2,1)}, u32[]{:S(2)}) copy-start(bf16[1,64,8192]{2,1,0:T(8,128)(2,1)} %param.7) | copy-start | bytes 3145732
  15.0 13.2 %collective-permute-start.5 = (bf16[128,1024]{1,0:T(8,128)(2,1)S(1)}, bf16[128,1024]{1,0:T(8,128)(2,1)S(1)}, u32[]{:S(2)}, u32[]{:S(2)}) collective-permute-start(bf16[128,1024]{1,0:T(8,128)(2,1)S(1)} %pass_block.3.refs_2_), channel_id=1, source_target_pairs={{0,4},{4,8},{8,12},{12,0},{1,5},{5,9},{9,13},{13,1},{2,6},{6,10},{... | collective-permute-start | bytes 786440 | tf_op jit(solution)/shard_map/ppermute | solution.py:32
  22.6 11.2 %copy-start.14 = (bf16[128,1024]{1,0:T(8,128)(2,1)}, bf16[128,1024]{1,0:T(8,128)(2,1)S(1)}, u32[]{:S(2)}) copy-start(bf16[128,1024]{1,0:T(8,128)(2,1)S(1)} %pass_block.4.refs_3_) | copy-start | bytes 786436
  22.6 11.2 %collective-permute-start.6 = (bf16[128,1024]{1,0:T(8,128)(2,1)S(1)}, bf16[128,1024]{1,0:T(8,128)(2,1)S(1)}, u32[]{:S(2)}, u32[]{:S(2)}) collective-permute-start(bf16[128,1024]{1,0:T(8,128)(2,1)S(1)} %pass_block.4.refs_3_), channel_id=1, source_target_pairs={{0,4},{4,8},{8,12},{12,0},{1,5},{5,9},{9,13},{13,1},{2,6},{6,10},{... | collective-permute-start | bytes 786440 | tf_op jit(solution)/shard_map/ppermute | solution.py:32
  28.2 17.8 %copy-start.6 = (bf16[128,1024]{1,0:T(8,128)(2,1)}, bf16[128,1024]{1,0:T(8,128)(2,1)S(1)}, u32[]{:S(2)}) copy-start(bf16[128,1024]{1,0:T(8,128)(2,1)S(1)} %collective-permute-done.5.refs_4_) | copy-start | bytes 786436
  28.2 11.2 %collective-permute-start.7 = (bf16[128,1024]{1,0:T(8,128)(2,1)S(1)}, bf16[128,1024]{1,0:T(8,128)(2,1)S(1)}, u32[]{:S(2)}, u32[]{:S(2)}) collective-permute-start(bf16[128,1024]{1,0:T(8,128)(2,1)S(1)} %collective-permute-done.5.refs_4_), channel_id=1, source_target_pairs={{0,4},{4,8},{8,12},{12,0},{1,5},{5,9},{9,13},{13,1},{2,6},{6,10},{... | collective-permute-start | bytes 786440 | tf_op jit(solution)/shard_map/ppermute | solution.py:32
  29.1 1.5 %collective-permute-start.9 = (bf16[64,1024]{1,0:T(8,128)(2,1)S(1)}, bf16[64,1024]{1,0:T(8,128)(2,1)}, u32[]{:S(2)}, u32[]{:S(2)}) collective-permute-start(bf16[64,1024]{1,0:T(8,128)(2,1)S(1)} %get-tuple-element.28), channel_id=1, source_target_pairs={{0,1},{1,0},{2,3},{3,2},{4,5},{5,4},{6,7},{7,6},{8,9},{9,8},{10,11... | collective-permute-start | bytes 393224 | tf_op jit(solution)/shard_map/ppermute | solution.py:28
  33.8 16.5 %copy-start.8 = (bf16[128,1024]{1,0:T(8,128)(2,1)}, bf16[128,1024]{1,0:T(8,128)(2,1)S(1)}, u32[]{:S(2)}) copy-start(bf16[128,1024]{1,0:T(8,128)(2,1)S(1)} %collective-permute-done.6.refs_5_) | copy-start | bytes 786436
  33.8 12.2 %collective-permute-start.8 = (bf16[128,1024]{1,0:T(8,128)(2,1)S(1)}, bf16[128,1024]{1,0:T(8,128)(2,1)}, u32[]{:S(2)}, u32[]{:S(2)}) collective-permute-start(bf16[128,1024]{1,0:T(8,128)(2,1)S(1)} %collective-permute-done.6.refs_5_), channel_id=1, source_target_pairs={{0,4},{4,8},{8,12},{12,0},{1,5},{5,9},{9,13},{13,1},{2,6},{6,10},{... | collective-permute-start | bytes 786440 | tf_op jit(solution)/shard_map/ppermute | solution.py:32
  40.2 10.2 %collective-permute-start.12 = (bf16[128,1024]{1,0:T(8,128)(2,1)S(1)}, bf16[128,1024]{1,0:T(8,128)(2,1)S(1)}, u32[]{:S(2)}, u32[]{:S(2)}) collective-permute-start(bf16[128,1024]{1,0:T(8,128)(2,1)S(1)} %pad_maximum_fusion.refs_0_), channel_id=1, source_target_pairs={{0,4},{4,8},{8,12},{12,0},{1,5},{5,9},{9,13},{13,1},{2,6},{6,10},{... | collective-permute-start | bytes 786440 | tf_op jit(solution)/shard_map/ppermute | solution.py:32
  40.2 5.8 %collective-permute-start.10 = (bf16[64,1024]{1,0:T(8,128)(2,1)}, bf16[64,1024]{1,0:T(8,128)(2,1)S(1)}, u32[]{:S(2)}, u32[]{:S(2)}) collective-permute-start(bf16[64,1024]{1,0:T(8,128)(2,1)} %get-tuple-element.30), channel_id=1, source_target_pairs={{0,2},{1,3},{2,0},{3,1},{4,6},{5,7},{6,4},{7,5},{8,10},{9,11},{10,... | collective-permute-start | bytes 393224 | tf_op jit(solution)/shard_map/ppermute | solution.py:28
  42.3 6.0 %collective-permute-start.11 = (bf16[64,1024]{1,0:T(8,128)(2,1)}, bf16[64,1024]{1,0:T(8,128)(2,1)S(1)}, u32[]{:S(2)}, u32[]{:S(2)}) collective-permute-start(bf16[64,1024]{1,0:T(8,128)(2,1)} %get-tuple-element.32), channel_id=1, source_target_pairs={{0,3},{1,2},{2,1},{3,0},{4,7},{5,6},{6,5},{7,4},{8,11},{9,10},{10,... | collective-permute-start | bytes 393224 | tf_op jit(solution)/shard_map/ppermute | solution.py:28
  48.3 13.8 %collective-permute-start.13 = (bf16[128,1024]{1,0:T(8,128)(2,1)S(1)}, bf16[128,1024]{1,0:T(8,128)(2,1)S(1)}, u32[]{:S(2)}, u32[]{:S(2)}) collective-permute-start(bf16[128,1024]{1,0:T(8,128)(2,1)S(1)} %join_blocks.5.refs_1_), channel_id=1, source_target_pairs={{0,4},{4,8},{8,12},{12,0},{1,5},{5,9},{9,13},{13,1},{2,6},{6,10},{... | collective-permute-start | bytes 786440 | tf_op jit(solution)/shard_map/ppermute | solution.py:32
  50.4 17.1 %collective-permute-start.14 = (bf16[128,1024]{1,0:T(8,128)(2,1)S(1)}, bf16[128,1024]{1,0:T(8,128)(2,1)S(1)}, u32[]{:S(2)}, u32[]{:S(2)}) collective-permute-start(bf16[128,1024]{1,0:T(8,128)(2,1)S(1)} %pass_block.5.refs_2_), channel_id=1, source_target_pairs={{0,4},{4,8},{8,12},{12,0},{1,5},{5,9},{9,13},{13,1},{2,6},{6,10},{... | collective-permute-start | bytes 786440 | tf_op jit(solution)/shard_map/ppermute | solution.py:32
  62.0 9.5 %collective-permute-start.15 = (bf16[128,1024]{1,0:T(8,128)(2,1)S(1)}, bf16[128,1024]{1,0:T(8,128)(2,1)S(1)}, u32[]{:S(2)}, u32[]{:S(2)}) collective-permute-start(bf16[128,1024]{1,0:T(8,128)(2,1)S(1)} %collective-permute-done.13.refs_3_), channel_id=1, source_target_pairs={{0,4},{4,8},{8,12},{12,0},{1,5},{5,9},{9,13},{13,1},{2,6},{6,10},{... | collective-permute-start | bytes 786440 | tf_op jit(solution)/shard_map/ppermute | solution.py:32
  64.1 9.4 %all-to-all-start.1 = ((f32[8,64,128]{2,1,0:T(8,128)}), f32[8,64,128]{2,1,0:T(8,128)S(1)}, u32[]{:S(2)}, u32[]{:S(2)}) async-start(f32[8,64,128]{2,1,0:T(8,128)} %get-tuple-element.26), calls=%async_computation.1 | async-start | bytes 524288 | tf_op jit(solution)/shard_map/all_to_all | solution.py:40
  67.5 11.0 %collective-permute-start.16 = (bf16[128,1024]{1,0:T(8,128)(2,1)S(1)}, bf16[128,1024]{1,0:T(8,128)(2,1)S(1)}, u32[]{:S(2)}, u32[]{:S(2)}) collective-permute-start(bf16[128,1024]{1,0:T(8,128)(2,1)S(1)} %collective-permute-done.14.refs_4_), channel_id=1, source_target_pairs={{0,4},{4,8},{8,12},{12,0},{1,5},{5,9},{9,13},{13,1},{2,6},{6,10},{... | collective-permute-start | bytes 786440 | tf_op jit(solution)/shard_map/ppermute | solution.py:32
  71.5 12.0 %collective-permute-start.17 = (bf16[128,1024]{1,0:T(8,128)(2,1)S(1)}, bf16[128,1024]{1,0:T(8,128)(2,1)S(1)}, u32[]{:S(2)}, u32[]{:S(2)}) collective-permute-start(bf16[128,1024]{1,0:T(8,128)(2,1)S(1)} %collective-permute-done.15.refs_5_), channel_id=1, source_target_pairs={{0,4},{4,8},{8,12},{12,0},{1,5},{5,9},{9,13},{13,1},{2,6},{6,10},{... | collective-permute-start | bytes 786440 | tf_op jit(solution)/shard_map/ppermute | solution.py:32
  74.1 8.5 %all-to-all-start.2 = ((bf16[8,64,128]{2,1,0:T(8,128)(2,1)}), bf16[8,64,128]{2,1,0:T(8,128)(2,1)S(1)}, u32[]{:S(2)}, u32[]{:S(2)}) async-start(bf16[8,64,128]{2,1,0:T(8,128)(2,1)} %summed_copies.1), calls=%async_computation.2 | async-start | bytes 262144 | tf_op jit(solution)/shard_map/all_to_all | solution.py:40
  84.9 10.2 %collective-permute-start.18 = (bf16[128,1024]{1,0:T(8,128)(2,1)S(1)}, bf16[128,1024]{1,0:T(8,128)(2,1)S(1)}, u32[]{:S(2)}, u32[]{:S(2)}) collective-permute-start(bf16[128,1024]{1,0:T(8,128)(2,1)S(1)} %get-tuple-element.35), channel_id=1, source_target_pairs={{0,18},{1,19},{2,16},{3,17},{16,2},{17,3},{18,0},{19,1},{4,22},{5,... | collective-permute-start | bytes 786440 | tf_op jit(solution)/shard_map/ppermute | solution.py:28
  87.6 12.4 %collective-permute-start.19 = (bf16[128,1024]{1,0:T(8,128)(2,1)S(1)}, bf16[128,1024]{1,0:T(8,128)(2,1)S(1)}, u32[]{:S(2)}, u32[]{:S(2)}) collective-permute-start(bf16[128,1024]{1,0:T(8,128)(2,1)S(1)} %get-tuple-element.36), channel_id=1, source_target_pairs={{0,19},{1,18},{2,17},{3,16},{16,3},{17,2},{18,1},{19,0},{4,23},{5,... | collective-permute-start | bytes 786440 | tf_op jit(solution)/shard_map/ppermute | solution.py:28
  90.2 16.4 %collective-permute-start.20 = (bf16[128,1024]{1,0:T(8,128)(2,1)S(1)}, bf16[128,1024]{1,0:T(8,128)(2,1)S(1)}, u32[]{:S(2)}, u32[]{:S(2)}) collective-permute-start(bf16[128,1024]{1,0:T(8,128)(2,1)S(1)} %get-tuple-element.37), channel_id=1, source_target_pairs={{0,16},{1,17},{2,18},{3,19},{16,0},{17,1},{18,2},{19,3},{4,20},{5,... | collective-permute-start | bytes 786440 | tf_op jit(solution)/shard_map/ppermute | solution.py:28
  90.9 18.6 %collective-permute-start.21 = (bf16[128,1024]{1,0:T(8,128)(2,1)S(1)}, bf16[128,1024]{1,0:T(8,128)(2,1)S(1)}, u32[]{:S(2)}, u32[]{:S(2)}) collective-permute-start(bf16[128,1024]{1,0:T(8,128)(2,1)S(1)} %get-tuple-element.38), channel_id=1, source_target_pairs={{0,17},{1,16},{2,19},{3,18},{16,1},{17,0},{18,3},{19,2},{4,21},{5,... | collective-permute-start | bytes 786440 | tf_op jit(solution)/shard_map/ppermute | solution.py:28
  92.1 17.5 %collective-permute-start.22 = (bf16[128,1024]{1,0:T(8,128)(2,1)S(1)}, bf16[128,1024]{1,0:T(8,128)(2,1)S(1)}, u32[]{:S(2)}, u32[]{:S(2)}) collective-permute-start(bf16[128,1024]{1,0:T(8,128)(2,1)S(1)} %get-tuple-element.39), channel_id=1, source_target_pairs={{0,2},{1,3},{2,0},{3,1},{16,18},{17,19},{18,16},{19,17},{4,6},{5,7... | collective-permute-start | bytes 786440 | tf_op jit(solution)/shard_map/ppermute | solution.py:28
  95.1 15.3 %collective-permute-start.23 = (bf16[128,1024]{1,0:T(8,128)(2,1)S(1)}, bf16[128,1024]{1,0:T(8,128)(2,1)S(1)}, u32[]{:S(2)}, u32[]{:S(2)}) collective-permute-start(bf16[128,1024]{1,0:T(8,128)(2,1)S(1)} %get-tuple-element.40), channel_id=1, source_target_pairs={{0,3},{1,2},{2,1},{3,0},{16,19},{17,18},{18,17},{19,16},{4,7},{5,6... | collective-permute-start | bytes 786440 | tf_op jit(solution)/shard_map/ppermute | solution.py:28
  100.0 10.4 %collective-permute-start.24 = (bf16[128,1024]{1,0:T(8,128)(2,1)S(1)}, bf16[128,1024]{1,0:T(8,128)(2,1)S(1)}, u32[]{:S(2)}, u32[]{:S(2)}) collective-permute-start(bf16[128,1024]{1,0:T(8,128)(2,1)S(1)} %get-tuple-element.41), channel_id=1, source_target_pairs={{0,1},{1,0},{2,3},{3,2},{16,17},{17,16},{18,19},{19,18},{4,5},{5,4... | collective-permute-start | bytes 786440 | tf_op jit(solution)/shard_map/ppermute | solution.py:28
  (13 other events, 25.6 us)

commit v23 on v21

--- a/solution.py
+++ b/solution.py
@@ -1,4 +1,5 @@
 import functools
+import math
 
 import jax
 import jax.numpy as jnp
@@ -182,12 +183,16 @@
     )(terms)
 
 
+def rows_at_once(members):
+    return members if members <= BLOCK else math.gcd(BLOCK, members)
+
+
 def up_kernel(map_count, rank, offsets, labels_ref, me_ref, ids_ref, shrunk_ref, *refs):
     half, members = shrunk_ref.shape[1], len(offsets)
     maps, outs = refs[:map_count], refs[map_count : map_count + members]
     spread_ref = refs[-1]
     tok = 2 * half
-    block = min(BLOCK, members)
+    block = rows_at_once(members)
     tiles = spread_ref.shape[1] // LANES
     lane = lax.broadcasted_iota(jnp.int32, (half, LANES), 1)
     held = jnp.concatenate([m[...] for m in maps], axis=0)
@@ -219,8 +224,8 @@
         out_shape=[jax.ShapeDtypeStruct((tok, piece), jnp.bfloat16)] * members,
         in_specs=[IN_SMEM, IN_SMEM, IN_VMEM, IN_VMEM] + [IN_VMEM] * len(maps),
         out_specs=[IN_VMEM] * members,
-        scratch_shapes=[pltpu.VMEM((min(BLOCK, members) * tok, map_rows), jnp.bfloat16)],
-        compiler_params=params(2 * min(BLOCK, members) * tok * map_rows),
+        scratch_shapes=[pltpu.VMEM((rows_at_once(members) * tok, map_rows), jnp.bfloat16)],
+        compiler_params=params(2 * rows_at_once(members) * tok * map_rows),
         cost_estimate=pl.CostEstimate(
             flops=2 * map_rows * members * tok * piece,
             bytes_accessed=2 * piece * (map_rows + members * tok),
@@ -304,7 +309,7 @@
     packed, id_rows = down_product(labels, rows, down_maps, rank)
     up_near, up_far = rings(
         after(jnp.concatenate(up[:middle], axis=0), down_near[-1]),
-        jnp.concatenate([after(block, down_far[-1]) for block in up[middle:]], axis=0),
+        joined([after(block, down_far[-1]) for block in up[middle:]], SLIGHTLY_AHEAD),
         SLIGHTLY_AHEAD,
         0,
         far_second_after=[packed],
@@ -313,7 +318,7 @@
     shrunk = swap(summed_copies(swap(packed)))
     offsets = sorted(range(1, members), key=lambda n: (-(n >= inner) - (n % inner >= 2), -(n >= inner), n)) + [0]
     results = []
-    for some in offsets[: members // 2], offsets[members // 2 :]:
+    for some in offsets[: members // 4], offsets[members // 4 :]:
         results += up_product(labels, me.reshape(1), id_rows, shrunk, up_maps, rank, some)
     returned = [to_partner(r, PLANE, members, n) for r, n in zip(results[:-1], offsets)]
     return place(me.reshape(1), offsets, returned + results[-1:])

time: 110 us -> 117 us (1.064)
  local copies, waits for them, and re-layouts: 5.84 us -> 12.8 us
  Pallas kernels: 15.5 us -> 13.1 us
  starting transfers between devices: 30.3 us -> 31.9 us
    unnamed x15 -> x36, local copies, waits for them, and re-layouts: 2.86 us -> 9.68 us
    ppermute x12, starting transfers between devices: 6.52 us -> 9.11 us  [next_on_ring(): lax.ppermute(block, 'outer', [(i, (i + 1) % outer) for i in range(outer)])]
    ppermute x12, waiting for transfers between devices: 32.7 us -> 34.6 us  [next_on_ring(): lax.ppermute(block, 'outer', [(i, (i + 1) % outer) for i in range(outer)])]
    pallas_call x5 -> x6, Pallas kernels: 2.49 us -> 1.8 us  [joined(): pl.pallas_call(join_kernel, out_shape=jax.ShapeDtypeStruct((len(blocks) *...]
  transfers between devices with their start and end apart: 28 -> 28, of which waited for: 18 -> 18; matrix products, arithmetic and copies ran while one was open for 3% -> 3% of each run, Pallas kernels for 11% -> 9%
where the time goes in v23:
time: 117 us
  waiting for transfers between devices  57.7 us (49%)
  starting transfers between devices  31.9 us (27%)
  Pallas kernels  13.1 us (11%)
  local copies, waits for them, and re-layouts  12.8 us (11%)
    ppermute x12, waiting for transfers between devices, next_on_ring(): lax.ppermute(block, 'outer', [(i, (i + 1) % outer) for i in range(outer)])  34.6 us
    ppermute x13, waiting for transfers between devices, to_partner(): return lax.ppermute(value, axes, [(i, i ^ offset) for i in range(size)])  17.9 us
    ppermute x13, starting transfers between devices, to_partner(): return lax.ppermute(value, axes, [(i, i ^ offset) for i in range(size)])  12.2 us
    all_to_all x3, starting transfers between devices, swap(): return lax.all_to_all(value, PLANE, split_axis=0, concat_axis=0, tiled=True)  10.6 us
    unnamed x36, local copies, waits for them, and re-layouts  9.68 us
    ppermute x12, starting transfers between devices, next_on_ring(): lax.ppermute(block, 'outer', [(i, (i + 1) % outer) for i in range(outer)])  9.11 us
    all_to_all x3, waiting for transfers between devices, swap(): return lax.all_to_all(value, PLANE, split_axis=0, concat_axis=0, tiled=True)  5.23 us
    pallas_call x2, Pallas kernels, up_product(): pl.pallas_call(functools.partial(up_kernel, len(maps), rank, offsets), ou...  3.96 us
  transfers between devices with their start and end apart: 28, of which 18 were waited for; matrix products, arithmetic and copies ran while one was open for 3% of the time, Pallas kernels for 9%

profile of v23, /device:TPU:0, one launch (start us, length us, event | category | flops | bytes accessed | tf_op | source)
XLA Modules:
  0.0 116.7 jit_solution(8867174224299262436)
XLA Ops:
  0.0 1.1 dynamic-slice_bitcast_fusion.4
  1.7 2.6 %collective-permute-start.1 = (bf16[64,1024]{1,0:T(8,128)(2,1)S(1)}, bf16[64,1024]{1,0:T(8,128)(2,1)S(1)}, u32[]{:S(2)}, u32[]{:S(2)}) collective-permute-start(bf16[64,1024]{1,0:T(8,128)(2,1)S(1)} %get-tuple-element.50), channel_id=1, source_target_pairs={{0,2},{1,3},{2,0},{3,1},{4,6},{5,7},{6,4},{7,5},{8,10},{9,11},{10,... | collective-permute-start | bytes 393224 | tf_op jit(solution)/shard_map/ppermute | solution.py:28
  4.4 1.8 %collective-permute-start.3 = (bf16[128,1024]{1,0:T(8,128)(2,1)S(1)}, bf16[128,1024]{1,0:T(8,128)(2,1)S(1)}, u32[]{:S(2)}, u32[]{:S(2)}) collective-permute-start(bf16[128,1024]{1,0:T(8,128)(2,1)S(1)} %join_blocks.6.refs_0_), channel_id=1, source_target_pairs={{0,4},{4,8},{8,12},{12,0},{1,5},{5,9},{9,13},{13,1},{2,6},{6,10},{... | collective-permute-start | bytes 786440 | tf_op jit(solution)/shard_map/ppermute | solution.py:32
  6.2 1.6 %outgoing_rows.1 = bf16[8,136,1024]{2,1,0:T(8,128)(2,1)} custom-call(bf16[128,8192]{1,0:T(8,128)(2,1)S(1)} %copy-done, s32[1,128]{1,0:T(1,128)S(1)} %bitcast.26), custom_call_target="tpu_custom_call" | custom-call | tf_op jit(solution)/shard_map/outgoing_rows/pallas_call | solution.py:95
  7.9 3.8 %all-to-all-start = ((bf16[8,136,1024]{2,1,0:T(8,128)(2,1)}), bf16[8,136,1024]{2,1,0:T(8,128)(2,1)S(1)}, u32[]{:S(2)}, u32[]{:S(2)}) async-start(bf16[8,136,1024]{2,1,0:T(8,128)(2,1)} %outgoing_rows.1), calls=%async_computation | async-start | bytes 4456448 | tf_op jit(solution)/shard_map/all_to_all | solution.py:40
  11.7 1.6 %collective-permute-start.4 = (bf16[128,1024]{1,0:T(8,128)(2,1)S(1)}, bf16[128,1024]{1,0:T(8,128)(2,1)S(1)}, u32[]{:S(2)}, u32[]{:S(2)}) collective-permute-start(bf16[128,1024]{1,0:T(8,128)(2,1)S(1)} %join_blocks.7.refs_1_), channel_id=1, source_target_pairs={{0,4},{4,8},{8,12},{12,0},{1,5},{5,9},{9,13},{13,1},{2,6},{6,10},{... | collective-permute-start | bytes 786440 | tf_op jit(solution)/shard_map/ppermute | solution.py:32
  13.3 1.7 %collective-permute-done.3.refs_0_.refs_2_ = bf16[128,1024]{1,0:T(8,128)(2,1)S(1)} collective-permute-done((bf16[128,1024]{1,0:T(8,128)(2,1)S(1)}, bf16[128,1024]{1,0:T(8,128)(2,1)S(1)}, u32[]{:S(2)}, u32[]{:S(2)}) %collective-permute-start.3) | collective-permute-done | bytes 262176 | tf_op jit(solution)/shard_map/ppermute | solution.py:32
  15.7 6.9 %collective-permute-done.4.refs_0_.refs_3_ = bf16[128,1024]{1,0:T(8,128)(2,1)S(1)} collective-permute-done((bf16[128,1024]{1,0:T(8,128)(2,1)S(1)}, bf16[128,1024]{1,0:T(8,128)(2,1)S(1)}, u32[]{:S(2)}, u32[]{:S(2)}) %collective-permute-start.4) | collective-permute-done | bytes 262176 | tf_op jit(solution)/shard_map/ppermute | solution.py:32
  23.3 1.9 %dynamic-slice_bitcast_fusion = (bf16[64,1024]{1,0:T(8,128)(2,1)}, bf16[64,1024]{1,0:T(8,128)(2,1)}, bf16[64,1024]{1,0:T(8,128)(2,1)}, bf16[64,1024]{1,0:T(8,128)(2,1)}) fusion(bf16[1,64,8192]{2,1,0:T(8,128)(2,1)} %param.7, s32[]{:T(128)S(6)} %select_n.32, s32[]{:T(128)S(6)} %select_n.30, s32[]{:T(128)S(6)} %select_n.29, s32[]{:T(128)S(6)} %select_n.31), kind=kLoop, calls=%fused_computation.1 | loop fusion | bytes 1048592 | tf_op jit(solution)/shard_map/dynamic_slice | solution.py:275
  25.2 2.1 %collective-permute-start.10 = (bf16[64,1024]{1,0:T(8,128)(2,1)}, bf16[64,1024]{1,0:T(8,128)(2,1)}, u32[]{:S(2)}, u32[]{:S(2)}) collective-permute-start(bf16[64,1024]{1,0:T(8,128)(2,1)} %get-tuple-element.30), channel_id=1, source_target_pairs={{0,2},{1,3},{2,0},{3,1},{4,6},{5,7},{6,4},{7,5},{8,10},{9,11},{10,... | collective-permute-start | bytes 393224 | tf_op jit(solution)/shard_map/ppermute | solution.py:28
  28.8 5.5 %collective-permute-done.6.refs_5_ = bf16[128,1024]{1,0:T(8,128)(2,1)S(1)} collective-permute-done((bf16[128,1024]{1,0:T(8,128)(2,1)S(1)}, bf16[128,1024]{1,0:T(8,128)(2,1)S(1)}, u32[]{:S(2)}, u32[]{:S(2)}) %collective-permute-start.6) | collective-permute-done | bytes 262176 | tf_op jit(solution)/shard_map/ppermute | solution.py:32
  35.5 4.5 %collective-permute-done.7.refs_6_ = bf16[128,1024]{1,0:T(8,128)(2,1)S(1)} collective-permute-done((bf16[128,1024]{1,0:T(8,128)(2,1)S(1)}, bf16[128,1024]{1,0:T(8,128)(2,1)S(1)}, u32[]{:S(2)}, u32[]{:S(2)}) %collective-permute-start.7) | collective-permute-done | bytes 262176 | tf_op jit(solution)/shard_map/ppermute | solution.py:32
  40.7 1.4 %collective-permute-done.10.refs_0_ = bf16[64,1024]{1,0:T(8,128)(2,1)} collective-permute-done((bf16[64,1024]{1,0:T(8,128)(2,1)}, bf16[64,1024]{1,0:T(8,128)(2,1)}, u32[]{:S(2)}, u32[]{:S(2)}) %collective-permute-start.10) | collective-permute-done | bytes 131104 | tf_op jit(solution)/shard_map/ppermute | solution.py:28
  42.1 2.7 %collective-permute-done.8.refs_7_ = bf16[128,1024]{1,0:T(8,128)(2,1)S(1)} collective-permute-done((bf16[128,1024]{1,0:T(8,128)(2,1)S(1)}, bf16[128,1024]{1,0:T(8,128)(2,1)S(1)}, u32[]{:S(2)}, u32[]{:S(2)}) %collective-permute-start.8) | collective-permute-done | bytes 262176 | tf_op jit(solution)/shard_map/ppermute | solution.py:32
  46.5 1.6 %collective-permute-start.13 = (bf16[128,1024]{1,0:T(8,128)(2,1)S(1)}, bf16[128,1024]{1,0:T(8,128)(2,1)S(1)}, u32[]{:S(2)}, u32[]{:S(2)}) collective-permute-start(bf16[128,1024]{1,0:T(8,128)(2,1)S(1)} %join_blocks.10.refs_1_), channel_id=1, source_target_pairs={{0,4},{4,8},{8,12},{12,0},{1,5},{5,9},{9,13},{13,1},{2,6},{6,10},{... | collective-permute-start | bytes 786440 | tf_op jit(solution)/shard_map/ppermute | solution.py:32
  48.2 7.7 %collective-permute-done.12.refs_0_.refs_2_ = bf16[128,1024]{1,0:T(8,128)(2,1)S(1)} collective-permute-done((bf16[128,1024]{1,0:T(8,128)(2,1)S(1)}, bf16[128,1024]{1,0:T(8,128)(2,1)S(1)}, u32[]{:S(2)}, u32[]{:S(2)}) %collective-permute-start.12) | collective-permute-done | bytes 262176 | tf_op jit(solution)/shard_map/ppermute | solution.py:32
  64.2 3.7 %down_product.1 = (f32[8,64,128]{2,1,0:T(8,128)}, f32[8,128]{1,0:T(8,128)S(1)}) custom-call(s32[16]{0:T(128)S(1)} %add.61.labels_ref, bf16[8,136,1024]{2,1,0:T(8,128)(2,1)S(1)} %all-to-all-done.rows_ref, bf16[128,1024]{1,0:T(8,128)(2,1)S(1)} %copy-done.3, bf16[128,1024]{1,0:T(8,128)(2,1)S(1)} %copy-done.7, bf16[128,1024]{1,0:T(8,128)(2,1)S(1)} %copy-done.5, ...), custom_call_target="tpu_custom_call" | custom-call | flops 2147483648 | bytes 4194304 | tf_op jit(solution)/shard_map/down_product/pallas_call | solution.py:147
  68.3 3.5 %all-to-all-start.1 = ((f32[8,64,128]{2,1,0:T(8,128)}), f32[8,64,128]{2,1,0:T(8,128)S(1)}, u32[]{:S(2)}, u32[]{:S(2)}) async-start(f32[8,64,128]{2,1,0:T(8,128)} %get-tuple-element.26), calls=%async_computation.1 | async-start | bytes 524288 | tf_op jit(solution)/shard_map/all_to_all | solution.py:40
  71.8 1.6 %collective-permute-start.16 = (bf16[128,1024]{1,0:T(8,128)(2,1)S(1)}, bf16[128,1024]{1,0:T(8,128)(2,1)S(1)}, u32[]{:S(2)}, u32[]{:S(2)}) collective-permute-start(bf16[128,1024]{1,0:T(8,128)(2,1)S(1)} %collective-permute-done.14.refs_4_), channel_id=1, source_target_pairs={{0,4},{4,8},{8,12},{12,0},{1,5},{5,9},{9,13},{13,1},{2,6},{6,10},{... | collective-permute-start | bytes 786440 | tf_op jit(solution)/shard_map/ppermute | solution.py:32
  73.3 2.7 %collective-permute-done.15.refs_5_ = bf16[128,1024]{1,0:T(8,128)(2,1)S(1)} collective-permute-done((bf16[128,1024]{1,0:T(8,128)(2,1)S(1)}, bf16[128,1024]{1,0:T(8,128)(2,1)S(1)}, u32[]{:S(2)}, u32[]{:S(2)}) %collective-permute-start.15) | collective-permute-done | bytes 262176 | tf_op jit(solution)/shard_map/ppermute | solution.py:32
  78.5 3.4 %all-to-all-start.2 = ((bf16[8,64,128]{2,1,0:T(8,128)(2,1)}), bf16[8,64,128]{2,1,0:T(8,128)(2,1)S(1)}, u32[]{:S(2)}, u32[]{:S(2)}) async-start(bf16[8,64,128]{2,1,0:T(8,128)(2,1)} %summed_copies.1), calls=%async_computation.2 | async-start | bytes 262144 | tf_op jit(solution)/shard_map/all_to_all | solution.py:40
  82.8 4.2 %all-to-all-done.2.shrunk_ref = bf16[8,64,128]{2,1,0:T(8,128)(2,1)S(1)} async-done(((bf16[8,64,128]{2,1,0:T(8,128)(2,1)}), bf16[8,64,128]{2,1,0:T(8,128)(2,1)S(1)}, u32[]{:S(2)}, u32[]{:S(2)}) %all-to-all-start.2) | async-done | bytes 131104 | tf_op jit(solution)/shard_map/all_to_all | solution.py:40
  87.0 1.2 %collective-permute-done.17.refs_7_ = bf16[128,1024]{1,0:T(8,128)(2,1)S(1)} collective-permute-done((bf16[128,1024]{1,0:T(8,128)(2,1)S(1)}, bf16[128,1024]{1,0:T(8,128)(2,1)S(1)}, u32[]{:S(2)}, u32[]{:S(2)}) %collective-permute-start.17) | collective-permute-done | bytes 262176 | tf_op jit(solution)/shard_map/ppermute | solution.py:32
  88.2 1.4 %up_product.2 = (bf16[128,1024]{1,0:T(8,128)(2,1)S(1)}, bf16[128,1024]{1,0:T(8,128)(2,1)S(1)}) custom-call(s32[16]{0:T(128)S(1)} %add.61.labels_ref, s32[1]{0:T(128)} %bitcast.me_ref, f32[8,128]{1,0:T(8,128)S(1)} %get-tuple-element.25.ids_ref, bf16[8,64,128]{2,1,0:T(8,128)(2,1)S(1)} %all-to-all-done.2.shrunk_ref, ...), custom_call_target="tpu_custom_call" | custom-call | flops 536870912 | bytes 2621440 | tf_op jit(solution)/shard_map/up_product/pallas_call | solution.py:222
  89.5 2.6 %collective-permute-start.18 = (bf16[128,1024]{1,0:T(8,128)(2,1)S(1)}, bf16[128,1024]{1,0:T(8,128)(2,1)S(1)}, u32[]{:S(2)}, u32[]{:S(2)}) collective-permute-start(bf16[128,1024]{1,0:T(8,128)(2,1)S(1)} %get-tuple-element.35), channel_id=1, source_target_pairs={{0,18},{1,19},{2,16},{3,17},{16,2},{17,3},{18,0},{19,1},{4,22},{5,... | collective-permute-start | bytes 786440 | tf_op jit(solution)/shard_map/ppermute | solution.py:28
  92.2 2.6 %up_product.3 = (bf16[128,1024]{1,0:T(8,128)(2,1)S(1)}, bf16[128,1024]{1,0:T(8,128)(2,1)S(1)}, bf16[128,1024]{1,0:T(8,128)(2,1)S(1)}, bf16[128,1024]{1,0:T(8,128...) custom-call(s32[16]{0:T(128)S(1)} %add.61.labels_ref, s32[1]{0:T(128)} %bitcast.me_ref, ...), custom_call_target="tpu_custom_call" | custom-call | flops 1610612736 | bytes 3670016 | tf_op jit(solution)/shard_map/up_product/pallas_call | solution.py:222
  96.7 1.7 %collective-permute-start.22 = (bf16[128,1024]{1,0:T(8,128)(2,1)S(1)}, bf16[128,1024]{1,0:T(8,128)(2,1)S(1)}, u32[]{:S(2)}, u32[]{:S(2)}) collective-permute-start(bf16[128,1024]{1,0:T(8,128)(2,1)S(1)} %get-tuple-element.39), channel_id=1, source_target_pairs={{0,2},{1,3},{2,0},{3,1},{16,18},{17,19},{18,16},{19,17},{4,6},{5,7... | collective-permute-start | bytes 786440 | tf_op jit(solution)/shard_map/ppermute | solution.py:28
  98.3 1.4 %collective-permute-done.18.refs_0_ = bf16[128,1024]{1,0:T(8,128)(2,1)S(1)} collective-permute-done((bf16[128,1024]{1,0:T(8,128)(2,1)S(1)}, bf16[128,1024]{1,0:T(8,128)(2,1)S(1)}, u32[]{:S(2)}, u32[]{:S(2)}) %collective-permute-start.18) | collective-permute-done | bytes 262176 | tf_op jit(solution)/shard_map/ppermute | solution.py:28
  99.7 4.9 %collective-permute-done.19.refs_1_ = bf16[128,1024]{1,0:T(8,128)(2,1)S(1)} collective-permute-done((bf16[128,1024]{1,0:T(8,128)(2,1)S(1)}, bf16[128,1024]{1,0:T(8,128)(2,1)S(1)}, u32[]{:S(2)}, u32[]{:S(2)}) %collective-permute-start.19) | collective-permute-done | bytes 262176 | tf_op jit(solution)/shard_map/ppermute | solution.py:28
  105.2 6.0 %collective-permute-done.20.refs_2_ = bf16[128,1024]{1,0:T(8,128)(2,1)S(1)} collective-permute-done((bf16[128,1024]{1,0:T(8,128)(2,1)S(1)}, bf16[128,1024]{1,0:T(8,128)(2,1)S(1)}, u32[]{:S(2)}, u32[]{:S(2)}) %collective-permute-start.20) | collective-permute-done | bytes 262176 | tf_op jit(solution)/shard_map/ppermute | solution.py:28
  111.2 3.2 %collective-permute-done.21.refs_3_ = bf16[128,1024]{1,0:T(8,128)(2,1)S(1)} collective-permute-done((bf16[128,1024]{1,0:T(8,128)(2,1)S(1)}, bf16[128,1024]{1,0:T(8,128)(2,1)S(1)}, u32[]{:S(2)}, u32[]{:S(2)}) %collective-permute-start.21) | collective-permute-done | bytes 262176 | tf_op jit(solution)/shard_map/ppermute | solution.py:28
  115.4 1.4 %place_results.1 = bf16[128,8192]{1,0:T(8,128)(2,1)} custom-call(s32[1]{0:T(128)} %bitcast.me_ref, bf16[128,1024]{1,0:T(8,128)(2,1)S(1)} %collective-permute-done.18.refs_0_, bf16[128,1024]{1,0:T(8,128)(2,1)S(1)} %collective-permute-done.19.refs_1_, bf16[128,1024]{1,0:T(8,128)(2,1)S(1)} %collective-permute-done.20.refs_2_, ...), custom_call_target="tpu_custom_call" | custom-call | tf_op jit(solution)/shard_map/place_results/pallas_call | solution.py:253
  (78 shorter events, 22.7 us)
Async XLA Ops:
  1.1 3.2 %collective-permute-start = (bf16[64,1024]{1,0:T(8,128)(2,1)S(1)}, bf16[64,1024]{1,0:T(8,128)(2,1)S(1)}, u32[]{:S(2)}, u32[]{:S(2)}) collective-permute-start(bf16[64,1024]{1,0:T(8,128)(2,1)S(1)} %get-tuple-element.48), channel_id=1, source_target_pairs={{0,1},{1,0},{2,3},{3,2},{4,5},{5,4},{6,7},{7,6},{8,9},{9,8},{10,11... | collective-permute-start | bytes 393224 | tf_op jit(solution)/shard_map/ppermute | solution.py:28
  1.7 10.0 %collective-permute-start.1 = (bf16[64,1024]{1,0:T(8,128)(2,1)S(1)}, bf16[64,1024]{1,0:T(8,128)(2,1)S(1)}, u32[]{:S(2)}, u32[]{:S(2)}) collective-permute-start(bf16[64,1024]{1,0:T(8,128)(2,1)S(1)} %get-tuple-element.50), channel_id=1, source_target_pairs={{0,2},{1,3},{2,0},{3,1},{4,6},{5,7},{6,4},{7,5},{8,10},{9,11},{10,... | collective-permute-start | bytes 393224 | tf_op jit(solution)/shard_map/ppermute | solution.py:28
  4.2 7.4 %collective-permute-start.2 = (bf16[64,1024]{1,0:T(8,128)(2,1)S(1)}, bf16[64,1024]{1,0:T(8,128)(2,1)S(1)}, u32[]{:S(2)}, u32[]{:S(2)}) collective-permute-start(bf16[64,1024]{1,0:T(8,128)(2,1)S(1)} %get-tuple-element.47), channel_id=1, source_target_pairs={{0,3},{1,2},{2,1},{3,0},{4,7},{5,6},{6,5},{7,4},{8,11},{9,10},{10,... | collective-permute-start | bytes 393224 | tf_op jit(solution)/shard_map/ppermute | solution.py:28
  4.3 3.5 %copy-start.2 = (bf16[128,1024]{1,0:T(8,128)(2,1)}, bf16[128,1024]{1,0:T(8,128)(2,1)S(1)}, u32[]{:S(2)}) copy-start(bf16[128,1024]{1,0:T(8,128)(2,1)S(1)} %join_blocks.6.refs_0_) | copy-start | bytes 786436
  4.4 10.7 %collective-permute-start.3 = (bf16[128,1024]{1,0:T(8,128)(2,1)S(1)}, bf16[128,1024]{1,0:T(8,128)(2,1)S(1)}, u32[]{:S(2)}, u32[]{:S(2)}) collective-permute-start(bf16[128,1024]{1,0:T(8,128)(2,1)S(1)} %join_blocks.6.refs_0_), channel_id=1, source_target_pairs={{0,4},{4,8},{8,12},{12,0},{1,5},{5,9},{9,13},{13,1},{2,6},{6,10},{... | collective-permute-start | bytes 786440 | tf_op jit(solution)/shard_map/ppermute | solution.py:32
  7.9 48.7 %all-to-all-start = ((bf16[8,136,1024]{2,1,0:T(8,128)(2,1)}), bf16[8,136,1024]{2,1,0:T(8,128)(2,1)S(1)}, u32[]{:S(2)}, u32[]{:S(2)}) async-start(bf16[8,136,1024]{2,1,0:T(8,128)(2,1)} %outgoing_rows.1), calls=%async_computation | async-start | bytes 4456448 | tf_op jit(solution)/shard_map/all_to_all | solution.py:40
  11.6 3.4 %copy-start.6 = (bf16[128,1024]{1,0:T(8,128)(2,1)}, bf16[128,1024]{1,0:T(8,128)(2,1)S(1)}, u32[]{:S(2)}) copy-start(bf16[128,1024]{1,0:T(8,128)(2,1)S(1)} %join_blocks.7.refs_1_) | copy-start | bytes 786436
  11.7 10.9 %collective-permute-start.4 = (bf16[128,1024]{1,0:T(8,128)(2,1)S(1)}, bf16[128,1024]{1,0:T(8,128)(2,1)S(1)}, u32[]{:S(2)}, u32[]{:S(2)}) collective-permute-start(bf16[128,1024]{1,0:T(8,128)(2,1)S(1)} %join_blocks.7.refs_1_), channel_id=1, source_target_pairs={{0,4},{4,8},{8,12},{12,0},{1,5},{5,9},{9,13},{13,1},{2,6},{6,10},{... | collective-permute-start | bytes 786440 | tf_op jit(solution)/shard_map/ppermute | solution.py:32
  15.7 12.5 %collective-permute-start.5 = (bf16[128,1024]{1,0:T(8,128)(2,1)S(1)}, bf16[128,1024]{1,0:T(8,128)(2,1)S(1)}, u32[]{:S(2)}, u32[]{:S(2)}) collective-permute-start(bf16[128,1024]{1,0:T(8,128)(2,1)S(1)} %join_blocks.8), channel_id=1, source_target_pairs={{0,4},{4,8},{8,12},{12,0},{1,5},{5,9},{9,13},{13,1},{2,6},{6,10},{... | collective-permute-start | bytes 786440 | tf_op jit(solution)/shard_map/ppermute | solution.py:32
  23.3 11.0 %collective-permute-start.6 = (bf16[128,1024]{1,0:T(8,128)(2,1)S(1)}, bf16[128,1024]{1,0:T(8,128)(2,1)S(1)}, u32[]{:S(2)}, u32[]{:S(2)}) collective-permute-start(bf16[128,1024]{1,0:T(8,128)(2,1)S(1)} %join_blocks.9), channel_id=1, source_target_pairs={{0,4},{4,8},{8,12},{12,0},{1,5},{5,9},{9,13},{13,1},{2,6},{6,10},{... | collective-permute-start | bytes 786440 | tf_op jit(solution)/shard_map/ppermute | solution.py:32
  25.2 9.3 %collective-permute-start.9 = (bf16[64,1024]{1,0:T(8,128)(2,1)}, bf16[64,1024]{1,0:T(8,128)(2,1)}, u32[]{:S(2)}, u32[]{:S(2)}) collective-permute-start(bf16[64,1024]{1,0:T(8,128)(2,1)} %get-tuple-element.28), channel_id=1, source_target_pairs={{0,1},{1,0},{2,3},{3,2},{4,5},{5,4},{6,7},{7,6},{8,9},{9,8},{10,11... | collective-permute-start | bytes 393224 | tf_op jit(solution)/shard_map/ppermute | solution.py:28
  25.2 16.9 %collective-permute-start.10 = (bf16[64,1024]{1,0:T(8,128)(2,1)}, bf16[64,1024]{1,0:T(8,128)(2,1)}, u32[]{:S(2)}, u32[]{:S(2)}) collective-permute-start(bf16[64,1024]{1,0:T(8,128)(2,1)} %get-tuple-element.30), channel_id=1, source_target_pairs={{0,2},{1,3},{2,0},{3,1},{4,6},{5,7},{6,4},{7,5},{8,10},{9,11},{10,... | collective-permute-start | bytes 393224 | tf_op jit(solution)/shard_map/ppermute | solution.py:28
  27.3 17.5 %collective-permute-start.11 = (bf16[64,1024]{1,0:T(8,128)(2,1)}, bf16[64,1024]{1,0:T(8,128)(2,1)}, u32[]{:S(2)}, u32[]{:S(2)}) collective-permute-start(bf16[64,1024]{1,0:T(8,128)(2,1)} %get-tuple-element.32), channel_id=1, source_target_pairs={{0,3},{1,2},{2,1},{3,0},{4,7},{5,6},{6,5},{7,4},{8,11},{9,10},{10,... | collective-permute-start | bytes 393224 | tf_op jit(solution)/shard_map/ppermute | solution.py:28
  28.2 16.5 %copy-start.10 = (bf16[128,1024]{1,0:T(8,128)(2,1)}, bf16[128,1024]{1,0:T(8,128)(2,1)S(1)}, u32[]{:S(2)}) copy-start(bf16[128,1024]{1,0:T(8,128)(2,1)S(1)} %collective-permute-done.5.refs_4_) | copy-start | bytes 786436
  28.2 11.7 %collective-permute-start.7 = (bf16[128,1024]{1,0:T(8,128)(2,1)S(1)}, bf16[128,1024]{1,0:T(8,128)(2,1)S(1)}, u32[]{:S(2)}, u32[]{:S(2)}) collective-permute-start(bf16[128,1024]{1,0:T(8,128)(2,1)S(1)} %collective-permute-done.5.refs_4_), channel_id=1, source_target_pairs={{0,4},{4,8},{8,12},{12,0},{1,5},{5,9},{9,13},{13,1},{2,6},{6,10},{... | collective-permute-start | bytes 786440 | tf_op jit(solution)/shard_map/ppermute | solution.py:32
  34.3 10.4 %copy-start.12 = (bf16[128,1024]{1,0:T(8,128)(2,1)}, bf16[128,1024]{1,0:T(8,128)(2,1)S(1)}, u32[]{:S(2)}) copy-start(bf16[128,1024]{1,0:T(8,128)(2,1)S(1)} %collective-permute-done.6.refs_5_) | copy-start | bytes 786436
  34.3 10.4 %collective-permute-start.8 = (bf16[128,1024]{1,0:T(8,128)(2,1)S(1)}, bf16[128,1024]{1,0:T(8,128)(2,1)S(1)}, u32[]{:S(2)}, u32[]{:S(2)}) collective-permute-start(bf16[128,1024]{1,0:T(8,128)(2,1)S(1)} %collective-permute-done.6.refs_5_), channel_id=1, source_target_pairs={{0,4},{4,8},{8,12},{12,0},{1,5},{5,9},{9,13},{13,1},{2,6},{6,10},{... | collective-permute-start | bytes 786440 | tf_op jit(solution)/shard_map/ppermute | solution.py:32
  44.8 11.1 %collective-permute-start.12 = (bf16[128,1024]{1,0:T(8,128)(2,1)S(1)}, bf16[128,1024]{1,0:T(8,128)(2,1)S(1)}, u32[]{:S(2)}, u32[]{:S(2)}) collective-permute-start(bf16[128,1024]{1,0:T(8,128)(2,1)S(1)} %pad_maximum_fusion.refs_0_), channel_id=1, source_target_pairs={{0,4},{4,8},{8,12},{12,0},{1,5},{5,9},{9,13},{13,1},{2,6},{6,10},{... | collective-permute-start | bytes 786440 | tf_op jit(solution)/shard_map/ppermute | solution.py:32
  46.5 21.4 %collective-permute-start.13 = (bf16[128,1024]{1,0:T(8,128)(2,1)S(1)}, bf16[128,1024]{1,0:T(8,128)(2,1)S(1)}, u32[]{:S(2)}, u32[]{:S(2)}) collective-permute-start(bf16[128,1024]{1,0:T(8,128)(2,1)S(1)} %join_blocks.10.refs_1_), channel_id=1, source_target_pairs={{0,4},{4,8},{8,12},{12,0},{1,5},{5,9},{9,13},{13,1},{2,6},{6,10},{... | collective-permute-start | bytes 786440 | tf_op jit(solution)/shard_map/ppermute | solution.py:32
  56.6 15.2 %collective-permute-start.14 = (bf16[128,1024]{1,0:T(8,128)(2,1)}, bf16[128,1024]{1,0:T(8,128)(2,1)S(1)}, u32[]{:S(2)}, u32[]{:S(2)}) collective-permute-start(bf16[128,1024]{1,0:T(8,128)(2,1)} %join_blocks.11), channel_id=1, source_target_pairs={{0,4},{4,8},{8,12},{12,0},{1,5},{5,9},{9,13},{13,1},{2,6},{6,10},{... | collective-permute-start | bytes 786440 | tf_op jit(solution)/shard_map/ppermute | solution.py:32
  67.9 8.2 %collective-permute-start.15 = (bf16[128,1024]{1,0:T(8,128)(2,1)S(1)}, bf16[128,1024]{1,0:T(8,128)(2,1)S(1)}, u32[]{:S(2)}, u32[]{:S(2)}) collective-permute-start(bf16[128,1024]{1,0:T(8,128)(2,1)S(1)} %collective-permute-done.13.refs_3_), channel_id=1, source_target_pairs={{0,4},{4,8},{8,12},{12,0},{1,5},{5,9},{9,13},{13,1},{2,6},{6,10},{... | collective-permute-start | bytes 786440 | tf_op jit(solution)/shard_map/ppermute | solution.py:32
  68.3 9.5 %all-to-all-start.1 = ((f32[8,64,128]{2,1,0:T(8,128)}), f32[8,64,128]{2,1,0:T(8,128)S(1)}, u32[]{:S(2)}, u32[]{:S(2)}) async-start(f32[8,64,128]{2,1,0:T(8,128)} %get-tuple-element.26), calls=%async_computation.1 | async-start | bytes 524288 | tf_op jit(solution)/shard_map/all_to_all | solution.py:40
  71.8 11.0 %collective-permute-start.16 = (bf16[128,1024]{1,0:T(8,128)(2,1)S(1)}, bf16[128,1024]{1,0:T(8,128)(2,1)S(1)}, u32[]{:S(2)}, u32[]{:S(2)}) collective-permute-start(bf16[128,1024]{1,0:T(8,128)(2,1)S(1)} %collective-permute-done.14.refs_4_), channel_id=1, source_target_pairs={{0,4},{4,8},{8,12},{12,0},{1,5},{5,9},{9,13},{13,1},{2,6},{6,10},{... | collective-permute-start | bytes 786440 | tf_op jit(solution)/shard_map/ppermute | solution.py:32
  76.1 12.1 %collective-permute-start.17 = (bf16[128,1024]{1,0:T(8,128)(2,1)S(1)}, bf16[128,1024]{1,0:T(8,128)(2,1)S(1)}, u32[]{:S(2)}, u32[]{:S(2)}) collective-permute-start(bf16[128,1024]{1,0:T(8,128)(2,1)S(1)} %collective-permute-done.15.refs_5_), channel_id=1, source_target_pairs={{0,4},{4,8},{8,12},{12,0},{1,5},{5,9},{9,13},{13,1},{2,6},{6,10},{... | collective-permute-start | bytes 786440 | tf_op jit(solution)/shard_map/ppermute | solution.py:32
  78.5 8.5 %all-to-all-start.2 = ((bf16[8,64,128]{2,1,0:T(8,128)(2,1)}), bf16[8,64,128]{2,1,0:T(8,128)(2,1)S(1)}, u32[]{:S(2)}, u32[]{:S(2)}) async-start(bf16[8,64,128]{2,1,0:T(8,128)(2,1)} %summed_copies.1), calls=%async_computation.2 | async-start | bytes 262144 | tf_op jit(solution)/shard_map/all_to_all | solution.py:40
  89.5 10.2 %collective-permute-start.18 = (bf16[128,1024]{1,0:T(8,128)(2,1)S(1)}, bf16[128,1024]{1,0:T(8,128)(2,1)S(1)}, u32[]{:S(2)}, u32[]{:S(2)}) collective-permute-start(bf16[128,1024]{1,0:T(8,128)(2,1)S(1)} %get-tuple-element.35), channel_id=1, source_target_pairs={{0,18},{1,19},{2,16},{3,17},{16,2},{17,3},{18,0},{19,1},{4,22},{5,... | collective-permute-start | bytes 786440 | tf_op jit(solution)/shard_map/ppermute | solution.py:28
  92.2 12.4 %collective-permute-start.19 = (bf16[128,1024]{1,0:T(8,128)(2,1)S(1)}, bf16[128,1024]{1,0:T(8,128)(2,1)S(1)}, u32[]{:S(2)}, u32[]{:S(2)}) collective-permute-start(bf16[128,1024]{1,0:T(8,128)(2,1)S(1)} %get-tuple-element.36), channel_id=1, source_target_pairs={{0,19},{1,18},{2,17},{3,16},{16,3},{17,2},{18,1},{19,0},{4,23},{5,... | collective-permute-start | bytes 786440 | tf_op jit(solution)/shard_map/ppermute | solution.py:28
  94.8 16.4 %collective-permute-start.20 = (bf16[128,1024]{1,0:T(8,128)(2,1)S(1)}, bf16[128,1024]{1,0:T(8,128)(2,1)S(1)}, u32[]{:S(2)}, u32[]{:S(2)}) collective-permute-start(bf16[128,1024]{1,0:T(8,128)(2,1)S(1)} %get-tuple-element.37), channel_id=1, source_target_pairs={{0,16},{1,17},{2,18},{3,19},{16,0},{17,1},{18,2},{19,3},{4,20},{5,... | collective-permute-start | bytes 786440 | tf_op jit(solution)/shard_map/ppermute | solution.py:28
  95.8 18.6 %collective-permute-start.21 = (bf16[128,1024]{1,0:T(8,128)(2,1)S(1)}, bf16[128,1024]{1,0:T(8,128)(2,1)S(1)}, u32[]{:S(2)}, u32[]{:S(2)}) collective-permute-start(bf16[128,1024]{1,0:T(8,128)(2,1)S(1)} %get-tuple-element.38), channel_id=1, source_target_pairs={{0,17},{1,16},{2,19},{3,18},{16,1},{17,0},{18,3},{19,2},{4,21},{5,... | collective-permute-start | bytes 786440 | tf_op jit(solution)/shard_map/ppermute | solution.py:28
  96.7 17.8 %collective-permute-start.22 = (bf16[128,1024]{1,0:T(8,128)(2,1)S(1)}, bf16[128,1024]{1,0:T(8,128)(2,1)S(1)}, u32[]{:S(2)}, u32[]{:S(2)}) collective-permute-start(bf16[128,1024]{1,0:T(8,128)(2,1)S(1)} %get-tuple-element.39), channel_id=1, source_target_pairs={{0,2},{1,3},{2,0},{3,1},{16,18},{17,19},{18,16},{19,17},{4,6},{5,7... | collective-permute-start | bytes 786440 | tf_op jit(solution)/shard_map/ppermute | solution.py:28
  99.7 15.7 %collective-permute-start.23 = (bf16[128,1024]{1,0:T(8,128)(2,1)S(1)}, bf16[128,1024]{1,0:T(8,128)(2,1)S(1)}, u32[]{:S(2)}, u32[]{:S(2)}) collective-permute-start(bf16[128,1024]{1,0:T(8,128)(2,1)S(1)} %get-tuple-element.40), channel_id=1, source_target_pairs={{0,3},{1,2},{2,1},{3,0},{16,19},{17,18},{18,17},{19,16},{4,7},{5,6... | collective-permute-start | bytes 786440 | tf_op jit(solution)/shard_map/ppermute | solution.py:28
  104.6 10.8 %collective-permute-start.24 = (bf16[128,1024]{1,0:T(8,128)(2,1)S(1)}, bf16[128,1024]{1,0:T(8,128)(2,1)S(1)}, u32[]{:S(2)}, u32[]{:S(2)}) collective-permute-start(bf16[128,1024]{1,0:T(8,128)(2,1)S(1)} %get-tuple-element.41), channel_id=1, source_target_pairs={{0,1},{1,0},{2,3},{3,2},{16,17},{17,16},{18,19},{19,18},{4,5},{5,4... | collective-permute-start | bytes 786440 | tf_op jit(solution)/shard_map/ppermute | solution.py:28
  (14 other events, 15.2 us)

commit v24 on v23

--- a/solution.py
+++ b/solution.py
@@ -20,8 +20,8 @@
 ANYWHERE = pl.BlockSpec(memory_space=pl.ANY)
 
 
-def params(scratch_bytes=0):
-    return pltpu.CompilerParams(vmem_limit_bytes=(12 << 20) + 2 * scratch_bytes)
+def params(product_bytes=0):
+    return pltpu.CompilerParams(vmem_limit_bytes=(12 << 20) + 2 * product_bytes if product_bytes else 5 << 20)
 
 
 def to_partner(value, axes, size, offset):
@@ -309,7 +309,7 @@
     packed, id_rows = down_product(labels, rows, down_maps, rank)
     up_near, up_far = rings(
         after(jnp.concatenate(up[:middle], axis=0), down_near[-1]),
-        joined([after(block, down_far[-1]) for block in up[middle:]], SLIGHTLY_AHEAD),
+        jnp.concatenate([after(block, down_far[-1]) for block in up[middle:]], axis=0),
         SLIGHTLY_AHEAD,
         0,
         far_second_after=[packed],

time: 117 us -> 113 us (0.966)
  waiting for transfers between devices: 57.7 us -> 55.8 us
  starting transfers between devices: 31.9 us -> 30.4 us
    ppermute x12, waiting for transfers between devices: 34.6 us -> 30.8 us  [next_on_ring(): lax.ppermute(block, 'outer', [(i, (i + 1) % outer) for i in range(outer)])]
    ppermute x12, starting transfers between devices: 9.11 us -> 6.47 us  [next_on_ring(): lax.ppermute(block, 'outer', [(i, (i + 1) % outer) for i in range(outer)])]
    all_to_all x3, waiting for transfers between devices: 5.23 us -> 6.78 us  [swap(): return lax.all_to_all(value, PLANE, split_axis=0, concat_axis=0, tiled=True)]
    unnamed x36 -> x39, local copies, waits for them, and re-layouts: 9.68 us -> 10 us
  transfers between devices with their start and end apart: 28 -> 28, of which waited for: 18 -> 18; matrix products, arithmetic and copies ran while one was open for 3% -> 4% of each run, Pallas kernels for 9% -> 8%
where the time goes in v24:
time: 113 us
  waiting for transfers between devices  55.8 us (49%)
  starting transfers between devices  30.4 us (27%)
  local copies, waits for them, and re-layouts  13 us (12%)
  Pallas kernels  12.1 us (11%)
  other arithmetic  1.16 us (1%)
    ppermute x12, waiting for transfers between devices, next_on_ring(): lax.ppermute(block, 'outer', [(i, (i + 1) % outer) for i in range(outer)])  30.8 us
    ppermute x13, waiting for transfers between devices, to_partner(): return lax.ppermute(value, axes, [(i, i ^ offset) for i in range(size)])  18.2 us
    ppermute x13, starting transfers between devices, to_partner(): return lax.ppermute(value, axes, [(i, i ^ offset) for i in range(size)])  12.3 us
    all_to_all x3, starting transfers between devices, swap(): return lax.all_to_all(value, PLANE, split_axis=0, concat_axis=0, tiled=True)  11.6 us
    unnamed x39, local copies, waits for them, and re-layouts  10 us
    all_to_all x3, waiting for transfers between devices, swap(): return lax.all_to_all(value, PLANE, split_axis=0, concat_axis=0, tiled=True)  6.78 us
    ppermute x12, starting transfers between devices, next_on_ring(): lax.ppermute(block, 'outer', [(i, (i + 1) % outer) for i in range(outer)])  6.47 us
    pallas_call x2, Pallas kernels, up_product(): pl.pallas_call(functools.partial(up_kernel, len(maps), rank, offsets), ou...  3.97 us
  transfers between devices with their start and end apart: 28, of which 18 were waited for; matrix products, arithmetic and copies ran while one was open for 4% of the time, Pallas kernels for 8%

profile of v24, /device:TPU:0, one launch (start us, length us, event | category | flops | bytes accessed | tf_op | source)
XLA Modules:
  0.0 112.7 jit_solution(10759261424858097102)
XLA Ops:
  1.7 2.6 %collective-permute-start.1 = (bf16[64,1024]{1,0:T(8,128)(2,1)S(1)}, bf16[64,1024]{1,0:T(8,128)(2,1)S(1)}, u32[]{:S(2)}, u32[]{:S(2)}) collective-permute-start(bf16[64,1024]{1,0:T(8,128)(2,1)S(1)} %get-tuple-element.50), channel_id=1, source_target_pairs={{0,2},{1,3},{2,0},{3,1},{4,6},{5,7},{6,4},{7,5},{8,10},{9,11},{10,... | collective-permute-start | bytes 393224 | tf_op jit(solution)/shard_map/ppermute | solution.py:28
  4.4 1.8 %collective-permute-start.3 = (bf16[128,1024]{1,0:T(8,128)(2,1)S(1)}, bf16[128,1024]{1,0:T(8,128)(2,1)S(1)}, u32[]{:S(2)}, u32[]{:S(2)}) collective-permute-start(bf16[128,1024]{1,0:T(8,128)(2,1)S(1)} %join_blocks.5.refs_0_), channel_id=1, source_target_pairs={{0,4},{4,8},{8,12},{12,0},{1,5},{5,9},{9,13},{13,1},{2,6},{6,10},{... | collective-permute-start | bytes 786440 | tf_op jit(solution)/shard_map/ppermute | solution.py:32
  6.2 1.6 %outgoing_rows.1 = bf16[8,136,1024]{2,1,0:T(8,128)(2,1)} custom-call(bf16[128,8192]{1,0:T(8,128)(2,1)S(1)} %copy-done, s32[1,128]{1,0:T(1,128)S(1)} %bitcast.26), custom_call_target="tpu_custom_call" | custom-call | tf_op jit(solution)/shard_map/outgoing_rows/pallas_call | solution.py:95
  7.8 3.8 %all-to-all-start = ((bf16[8,136,1024]{2,1,0:T(8,128)(2,1)}), bf16[8,136,1024]{2,1,0:T(8,128)(2,1)S(1)}, u32[]{:S(2)}, u32[]{:S(2)}) async-start(bf16[8,136,1024]{2,1,0:T(8,128)(2,1)} %outgoing_rows.1), calls=%async_computation | async-start | bytes 4456448 | tf_op jit(solution)/shard_map/all_to_all | solution.py:40
  11.7 1.6 %collective-permute-start.4 = (bf16[128,1024]{1,0:T(8,128)(2,1)S(1)}, bf16[128,1024]{1,0:T(8,128)(2,1)S(1)}, u32[]{:S(2)}, u32[]{:S(2)}) collective-permute-start(bf16[128,1024]{1,0:T(8,128)(2,1)S(1)} %join_blocks.6.refs_1_), channel_id=1, source_target_pairs={{0,4},{4,8},{8,12},{12,0},{1,5},{5,9},{9,13},{13,1},{2,6},{6,10},{... | collective-permute-start | bytes 786440 | tf_op jit(solution)/shard_map/ppermute | solution.py:32
  13.3 1.8 %collective-permute-done.3.refs_0_.refs_2_ = bf16[128,1024]{1,0:T(8,128)(2,1)S(1)} collective-permute-done((bf16[128,1024]{1,0:T(8,128)(2,1)S(1)}, bf16[128,1024]{1,0:T(8,128)(2,1)S(1)}, u32[]{:S(2)}, u32[]{:S(2)}) %collective-permute-start.3) | collective-permute-done | bytes 262176 | tf_op jit(solution)/shard_map/ppermute | solution.py:32
  15.8 6.8 %collective-permute-done.4.refs_0_.refs_3_ = bf16[128,1024]{1,0:T(8,128)(2,1)S(1)} collective-permute-done((bf16[128,1024]{1,0:T(8,128)(2,1)S(1)}, bf16[128,1024]{1,0:T(8,128)(2,1)S(1)}, u32[]{:S(2)}, u32[]{:S(2)}) %collective-permute-start.4) | collective-permute-done | bytes 262176 | tf_op jit(solution)/shard_map/ppermute | solution.py:32
  23.3 4.9 %collective-permute-done.5.refs_4_ = bf16[128,1024]{1,0:T(8,128)(2,1)S(1)} collective-permute-done((bf16[128,1024]{1,0:T(8,128)(2,1)S(1)}, bf16[128,1024]{1,0:T(8,128)(2,1)S(1)}, u32[]{:S(2)}, u32[]{:S(2)}) %collective-permute-start.5) | collective-permute-done | bytes 262176 | tf_op jit(solution)/shard_map/ppermute | solution.py:32
  29.1 2.1 %collective-permute-start.10 = (bf16[64,1024]{1,0:T(8,128)(2,1)}, bf16[64,1024]{1,0:T(8,128)(2,1)}, u32[]{:S(2)}, u32[]{:S(2)}) collective-permute-start(bf16[64,1024]{1,0:T(8,128)(2,1)} %get-tuple-element.30), channel_id=1, source_target_pairs={{0,2},{1,3},{2,0},{3,1},{4,6},{5,7},{6,4},{7,5},{8,10},{9,11},{10,... | collective-permute-start | bytes 393224 | tf_op jit(solution)/shard_map/ppermute | solution.py:28
  31.5 2.9 %collective-permute-done.6.refs_5_ = bf16[128,1024]{1,0:T(8,128)(2,1)S(1)} collective-permute-done((bf16[128,1024]{1,0:T(8,128)(2,1)S(1)}, bf16[128,1024]{1,0:T(8,128)(2,1)S(1)}, u32[]{:S(2)}, u32[]{:S(2)}) %collective-permute-start.6) | collective-permute-done | bytes 262176 | tf_op jit(solution)/shard_map/ppermute | solution.py:32
  35.5 4.5 %collective-permute-done.7.refs_6_ = bf16[128,1024]{1,0:T(8,128)(2,1)S(1)} collective-permute-done((bf16[128,1024]{1,0:T(8,128)(2,1)S(1)}, bf16[128,1024]{1,0:T(8,128)(2,1)S(1)}, u32[]{:S(2)}, u32[]{:S(2)}) %collective-permute-start.7) | collective-permute-done | bytes 262176 | tf_op jit(solution)/shard_map/ppermute | solution.py:32
  40.1 2.0 %collective-permute-done.10 = bf16[64,1024]{1,0:T(8,128)(2,1)} collective-permute-done((bf16[64,1024]{1,0:T(8,128)(2,1)}, bf16[64,1024]{1,0:T(8,128)(2,1)}, u32[]{:S(2)}, u32[]{:S(2)}) %collective-permute-start.10) | collective-permute-done | bytes 131104 | tf_op jit(solution)/shard_map/ppermute | solution.py:28
  42.1 3.5 %collective-permute-done.8.refs_7_ = bf16[128,1024]{1,0:T(8,128)(2,1)S(1)} collective-permute-done((bf16[128,1024]{1,0:T(8,128)(2,1)S(1)}, bf16[128,1024]{1,0:T(8,128)(2,1)S(1)}, u32[]{:S(2)}, u32[]{:S(2)}) %collective-permute-start.8) | collective-permute-done | bytes 262176 | tf_op jit(solution)/shard_map/ppermute | solution.py:32
  47.6 2.8 %collective-permute-done.12.refs_0_.refs_2_ = bf16[128,1024]{1,0:T(8,128)(2,1)S(1)} collective-permute-done((bf16[128,1024]{1,0:T(8,128)(2,1)S(1)}, bf16[128,1024]{1,0:T(8,128)(2,1)S(1)}, u32[]{:S(2)}, u32[]{:S(2)}) %collective-permute-start.12) | collective-permute-done | bytes 262176 | tf_op jit(solution)/shard_map/ppermute | solution.py:32
  58.7 3.7 %down_product.1 = (f32[8,64,128]{2,1,0:T(8,128)}, f32[8,128]{1,0:T(8,128)S(1)}) custom-call(s32[16]{0:T(128)S(1)} %add.61.labels_ref, bf16[8,136,1024]{2,1,0:T(8,128)(2,1)S(1)} %all-to-all-done.rows_ref, bf16[128,1024]{1,0:T(8,128)(2,1)S(1)} %copy-done.3, bf16[128,1024]{1,0:T(8,128)(2,1)S(1)} %copy-done.7, bf16[128,1024]{1,0:T(8,128)(2,1)S(1)} %copy-done.5, ...), custom_call_target="tpu_custom_call" | custom-call | flops 2147483648 | bytes 4194304 | tf_op jit(solution)/shard_map/down_product/pallas_call | solution.py:147
  62.4 1.3 %collective-permute-start.15 = (bf16[128,1024]{1,0:T(8,128)(2,1)S(1)}, bf16[128,1024]{1,0:T(8,128)(2,1)S(1)}, u32[]{:S(2)}, u32[]{:S(2)}) collective-permute-start(bf16[128,1024]{1,0:T(8,128)(2,1)S(1)} %collective-permute-done.13.refs_3_), channel_id=1, source_target_pairs={{0,4},{4,8},{8,12},{12,0},{1,5},{5,9},{9,13},{13,1},{2,6},{6,10},{... | collective-permute-start | bytes 786440 | tf_op jit(solution)/shard_map/ppermute | solution.py:32
  63.7 4.5 %all-to-all-start.1 = ((f32[8,64,128]{2,1,0:T(8,128)}), f32[8,64,128]{2,1,0:T(8,128)S(1)}, u32[]{:S(2)}, u32[]{:S(2)}) async-start(f32[8,64,128]{2,1,0:T(8,128)} %get-tuple-element.26), calls=%async_computation.1 | async-start | bytes 524288 | tf_op jit(solution)/shard_map/all_to_all | solution.py:40
  68.2 1.6 %collective-permute-start.16 = (bf16[128,1024]{1,0:T(8,128)(2,1)S(1)}, bf16[128,1024]{1,0:T(8,128)(2,1)S(1)}, u32[]{:S(2)}, u32[]{:S(2)}) collective-permute-start(bf16[128,1024]{1,0:T(8,128)(2,1)S(1)} %collective-permute-done.14.refs_4_), channel_id=1, source_target_pairs={{0,4},{4,8},{8,12},{12,0},{1,5},{5,9},{9,13},{13,1},{2,6},{6,10},{... | collective-permute-start | bytes 786440 | tf_op jit(solution)/shard_map/ppermute | solution.py:32
  69.8 1.9 %collective-permute-done.15.refs_5_ = bf16[128,1024]{1,0:T(8,128)(2,1)S(1)} collective-permute-done((bf16[128,1024]{1,0:T(8,128)(2,1)S(1)}, bf16[128,1024]{1,0:T(8,128)(2,1)S(1)}, u32[]{:S(2)}, u32[]{:S(2)}) %collective-permute-start.15) | collective-permute-done | bytes 262176 | tf_op jit(solution)/shard_map/ppermute | solution.py:32
  71.7 2.5 %all-to-all-done.1.terms_ref = f32[8,64,128]{2,1,0:T(8,128)S(1)} async-done(((f32[8,64,128]{2,1,0:T(8,128)}), f32[8,64,128]{2,1,0:T(8,128)S(1)}, u32[]{:S(2)}, u32[]{:S(2)}) %all-to-all-start.1) | async-done | bytes 262176 | tf_op jit(solution)/shard_map/all_to_all | solution.py:40
  74.9 3.4 %all-to-all-start.2 = ((bf16[8,64,128]{2,1,0:T(8,128)(2,1)}), bf16[8,64,128]{2,1,0:T(8,128)(2,1)S(1)}, u32[]{:S(2)}, u32[]{:S(2)}) async-start(bf16[8,64,128]{2,1,0:T(8,128)(2,1)} %summed_copies.1), calls=%async_computation.2 | async-start | bytes 262144 | tf_op jit(solution)/shard_map/all_to_all | solution.py:40
  79.1 4.3 %all-to-all-done.2.shrunk_ref = bf16[8,64,128]{2,1,0:T(8,128)(2,1)S(1)} async-done(((bf16[8,64,128]{2,1,0:T(8,128)(2,1)}), bf16[8,64,128]{2,1,0:T(8,128)(2,1)S(1)}, u32[]{:S(2)}, u32[]{:S(2)}) %all-to-all-start.2) | async-done | bytes 131104 | tf_op jit(solution)/shard_map/all_to_all | solution.py:40
  84.3 1.4 %up_product.2 = (bf16[128,1024]{1,0:T(8,128)(2,1)S(1)}, bf16[128,1024]{1,0:T(8,128)(2,1)S(1)}) custom-call(s32[16]{0:T(128)S(1)} %add.61.labels_ref, s32[1]{0:T(128)} %bitcast.me_ref, f32[8,128]{1,0:T(8,128)S(1)} %get-tuple-element.25.ids_ref, bf16[8,64,128]{2,1,0:T(8,128)(2,1)S(1)} %all-to-all-done.2.shrunk_ref, ...), custom_call_target="tpu_custom_call" | custom-call | flops 536870912 | bytes 2621440 | tf_op jit(solution)/shard_map/up_product/pallas_call | solution.py:222
  85.7 2.6 %collective-permute-start.18 = (bf16[128,1024]{1,0:T(8,128)(2,1)S(1)}, bf16[128,1024]{1,0:T(8,128)(2,1)S(1)}, u32[]{:S(2)}, u32[]{:S(2)}) collective-permute-start(bf16[128,1024]{1,0:T(8,128)(2,1)S(1)} %get-tuple-element.35), channel_id=1, source_target_pairs={{0,18},{1,19},{2,16},{3,17},{16,2},{17,3},{18,0},{19,1},{4,22},{5,... | collective-permute-start | bytes 786440 | tf_op jit(solution)/shard_map/ppermute | solution.py:28
  88.3 2.6 %up_product.3 = (bf16[128,1024]{1,0:T(8,128)(2,1)S(1)}, bf16[128,1024]{1,0:T(8,128)(2,1)S(1)}, bf16[128,1024]{1,0:T(8,128)(2,1)S(1)}, bf16[128,1024]{1,0:T(8,128...) custom-call(s32[16]{0:T(128)S(1)} %add.61.labels_ref, s32[1]{0:T(128)} %bitcast.me_ref, ...), custom_call_target="tpu_custom_call" | custom-call | flops 1610612736 | bytes 3670016 | tf_op jit(solution)/shard_map/up_product/pallas_call | solution.py:222
  91.7 1.2 %collective-permute-start.21 = (bf16[128,1024]{1,0:T(8,128)(2,1)S(1)}, bf16[128,1024]{1,0:T(8,128)(2,1)S(1)}, u32[]{:S(2)}, u32[]{:S(2)}) collective-permute-start(bf16[128,1024]{1,0:T(8,128)(2,1)S(1)} %get-tuple-element.38), channel_id=1, source_target_pairs={{0,17},{1,16},{2,19},{3,18},{16,1},{17,0},{18,3},{19,2},{4,21},{5,... | collective-permute-start | bytes 786440 | tf_op jit(solution)/shard_map/ppermute | solution.py:28
  92.8 1.7 %collective-permute-start.22 = (bf16[128,1024]{1,0:T(8,128)(2,1)S(1)}, bf16[128,1024]{1,0:T(8,128)(2,1)S(1)}, u32[]{:S(2)}, u32[]{:S(2)}) collective-permute-start(bf16[128,1024]{1,0:T(8,128)(2,1)S(1)} %get-tuple-element.39), channel_id=1, source_target_pairs={{0,2},{1,3},{2,0},{3,1},{16,18},{17,19},{18,16},{19,17},{4,6},{5,7... | collective-permute-start | bytes 786440 | tf_op jit(solution)/shard_map/ppermute | solution.py:28
  94.5 1.4 %collective-permute-done.18.refs_0_ = bf16[128,1024]{1,0:T(8,128)(2,1)S(1)} collective-permute-done((bf16[128,1024]{1,0:T(8,128)(2,1)S(1)}, bf16[128,1024]{1,0:T(8,128)(2,1)S(1)}, u32[]{:S(2)}, u32[]{:S(2)}) %collective-permute-start.18) | collective-permute-done | bytes 262176 | tf_op jit(solution)/shard_map/ppermute | solution.py:28
  95.9 4.9 %collective-permute-done.19.refs_1_ = bf16[128,1024]{1,0:T(8,128)(2,1)S(1)} collective-permute-done((bf16[128,1024]{1,0:T(8,128)(2,1)S(1)}, bf16[128,1024]{1,0:T(8,128)(2,1)S(1)}, u32[]{:S(2)}, u32[]{:S(2)}) %collective-permute-start.19) | collective-permute-done | bytes 262176 | tf_op jit(solution)/shard_map/ppermute | solution.py:28
  101.3 6.0 %collective-permute-done.20.refs_2_ = bf16[128,1024]{1,0:T(8,128)(2,1)S(1)} collective-permute-done((bf16[128,1024]{1,0:T(8,128)(2,1)S(1)}, bf16[128,1024]{1,0:T(8,128)(2,1)S(1)}, u32[]{:S(2)}, u32[]{:S(2)}) %collective-permute-start.20) | collective-permute-done | bytes 262176 | tf_op jit(solution)/shard_map/ppermute | solution.py:28
  107.4 2.9 %collective-permute-done.21.refs_3_ = bf16[128,1024]{1,0:T(8,128)(2,1)S(1)} collective-permute-done((bf16[128,1024]{1,0:T(8,128)(2,1)S(1)}, bf16[128,1024]{1,0:T(8,128)(2,1)S(1)}, u32[]{:S(2)}, u32[]{:S(2)}) %collective-permute-start.21) | collective-permute-done | bytes 262176 | tf_op jit(solution)/shard_map/ppermute | solution.py:28
  111.3 1.4 %place_results.1 = bf16[128,8192]{1,0:T(8,128)(2,1)} custom-call(s32[1]{0:T(128)} %bitcast.me_ref, bf16[128,1024]{1,0:T(8,128)(2,1)S(1)} %collective-permute-done.18.refs_0_, bf16[128,1024]{1,0:T(8,128)(2,1)S(1)} %collective-permute-done.19.refs_1_, bf16[128,1024]{1,0:T(8,128)(2,1)S(1)} %collective-permute-done.20.refs_2_, ...), custom_call_target="tpu_custom_call" | custom-call | tf_op jit(solution)/shard_map/place_results/pallas_call | solution.py:253
  (81 shorter events, 20.7 us)
Async XLA Ops:
  1.1 3.2 %collective-permute-start = (bf16[64,1024]{1,0:T(8,128)(2,1)S(1)}, bf16[64,1024]{1,0:T(8,128)(2,1)S(1)}, u32[]{:S(2)}, u32[]{:S(2)}) collective-permute-start(bf16[64,1024]{1,0:T(8,128)(2,1)S(1)} %get-tuple-element.48), channel_id=1, source_target_pairs={{0,1},{1,0},{2,3},{3,2},{4,5},{5,4},{6,7},{7,6},{8,9},{9,8},{10,11... | collective-permute-start | bytes 393224 | tf_op jit(solution)/shard_map/ppermute | solution.py:28
  1.7 9.9 %collective-permute-start.1 = (bf16[64,1024]{1,0:T(8,128)(2,1)S(1)}, bf16[64,1024]{1,0:T(8,128)(2,1)S(1)}, u32[]{:S(2)}, u32[]{:S(2)}) collective-permute-start(bf16[64,1024]{1,0:T(8,128)(2,1)S(1)} %get-tuple-element.50), channel_id=1, source_target_pairs={{0,2},{1,3},{2,0},{3,1},{4,6},{5,7},{6,4},{7,5},{8,10},{9,11},{10,... | collective-permute-start | bytes 393224 | tf_op jit(solution)/shard_map/ppermute | solution.py:28
  4.2 7.4 %collective-permute-start.2 = (bf16[64,1024]{1,0:T(8,128)(2,1)S(1)}, bf16[64,1024]{1,0:T(8,128)(2,1)S(1)}, u32[]{:S(2)}, u32[]{:S(2)}) collective-permute-start(bf16[64,1024]{1,0:T(8,128)(2,1)S(1)} %get-tuple-element.47), channel_id=1, source_target_pairs={{0,3},{1,2},{2,1},{3,0},{4,7},{5,6},{6,5},{7,4},{8,11},{9,10},{10,... | collective-permute-start | bytes 393224 | tf_op jit(solution)/shard_map/ppermute | solution.py:28
  4.4 10.7 %collective-permute-start.3 = (bf16[128,1024]{1,0:T(8,128)(2,1)S(1)}, bf16[128,1024]{1,0:T(8,128)(2,1)S(1)}, u32[]{:S(2)}, u32[]{:S(2)}) collective-permute-start(bf16[128,1024]{1,0:T(8,128)(2,1)S(1)} %join_blocks.5.refs_0_), channel_id=1, source_target_pairs={{0,4},{4,8},{8,12},{12,0},{1,5},{5,9},{9,13},{13,1},{2,6},{6,10},{... | collective-permute-start | bytes 786440 | tf_op jit(solution)/shard_map/ppermute | solution.py:32
  7.8 43.3 %all-to-all-start = ((bf16[8,136,1024]{2,1,0:T(8,128)(2,1)}), bf16[8,136,1024]{2,1,0:T(8,128)(2,1)S(1)}, u32[]{:S(2)}, u32[]{:S(2)}) async-start(bf16[8,136,1024]{2,1,0:T(8,128)(2,1)} %outgoing_rows.1), calls=%async_computation | async-start | bytes 4456448 | tf_op jit(solution)/shard_map/all_to_all | solution.py:40
  11.7 10.9 %collective-permute-start.4 = (bf16[128,1024]{1,0:T(8,128)(2,1)S(1)}, bf16[128,1024]{1,0:T(8,128)(2,1)S(1)}, u32[]{:S(2)}, u32[]{:S(2)}) collective-permute-start(bf16[128,1024]{1,0:T(8,128)(2,1)S(1)} %join_blocks.6.refs_1_), channel_id=1, source_target_pairs={{0,4},{4,8},{8,12},{12,0},{1,5},{5,9},{9,13},{13,1},{2,6},{6,10},{... | collective-permute-start | bytes 786440 | tf_op jit(solution)/shard_map/ppermute | solution.py:32
  15.7 12.5 %copy-start.18 = (bf16[1,64,8192]{2,1,0:T(8,128)(2,1)S(1)}, bf16[1,64,8192]{2,1,0:T(8,128)(2,1)}, u32[]{:S(2)}) copy-start(bf16[1,64,8192]{2,1,0:T(8,128)(2,1)} %param.7) | copy-start | bytes 3145732
  15.7 12.5 %collective-permute-start.5 = (bf16[128,1024]{1,0:T(8,128)(2,1)S(1)}, bf16[128,1024]{1,0:T(8,128)(2,1)S(1)}, u32[]{:S(2)}, u32[]{:S(2)}) collective-permute-start(bf16[128,1024]{1,0:T(8,128)(2,1)S(1)} %join_blocks.7), channel_id=1, source_target_pairs={{0,4},{4,8},{8,12},{12,0},{1,5},{5,9},{9,13},{13,1},{2,6},{6,10},{... | collective-permute-start | bytes 786440 | tf_op jit(solution)/shard_map/ppermute | solution.py:32
  23.3 11.0 %collective-permute-start.6 = (bf16[128,1024]{1,0:T(8,128)(2,1)S(1)}, bf16[128,1024]{1,0:T(8,128)(2,1)S(1)}, u32[]{:S(2)}, u32[]{:S(2)}) collective-permute-start(bf16[128,1024]{1,0:T(8,128)(2,1)S(1)} %join_blocks.8), channel_id=1, source_target_pairs={{0,4},{4,8},{8,12},{12,0},{1,5},{5,9},{9,13},{13,1},{2,6},{6,10},{... | collective-permute-start | bytes 786440 | tf_op jit(solution)/shard_map/ppermute | solution.py:32
  28.2 7.2 %copy-start.10 = (bf16[128,1024]{1,0:T(8,128)(2,1)}, bf16[128,1024]{1,0:T(8,128)(2,1)S(1)}, u32[]{:S(2)}) copy-start(bf16[128,1024]{1,0:T(8,128)(2,1)S(1)} %collective-permute-done.5.refs_4_) | copy-start | bytes 786436
  28.2 11.8 %collective-permute-start.7 = (bf16[128,1024]{1,0:T(8,128)(2,1)S(1)}, bf16[128,1024]{1,0:T(8,128)(2,1)S(1)}, u32[]{:S(2)}, u32[]{:S(2)}) collective-permute-start(bf16[128,1024]{1,0:T(8,128)(2,1)S(1)} %collective-permute-done.5.refs_4_), channel_id=1, source_target_pairs={{0,4},{4,8},{8,12},{12,0},{1,5},{5,9},{9,13},{13,1},{2,6},{6,10},{... | collective-permute-start | bytes 786440 | tf_op jit(solution)/shard_map/ppermute | solution.py:32
  29.1 5.2 %collective-permute-start.9 = (bf16[64,1024]{1,0:T(8,128)(2,1)}, bf16[64,1024]{1,0:T(8,128)(2,1)}, u32[]{:S(2)}, u32[]{:S(2)}) collective-permute-start(bf16[64,1024]{1,0:T(8,128)(2,1)} %get-tuple-element.28), channel_id=1, source_target_pairs={{0,1},{1,0},{2,3},{3,2},{4,5},{5,4},{6,7},{7,6},{8,9},{9,8},{10,11... | collective-permute-start | bytes 393224 | tf_op jit(solution)/shard_map/ppermute | solution.py:28
  29.1 12.9 %collective-permute-start.10 = (bf16[64,1024]{1,0:T(8,128)(2,1)}, bf16[64,1024]{1,0:T(8,128)(2,1)}, u32[]{:S(2)}, u32[]{:S(2)}) collective-permute-start(bf16[64,1024]{1,0:T(8,128)(2,1)} %get-tuple-element.30), channel_id=1, source_target_pairs={{0,2},{1,3},{2,0},{3,1},{4,6},{5,7},{6,4},{7,5},{8,10},{9,11},{10,... | collective-permute-start | bytes 393224 | tf_op jit(solution)/shard_map/ppermute | solution.py:28
  31.3 14.3 %collective-permute-start.11 = (bf16[64,1024]{1,0:T(8,128)(2,1)}, bf16[64,1024]{1,0:T(8,128)(2,1)}, u32[]{:S(2)}, u32[]{:S(2)}) collective-permute-start(bf16[64,1024]{1,0:T(8,128)(2,1)} %get-tuple-element.32), channel_id=1, source_target_pairs={{0,3},{1,2},{2,1},{3,0},{4,7},{5,6},{6,5},{7,4},{8,11},{9,10},{10,... | collective-permute-start | bytes 393224 | tf_op jit(solution)/shard_map/ppermute | solution.py:28
  34.4 11.2 %copy-start.12 = (bf16[128,1024]{1,0:T(8,128)(2,1)}, bf16[128,1024]{1,0:T(8,128)(2,1)S(1)}, u32[]{:S(2)}) copy-start(bf16[128,1024]{1,0:T(8,128)(2,1)S(1)} %collective-permute-done.6.refs_5_) | copy-start | bytes 786436
  34.4 11.2 %collective-permute-start.8 = (bf16[128,1024]{1,0:T(8,128)(2,1)S(1)}, bf16[128,1024]{1,0:T(8,128)(2,1)S(1)}, u32[]{:S(2)}, u32[]{:S(2)}) collective-permute-start(bf16[128,1024]{1,0:T(8,128)(2,1)S(1)} %collective-permute-done.6.refs_5_), channel_id=1, source_target_pairs={{0,4},{4,8},{8,12},{12,0},{1,5},{5,9},{9,13},{13,1},{2,6},{6,10},{... | collective-permute-start | bytes 786440 | tf_op jit(solution)/shard_map/ppermute | solution.py:32
  40.0 6.6 %copy-start.14 = (bf16[128,1024]{1,0:T(8,128)(2,1)}, bf16[128,1024]{1,0:T(8,128)(2,1)S(1)}, u32[]{:S(2)}) copy-start(bf16[128,1024]{1,0:T(8,128)(2,1)S(1)} %collective-permute-done.7.refs_6_) | copy-start | bytes 786436
  40.0 10.4 %collective-permute-start.12 = (bf16[128,1024]{1,0:T(8,128)(2,1)S(1)}, bf16[128,1024]{1,0:T(8,128)(2,1)S(1)}, u32[]{:S(2)}, u32[]{:S(2)}) collective-permute-start(bf16[128,1024]{1,0:T(8,128)(2,1)S(1)} %pad_maximum_fusion.refs_0_), channel_id=1, source_target_pairs={{0,4},{4,8},{8,12},{12,0},{1,5},{5,9},{9,13},{13,1},{2,6},{6,10},{... | collective-permute-start | bytes 786440 | tf_op jit(solution)/shard_map/ppermute | solution.py:32
  47.5 14.9 %collective-permute-start.13 = (bf16[128,1024]{1,0:T(8,128)(2,1)S(1)}, bf16[128,1024]{1,0:T(8,128)(2,1)S(1)}, u32[]{:S(2)}, u32[]{:S(2)}) collective-permute-start(bf16[128,1024]{1,0:T(8,128)(2,1)S(1)} %constant_dynamic-update-slice_fusion.refs_1_), channel_id=1, source_target_pairs={{0,4},{4,8},{8,12},{12,0},{1,5},{5,9},{9,13},{13,1},{2,6},{6,10},{... | collective-permute-start | bytes 786440 | tf_op jit(solution)/shard_map/ppermute | solution.py:32
  51.1 17.1 %collective-permute-start.14 = (bf16[128,1024]{1,0:T(8,128)(2,1)}, bf16[128,1024]{1,0:T(8,128)(2,1)S(1)}, u32[]{:S(2)}, u32[]{:S(2)}) collective-permute-start(bf16[128,1024]{1,0:T(8,128)(2,1)} %join_blocks.9), channel_id=1, source_target_pairs={{0,4},{4,8},{8,12},{12,0},{1,5},{5,9},{9,13},{13,1},{2,6},{6,10},{... | collective-permute-start | bytes 786440 | tf_op jit(solution)/shard_map/ppermute | solution.py:32
  62.4 9.3 %collective-permute-start.15 = (bf16[128,1024]{1,0:T(8,128)(2,1)S(1)}, bf16[128,1024]{1,0:T(8,128)(2,1)S(1)}, u32[]{:S(2)}, u32[]{:S(2)}) collective-permute-start(bf16[128,1024]{1,0:T(8,128)(2,1)S(1)} %collective-permute-done.13.refs_3_), channel_id=1, source_target_pairs={{0,4},{4,8},{8,12},{12,0},{1,5},{5,9},{9,13},{13,1},{2,6},{6,10},{... | collective-permute-start | bytes 786440 | tf_op jit(solution)/shard_map/ppermute | solution.py:32
  63.7 10.5 %all-to-all-start.1 = ((f32[8,64,128]{2,1,0:T(8,128)}), f32[8,64,128]{2,1,0:T(8,128)S(1)}, u32[]{:S(2)}, u32[]{:S(2)}) async-start(f32[8,64,128]{2,1,0:T(8,128)} %get-tuple-element.26), calls=%async_computation.1 | async-start | bytes 524288 | tf_op jit(solution)/shard_map/all_to_all | solution.py:40
  68.2 11.0 %collective-permute-start.16 = (bf16[128,1024]{1,0:T(8,128)(2,1)S(1)}, bf16[128,1024]{1,0:T(8,128)(2,1)S(1)}, u32[]{:S(2)}, u32[]{:S(2)}) collective-permute-start(bf16[128,1024]{1,0:T(8,128)(2,1)S(1)} %collective-permute-done.14.refs_4_), channel_id=1, source_target_pairs={{0,4},{4,8},{8,12},{12,0},{1,5},{5,9},{9,13},{13,1},{2,6},{6,10},{... | collective-permute-start | bytes 786440 | tf_op jit(solution)/shard_map/ppermute | solution.py:32
  71.7 12.6 %collective-permute-start.17 = (bf16[128,1024]{1,0:T(8,128)(2,1)S(1)}, bf16[128,1024]{1,0:T(8,128)(2,1)S(1)}, u32[]{:S(2)}, u32[]{:S(2)}) collective-permute-start(bf16[128,1024]{1,0:T(8,128)(2,1)S(1)} %collective-permute-done.15.refs_5_), channel_id=1, source_target_pairs={{0,4},{4,8},{8,12},{12,0},{1,5},{5,9},{9,13},{13,1},{2,6},{6,10},{... | collective-permute-start | bytes 786440 | tf_op jit(solution)/shard_map/ppermute | solution.py:32
  74.9 8.5 %all-to-all-start.2 = ((bf16[8,64,128]{2,1,0:T(8,128)(2,1)}), bf16[8,64,128]{2,1,0:T(8,128)(2,1)S(1)}, u32[]{:S(2)}, u32[]{:S(2)}) async-start(bf16[8,64,128]{2,1,0:T(8,128)(2,1)} %summed_copies.1), calls=%async_computation.2 | async-start | bytes 262144 | tf_op jit(solution)/shard_map/all_to_all | solution.py:40
  85.7 10.2 %collective-permute-start.18 = (bf16[128,1024]{1,0:T(8,128)(2,1)S(1)}, bf16[128,1024]{1,0:T(8,128)(2,1)S(1)}, u32[]{:S(2)}, u32[]{:S(2)}) collective-permute-start(bf16[128,1024]{1,0:T(8,128)(2,1)S(1)} %get-tuple-element.35), channel_id=1, source_target_pairs={{0,18},{1,19},{2,16},{3,17},{16,2},{17,3},{18,0},{19,1},{4,22},{5,... | collective-permute-start | bytes 786440 | tf_op jit(solution)/shard_map/ppermute | solution.py:28
  88.3 12.4 %collective-permute-start.19 = (bf16[128,1024]{1,0:T(8,128)(2,1)S(1)}, bf16[128,1024]{1,0:T(8,128)(2,1)S(1)}, u32[]{:S(2)}, u32[]{:S(2)}) collective-permute-start(bf16[128,1024]{1,0:T(8,128)(2,1)S(1)} %get-tuple-element.36), channel_id=1, source_target_pairs={{0,19},{1,18},{2,17},{3,16},{16,3},{17,2},{18,1},{19,0},{4,23},{5,... | collective-permute-start | bytes 786440 | tf_op jit(solution)/shard_map/ppermute | solution.py:28
  90.9 16.4 %collective-permute-start.20 = (bf16[128,1024]{1,0:T(8,128)(2,1)S(1)}, bf16[128,1024]{1,0:T(8,128)(2,1)S(1)}, u32[]{:S(2)}, u32[]{:S(2)}) collective-permute-start(bf16[128,1024]{1,0:T(8,128)(2,1)S(1)} %get-tuple-element.37), channel_id=1, source_target_pairs={{0,16},{1,17},{2,18},{3,19},{16,0},{17,1},{18,2},{19,3},{4,20},{5,... | collective-permute-start | bytes 786440 | tf_op jit(solution)/shard_map/ppermute | solution.py:28
  91.7 18.6 %collective-permute-start.21 = (bf16[128,1024]{1,0:T(8,128)(2,1)S(1)}, bf16[128,1024]{1,0:T(8,128)(2,1)S(1)}, u32[]{:S(2)}, u32[]{:S(2)}) collective-permute-start(bf16[128,1024]{1,0:T(8,128)(2,1)S(1)} %get-tuple-element.38), channel_id=1, source_target_pairs={{0,17},{1,16},{2,19},{3,18},{16,1},{17,0},{18,3},{19,2},{4,21},{5,... | collective-permute-start | bytes 786440 | tf_op jit(solution)/shard_map/ppermute | solution.py:28
  92.8 17.4 %collective-permute-start.22 = (bf16[128,1024]{1,0:T(8,128)(2,1)S(1)}, bf16[128,1024]{1,0:T(8,128)(2,1)S(1)}, u32[]{:S(2)}, u32[]{:S(2)}) collective-permute-start(bf16[128,1024]{1,0:T(8,128)(2,1)S(1)} %get-tuple-element.39), channel_id=1, source_target_pairs={{0,2},{1,3},{2,0},{3,1},{16,18},{17,19},{18,16},{19,17},{4,6},{5,7... | collective-permute-start | bytes 786440 | tf_op jit(solution)/shard_map/ppermute | solution.py:28
  95.9 15.4 %collective-permute-start.23 = (bf16[128,1024]{1,0:T(8,128)(2,1)S(1)}, bf16[128,1024]{1,0:T(8,128)(2,1)S(1)}, u32[]{:S(2)}, u32[]{:S(2)}) collective-permute-start(bf16[128,1024]{1,0:T(8,128)(2,1)S(1)} %get-tuple-element.40), channel_id=1, source_target_pairs={{0,3},{1,2},{2,1},{3,0},{16,19},{17,18},{18,17},{19,16},{4,7},{5,6... | collective-permute-start | bytes 786440 | tf_op jit(solution)/shard_map/ppermute | solution.py:28
  100.7 10.6 %collective-permute-start.24 = (bf16[128,1024]{1,0:T(8,128)(2,1)S(1)}, bf16[128,1024]{1,0:T(8,128)(2,1)S(1)}, u32[]{:S(2)}, u32[]{:S(2)}) collective-permute-start(bf16[128,1024]{1,0:T(8,128)(2,1)S(1)} %get-tuple-element.41), channel_id=1, source_target_pairs={{0,1},{1,0},{2,3},{3,2},{16,17},{17,16},{18,19},{19,18},{4,5},{5,4... | collective-permute-start | bytes 786440 | tf_op jit(solution)/shard_map/ppermute | solution.py:28
  (15 other events, 24.5 us)

commit v25 on v21

--- a/solution.py
+++ b/solution.py
@@ -133,7 +133,7 @@
         for n in range(block):
             total = total_ref[n * tok : (n + 1) * tok, :]
             total += pltpu.roll(total, LANES // 2, 1)
-            packed_ref[first + n] = jnp.where(lane < rank, total[:half], total[half:])
+            packed_ref[first + n] = jnp.where(lane < rank, total[:half], total[half:]).astype(jnp.bfloat16)
         return 0
 
     lax.fori_loop(0, members // block, one, 0)
@@ -146,7 +146,7 @@
     return pl.pallas_call(
         functools.partial(down_kernel, len(maps), rank),
         out_shape=[
-            jax.ShapeDtypeStruct((members, tok // 2, LANES), jnp.float32),
+            jax.ShapeDtypeStruct((members, tok // 2, LANES), jnp.bfloat16),
             jax.ShapeDtypeStruct((members, tok), jnp.float32),
         ],
         in_specs=[IN_SMEM, IN_VMEM] + [IN_VMEM] * len(maps),
@@ -166,7 +166,7 @@
 
 
 def copies_kernel(terms_ref, out_ref):
-    own = jnp.sum(terms_ref[...], axis=0).astype(jnp.bfloat16)
+    own = jnp.sum(terms_ref[...].astype(jnp.float32), axis=0).astype(jnp.bfloat16)
     for member in range(out_ref.shape[0]):
         out_ref[member] = own
 
@@ -298,13 +298,17 @@
     down_near, down_far = rings(joined(down[:middle], AHEAD), joined(down[middle:], AHEAD), SLIGHTLY_AHEAD, SLIGHTLY_AHEAD)
     ids = token_adapter_index.reshape(1, tok)
     rows = swap(outgoing_rows(after(hidden, down_near[0]), ids, members))
-    up = exchanged([after(block, down_near[1]) for block in slices(adapter_up_maps[0])])
+    own_up = [after(block, down_near[1]) for block in slices(adapter_up_maps[0])]
+    halves = [jnp.concatenate([own_up[n], own_up[n + middle]], axis=0) for n in range(middle)]
+    halves = halves[:1] + [to_partner(halves[n], "inner", inner, n) for n in range(1, middle)]
+    up_first_near = jnp.concatenate([h[:rank] for h in halves], axis=0)
+    up_first_far = to_partner(jnp.concatenate([h[rank:] for h in halves], axis=0), "inner", inner, middle)
 
     down_maps = [m for pair in zip(down_near, down_far) for m in pair]
     packed, id_rows = down_product(labels, rows, down_maps, rank)
     up_near, up_far = rings(
-        after(jnp.concatenate(up[:middle], axis=0), down_near[-1]),
-        jnp.concatenate([after(block, down_far[-1]) for block in up[middle:]], axis=0),
+        after(up_first_near, down_near[-1]),
+        after(up_first_far, down_far[-1]),
         SLIGHTLY_AHEAD,
         0,
         far_second_after=[packed],

time: 110 us -> 121 us (1.10)
  blocking collectives: 0 us -> 9.2 us
  waiting for transfers between devices: 57 us -> 65 us
  starting transfers between devices: 30.3 us -> 24.2 us
  Pallas kernels: 15.5 us -> 12.9 us
  local copies, waits for them, and re-layouts: 5.84 us -> 8.39 us
    ppermute x12, waiting for transfers between devices: 32.7 us -> 44.6 us  [next_on_ring(): lax.ppermute(block, 'outer', [(i, (i + 1) % outer) for i in range(outer)])]
    all_to_all x0 -> x1, blocking collectives: none -> 9.2 us  [swap(): return lax.all_to_all(value, PLANE, split_axis=0, concat_axis=0, tiled=True)]
    all_to_all x3 -> x2, starting transfers between devices: 11.5 us -> 7.11 us  [swap(): return lax.all_to_all(value, PLANE, split_axis=0, concat_axis=0, tiled=True)]
    ppermute x13 -> x12, waiting for transfers between devices: 17.9 us -> 15.3 us  [to_partner(): return lax.ppermute(value, axes, [(i, i ^ offset) for i in range(size)])]
    ppermute x12, starting transfers between devices: 6.52 us -> 3.95 us  [next_on_ring(): lax.ppermute(block, 'outer', [(i, (i + 1) % outer) for i in range(outer)])]
    unnamed x15 -> x28, local copies, waits for them, and re-layouts: 2.86 us -> 5.24 us
    pallas_call x5, Pallas kernels: 2.49 us -> 0.81 us  [joined(): pl.pallas_call(join_kernel, out_shape=jax.ShapeDtypeStruct((len(blocks) *...]
    all_to_all x3 -> x2, waiting for transfers between devices: 6.38 us -> 5.1 us  [swap(): return lax.all_to_all(value, PLANE, split_axis=0, concat_axis=0, tiled=True)]
  transfers between devices with their start and end apart: 28 -> 26, of which waited for: 18 -> 15; matrix products, arithmetic and copies ran while one was open for 3% -> 2% of each run, Pallas kernels for 11% -> 8%
where the time goes in v25:
time: 121 us
  waiting for transfers between devices  65 us (54%)
  starting transfers between devices  24.2 us (20%)
  Pallas kernels  12.9 us (11%)
  blocking collectives  9.2 us (8%)
  local copies, waits for them, and re-layouts  8.39 us (7%)
    ppermute x12, waiting for transfers between devices, next_on_ring(): lax.ppermute(block, 'outer', [(i, (i + 1) % outer) for i in range(outer)])  44.6 us
    ppermute x12, waiting for transfers between devices, to_partner(): return lax.ppermute(value, axes, [(i, i ^ offset) for i in range(size)])  15.3 us
    ppermute x12, starting transfers between devices, to_partner(): return lax.ppermute(value, axes, [(i, i ^ offset) for i in range(size)])  13.1 us
    all_to_all x1, blocking collectives, swap(): return lax.all_to_all(value, PLANE, split_axis=0, concat_axis=0, tiled=True)  9.2 us
    all_to_all x2, starting transfers between devices, swap(): return lax.all_to_all(value, PLANE, split_axis=0, concat_axis=0, tiled=True)  7.11 us
    unnamed x28, local copies, waits for them, and re-layouts  5.24 us
    all_to_all x2, waiting for transfers between devices, swap(): return lax.all_to_all(value, PLANE, split_axis=0, concat_axis=0, tiled=True)  5.1 us
    pallas_call x2, Pallas kernels, up_product(): pl.pallas_call(functools.partial(up_kernel, len(maps), rank, offsets), ou...  4.95 us
  transfers between devices with their start and end apart: 26, of which 15 were waited for; matrix products, arithmetic and copies ran while one was open for 2% of the time, Pallas kernels for 8%

profile of v25, /device:TPU:0, one launch (start us, length us, event | category | flops | bytes accessed | tf_op | source)
XLA Modules:
  0.0 120.8 jit_solution(15586253381161535839)
XLA Ops:
  0.0 1.1 dynamic-slice_bitcast_fusion.4
  1.7 2.6 %collective-permute-start.1 = (bf16[64,1024]{1,0:T(8,128)(2,1)S(1)}, bf16[64,1024]{1,0:T(8,128)(2,1)S(1)}, u32[]{:S(2)}, u32[]{:S(2)}) collective-permute-start(bf16[64,1024]{1,0:T(8,128)(2,1)S(1)} %get-tuple-element.48), channel_id=1, source_target_pairs={{0,2},{1,3},{2,0},{3,1},{4,6},{5,7},{6,4},{7,5},{8,10},{9,11},{10,... | collective-permute-start | bytes 393224 | tf_op jit(solution)/shard_map/ppermute | solution.py:27
  4.3 1.9 %dynamic-slice_bitcast_fusion = (bf16[64,1024]{1,0:T(8,128)(2,1)}, bf16[64,1024]{1,0:T(8,128)(2,1)}, bf16[64,1024]{1,0:T(8,128)(2,1)}, bf16[64,1024]{1,0:T(8,128)(2,1)}) fusion(bf16[1,64,8192]{2,1,0:T(8,128)(2,1)} %param.7, s32[]{:T(128)S(6)} %select_n.31, s32[]{:T(128)S(6)} %select_n.30, s32[]{:T(128)S(6)} %select_n.29, s32[]{:T(128)S(6)} %select_n.32), kind=kLoop, calls=%fused_computation.3 | loop fusion | bytes 1048592 | tf_op jit(solution)/shard_map/dynamic_slice | solution.py:270
  6.3 1.8 %collective-permute-start.3 = (bf16[128,1024]{1,0:T(8,128)(2,1)S(1)}, bf16[128,1024]{1,0:T(8,128)(2,1)S(1)}, u32[]{:S(2)}, u32[]{:S(2)}) collective-permute-start(bf16[128,1024]{1,0:T(8,128)(2,1)S(1)} %join_blocks.5.refs_0_), channel_id=1, source_target_pairs={{0,4},{4,8},{8,12},{12,0},{1,5},{5,9},{9,13},{13,1},{2,6},{6,10},{... | collective-permute-start | bytes 786440 | tf_op jit(solution)/shard_map/ppermute | solution.py:31
  8.1 1.6 %outgoing_rows.1 = bf16[8,136,1024]{2,1,0:T(8,128)(2,1)} custom-call(bf16[128,8192]{1,0:T(8,128)(2,1)S(1)} %copy-done, s32[1,128]{1,0:T(1,128)S(1)} %bitcast.26), custom_call_target="tpu_custom_call" | custom-call | tf_op jit(solution)/shard_map/outgoing_rows/pallas_call | solution.py:94
  9.8 3.7 %all-to-all-start = ((bf16[8,136,1024]{2,1,0:T(8,128)(2,1)}), bf16[8,136,1024]{2,1,0:T(8,128)(2,1)S(1)}, u32[]{:S(2)}, u32[]{:S(2)}) async-start(bf16[8,136,1024]{2,1,0:T(8,128)(2,1)} %outgoing_rows.1), calls=%async_computation | async-start | bytes 4456448 | tf_op jit(solution)/shard_map/all_to_all | solution.py:39
  13.6 1.6 %collective-permute-start.4 = (bf16[128,1024]{1,0:T(8,128)(2,1)S(1)}, bf16[128,1024]{1,0:T(8,128)(2,1)S(1)}, u32[]{:S(2)}, u32[]{:S(2)}) collective-permute-start(bf16[128,1024]{1,0:T(8,128)(2,1)S(1)} %join_blocks.6.refs_1_), channel_id=1, source_target_pairs={{0,4},{4,8},{8,12},{12,0},{1,5},{5,9},{9,13},{13,1},{2,6},{6,10},{... | collective-permute-start | bytes 786440 | tf_op jit(solution)/shard_map/ppermute | solution.py:31
  15.2 1.8 %collective-permute-done.3.refs_0_.refs_2_ = bf16[128,1024]{1,0:T(8,128)(2,1)S(1)} collective-permute-done((bf16[128,1024]{1,0:T(8,128)(2,1)S(1)}, bf16[128,1024]{1,0:T(8,128)(2,1)S(1)}, u32[]{:S(2)}, u32[]{:S(2)}) %collective-permute-start.3) | collective-permute-done | bytes 262176 | tf_op jit(solution)/shard_map/ppermute | solution.py:31
  17.2 7.3 %collective-permute-done.4.refs_0_.refs_3_ = bf16[128,1024]{1,0:T(8,128)(2,1)S(1)} collective-permute-done((bf16[128,1024]{1,0:T(8,128)(2,1)S(1)}, bf16[128,1024]{1,0:T(8,128)(2,1)S(1)}, u32[]{:S(2)}, u32[]{:S(2)}) %collective-permute-start.4) | collective-permute-done | bytes 262176 | tf_op jit(solution)/shard_map/ppermute | solution.py:31
  25.2 4.9 %collective-permute-done.5.refs_4_ = bf16[128,1024]{1,0:T(8,128)(2,1)S(1)} collective-permute-done((bf16[128,1024]{1,0:T(8,128)(2,1)S(1)}, bf16[128,1024]{1,0:T(8,128)(2,1)S(1)}, u32[]{:S(2)}, u32[]{:S(2)}) %collective-permute-start.5) | collective-permute-done | bytes 262176 | tf_op jit(solution)/shard_map/ppermute | solution.py:31
  30.9 2.1 %collective-permute-start.10 = (bf16[128,1024]{1,0:T(8,128)(2,1)}, bf16[128,1024]{1,0:T(8,128)(2,1)S(1)}, u32[]{:S(2)}, u32[]{:S(2)}) collective-permute-start(bf16[128,1024]{1,0:T(8,128)(2,1)} %pad_maximum_fusion.2), channel_id=1, source_target_pairs={{0,2},{1,3},{2,0},{3,1},{4,6},{5,7},{6,4},{7,5},{8,10},{9,11},{10,... | collective-permute-start | bytes 786440 | tf_op jit(solution)/shard_map/ppermute | solution.py:27
  33.0 3.4 %collective-permute-done.6.refs_5_ = bf16[128,1024]{1,0:T(8,128)(2,1)} collective-permute-done((bf16[128,1024]{1,0:T(8,128)(2,1)S(1)}, bf16[128,1024]{1,0:T(8,128)(2,1)}, u32[]{:S(2)}, u32[]{:S(2)}) %collective-permute-start.6) | collective-permute-done | bytes 262176 | tf_op jit(solution)/shard_map/ppermute | solution.py:31
  36.4 5.5 %collective-permute-done.7.refs_6_ = bf16[128,1024]{1,0:T(8,128)(2,1)S(1)} collective-permute-done((bf16[128,1024]{1,0:T(8,128)(2,1)S(1)}, bf16[128,1024]{1,0:T(8,128)(2,1)S(1)}, u32[]{:S(2)}, u32[]{:S(2)}) %collective-permute-start.7) | collective-permute-done | bytes 262176 | tf_op jit(solution)/shard_map/ppermute | solution.py:31
  42.8 4.9 %collective-permute-done.8.refs_7_ = bf16[128,1024]{1,0:T(8,128)(2,1)} collective-permute-done((bf16[128,1024]{1,0:T(8,128)(2,1)}, bf16[128,1024]{1,0:T(8,128)(2,1)}, u32[]{:S(2)}, u32[]{:S(2)}) %collective-permute-start.8) | collective-permute-done | bytes 262176 | tf_op jit(solution)/shard_map/ppermute | solution.py:31
  47.8 5.9 %collective-permute-done.11.refs_0_.refs_2_ = bf16[128,1024]{1,0:T(8,128)(2,1)S(1)} collective-permute-done((bf16[128,1024]{1,0:T(8,128)(2,1)S(1)}, bf16[128,1024]{1,0:T(8,128)(2,1)S(1)}, u32[]{:S(2)}, u32[]{:S(2)}) %collective-permute-start.11) | collective-permute-done | bytes 262176 | tf_op jit(solution)/shard_map/ppermute | solution.py:31
  58.2 3.5 %down_product.1 = (bf16[8,64,128]{2,1,0:T(8,128)(2,1)S(1)}, f32[8,128]{1,0:T(8,128)S(1)}) custom-call(s32[16]{0:T(128)S(1)} %add.61.labels_ref, bf16[8,136,1024]{2,1,0:T(8,128)(2,1)S(1)} %all-to-all-done.rows_ref, bf16[128,1024]{1,0:T(8,128)(2,1)S(1)} %join_blocks.5.refs_0_, bf16[128,1024]{1,0:T(8,128)(2,1)S(1)} %copy-done.3, ...), custom_call_target="tpu_custom_call" | custom-call | flops 2147483648 | bytes 4194304 | tf_op jit(solution)/shard_map/down_product/pallas_call | solution.py:146
  62.0 1.5 %collective-permute-done.13.refs_4_ = bf16[128,1024]{1,0:T(8,128)(2,1)} collective-permute-done((bf16[128,1024]{1,0:T(8,128)(2,1)}, bf16[128,1024]{1,0:T(8,128)(2,1)}, u32[]{:S(2)}, u32[]{:S(2)}) %collective-permute-start.13) | collective-permute-done | bytes 262176 | tf_op jit(solution)/shard_map/ppermute | solution.py:31
  63.6 9.4 %collective-permute-done.14.refs_5_ = bf16[128,1024]{1,0:T(8,128)(2,1)S(1)} collective-permute-done((bf16[128,1024]{1,0:T(8,128)(2,1)}, bf16[128,1024]{1,0:T(8,128)(2,1)S(1)}, u32[]{:S(2)}, u32[]{:S(2)}) %collective-permute-start.14) | collective-permute-done | bytes 262176 | tf_op jit(solution)/shard_map/ppermute | solution.py:31
  73.0 9.2 %all_to_all.15.terms_ref = bf16[8,64,128]{2,1,0:T(8,128)(2,1)S(1)} all-to-all(bf16[8,64,128]{2,1,0:T(8,128)(2,1)S(1)} %get-tuple-element.25), channel_id=1, replica_groups=mesh['groups'=2,'outer'=4,'inner'=4] {'groups','inner'}, dimensions={0} | all-to-all | bytes 262144 | tf_op jit(solution)/shard_map/all_to_all | solution.py:39
  82.9 3.4 %all-to-all-start.2 = ((bf16[8,64,128]{2,1,0:T(8,128)(2,1)}), bf16[8,64,128]{2,1,0:T(8,128)(2,1)S(1)}, u32[]{:S(2)}, u32[]{:S(2)}) async-start(bf16[8,64,128]{2,1,0:T(8,128)(2,1)} %summed_copies.1), calls=%async_computation.2 | async-start | bytes 262144 | tf_op jit(solution)/shard_map/all_to_all | solution.py:39
  86.3 5.1 %all-to-all-done.2.shrunk_ref = bf16[8,64,128]{2,1,0:T(8,128)(2,1)S(1)} async-done(((bf16[8,64,128]{2,1,0:T(8,128)(2,1)}), bf16[8,64,128]{2,1,0:T(8,128)(2,1)S(1)}, u32[]{:S(2)}, u32[]{:S(2)}) %all-to-all-start.2) | async-done | bytes 131104 | tf_op jit(solution)/shard_map/all_to_all | solution.py:39
  91.4 2.5 %up_product.2 = (bf16[128,1024]{1,0:T(8,128)(2,1)S(1)}, bf16[128,1024]{1,0:T(8,128)(2,1)S(1)}, bf16[128,1024]{1,0:T(8,128)(2,1)S(1)}, bf16[128,1024]{1,0:T(8,128)(2,1)S(1)}) custom-call(s32[16]{0:T(128)S(1)} %add.61.labels_ref, s32[1]{0:T(128)} %bitcast.me_ref, f32[8,128]{1,0:T(8,128)S(1)} %get-tuple-element.24.ids_ref, ...), custom_call_target="tpu_custom_call" | custom-call | flops 1073741824 | bytes 3145728 | tf_op jit(solution)/shard_map/up_product/pallas_call | solution.py:217
  95.8 1.2 collective-permute-start.19
  97.0 1.4 %collective-permute-start.20 = (bf16[128,1024]{1,0:T(8,128)(2,1)S(1)}, bf16[128,1024]{1,0:T(8,128)(2,1)S(1)}, u32[]{:S(2)}, u32[]{:S(2)}) collective-permute-start(bf16[128,1024]{1,0:T(8,128)(2,1)S(1)} %get-tuple-element.36), channel_id=1, source_target_pairs={{0,17},{1,16},{2,19},{3,18},{16,1},{17,0},{18,3},{19,2},{4,21},{5,... | collective-permute-start | bytes 786440 | tf_op jit(solution)/shard_map/ppermute | solution.py:27
  98.3 2.5 %up_product.3 = (bf16[128,1024]{1,0:T(8,128)(2,1)S(1)}, bf16[128,1024]{1,0:T(8,128)(2,1)S(1)}, bf16[128,1024]{1,0:T(8,128)(2,1)S(1)}, bf16[128,1024]{1,0:T(8,128)(2,1)S(1)}) custom-call(s32[16]{0:T(128)S(1)} %add.61.labels_ref, s32[1]{0:T(128)} %bitcast.me_ref, f32[8,128]{1,0:T(8,128)S(1)} %get-tuple-element.24.ids_ref, ...), custom_call_target="tpu_custom_call" | custom-call | flops 1073741824 | bytes 3145728 | tf_op jit(solution)/shard_map/up_product/pallas_call | solution.py:217
  101.8 2.4 %collective-permute-done.17.refs_0_ = bf16[128,1024]{1,0:T(8,128)(2,1)S(1)} collective-permute-done((bf16[128,1024]{1,0:T(8,128)(2,1)S(1)}, bf16[128,1024]{1,0:T(8,128)(2,1)S(1)}, u32[]{:S(2)}, u32[]{:S(2)}) %collective-permute-start.17) | collective-permute-done | bytes 262176 | tf_op jit(solution)/shard_map/ppermute | solution.py:27
  104.2 3.0 %collective-permute-done.18.refs_1_ = bf16[128,1024]{1,0:T(8,128)(2,1)S(1)} collective-permute-done((bf16[128,1024]{1,0:T(8,128)(2,1)S(1)}, bf16[128,1024]{1,0:T(8,128)(2,1)S(1)}, u32[]{:S(2)}, u32[]{:S(2)}) %collective-permute-start.18) | collective-permute-done | bytes 262176 | tf_op jit(solution)/shard_map/ppermute | solution.py:27
  107.2 2.4 %collective-permute-start.23 = (bf16[128,1024]{1,0:T(8,128)(2,1)S(1)}, bf16[128,1024]{1,0:T(8,128)(2,1)S(1)}, u32[]{:S(2)}, u32[]{:S(2)}) collective-permute-start(bf16[128,1024]{1,0:T(8,128)(2,1)S(1)} %get-tuple-element.39), channel_id=1, source_target_pairs={{0,1},{1,0},{2,3},{3,2},{16,17},{17,16},{18,19},{19,18},{4,5},{5,4... | collective-permute-start | bytes 786440 | tf_op jit(solution)/shard_map/ppermute | solution.py:27
  109.5 5.2 %collective-permute-done.19.refs_2_ = bf16[128,1024]{1,0:T(8,128)(2,1)S(1)} collective-permute-done((bf16[128,1024]{1,0:T(8,128)(2,1)S(1)}, bf16[128,1024]{1,0:T(8,128)(2,1)S(1)}, u32[]{:S(2)}, u32[]{:S(2)}) %collective-permute-start.19) | collective-permute-done | bytes 262176 | tf_op jit(solution)/shard_map/ppermute | solution.py:27
  114.8 3.1 %collective-permute-done.20.refs_3_ = bf16[128,1024]{1,0:T(8,128)(2,1)S(1)} collective-permute-done((bf16[128,1024]{1,0:T(8,128)(2,1)S(1)}, bf16[128,1024]{1,0:T(8,128)(2,1)S(1)}, u32[]{:S(2)}, u32[]{:S(2)}) %collective-permute-start.20) | collective-permute-done | bytes 262176 | tf_op jit(solution)/shard_map/ppermute | solution.py:27
  117.9 1.5 %collective-permute-done.22.refs_5_ = bf16[128,1024]{1,0:T(8,128)(2,1)S(1)} collective-permute-done((bf16[128,1024]{1,0:T(8,128)(2,1)S(1)}, bf16[128,1024]{1,0:T(8,128)(2,1)S(1)}, u32[]{:S(2)}, u32[]{:S(2)}) %collective-permute-start.22) | collective-permute-done | bytes 262176 | tf_op jit(solution)/shard_map/ppermute | solution.py:27
  119.4 1.4 %place_results.1 = bf16[128,8192]{1,0:T(8,128)(2,1)} custom-call(s32[1]{0:T(128)} %bitcast.me_ref, bf16[128,1024]{1,0:T(8,128)(2,1)S(1)} %collective-permute-done.17.refs_0_, bf16[128,1024]{1,0:T(8,128)(2,1)S(1)} %collective-permute-done.18.refs_1_, bf16[128,1024]{1,0:T(8,128)(2,1)S(1)} %collective-permute-done.19.refs_2_, ...), custom_call_target="tpu_custom_call" | custom-call | tf_op jit(solution)/shard_map/place_results/pallas_call | solution.py:248
  (69 shorter events, 11.8 us)
Async XLA Ops:
  1.1 5.1 %collective-permute-start = (bf16[64,1024]{1,0:T(8,128)(2,1)S(1)}, bf16[64,1024]{1,0:T(8,128)(2,1)S(1)}, u32[]{:S(2)}, u32[]{:S(2)}) collective-permute-start(bf16[64,1024]{1,0:T(8,128)(2,1)S(1)} %get-tuple-element.46), channel_id=1, source_target_pairs={{0,1},{1,0},{2,3},{3,2},{4,5},{5,4},{6,7},{7,6},{8,9},{9,8},{10,11... | collective-permute-start | bytes 393224 | tf_op jit(solution)/shard_map/ppermute | solution.py:27
  1.7 11.8 %collective-permute-start.1 = (bf16[64,1024]{1,0:T(8,128)(2,1)S(1)}, bf16[64,1024]{1,0:T(8,128)(2,1)S(1)}, u32[]{:S(2)}, u32[]{:S(2)}) collective-permute-start(bf16[64,1024]{1,0:T(8,128)(2,1)S(1)} %get-tuple-element.48), channel_id=1, source_target_pairs={{0,2},{1,3},{2,0},{3,1},{4,6},{5,7},{6,4},{7,5},{8,10},{9,11},{10,... | collective-permute-start | bytes 393224 | tf_op jit(solution)/shard_map/ppermute | solution.py:27
  4.2 9.2 %collective-permute-start.2 = (bf16[64,1024]{1,0:T(8,128)(2,1)S(1)}, bf16[64,1024]{1,0:T(8,128)(2,1)S(1)}, u32[]{:S(2)}, u32[]{:S(2)}) collective-permute-start(bf16[64,1024]{1,0:T(8,128)(2,1)S(1)} %get-tuple-element.45), channel_id=1, source_target_pairs={{0,3},{1,2},{2,1},{3,0},{4,7},{5,6},{6,5},{7,4},{8,11},{9,10},{10,... | collective-permute-start | bytes 393224 | tf_op jit(solution)/shard_map/ppermute | solution.py:27
  6.3 10.7 %collective-permute-start.3 = (bf16[128,1024]{1,0:T(8,128)(2,1)S(1)}, bf16[128,1024]{1,0:T(8,128)(2,1)S(1)}, u32[]{:S(2)}, u32[]{:S(2)}) collective-permute-start(bf16[128,1024]{1,0:T(8,128)(2,1)S(1)} %join_blocks.5.refs_0_), channel_id=1, source_target_pairs={{0,4},{4,8},{8,12},{12,0},{1,5},{5,9},{9,13},{13,1},{2,6},{6,10},{... | collective-permute-start | bytes 786440 | tf_op jit(solution)/shard_map/ppermute | solution.py:31
  9.8 44.6 %all-to-all-start = ((bf16[8,136,1024]{2,1,0:T(8,128)(2,1)}), bf16[8,136,1024]{2,1,0:T(8,128)(2,1)S(1)}, u32[]{:S(2)}, u32[]{:S(2)}) async-start(bf16[8,136,1024]{2,1,0:T(8,128)(2,1)} %outgoing_rows.1), calls=%async_computation | async-start | bytes 4456448 | tf_op jit(solution)/shard_map/all_to_all | solution.py:39
  13.5 3.4 %copy-start.2 = (bf16[128,1024]{1,0:T(8,128)(2,1)}, bf16[128,1024]{1,0:T(8,128)(2,1)S(1)}, u32[]{:S(2)}) copy-start(bf16[128,1024]{1,0:T(8,128)(2,1)S(1)} %join_blocks.6.refs_1_) | copy-start | bytes 786436
  13.5 3.5 %copy-start.12 = (bf16[64,1024]{1,0:T(8,128)(2,1)S(1)}, bf16[64,1024]{1,0:T(8,128)(2,1)}, u32[]{:S(2)}) copy-start(bf16[64,1024]{1,0:T(8,128)(2,1)} %get-tuple-element.27) | copy-start | bytes 393220
  13.6 3.5 %copy-start.13 = (bf16[64,1024]{1,0:T(8,128)(2,1)S(1)}, bf16[64,1024]{1,0:T(8,128)(2,1)}, u32[]{:S(2)}) copy-start(bf16[64,1024]{1,0:T(8,128)(2,1)} %get-tuple-element.28) | copy-start | bytes 393220
  13.6 11.0 %collective-permute-start.4 = (bf16[128,1024]{1,0:T(8,128)(2,1)S(1)}, bf16[128,1024]{1,0:T(8,128)(2,1)S(1)}, u32[]{:S(2)}, u32[]{:S(2)}) collective-permute-start(bf16[128,1024]{1,0:T(8,128)(2,1)S(1)} %join_blocks.6.refs_1_), channel_id=1, source_target_pairs={{0,4},{4,8},{8,12},{12,0},{1,5},{5,9},{9,13},{13,1},{2,6},{6,10},{... | collective-permute-start | bytes 786440 | tf_op jit(solution)/shard_map/ppermute | solution.py:31
  17.0 13.2 %collective-permute-start.5 = (bf16[128,1024]{1,0:T(8,128)(2,1)S(1)}, bf16[128,1024]{1,0:T(8,128)(2,1)S(1)}, u32[]{:S(2)}, u32[]{:S(2)}) collective-permute-start(bf16[128,1024]{1,0:T(8,128)(2,1)S(1)} %join_blocks.7), channel_id=1, source_target_pairs={{0,4},{4,8},{8,12},{12,0},{1,5},{5,9},{9,13},{13,1},{2,6},{6,10},{... | collective-permute-start | bytes 786440 | tf_op jit(solution)/shard_map/ppermute | solution.py:31
  17.1 13.1 %copy-start.11 = (bf16[64,1024]{1,0:T(8,128)(2,1)S(1)}, bf16[64,1024]{1,0:T(8,128)(2,1)}, u32[]{:S(2)}) copy-start(bf16[64,1024]{1,0:T(8,128)(2,1)} %get-tuple-element.30) | copy-start | bytes 393220
  17.1 19.3 %copy-start.10 = (bf16[64,1024]{1,0:T(8,128)(2,1)S(1)}, bf16[64,1024]{1,0:T(8,128)(2,1)}, u32[]{:S(2)}) copy-start(bf16[64,1024]{1,0:T(8,128)(2,1)} %get-tuple-element.26) | copy-start | bytes 393220
  17.1 13.0 %collective-permute-start.9 = (bf16[128,1024]{1,0:T(8,128)(2,1)S(1)}, bf16[128,1024]{1,0:T(8,128)(2,1)S(1)}, u32[]{:S(2)}, u32[]{:S(2)}) collective-permute-start(bf16[128,1024]{1,0:T(8,128)(2,1)S(1)} %pad_maximum_fusion), channel_id=1, source_target_pairs={{0,1},{1,0},{2,3},{3,2},{4,5},{5,4},{6,7},{7,6},{8,9},{9,8},{10,11... | collective-permute-start | bytes 786440 | tf_op jit(solution)/shard_map/ppermute | solution.py:27
  25.2 11.1 %collective-permute-start.6 = (bf16[128,1024]{1,0:T(8,128)(2,1)S(1)}, bf16[128,1024]{1,0:T(8,128)(2,1)}, u32[]{:S(2)}, u32[]{:S(2)}) collective-permute-start(bf16[128,1024]{1,0:T(8,128)(2,1)S(1)} %join_blocks.8), channel_id=1, source_target_pairs={{0,4},{4,8},{8,12},{12,0},{1,5},{5,9},{9,13},{13,1},{2,6},{6,10},{... | collective-permute-start | bytes 786440 | tf_op jit(solution)/shard_map/ppermute | solution.py:31
  30.1 12.5 %copy-start.6 = (bf16[128,1024]{1,0:T(8,128)(2,1)}, bf16[128,1024]{1,0:T(8,128)(2,1)S(1)}, u32[]{:S(2)}) copy-start(bf16[128,1024]{1,0:T(8,128)(2,1)S(1)} %collective-permute-done.5.refs_4_) | copy-start | bytes 786436
  30.1 11.7 %collective-permute-start.7 = (bf16[128,1024]{1,0:T(8,128)(2,1)S(1)}, bf16[128,1024]{1,0:T(8,128)(2,1)S(1)}, u32[]{:S(2)}, u32[]{:S(2)}) collective-permute-start(bf16[128,1024]{1,0:T(8,128)(2,1)S(1)} %collective-permute-done.5.refs_4_), channel_id=1, source_target_pairs={{0,4},{4,8},{8,12},{12,0},{1,5},{5,9},{9,13},{13,1},{2,6},{6,10},{... | collective-permute-start | bytes 786440 | tf_op jit(solution)/shard_map/ppermute | solution.py:31
  30.9 16.8 %collective-permute-start.10 = (bf16[128,1024]{1,0:T(8,128)(2,1)}, bf16[128,1024]{1,0:T(8,128)(2,1)S(1)}, u32[]{:S(2)}, u32[]{:S(2)}) collective-permute-start(bf16[128,1024]{1,0:T(8,128)(2,1)} %pad_maximum_fusion.2), channel_id=1, source_target_pairs={{0,2},{1,3},{2,0},{3,1},{4,6},{5,7},{6,4},{7,5},{8,10},{9,11},{10,... | collective-permute-start | bytes 786440 | tf_op jit(solution)/shard_map/ppermute | solution.py:27
  36.4 11.4 %collective-permute-start.8 = (bf16[128,1024]{1,0:T(8,128)(2,1)}, bf16[128,1024]{1,0:T(8,128)(2,1)}, u32[]{:S(2)}, u32[]{:S(2)}) collective-permute-start(bf16[128,1024]{1,0:T(8,128)(2,1)} %collective-permute-done.6.refs_5_), channel_id=1, source_target_pairs={{0,4},{4,8},{8,12},{12,0},{1,5},{5,9},{9,13},{13,1},{2,6},{6,10},{... | collective-permute-start | bytes 786440 | tf_op jit(solution)/shard_map/ppermute | solution.py:31
  42.6 11.0 %collective-permute-start.11 = (bf16[128,1024]{1,0:T(8,128)(2,1)S(1)}, bf16[128,1024]{1,0:T(8,128)(2,1)S(1)}, u32[]{:S(2)}, u32[]{:S(2)}) collective-permute-start(bf16[128,1024]{1,0:T(8,128)(2,1)S(1)} %pad_maximum_fusion.1.refs_0_), channel_id=1, source_target_pairs={{0,4},{4,8},{8,12},{12,0},{1,5},{5,9},{9,13},{13,1},{2,6},{6,10},{... | collective-permute-start | bytes 786440 | tf_op jit(solution)/shard_map/ppermute | solution.py:31
  47.7 14.0 %collective-permute-start.12 = (bf16[128,1024]{1,0:T(8,128)(2,1)S(1)}, bf16[128,1024]{1,0:T(8,128)(2,1)}, u32[]{:S(2)}, u32[]{:S(2)}) collective-permute-start(bf16[128,1024]{1,0:T(8,128)(2,1)S(1)} %collective-permute-done.10.refs_1_), channel_id=1, source_target_pairs={{0,4},{4,8},{8,12},{12,0},{1,5},{5,9},{9,13},{13,1},{2,6},{6,10},{... | collective-permute-start | bytes 786440 | tf_op jit(solution)/shard_map/ppermute | solution.py:31
  54.4 9.2 %collective-permute-start.13 = (bf16[128,1024]{1,0:T(8,128)(2,1)}, bf16[128,1024]{1,0:T(8,128)(2,1)}, u32[]{:S(2)}, u32[]{:S(2)}) collective-permute-start(bf16[128,1024]{1,0:T(8,128)(2,1)} %join_blocks.9), channel_id=1, source_target_pairs={{0,4},{4,8},{8,12},{12,0},{1,5},{5,9},{9,13},{13,1},{2,6},{6,10},{... | collective-permute-start | bytes 786440 | tf_op jit(solution)/shard_map/ppermute | solution.py:31
  61.7 11.3 %collective-permute-start.14 = (bf16[128,1024]{1,0:T(8,128)(2,1)}, bf16[128,1024]{1,0:T(8,128)(2,1)S(1)}, u32[]{:S(2)}, u32[]{:S(2)}) collective-permute-start(bf16[128,1024]{1,0:T(8,128)(2,1)} %collective-permute-done.12.refs_3_), channel_id=1, source_target_pairs={{0,4},{4,8},{8,12},{12,0},{1,5},{5,9},{9,13},{13,1},{2,6},{6,10},{... | collective-permute-start | bytes 786440 | tf_op jit(solution)/shard_map/ppermute | solution.py:31
  63.6 22.7 %collective-permute-start.15 = (bf16[128,1024]{1,0:T(8,128)(2,1)}, bf16[128,1024]{1,0:T(8,128)(2,1)S(1)}, u32[]{:S(2)}, u32[]{:S(2)}) collective-permute-start(bf16[128,1024]{1,0:T(8,128)(2,1)} %collective-permute-done.13.refs_4_), channel_id=1, source_target_pairs={{0,4},{4,8},{8,12},{12,0},{1,5},{5,9},{9,13},{13,1},{2,6},{6,10},{... | collective-permute-start | bytes 786440 | tf_op jit(solution)/shard_map/ppermute | solution.py:31
  73.0 18.4 %collective-permute-start.16 = (bf16[128,1024]{1,0:T(8,128)(2,1)S(1)}, bf16[128,1024]{1,0:T(8,128)(2,1)S(1)}, u32[]{:S(2)}, u32[]{:S(2)}) collective-permute-start(bf16[128,1024]{1,0:T(8,128)(2,1)S(1)} %collective-permute-done.14.refs_5_), channel_id=1, source_target_pairs={{0,4},{4,8},{8,12},{12,0},{1,5},{5,9},{9,13},{13,1},{2,6},{6,10},{... | collective-permute-start | bytes 786440 | tf_op jit(solution)/shard_map/ppermute | solution.py:31
  82.9 8.5 %all-to-all-start.2 = ((bf16[8,64,128]{2,1,0:T(8,128)(2,1)}), bf16[8,64,128]{2,1,0:T(8,128)(2,1)S(1)}, u32[]{:S(2)}, u32[]{:S(2)}) async-start(bf16[8,64,128]{2,1,0:T(8,128)(2,1)} %summed_copies.1), calls=%async_computation.2 | async-start | bytes 262144 | tf_op jit(solution)/shard_map/all_to_all | solution.py:39
  93.9 10.3 %collective-permute-start.17 = (bf16[128,1024]{1,0:T(8,128)(2,1)S(1)}, bf16[128,1024]{1,0:T(8,128)(2,1)S(1)}, u32[]{:S(2)}, u32[]{:S(2)}) collective-permute-start(bf16[128,1024]{1,0:T(8,128)(2,1)S(1)} %get-tuple-element.33), channel_id=1, source_target_pairs={{0,18},{1,19},{2,16},{3,17},{16,2},{17,3},{18,0},{19,1},{4,22},{5,... | collective-permute-start | bytes 786440 | tf_op jit(solution)/shard_map/ppermute | solution.py:27
  94.8 12.4 %collective-permute-start.18 = (bf16[128,1024]{1,0:T(8,128)(2,1)S(1)}, bf16[128,1024]{1,0:T(8,128)(2,1)S(1)}, u32[]{:S(2)}, u32[]{:S(2)}) collective-permute-start(bf16[128,1024]{1,0:T(8,128)(2,1)S(1)} %get-tuple-element.34), channel_id=1, source_target_pairs={{0,19},{1,18},{2,17},{3,16},{16,3},{17,2},{18,1},{19,0},{4,23},{5,... | collective-permute-start | bytes 786440 | tf_op jit(solution)/shard_map/ppermute | solution.py:27
  95.8 19.0 %collective-permute-start.19 = (bf16[128,1024]{1,0:T(8,128)(2,1)S(1)}, bf16[128,1024]{1,0:T(8,128)(2,1)S(1)}, u32[]{:S(2)}, u32[]{:S(2)}) collective-permute-start(bf16[128,1024]{1,0:T(8,128)(2,1)S(1)} %get-tuple-element.35), channel_id=1, source_target_pairs={{0,16},{1,17},{2,18},{3,19},{16,0},{17,1},{18,2},{19,3},{4,20},{5,... | collective-permute-start | bytes 786440 | tf_op jit(solution)/shard_map/ppermute | solution.py:27
  97.0 20.9 %collective-permute-start.20 = (bf16[128,1024]{1,0:T(8,128)(2,1)S(1)}, bf16[128,1024]{1,0:T(8,128)(2,1)S(1)}, u32[]{:S(2)}, u32[]{:S(2)}) collective-permute-start(bf16[128,1024]{1,0:T(8,128)(2,1)S(1)} %get-tuple-element.36), channel_id=1, source_target_pairs={{0,17},{1,16},{2,19},{3,18},{16,1},{17,0},{18,3},{19,2},{4,21},{5,... | collective-permute-start | bytes 786440 | tf_op jit(solution)/shard_map/ppermute | solution.py:27
  100.8 17.1 %collective-permute-start.21 = (bf16[128,1024]{1,0:T(8,128)(2,1)S(1)}, bf16[128,1024]{1,0:T(8,128)(2,1)S(1)}, u32[]{:S(2)}, u32[]{:S(2)}) collective-permute-start(bf16[128,1024]{1,0:T(8,128)(2,1)S(1)} %get-tuple-element.37), channel_id=1, source_target_pairs={{0,2},{1,3},{2,0},{3,1},{16,18},{17,19},{18,16},{19,17},{4,6},{5,7... | collective-permute-start | bytes 786440 | tf_op jit(solution)/shard_map/ppermute | solution.py:27
  104.2 15.2 %collective-permute-start.22 = (bf16[128,1024]{1,0:T(8,128)(2,1)S(1)}, bf16[128,1024]{1,0:T(8,128)(2,1)S(1)}, u32[]{:S(2)}, u32[]{:S(2)}) collective-permute-start(bf16[128,1024]{1,0:T(8,128)(2,1)S(1)} %get-tuple-element.38), channel_id=1, source_target_pairs={{0,3},{1,2},{2,1},{3,0},{16,19},{17,18},{18,17},{19,16},{4,7},{5,6... | collective-permute-start | bytes 786440 | tf_op jit(solution)/shard_map/ppermute | solution.py:27
  107.2 12.2 %collective-permute-start.23 = (bf16[128,1024]{1,0:T(8,128)(2,1)S(1)}, bf16[128,1024]{1,0:T(8,128)(2,1)S(1)}, u32[]{:S(2)}, u32[]{:S(2)}) collective-permute-start(bf16[128,1024]{1,0:T(8,128)(2,1)S(1)} %get-tuple-element.39), channel_id=1, source_target_pairs={{0,1},{1,0},{2,3},{3,2},{16,17},{17,16},{18,19},{19,18},{4,5},{5,4... | collective-permute-start | bytes 786440 | tf_op jit(solution)/shard_map/ppermute | solution.py:27
  (8 other events, 9.0 us)

commit v26 on v21

--- a/solution.py
+++ b/solution.py
@@ -304,7 +304,7 @@
     packed, id_rows = down_product(labels, rows, down_maps, rank)
     up_near, up_far = rings(
         after(jnp.concatenate(up[:middle], axis=0), down_near[-1]),
-        jnp.concatenate([after(block, down_far[-1]) for block in up[middle:]], axis=0),
+        joined([after(block, down_far[-1]) for block in up[middle:]], SLIGHTLY_AHEAD // 4),
         SLIGHTLY_AHEAD,
         0,
         far_second_after=[packed],

time: 110 us -> 110 us (level)
  waiting for transfers between devices: 57 us -> 59.3 us
  local copies, waits for them, and re-layouts: 5.84 us -> 4 us
  starting transfers between devices: 30.3 us -> 28.7 us
    ppermute x12, waiting for transfers between devices: 32.7 us -> 35.8 us  [next_on_ring(): lax.ppermute(block, 'outer', [(i, (i + 1) % outer) for i in range(outer)])]
    ppermute x12, starting transfers between devices: 6.52 us -> 4.82 us  [next_on_ring(): lax.ppermute(block, 'outer', [(i, (i + 1) % outer) for i in range(outer)])]
    unnamed x15 -> x14, local copies, waits for them, and re-layouts: 2.86 us -> 1.94 us
    pallas_call x5 -> x6, Pallas kernels: 2.49 us -> 3.23 us  [joined(): pl.pallas_call(join_kernel, out_shape=jax.ShapeDtypeStruct((len(blocks) *...]
  transfers between devices with their start and end apart: 28 -> 28, of which waited for: 18 -> 20; matrix products, arithmetic and copies ran while one was open for 3% -> 2% of each run, Pallas kernels for 11% -> 11%
where the time goes in v26:
time: 110 us; the launch traced here: 109 us
  waiting for transfers between devices  59.3 us (54%)
  starting transfers between devices  28.7 us (26%)
  Pallas kernels  16.2 us (15%)
  local copies, waits for them, and re-layouts  4 us (4%)
    ppermute x12, waiting for transfers between devices, next_on_ring(): lax.ppermute(block, 'outer', [(i, (i + 1) % outer) for i in range(outer)])  35.8 us
    ppermute x13, waiting for transfers between devices, to_partner(): return lax.ppermute(value, axes, [(i, i ^ offset) for i in range(size)])  18.1 us
    ppermute x13, starting transfers between devices, to_partner(): return lax.ppermute(value, axes, [(i, i ^ offset) for i in range(size)])  12.3 us
    all_to_all x3, starting transfers between devices, swap(): return lax.all_to_all(value, PLANE, split_axis=0, concat_axis=0, tiled=True)  11.6 us
    all_to_all x3, waiting for transfers between devices, swap(): return lax.all_to_all(value, PLANE, split_axis=0, concat_axis=0, tiled=True)  5.38 us
    pallas_call x2, Pallas kernels, up_product(): pl.pallas_call(functools.partial(up_kernel, len(maps), rank, offsets), ou...  5.09 us
    ppermute x12, starting transfers between devices, next_on_ring(): lax.ppermute(block, 'outer', [(i, (i + 1) % outer) for i in range(outer)])  4.82 us
    pallas_call x1, Pallas kernels, down_product(): pl.pallas_call(functools.partial(down_kernel, len(maps), rank), out_shape...  4.25 us
  transfers between devices with their start and end apart: 28, of which 20 were waited for; matrix products, arithmetic and copies ran while one was open for 2% of the time, Pallas kernels for 11%

profile of v26, /device:TPU:0, one launch (start us, length us, event | category | flops | bytes accessed | tf_op | source)
XLA Modules:
  0.0 109.4 jit_solution(18377618071716989783)
XLA Ops:
  1.7 2.6 %collective-permute-start.1 = (bf16[64,1024]{1,0:T(8,128)(2,1)S(1)}, bf16[64,1024]{1,0:T(8,128)(2,1)S(1)}, u32[]{:S(2)}, u32[]{:S(2)}) collective-permute-start(bf16[64,1024]{1,0:T(8,128)(2,1)S(1)} %get-tuple-element.50), channel_id=1, source_target_pairs={{0,2},{1,3},{2,0},{3,1},{4,6},{5,7},{6,4},{7,5},{8,10},{9,11},{10,... | collective-permute-start | bytes 393224 | tf_op jit(solution)/shard_map/ppermute | solution.py:27
  4.3 1.8 %collective-permute-start.3 = (bf16[128,1024]{1,0:T(8,128)(2,1)S(1)}, bf16[128,1024]{1,0:T(8,128)(2,1)S(1)}, u32[]{:S(2)}, u32[]{:S(2)}) collective-permute-start(bf16[128,1024]{1,0:T(8,128)(2,1)S(1)} %join_blocks.6.refs_0_), channel_id=1, source_target_pairs={{0,4},{4,8},{8,12},{12,0},{1,5},{5,9},{9,13},{13,1},{2,6},{6,10},{... | collective-permute-start | bytes 786440 | tf_op jit(solution)/shard_map/ppermute | solution.py:31
  6.2 1.6 %outgoing_rows.1 = bf16[8,136,1024]{2,1,0:T(8,128)(2,1)} custom-call(bf16[128,8192]{1,0:T(8,128)(2,1)S(1)} %copy-done, s32[1,128]{1,0:T(1,128)S(1)} %bitcast.26), custom_call_target="tpu_custom_call" | custom-call | tf_op jit(solution)/shard_map/outgoing_rows/pallas_call | solution.py:94
  7.8 3.7 %all-to-all-start = ((bf16[8,136,1024]{2,1,0:T(8,128)(2,1)}), bf16[8,136,1024]{2,1,0:T(8,128)(2,1)S(1)}, u32[]{:S(2)}, u32[]{:S(2)}) async-start(bf16[8,136,1024]{2,1,0:T(8,128)(2,1)} %outgoing_rows.1), calls=%async_computation | async-start | bytes 4456448 | tf_op jit(solution)/shard_map/all_to_all | solution.py:39
  11.6 1.6 %collective-permute-start.4 = (bf16[128,1024]{1,0:T(8,128)(2,1)S(1)}, bf16[128,1024]{1,0:T(8,128)(2,1)S(1)}, u32[]{:S(2)}, u32[]{:S(2)}) collective-permute-start(bf16[128,1024]{1,0:T(8,128)(2,1)S(1)} %join_blocks.7.refs_1_), channel_id=1, source_target_pairs={{0,4},{4,8},{8,12},{12,0},{1,5},{5,9},{9,13},{13,1},{2,6},{6,10},{... | collective-permute-start | bytes 786440 | tf_op jit(solution)/shard_map/ppermute | solution.py:31
  13.2 1.8 %collective-permute-done.3.refs_0_.refs_2_ = bf16[128,1024]{1,0:T(8,128)(2,1)S(1)} collective-permute-done((bf16[128,1024]{1,0:T(8,128)(2,1)S(1)}, bf16[128,1024]{1,0:T(8,128)(2,1)S(1)}, u32[]{:S(2)}, u32[]{:S(2)}) %collective-permute-start.3) | collective-permute-done | bytes 262176 | tf_op jit(solution)/shard_map/ppermute | solution.py:31
  15.1 7.4 %collective-permute-done.4.refs_0_.refs_3_ = bf16[128,1024]{1,0:T(8,128)(2,1)S(1)} collective-permute-done((bf16[128,1024]{1,0:T(8,128)(2,1)S(1)}, bf16[128,1024]{1,0:T(8,128)(2,1)S(1)}, u32[]{:S(2)}, u32[]{:S(2)}) %collective-permute-start.4) | collective-permute-done | bytes 262176 | tf_op jit(solution)/shard_map/ppermute | solution.py:31
  23.3 4.8 %collective-permute-done.5.refs_4_ = bf16[128,1024]{1,0:T(8,128)(2,1)S(1)} collective-permute-done((bf16[128,1024]{1,0:T(8,128)(2,1)S(1)}, bf16[128,1024]{1,0:T(8,128)(2,1)S(1)}, u32[]{:S(2)}, u32[]{:S(2)}) %collective-permute-start.5) | collective-permute-done | bytes 262176 | tf_op jit(solution)/shard_map/ppermute | solution.py:31
  29.0 2.1 %collective-permute-start.10 = (bf16[64,1024]{1,0:T(8,128)(2,1)}, bf16[64,1024]{1,0:T(8,128)(2,1)}, u32[]{:S(2)}, u32[]{:S(2)}) collective-permute-start(bf16[64,1024]{1,0:T(8,128)(2,1)} %get-tuple-element.30), channel_id=1, source_target_pairs={{0,2},{1,3},{2,0},{3,1},{4,6},{5,7},{6,4},{7,5},{8,10},{9,11},{10,... | collective-permute-start | bytes 393224 | tf_op jit(solution)/shard_map/ppermute | solution.py:27
  31.3 3.3 %collective-permute-done.6.refs_5_ = bf16[128,1024]{1,0:T(8,128)(2,1)} collective-permute-done((bf16[128,1024]{1,0:T(8,128)(2,1)}, bf16[128,1024]{1,0:T(8,128)(2,1)}, u32[]{:S(2)}, u32[]{:S(2)}) %collective-permute-start.6) | collective-permute-done | bytes 262176 | tf_op jit(solution)/shard_map/ppermute | solution.py:31
  35.7 4.6 %collective-permute-done.7.refs_6_ = bf16[128,1024]{1,0:T(8,128)(2,1)} collective-permute-done((bf16[128,1024]{1,0:T(8,128)(2,1)S(1)}, bf16[128,1024]{1,0:T(8,128)(2,1)}, u32[]{:S(2)}, u32[]{:S(2)}) %collective-permute-start.7) | collective-permute-done | bytes 262176 | tf_op jit(solution)/shard_map/ppermute | solution.py:31
  40.5 1.6 %collective-permute-done.10.refs_0_ = bf16[64,1024]{1,0:T(8,128)(2,1)} collective-permute-done((bf16[64,1024]{1,0:T(8,128)(2,1)}, bf16[64,1024]{1,0:T(8,128)(2,1)}, u32[]{:S(2)}, u32[]{:S(2)}) %collective-permute-start.10) | collective-permute-done | bytes 131104 | tf_op jit(solution)/shard_map/ppermute | solution.py:27
  42.0 4.0 %collective-permute-done.8.refs_7_ = bf16[128,1024]{1,0:T(8,128)(2,1)} collective-permute-done((bf16[128,1024]{1,0:T(8,128)(2,1)}, bf16[128,1024]{1,0:T(8,128)(2,1)}, u32[]{:S(2)}, u32[]{:S(2)}) %collective-permute-start.8) | collective-permute-done | bytes 262176 | tf_op jit(solution)/shard_map/ppermute | solution.py:31
  46.1 1.7 %join_blocks.10.refs_1_ = bf16[128,1024]{1,0:T(8,128)(2,1)} custom-call(bf16[64,1024]{1,0:T(8,128)(2,1)} %collective-permute-done.10.refs_0_, bf16[64,1024]{1,0:T(8,128)(2,1)} %collective-permute-done.11.refs_1_), custom_call_target="tpu_custom_call" | custom-call | flops 1500000000 | bytes 1000000 | tf_op jit(solution)/shard_map/join_blocks/pallas_call | solution.py:60
  47.7 2.5 %collective-permute-done.12.refs_0_.refs_2_ = bf16[128,1024]{1,0:T(8,128)(2,1)S(1)} collective-permute-done((bf16[128,1024]{1,0:T(8,128)(2,1)S(1)}, bf16[128,1024]{1,0:T(8,128)(2,1)S(1)}, u32[]{:S(2)}, u32[]{:S(2)}) %collective-permute-start.12) | collective-permute-done | bytes 262176 | tf_op jit(solution)/shard_map/ppermute | solution.py:31
  52.9 4.3 %down_product.1 = (f32[8,64,128]{2,1,0:T(8,128)}, f32[8,128]{1,0:T(8,128)S(1)}) custom-call(s32[16]{0:T(128)S(1)} %add.61.labels_ref, bf16[8,136,1024]{2,1,0:T(8,128)(2,1)S(1)} %all-to-all-done.rows_ref, bf16[128,1024]{1,0:T(8,128)(2,1)S(1)} %join_blocks.6.refs_0_, bf16[128,1024]{1,0:T(8,128)(2,1)S(1)} %join_blocks.7.refs_1_, ...), custom_call_target="tpu_custom_call" | custom-call | flops 2147483648 | bytes 4194304 | tf_op jit(solution)/shard_map/down_product/pallas_call | solution.py:146
  57.1 1.4 %collective-permute-done.13.refs_3_ = bf16[128,1024]{1,0:T(8,128)(2,1)} collective-permute-done((bf16[128,1024]{1,0:T(8,128)(2,1)}, bf16[128,1024]{1,0:T(8,128)(2,1)}, u32[]{:S(2)}, u32[]{:S(2)}) %collective-permute-start.13) | collective-permute-done | bytes 262176 | tf_op jit(solution)/shard_map/ppermute | solution.py:31
  58.5 4.5 %all-to-all-start.1 = ((f32[8,64,128]{2,1,0:T(8,128)}), f32[8,64,128]{2,1,0:T(8,128)S(1)}, u32[]{:S(2)}, u32[]{:S(2)}) async-start(f32[8,64,128]{2,1,0:T(8,128)} %get-tuple-element.26), calls=%async_computation.1 | async-start | bytes 524288 | tf_op jit(solution)/shard_map/all_to_all | solution.py:39
  64.4 3.2 %collective-permute-done.15.refs_5_ = bf16[128,1024]{1,0:T(8,128)(2,1)S(1)} collective-permute-done((bf16[128,1024]{1,0:T(8,128)(2,1)}, bf16[128,1024]{1,0:T(8,128)(2,1)S(1)}, u32[]{:S(2)}, u32[]{:S(2)}) %collective-permute-start.15) | collective-permute-done | bytes 262176 | tf_op jit(solution)/shard_map/ppermute | solution.py:31
  67.6 1.4 %all-to-all-done.1.terms_ref = f32[8,64,128]{2,1,0:T(8,128)S(1)} async-done(((f32[8,64,128]{2,1,0:T(8,128)}), f32[8,64,128]{2,1,0:T(8,128)S(1)}, u32[]{:S(2)}, u32[]{:S(2)}) %all-to-all-start.1) | async-done | bytes 262176 | tf_op jit(solution)/shard_map/all_to_all | solution.py:39
  69.8 3.4 %all-to-all-start.2 = ((bf16[8,64,128]{2,1,0:T(8,128)(2,1)}), bf16[8,64,128]{2,1,0:T(8,128)(2,1)S(1)}, u32[]{:S(2)}, u32[]{:S(2)}) async-start(bf16[8,64,128]{2,1,0:T(8,128)(2,1)} %summed_copies.1), calls=%async_computation.2 | async-start | bytes 262144 | tf_op jit(solution)/shard_map/all_to_all | solution.py:39
  74.3 3.9 %all-to-all-done.2.shrunk_ref = bf16[8,64,128]{2,1,0:T(8,128)(2,1)S(1)} async-done(((bf16[8,64,128]{2,1,0:T(8,128)(2,1)}), bf16[8,64,128]{2,1,0:T(8,128)(2,1)S(1)}, u32[]{:S(2)}, u32[]{:S(2)}) %all-to-all-start.2) | async-done | bytes 131104 | tf_op jit(solution)/shard_map/all_to_all | solution.py:39
  78.2 1.4 %collective-permute-done.17.refs_7_ = bf16[128,1024]{1,0:T(8,128)(2,1)S(1)} collective-permute-done((bf16[128,1024]{1,0:T(8,128)(2,1)S(1)}, bf16[128,1024]{1,0:T(8,128)(2,1)S(1)}, u32[]{:S(2)}, u32[]{:S(2)}) %collective-permute-start.17) | collective-permute-done | bytes 262176 | tf_op jit(solution)/shard_map/ppermute | solution.py:31
  79.7 2.5 %up_product.2 = (bf16[128,1024]{1,0:T(8,128)(2,1)S(1)}, bf16[128,1024]{1,0:T(8,128)(2,1)S(1)}, bf16[128,1024]{1,0:T(8,128)(2,1)S(1)}, bf16[128,1024]{1,0:T(8,128)(2,1)S(1)}) custom-call(s32[16]{0:T(128)S(1)} %add.61.labels_ref, s32[1]{0:T(128)} %bitcast.me_ref, f32[8,128]{1,0:T(8,128)S(1)} %get-tuple-element.25.ids_ref, ...), custom_call_target="tpu_custom_call" | custom-call | flops 1073741824 | bytes 3145728 | tf_op jit(solution)/shard_map/up_product/pallas_call | solution.py:217
  82.2 2.6 %collective-permute-start.18 = (bf16[128,1024]{1,0:T(8,128)(2,1)S(1)}, bf16[128,1024]{1,0:T(8,128)(2,1)S(1)}, u32[]{:S(2)}, u32[]{:S(2)}) collective-permute-start(bf16[128,1024]{1,0:T(8,128)(2,1)S(1)} %get-tuple-element.35), channel_id=1, source_target_pairs={{0,18},{1,19},{2,16},{3,17},{16,2},{17,3},{18,0},{19,1},{4,22},{5,... | collective-permute-start | bytes 786440 | tf_op jit(solution)/shard_map/ppermute | solution.py:27
  86.7 2.5 %up_product.3 = (bf16[128,1024]{1,0:T(8,128)(2,1)S(1)}, bf16[128,1024]{1,0:T(8,128)(2,1)S(1)}, bf16[128,1024]{1,0:T(8,128)(2,1)S(1)}, bf16[128,1024]{1,0:T(8,128)(2,1)S(1)}) custom-call(s32[16]{0:T(128)S(1)} %add.61.labels_ref, s32[1]{0:T(128)} %bitcast.me_ref, f32[8,128]{1,0:T(8,128)S(1)} %get-tuple-element.25.ids_ref, ...), custom_call_target="tpu_custom_call" | custom-call | flops 1073741824 | bytes 3145728 | tf_op jit(solution)/shard_map/up_product/pallas_call | solution.py:217
  89.2 1.7 %collective-permute-start.22 = (bf16[128,1024]{1,0:T(8,128)(2,1)S(1)}, bf16[128,1024]{1,0:T(8,128)(2,1)S(1)}, u32[]{:S(2)}, u32[]{:S(2)}) collective-permute-start(bf16[128,1024]{1,0:T(8,128)(2,1)S(1)} %get-tuple-element.39), channel_id=1, source_target_pairs={{0,2},{1,3},{2,0},{3,1},{16,18},{17,19},{18,16},{19,17},{4,6},{5,7... | collective-permute-start | bytes 786440 | tf_op jit(solution)/shard_map/ppermute | solution.py:27
  90.9 1.4 %collective-permute-done.18.refs_0_ = bf16[128,1024]{1,0:T(8,128)(2,1)S(1)} collective-permute-done((bf16[128,1024]{1,0:T(8,128)(2,1)S(1)}, bf16[128,1024]{1,0:T(8,128)(2,1)S(1)}, u32[]{:S(2)}, u32[]{:S(2)}) %collective-permute-start.18) | collective-permute-done | bytes 262176 | tf_op jit(solution)/shard_map/ppermute | solution.py:27
  92.4 4.9 %collective-permute-done.19.refs_1_ = bf16[128,1024]{1,0:T(8,128)(2,1)S(1)} collective-permute-done((bf16[128,1024]{1,0:T(8,128)(2,1)S(1)}, bf16[128,1024]{1,0:T(8,128)(2,1)S(1)}, u32[]{:S(2)}, u32[]{:S(2)}) %collective-permute-start.19) | collective-permute-done | bytes 262176 | tf_op jit(solution)/shard_map/ppermute | solution.py:27
  97.8 6.0 %collective-permute-done.20.refs_2_ = bf16[128,1024]{1,0:T(8,128)(2,1)S(1)} collective-permute-done((bf16[128,1024]{1,0:T(8,128)(2,1)S(1)}, bf16[128,1024]{1,0:T(8,128)(2,1)S(1)}, u32[]{:S(2)}, u32[]{:S(2)}) %collective-permute-start.20) | collective-permute-done | bytes 262176 | tf_op jit(solution)/shard_map/ppermute | solution.py:27
  103.9 2.8 %collective-permute-done.21.refs_3_ = bf16[128,1024]{1,0:T(8,128)(2,1)S(1)} collective-permute-done((bf16[128,1024]{1,0:T(8,128)(2,1)S(1)}, bf16[128,1024]{1,0:T(8,128)(2,1)S(1)}, u32[]{:S(2)}, u32[]{:S(2)}) %collective-permute-start.21) | collective-permute-done | bytes 262176 | tf_op jit(solution)/shard_map/ppermute | solution.py:27
  108.0 1.4 %place_results.1 = bf16[128,8192]{1,0:T(8,128)(2,1)} custom-call(s32[1]{0:T(128)} %bitcast.me_ref, bf16[128,1024]{1,0:T(8,128)(2,1)S(1)} %collective-permute-done.18.refs_0_, bf16[128,1024]{1,0:T(8,128)(2,1)S(1)} %collective-permute-done.19.refs_1_, bf16[128,1024]{1,0:T(8,128)(2,1)S(1)} %collective-permute-done.20.refs_2_, ...), custom_call_target="tpu_custom_call" | custom-call | tf_op jit(solution)/shard_map/place_results/pallas_call | solution.py:248
  (56 shorter events, 14.4 us)
Async XLA Ops:
  1.1 3.2 %collective-permute-start = (bf16[64,1024]{1,0:T(8,128)(2,1)S(1)}, bf16[64,1024]{1,0:T(8,128)(2,1)S(1)}, u32[]{:S(2)}, u32[]{:S(2)}) collective-permute-start(bf16[64,1024]{1,0:T(8,128)(2,1)S(1)} %get-tuple-element.48), channel_id=1, source_target_pairs={{0,1},{1,0},{2,3},{3,2},{4,5},{5,4},{6,7},{7,6},{8,9},{9,8},{10,11... | collective-permute-start | bytes 393224 | tf_op jit(solution)/shard_map/ppermute | solution.py:27
  1.7 9.9 %collective-permute-start.1 = (bf16[64,1024]{1,0:T(8,128)(2,1)S(1)}, bf16[64,1024]{1,0:T(8,128)(2,1)S(1)}, u32[]{:S(2)}, u32[]{:S(2)}) collective-permute-start(bf16[64,1024]{1,0:T(8,128)(2,1)S(1)} %get-tuple-element.50), channel_id=1, source_target_pairs={{0,2},{1,3},{2,0},{3,1},{4,6},{5,7},{6,4},{7,5},{8,10},{9,11},{10,... | collective-permute-start | bytes 393224 | tf_op jit(solution)/shard_map/ppermute | solution.py:27
  4.2 7.3 %collective-permute-start.2 = (bf16[64,1024]{1,0:T(8,128)(2,1)S(1)}, bf16[64,1024]{1,0:T(8,128)(2,1)S(1)}, u32[]{:S(2)}, u32[]{:S(2)}) collective-permute-start(bf16[64,1024]{1,0:T(8,128)(2,1)S(1)} %get-tuple-element.47), channel_id=1, source_target_pairs={{0,3},{1,2},{2,1},{3,0},{4,7},{5,6},{6,5},{7,4},{8,11},{9,10},{10,... | collective-permute-start | bytes 393224 | tf_op jit(solution)/shard_map/ppermute | solution.py:27
  4.3 1.9 %copy-start = (bf16[128,8192]{1,0:T(8,128)(2,1)S(1)}, bf16[128,8192]{1,0:T(8,128)(2,1)}, u32[]{:S(2)}) copy-start(bf16[128,8192]{1,0:T(8,128)(2,1)} %hidden_ref) | copy-start | bytes 6291460
  4.3 1.9 %copy-start.1 = (s32[128,1]{0,1:T(1,128)S(1)}, s32[128,1]{0,1:T(1,128)}, u32[]{:S(2)}) copy-start(s32[128,1]{0,1:T(1,128)} %param.4) | copy-start | bytes 1540
  4.3 10.7 %collective-permute-start.3 = (bf16[128,1024]{1,0:T(8,128)(2,1)S(1)}, bf16[128,1024]{1,0:T(8,128)(2,1)S(1)}, u32[]{:S(2)}, u32[]{:S(2)}) collective-permute-start(bf16[128,1024]{1,0:T(8,128)(2,1)S(1)} %join_blocks.6.refs_0_), channel_id=1, source_target_pairs={{0,4},{4,8},{8,12},{12,0},{1,5},{5,9},{9,13},{13,1},{2,6},{6,10},{... | collective-permute-start | bytes 786440 | tf_op jit(solution)/shard_map/ppermute | solution.py:31
  7.8 43.2 %all-to-all-start = ((bf16[8,136,1024]{2,1,0:T(8,128)(2,1)}), bf16[8,136,1024]{2,1,0:T(8,128)(2,1)S(1)}, u32[]{:S(2)}, u32[]{:S(2)}) async-start(bf16[8,136,1024]{2,1,0:T(8,128)(2,1)} %outgoing_rows.1), calls=%async_computation | async-start | bytes 4456448 | tf_op jit(solution)/shard_map/all_to_all | solution.py:39
  11.6 11.0 %collective-permute-start.4 = (bf16[128,1024]{1,0:T(8,128)(2,1)S(1)}, bf16[128,1024]{1,0:T(8,128)(2,1)S(1)}, u32[]{:S(2)}, u32[]{:S(2)}) collective-permute-start(bf16[128,1024]{1,0:T(8,128)(2,1)S(1)} %join_blocks.7.refs_1_), channel_id=1, source_target_pairs={{0,4},{4,8},{8,12},{12,0},{1,5},{5,9},{9,13},{13,1},{2,6},{6,10},{... | collective-permute-start | bytes 786440 | tf_op jit(solution)/shard_map/ppermute | solution.py:31
  15.0 13.1 %copy-start.6 = (bf16[1,64,8192]{2,1,0:T(8,128)(2,1)S(1)}, bf16[1,64,8192]{2,1,0:T(8,128)(2,1)}, u32[]{:S(2)}) copy-start(bf16[1,64,8192]{2,1,0:T(8,128)(2,1)} %param.7) | copy-start | bytes 3145732
  15.1 13.1 %collective-permute-start.5 = (bf16[128,1024]{1,0:T(8,128)(2,1)S(1)}, bf16[128,1024]{1,0:T(8,128)(2,1)S(1)}, u32[]{:S(2)}, u32[]{:S(2)}) collective-permute-start(bf16[128,1024]{1,0:T(8,128)(2,1)S(1)} %join_blocks.8), channel_id=1, source_target_pairs={{0,4},{4,8},{8,12},{12,0},{1,5},{5,9},{9,13},{13,1},{2,6},{6,10},{... | collective-permute-start | bytes 786440 | tf_op jit(solution)/shard_map/ppermute | solution.py:31
  23.3 11.4 %collective-permute-start.6 = (bf16[128,1024]{1,0:T(8,128)(2,1)}, bf16[128,1024]{1,0:T(8,128)(2,1)}, u32[]{:S(2)}, u32[]{:S(2)}) collective-permute-start(bf16[128,1024]{1,0:T(8,128)(2,1)} %join_blocks.9), channel_id=1, source_target_pairs={{0,4},{4,8},{8,12},{12,0},{1,5},{5,9},{9,13},{13,1},{2,6},{6,10},{... | collective-permute-start | bytes 786440 | tf_op jit(solution)/shard_map/ppermute | solution.py:31
  28.2 7.5 %copy-start.4 = (bf16[128,1024]{1,0:T(8,128)(2,1)}, bf16[128,1024]{1,0:T(8,128)(2,1)S(1)}, u32[]{:S(2)}) copy-start(bf16[128,1024]{1,0:T(8,128)(2,1)S(1)} %collective-permute-done.5.refs_4_) | copy-start | bytes 786436
  28.2 12.1 %collective-permute-start.7 = (bf16[128,1024]{1,0:T(8,128)(2,1)S(1)}, bf16[128,1024]{1,0:T(8,128)(2,1)}, u32[]{:S(2)}, u32[]{:S(2)}) collective-permute-start(bf16[128,1024]{1,0:T(8,128)(2,1)S(1)} %collective-permute-done.5.refs_4_), channel_id=1, source_target_pairs={{0,4},{4,8},{8,12},{12,0},{1,5},{5,9},{9,13},{13,1},{2,6},{6,10},{... | collective-permute-start | bytes 786440 | tf_op jit(solution)/shard_map/ppermute | solution.py:31
  29.0 5.7 %collective-permute-start.9 = (bf16[64,1024]{1,0:T(8,128)(2,1)S(1)}, bf16[64,1024]{1,0:T(8,128)(2,1)}, u32[]{:S(2)}, u32[]{:S(2)}) collective-permute-start(bf16[64,1024]{1,0:T(8,128)(2,1)S(1)} %get-tuple-element.28), channel_id=1, source_target_pairs={{0,1},{1,0},{2,3},{3,2},{4,5},{5,4},{6,7},{7,6},{8,9},{9,8},{10,11... | collective-permute-start | bytes 393224 | tf_op jit(solution)/shard_map/ppermute | solution.py:27
  29.0 13.0 %collective-permute-start.10 = (bf16[64,1024]{1,0:T(8,128)(2,1)}, bf16[64,1024]{1,0:T(8,128)(2,1)}, u32[]{:S(2)}, u32[]{:S(2)}) collective-permute-start(bf16[64,1024]{1,0:T(8,128)(2,1)} %get-tuple-element.30), channel_id=1, source_target_pairs={{0,2},{1,3},{2,0},{3,1},{4,6},{5,7},{6,4},{7,5},{8,10},{9,11},{10,... | collective-permute-start | bytes 393224 | tf_op jit(solution)/shard_map/ppermute | solution.py:27
  31.2 14.9 %collective-permute-start.11 = (bf16[64,1024]{1,0:T(8,128)(2,1)}, bf16[64,1024]{1,0:T(8,128)(2,1)}, u32[]{:S(2)}, u32[]{:S(2)}) collective-permute-start(bf16[64,1024]{1,0:T(8,128)(2,1)} %get-tuple-element.32), channel_id=1, source_target_pairs={{0,3},{1,2},{2,1},{3,0},{4,7},{5,6},{6,5},{7,4},{8,11},{9,10},{10,... | collective-permute-start | bytes 393224 | tf_op jit(solution)/shard_map/ppermute | solution.py:27
  34.7 11.4 %collective-permute-start.8 = (bf16[128,1024]{1,0:T(8,128)(2,1)}, bf16[128,1024]{1,0:T(8,128)(2,1)}, u32[]{:S(2)}, u32[]{:S(2)}) collective-permute-start(bf16[128,1024]{1,0:T(8,128)(2,1)} %collective-permute-done.6.refs_5_), channel_id=1, source_target_pairs={{0,4},{4,8},{8,12},{12,0},{1,5},{5,9},{9,13},{13,1},{2,6},{6,10},{... | collective-permute-start | bytes 786440 | tf_op jit(solution)/shard_map/ppermute | solution.py:31
  40.3 9.9 %collective-permute-start.12 = (bf16[128,1024]{1,0:T(8,128)(2,1)S(1)}, bf16[128,1024]{1,0:T(8,128)(2,1)S(1)}, u32[]{:S(2)}, u32[]{:S(2)}) collective-permute-start(bf16[128,1024]{1,0:T(8,128)(2,1)S(1)} %pad_maximum_fusion.refs_0_), channel_id=1, source_target_pairs={{0,4},{4,8},{8,12},{12,0},{1,5},{5,9},{9,13},{13,1},{2,6},{6,10},{... | collective-permute-start | bytes 786440 | tf_op jit(solution)/shard_map/ppermute | solution.py:31
  47.7 10.8 %collective-permute-start.13 = (bf16[128,1024]{1,0:T(8,128)(2,1)}, bf16[128,1024]{1,0:T(8,128)(2,1)}, u32[]{:S(2)}, u32[]{:S(2)}) collective-permute-start(bf16[128,1024]{1,0:T(8,128)(2,1)} %join_blocks.10.refs_1_), channel_id=1, source_target_pairs={{0,4},{4,8},{8,12},{12,0},{1,5},{5,9},{9,13},{13,1},{2,6},{6,10},{... | collective-permute-start | bytes 786440 | tf_op jit(solution)/shard_map/ppermute | solution.py:31
  51.0 12.2 %collective-permute-start.14 = (bf16[128,1024]{1,0:T(8,128)(2,1)}, bf16[128,1024]{1,0:T(8,128)(2,1)}, u32[]{:S(2)}, u32[]{:S(2)}) collective-permute-start(bf16[128,1024]{1,0:T(8,128)(2,1)} %join_blocks.11), channel_id=1, source_target_pairs={{0,4},{4,8},{8,12},{12,0},{1,5},{5,9},{9,13},{13,1},{2,6},{6,10},{... | collective-permute-start | bytes 786440 | tf_op jit(solution)/shard_map/ppermute | solution.py:31
  58.5 9.1 %collective-permute-start.15 = (bf16[128,1024]{1,0:T(8,128)(2,1)}, bf16[128,1024]{1,0:T(8,128)(2,1)S(1)}, u32[]{:S(2)}, u32[]{:S(2)}) collective-permute-start(bf16[128,1024]{1,0:T(8,128)(2,1)} %collective-permute-done.13.refs_3_), channel_id=1, source_target_pairs={{0,4},{4,8},{8,12},{12,0},{1,5},{5,9},{9,13},{13,1},{2,6},{6,10},{... | collective-permute-start | bytes 786440 | tf_op jit(solution)/shard_map/ppermute | solution.py:31
  58.5 10.5 %all-to-all-start.1 = ((f32[8,64,128]{2,1,0:T(8,128)}), f32[8,64,128]{2,1,0:T(8,128)S(1)}, u32[]{:S(2)}, u32[]{:S(2)}) async-start(f32[8,64,128]{2,1,0:T(8,128)} %get-tuple-element.26), calls=%async_computation.1 | async-start | bytes 524288 | tf_op jit(solution)/shard_map/all_to_all | solution.py:39
  63.1 11.2 %collective-permute-start.16 = (bf16[128,1024]{1,0:T(8,128)(2,1)}, bf16[128,1024]{1,0:T(8,128)(2,1)S(1)}, u32[]{:S(2)}, u32[]{:S(2)}) collective-permute-start(bf16[128,1024]{1,0:T(8,128)(2,1)} %collective-permute-done.14.refs_4_), channel_id=1, source_target_pairs={{0,4},{4,8},{8,12},{12,0},{1,5},{5,9},{9,13},{13,1},{2,6},{6,10},{... | collective-permute-start | bytes 786440 | tf_op jit(solution)/shard_map/ppermute | solution.py:31
  67.6 12.0 %collective-permute-start.17 = (bf16[128,1024]{1,0:T(8,128)(2,1)S(1)}, bf16[128,1024]{1,0:T(8,128)(2,1)S(1)}, u32[]{:S(2)}, u32[]{:S(2)}) collective-permute-start(bf16[128,1024]{1,0:T(8,128)(2,1)S(1)} %collective-permute-done.15.refs_5_), channel_id=1, source_target_pairs={{0,4},{4,8},{8,12},{12,0},{1,5},{5,9},{9,13},{13,1},{2,6},{6,10},{... | collective-permute-start | bytes 786440 | tf_op jit(solution)/shard_map/ppermute | solution.py:31
  69.8 8.5 %all-to-all-start.2 = ((bf16[8,64,128]{2,1,0:T(8,128)(2,1)}), bf16[8,64,128]{2,1,0:T(8,128)(2,1)S(1)}, u32[]{:S(2)}, u32[]{:S(2)}) async-start(bf16[8,64,128]{2,1,0:T(8,128)(2,1)} %summed_copies.1), calls=%async_computation.2 | async-start | bytes 262144 | tf_op jit(solution)/shard_map/all_to_all | solution.py:39
  82.2 10.2 %collective-permute-start.18 = (bf16[128,1024]{1,0:T(8,128)(2,1)S(1)}, bf16[128,1024]{1,0:T(8,128)(2,1)S(1)}, u32[]{:S(2)}, u32[]{:S(2)}) collective-permute-start(bf16[128,1024]{1,0:T(8,128)(2,1)S(1)} %get-tuple-element.35), channel_id=1, source_target_pairs={{0,18},{1,19},{2,16},{3,17},{16,2},{17,3},{18,0},{19,1},{4,22},{5,... | collective-permute-start | bytes 786440 | tf_op jit(solution)/shard_map/ppermute | solution.py:27
  84.8 12.4 %collective-permute-start.19 = (bf16[128,1024]{1,0:T(8,128)(2,1)S(1)}, bf16[128,1024]{1,0:T(8,128)(2,1)S(1)}, u32[]{:S(2)}, u32[]{:S(2)}) collective-permute-start(bf16[128,1024]{1,0:T(8,128)(2,1)S(1)} %get-tuple-element.36), channel_id=1, source_target_pairs={{0,19},{1,18},{2,17},{3,16},{16,3},{17,2},{18,1},{19,0},{4,23},{5,... | collective-permute-start | bytes 786440 | tf_op jit(solution)/shard_map/ppermute | solution.py:27
  84.8 19.1 %collective-permute-start.20 = (bf16[128,1024]{1,0:T(8,128)(2,1)S(1)}, bf16[128,1024]{1,0:T(8,128)(2,1)S(1)}, u32[]{:S(2)}, u32[]{:S(2)}) collective-permute-start(bf16[128,1024]{1,0:T(8,128)(2,1)S(1)} %get-tuple-element.37), channel_id=1, source_target_pairs={{0,16},{1,17},{2,18},{3,19},{16,0},{17,1},{18,2},{19,3},{4,20},{5,... | collective-permute-start | bytes 786440 | tf_op jit(solution)/shard_map/ppermute | solution.py:27
  85.4 21.3 %collective-permute-start.21 = (bf16[128,1024]{1,0:T(8,128)(2,1)S(1)}, bf16[128,1024]{1,0:T(8,128)(2,1)S(1)}, u32[]{:S(2)}, u32[]{:S(2)}) collective-permute-start(bf16[128,1024]{1,0:T(8,128)(2,1)S(1)} %get-tuple-element.38), channel_id=1, source_target_pairs={{0,17},{1,16},{2,19},{3,18},{16,1},{17,0},{18,3},{19,2},{4,21},{5,... | collective-permute-start | bytes 786440 | tf_op jit(solution)/shard_map/ppermute | solution.py:27
  89.2 17.5 %collective-permute-start.22 = (bf16[128,1024]{1,0:T(8,128)(2,1)S(1)}, bf16[128,1024]{1,0:T(8,128)(2,1)S(1)}, u32[]{:S(2)}, u32[]{:S(2)}) collective-permute-start(bf16[128,1024]{1,0:T(8,128)(2,1)S(1)} %get-tuple-element.39), channel_id=1, source_target_pairs={{0,2},{1,3},{2,0},{3,1},{16,18},{17,19},{18,16},{19,17},{4,6},{5,7... | collective-permute-start | bytes 786440 | tf_op jit(solution)/shard_map/ppermute | solution.py:27
  92.4 15.6 %collective-permute-start.23 = (bf16[128,1024]{1,0:T(8,128)(2,1)S(1)}, bf16[128,1024]{1,0:T(8,128)(2,1)S(1)}, u32[]{:S(2)}, u32[]{:S(2)}) collective-permute-start(bf16[128,1024]{1,0:T(8,128)(2,1)S(1)} %get-tuple-element.40), channel_id=1, source_target_pairs={{0,3},{1,2},{2,1},{3,0},{16,19},{17,18},{18,17},{19,16},{4,7},{5,6... | collective-permute-start | bytes 786440 | tf_op jit(solution)/shard_map/ppermute | solution.py:27
  97.3 10.7 %collective-permute-start.24 = (bf16[128,1024]{1,0:T(8,128)(2,1)S(1)}, bf16[128,1024]{1,0:T(8,128)(2,1)S(1)}, u32[]{:S(2)}, u32[]{:S(2)}) collective-permute-start(bf16[128,1024]{1,0:T(8,128)(2,1)S(1)} %get-tuple-element.41), channel_id=1, source_target_pairs={{0,1},{1,0},{2,3},{3,2},{16,17},{17,16},{18,19},{19,18},{4,5},{5,4... | collective-permute-start | bytes 786440 | tf_op jit(solution)/shard_map/ppermute | solution.py:27
  (3 other events, 2.7 us)

commit v27 on v26

--- a/solution.py
+++ b/solution.py
@@ -304,7 +304,7 @@
     packed, id_rows = down_product(labels, rows, down_maps, rank)
     up_near, up_far = rings(
         after(jnp.concatenate(up[:middle], axis=0), down_near[-1]),
-        joined([after(block, down_far[-1]) for block in up[middle:]], SLIGHTLY_AHEAD // 4),
+        joined([after(block, down_near[-1]) for block in up[middle:]], SLIGHTLY_AHEAD // 4),
         SLIGHTLY_AHEAD,
         0,
         far_second_after=[packed],

time: 110 us -> 115 us (1.045)
  local copies, waits for them, and re-layouts: 4 us -> 7.34 us
  waiting for transfers between devices: 59.3 us -> 62.5 us
    ppermute x12, waiting for transfers between devices: 35.8 us -> 40.5 us  [next_on_ring(): lax.ppermute(block, 'outer', [(i, (i + 1) % outer) for i in range(outer)])]
    unnamed x14 -> x16, local copies, waits for them, and re-layouts: 1.94 us -> 4.28 us
    ppermute x13, waiting for transfers between devices: 18.1 us -> 16.5 us  [to_partner(): return lax.ppermute(value, axes, [(i, i ^ offset) for i in range(size)])]
  transfers between devices with their start and end apart: 28 -> 28, of which waited for: 20 -> 17; matrix products, arithmetic and copies ran while one was open for 2% -> 2% of each run, Pallas kernels for 11% -> 11%
where the time goes in v27:
time: 115 us; the launch traced here: 114 us
  waiting for transfers between devices  62.5 us (54%)
  starting transfers between devices  28.2 us (25%)
  Pallas kernels  16.1 us (14%)
  local copies, waits for them, and re-layouts  7.34 us (6%)
    ppermute x12, waiting for transfers between devices, next_on_ring(): lax.ppermute(block, 'outer', [(i, (i + 1) % outer) for i in range(outer)])  40.5 us
    ppermute x13, waiting for transfers between devices, to_partner(): return lax.ppermute(value, axes, [(i, i ^ offset) for i in range(size)])  16.5 us
    ppermute x13, starting transfers between devices, to_partner(): return lax.ppermute(value, axes, [(i, i ^ offset) for i in range(size)])  11.6 us
    all_to_all x3, starting transfers between devices, swap(): return lax.all_to_all(value, PLANE, split_axis=0, concat_axis=0, tiled=True)  11 us
    ppermute x12, starting transfers between devices, next_on_ring(): lax.ppermute(block, 'outer', [(i, (i + 1) % outer) for i in range(outer)])  5.59 us
    all_to_all x3, waiting for transfers between devices, swap(): return lax.all_to_all(value, PLANE, split_axis=0, concat_axis=0, tiled=True)  5.53 us
    pallas_call x2, Pallas kernels, up_product(): pl.pallas_call(functools.partial(up_kernel, len(maps), rank, offsets), ou...  5.1 us
    unnamed x16, local copies, waits for them, and re-layouts  4.28 us
  transfers between devices with their start and end apart: 28, of which 17 were waited for; matrix products, arithmetic and copies ran while one was open for 2% of the time, Pallas kernels for 11%

profile of v27, /device:TPU:0, one launch (start us, length us, event | category | flops | bytes accessed | tf_op | source)
XLA Modules:
  0.0 114.5 jit_solution(12627673900349776098)
XLA Ops:
  1.7 2.6 %collective-permute-start.1 = (bf16[64,1024]{1,0:T(8,128)(2,1)S(1)}, bf16[64,1024]{1,0:T(8,128)(2,1)S(1)}, u32[]{:S(2)}, u32[]{:S(2)}) collective-permute-start(bf16[64,1024]{1,0:T(8,128)(2,1)S(1)} %get-tuple-element.50), channel_id=1, source_target_pairs={{0,2},{1,3},{2,0},{3,1},{4,6},{5,7},{6,4},{7,5},{8,10},{9,11},{10,... | collective-permute-start | bytes 393224 | tf_op jit(solution)/shard_map/ppermute | solution.py:27
  4.3 1.8 %collective-permute-start.3 = (bf16[128,1024]{1,0:T(8,128)(2,1)S(1)}, bf16[128,1024]{1,0:T(8,128)(2,1)S(1)}, u32[]{:S(2)}, u32[]{:S(2)}) collective-permute-start(bf16[128,1024]{1,0:T(8,128)(2,1)S(1)} %join_blocks.6.refs_0_), channel_id=1, source_target_pairs={{0,4},{4,8},{8,12},{12,0},{1,5},{5,9},{9,13},{13,1},{2,6},{6,10},{... | collective-permute-start | bytes 786440 | tf_op jit(solution)/shard_map/ppermute | solution.py:31
  6.2 1.6 %outgoing_rows.1 = bf16[8,136,1024]{2,1,0:T(8,128)(2,1)} custom-call(bf16[128,8192]{1,0:T(8,128)(2,1)S(1)} %copy-done, s32[1,128]{1,0:T(1,128)S(1)} %bitcast.26), custom_call_target="tpu_custom_call" | custom-call | tf_op jit(solution)/shard_map/outgoing_rows/pallas_call | solution.py:94
  7.8 3.7 %all-to-all-start = ((bf16[8,136,1024]{2,1,0:T(8,128)(2,1)}), bf16[8,136,1024]{2,1,0:T(8,128)(2,1)S(1)}, u32[]{:S(2)}, u32[]{:S(2)}) async-start(bf16[8,136,1024]{2,1,0:T(8,128)(2,1)} %outgoing_rows.1), calls=%async_computation | async-start | bytes 4456448 | tf_op jit(solution)/shard_map/all_to_all | solution.py:39
  11.6 1.6 %collective-permute-start.4 = (bf16[128,1024]{1,0:T(8,128)(2,1)S(1)}, bf16[128,1024]{1,0:T(8,128)(2,1)S(1)}, u32[]{:S(2)}, u32[]{:S(2)}) collective-permute-start(bf16[128,1024]{1,0:T(8,128)(2,1)S(1)} %join_blocks.7.refs_1_), channel_id=1, source_target_pairs={{0,4},{4,8},{8,12},{12,0},{1,5},{5,9},{9,13},{13,1},{2,6},{6,10},{... | collective-permute-start | bytes 786440 | tf_op jit(solution)/shard_map/ppermute | solution.py:31
  13.2 1.8 %collective-permute-done.3.refs_0_.refs_2_ = bf16[128,1024]{1,0:T(8,128)(2,1)S(1)} collective-permute-done((bf16[128,1024]{1,0:T(8,128)(2,1)S(1)}, bf16[128,1024]{1,0:T(8,128)(2,1)S(1)}, u32[]{:S(2)}, u32[]{:S(2)}) %collective-permute-start.3) | collective-permute-done | bytes 262176 | tf_op jit(solution)/shard_map/ppermute | solution.py:31
  15.1 1.9 %dynamic-slice_bitcast_fusion = (bf16[64,1024]{1,0:T(8,128)(2,1)}, bf16[64,1024]{1,0:T(8,128)(2,1)S(1)}, bf16[64,1024]{1,0:T(8,128)(2,1)S(1)}, bf16[64,1024]{1,0:T(8,128)(2,1)}) fusion(bf16[1,64,8192]{2,1,0:T(8,128)(2,1)} %param.7, s32[]{:T(128)S(6)} %select_n.32, s32[]{:T(128)S(6)} %select_n.30, s32[]{:T(128)S(6)} %select_n.29, s32[]{:T(128)S(6)} %select_n.31), kind=kLoop, calls=%fused_computation.1 | loop fusion | bytes 1048592 | tf_op jit(solution)/shard_map/dynamic_slice | solution.py:270
  17.0 5.6 %collective-permute-done.4.refs_0_.refs_3_ = bf16[128,1024]{1,0:T(8,128)(2,1)S(1)} collective-permute-done((bf16[128,1024]{1,0:T(8,128)(2,1)S(1)}, bf16[128,1024]{1,0:T(8,128)(2,1)S(1)}, u32[]{:S(2)}, u32[]{:S(2)}) %collective-permute-start.4) | collective-permute-done | bytes 262176 | tf_op jit(solution)/shard_map/ppermute | solution.py:31
  22.5 5.3 %collective-permute-done.5.refs_4_ = bf16[128,1024]{1,0:T(8,128)(2,1)} collective-permute-done((bf16[128,1024]{1,0:T(8,128)(2,1)S(1)}, bf16[128,1024]{1,0:T(8,128)(2,1)}, u32[]{:S(2)}, u32[]{:S(2)}) %collective-permute-start.5) | collective-permute-done | bytes 262176 | tf_op jit(solution)/shard_map/ppermute | solution.py:31
  28.6 1.4 %collective-permute-start.6 = (bf16[128,1024]{1,0:T(8,128)(2,1)}, bf16[128,1024]{1,0:T(8,128)(2,1)}, u32[]{:S(2)}, u32[]{:S(2)}) collective-permute-start(bf16[128,1024]{1,0:T(8,128)(2,1)} %join_blocks.9), channel_id=1, source_target_pairs={{0,4},{4,8},{8,12},{12,0},{1,5},{5,9},{9,13},{13,1},{2,6},{6,10},{... | collective-permute-start | bytes 786440 | tf_op jit(solution)/shard_map/ppermute | solution.py:31
  29.9 1.7 %collective-permute-start.10 = (bf16[64,1024]{1,0:T(8,128)(2,1)}, bf16[64,1024]{1,0:T(8,128)(2,1)}, u32[]{:S(2)}, u32[]{:S(2)}) collective-permute-start(bf16[64,1024]{1,0:T(8,128)(2,1)} %get-tuple-element.30), channel_id=1, source_target_pairs={{0,2},{1,3},{2,0},{3,1},{4,6},{5,7},{6,4},{7,5},{8,10},{9,11},{10,... | collective-permute-start | bytes 393224 | tf_op jit(solution)/shard_map/ppermute | solution.py:27
  31.6 7.4 %collective-permute-done.7.refs_6_ = bf16[128,1024]{1,0:T(8,128)(2,1)S(1)} collective-permute-done((bf16[128,1024]{1,0:T(8,128)(2,1)}, bf16[128,1024]{1,0:T(8,128)(2,1)S(1)}, u32[]{:S(2)}, u32[]{:S(2)}) %collective-permute-start.7) | collective-permute-done | bytes 262176 | tf_op jit(solution)/shard_map/ppermute | solution.py:31
  39.9 4.9 %collective-permute-done.6.refs_5_ = bf16[128,1024]{1,0:T(8,128)(2,1)} collective-permute-done((bf16[128,1024]{1,0:T(8,128)(2,1)}, bf16[128,1024]{1,0:T(8,128)(2,1)}, u32[]{:S(2)}, u32[]{:S(2)}) %collective-permute-start.6) | collective-permute-done | bytes 262176 | tf_op jit(solution)/shard_map/ppermute | solution.py:31
  44.8 1.7 %join_blocks.10.refs_1_ = bf16[128,1024]{1,0:T(8,128)(2,1)} custom-call(bf16[64,1024]{1,0:T(8,128)(2,1)} %collective-permute-done.10.refs_0_, bf16[64,1024]{1,0:T(8,128)(2,1)} %collective-permute-done.11.refs_1_), custom_call_target="tpu_custom_call" | custom-call | flops 1500000000 | bytes 1000000 | tf_op jit(solution)/shard_map/join_blocks/pallas_call | solution.py:60
  47.2 3.7 %collective-permute-done.12.refs_0_.refs_2_ = bf16[128,1024]{1,0:T(8,128)(2,1)S(1)} collective-permute-done((bf16[128,1024]{1,0:T(8,128)(2,1)S(1)}, bf16[128,1024]{1,0:T(8,128)(2,1)S(1)}, u32[]{:S(2)}, u32[]{:S(2)}) %collective-permute-start.12) | collective-permute-done | bytes 262176 | tf_op jit(solution)/shard_map/ppermute | solution.py:31
  51.6 4.9 %collective-permute-done.8.refs_7_ = bf16[128,1024]{1,0:T(8,128)(2,1)S(1)} collective-permute-done((bf16[128,1024]{1,0:T(8,128)(2,1)}, bf16[128,1024]{1,0:T(8,128)(2,1)S(1)}, u32[]{:S(2)}, u32[]{:S(2)}) %collective-permute-start.8) | collective-permute-done | bytes 262176 | tf_op jit(solution)/shard_map/ppermute | solution.py:31
  60.0 4.2 %down_product.1 = (f32[8,64,128]{2,1,0:T(8,128)}, f32[8,128]{1,0:T(8,128)S(1)}) custom-call(s32[16]{0:T(128)S(1)} %add.61.labels_ref, bf16[8,136,1024]{2,1,0:T(8,128)(2,1)S(1)} %all-to-all-done.rows_ref, bf16[128,1024]{1,0:T(8,128)(2,1)S(1)} %join_blocks.6.refs_0_, bf16[128,1024]{1,0:T(8,128)(2,1)S(1)} %join_blocks.7.refs_1_, ...), custom_call_target="tpu_custom_call" | custom-call | flops 2147483648 | bytes 4194304 | tf_op jit(solution)/shard_map/down_product/pallas_call | solution.py:146
  64.2 3.9 %all-to-all-start.1 = ((f32[8,64,128]{2,1,0:T(8,128)}), f32[8,64,128]{2,1,0:T(8,128)S(1)}, u32[]{:S(2)}, u32[]{:S(2)}) async-start(f32[8,64,128]{2,1,0:T(8,128)} %get-tuple-element.26), calls=%async_computation.1 | async-start | bytes 524288 | tf_op jit(solution)/shard_map/all_to_all | solution.py:39
  68.2 4.4 %collective-permute-done.15.refs_5_ = bf16[128,1024]{1,0:T(8,128)(2,1)S(1)} collective-permute-done((bf16[128,1024]{1,0:T(8,128)(2,1)}, bf16[128,1024]{1,0:T(8,128)(2,1)S(1)}, u32[]{:S(2)}, u32[]{:S(2)}) %collective-permute-start.15) | collective-permute-done | bytes 262176 | tf_op jit(solution)/shard_map/ppermute | solution.py:31
  72.6 1.6 %all-to-all-done.1.terms_ref = f32[8,64,128]{2,1,0:T(8,128)S(1)} async-done(((f32[8,64,128]{2,1,0:T(8,128)}), f32[8,64,128]{2,1,0:T(8,128)S(1)}, u32[]{:S(2)}, u32[]{:S(2)}) %all-to-all-start.1) | async-done | bytes 262176 | tf_op jit(solution)/shard_map/all_to_all | solution.py:39
  74.8 3.4 %all-to-all-start.2 = ((bf16[8,64,128]{2,1,0:T(8,128)(2,1)}), bf16[8,64,128]{2,1,0:T(8,128)(2,1)S(1)}, u32[]{:S(2)}, u32[]{:S(2)}) async-start(bf16[8,64,128]{2,1,0:T(8,128)(2,1)} %summed_copies.1), calls=%async_computation.2 | async-start | bytes 262144 | tf_op jit(solution)/shard_map/all_to_all | solution.py:39
  79.3 4.0 %all-to-all-done.2.shrunk_ref = bf16[8,64,128]{2,1,0:T(8,128)(2,1)S(1)} async-done(((bf16[8,64,128]{2,1,0:T(8,128)(2,1)}), bf16[8,64,128]{2,1,0:T(8,128)(2,1)S(1)}, u32[]{:S(2)}, u32[]{:S(2)}) %all-to-all-start.2) | async-done | bytes 131104 | tf_op jit(solution)/shard_map/all_to_all | solution.py:39
  83.3 1.4 %collective-permute-done.17.refs_7_ = bf16[128,1024]{1,0:T(8,128)(2,1)S(1)} collective-permute-done((bf16[128,1024]{1,0:T(8,128)(2,1)S(1)}, bf16[128,1024]{1,0:T(8,128)(2,1)S(1)}, u32[]{:S(2)}, u32[]{:S(2)}) %collective-permute-start.17) | collective-permute-done | bytes 262176 | tf_op jit(solution)/shard_map/ppermute | solution.py:31
  84.7 2.6 %up_product.2 = (bf16[128,1024]{1,0:T(8,128)(2,1)S(1)}, bf16[128,1024]{1,0:T(8,128)(2,1)S(1)}, bf16[128,1024]{1,0:T(8,128)(2,1)S(1)}, bf16[128,1024]{1,0:T(8,128)(2,1)S(1)}) custom-call(s32[16]{0:T(128)S(1)} %add.61.labels_ref, s32[1]{0:T(128)} %bitcast.me_ref, f32[8,128]{1,0:T(8,128)S(1)} %get-tuple-element.25.ids_ref, ...), custom_call_target="tpu_custom_call" | custom-call | flops 1073741824 | bytes 3145728 | tf_op jit(solution)/shard_map/up_product/pallas_call | solution.py:217
  87.3 2.6 %collective-permute-start.18 = (bf16[128,1024]{1,0:T(8,128)(2,1)S(1)}, bf16[128,1024]{1,0:T(8,128)(2,1)S(1)}, u32[]{:S(2)}, u32[]{:S(2)}) collective-permute-start(bf16[128,1024]{1,0:T(8,128)(2,1)S(1)} %get-tuple-element.35), channel_id=1, source_target_pairs={{0,18},{1,19},{2,16},{3,17},{16,2},{17,3},{18,0},{19,1},{4,22},{5,... | collective-permute-start | bytes 786440 | tf_op jit(solution)/shard_map/ppermute | solution.py:27
  91.7 2.5 %up_product.3 = (bf16[128,1024]{1,0:T(8,128)(2,1)S(1)}, bf16[128,1024]{1,0:T(8,128)(2,1)S(1)}, bf16[128,1024]{1,0:T(8,128)(2,1)S(1)}, bf16[128,1024]{1,0:T(8,128)(2,1)S(1)}) custom-call(s32[16]{0:T(128)S(1)} %add.61.labels_ref, s32[1]{0:T(128)} %bitcast.me_ref, f32[8,128]{1,0:T(8,128)S(1)} %get-tuple-element.25.ids_ref, ...), custom_call_target="tpu_custom_call" | custom-call | flops 1073741824 | bytes 3145728 | tf_op jit(solution)/shard_map/up_product/pallas_call | solution.py:217
  94.3 1.7 %collective-permute-start.22 = (bf16[128,1024]{1,0:T(8,128)(2,1)S(1)}, bf16[128,1024]{1,0:T(8,128)(2,1)S(1)}, u32[]{:S(2)}, u32[]{:S(2)}) collective-permute-start(bf16[128,1024]{1,0:T(8,128)(2,1)S(1)} %get-tuple-element.39), channel_id=1, source_target_pairs={{0,2},{1,3},{2,0},{3,1},{16,18},{17,19},{18,16},{19,17},{4,6},{5,7... | collective-permute-start | bytes 786440 | tf_op jit(solution)/shard_map/ppermute | solution.py:27
  96.0 1.4 %collective-permute-done.18.refs_0_ = bf16[128,1024]{1,0:T(8,128)(2,1)S(1)} collective-permute-done((bf16[128,1024]{1,0:T(8,128)(2,1)S(1)}, bf16[128,1024]{1,0:T(8,128)(2,1)S(1)}, u32[]{:S(2)}, u32[]{:S(2)}) %collective-permute-start.18) | collective-permute-done | bytes 262176 | tf_op jit(solution)/shard_map/ppermute | solution.py:27
  97.4 4.9 %collective-permute-done.19.refs_1_ = bf16[128,1024]{1,0:T(8,128)(2,1)S(1)} collective-permute-done((bf16[128,1024]{1,0:T(8,128)(2,1)S(1)}, bf16[128,1024]{1,0:T(8,128)(2,1)S(1)}, u32[]{:S(2)}, u32[]{:S(2)}) %collective-permute-start.19) | collective-permute-done | bytes 262176 | tf_op jit(solution)/shard_map/ppermute | solution.py:27
  102.9 6.0 %collective-permute-done.20.refs_2_ = bf16[128,1024]{1,0:T(8,128)(2,1)S(1)} collective-permute-done((bf16[128,1024]{1,0:T(8,128)(2,1)S(1)}, bf16[128,1024]{1,0:T(8,128)(2,1)S(1)}, u32[]{:S(2)}, u32[]{:S(2)}) %collective-permute-start.20) | collective-permute-done | bytes 262176 | tf_op jit(solution)/shard_map/ppermute | solution.py:27
  108.9 3.2 %collective-permute-done.21.refs_3_ = bf16[128,1024]{1,0:T(8,128)(2,1)S(1)} collective-permute-done((bf16[128,1024]{1,0:T(8,128)(2,1)S(1)}, bf16[128,1024]{1,0:T(8,128)(2,1)S(1)}, u32[]{:S(2)}, u32[]{:S(2)}) %collective-permute-start.21) | collective-permute-done | bytes 262176 | tf_op jit(solution)/shard_map/ppermute | solution.py:27
  113.1 1.4 %place_results.1 = bf16[128,8192]{1,0:T(8,128)(2,1)} custom-call(s32[1]{0:T(128)} %bitcast.me_ref, bf16[128,1024]{1,0:T(8,128)(2,1)S(1)} %collective-permute-done.18.refs_0_, bf16[128,1024]{1,0:T(8,128)(2,1)S(1)} %collective-permute-done.19.refs_1_, bf16[128,1024]{1,0:T(8,128)(2,1)S(1)} %collective-permute-done.20.refs_2_, ...), custom_call_target="tpu_custom_call" | custom-call | tf_op jit(solution)/shard_map/place_results/pallas_call | solution.py:248
  (58 shorter events, 13.7 us)
Async XLA Ops:
  1.1 3.2 %collective-permute-start = (bf16[64,1024]{1,0:T(8,128)(2,1)S(1)}, bf16[64,1024]{1,0:T(8,128)(2,1)S(1)}, u32[]{:S(2)}, u32[]{:S(2)}) collective-permute-start(bf16[64,1024]{1,0:T(8,128)(2,1)S(1)} %get-tuple-element.48), channel_id=1, source_target_pairs={{0,1},{1,0},{2,3},{3,2},{4,5},{5,4},{6,7},{7,6},{8,9},{9,8},{10,11... | collective-permute-start | bytes 393224 | tf_op jit(solution)/shard_map/ppermute | solution.py:27
  1.7 9.9 %collective-permute-start.1 = (bf16[64,1024]{1,0:T(8,128)(2,1)S(1)}, bf16[64,1024]{1,0:T(8,128)(2,1)S(1)}, u32[]{:S(2)}, u32[]{:S(2)}) collective-permute-start(bf16[64,1024]{1,0:T(8,128)(2,1)S(1)} %get-tuple-element.50), channel_id=1, source_target_pairs={{0,2},{1,3},{2,0},{3,1},{4,6},{5,7},{6,4},{7,5},{8,10},{9,11},{10,... | collective-permute-start | bytes 393224 | tf_op jit(solution)/shard_map/ppermute | solution.py:27
  4.2 7.3 %collective-permute-start.2 = (bf16[64,1024]{1,0:T(8,128)(2,1)S(1)}, bf16[64,1024]{1,0:T(8,128)(2,1)S(1)}, u32[]{:S(2)}, u32[]{:S(2)}) collective-permute-start(bf16[64,1024]{1,0:T(8,128)(2,1)S(1)} %get-tuple-element.47), channel_id=1, source_target_pairs={{0,3},{1,2},{2,1},{3,0},{4,7},{5,6},{6,5},{7,4},{8,11},{9,10},{10,... | collective-permute-start | bytes 393224 | tf_op jit(solution)/shard_map/ppermute | solution.py:27
  4.3 1.9 %copy-start = (bf16[128,8192]{1,0:T(8,128)(2,1)S(1)}, bf16[128,8192]{1,0:T(8,128)(2,1)}, u32[]{:S(2)}) copy-start(bf16[128,8192]{1,0:T(8,128)(2,1)} %hidden_ref) | copy-start | bytes 6291460
  4.3 1.9 %copy-start.1 = (s32[128,1]{0,1:T(1,128)S(1)}, s32[128,1]{0,1:T(1,128)}, u32[]{:S(2)}) copy-start(s32[128,1]{0,1:T(1,128)} %param.4) | copy-start | bytes 1540
  4.3 10.7 %collective-permute-start.3 = (bf16[128,1024]{1,0:T(8,128)(2,1)S(1)}, bf16[128,1024]{1,0:T(8,128)(2,1)S(1)}, u32[]{:S(2)}, u32[]{:S(2)}) collective-permute-start(bf16[128,1024]{1,0:T(8,128)(2,1)S(1)} %join_blocks.6.refs_0_), channel_id=1, source_target_pairs={{0,4},{4,8},{8,12},{12,0},{1,5},{5,9},{9,13},{13,1},{2,6},{6,10},{... | collective-permute-start | bytes 786440 | tf_op jit(solution)/shard_map/ppermute | solution.py:31
  7.8 49.4 %all-to-all-start = ((bf16[8,136,1024]{2,1,0:T(8,128)(2,1)}), bf16[8,136,1024]{2,1,0:T(8,128)(2,1)S(1)}, u32[]{:S(2)}, u32[]{:S(2)}) async-start(bf16[8,136,1024]{2,1,0:T(8,128)(2,1)} %outgoing_rows.1), calls=%async_computation | async-start | bytes 4456448 | tf_op jit(solution)/shard_map/all_to_all | solution.py:39
  11.6 11.0 %collective-permute-start.4 = (bf16[128,1024]{1,0:T(8,128)(2,1)S(1)}, bf16[128,1024]{1,0:T(8,128)(2,1)S(1)}, u32[]{:S(2)}, u32[]{:S(2)}) collective-permute-start(bf16[128,1024]{1,0:T(8,128)(2,1)S(1)} %join_blocks.7.refs_1_), channel_id=1, source_target_pairs={{0,4},{4,8},{8,12},{12,0},{1,5},{5,9},{9,13},{13,1},{2,6},{6,10},{... | collective-permute-start | bytes 786440 | tf_op jit(solution)/shard_map/ppermute | solution.py:31
  15.0 12.8 %collective-permute-start.5 = (bf16[128,1024]{1,0:T(8,128)(2,1)S(1)}, bf16[128,1024]{1,0:T(8,128)(2,1)}, u32[]{:S(2)}, u32[]{:S(2)}) collective-permute-start(bf16[128,1024]{1,0:T(8,128)(2,1)S(1)} %join_blocks.8), channel_id=1, source_target_pairs={{0,4},{4,8},{8,12},{12,0},{1,5},{5,9},{9,13},{13,1},{2,6},{6,10},{... | collective-permute-start | bytes 786440 | tf_op jit(solution)/shard_map/ppermute | solution.py:31
  17.0 14.6 %collective-permute-start.9 = (bf16[64,1024]{1,0:T(8,128)(2,1)S(1)}, bf16[64,1024]{1,0:T(8,128)(2,1)S(1)}, u32[]{:S(2)}, u32[]{:S(2)}) collective-permute-start(bf16[64,1024]{1,0:T(8,128)(2,1)S(1)} %get-tuple-element.28), channel_id=1, source_target_pairs={{0,1},{1,0},{2,3},{3,2},{4,5},{5,4},{6,7},{7,6},{8,9},{9,8},{10,11... | collective-permute-start | bytes 393224 | tf_op jit(solution)/shard_map/ppermute | solution.py:27
  22.5 6.1 %copy-start.2 = (bf16[128,1024]{1,0:T(8,128)(2,1)}, bf16[128,1024]{1,0:T(8,128)(2,1)S(1)}, u32[]{:S(2)}) copy-start(bf16[128,1024]{1,0:T(8,128)(2,1)S(1)} %collective-permute-done.4.refs_0_.refs_3_) | copy-start | bytes 786436
  27.9 11.2 %collective-permute-start.7 = (bf16[128,1024]{1,0:T(8,128)(2,1)}, bf16[128,1024]{1,0:T(8,128)(2,1)S(1)}, u32[]{:S(2)}, u32[]{:S(2)}) collective-permute-start(bf16[128,1024]{1,0:T(8,128)(2,1)} %collective-permute-done.5.refs_4_), channel_id=1, source_target_pairs={{0,4},{4,8},{8,12},{12,0},{1,5},{5,9},{9,13},{13,1},{2,6},{6,10},{... | collective-permute-start | bytes 786440 | tf_op jit(solution)/shard_map/ppermute | solution.py:31
  28.6 16.2 %collective-permute-start.6 = (bf16[128,1024]{1,0:T(8,128)(2,1)}, bf16[128,1024]{1,0:T(8,128)(2,1)}, u32[]{:S(2)}, u32[]{:S(2)}) collective-permute-start(bf16[128,1024]{1,0:T(8,128)(2,1)} %join_blocks.9), channel_id=1, source_target_pairs={{0,4},{4,8},{8,12},{12,0},{1,5},{5,9},{9,13},{13,1},{2,6},{6,10},{... | collective-permute-start | bytes 786440 | tf_op jit(solution)/shard_map/ppermute | solution.py:31
  29.9 14.9 %collective-permute-start.10 = (bf16[64,1024]{1,0:T(8,128)(2,1)}, bf16[64,1024]{1,0:T(8,128)(2,1)}, u32[]{:S(2)}, u32[]{:S(2)}) collective-permute-start(bf16[64,1024]{1,0:T(8,128)(2,1)} %get-tuple-element.30), channel_id=1, source_target_pairs={{0,2},{1,3},{2,0},{3,1},{4,6},{5,7},{6,4},{7,5},{8,10},{9,11},{10,... | collective-permute-start | bytes 393224 | tf_op jit(solution)/shard_map/ppermute | solution.py:27
  31.6 13.2 %collective-permute-start.11 = (bf16[64,1024]{1,0:T(8,128)(2,1)}, bf16[64,1024]{1,0:T(8,128)(2,1)}, u32[]{:S(2)}, u32[]{:S(2)}) collective-permute-start(bf16[64,1024]{1,0:T(8,128)(2,1)} %get-tuple-element.32), channel_id=1, source_target_pairs={{0,3},{1,2},{2,1},{3,0},{4,7},{5,6},{6,5},{7,4},{8,11},{9,10},{10,... | collective-permute-start | bytes 393224 | tf_op jit(solution)/shard_map/ppermute | solution.py:27
  39.8 11.0 %collective-permute-start.12 = (bf16[128,1024]{1,0:T(8,128)(2,1)S(1)}, bf16[128,1024]{1,0:T(8,128)(2,1)S(1)}, u32[]{:S(2)}, u32[]{:S(2)}) collective-permute-start(bf16[128,1024]{1,0:T(8,128)(2,1)S(1)} %pad_maximum_fusion.refs_0_), channel_id=1, source_target_pairs={{0,4},{4,8},{8,12},{12,0},{1,5},{5,9},{9,13},{13,1},{2,6},{6,10},{... | collective-permute-start | bytes 786440 | tf_op jit(solution)/shard_map/ppermute | solution.py:31
  44.8 11.6 %collective-permute-start.8 = (bf16[128,1024]{1,0:T(8,128)(2,1)}, bf16[128,1024]{1,0:T(8,128)(2,1)S(1)}, u32[]{:S(2)}, u32[]{:S(2)}) collective-permute-start(bf16[128,1024]{1,0:T(8,128)(2,1)} %collective-permute-done.6.refs_5_), channel_id=1, source_target_pairs={{0,4},{4,8},{8,12},{12,0},{1,5},{5,9},{9,13},{13,1},{2,6},{6,10},{... | collective-permute-start | bytes 786440 | tf_op jit(solution)/shard_map/ppermute | solution.py:31
  46.5 17.7 %collective-permute-start.13 = (bf16[128,1024]{1,0:T(8,128)(2,1)}, bf16[128,1024]{1,0:T(8,128)(2,1)}, u32[]{:S(2)}, u32[]{:S(2)}) collective-permute-start(bf16[128,1024]{1,0:T(8,128)(2,1)} %join_blocks.10.refs_1_), channel_id=1, source_target_pairs={{0,4},{4,8},{8,12},{12,0},{1,5},{5,9},{9,13},{13,1},{2,6},{6,10},{... | collective-permute-start | bytes 786440 | tf_op jit(solution)/shard_map/ppermute | solution.py:31
  51.6 16.5 %collective-permute-start.14 = (bf16[128,1024]{1,0:T(8,128)(2,1)}, bf16[128,1024]{1,0:T(8,128)(2,1)}, u32[]{:S(2)}, u32[]{:S(2)}) collective-permute-start(bf16[128,1024]{1,0:T(8,128)(2,1)} %join_blocks.11), channel_id=1, source_target_pairs={{0,4},{4,8},{8,12},{12,0},{1,5},{5,9},{9,13},{13,1},{2,6},{6,10},{... | collective-permute-start | bytes 786440 | tf_op jit(solution)/shard_map/ppermute | solution.py:31
  57.2 1.0 copy-start.3
  64.2 8.4 %collective-permute-start.15 = (bf16[128,1024]{1,0:T(8,128)(2,1)}, bf16[128,1024]{1,0:T(8,128)(2,1)S(1)}, u32[]{:S(2)}, u32[]{:S(2)}) collective-permute-start(bf16[128,1024]{1,0:T(8,128)(2,1)} %collective-permute-done.13.refs_3_), channel_id=1, source_target_pairs={{0,4},{4,8},{8,12},{12,0},{1,5},{5,9},{9,13},{13,1},{2,6},{6,10},{... | collective-permute-start | bytes 786440 | tf_op jit(solution)/shard_map/ppermute | solution.py:31
  64.2 9.9 %all-to-all-start.1 = ((f32[8,64,128]{2,1,0:T(8,128)}), f32[8,64,128]{2,1,0:T(8,128)S(1)}, u32[]{:S(2)}, u32[]{:S(2)}) async-start(f32[8,64,128]{2,1,0:T(8,128)} %get-tuple-element.26), calls=%async_computation.1 | async-start | bytes 524288 | tf_op jit(solution)/shard_map/all_to_all | solution.py:39
  68.1 11.2 %collective-permute-start.16 = (bf16[128,1024]{1,0:T(8,128)(2,1)}, bf16[128,1024]{1,0:T(8,128)(2,1)S(1)}, u32[]{:S(2)}, u32[]{:S(2)}) collective-permute-start(bf16[128,1024]{1,0:T(8,128)(2,1)} %collective-permute-done.14.refs_4_), channel_id=1, source_target_pairs={{0,4},{4,8},{8,12},{12,0},{1,5},{5,9},{9,13},{13,1},{2,6},{6,10},{... | collective-permute-start | bytes 786440 | tf_op jit(solution)/shard_map/ppermute | solution.py:31
  72.6 12.1 %collective-permute-start.17 = (bf16[128,1024]{1,0:T(8,128)(2,1)S(1)}, bf16[128,1024]{1,0:T(8,128)(2,1)S(1)}, u32[]{:S(2)}, u32[]{:S(2)}) collective-permute-start(bf16[128,1024]{1,0:T(8,128)(2,1)S(1)} %collective-permute-done.15.refs_5_), channel_id=1, source_target_pairs={{0,4},{4,8},{8,12},{12,0},{1,5},{5,9},{9,13},{13,1},{2,6},{6,10},{... | collective-permute-start | bytes 786440 | tf_op jit(solution)/shard_map/ppermute | solution.py:31
  74.8 8.5 %all-to-all-start.2 = ((bf16[8,64,128]{2,1,0:T(8,128)(2,1)}), bf16[8,64,128]{2,1,0:T(8,128)(2,1)S(1)}, u32[]{:S(2)}, u32[]{:S(2)}) async-start(bf16[8,64,128]{2,1,0:T(8,128)(2,1)} %summed_copies.1), calls=%async_computation.2 | async-start | bytes 262144 | tf_op jit(solution)/shard_map/all_to_all | solution.py:39
  87.3 10.2 %collective-permute-start.18 = (bf16[128,1024]{1,0:T(8,128)(2,1)S(1)}, bf16[128,1024]{1,0:T(8,128)(2,1)S(1)}, u32[]{:S(2)}, u32[]{:S(2)}) collective-permute-start(bf16[128,1024]{1,0:T(8,128)(2,1)S(1)} %get-tuple-element.35), channel_id=1, source_target_pairs={{0,18},{1,19},{2,16},{3,17},{16,2},{17,3},{18,0},{19,1},{4,22},{5,... | collective-permute-start | bytes 786440 | tf_op jit(solution)/shard_map/ppermute | solution.py:27
  89.9 12.4 %collective-permute-start.19 = (bf16[128,1024]{1,0:T(8,128)(2,1)S(1)}, bf16[128,1024]{1,0:T(8,128)(2,1)S(1)}, u32[]{:S(2)}, u32[]{:S(2)}) collective-permute-start(bf16[128,1024]{1,0:T(8,128)(2,1)S(1)} %get-tuple-element.36), channel_id=1, source_target_pairs={{0,19},{1,18},{2,17},{3,16},{16,3},{17,2},{18,1},{19,0},{4,23},{5,... | collective-permute-start | bytes 786440 | tf_op jit(solution)/shard_map/ppermute | solution.py:27
  89.9 19.0 %collective-permute-start.20 = (bf16[128,1024]{1,0:T(8,128)(2,1)S(1)}, bf16[128,1024]{1,0:T(8,128)(2,1)S(1)}, u32[]{:S(2)}, u32[]{:S(2)}) collective-permute-start(bf16[128,1024]{1,0:T(8,128)(2,1)S(1)} %get-tuple-element.37), channel_id=1, source_target_pairs={{0,16},{1,17},{2,18},{3,19},{16,0},{17,1},{18,2},{19,3},{4,20},{5,... | collective-permute-start | bytes 786440 | tf_op jit(solution)/shard_map/ppermute | solution.py:27
  90.9 21.3 %collective-permute-start.21 = (bf16[128,1024]{1,0:T(8,128)(2,1)S(1)}, bf16[128,1024]{1,0:T(8,128)(2,1)S(1)}, u32[]{:S(2)}, u32[]{:S(2)}) collective-permute-start(bf16[128,1024]{1,0:T(8,128)(2,1)S(1)} %get-tuple-element.38), channel_id=1, source_target_pairs={{0,17},{1,16},{2,19},{3,18},{16,1},{17,0},{18,3},{19,2},{4,21},{5,... | collective-permute-start | bytes 786440 | tf_op jit(solution)/shard_map/ppermute | solution.py:27
  94.3 17.9 %collective-permute-start.22 = (bf16[128,1024]{1,0:T(8,128)(2,1)S(1)}, bf16[128,1024]{1,0:T(8,128)(2,1)S(1)}, u32[]{:S(2)}, u32[]{:S(2)}) collective-permute-start(bf16[128,1024]{1,0:T(8,128)(2,1)S(1)} %get-tuple-element.39), channel_id=1, source_target_pairs={{0,2},{1,3},{2,0},{3,1},{16,18},{17,19},{18,16},{19,17},{4,6},{5,7... | collective-permute-start | bytes 786440 | tf_op jit(solution)/shard_map/ppermute | solution.py:27
  97.4 15.7 %collective-permute-start.23 = (bf16[128,1024]{1,0:T(8,128)(2,1)S(1)}, bf16[128,1024]{1,0:T(8,128)(2,1)S(1)}, u32[]{:S(2)}, u32[]{:S(2)}) collective-permute-start(bf16[128,1024]{1,0:T(8,128)(2,1)S(1)} %get-tuple-element.40), channel_id=1, source_target_pairs={{0,3},{1,2},{2,1},{3,0},{16,19},{17,18},{18,17},{19,16},{4,7},{5,6... | collective-permute-start | bytes 786440 | tf_op jit(solution)/shard_map/ppermute | solution.py:27
  102.3 10.8 %collective-permute-start.24 = (bf16[128,1024]{1,0:T(8,128)(2,1)S(1)}, bf16[128,1024]{1,0:T(8,128)(2,1)S(1)}, u32[]{:S(2)}, u32[]{:S(2)}) collective-permute-start(bf16[128,1024]{1,0:T(8,128)(2,1)S(1)} %get-tuple-element.41), channel_id=1, source_target_pairs={{0,1},{1,0},{2,3},{3,2},{16,17},{17,16},{18,19},{19,18},{4,5},{5,4... | collective-permute-start | bytes 786440 | tf_op jit(solution)/shard_map/ppermute | solution.py:27
  (4 other events, 3.3 us)

commit v28 on v26

--- a/solution.py
+++ b/solution.py
@@ -313,7 +313,8 @@
     shrunk = swap(summed_copies(swap(packed)))
     offsets = sorted(range(1, members), key=lambda n: (-(n >= inner) - (n % inner >= 2), -(n >= inner), n)) + [0]
     results = []
-    for some in offsets[: members // 2], offsets[members // 2 :]:
+    quarter = members // 4
+    for some in offsets[:quarter], offsets[quarter : 2 * quarter], offsets[2 * quarter :]:
         results += up_product(labels, me.reshape(1), id_rows, shrunk, up_maps, rank, some)
     returned = [to_partner(r, PLANE, members, n) for r, n in zip(results[:-1], offsets)]
     return place(me.reshape(1), offsets, returned + results[-1:])

time: 110 us -> 114 us (1.036)
  local copies, waits for them, and re-layouts: 4 us -> 12.5 us
  waiting for transfers between devices: 59.3 us -> 54.7 us
  Pallas kernels: 16.2 us -> 13.2 us
  starting transfers between devices: 28.7 us -> 31 us
    unnamed x14 -> x40, local copies, waits for them, and re-layouts: 1.94 us -> 10.4 us
    ppermute x12, waiting for transfers between devices: 35.8 us -> 31.8 us  [next_on_ring(): lax.ppermute(block, 'outer', [(i, (i + 1) % outer) for i in range(outer)])]
    ppermute x12, starting transfers between devices: 4.82 us -> 7.31 us  [next_on_ring(): lax.ppermute(block, 'outer', [(i, (i + 1) % outer) for i in range(outer)])]
    ppermute x13, waiting for transfers between devices: 18.1 us -> 16.7 us  [to_partner(): return lax.ppermute(value, axes, [(i, i ^ offset) for i in range(size)])]
    pallas_call x6, Pallas kernels: 3.23 us -> 1.88 us  [joined(): pl.pallas_call(join_kernel, out_shape=jax.ShapeDtypeStruct((len(blocks) *...]
    pallas_call x1, Pallas kernels: 4.25 us -> 2.97 us  [down_product(): pl.pallas_call(functools.partial(down_kernel, len(maps), rank), out_shape...]
    pallas_call x2 -> x3, Pallas kernels: 5.09 us -> 4.69 us  [up_product(): pl.pallas_call(functools.partial(up_kernel, len(maps), rank, offsets), ou...]
  transfers between devices with their start and end apart: 28 -> 28, of which waited for: 20 -> 18; matrix products, arithmetic and copies ran while one was open for 2% -> 2% of each run, Pallas kernels for 11% -> 9%
where the time goes in v28:
time: 114 us; the launch traced here: 113 us
  waiting for transfers between devices  54.7 us (48%)
  starting transfers between devices  31 us (27%)
  Pallas kernels  13.2 us (12%)
  local copies, waits for them, and re-layouts  12.5 us (11%)
  other arithmetic  1.16 us (1%)
    ppermute x12, waiting for transfers between devices, next_on_ring(): lax.ppermute(block, 'outer', [(i, (i + 1) % outer) for i in range(outer)])  31.8 us
    ppermute x13, waiting for transfers between devices, to_partner(): return lax.ppermute(value, axes, [(i, i ^ offset) for i in range(size)])  16.7 us
    ppermute x13, starting transfers between devices, to_partner(): return lax.ppermute(value, axes, [(i, i ^ offset) for i in range(size)])  12.4 us
    all_to_all x3, starting transfers between devices, swap(): return lax.all_to_all(value, PLANE, split_axis=0, concat_axis=0, tiled=True)  11.4 us
    unnamed x40, local copies, waits for them, and re-layouts  10.4 us
    ppermute x12, starting transfers between devices, next_on_ring(): lax.ppermute(block, 'outer', [(i, (i + 1) % outer) for i in range(outer)])  7.31 us
    all_to_all x3, waiting for transfers between devices, swap(): return lax.all_to_all(value, PLANE, split_axis=0, concat_axis=0, tiled=True)  6.26 us
    pallas_call x3, Pallas kernels, up_product(): pl.pallas_call(functools.partial(up_kernel, len(maps), rank, offsets), ou...  4.69 us
  transfers between devices with their start and end apart: 28, of which 18 were waited for; matrix products, arithmetic and copies ran while one was open for 2% of the time, Pallas kernels for 9%

profile of v28, /device:TPU:0, one launch (start us, length us, event | category | flops | bytes accessed | tf_op | source)
XLA Modules:
  0.0 112.8 jit_solution(14428133126561379109)
XLA Ops:
  1.7 2.6 %collective-permute-start.1 = (bf16[64,1024]{1,0:T(8,128)(2,1)S(1)}, bf16[64,1024]{1,0:T(8,128)(2,1)S(1)}, u32[]{:S(2)}, u32[]{:S(2)}) collective-permute-start(bf16[64,1024]{1,0:T(8,128)(2,1)S(1)} %get-tuple-element.50), channel_id=1, source_target_pairs={{0,2},{1,3},{2,0},{3,1},{4,6},{5,7},{6,4},{7,5},{8,10},{9,11},{10,... | collective-permute-start | bytes 393224 | tf_op jit(solution)/shard_map/ppermute | solution.py:27
  4.4 1.8 %collective-permute-start.3 = (bf16[128,1024]{1,0:T(8,128)(2,1)S(1)}, bf16[128,1024]{1,0:T(8,128)(2,1)S(1)}, u32[]{:S(2)}, u32[]{:S(2)}) collective-permute-start(bf16[128,1024]{1,0:T(8,128)(2,1)S(1)} %join_blocks.6.refs_0_), channel_id=1, source_target_pairs={{0,4},{4,8},{8,12},{12,0},{1,5},{5,9},{9,13},{13,1},{2,6},{6,10},{... | collective-permute-start | bytes 786440 | tf_op jit(solution)/shard_map/ppermute | solution.py:31
  6.2 1.6 %outgoing_rows.1 = bf16[8,136,1024]{2,1,0:T(8,128)(2,1)} custom-call(bf16[128,8192]{1,0:T(8,128)(2,1)S(1)} %copy-done, s32[1,128]{1,0:T(1,128)S(1)} %bitcast.26), custom_call_target="tpu_custom_call" | custom-call | tf_op jit(solution)/shard_map/outgoing_rows/pallas_call | solution.py:94
  7.8 3.8 %all-to-all-start = ((bf16[8,136,1024]{2,1,0:T(8,128)(2,1)}), bf16[8,136,1024]{2,1,0:T(8,128)(2,1)S(1)}, u32[]{:S(2)}, u32[]{:S(2)}) async-start(bf16[8,136,1024]{2,1,0:T(8,128)(2,1)} %outgoing_rows.1), calls=%async_computation | async-start | bytes 4456448 | tf_op jit(solution)/shard_map/all_to_all | solution.py:39
  11.6 1.6 %collective-permute-start.4 = (bf16[128,1024]{1,0:T(8,128)(2,1)S(1)}, bf16[128,1024]{1,0:T(8,128)(2,1)S(1)}, u32[]{:S(2)}, u32[]{:S(2)}) collective-permute-start(bf16[128,1024]{1,0:T(8,128)(2,1)S(1)} %join_blocks.7.refs_1_), channel_id=1, source_target_pairs={{0,4},{4,8},{8,12},{12,0},{1,5},{5,9},{9,13},{13,1},{2,6},{6,10},{... | collective-permute-start | bytes 786440 | tf_op jit(solution)/shard_map/ppermute | solution.py:31
  13.3 1.8 %collective-permute-done.3.refs_0_.refs_2_ = bf16[128,1024]{1,0:T(8,128)(2,1)S(1)} collective-permute-done((bf16[128,1024]{1,0:T(8,128)(2,1)S(1)}, bf16[128,1024]{1,0:T(8,128)(2,1)S(1)}, u32[]{:S(2)}, u32[]{:S(2)}) %collective-permute-start.3) | collective-permute-done | bytes 262176 | tf_op jit(solution)/shard_map/ppermute | solution.py:31
  15.7 6.8 %collective-permute-done.4.refs_0_.refs_3_ = bf16[128,1024]{1,0:T(8,128)(2,1)S(1)} collective-permute-done((bf16[128,1024]{1,0:T(8,128)(2,1)S(1)}, bf16[128,1024]{1,0:T(8,128)(2,1)S(1)}, u32[]{:S(2)}, u32[]{:S(2)}) %collective-permute-start.4) | collective-permute-done | bytes 262176 | tf_op jit(solution)/shard_map/ppermute | solution.py:31
  23.3 4.9 %collective-permute-done.5.refs_4_ = bf16[128,1024]{1,0:T(8,128)(2,1)S(1)} collective-permute-done((bf16[128,1024]{1,0:T(8,128)(2,1)S(1)}, bf16[128,1024]{1,0:T(8,128)(2,1)S(1)}, u32[]{:S(2)}, u32[]{:S(2)}) %collective-permute-start.5) | collective-permute-done | bytes 262176 | tf_op jit(solution)/shard_map/ppermute | solution.py:31
  29.1 2.1 %collective-permute-start.10 = (bf16[64,1024]{1,0:T(8,128)(2,1)}, bf16[64,1024]{1,0:T(8,128)(2,1)}, u32[]{:S(2)}, u32[]{:S(2)}) collective-permute-start(bf16[64,1024]{1,0:T(8,128)(2,1)} %get-tuple-element.30), channel_id=1, source_target_pairs={{0,2},{1,3},{2,0},{3,1},{4,6},{5,7},{6,4},{7,5},{8,10},{9,11},{10,... | collective-permute-start | bytes 393224 | tf_op jit(solution)/shard_map/ppermute | solution.py:27
  31.4 2.9 %collective-permute-done.6.refs_5_ = bf16[128,1024]{1,0:T(8,128)(2,1)S(1)} collective-permute-done((bf16[128,1024]{1,0:T(8,128)(2,1)S(1)}, bf16[128,1024]{1,0:T(8,128)(2,1)S(1)}, u32[]{:S(2)}, u32[]{:S(2)}) %collective-permute-start.6) | collective-permute-done | bytes 262176 | tf_op jit(solution)/shard_map/ppermute | solution.py:31
  35.4 4.5 %collective-permute-done.7.refs_6_ = bf16[128,1024]{1,0:T(8,128)(2,1)S(1)} collective-permute-done((bf16[128,1024]{1,0:T(8,128)(2,1)S(1)}, bf16[128,1024]{1,0:T(8,128)(2,1)S(1)}, u32[]{:S(2)}, u32[]{:S(2)}) %collective-permute-start.7) | collective-permute-done | bytes 262176 | tf_op jit(solution)/shard_map/ppermute | solution.py:31
  40.8 1.3 %collective-permute-done.10.refs_0_ = bf16[64,1024]{1,0:T(8,128)(2,1)} collective-permute-done((bf16[64,1024]{1,0:T(8,128)(2,1)}, bf16[64,1024]{1,0:T(8,128)(2,1)}, u32[]{:S(2)}, u32[]{:S(2)}) %collective-permute-start.10) | collective-permute-done | bytes 131104 | tf_op jit(solution)/shard_map/ppermute | solution.py:27
  42.1 3.5 %collective-permute-done.8.refs_7_ = bf16[128,1024]{1,0:T(8,128)(2,1)S(1)} collective-permute-done((bf16[128,1024]{1,0:T(8,128)(2,1)S(1)}, bf16[128,1024]{1,0:T(8,128)(2,1)S(1)}, u32[]{:S(2)}, u32[]{:S(2)}) %collective-permute-start.8) | collective-permute-done | bytes 262176 | tf_op jit(solution)/shard_map/ppermute | solution.py:31
  46.7 4.0 %collective-permute-done.12.refs_0_.refs_2_ = bf16[128,1024]{1,0:T(8,128)(2,1)S(1)} collective-permute-done((bf16[128,1024]{1,0:T(8,128)(2,1)S(1)}, bf16[128,1024]{1,0:T(8,128)(2,1)S(1)}, u32[]{:S(2)}, u32[]{:S(2)}) %collective-permute-start.12) | collective-permute-done | bytes 262176 | tf_op jit(solution)/shard_map/ppermute | solution.py:31
  59.0 3.0 %down_product.1 = (f32[8,64,128]{2,1,0:T(8,128)S(1)}, f32[8,128]{1,0:T(8,128)S(1)}) custom-call(s32[16]{0:T(128)S(1)} %add.61.labels_ref, bf16[8,136,1024]{2,1,0:T(8,128)(2,1)S(1)} %all-to-all-done.rows_ref, bf16[128,1024]{1,0:T(8,128)(2,1)S(1)} %copy-done.4, bf16[128,1024]{1,0:T(8,128)(2,1)S(1)} %copy-done.8, bf16[128,1024]{1,0:T(8,128)(2,1)S(1)} %copy-done.6, ...), custom_call_target="tpu_custom_call" | custom-call | flops 2147483648 | bytes 4194304 | tf_op jit(solution)/shard_map/down_product/pallas_call | solution.py:146
  62.7 1.3 %collective-permute-start.15 = (bf16[128,1024]{1,0:T(8,128)(2,1)S(1)}, bf16[128,1024]{1,0:T(8,128)(2,1)S(1)}, u32[]{:S(2)}, u32[]{:S(2)}) collective-permute-start(bf16[128,1024]{1,0:T(8,128)(2,1)S(1)} %collective-permute-done.13.refs_3_), channel_id=1, source_target_pairs={{0,4},{4,8},{8,12},{12,0},{1,5},{5,9},{9,13},{13,1},{2,6},{6,10},{... | collective-permute-start | bytes 786440 | tf_op jit(solution)/shard_map/ppermute | solution.py:31
  64.1 4.2 %all-to-all-start.1 = ((f32[8,64,128]{2,1,0:T(8,128)}), f32[8,64,128]{2,1,0:T(8,128)S(1)}, u32[]{:S(2)}, u32[]{:S(2)}) async-start(f32[8,64,128]{2,1,0:T(8,128)} %copy-done.1), calls=%async_computation.1 | async-start | bytes 524288 | tf_op jit(solution)/shard_map/all_to_all | solution.py:39
  68.3 1.6 %collective-permute-start.16 = (bf16[128,1024]{1,0:T(8,128)(2,1)S(1)}, bf16[128,1024]{1,0:T(8,128)(2,1)S(1)}, u32[]{:S(2)}, u32[]{:S(2)}) collective-permute-start(bf16[128,1024]{1,0:T(8,128)(2,1)S(1)} %collective-permute-done.14.refs_4_), channel_id=1, source_target_pairs={{0,4},{4,8},{8,12},{12,0},{1,5},{5,9},{9,13},{13,1},{2,6},{6,10},{... | collective-permute-start | bytes 786440 | tf_op jit(solution)/shard_map/ppermute | solution.py:31
  69.9 1.6 %collective-permute-done.15.refs_5_ = bf16[128,1024]{1,0:T(8,128)(2,1)S(1)} collective-permute-done((bf16[128,1024]{1,0:T(8,128)(2,1)S(1)}, bf16[128,1024]{1,0:T(8,128)(2,1)S(1)}, u32[]{:S(2)}, u32[]{:S(2)}) %collective-permute-start.15) | collective-permute-done | bytes 262176 | tf_op jit(solution)/shard_map/ppermute | solution.py:31
  72.3 2.0 %all-to-all-done.1.terms_ref = f32[8,64,128]{2,1,0:T(8,128)S(1)} async-done(((f32[8,64,128]{2,1,0:T(8,128)}), f32[8,64,128]{2,1,0:T(8,128)S(1)}, u32[]{:S(2)}, u32[]{:S(2)}) %all-to-all-start.1) | async-done | bytes 262176 | tf_op jit(solution)/shard_map/all_to_all | solution.py:39
  75.0 3.4 %all-to-all-start.2 = ((bf16[8,64,128]{2,1,0:T(8,128)(2,1)}), bf16[8,64,128]{2,1,0:T(8,128)(2,1)S(1)}, u32[]{:S(2)}, u32[]{:S(2)}) async-start(bf16[8,64,128]{2,1,0:T(8,128)(2,1)} %summed_copies.1), calls=%async_computation.2 | async-start | bytes 262144 | tf_op jit(solution)/shard_map/all_to_all | solution.py:39
  79.3 4.3 %all-to-all-done.2.shrunk_ref = bf16[8,64,128]{2,1,0:T(8,128)(2,1)S(1)} async-done(((bf16[8,64,128]{2,1,0:T(8,128)(2,1)}), bf16[8,64,128]{2,1,0:T(8,128)(2,1)S(1)}, u32[]{:S(2)}, u32[]{:S(2)}) %all-to-all-start.2) | async-done | bytes 131104 | tf_op jit(solution)/shard_map/all_to_all | solution.py:39
  84.4 1.4 %up_product.3 = (bf16[128,1024]{1,0:T(8,128)(2,1)S(1)}, bf16[128,1024]{1,0:T(8,128)(2,1)S(1)}) custom-call(s32[16]{0:T(128)S(1)} %add.61.labels_ref, s32[1]{0:T(128)} %bitcast.me_ref, f32[8,128]{1,0:T(8,128)S(1)} %get-tuple-element.25.ids_ref, bf16[8,64,128]{2,1,0:T(8,128)(2,1)S(1)} %all-to-all-done.2.shrunk_ref, ...), custom_call_target="tpu_custom_call" | custom-call | flops 536870912 | bytes 2621440 | tf_op jit(solution)/shard_map/up_product/pallas_call | solution.py:217
  85.8 2.6 %collective-permute-start.18 = (bf16[128,1024]{1,0:T(8,128)(2,1)S(1)}, bf16[128,1024]{1,0:T(8,128)(2,1)S(1)}, u32[]{:S(2)}, u32[]{:S(2)}) collective-permute-start(bf16[128,1024]{1,0:T(8,128)(2,1)S(1)} %get-tuple-element.35), channel_id=1, source_target_pairs={{0,18},{1,19},{2,16},{3,17},{16,2},{17,3},{18,0},{19,1},{4,22},{5,... | collective-permute-start | bytes 786440 | tf_op jit(solution)/shard_map/ppermute | solution.py:27
  88.4 1.4 %up_product.4 = (bf16[128,1024]{1,0:T(8,128)(2,1)S(1)}, bf16[128,1024]{1,0:T(8,128)(2,1)S(1)}) custom-call(s32[16]{0:T(128)S(1)} %add.61.labels_ref, s32[1]{0:T(128)} %bitcast.me_ref, f32[8,128]{1,0:T(8,128)S(1)} %get-tuple-element.25.ids_ref, bf16[8,64,128]{2,1,0:T(8,128)(2,1)S(1)} %all-to-all-done.2.shrunk_ref, ...), custom_call_target="tpu_custom_call" | custom-call | flops 536870912 | bytes 2621440 | tf_op jit(solution)/shard_map/up_product/pallas_call | solution.py:217
  90.5 1.2 %collective-permute-start.21 = (bf16[128,1024]{1,0:T(8,128)(2,1)S(1)}, bf16[128,1024]{1,0:T(8,128)(2,1)S(1)}, u32[]{:S(2)}, u32[]{:S(2)}) collective-permute-start(bf16[128,1024]{1,0:T(8,128)(2,1)S(1)} %get-tuple-element.38), channel_id=1, source_target_pairs={{0,17},{1,16},{2,19},{3,18},{16,1},{17,0},{18,3},{19,2},{4,21},{5,... | collective-permute-start | bytes 786440 | tf_op jit(solution)/shard_map/ppermute | solution.py:27
  91.7 2.0 %up_product.5 = (bf16[128,1024]{1,0:T(8,128)(2,1)S(1)}, bf16[128,1024]{1,0:T(8,128)(2,1)S(1)}, bf16[128,1024]{1,0:T(8,128)(2,1)S(1)}, bf16[128,1024]{1,0:T(8,128)(2,1)S(1)}) custom-call(s32[16]{0:T(128)S(1)} %add.61.labels_ref, s32[1]{0:T(128)} %bitcast.me_ref, f32[8,128]{1,0:T(8,128)S(1)} %get-tuple-element.25.ids_ref, ...), custom_call_target="tpu_custom_call" | custom-call | flops 1073741824 | bytes 3145728 | tf_op jit(solution)/shard_map/up_product/pallas_call | solution.py:217
  93.7 1.7 %collective-permute-start.22 = (bf16[128,1024]{1,0:T(8,128)(2,1)S(1)}, bf16[128,1024]{1,0:T(8,128)(2,1)S(1)}, u32[]{:S(2)}, u32[]{:S(2)}) collective-permute-start(bf16[128,1024]{1,0:T(8,128)(2,1)S(1)} %get-tuple-element.39), channel_id=1, source_target_pairs={{0,2},{1,3},{2,0},{3,1},{16,18},{17,19},{18,16},{19,17},{4,6},{5,7... | collective-permute-start | bytes 786440 | tf_op jit(solution)/shard_map/ppermute | solution.py:27
  96.0 4.9 %collective-permute-done.19.refs_1_ = bf16[128,1024]{1,0:T(8,128)(2,1)S(1)} collective-permute-done((bf16[128,1024]{1,0:T(8,128)(2,1)S(1)}, bf16[128,1024]{1,0:T(8,128)(2,1)S(1)}, u32[]{:S(2)}, u32[]{:S(2)}) %collective-permute-start.19) | collective-permute-done | bytes 262176 | tf_op jit(solution)/shard_map/ppermute | solution.py:27
  101.5 6.0 %collective-permute-done.20.refs_2_ = bf16[128,1024]{1,0:T(8,128)(2,1)S(1)} collective-permute-done((bf16[128,1024]{1,0:T(8,128)(2,1)S(1)}, bf16[128,1024]{1,0:T(8,128)(2,1)S(1)}, u32[]{:S(2)}, u32[]{:S(2)}) %collective-permute-start.20) | collective-permute-done | bytes 262176 | tf_op jit(solution)/shard_map/ppermute | solution.py:27
  107.5 2.9 %collective-permute-done.21.refs_3_ = bf16[128,1024]{1,0:T(8,128)(2,1)S(1)} collective-permute-done((bf16[128,1024]{1,0:T(8,128)(2,1)S(1)}, bf16[128,1024]{1,0:T(8,128)(2,1)S(1)}, u32[]{:S(2)}, u32[]{:S(2)}) %collective-permute-start.21) | collective-permute-done | bytes 262176 | tf_op jit(solution)/shard_map/ppermute | solution.py:27
  111.4 1.4 %place_results.1 = bf16[128,8192]{1,0:T(8,128)(2,1)} custom-call(s32[1]{0:T(128)} %bitcast.me_ref, bf16[128,1024]{1,0:T(8,128)(2,1)S(1)} %collective-permute-done.18.refs_0_, bf16[128,1024]{1,0:T(8,128)(2,1)S(1)} %collective-permute-done.19.refs_1_, bf16[128,1024]{1,0:T(8,128)(2,1)S(1)} %collective-permute-done.20.refs_2_, ...), custom_call_target="tpu_custom_call" | custom-call | tf_op jit(solution)/shard_map/place_results/pallas_call | solution.py:248
  (83 shorter events, 22.6 us)
Async XLA Ops:
  1.1 3.2 %collective-permute-start = (bf16[64,1024]{1,0:T(8,128)(2,1)S(1)}, bf16[64,1024]{1,0:T(8,128)(2,1)S(1)}, u32[]{:S(2)}, u32[]{:S(2)}) collective-permute-start(bf16[64,1024]{1,0:T(8,128)(2,1)S(1)} %get-tuple-element.48), channel_id=1, source_target_pairs={{0,1},{1,0},{2,3},{3,2},{4,5},{5,4},{6,7},{7,6},{8,9},{9,8},{10,11... | collective-permute-start | bytes 393224 | tf_op jit(solution)/shard_map/ppermute | solution.py:27
  1.7 9.9 %collective-permute-start.1 = (bf16[64,1024]{1,0:T(8,128)(2,1)S(1)}, bf16[64,1024]{1,0:T(8,128)(2,1)S(1)}, u32[]{:S(2)}, u32[]{:S(2)}) collective-permute-start(bf16[64,1024]{1,0:T(8,128)(2,1)S(1)} %get-tuple-element.50), channel_id=1, source_target_pairs={{0,2},{1,3},{2,0},{3,1},{4,6},{5,7},{6,4},{7,5},{8,10},{9,11},{10,... | collective-permute-start | bytes 393224 | tf_op jit(solution)/shard_map/ppermute | solution.py:27
  4.2 7.4 %collective-permute-start.2 = (bf16[64,1024]{1,0:T(8,128)(2,1)S(1)}, bf16[64,1024]{1,0:T(8,128)(2,1)S(1)}, u32[]{:S(2)}, u32[]{:S(2)}) collective-permute-start(bf16[64,1024]{1,0:T(8,128)(2,1)S(1)} %get-tuple-element.47), channel_id=1, source_target_pairs={{0,3},{1,2},{2,1},{3,0},{4,7},{5,6},{6,5},{7,4},{8,11},{9,10},{10,... | collective-permute-start | bytes 393224 | tf_op jit(solution)/shard_map/ppermute | solution.py:27
  4.3 3.5 %copy-start.3 = (bf16[128,1024]{1,0:T(8,128)(2,1)}, bf16[128,1024]{1,0:T(8,128)(2,1)S(1)}, u32[]{:S(2)}) copy-start(bf16[128,1024]{1,0:T(8,128)(2,1)S(1)} %join_blocks.6.refs_0_) | copy-start | bytes 786436
  4.4 10.7 %collective-permute-start.3 = (bf16[128,1024]{1,0:T(8,128)(2,1)S(1)}, bf16[128,1024]{1,0:T(8,128)(2,1)S(1)}, u32[]{:S(2)}, u32[]{:S(2)}) collective-permute-start(bf16[128,1024]{1,0:T(8,128)(2,1)S(1)} %join_blocks.6.refs_0_), channel_id=1, source_target_pairs={{0,4},{4,8},{8,12},{12,0},{1,5},{5,9},{9,13},{13,1},{2,6},{6,10},{... | collective-permute-start | bytes 786440 | tf_op jit(solution)/shard_map/ppermute | solution.py:31
  7.8 43.6 %all-to-all-start = ((bf16[8,136,1024]{2,1,0:T(8,128)(2,1)}), bf16[8,136,1024]{2,1,0:T(8,128)(2,1)S(1)}, u32[]{:S(2)}, u32[]{:S(2)}) async-start(bf16[8,136,1024]{2,1,0:T(8,128)(2,1)} %outgoing_rows.1), calls=%async_computation | async-start | bytes 4456448 | tf_op jit(solution)/shard_map/all_to_all | solution.py:39
  11.6 10.9 %collective-permute-start.4 = (bf16[128,1024]{1,0:T(8,128)(2,1)S(1)}, bf16[128,1024]{1,0:T(8,128)(2,1)S(1)}, u32[]{:S(2)}, u32[]{:S(2)}) collective-permute-start(bf16[128,1024]{1,0:T(8,128)(2,1)S(1)} %join_blocks.7.refs_1_), channel_id=1, source_target_pairs={{0,4},{4,8},{8,12},{12,0},{1,5},{5,9},{9,13},{13,1},{2,6},{6,10},{... | collective-permute-start | bytes 786440 | tf_op jit(solution)/shard_map/ppermute | solution.py:31
  15.7 12.5 %copy-start.19 = (bf16[1,64,8192]{2,1,0:T(8,128)(2,1)S(1)}, bf16[1,64,8192]{2,1,0:T(8,128)(2,1)}, u32[]{:S(2)}) copy-start(bf16[1,64,8192]{2,1,0:T(8,128)(2,1)} %param.7) | copy-start | bytes 3145732
  15.7 12.5 %collective-permute-start.5 = (bf16[128,1024]{1,0:T(8,128)(2,1)S(1)}, bf16[128,1024]{1,0:T(8,128)(2,1)S(1)}, u32[]{:S(2)}, u32[]{:S(2)}) collective-permute-start(bf16[128,1024]{1,0:T(8,128)(2,1)S(1)} %join_blocks.8), channel_id=1, source_target_pairs={{0,4},{4,8},{8,12},{12,0},{1,5},{5,9},{9,13},{13,1},{2,6},{6,10},{... | collective-permute-start | bytes 786440 | tf_op jit(solution)/shard_map/ppermute | solution.py:31
  23.3 11.0 %collective-permute-start.6 = (bf16[128,1024]{1,0:T(8,128)(2,1)S(1)}, bf16[128,1024]{1,0:T(8,128)(2,1)S(1)}, u32[]{:S(2)}, u32[]{:S(2)}) collective-permute-start(bf16[128,1024]{1,0:T(8,128)(2,1)S(1)} %join_blocks.9), channel_id=1, source_target_pairs={{0,4},{4,8},{8,12},{12,0},{1,5},{5,9},{9,13},{13,1},{2,6},{6,10},{... | collective-permute-start | bytes 786440 | tf_op jit(solution)/shard_map/ppermute | solution.py:31
  28.2 17.4 %copy-start.11 = (bf16[128,1024]{1,0:T(8,128)(2,1)}, bf16[128,1024]{1,0:T(8,128)(2,1)S(1)}, u32[]{:S(2)}) copy-start(bf16[128,1024]{1,0:T(8,128)(2,1)S(1)} %collective-permute-done.5.refs_4_) | copy-start | bytes 786436
  28.2 11.7 %collective-permute-start.7 = (bf16[128,1024]{1,0:T(8,128)(2,1)S(1)}, bf16[128,1024]{1,0:T(8,128)(2,1)S(1)}, u32[]{:S(2)}, u32[]{:S(2)}) collective-permute-start(bf16[128,1024]{1,0:T(8,128)(2,1)S(1)} %collective-permute-done.5.refs_4_), channel_id=1, source_target_pairs={{0,4},{4,8},{8,12},{12,0},{1,5},{5,9},{9,13},{13,1},{2,6},{6,10},{... | collective-permute-start | bytes 786440 | tf_op jit(solution)/shard_map/ppermute | solution.py:31
  29.1 5.2 %collective-permute-start.9 = (bf16[64,1024]{1,0:T(8,128)(2,1)}, bf16[64,1024]{1,0:T(8,128)(2,1)}, u32[]{:S(2)}, u32[]{:S(2)}) collective-permute-start(bf16[64,1024]{1,0:T(8,128)(2,1)} %get-tuple-element.28), channel_id=1, source_target_pairs={{0,1},{1,0},{2,3},{3,2},{4,5},{5,4},{6,7},{7,6},{8,9},{9,8},{10,11... | collective-permute-start | bytes 393224 | tf_op jit(solution)/shard_map/ppermute | solution.py:27
  29.1 13.0 %collective-permute-start.10 = (bf16[64,1024]{1,0:T(8,128)(2,1)}, bf16[64,1024]{1,0:T(8,128)(2,1)}, u32[]{:S(2)}, u32[]{:S(2)}) collective-permute-start(bf16[64,1024]{1,0:T(8,128)(2,1)} %get-tuple-element.30), channel_id=1, source_target_pairs={{0,2},{1,3},{2,0},{3,1},{4,6},{5,7},{6,4},{7,5},{8,10},{9,11},{10,... | collective-permute-start | bytes 393224 | tf_op jit(solution)/shard_map/ppermute | solution.py:27
  31.2 14.3 %collective-permute-start.11 = (bf16[64,1024]{1,0:T(8,128)(2,1)}, bf16[64,1024]{1,0:T(8,128)(2,1)}, u32[]{:S(2)}, u32[]{:S(2)}) collective-permute-start(bf16[64,1024]{1,0:T(8,128)(2,1)} %get-tuple-element.32), channel_id=1, source_target_pairs={{0,3},{1,2},{2,1},{3,0},{4,7},{5,6},{6,5},{7,4},{8,11},{9,10},{10,... | collective-permute-start | bytes 393224 | tf_op jit(solution)/shard_map/ppermute | solution.py:27
  34.3 11.2 %copy-start.13 = (bf16[128,1024]{1,0:T(8,128)(2,1)}, bf16[128,1024]{1,0:T(8,128)(2,1)S(1)}, u32[]{:S(2)}) copy-start(bf16[128,1024]{1,0:T(8,128)(2,1)S(1)} %collective-permute-done.6.refs_5_) | copy-start | bytes 786436
  34.3 11.2 %collective-permute-start.8 = (bf16[128,1024]{1,0:T(8,128)(2,1)S(1)}, bf16[128,1024]{1,0:T(8,128)(2,1)S(1)}, u32[]{:S(2)}, u32[]{:S(2)}) collective-permute-start(bf16[128,1024]{1,0:T(8,128)(2,1)S(1)} %collective-permute-done.6.refs_5_), channel_id=1, source_target_pairs={{0,4},{4,8},{8,12},{12,0},{1,5},{5,9},{9,13},{13,1},{2,6},{6,10},{... | collective-permute-start | bytes 786440 | tf_op jit(solution)/shard_map/ppermute | solution.py:31
  40.7 10.1 %collective-permute-start.12 = (bf16[128,1024]{1,0:T(8,128)(2,1)S(1)}, bf16[128,1024]{1,0:T(8,128)(2,1)S(1)}, u32[]{:S(2)}, u32[]{:S(2)}) collective-permute-start(bf16[128,1024]{1,0:T(8,128)(2,1)S(1)} %pad_maximum_fusion.refs_0_), channel_id=1, source_target_pairs={{0,4},{4,8},{8,12},{12,0},{1,5},{5,9},{9,13},{13,1},{2,6},{6,10},{... | collective-permute-start | bytes 786440 | tf_op jit(solution)/shard_map/ppermute | solution.py:31
  46.7 16.0 %collective-permute-start.13 = (bf16[128,1024]{1,0:T(8,128)(2,1)S(1)}, bf16[128,1024]{1,0:T(8,128)(2,1)S(1)}, u32[]{:S(2)}, u32[]{:S(2)}) collective-permute-start(bf16[128,1024]{1,0:T(8,128)(2,1)S(1)} %join_blocks.10.refs_1_), channel_id=1, source_target_pairs={{0,4},{4,8},{8,12},{12,0},{1,5},{5,9},{9,13},{13,1},{2,6},{6,10},{... | collective-permute-start | bytes 786440 | tf_op jit(solution)/shard_map/ppermute | solution.py:31
  51.4 16.9 %collective-permute-start.14 = (bf16[128,1024]{1,0:T(8,128)(2,1)}, bf16[128,1024]{1,0:T(8,128)(2,1)S(1)}, u32[]{:S(2)}, u32[]{:S(2)}) collective-permute-start(bf16[128,1024]{1,0:T(8,128)(2,1)} %join_blocks.11), channel_id=1, source_target_pairs={{0,4},{4,8},{8,12},{12,0},{1,5},{5,9},{9,13},{13,1},{2,6},{6,10},{... | collective-permute-start | bytes 786440 | tf_op jit(solution)/shard_map/ppermute | solution.py:31
  62.7 8.8 %collective-permute-start.15 = (bf16[128,1024]{1,0:T(8,128)(2,1)S(1)}, bf16[128,1024]{1,0:T(8,128)(2,1)S(1)}, u32[]{:S(2)}, u32[]{:S(2)}) collective-permute-start(bf16[128,1024]{1,0:T(8,128)(2,1)S(1)} %collective-permute-done.13.refs_3_), channel_id=1, source_target_pairs={{0,4},{4,8},{8,12},{12,0},{1,5},{5,9},{9,13},{13,1},{2,6},{6,10},{... | collective-permute-start | bytes 786440 | tf_op jit(solution)/shard_map/ppermute | solution.py:31
  64.1 10.3 %all-to-all-start.1 = ((f32[8,64,128]{2,1,0:T(8,128)}), f32[8,64,128]{2,1,0:T(8,128)S(1)}, u32[]{:S(2)}, u32[]{:S(2)}) async-start(f32[8,64,128]{2,1,0:T(8,128)} %copy-done.1), calls=%async_computation.1 | async-start | bytes 524288 | tf_op jit(solution)/shard_map/all_to_all | solution.py:39
  68.3 11.0 %collective-permute-start.16 = (bf16[128,1024]{1,0:T(8,128)(2,1)S(1)}, bf16[128,1024]{1,0:T(8,128)(2,1)S(1)}, u32[]{:S(2)}, u32[]{:S(2)}) collective-permute-start(bf16[128,1024]{1,0:T(8,128)(2,1)S(1)} %collective-permute-done.14.refs_4_), channel_id=1, source_target_pairs={{0,4},{4,8},{8,12},{12,0},{1,5},{5,9},{9,13},{13,1},{2,6},{6,10},{... | collective-permute-start | bytes 786440 | tf_op jit(solution)/shard_map/ppermute | solution.py:31
  71.5 12.9 %collective-permute-start.17 = (bf16[128,1024]{1,0:T(8,128)(2,1)S(1)}, bf16[128,1024]{1,0:T(8,128)(2,1)S(1)}, u32[]{:S(2)}, u32[]{:S(2)}) collective-permute-start(bf16[128,1024]{1,0:T(8,128)(2,1)S(1)} %collective-permute-done.15.refs_5_), channel_id=1, source_target_pairs={{0,4},{4,8},{8,12},{12,0},{1,5},{5,9},{9,13},{13,1},{2,6},{6,10},{... | collective-permute-start | bytes 786440 | tf_op jit(solution)/shard_map/ppermute | solution.py:31
  75.0 8.5 %all-to-all-start.2 = ((bf16[8,64,128]{2,1,0:T(8,128)(2,1)}), bf16[8,64,128]{2,1,0:T(8,128)(2,1)S(1)}, u32[]{:S(2)}, u32[]{:S(2)}) async-start(bf16[8,64,128]{2,1,0:T(8,128)(2,1)} %summed_copies.1), calls=%async_computation.2 | async-start | bytes 262144 | tf_op jit(solution)/shard_map/all_to_all | solution.py:39
  85.8 10.2 %collective-permute-start.18 = (bf16[128,1024]{1,0:T(8,128)(2,1)S(1)}, bf16[128,1024]{1,0:T(8,128)(2,1)S(1)}, u32[]{:S(2)}, u32[]{:S(2)}) collective-permute-start(bf16[128,1024]{1,0:T(8,128)(2,1)S(1)} %get-tuple-element.35), channel_id=1, source_target_pairs={{0,18},{1,19},{2,16},{3,17},{16,2},{17,3},{18,0},{19,1},{4,22},{5,... | collective-permute-start | bytes 786440 | tf_op jit(solution)/shard_map/ppermute | solution.py:27
  88.4 12.4 %collective-permute-start.19 = (bf16[128,1024]{1,0:T(8,128)(2,1)S(1)}, bf16[128,1024]{1,0:T(8,128)(2,1)S(1)}, u32[]{:S(2)}, u32[]{:S(2)}) collective-permute-start(bf16[128,1024]{1,0:T(8,128)(2,1)S(1)} %get-tuple-element.36), channel_id=1, source_target_pairs={{0,19},{1,18},{2,17},{3,16},{16,3},{17,2},{18,1},{19,0},{4,23},{5,... | collective-permute-start | bytes 786440 | tf_op jit(solution)/shard_map/ppermute | solution.py:27
  89.8 17.7 %collective-permute-start.20 = (bf16[128,1024]{1,0:T(8,128)(2,1)S(1)}, bf16[128,1024]{1,0:T(8,128)(2,1)S(1)}, u32[]{:S(2)}, u32[]{:S(2)}) collective-permute-start(bf16[128,1024]{1,0:T(8,128)(2,1)S(1)} %get-tuple-element.37), channel_id=1, source_target_pairs={{0,16},{1,17},{2,18},{3,19},{16,0},{17,1},{18,2},{19,3},{4,20},{5,... | collective-permute-start | bytes 786440 | tf_op jit(solution)/shard_map/ppermute | solution.py:27
  90.5 19.8 %collective-permute-start.21 = (bf16[128,1024]{1,0:T(8,128)(2,1)S(1)}, bf16[128,1024]{1,0:T(8,128)(2,1)S(1)}, u32[]{:S(2)}, u32[]{:S(2)}) collective-permute-start(bf16[128,1024]{1,0:T(8,128)(2,1)S(1)} %get-tuple-element.38), channel_id=1, source_target_pairs={{0,17},{1,16},{2,19},{3,18},{16,1},{17,0},{18,3},{19,2},{4,21},{5,... | collective-permute-start | bytes 786440 | tf_op jit(solution)/shard_map/ppermute | solution.py:27
  93.7 16.7 %collective-permute-start.22 = (bf16[128,1024]{1,0:T(8,128)(2,1)S(1)}, bf16[128,1024]{1,0:T(8,128)(2,1)S(1)}, u32[]{:S(2)}, u32[]{:S(2)}) collective-permute-start(bf16[128,1024]{1,0:T(8,128)(2,1)S(1)} %get-tuple-element.39), channel_id=1, source_target_pairs={{0,2},{1,3},{2,0},{3,1},{16,18},{17,19},{18,16},{19,17},{4,6},{5,7... | collective-permute-start | bytes 786440 | tf_op jit(solution)/shard_map/ppermute | solution.py:27
  96.0 15.5 %collective-permute-start.23 = (bf16[128,1024]{1,0:T(8,128)(2,1)S(1)}, bf16[128,1024]{1,0:T(8,128)(2,1)S(1)}, u32[]{:S(2)}, u32[]{:S(2)}) collective-permute-start(bf16[128,1024]{1,0:T(8,128)(2,1)S(1)} %get-tuple-element.40), channel_id=1, source_target_pairs={{0,3},{1,2},{2,1},{3,0},{16,19},{17,18},{18,17},{19,16},{4,7},{5,6... | collective-permute-start | bytes 786440 | tf_op jit(solution)/shard_map/ppermute | solution.py:27
  100.9 10.6 %collective-permute-start.24 = (bf16[128,1024]{1,0:T(8,128)(2,1)S(1)}, bf16[128,1024]{1,0:T(8,128)(2,1)S(1)}, u32[]{:S(2)}, u32[]{:S(2)}) collective-permute-start(bf16[128,1024]{1,0:T(8,128)(2,1)S(1)} %get-tuple-element.41), channel_id=1, source_target_pairs={{0,1},{1,0},{2,3},{3,2},{16,17},{17,16},{18,19},{19,18},{4,5},{5,4... | collective-permute-start | bytes 786440 | tf_op jit(solution)/shard_map/ppermute | solution.py:27
  (16 other events, 18.7 us)

commit v29 on v26

--- a/solution.py
+++ b/solution.py
@@ -231,7 +231,7 @@
 
 
 def place_kernel(offsets, me_ref, *refs):
-    blocks, out_ref, sems = refs[:-2], refs[-2], refs[-1]
+    blocks, out_ref, sems = refs[: len(offsets)], refs[-2], refs[-1]
     share = blocks[0].shape[1]
     copies = []
     for n, block in enumerate(blocks):
@@ -243,17 +243,19 @@
         copy.wait()
 
 
-def place(me, offsets, blocks):
-    tok, share = blocks[0].shape
+def place(me, offsets, blocks, width, placed=()):
+    tok = blocks[0].shape[0]
+    count = len(blocks)
     return pl.pallas_call(
         functools.partial(place_kernel, offsets),
-        out_shape=jax.ShapeDtypeStruct((tok, len(blocks) * share), jnp.bfloat16),
-        in_specs=[IN_SMEM] + [ANYWHERE] * len(blocks),
+        out_shape=jax.ShapeDtypeStruct((tok, width), jnp.bfloat16),
+        in_specs=[IN_SMEM] + [ANYWHERE] * (count + len(placed)),
         out_specs=ANYWHERE,
-        scratch_shapes=[pltpu.SemaphoreType.DMA((len(blocks),))],
+        scratch_shapes=[pltpu.SemaphoreType.DMA((count,))],
+        input_output_aliases={1 + count: 0} if placed else {},
         compiler_params=params(),
         name="place_results",
-    )(me, *blocks)
+    )(me, *blocks, *placed)
 
 
 def per_device(token_adapter_index, hidden, adapter_down_maps, adapter_up_maps):
@@ -316,7 +318,9 @@
     for some in offsets[: members // 2], offsets[members // 2 :]:
         results += up_product(labels, me.reshape(1), id_rows, shrunk, up_maps, rank, some)
     returned = [to_partner(r, PLANE, members, n) for r, n in zip(results[:-1], offsets)]
-    return place(me.reshape(1), offsets, returned + results[-1:])
+    early = (members - 1) // 2
+    placed = place(me.reshape(1), offsets[:early] + [0], returned[:early] + results[-1:], width)
+    return place(me.reshape(1), offsets[early:-1], returned[early:], width, [placed])
 
 
 def solution(mesh):

time: 110 us -> 109 us (level)
  local copies, waits for them, and re-layouts: 4 us -> 2.01 us
  Pallas kernels: 16.2 us -> 17.3 us
    all_to_all x3, waiting for transfers between devices: 5.38 us -> 2.89 us  [swap(): return lax.all_to_all(value, PLANE, split_axis=0, concat_axis=0, tiled=True)]
    ppermute x12, waiting for transfers between devices: 35.8 us -> 38.2 us  [next_on_ring(): lax.ppermute(block, 'outer', [(i, (i + 1) % outer) for i in range(outer)])]
    unnamed x14 -> x6, local copies, waits for them, and re-layouts: 1.94 us -> 0.01 us
  transfers between devices with their start and end apart: 28 -> 28, of which waited for: 20 -> 18; matrix products, arithmetic and copies ran while one was open for 2% -> 2% of each run, Pallas kernels for 11% -> 13%
where the time goes in v29:
time: 109 us; the launch traced here: 108 us
  waiting for transfers between devices  59 us (54%)
  starting transfers between devices  28.8 us (26%)
  Pallas kernels  17.3 us (16%)
  local copies, waits for them, and re-layouts  2.01 us (2%)
    ppermute x12, waiting for transfers between devices, next_on_ring(): lax.ppermute(block, 'outer', [(i, (i + 1) % outer) for i in range(outer)])  38.2 us
    ppermute x13, waiting for transfers between devices, to_partner(): return lax.ppermute(value, axes, [(i, i ^ offset) for i in range(size)])  17.9 us
    ppermute x13, starting transfers between devices, to_partner(): return lax.ppermute(value, axes, [(i, i ^ offset) for i in range(size)])  12 us
    all_to_all x3, starting transfers between devices, swap(): return lax.all_to_all(value, PLANE, split_axis=0, concat_axis=0, tiled=True)  11.5 us
    ppermute x12, starting transfers between devices, next_on_ring(): lax.ppermute(block, 'outer', [(i, (i + 1) % outer) for i in range(outer)])  5.28 us
    pallas_call x2, Pallas kernels, up_product(): pl.pallas_call(functools.partial(up_kernel, len(maps), rank, offsets), ou...  5.25 us
    pallas_call x1, Pallas kernels, down_product(): pl.pallas_call(functools.partial(down_kernel, len(maps), rank), out_shape...  4.34 us
    pallas_call x6, Pallas kernels, joined(): pl.pallas_call(join_kernel, out_shape=jax.ShapeDtypeStruct((len(blocks) *...  3.43 us
  transfers between devices with their start and end apart: 28, of which 18 were waited for; matrix products, arithmetic and copies ran while one was open for 2% of the time, Pallas kernels for 13%

profile of v29, /device:TPU:0, one launch (start us, length us, event | category | flops | bytes accessed | tf_op | source)
XLA Modules:
  0.0 108.3 jit_solution(7365504371242228906)
XLA Ops:
  1.7 2.6 %collective-permute-start.1 = (bf16[64,1024]{1,0:T(8,128)(2,1)S(1)}, bf16[64,1024]{1,0:T(8,128)(2,1)S(1)}, u32[]{:S(2)}, u32[]{:S(2)}) collective-permute-start(bf16[64,1024]{1,0:T(8,128)(2,1)S(1)} %get-tuple-element.50), channel_id=1, source_target_pairs={{0,2},{1,3},{2,0},{3,1},{4,6},{5,7},{6,4},{7,5},{8,10},{9,11},{10,... | collective-permute-start | bytes 393224 | tf_op jit(solution)/shard_map/ppermute | solution.py:27
  4.3 1.8 %collective-permute-start.3 = (bf16[128,1024]{1,0:T(8,128)(2,1)S(1)}, bf16[128,1024]{1,0:T(8,128)(2,1)S(1)}, u32[]{:S(2)}, u32[]{:S(2)}) collective-permute-start(bf16[128,1024]{1,0:T(8,128)(2,1)S(1)} %join_blocks.6.refs_0_), channel_id=1, source_target_pairs={{0,4},{4,8},{8,12},{12,0},{1,5},{5,9},{9,13},{13,1},{2,6},{6,10},{... | collective-permute-start | bytes 786440 | tf_op jit(solution)/shard_map/ppermute | solution.py:31
  6.2 1.6 %outgoing_rows.1 = bf16[8,136,1024]{2,1,0:T(8,128)(2,1)} custom-call(bf16[128,8192]{1,0:T(8,128)(2,1)S(1)} %copy-done, s32[1,128]{1,0:T(1,128)S(1)} %bitcast.26), custom_call_target="tpu_custom_call" | custom-call | tf_op jit(solution)/shard_map/outgoing_rows/pallas_call | solution.py:94
  7.8 3.7 %all-to-all-start = ((bf16[8,136,1024]{2,1,0:T(8,128)(2,1)}), bf16[8,136,1024]{2,1,0:T(8,128)(2,1)S(1)}, u32[]{:S(2)}, u32[]{:S(2)}) async-start(bf16[8,136,1024]{2,1,0:T(8,128)(2,1)} %outgoing_rows.1), calls=%async_computation | async-start | bytes 4456448 | tf_op jit(solution)/shard_map/all_to_all | solution.py:39
  11.6 1.6 %collective-permute-start.4 = (bf16[128,1024]{1,0:T(8,128)(2,1)S(1)}, bf16[128,1024]{1,0:T(8,128)(2,1)S(1)}, u32[]{:S(2)}, u32[]{:S(2)}) collective-permute-start(bf16[128,1024]{1,0:T(8,128)(2,1)S(1)} %join_blocks.7.refs_1_), channel_id=1, source_target_pairs={{0,4},{4,8},{8,12},{12,0},{1,5},{5,9},{9,13},{13,1},{2,6},{6,10},{... | collective-permute-start | bytes 786440 | tf_op jit(solution)/shard_map/ppermute | solution.py:31
  13.2 1.8 %collective-permute-done.3.refs_0_.refs_2_ = bf16[128,1024]{1,0:T(8,128)(2,1)S(1)} collective-permute-done((bf16[128,1024]{1,0:T(8,128)(2,1)S(1)}, bf16[128,1024]{1,0:T(8,128)(2,1)S(1)}, u32[]{:S(2)}, u32[]{:S(2)}) %collective-permute-start.3) | collective-permute-done | bytes 262176 | tf_op jit(solution)/shard_map/ppermute | solution.py:31
  15.1 7.4 %collective-permute-done.4.refs_0_.refs_3_ = bf16[128,1024]{1,0:T(8,128)(2,1)S(1)} collective-permute-done((bf16[128,1024]{1,0:T(8,128)(2,1)S(1)}, bf16[128,1024]{1,0:T(8,128)(2,1)S(1)}, u32[]{:S(2)}, u32[]{:S(2)}) %collective-permute-start.4) | collective-permute-done | bytes 262176 | tf_op jit(solution)/shard_map/ppermute | solution.py:31
  22.6 5.6 %collective-permute-done.5.refs_4_ = bf16[128,1024]{1,0:T(8,128)(2,1)} collective-permute-done((bf16[128,1024]{1,0:T(8,128)(2,1)S(1)}, bf16[128,1024]{1,0:T(8,128)(2,1)}, u32[]{:S(2)}, u32[]{:S(2)}) %collective-permute-start.5) | collective-permute-done | bytes 262176 | tf_op jit(solution)/shard_map/ppermute | solution.py:31
  29.1 2.1 %collective-permute-start.10 = (bf16[64,1024]{1,0:T(8,128)(2,1)}, bf16[64,1024]{1,0:T(8,128)(2,1)}, u32[]{:S(2)}, u32[]{:S(2)}) collective-permute-start(bf16[64,1024]{1,0:T(8,128)(2,1)} %get-tuple-element.30), channel_id=1, source_target_pairs={{0,2},{1,3},{2,0},{3,1},{4,6},{5,7},{6,4},{7,5},{8,10},{9,11},{10,... | collective-permute-start | bytes 393224 | tf_op jit(solution)/shard_map/ppermute | solution.py:27
  31.4 2.5 %collective-permute-done.6.refs_5_ = bf16[128,1024]{1,0:T(8,128)(2,1)} collective-permute-done((bf16[128,1024]{1,0:T(8,128)(2,1)S(1)}, bf16[128,1024]{1,0:T(8,128)(2,1)}, u32[]{:S(2)}, u32[]{:S(2)}) %collective-permute-start.6) | collective-permute-done | bytes 262176 | tf_op jit(solution)/shard_map/ppermute | solution.py:31
  34.9 4.7 %collective-permute-done.7.refs_6_ = bf16[128,1024]{1,0:T(8,128)(2,1)} collective-permute-done((bf16[128,1024]{1,0:T(8,128)(2,1)}, bf16[128,1024]{1,0:T(8,128)(2,1)}, u32[]{:S(2)}, u32[]{:S(2)}) %collective-permute-start.7) | collective-permute-done | bytes 262176 | tf_op jit(solution)/shard_map/ppermute | solution.py:31
  39.8 2.2 %collective-permute-done.10.refs_0_ = bf16[64,1024]{1,0:T(8,128)(2,1)} collective-permute-done((bf16[64,1024]{1,0:T(8,128)(2,1)}, bf16[64,1024]{1,0:T(8,128)(2,1)}, u32[]{:S(2)}, u32[]{:S(2)}) %collective-permute-start.10) | collective-permute-done | bytes 131104 | tf_op jit(solution)/shard_map/ppermute | solution.py:27
  42.0 3.2 %collective-permute-done.8.refs_7_ = bf16[128,1024]{1,0:T(8,128)(2,1)} collective-permute-done((bf16[128,1024]{1,0:T(8,128)(2,1)}, bf16[128,1024]{1,0:T(8,128)(2,1)}, u32[]{:S(2)}, u32[]{:S(2)}) %collective-permute-start.8) | collective-permute-done | bytes 262176 | tf_op jit(solution)/shard_map/ppermute | solution.py:31
  45.2 1.7 %join_blocks.10.refs_1_ = bf16[128,1024]{1,0:T(8,128)(2,1)} custom-call(bf16[64,1024]{1,0:T(8,128)(2,1)} %collective-permute-done.10.refs_0_, bf16[64,1024]{1,0:T(8,128)(2,1)} %collective-permute-done.11.refs_1_), custom_call_target="tpu_custom_call" | custom-call | flops 1500000000 | bytes 1000000 | tf_op jit(solution)/shard_map/join_blocks/pallas_call | solution.py:60
  47.1 3.2 %collective-permute-done.12.refs_0_.refs_2_ = bf16[128,1024]{1,0:T(8,128)(2,1)} collective-permute-done((bf16[128,1024]{1,0:T(8,128)(2,1)S(1)}, bf16[128,1024]{1,0:T(8,128)(2,1)}, u32[]{:S(2)}, u32[]{:S(2)}) %collective-permute-start.12) | collective-permute-done | bytes 262176 | tf_op jit(solution)/shard_map/ppermute | solution.py:31
  50.3 1.7 %join_blocks.11 = bf16[128,1024]{1,0:T(8,128)(2,1)} custom-call(bf16[128,1024]{1,0:T(8,128)(2,1)} %collective-permute-done.12.refs_0_.refs_2_), custom_call_target="tpu_custom_call" | custom-call | flops 6000000000 | bytes 1000000 | tf_op jit(solution)/shard_map/join_blocks/pallas_call | solution.py:60
  52.0 4.3 %down_product.1 = (f32[8,64,128]{2,1,0:T(8,128)}, f32[8,128]{1,0:T(8,128)S(1)}) custom-call(s32[16]{0:T(128)S(1)} %add.61.labels_ref, bf16[8,136,1024]{2,1,0:T(8,128)(2,1)S(1)} %all-to-all-done.rows_ref, bf16[128,1024]{1,0:T(8,128)(2,1)S(1)} %join_blocks.6.refs_0_, bf16[128,1024]{1,0:T(8,128)(2,1)S(1)} %join_blocks.7.refs_1_, ...), custom_call_target="tpu_custom_call" | custom-call | flops 2147483648 | bytes 4194304 | tf_op jit(solution)/shard_map/down_product/pallas_call | solution.py:146
  56.6 1.2 %collective-permute-start.15 = (bf16[128,1024]{1,0:T(8,128)(2,1)}, bf16[128,1024]{1,0:T(8,128)(2,1)S(1)}, u32[]{:S(2)}, u32[]{:S(2)}) collective-permute-start(bf16[128,1024]{1,0:T(8,128)(2,1)} %collective-permute-done.13.refs_3_), channel_id=1, source_target_pairs={{0,4},{4,8},{8,12},{12,0},{1,5},{5,9},{9,13},{13,1},{2,6},{6,10},{... | collective-permute-start | bytes 786440 | tf_op jit(solution)/shard_map/ppermute | solution.py:31
  57.7 4.4 %all-to-all-start.1 = ((f32[8,64,128]{2,1,0:T(8,128)}), f32[8,64,128]{2,1,0:T(8,128)S(1)}, u32[]{:S(2)}, u32[]{:S(2)}) async-start(f32[8,64,128]{2,1,0:T(8,128)} %get-tuple-element.26), calls=%async_computation.1 | async-start | bytes 524288 | tf_op jit(solution)/shard_map/all_to_all | solution.py:39
  62.1 1.3 %collective-permute-done.14.refs_4_ = bf16[128,1024]{1,0:T(8,128)(2,1)} collective-permute-done((bf16[128,1024]{1,0:T(8,128)(2,1)}, bf16[128,1024]{1,0:T(8,128)(2,1)}, u32[]{:S(2)}, u32[]{:S(2)}) %collective-permute-start.14) | collective-permute-done | bytes 262176 | tf_op jit(solution)/shard_map/ppermute | solution.py:31
  63.7 4.3 %collective-permute-done.15.refs_5_ = bf16[128,1024]{1,0:T(8,128)(2,1)S(1)} collective-permute-done((bf16[128,1024]{1,0:T(8,128)(2,1)}, bf16[128,1024]{1,0:T(8,128)(2,1)S(1)}, u32[]{:S(2)}, u32[]{:S(2)}) %collective-permute-start.15) | collective-permute-done | bytes 262176 | tf_op jit(solution)/shard_map/ppermute | solution.py:31
  68.8 3.4 %all-to-all-start.2 = ((bf16[8,64,128]{2,1,0:T(8,128)(2,1)}), bf16[8,64,128]{2,1,0:T(8,128)(2,1)S(1)}, u32[]{:S(2)}, u32[]{:S(2)}) async-start(bf16[8,64,128]{2,1,0:T(8,128)(2,1)} %summed_copies.1), calls=%async_computation.2 | async-start | bytes 262144 | tf_op jit(solution)/shard_map/all_to_all | solution.py:39
  72.2 2.4 %collective-permute-done.16.refs_6_ = bf16[128,1024]{1,0:T(8,128)(2,1)S(1)} collective-permute-done((bf16[128,1024]{1,0:T(8,128)(2,1)}, bf16[128,1024]{1,0:T(8,128)(2,1)S(1)}, u32[]{:S(2)}, u32[]{:S(2)}) %collective-permute-start.16) | collective-permute-done | bytes 262176 | tf_op jit(solution)/shard_map/ppermute | solution.py:31
  74.6 2.7 %all-to-all-done.2.shrunk_ref = bf16[8,64,128]{2,1,0:T(8,128)(2,1)S(1)} async-done(((bf16[8,64,128]{2,1,0:T(8,128)(2,1)}), bf16[8,64,128]{2,1,0:T(8,128)(2,1)S(1)}, u32[]{:S(2)}, u32[]{:S(2)}) %all-to-all-start.2) | async-done | bytes 131104 | tf_op jit(solution)/shard_map/all_to_all | solution.py:39
  77.3 1.5 %collective-permute-done.17.refs_7_ = bf16[128,1024]{1,0:T(8,128)(2,1)S(1)} collective-permute-done((bf16[128,1024]{1,0:T(8,128)(2,1)S(1)}, bf16[128,1024]{1,0:T(8,128)(2,1)S(1)}, u32[]{:S(2)}, u32[]{:S(2)}) %collective-permute-start.17) | collective-permute-done | bytes 262176 | tf_op jit(solution)/shard_map/ppermute | solution.py:31
  78.9 2.6 %up_product.2 = (bf16[128,1024]{1,0:T(8,128)(2,1)S(1)}, bf16[128,1024]{1,0:T(8,128)(2,1)S(1)}, bf16[128,1024]{1,0:T(8,128)(2,1)S(1)}, bf16[128,1024]{1,0:T(8,128)(2,1)S(1)}) custom-call(s32[16]{0:T(128)S(1)} %add.61.labels_ref, s32[1]{0:T(128)} %bitcast.me_ref, f32[8,128]{1,0:T(8,128)S(1)} %get-tuple-element.25.ids_ref, ...), custom_call_target="tpu_custom_call" | custom-call | flops 1073741824 | bytes 3145728 | tf_op jit(solution)/shard_map/up_product/pallas_call | solution.py:217
  81.5 2.2 %collective-permute-start.22 = (bf16[128,1024]{1,0:T(8,128)(2,1)S(1)}, bf16[128,1024]{1,0:T(8,128)(2,1)S(1)}, u32[]{:S(2)}, u32[]{:S(2)}) collective-permute-start(bf16[128,1024]{1,0:T(8,128)(2,1)S(1)} %get-tuple-element.39), channel_id=1, source_target_pairs={{0,18},{1,19},{2,16},{3,17},{16,2},{17,3},{18,0},{19,1},{4,22},{5,... | collective-permute-start | bytes 786440 | tf_op jit(solution)/shard_map/ppermute | solution.py:27
  83.7 1.9 %collective-permute-start.18 = (bf16[128,1024]{1,0:T(8,128)(2,1)S(1)}, bf16[128,1024]{1,0:T(8,128)(2,1)S(1)}, u32[]{:S(2)}, u32[]{:S(2)}) collective-permute-start(bf16[128,1024]{1,0:T(8,128)(2,1)S(1)} %get-tuple-element.35), channel_id=1, source_target_pairs={{0,17},{1,16},{2,19},{3,18},{16,1},{17,0},{18,3},{19,2},{4,21},{5,... | collective-permute-start | bytes 786440 | tf_op jit(solution)/shard_map/ppermute | solution.py:27
  85.7 2.6 %up_product.3 = (bf16[128,1024]{1,0:T(8,128)(2,1)S(1)}, bf16[128,1024]{1,0:T(8,128)(2,1)S(1)}, bf16[128,1024]{1,0:T(8,128)(2,1)S(1)}, bf16[128,1024]{1,0:T(8,128)(2,1)S(1)}) custom-call(s32[16]{0:T(128)S(1)} %add.61.labels_ref, s32[1]{0:T(128)} %bitcast.me_ref, f32[8,128]{1,0:T(8,128)S(1)} %get-tuple-element.25.ids_ref, ...), custom_call_target="tpu_custom_call" | custom-call | flops 1073741824 | bytes 3145728 | tf_op jit(solution)/shard_map/up_product/pallas_call | solution.py:217
  88.3 1.3 %collective-permute-start.19 = (bf16[128,1024]{1,0:T(8,128)(2,1)S(1)}, bf16[128,1024]{1,0:T(8,128)(2,1)S(1)}, u32[]{:S(2)}, u32[]{:S(2)}) collective-permute-start(bf16[128,1024]{1,0:T(8,128)(2,1)S(1)} %get-tuple-element.36), channel_id=1, source_target_pairs={{0,2},{1,3},{2,0},{3,1},{16,18},{17,19},{18,16},{19,17},{4,6},{5,7... | collective-permute-start | bytes 786440 | tf_op jit(solution)/shard_map/ppermute | solution.py:27
  91.2 4.9 %collective-permute-done.23.refs_1_ = bf16[128,1024]{1,0:T(8,128)(2,1)S(1)} collective-permute-done((bf16[128,1024]{1,0:T(8,128)(2,1)S(1)}, bf16[128,1024]{1,0:T(8,128)(2,1)S(1)}, u32[]{:S(2)}, u32[]{:S(2)}) %collective-permute-start.23) | collective-permute-done | bytes 262176 | tf_op jit(solution)/shard_map/ppermute | solution.py:27
  96.6 9.7 %collective-permute-done.24.refs_2_ = bf16[128,1024]{1,0:T(8,128)(2,1)S(1)} collective-permute-done((bf16[128,1024]{1,0:T(8,128)(2,1)S(1)}, bf16[128,1024]{1,0:T(8,128)(2,1)S(1)}, u32[]{:S(2)}, u32[]{:S(2)}) %collective-permute-start.24) | collective-permute-done | bytes 262176 | tf_op jit(solution)/shard_map/ppermute | solution.py:27
  (49 shorter events, 9.7 us)
Async XLA Ops:
  1.1 3.2 %collective-permute-start = (bf16[64,1024]{1,0:T(8,128)(2,1)S(1)}, bf16[64,1024]{1,0:T(8,128)(2,1)S(1)}, u32[]{:S(2)}, u32[]{:S(2)}) collective-permute-start(bf16[64,1024]{1,0:T(8,128)(2,1)S(1)} %get-tuple-element.48), channel_id=1, source_target_pairs={{0,1},{1,0},{2,3},{3,2},{4,5},{5,4},{6,7},{7,6},{8,9},{9,8},{10,11... | collective-permute-start | bytes 393224 | tf_op jit(solution)/shard_map/ppermute | solution.py:27
  1.7 9.9 %collective-permute-start.1 = (bf16[64,1024]{1,0:T(8,128)(2,1)S(1)}, bf16[64,1024]{1,0:T(8,128)(2,1)S(1)}, u32[]{:S(2)}, u32[]{:S(2)}) collective-permute-start(bf16[64,1024]{1,0:T(8,128)(2,1)S(1)} %get-tuple-element.50), channel_id=1, source_target_pairs={{0,2},{1,3},{2,0},{3,1},{4,6},{5,7},{6,4},{7,5},{8,10},{9,11},{10,... | collective-permute-start | bytes 393224 | tf_op jit(solution)/shard_map/ppermute | solution.py:27
  4.2 7.3 %collective-permute-start.2 = (bf16[64,1024]{1,0:T(8,128)(2,1)S(1)}, bf16[64,1024]{1,0:T(8,128)(2,1)S(1)}, u32[]{:S(2)}, u32[]{:S(2)}) collective-permute-start(bf16[64,1024]{1,0:T(8,128)(2,1)S(1)} %get-tuple-element.47), channel_id=1, source_target_pairs={{0,3},{1,2},{2,1},{3,0},{4,7},{5,6},{6,5},{7,4},{8,11},{9,10},{10,... | collective-permute-start | bytes 393224 | tf_op jit(solution)/shard_map/ppermute | solution.py:27
  4.3 1.9 %copy-start = (bf16[128,8192]{1,0:T(8,128)(2,1)S(1)}, bf16[128,8192]{1,0:T(8,128)(2,1)}, u32[]{:S(2)}) copy-start(bf16[128,8192]{1,0:T(8,128)(2,1)} %hidden_ref) | copy-start | bytes 6291460
  4.3 1.9 %copy-start.1 = (s32[128,1]{0,1:T(1,128)S(1)}, s32[128,1]{0,1:T(1,128)}, u32[]{:S(2)}) copy-start(s32[128,1]{0,1:T(1,128)} %param.4) | copy-start | bytes 1540
  4.3 10.7 %collective-permute-start.3 = (bf16[128,1024]{1,0:T(8,128)(2,1)S(1)}, bf16[128,1024]{1,0:T(8,128)(2,1)S(1)}, u32[]{:S(2)}, u32[]{:S(2)}) collective-permute-start(bf16[128,1024]{1,0:T(8,128)(2,1)S(1)} %join_blocks.6.refs_0_), channel_id=1, source_target_pairs={{0,4},{4,8},{8,12},{12,0},{1,5},{5,9},{9,13},{13,1},{2,6},{6,10},{... | collective-permute-start | bytes 786440 | tf_op jit(solution)/shard_map/ppermute | solution.py:31
  7.8 44.2 %all-to-all-start = ((bf16[8,136,1024]{2,1,0:T(8,128)(2,1)}), bf16[8,136,1024]{2,1,0:T(8,128)(2,1)S(1)}, u32[]{:S(2)}, u32[]{:S(2)}) async-start(bf16[8,136,1024]{2,1,0:T(8,128)(2,1)} %outgoing_rows.1), calls=%async_computation | async-start | bytes 4456448 | tf_op jit(solution)/shard_map/all_to_all | solution.py:39
  11.6 11.0 %collective-permute-start.4 = (bf16[128,1024]{1,0:T(8,128)(2,1)S(1)}, bf16[128,1024]{1,0:T(8,128)(2,1)S(1)}, u32[]{:S(2)}, u32[]{:S(2)}) collective-permute-start(bf16[128,1024]{1,0:T(8,128)(2,1)S(1)} %join_blocks.7.refs_1_), channel_id=1, source_target_pairs={{0,4},{4,8},{8,12},{12,0},{1,5},{5,9},{9,13},{13,1},{2,6},{6,10},{... | collective-permute-start | bytes 786440 | tf_op jit(solution)/shard_map/ppermute | solution.py:31
  15.0 13.2 %copy-start.2 = (bf16[1,64,8192]{2,1,0:T(8,128)(2,1)S(1)}, bf16[1,64,8192]{2,1,0:T(8,128)(2,1)}, u32[]{:S(2)}) copy-start(bf16[1,64,8192]{2,1,0:T(8,128)(2,1)} %param.7) | copy-start | bytes 3145732
  15.1 13.2 %collective-permute-start.5 = (bf16[128,1024]{1,0:T(8,128)(2,1)S(1)}, bf16[128,1024]{1,0:T(8,128)(2,1)}, u32[]{:S(2)}, u32[]{:S(2)}) collective-permute-start(bf16[128,1024]{1,0:T(8,128)(2,1)S(1)} %join_blocks.8), channel_id=1, source_target_pairs={{0,4},{4,8},{8,12},{12,0},{1,5},{5,9},{9,13},{13,1},{2,6},{6,10},{... | collective-permute-start | bytes 786440 | tf_op jit(solution)/shard_map/ppermute | solution.py:31
  22.6 11.3 %collective-permute-start.6 = (bf16[128,1024]{1,0:T(8,128)(2,1)S(1)}, bf16[128,1024]{1,0:T(8,128)(2,1)}, u32[]{:S(2)}, u32[]{:S(2)}) collective-permute-start(bf16[128,1024]{1,0:T(8,128)(2,1)S(1)} %join_blocks.9), channel_id=1, source_target_pairs={{0,4},{4,8},{8,12},{12,0},{1,5},{5,9},{9,13},{13,1},{2,6},{6,10},{... | collective-permute-start | bytes 786440 | tf_op jit(solution)/shard_map/ppermute | solution.py:31
  28.3 11.4 %collective-permute-start.7 = (bf16[128,1024]{1,0:T(8,128)(2,1)}, bf16[128,1024]{1,0:T(8,128)(2,1)}, u32[]{:S(2)}, u32[]{:S(2)}) collective-permute-start(bf16[128,1024]{1,0:T(8,128)(2,1)} %collective-permute-done.5.refs_4_), channel_id=1, source_target_pairs={{0,4},{4,8},{8,12},{12,0},{1,5},{5,9},{9,13},{13,1},{2,6},{6,10},{... | collective-permute-start | bytes 786440 | tf_op jit(solution)/shard_map/ppermute | solution.py:31
  29.1 4.8 %collective-permute-start.9 = (bf16[64,1024]{1,0:T(8,128)(2,1)}, bf16[64,1024]{1,0:T(8,128)(2,1)}, u32[]{:S(2)}, u32[]{:S(2)}) collective-permute-start(bf16[64,1024]{1,0:T(8,128)(2,1)} %get-tuple-element.28), channel_id=1, source_target_pairs={{0,1},{1,0},{2,3},{3,2},{4,5},{5,4},{6,7},{7,6},{8,9},{9,8},{10,11... | collective-permute-start | bytes 393224 | tf_op jit(solution)/shard_map/ppermute | solution.py:27
  29.1 13.0 %collective-permute-start.10 = (bf16[64,1024]{1,0:T(8,128)(2,1)}, bf16[64,1024]{1,0:T(8,128)(2,1)}, u32[]{:S(2)}, u32[]{:S(2)}) collective-permute-start(bf16[64,1024]{1,0:T(8,128)(2,1)} %get-tuple-element.30), channel_id=1, source_target_pairs={{0,2},{1,3},{2,0},{3,1},{4,6},{5,7},{6,4},{7,5},{8,10},{9,11},{10,... | collective-permute-start | bytes 393224 | tf_op jit(solution)/shard_map/ppermute | solution.py:27
  31.2 14.0 %collective-permute-start.11 = (bf16[64,1024]{1,0:T(8,128)(2,1)}, bf16[64,1024]{1,0:T(8,128)(2,1)}, u32[]{:S(2)}, u32[]{:S(2)}) collective-permute-start(bf16[64,1024]{1,0:T(8,128)(2,1)} %get-tuple-element.32), channel_id=1, source_target_pairs={{0,3},{1,2},{2,1},{3,0},{4,7},{5,6},{6,5},{7,4},{8,11},{9,10},{10,... | collective-permute-start | bytes 393224 | tf_op jit(solution)/shard_map/ppermute | solution.py:27
  33.9 11.4 %collective-permute-start.8 = (bf16[128,1024]{1,0:T(8,128)(2,1)}, bf16[128,1024]{1,0:T(8,128)(2,1)}, u32[]{:S(2)}, u32[]{:S(2)}) collective-permute-start(bf16[128,1024]{1,0:T(8,128)(2,1)} %collective-permute-done.6.refs_5_), channel_id=1, source_target_pairs={{0,4},{4,8},{8,12},{12,0},{1,5},{5,9},{9,13},{13,1},{2,6},{6,10},{... | collective-permute-start | bytes 786440 | tf_op jit(solution)/shard_map/ppermute | solution.py:31
  39.6 10.7 %collective-permute-start.12 = (bf16[128,1024]{1,0:T(8,128)(2,1)S(1)}, bf16[128,1024]{1,0:T(8,128)(2,1)}, u32[]{:S(2)}, u32[]{:S(2)}) collective-permute-start(bf16[128,1024]{1,0:T(8,128)(2,1)S(1)} %pad_maximum_fusion.refs_0_), channel_id=1, source_target_pairs={{0,4},{4,8},{8,12},{12,0},{1,5},{5,9},{9,13},{13,1},{2,6},{6,10},{... | collective-permute-start | bytes 786440 | tf_op jit(solution)/shard_map/ppermute | solution.py:31
  46.9 9.6 %collective-permute-start.13 = (bf16[128,1024]{1,0:T(8,128)(2,1)}, bf16[128,1024]{1,0:T(8,128)(2,1)}, u32[]{:S(2)}, u32[]{:S(2)}) collective-permute-start(bf16[128,1024]{1,0:T(8,128)(2,1)} %join_blocks.10.refs_1_), channel_id=1, source_target_pairs={{0,4},{4,8},{8,12},{12,0},{1,5},{5,9},{9,13},{13,1},{2,6},{6,10},{... | collective-permute-start | bytes 786440 | tf_op jit(solution)/shard_map/ppermute | solution.py:31
  52.0 11.3 %collective-permute-start.14 = (bf16[128,1024]{1,0:T(8,128)(2,1)}, bf16[128,1024]{1,0:T(8,128)(2,1)}, u32[]{:S(2)}, u32[]{:S(2)}) collective-permute-start(bf16[128,1024]{1,0:T(8,128)(2,1)} %join_blocks.11), channel_id=1, source_target_pairs={{0,4},{4,8},{8,12},{12,0},{1,5},{5,9},{9,13},{13,1},{2,6},{6,10},{... | collective-permute-start | bytes 786440 | tf_op jit(solution)/shard_map/ppermute | solution.py:31
  56.6 11.4 %collective-permute-start.15 = (bf16[128,1024]{1,0:T(8,128)(2,1)}, bf16[128,1024]{1,0:T(8,128)(2,1)S(1)}, u32[]{:S(2)}, u32[]{:S(2)}) collective-permute-start(bf16[128,1024]{1,0:T(8,128)(2,1)} %collective-permute-done.13.refs_3_), channel_id=1, source_target_pairs={{0,4},{4,8},{8,12},{12,0},{1,5},{5,9},{9,13},{13,1},{2,6},{6,10},{... | collective-permute-start | bytes 786440 | tf_op jit(solution)/shard_map/ppermute | solution.py:31
  57.7 10.4 %all-to-all-start.1 = ((f32[8,64,128]{2,1,0:T(8,128)}), f32[8,64,128]{2,1,0:T(8,128)S(1)}, u32[]{:S(2)}, u32[]{:S(2)}) async-start(f32[8,64,128]{2,1,0:T(8,128)} %get-tuple-element.26), calls=%async_computation.1 | async-start | bytes 524288 | tf_op jit(solution)/shard_map/all_to_all | solution.py:39
  63.4 11.3 %collective-permute-start.16 = (bf16[128,1024]{1,0:T(8,128)(2,1)}, bf16[128,1024]{1,0:T(8,128)(2,1)S(1)}, u32[]{:S(2)}, u32[]{:S(2)}) collective-permute-start(bf16[128,1024]{1,0:T(8,128)(2,1)} %collective-permute-done.14.refs_4_), channel_id=1, source_target_pairs={{0,4},{4,8},{8,12},{12,0},{1,5},{5,9},{9,13},{13,1},{2,6},{6,10},{... | collective-permute-start | bytes 786440 | tf_op jit(solution)/shard_map/ppermute | solution.py:31
  68.0 10.9 %collective-permute-start.17 = (bf16[128,1024]{1,0:T(8,128)(2,1)S(1)}, bf16[128,1024]{1,0:T(8,128)(2,1)S(1)}, u32[]{:S(2)}, u32[]{:S(2)}) collective-permute-start(bf16[128,1024]{1,0:T(8,128)(2,1)S(1)} %collective-permute-done.15.refs_5_), channel_id=1, source_target_pairs={{0,4},{4,8},{8,12},{12,0},{1,5},{5,9},{9,13},{13,1},{2,6},{6,10},{... | collective-permute-start | bytes 786440 | tf_op jit(solution)/shard_map/ppermute | solution.py:31
  68.8 8.5 %all-to-all-start.2 = ((bf16[8,64,128]{2,1,0:T(8,128)(2,1)}), bf16[8,64,128]{2,1,0:T(8,128)(2,1)S(1)}, u32[]{:S(2)}, u32[]{:S(2)}) async-start(bf16[8,64,128]{2,1,0:T(8,128)(2,1)} %summed_copies.1), calls=%async_computation.2 | async-start | bytes 262144 | tf_op jit(solution)/shard_map/all_to_all | solution.py:39
  81.5 9.7 %collective-permute-start.22 = (bf16[128,1024]{1,0:T(8,128)(2,1)S(1)}, bf16[128,1024]{1,0:T(8,128)(2,1)S(1)}, u32[]{:S(2)}, u32[]{:S(2)}) collective-permute-start(bf16[128,1024]{1,0:T(8,128)(2,1)S(1)} %get-tuple-element.39), channel_id=1, source_target_pairs={{0,18},{1,19},{2,16},{3,17},{16,2},{17,3},{18,0},{19,1},{4,22},{5,... | collective-permute-start | bytes 786440 | tf_op jit(solution)/shard_map/ppermute | solution.py:27
  83.7 12.4 %collective-permute-start.23 = (bf16[128,1024]{1,0:T(8,128)(2,1)S(1)}, bf16[128,1024]{1,0:T(8,128)(2,1)S(1)}, u32[]{:S(2)}, u32[]{:S(2)}) collective-permute-start(bf16[128,1024]{1,0:T(8,128)(2,1)S(1)} %get-tuple-element.40), channel_id=1, source_target_pairs={{0,19},{1,18},{2,17},{3,16},{16,3},{17,2},{18,1},{19,0},{4,23},{5,... | collective-permute-start | bytes 786440 | tf_op jit(solution)/shard_map/ppermute | solution.py:27
  83.7 23.6 %collective-permute-start.18 = (bf16[128,1024]{1,0:T(8,128)(2,1)S(1)}, bf16[128,1024]{1,0:T(8,128)(2,1)S(1)}, u32[]{:S(2)}, u32[]{:S(2)}) collective-permute-start(bf16[128,1024]{1,0:T(8,128)(2,1)S(1)} %get-tuple-element.35), channel_id=1, source_target_pairs={{0,17},{1,16},{2,19},{3,18},{16,1},{17,0},{18,3},{19,2},{4,21},{5,... | collective-permute-start | bytes 786440 | tf_op jit(solution)/shard_map/ppermute | solution.py:27
  88.3 19.0 %collective-permute-start.19 = (bf16[128,1024]{1,0:T(8,128)(2,1)S(1)}, bf16[128,1024]{1,0:T(8,128)(2,1)S(1)}, u32[]{:S(2)}, u32[]{:S(2)}) collective-permute-start(bf16[128,1024]{1,0:T(8,128)(2,1)S(1)} %get-tuple-element.36), channel_id=1, source_target_pairs={{0,2},{1,3},{2,0},{3,1},{16,18},{17,19},{18,16},{19,17},{4,6},{5,7... | collective-permute-start | bytes 786440 | tf_op jit(solution)/shard_map/ppermute | solution.py:27
  89.6 16.7 %collective-permute-start.24 = (bf16[128,1024]{1,0:T(8,128)(2,1)S(1)}, bf16[128,1024]{1,0:T(8,128)(2,1)S(1)}, u32[]{:S(2)}, u32[]{:S(2)}) collective-permute-start(bf16[128,1024]{1,0:T(8,128)(2,1)S(1)} %get-tuple-element.41), channel_id=1, source_target_pairs={{0,16},{1,17},{2,18},{3,19},{16,0},{17,1},{18,2},{19,3},{4,20},{5,... | collective-permute-start | bytes 786440 | tf_op jit(solution)/shard_map/ppermute | solution.py:27
  91.2 16.1 %collective-permute-start.20 = (bf16[128,1024]{1,0:T(8,128)(2,1)S(1)}, bf16[128,1024]{1,0:T(8,128)(2,1)S(1)}, u32[]{:S(2)}, u32[]{:S(2)}) collective-permute-start(bf16[128,1024]{1,0:T(8,128)(2,1)S(1)} %get-tuple-element.37), channel_id=1, source_target_pairs={{0,3},{1,2},{2,1},{3,0},{16,19},{17,18},{18,17},{19,16},{4,7},{5,6... | collective-permute-start | bytes 786440 | tf_op jit(solution)/shard_map/ppermute | solution.py:27
  96.1 11.2 %collective-permute-start.21 = (bf16[128,1024]{1,0:T(8,128)(2,1)S(1)}, bf16[128,1024]{1,0:T(8,128)(2,1)S(1)}, u32[]{:S(2)}, u32[]{:S(2)}) collective-permute-start(bf16[128,1024]{1,0:T(8,128)(2,1)S(1)} %get-tuple-element.38), channel_id=1, source_target_pairs={{0,1},{1,0},{2,3},{3,2},{16,17},{17,16},{18,19},{19,18},{4,5},{5,4... | collective-permute-start | bytes 786440 | tf_op jit(solution)/shard_map/ppermute | solution.py:27

commit v30 on v29

--- a/solution.py
+++ b/solution.py
@@ -318,7 +318,7 @@
     for some in offsets[: members // 2], offsets[members // 2 :]:
         results += up_product(labels, me.reshape(1), id_rows, shrunk, up_maps, rank, some)
     returned = [to_partner(r, PLANE, members, n) for r, n in zip(results[:-1], offsets)]
-    early = (members - 1) // 2
+    early = (members - 1) // 3
     placed = place(me.reshape(1), offsets[:early] + [0], returned[:early] + results[-1:], width)
     return place(me.reshape(1), offsets[early:-1], returned[early:], width, [placed])
 

time: 109 us -> 110 us (level)
  local copies, waits for them, and re-layouts: 2.01 us -> 4 us
    all_to_all x3, waiting for transfers between devices: 2.89 us -> 5.38 us  [swap(): return lax.all_to_all(value, PLANE, split_axis=0, concat_axis=0, tiled=True)]
    ppermute x12, waiting for transfers between devices: 38.2 us -> 35.8 us  [next_on_ring(): lax.ppermute(block, 'outer', [(i, (i + 1) % outer) for i in range(outer)])]
    unnamed x6 -> x14, local copies, waits for them, and re-layouts: 0.01 us -> 1.94 us
  transfers between devices with their start and end apart: 28 -> 28, of which waited for: 18 -> 20; matrix products, arithmetic and copies ran while one was open for 2% -> 2% of each run, Pallas kernels for 13% -> 12%
where the time goes in v30:
time: 110 us; the launch traced here: 109 us
  waiting for transfers between devices  58.4 us (53%)
  starting transfers between devices  28.7 us (26%)
  Pallas kernels  16.9 us (15%)
  local copies, waits for them, and re-layouts  4 us (4%)
    ppermute x12, waiting for transfers between devices, next_on_ring(): lax.ppermute(block, 'outer', [(i, (i + 1) % outer) for i in range(outer)])  35.8 us
    ppermute x13, waiting for transfers between devices, to_partner(): return lax.ppermute(value, axes, [(i, i ^ offset) for i in range(size)])  17.2 us
    ppermute x13, starting transfers between devices, to_partner(): return lax.ppermute(value, axes, [(i, i ^ offset) for i in range(size)])  12.3 us
    all_to_all x3, starting transfers between devices, swap(): return lax.all_to_all(value, PLANE, split_axis=0, concat_axis=0, tiled=True)  11.6 us
    all_to_all x3, waiting for transfers between devices, swap(): return lax.all_to_all(value, PLANE, split_axis=0, concat_axis=0, tiled=True)  5.38 us
    pallas_call x2, Pallas kernels, up_product(): pl.pallas_call(functools.partial(up_kernel, len(maps), rank, offsets), ou...  5.09 us
    ppermute x12, starting transfers between devices, next_on_ring(): lax.ppermute(block, 'outer', [(i, (i + 1) % outer) for i in range(outer)])  4.82 us
    pallas_call x1, Pallas kernels, down_product(): pl.pallas_call(functools.partial(down_kernel, len(maps), rank), out_shape...  4.25 us
  transfers between devices with their start and end apart: 28, of which 20 were waited for; matrix products, arithmetic and copies ran while one was open for 2% of the time, Pallas kernels for 12%

profile of v30, /device:TPU:0, one launch (start us, length us, event | category | flops | bytes accessed | tf_op | source)
XLA Modules:
  0.0 109.1 jit_solution(4602556292178133815)
XLA Ops:
  1.7 2.6 %collective-permute-start.1 = (bf16[64,1024]{1,0:T(8,128)(2,1)S(1)}, bf16[64,1024]{1,0:T(8,128)(2,1)S(1)}, u32[]{:S(2)}, u32[]{:S(2)}) collective-permute-start(bf16[64,1024]{1,0:T(8,128)(2,1)S(1)} %get-tuple-element.50), channel_id=1, source_target_pairs={{0,2},{1,3},{2,0},{3,1},{4,6},{5,7},{6,4},{7,5},{8,10},{9,11},{10,... | collective-permute-start | bytes 393224 | tf_op jit(solution)/shard_map/ppermute | solution.py:27
  4.3 1.8 %collective-permute-start.3 = (bf16[128,1024]{1,0:T(8,128)(2,1)S(1)}, bf16[128,1024]{1,0:T(8,128)(2,1)S(1)}, u32[]{:S(2)}, u32[]{:S(2)}) collective-permute-start(bf16[128,1024]{1,0:T(8,128)(2,1)S(1)} %join_blocks.6.refs_0_), channel_id=1, source_target_pairs={{0,4},{4,8},{8,12},{12,0},{1,5},{5,9},{9,13},{13,1},{2,6},{6,10},{... | collective-permute-start | bytes 786440 | tf_op jit(solution)/shard_map/ppermute | solution.py:31
  6.2 1.6 %outgoing_rows.1 = bf16[8,136,1024]{2,1,0:T(8,128)(2,1)} custom-call(bf16[128,8192]{1,0:T(8,128)(2,1)S(1)} %copy-done, s32[1,128]{1,0:T(1,128)S(1)} %bitcast.26), custom_call_target="tpu_custom_call" | custom-call | tf_op jit(solution)/shard_map/outgoing_rows/pallas_call | solution.py:94
  7.8 3.7 %all-to-all-start = ((bf16[8,136,1024]{2,1,0:T(8,128)(2,1)}), bf16[8,136,1024]{2,1,0:T(8,128)(2,1)S(1)}, u32[]{:S(2)}, u32[]{:S(2)}) async-start(bf16[8,136,1024]{2,1,0:T(8,128)(2,1)} %outgoing_rows.1), calls=%async_computation | async-start | bytes 4456448 | tf_op jit(solution)/shard_map/all_to_all | solution.py:39
  11.6 1.6 %collective-permute-start.4 = (bf16[128,1024]{1,0:T(8,128)(2,1)S(1)}, bf16[128,1024]{1,0:T(8,128)(2,1)S(1)}, u32[]{:S(2)}, u32[]{:S(2)}) collective-permute-start(bf16[128,1024]{1,0:T(8,128)(2,1)S(1)} %join_blocks.7.refs_1_), channel_id=1, source_target_pairs={{0,4},{4,8},{8,12},{12,0},{1,5},{5,9},{9,13},{13,1},{2,6},{6,10},{... | collective-permute-start | bytes 786440 | tf_op jit(solution)/shard_map/ppermute | solution.py:31
  13.2 1.8 %collective-permute-done.3.refs_0_.refs_2_ = bf16[128,1024]{1,0:T(8,128)(2,1)S(1)} collective-permute-done((bf16[128,1024]{1,0:T(8,128)(2,1)S(1)}, bf16[128,1024]{1,0:T(8,128)(2,1)S(1)}, u32[]{:S(2)}, u32[]{:S(2)}) %collective-permute-start.3) | collective-permute-done | bytes 262176 | tf_op jit(solution)/shard_map/ppermute | solution.py:31
  15.1 7.4 %collective-permute-done.4.refs_0_.refs_3_ = bf16[128,1024]{1,0:T(8,128)(2,1)S(1)} collective-permute-done((bf16[128,1024]{1,0:T(8,128)(2,1)S(1)}, bf16[128,1024]{1,0:T(8,128)(2,1)S(1)}, u32[]{:S(2)}, u32[]{:S(2)}) %collective-permute-start.4) | collective-permute-done | bytes 262176 | tf_op jit(solution)/shard_map/ppermute | solution.py:31
  23.3 4.8 %collective-permute-done.5.refs_4_ = bf16[128,1024]{1,0:T(8,128)(2,1)S(1)} collective-permute-done((bf16[128,1024]{1,0:T(8,128)(2,1)S(1)}, bf16[128,1024]{1,0:T(8,128)(2,1)S(1)}, u32[]{:S(2)}, u32[]{:S(2)}) %collective-permute-start.5) | collective-permute-done | bytes 262176 | tf_op jit(solution)/shard_map/ppermute | solution.py:31
  29.0 2.1 %collective-permute-start.10 = (bf16[64,1024]{1,0:T(8,128)(2,1)}, bf16[64,1024]{1,0:T(8,128)(2,1)}, u32[]{:S(2)}, u32[]{:S(2)}) collective-permute-start(bf16[64,1024]{1,0:T(8,128)(2,1)} %get-tuple-element.30), channel_id=1, source_target_pairs={{0,2},{1,3},{2,0},{3,1},{4,6},{5,7},{6,4},{7,5},{8,10},{9,11},{10,... | collective-permute-start | bytes 393224 | tf_op jit(solution)/shard_map/ppermute | solution.py:27
  31.3 3.3 %collective-permute-done.6.refs_5_ = bf16[128,1024]{1,0:T(8,128)(2,1)} collective-permute-done((bf16[128,1024]{1,0:T(8,128)(2,1)}, bf16[128,1024]{1,0:T(8,128)(2,1)}, u32[]{:S(2)}, u32[]{:S(2)}) %collective-permute-start.6) | collective-permute-done | bytes 262176 | tf_op jit(solution)/shard_map/ppermute | solution.py:31
  35.7 4.6 %collective-permute-done.7.refs_6_ = bf16[128,1024]{1,0:T(8,128)(2,1)} collective-permute-done((bf16[128,1024]{1,0:T(8,128)(2,1)S(1)}, bf16[128,1024]{1,0:T(8,128)(2,1)}, u32[]{:S(2)}, u32[]{:S(2)}) %collective-permute-start.7) | collective-permute-done | bytes 262176 | tf_op jit(solution)/shard_map/ppermute | solution.py:31
  40.5 1.6 %collective-permute-done.10.refs_0_ = bf16[64,1024]{1,0:T(8,128)(2,1)} collective-permute-done((bf16[64,1024]{1,0:T(8,128)(2,1)}, bf16[64,1024]{1,0:T(8,128)(2,1)}, u32[]{:S(2)}, u32[]{:S(2)}) %collective-permute-start.10) | collective-permute-done | bytes 131104 | tf_op jit(solution)/shard_map/ppermute | solution.py:27
  42.0 4.0 %collective-permute-done.8.refs_7_ = bf16[128,1024]{1,0:T(8,128)(2,1)} collective-permute-done((bf16[128,1024]{1,0:T(8,128)(2,1)}, bf16[128,1024]{1,0:T(8,128)(2,1)}, u32[]{:S(2)}, u32[]{:S(2)}) %collective-permute-start.8) | collective-permute-done | bytes 262176 | tf_op jit(solution)/shard_map/ppermute | solution.py:31
  46.1 1.7 %join_blocks.10.refs_1_ = bf16[128,1024]{1,0:T(8,128)(2,1)} custom-call(bf16[64,1024]{1,0:T(8,128)(2,1)} %collective-permute-done.10.refs_0_, bf16[64,1024]{1,0:T(8,128)(2,1)} %collective-permute-done.11.refs_1_), custom_call_target="tpu_custom_call" | custom-call | flops 1500000000 | bytes 1000000 | tf_op jit(solution)/shard_map/join_blocks/pallas_call | solution.py:60
  47.7 2.5 %collective-permute-done.12.refs_0_.refs_2_ = bf16[128,1024]{1,0:T(8,128)(2,1)S(1)} collective-permute-done((bf16[128,1024]{1,0:T(8,128)(2,1)S(1)}, bf16[128,1024]{1,0:T(8,128)(2,1)S(1)}, u32[]{:S(2)}, u32[]{:S(2)}) %collective-permute-start.12) | collective-permute-done | bytes 262176 | tf_op jit(solution)/shard_map/ppermute | solution.py:31
  52.9 4.3 %down_product.1 = (f32[8,64,128]{2,1,0:T(8,128)}, f32[8,128]{1,0:T(8,128)S(1)}) custom-call(s32[16]{0:T(128)S(1)} %add.61.labels_ref, bf16[8,136,1024]{2,1,0:T(8,128)(2,1)S(1)} %all-to-all-done.rows_ref, bf16[128,1024]{1,0:T(8,128)(2,1)S(1)} %join_blocks.6.refs_0_, bf16[128,1024]{1,0:T(8,128)(2,1)S(1)} %join_blocks.7.refs_1_, ...), custom_call_target="tpu_custom_call" | custom-call | flops 2147483648 | bytes 4194304 | tf_op jit(solution)/shard_map/down_product/pallas_call | solution.py:146
  57.1 1.4 %collective-permute-done.13.refs_3_ = bf16[128,1024]{1,0:T(8,128)(2,1)} collective-permute-done((bf16[128,1024]{1,0:T(8,128)(2,1)}, bf16[128,1024]{1,0:T(8,128)(2,1)}, u32[]{:S(2)}, u32[]{:S(2)}) %collective-permute-start.13) | collective-permute-done | bytes 262176 | tf_op jit(solution)/shard_map/ppermute | solution.py:31
  58.5 4.5 %all-to-all-start.1 = ((f32[8,64,128]{2,1,0:T(8,128)}), f32[8,64,128]{2,1,0:T(8,128)S(1)}, u32[]{:S(2)}, u32[]{:S(2)}) async-start(f32[8,64,128]{2,1,0:T(8,128)} %get-tuple-element.26), calls=%async_computation.1 | async-start | bytes 524288 | tf_op jit(solution)/shard_map/all_to_all | solution.py:39
  64.4 3.2 %collective-permute-done.15.refs_5_ = bf16[128,1024]{1,0:T(8,128)(2,1)S(1)} collective-permute-done((bf16[128,1024]{1,0:T(8,128)(2,1)}, bf16[128,1024]{1,0:T(8,128)(2,1)S(1)}, u32[]{:S(2)}, u32[]{:S(2)}) %collective-permute-start.15) | collective-permute-done | bytes 262176 | tf_op jit(solution)/shard_map/ppermute | solution.py:31
  67.6 1.4 %all-to-all-done.1.terms_ref = f32[8,64,128]{2,1,0:T(8,128)S(1)} async-done(((f32[8,64,128]{2,1,0:T(8,128)}), f32[8,64,128]{2,1,0:T(8,128)S(1)}, u32[]{:S(2)}, u32[]{:S(2)}) %all-to-all-start.1) | async-done | bytes 262176 | tf_op jit(solution)/shard_map/all_to_all | solution.py:39
  69.8 3.4 %all-to-all-start.2 = ((bf16[8,64,128]{2,1,0:T(8,128)(2,1)}), bf16[8,64,128]{2,1,0:T(8,128)(2,1)S(1)}, u32[]{:S(2)}, u32[]{:S(2)}) async-start(bf16[8,64,128]{2,1,0:T(8,128)(2,1)} %summed_copies.1), calls=%async_computation.2 | async-start | bytes 262144 | tf_op jit(solution)/shard_map/all_to_all | solution.py:39
  74.3 3.9 %all-to-all-done.2.shrunk_ref = bf16[8,64,128]{2,1,0:T(8,128)(2,1)S(1)} async-done(((bf16[8,64,128]{2,1,0:T(8,128)(2,1)}), bf16[8,64,128]{2,1,0:T(8,128)(2,1)S(1)}, u32[]{:S(2)}, u32[]{:S(2)}) %all-to-all-start.2) | async-done | bytes 131104 | tf_op jit(solution)/shard_map/all_to_all | solution.py:39
  78.2 1.4 %collective-permute-done.17.refs_7_ = bf16[128,1024]{1,0:T(8,128)(2,1)S(1)} collective-permute-done((bf16[128,1024]{1,0:T(8,128)(2,1)S(1)}, bf16[128,1024]{1,0:T(8,128)(2,1)S(1)}, u32[]{:S(2)}, u32[]{:S(2)}) %collective-permute-start.17) | collective-permute-done | bytes 262176 | tf_op jit(solution)/shard_map/ppermute | solution.py:31
  79.7 2.5 %up_product.2 = (bf16[128,1024]{1,0:T(8,128)(2,1)S(1)}, bf16[128,1024]{1,0:T(8,128)(2,1)S(1)}, bf16[128,1024]{1,0:T(8,128)(2,1)S(1)}, bf16[128,1024]{1,0:T(8,128)(2,1)S(1)}) custom-call(s32[16]{0:T(128)S(1)} %add.61.labels_ref, s32[1]{0:T(128)} %bitcast.me_ref, f32[8,128]{1,0:T(8,128)S(1)} %get-tuple-element.25.ids_ref, ...), custom_call_target="tpu_custom_call" | custom-call | flops 1073741824 | bytes 3145728 | tf_op jit(solution)/shard_map/up_product/pallas_call | solution.py:217
  82.2 2.6 %collective-permute-start.23 = (bf16[128,1024]{1,0:T(8,128)(2,1)S(1)}, bf16[128,1024]{1,0:T(8,128)(2,1)S(1)}, u32[]{:S(2)}, u32[]{:S(2)}) collective-permute-start(bf16[128,1024]{1,0:T(8,128)(2,1)S(1)} %get-tuple-element.40), channel_id=1, source_target_pairs={{0,18},{1,19},{2,16},{3,17},{16,2},{17,3},{18,0},{19,1},{4,22},{5,... | collective-permute-start | bytes 786440 | tf_op jit(solution)/shard_map/ppermute | solution.py:27
  86.7 2.5 %up_product.3 = (bf16[128,1024]{1,0:T(8,128)(2,1)S(1)}, bf16[128,1024]{1,0:T(8,128)(2,1)S(1)}, bf16[128,1024]{1,0:T(8,128)(2,1)S(1)}, bf16[128,1024]{1,0:T(8,128)(2,1)S(1)}) custom-call(s32[16]{0:T(128)S(1)} %add.61.labels_ref, s32[1]{0:T(128)} %bitcast.me_ref, f32[8,128]{1,0:T(8,128)S(1)} %get-tuple-element.25.ids_ref, ...), custom_call_target="tpu_custom_call" | custom-call | flops 1073741824 | bytes 3145728 | tf_op jit(solution)/shard_map/up_product/pallas_call | solution.py:217
  89.2 1.7 %collective-permute-start.20 = (bf16[128,1024]{1,0:T(8,128)(2,1)S(1)}, bf16[128,1024]{1,0:T(8,128)(2,1)S(1)}, u32[]{:S(2)}, u32[]{:S(2)}) collective-permute-start(bf16[128,1024]{1,0:T(8,128)(2,1)S(1)} %get-tuple-element.37), channel_id=1, source_target_pairs={{0,2},{1,3},{2,0},{3,1},{16,18},{17,19},{18,16},{19,17},{4,6},{5,7... | collective-permute-start | bytes 786440 | tf_op jit(solution)/shard_map/ppermute | solution.py:27
  90.9 1.4 %collective-permute-done.23.refs_0_ = bf16[128,1024]{1,0:T(8,128)(2,1)S(1)} collective-permute-done((bf16[128,1024]{1,0:T(8,128)(2,1)S(1)}, bf16[128,1024]{1,0:T(8,128)(2,1)S(1)}, u32[]{:S(2)}, u32[]{:S(2)}) %collective-permute-start.23) | collective-permute-done | bytes 262176 | tf_op jit(solution)/shard_map/ppermute | solution.py:27
  92.4 4.9 %collective-permute-done.24.refs_1_ = bf16[128,1024]{1,0:T(8,128)(2,1)S(1)} collective-permute-done((bf16[128,1024]{1,0:T(8,128)(2,1)S(1)}, bf16[128,1024]{1,0:T(8,128)(2,1)S(1)}, u32[]{:S(2)}, u32[]{:S(2)}) %collective-permute-start.24) | collective-permute-done | bytes 262176 | tf_op jit(solution)/shard_map/ppermute | solution.py:27
  98.8 5.1 %collective-permute-done.18.refs_0_ = bf16[128,1024]{1,0:T(8,128)(2,1)S(1)} collective-permute-done((bf16[128,1024]{1,0:T(8,128)(2,1)S(1)}, bf16[128,1024]{1,0:T(8,128)(2,1)S(1)}, u32[]{:S(2)}, u32[]{:S(2)}) %collective-permute-start.18) | collective-permute-done | bytes 262176 | tf_op jit(solution)/shard_map/ppermute | solution.py:27
  103.9 2.8 %collective-permute-done.19.refs_1_ = bf16[128,1024]{1,0:T(8,128)(2,1)S(1)} collective-permute-done((bf16[128,1024]{1,0:T(8,128)(2,1)S(1)}, bf16[128,1024]{1,0:T(8,128)(2,1)S(1)}, u32[]{:S(2)}, u32[]{:S(2)}) %collective-permute-start.19) | collective-permute-done | bytes 262176 | tf_op jit(solution)/shard_map/ppermute | solution.py:27
  106.7 1.3 %collective-permute-done.21.refs_3_ = bf16[128,1024]{1,0:T(8,128)(2,1)S(1)} collective-permute-done((bf16[128,1024]{1,0:T(8,128)(2,1)S(1)}, bf16[128,1024]{1,0:T(8,128)(2,1)S(1)}, u32[]{:S(2)}, u32[]{:S(2)}) %collective-permute-start.21) | collective-permute-done | bytes 262176 | tf_op jit(solution)/shard_map/ppermute | solution.py:27
  (57 shorter events, 15.1 us)
Async XLA Ops:
  1.1 3.2 %collective-permute-start = (bf16[64,1024]{1,0:T(8,128)(2,1)S(1)}, bf16[64,1024]{1,0:T(8,128)(2,1)S(1)}, u32[]{:S(2)}, u32[]{:S(2)}) collective-permute-start(bf16[64,1024]{1,0:T(8,128)(2,1)S(1)} %get-tuple-element.48), channel_id=1, source_target_pairs={{0,1},{1,0},{2,3},{3,2},{4,5},{5,4},{6,7},{7,6},{8,9},{9,8},{10,11... | collective-permute-start | bytes 393224 | tf_op jit(solution)/shard_map/ppermute | solution.py:27
  1.7 9.9 %collective-permute-start.1 = (bf16[64,1024]{1,0:T(8,128)(2,1)S(1)}, bf16[64,1024]{1,0:T(8,128)(2,1)S(1)}, u32[]{:S(2)}, u32[]{:S(2)}) collective-permute-start(bf16[64,1024]{1,0:T(8,128)(2,1)S(1)} %get-tuple-element.50), channel_id=1, source_target_pairs={{0,2},{1,3},{2,0},{3,1},{4,6},{5,7},{6,4},{7,5},{8,10},{9,11},{10,... | collective-permute-start | bytes 393224 | tf_op jit(solution)/shard_map/ppermute | solution.py:27
  4.2 7.3 %collective-permute-start.2 = (bf16[64,1024]{1,0:T(8,128)(2,1)S(1)}, bf16[64,1024]{1,0:T(8,128)(2,1)S(1)}, u32[]{:S(2)}, u32[]{:S(2)}) collective-permute-start(bf16[64,1024]{1,0:T(8,128)(2,1)S(1)} %get-tuple-element.47), channel_id=1, source_target_pairs={{0,3},{1,2},{2,1},{3,0},{4,7},{5,6},{6,5},{7,4},{8,11},{9,10},{10,... | collective-permute-start | bytes 393224 | tf_op jit(solution)/shard_map/ppermute | solution.py:27
  4.3 1.9 %copy-start = (bf16[128,8192]{1,0:T(8,128)(2,1)S(1)}, bf16[128,8192]{1,0:T(8,128)(2,1)}, u32[]{:S(2)}) copy-start(bf16[128,8192]{1,0:T(8,128)(2,1)} %hidden_ref) | copy-start | bytes 6291460
  4.3 1.9 %copy-start.1 = (s32[128,1]{0,1:T(1,128)S(1)}, s32[128,1]{0,1:T(1,128)}, u32[]{:S(2)}) copy-start(s32[128,1]{0,1:T(1,128)} %param.4) | copy-start | bytes 1540
  4.3 10.7 %collective-permute-start.3 = (bf16[128,1024]{1,0:T(8,128)(2,1)S(1)}, bf16[128,1024]{1,0:T(8,128)(2,1)S(1)}, u32[]{:S(2)}, u32[]{:S(2)}) collective-permute-start(bf16[128,1024]{1,0:T(8,128)(2,1)S(1)} %join_blocks.6.refs_0_), channel_id=1, source_target_pairs={{0,4},{4,8},{8,12},{12,0},{1,5},{5,9},{9,13},{13,1},{2,6},{6,10},{... | collective-permute-start | bytes 786440 | tf_op jit(solution)/shard_map/ppermute | solution.py:31
  7.8 43.2 %all-to-all-start = ((bf16[8,136,1024]{2,1,0:T(8,128)(2,1)}), bf16[8,136,1024]{2,1,0:T(8,128)(2,1)S(1)}, u32[]{:S(2)}, u32[]{:S(2)}) async-start(bf16[8,136,1024]{2,1,0:T(8,128)(2,1)} %outgoing_rows.1), calls=%async_computation | async-start | bytes 4456448 | tf_op jit(solution)/shard_map/all_to_all | solution.py:39
  11.6 11.0 %collective-permute-start.4 = (bf16[128,1024]{1,0:T(8,128)(2,1)S(1)}, bf16[128,1024]{1,0:T(8,128)(2,1)S(1)}, u32[]{:S(2)}, u32[]{:S(2)}) collective-permute-start(bf16[128,1024]{1,0:T(8,128)(2,1)S(1)} %join_blocks.7.refs_1_), channel_id=1, source_target_pairs={{0,4},{4,8},{8,12},{12,0},{1,5},{5,9},{9,13},{13,1},{2,6},{6,10},{... | collective-permute-start | bytes 786440 | tf_op jit(solution)/shard_map/ppermute | solution.py:31
  15.0 13.1 %copy-start.6 = (bf16[1,64,8192]{2,1,0:T(8,128)(2,1)S(1)}, bf16[1,64,8192]{2,1,0:T(8,128)(2,1)}, u32[]{:S(2)}) copy-start(bf16[1,64,8192]{2,1,0:T(8,128)(2,1)} %param.7) | copy-start | bytes 3145732
  15.1 13.1 %collective-permute-start.5 = (bf16[128,1024]{1,0:T(8,128)(2,1)S(1)}, bf16[128,1024]{1,0:T(8,128)(2,1)S(1)}, u32[]{:S(2)}, u32[]{:S(2)}) collective-permute-start(bf16[128,1024]{1,0:T(8,128)(2,1)S(1)} %join_blocks.8), channel_id=1, source_target_pairs={{0,4},{4,8},{8,12},{12,0},{1,5},{5,9},{9,13},{13,1},{2,6},{6,10},{... | collective-permute-start | bytes 786440 | tf_op jit(solution)/shard_map/ppermute | solution.py:31
  23.3 11.4 %collective-permute-start.6 = (bf16[128,1024]{1,0:T(8,128)(2,1)}, bf16[128,1024]{1,0:T(8,128)(2,1)}, u32[]{:S(2)}, u32[]{:S(2)}) collective-permute-start(bf16[128,1024]{1,0:T(8,128)(2,1)} %join_blocks.9), channel_id=1, source_target_pairs={{0,4},{4,8},{8,12},{12,0},{1,5},{5,9},{9,13},{13,1},{2,6},{6,10},{... | collective-permute-start | bytes 786440 | tf_op jit(solution)/shard_map/ppermute | solution.py:31
  28.2 7.5 %copy-start.4 = (bf16[128,1024]{1,0:T(8,128)(2,1)}, bf16[128,1024]{1,0:T(8,128)(2,1)S(1)}, u32[]{:S(2)}) copy-start(bf16[128,1024]{1,0:T(8,128)(2,1)S(1)} %collective-permute-done.5.refs_4_) | copy-start | bytes 786436
  28.2 12.1 %collective-permute-start.7 = (bf16[128,1024]{1,0:T(8,128)(2,1)S(1)}, bf16[128,1024]{1,0:T(8,128)(2,1)}, u32[]{:S(2)}, u32[]{:S(2)}) collective-permute-start(bf16[128,1024]{1,0:T(8,128)(2,1)S(1)} %collective-permute-done.5.refs_4_), channel_id=1, source_target_pairs={{0,4},{4,8},{8,12},{12,0},{1,5},{5,9},{9,13},{13,1},{2,6},{6,10},{... | collective-permute-start | bytes 786440 | tf_op jit(solution)/shard_map/ppermute | solution.py:31
  29.0 5.7 %collective-permute-start.9 = (bf16[64,1024]{1,0:T(8,128)(2,1)S(1)}, bf16[64,1024]{1,0:T(8,128)(2,1)}, u32[]{:S(2)}, u32[]{:S(2)}) collective-permute-start(bf16[64,1024]{1,0:T(8,128)(2,1)S(1)} %get-tuple-element.28), channel_id=1, source_target_pairs={{0,1},{1,0},{2,3},{3,2},{4,5},{5,4},{6,7},{7,6},{8,9},{9,8},{10,11... | collective-permute-start | bytes 393224 | tf_op jit(solution)/shard_map/ppermute | solution.py:27
  29.0 13.0 %collective-permute-start.10 = (bf16[64,1024]{1,0:T(8,128)(2,1)}, bf16[64,1024]{1,0:T(8,128)(2,1)}, u32[]{:S(2)}, u32[]{:S(2)}) collective-permute-start(bf16[64,1024]{1,0:T(8,128)(2,1)} %get-tuple-element.30), channel_id=1, source_target_pairs={{0,2},{1,3},{2,0},{3,1},{4,6},{5,7},{6,4},{7,5},{8,10},{9,11},{10,... | collective-permute-start | bytes 393224 | tf_op jit(solution)/shard_map/ppermute | solution.py:27
  31.2 14.9 %collective-permute-start.11 = (bf16[64,1024]{1,0:T(8,128)(2,1)}, bf16[64,1024]{1,0:T(8,128)(2,1)}, u32[]{:S(2)}, u32[]{:S(2)}) collective-permute-start(bf16[64,1024]{1,0:T(8,128)(2,1)} %get-tuple-element.32), channel_id=1, source_target_pairs={{0,3},{1,2},{2,1},{3,0},{4,7},{5,6},{6,5},{7,4},{8,11},{9,10},{10,... | collective-permute-start | bytes 393224 | tf_op jit(solution)/shard_map/ppermute | solution.py:27
  34.7 11.4 %collective-permute-start.8 = (bf16[128,1024]{1,0:T(8,128)(2,1)}, bf16[128,1024]{1,0:T(8,128)(2,1)}, u32[]{:S(2)}, u32[]{:S(2)}) collective-permute-start(bf16[128,1024]{1,0:T(8,128)(2,1)} %collective-permute-done.6.refs_5_), channel_id=1, source_target_pairs={{0,4},{4,8},{8,12},{12,0},{1,5},{5,9},{9,13},{13,1},{2,6},{6,10},{... | collective-permute-start | bytes 786440 | tf_op jit(solution)/shard_map/ppermute | solution.py:31
  40.3 9.9 %collective-permute-start.12 = (bf16[128,1024]{1,0:T(8,128)(2,1)S(1)}, bf16[128,1024]{1,0:T(8,128)(2,1)S(1)}, u32[]{:S(2)}, u32[]{:S(2)}) collective-permute-start(bf16[128,1024]{1,0:T(8,128)(2,1)S(1)} %pad_maximum_fusion.refs_0_), channel_id=1, source_target_pairs={{0,4},{4,8},{8,12},{12,0},{1,5},{5,9},{9,13},{13,1},{2,6},{6,10},{... | collective-permute-start | bytes 786440 | tf_op jit(solution)/shard_map/ppermute | solution.py:31
  47.7 10.8 %collective-permute-start.13 = (bf16[128,1024]{1,0:T(8,128)(2,1)}, bf16[128,1024]{1,0:T(8,128)(2,1)}, u32[]{:S(2)}, u32[]{:S(2)}) collective-permute-start(bf16[128,1024]{1,0:T(8,128)(2,1)} %join_blocks.10.refs_1_), channel_id=1, source_target_pairs={{0,4},{4,8},{8,12},{12,0},{1,5},{5,9},{9,13},{13,1},{2,6},{6,10},{... | collective-permute-start | bytes 786440 | tf_op jit(solution)/shard_map/ppermute | solution.py:31
  51.0 12.2 %collective-permute-start.14 = (bf16[128,1024]{1,0:T(8,128)(2,1)}, bf16[128,1024]{1,0:T(8,128)(2,1)}, u32[]{:S(2)}, u32[]{:S(2)}) collective-permute-start(bf16[128,1024]{1,0:T(8,128)(2,1)} %join_blocks.11), channel_id=1, source_target_pairs={{0,4},{4,8},{8,12},{12,0},{1,5},{5,9},{9,13},{13,1},{2,6},{6,10},{... | collective-permute-start | bytes 786440 | tf_op jit(solution)/shard_map/ppermute | solution.py:31
  58.5 9.1 %collective-permute-start.15 = (bf16[128,1024]{1,0:T(8,128)(2,1)}, bf16[128,1024]{1,0:T(8,128)(2,1)S(1)}, u32[]{:S(2)}, u32[]{:S(2)}) collective-permute-start(bf16[128,1024]{1,0:T(8,128)(2,1)} %collective-permute-done.13.refs_3_), channel_id=1, source_target_pairs={{0,4},{4,8},{8,12},{12,0},{1,5},{5,9},{9,13},{13,1},{2,6},{6,10},{... | collective-permute-start | bytes 786440 | tf_op jit(solution)/shard_map/ppermute | solution.py:31
  58.5 10.5 %all-to-all-start.1 = ((f32[8,64,128]{2,1,0:T(8,128)}), f32[8,64,128]{2,1,0:T(8,128)S(1)}, u32[]{:S(2)}, u32[]{:S(2)}) async-start(f32[8,64,128]{2,1,0:T(8,128)} %get-tuple-element.26), calls=%async_computation.1 | async-start | bytes 524288 | tf_op jit(solution)/shard_map/all_to_all | solution.py:39
  63.1 11.2 %collective-permute-start.16 = (bf16[128,1024]{1,0:T(8,128)(2,1)}, bf16[128,1024]{1,0:T(8,128)(2,1)S(1)}, u32[]{:S(2)}, u32[]{:S(2)}) collective-permute-start(bf16[128,1024]{1,0:T(8,128)(2,1)} %collective-permute-done.14.refs_4_), channel_id=1, source_target_pairs={{0,4},{4,8},{8,12},{12,0},{1,5},{5,9},{9,13},{13,1},{2,6},{6,10},{... | collective-permute-start | bytes 786440 | tf_op jit(solution)/shard_map/ppermute | solution.py:31
  67.6 12.0 %collective-permute-start.17 = (bf16[128,1024]{1,0:T(8,128)(2,1)S(1)}, bf16[128,1024]{1,0:T(8,128)(2,1)S(1)}, u32[]{:S(2)}, u32[]{:S(2)}) collective-permute-start(bf16[128,1024]{1,0:T(8,128)(2,1)S(1)} %collective-permute-done.15.refs_5_), channel_id=1, source_target_pairs={{0,4},{4,8},{8,12},{12,0},{1,5},{5,9},{9,13},{13,1},{2,6},{6,10},{... | collective-permute-start | bytes 786440 | tf_op jit(solution)/shard_map/ppermute | solution.py:31
  69.8 8.5 %all-to-all-start.2 = ((bf16[8,64,128]{2,1,0:T(8,128)(2,1)}), bf16[8,64,128]{2,1,0:T(8,128)(2,1)S(1)}, u32[]{:S(2)}, u32[]{:S(2)}) async-start(bf16[8,64,128]{2,1,0:T(8,128)(2,1)} %summed_copies.1), calls=%async_computation.2 | async-start | bytes 262144 | tf_op jit(solution)/shard_map/all_to_all | solution.py:39
  82.2 10.2 %collective-permute-start.23 = (bf16[128,1024]{1,0:T(8,128)(2,1)S(1)}, bf16[128,1024]{1,0:T(8,128)(2,1)S(1)}, u32[]{:S(2)}, u32[]{:S(2)}) collective-permute-start(bf16[128,1024]{1,0:T(8,128)(2,1)S(1)} %get-tuple-element.40), channel_id=1, source_target_pairs={{0,18},{1,19},{2,16},{3,17},{16,2},{17,3},{18,0},{19,1},{4,22},{5,... | collective-permute-start | bytes 786440 | tf_op jit(solution)/shard_map/ppermute | solution.py:27
  84.8 12.4 %collective-permute-start.24 = (bf16[128,1024]{1,0:T(8,128)(2,1)S(1)}, bf16[128,1024]{1,0:T(8,128)(2,1)S(1)}, u32[]{:S(2)}, u32[]{:S(2)}) collective-permute-start(bf16[128,1024]{1,0:T(8,128)(2,1)S(1)} %get-tuple-element.41), channel_id=1, source_target_pairs={{0,19},{1,18},{2,17},{3,16},{16,3},{17,2},{18,1},{19,0},{4,23},{5,... | collective-permute-start | bytes 786440 | tf_op jit(solution)/shard_map/ppermute | solution.py:27
  84.8 19.1 %collective-permute-start.18 = (bf16[128,1024]{1,0:T(8,128)(2,1)S(1)}, bf16[128,1024]{1,0:T(8,128)(2,1)S(1)}, u32[]{:S(2)}, u32[]{:S(2)}) collective-permute-start(bf16[128,1024]{1,0:T(8,128)(2,1)S(1)} %get-tuple-element.35), channel_id=1, source_target_pairs={{0,16},{1,17},{2,18},{3,19},{16,0},{17,1},{18,2},{19,3},{4,20},{5,... | collective-permute-start | bytes 786440 | tf_op jit(solution)/shard_map/ppermute | solution.py:27
  85.4 21.3 %collective-permute-start.19 = (bf16[128,1024]{1,0:T(8,128)(2,1)S(1)}, bf16[128,1024]{1,0:T(8,128)(2,1)S(1)}, u32[]{:S(2)}, u32[]{:S(2)}) collective-permute-start(bf16[128,1024]{1,0:T(8,128)(2,1)S(1)} %get-tuple-element.36), channel_id=1, source_target_pairs={{0,17},{1,16},{2,19},{3,18},{16,1},{17,0},{18,3},{19,2},{4,21},{5,... | collective-permute-start | bytes 786440 | tf_op jit(solution)/shard_map/ppermute | solution.py:27
  89.2 17.5 %collective-permute-start.20 = (bf16[128,1024]{1,0:T(8,128)(2,1)S(1)}, bf16[128,1024]{1,0:T(8,128)(2,1)S(1)}, u32[]{:S(2)}, u32[]{:S(2)}) collective-permute-start(bf16[128,1024]{1,0:T(8,128)(2,1)S(1)} %get-tuple-element.37), channel_id=1, source_target_pairs={{0,2},{1,3},{2,0},{3,1},{16,18},{17,19},{18,16},{19,17},{4,6},{5,7... | collective-permute-start | bytes 786440 | tf_op jit(solution)/shard_map/ppermute | solution.py:27
  92.4 15.6 %collective-permute-start.21 = (bf16[128,1024]{1,0:T(8,128)(2,1)S(1)}, bf16[128,1024]{1,0:T(8,128)(2,1)S(1)}, u32[]{:S(2)}, u32[]{:S(2)}) collective-permute-start(bf16[128,1024]{1,0:T(8,128)(2,1)S(1)} %get-tuple-element.38), channel_id=1, source_target_pairs={{0,3},{1,2},{2,1},{3,0},{16,19},{17,18},{18,17},{19,16},{4,7},{5,6... | collective-permute-start | bytes 786440 | tf_op jit(solution)/shard_map/ppermute | solution.py:27
  97.3 10.7 %collective-permute-start.22 = (bf16[128,1024]{1,0:T(8,128)(2,1)S(1)}, bf16[128,1024]{1,0:T(8,128)(2,1)S(1)}, u32[]{:S(2)}, u32[]{:S(2)}) collective-permute-start(bf16[128,1024]{1,0:T(8,128)(2,1)S(1)} %get-tuple-element.39), channel_id=1, source_target_pairs={{0,1},{1,0},{2,3},{3,2},{16,17},{17,16},{18,19},{19,18},{4,5},{5,4... | collective-permute-start | bytes 786440 | tf_op jit(solution)/shard_map/ppermute | solution.py:27
  (3 other events, 2.7 us)
